TPU v7x, 32 devices: a whole 2x2x4 slice. The times are simulated.
32 devices in a mesh: enc: 8 (over z, core), seq: 4 (over y, x).
Axes of the slice: x: 2, y: 2, z: 4, core: 2. Of those that a mesh axis runs over, the one named last changes fastest.
Arguments:
- queries: bfloat16 [8, 512, 8192], P('enc', 'seq'), may hold values from -160 to 160
- kv_pool: bfloat16 [32, 2, 128, 8192], P('enc', None, None, 'seq'), may hold values from -16 to 16
- send_lists: int32 [8, 8, 1], P('enc'), may hold values from 0 to 3, as said below
- block_slots: int32 [8, 8, 2], P('enc'), may hold values from 0 to 7, as said below
- grad_context: bfloat16 [8, 512, 8192], P('enc', 'seq'), may hold values from -24 to 24
Outputs:
- context: bfloat16 [8, 512, 8192], P('enc', 'seq')
- grad_queries: bfloat16 [8, 512, 8192], P('enc', 'seq')
- grad_pool: bfloat16 [32, 2, 128, 8192], P('enc', None, None, 'seq')
Inputs may be any that keep to these rules, and one draw needn't show every extreme that they name: send_lists[o, e] names 1 different local entries; each of a shard's 4 entries is named for at least one sequence. `block_slots`: the two slots of a block differ; every slot of a sequence is named by at least one of its blocks.
All inputs are finite; a program needn't handle non-finite values.
Results may differ from a plain program's by a relative error of at most 0.0065.
Values may be sent and summed in bfloat16 or wider, within the bound.
No kernel may reach another device: no remote copies, remote signals or barrier semaphores. Data moves between devices by JAX's collectives and lax.ppermute only.
A program may use at most 128 MiB of HBM per device.

v0:
```python
import jax
import jax.numpy as jnp
from jax import lax
from jax.sharding import PartitionSpec as P

DH = 128
BLOCK = 64
NBLEN = 128


def to_heads(token_major):
    return lax.all_to_all(token_major, "seq", split_axis=2, concat_axis=1, tiled=True)


def to_tokens(head_major):
    return lax.all_to_all(head_major, "seq", split_axis=1, concat_axis=2, tiled=True)


def fetch_slots(kv_pool, entries):
    outgoing = kv_pool[entries]
    arrived = lax.all_to_all(outgoing, "enc", split_axis=0, concat_axis=0, tiled=True)
    return arrived.reshape((-1,) + kv_pool.shape[1:])


def move_up(row_data):
    filler = jnp.zeros((BLOCK - 1, row_data.shape[1]), row_data.dtype)
    return jnp.concatenate([row_data[BLOCK - 1 :], filler], axis=0)


def move_down(row_data):
    filler = jnp.zeros((BLOCK - 1, row_data.shape[1]), row_data.dtype)
    return jnp.concatenate([filler, row_data[: row_data.shape[0] - BLOCK + 1]], axis=0)


def into_blocks(head_rows, heads_here):
    blocks = head_rows.shape[0] // BLOCK
    return move_up(head_rows).reshape(blocks, BLOCK, heads_here, DH).transpose(0, 2, 1, 3)


def out_of_blocks(block_rows):
    blocks, heads_here = (block_rows.shape[0], block_rows.shape[1])
    return move_down(block_rows.transpose(0, 2, 1, 3).reshape(blocks * BLOCK, heads_here * DH))


def forward_parts(head_rows, arrived, block_use):
    slots = arrived.shape[0]
    heads_here = arrived.shape[-1] // DH
    queries_moved = into_blocks(head_rows, heads_here)
    pool_heads = arrived.reshape(slots, 2, NBLEN, heads_here, DH).transpose(0, 1, 3, 2, 4)
    keys_used = [pool_heads[:, 0][block_use[:, 0]], pool_heads[:, 0][block_use[:, 1]]]
    values_used = [pool_heads[:, 1][block_use[:, 0]], pool_heads[:, 1][block_use[:, 1]]]
    scores = [
        jnp.einsum("chid,chjd->chij", queries_moved, keys, preferred_element_type=jnp.float32)
        * DH ** (-0.5)
        for keys in keys_used
    ]
    row_peak = jnp.maximum(
        jnp.max(scores[0], axis=-1, keepdims=True), jnp.max(scores[1], axis=-1, keepdims=True)
    )
    weights = [jnp.exp(part_scores - row_peak) for part_scores in scores]
    total = jnp.sum(weights[0], axis=-1, keepdims=True) + jnp.sum(
        weights[1], axis=-1, keepdims=True
    )
    row_probs = [part_weights / total for part_weights in weights]
    probs_low = [part_probs.astype(jnp.bfloat16) for part_probs in row_probs]
    return (queries_moved, keys_used, values_used, row_probs, probs_low)


def local(queries, kv_pool, send_lists, block_slots, grad_context):
    block_use = block_slots[0]
    entries = send_lists[0]
    head_width = kv_pool.shape[-1]
    heads_here = head_width // DH
    score_scale = DH ** (-0.5)
    arrived = fetch_slots(kv_pool, entries)
    slots = arrived.shape[0]
    queries_moved, keys_used, values_used, row_probs, probs_low = forward_parts(
        to_heads(queries)[0], arrived, block_use
    )
    out_blocks = jnp.einsum(
        "chij,chjd->chid", probs_low[0], values_used[0], preferred_element_type=jnp.float32
    )
    out_blocks = out_blocks + jnp.einsum(
        "chij,chjd->chid", probs_low[1], values_used[1], preferred_element_type=jnp.float32
    )
    context = to_tokens(out_of_blocks(out_blocks.astype(jnp.bfloat16))[None])
    head_grads = to_heads(grad_context)[0]
    grads_moved = into_blocks(head_grads, heads_here)
    grad_probs = [
        jnp.einsum("chid,chjd->chij", grads_moved, values, preferred_element_type=jnp.float32)
        for values in values_used
    ]
    row_inner = jnp.sum(row_probs[0] * grad_probs[0], axis=-1, keepdims=True) + jnp.sum(
        row_probs[1] * grad_probs[1], axis=-1, keepdims=True
    )
    grad_scores = [
        (row_probs[n] * (grad_probs[n] - row_inner) * score_scale).astype(jnp.bfloat16)
        for n in range(2)
    ]
    query_grads = jnp.einsum(
        "chij,chjd->chid", grad_scores[0], keys_used[0], preferred_element_type=jnp.float32
    )
    query_grads = query_grads + jnp.einsum(
        "chij,chjd->chid", grad_scores[1], keys_used[1], preferred_element_type=jnp.float32
    )
    grad_queries = to_tokens(out_of_blocks(query_grads.astype(jnp.bfloat16))[None])
    slot_range = jnp.arange(slots, dtype=jnp.int32)
    slot_key = jnp.zeros((slots, heads_here, NBLEN, DH), jnp.float32)
    slot_value = jnp.zeros((slots, heads_here, NBLEN, DH), jnp.float32)
    for n in range(2):
        picker = (block_use[:, n][:, None] == slot_range[None, :]).astype(jnp.bfloat16)
        key_part = jnp.einsum(
            "chij,chid->chjd", grad_scores[n], queries_moved, preferred_element_type=jnp.float32
        ).astype(jnp.bfloat16)
        value_part = jnp.einsum(
            "chij,chid->chjd", probs_low[n], grads_moved, preferred_element_type=jnp.float32
        ).astype(jnp.bfloat16)
        slot_key = slot_key + jnp.einsum(
            "cs,chjd->shjd", picker, key_part, preferred_element_type=jnp.float32
        )
        slot_value = slot_value + jnp.einsum(
            "cs,chjd->shjd", picker, value_part, preferred_element_type=jnp.float32
        )
    slot_grads = jnp.stack([slot_key.astype(jnp.bfloat16), slot_value.astype(jnp.bfloat16)], axis=1)
    slot_grads = slot_grads.transpose(0, 1, 3, 2, 4).reshape(slots, 2, NBLEN, head_width)
    returned = lax.all_to_all(
        slot_grads.reshape(entries.shape + slot_grads.shape[1:]),
        "enc",
        split_axis=0,
        concat_axis=0,
        tiled=True,
    )
    returned = returned.reshape((-1,) + kv_pool.shape[1:])
    owner_pick = (
        entries.reshape(-1)[:, None] == jnp.arange(kv_pool.shape[0], dtype=jnp.int32)[None, :]
    ).astype(jnp.bfloat16)
    pool_grads = jnp.einsum(
        "ep,ekjw->pkjw", owner_pick, returned, preferred_element_type=jnp.float32
    )
    return (context, grad_queries, pool_grads.astype(jnp.bfloat16))


def solution(mesh):
    in_specs = (
        P("enc", "seq", None),
        P("enc", None, None, "seq"),
        P("enc", None, None),
        P("enc", None, None),
        P("enc", "seq", None),
    )
    out_specs = (P("enc", "seq", None), P("enc", "seq", None), P("enc", None, None, "seq"))
    return jax.shard_map(local, mesh=mesh, in_specs=in_specs, out_specs=out_specs, check_vma=False)
```

profile of v0, /device:TPU:15, one launch (start us, length us, event | category | flops | bytes accessed | tf_op | source)
XLA Modules:
  0.0 777.2 jit_solution(7403043626981174117)
XLA Ops:
  0.6 9.5 %copy.57 = bf16[1,128,8192]{1,0,2:T(2,128)(2,1)} copy(bf16[1,128,8192]{2,1,0:T(8,128)(2,1)} %param.5) | data formatting | bytes 4194304 | tf_op args[0]
  10.6 45.1 %reduce = bf16[8192,128]{1,0:T(8,128)(2,1)S(1)} reduce(bf16[8192,1,128]{2,1,0:T(2,128)(2,1)} %bitcast.150, bf16[]{:T(256)} %broadcast.101), dimensions={1}, to_apply=%bitcast.110.reduce_sub_computation | reduce | bytes 4194306
  61.5 9.5 %copy.66 = bf16[1,128,8192]{1,0,2:T(2,128)(2,1)} copy(bf16[1,128,8192]{2,1,0:T(8,128)(2,1)} %param.9) | data formatting | bytes 4194304 | tf_op args[4]
  71.0 46.4 %reduce.2 = bf16[8192,128]{1,0:T(8,128)(2,1)} reduce(bf16[8192,1,128]{2,1,0:T(2,128)(2,1)} %bitcast.157, bf16[]{:T(256)} %broadcast.101), dimensions={1}, to_apply=%bitcast.114.reduce_sub_computation | reduce | bytes 4194306
  117.4 4.0 reshape.133
  121.4 4.5 all-to-all-start.3
  125.9 6.7 gather_fusion
  132.6 16.4 %all-to-all-done.3 = bf16[4,2,131072]{2,1,0:T(2,128)(2,1)} async-done(((bf16[4,2,131072]{2,1,0:T(2,128)(2,1)}), bf16[4,2,131072]{2,1,0:T(2,128)(2,1)}, u32[]{:S(2)}, u32[]{:S(2)}) %all-to-all-start.3) | async-done | bytes 2097184 | tf_op jit(solution)/shard_map/all_to_all | solution.py:12
  149.0 6.9 all-to-all-start.1
  167.2 5.0 reshape.134
  184.1 152.1 %all-to-all-done.1 = bf16[8,1,2,128,2048]{4,3,2,1,0:T(8,128)(2,1)} async-done(((bf16[8,1,2,128,2048]{4,3,2,1,0:T(8,128)(2,1)}), bf16[8,1,2,128,2048]{4,3,2,1,0:T(8,128)(2,1)}, u32[]{:S(2)}, u32[]{:S(2)}) %all-to-all-start.1) | async-done | bytes 8388640 | tf_op jit(solution)/shard_map/all_to_all | solution.py:21
  336.2 11.4 %copy.61 = bf16[8,1,2,128,2048]{3,4,2,0,1:T(8,128)(2,1)} copy(bf16[8,1,2,128,2048]{4,3,2,1,0:T(8,128)(2,1)} %all-to-all-done.1) | data formatting | bytes 16777216 | tf_op jit(solution)/shard_map/all_to_all | solution.py:21
  347.6 11.7 %copy.62 = bf16[8,2,128,16,128]{4,2,3,0,1:T(8,128)(2,1)} copy(bf16[8,2,128,16,128]{2,4,3,1,0:T(8,128)(2,1)} %bitcast.148) | data formatting | bytes 16777216 | tf_op jit(solution)/shard_map/reshape;reshape | solution.py:49
  359.3 6.2 slice_bitcast_fusion.1
  365.4 5.3 gather_fusion.3
  370.7 5.2 gather_fusion.1
  375.9 5.2 gather_fusion.2
  381.1 5.2 gather_fusion.4
  386.3 5.4 multiply_reduce_fusion.3
  394.8 4.0 fusion.19
  398.8 4.2 fusion.49
  406.0 6.5 convolution_convert_fusion
  412.5 8.1 %multiply_reduce_fusion = (f32[8,16,64]{2,1,0:T(8,128)S(1)}, f32[8,16,64]{2,1,0:T(8,128)S(1)}, f32[8,16,64,128]{3,2,1,0:T(8,128)}) fusion(f32[8,16,64]{2,1,0:T(8,128)S(1)} %add.65, f32[8,16,64]{2,1,0:T(8,128)S(1)} %max.8, f32[8,16,64,128]{3,2,1,0:T(8,128)S(1)} %get-tuple-element.33, f32[8,16,64,128]{3,2,1,0:T(8,128)S(1)} %fusion.28, ...), kind=kOutput, calls=%fused_computation.26 | convolution fusion | flops 278904832 | bytes 23199744 | tf_op jit(solution)/shard_map/chid,chjd->chij/dot_general | solution.py:90
  420.6 7.1 multiply_convert_fusion
  441.7 5.2 copy.156
  446.9 14.4 %reduce.1 = bf16[512,2048]{1,0:T(8,128)(2,1)} reduce(bf16[512,1,2048]{2,1,0:T(2,128)(2,1)} %bitcast.154, bf16[]{:T(256)} %broadcast.101), dimensions={1}, to_apply=%bitcast.141.reduce_sub_computation | reduce | bytes 4194306
  461.3 4.5 reshape.131
  465.8 6.1 all-to-all-start.2
  471.9 5.0 convolution_convert_fusion.2
  483.4 5.8 fusion.5
  489.6 5.2 copy.155
  494.9 14.7 %reduce.3 = bf16[512,2048]{1,0:T(8,128)(2,1)} reduce(bf16[512,1,2048]{2,1,0:T(2,128)(2,1)} %bitcast.151, bf16[]{:T(256)} %broadcast.101), dimensions={1}, to_apply=%bitcast.140.reduce_sub_computation | reduce | bytes 4194306
  509.6 4.5 reshape.135
  514.1 6.6 convolution_convert_fusion.1
  520.7 8.4 %fusion.4 = bf16[8,1,16,128,128]{4,0,3,2,1:T(8,128)(2,1)} fusion(f32[8,16,128,128]{3,0,2,1:T(8,128)} %fusion.5, bf16[8,16,128,128]{3,2,1,0:T(8,128)(2,1)S(1)} %convolution_convert_fusion.1, s32[8]{0:T(128)S(1)} %get-tuple-element.26), kind=kOutput, calls=%fused_computation.12 | convolution fusion | flops 37748800 | bytes 16777248 | tf_op jit(solution)/shard_map/cs,chjd->shjd/dot_general | solution.py:121
  533.0 4.9 fusion.9
  537.9 4.8 fusion.3
  542.7 6.2 maximum_bitcast_fusion
  548.9 12.5 %copy.76 = bf16[8,2,128,16,128]{2,4,3,1,0:T(8,128)(2,1)} copy(bf16[8,2,128,16,128]{4,0,2,3,1:T(8,128)(2,1)} %maximum_bitcast_fusion) | data formatting | bytes 16777216 | tf_op jit(solution)/shard_map/transpose | solution.py:125
  561.3 11.5 %copy.77 = bf16[8,1,2,128,2048]{4,3,2,1,0:T(8,128)(2,1)} copy(bf16[8,1,2,128,2048]{3,4,2,0,1:T(8,128)(2,1)} %bitcast.149) | data formatting | bytes 16777216 | tf_op jit(solution)/shard_map/reshape;reshape | solution.py:127
  572.8 9.7 %all-to-all-start.5 = ((bf16[8,1,2,128,2048]{4,3,2,1,0:T(8,128)(2,1)}), bf16[8,1,2,128,2048]{4,3,2,1,0:T(8,128)(2,1)}, u32[]{:S(2)}, u32[]{:S(2)}) async-start(bf16[8,1,2,128,2048]{4,3,2,1,0:T(8,128)(2,1)} %copy.77), calls=%async_computation.5 | async-start | bytes 16777216 | tf_op jit(solution)/shard_map/all_to_all | solution.py:126
  582.6 4.9 reshape.132
  587.5 4.8 copy.86
  596.3 4.1 copy.79
  609.6 4.3 copy.80
  613.9 149.0 %all-to-all-done.5 = bf16[8,1,2,128,2048]{4,3,2,1,0:T(8,128)(2,1)} async-done(((bf16[8,1,2,128,2048]{4,3,2,1,0:T(8,128)(2,1)}), bf16[8,1,2,128,2048]{4,3,2,1,0:T(8,128)(2,1)}, u32[]{:S(2)}, u32[]{:S(2)}) %all-to-all-start.5) | async-done | bytes 8388640 | tf_op jit(solution)/shard_map/all_to_all | solution.py:126
  762.9 9.5 %fusion.13 = bf16[4,2,128,2048]{3,0,2,1:T(4,128)(2,1)S(1)} fusion(bf16[8,1,2,128,2048]{4,3,2,1,0:T(8,128)(2,1)} %all-to-all-done.5, s32[8]{0:T(128)S(1)} %bitcast.175), kind=kOutput, calls=%fused_computation.33 | convolution fusion | flops 35651616 | bytes 12582944 | tf_op jit(solution)/shard_map/ep,ekjw->pkjw/dot_general | solution.py:137
  772.4 4.3 copy.81
  (77 shorter events, 73.5 us)
Async XLA Ops:
  57.7 63.7 %all-to-all-start = ((bf16[4,2,131072]{2,1,0:T(2,128)(2,1)}), bf16[4,2,131072]{2,1,0:T(2,128)(2,1)S(1)}, u32[]{:S(2)}, u32[]{:S(2)}) async-start(bf16[4,2,131072]{2,1,0:T(2,128)(2,1)} %reshape.129), calls=%async_computation | async-start | bytes 4194304 | tf_op jit(solution)/shard_map/all_to_all | solution.py:12
  117.4 8.5 %copy-start.14 = (s32[1,8,1]{1,2,0:T(1,128)S(1)}, s32[1,8,1]{1,2,0:T(1,128)}, u32[]{:S(2)}) copy-start(s32[1,8,1]{1,2,0:T(1,128)} %param.7) | copy-start | bytes 100
  121.4 27.6 %all-to-all-start.3 = ((bf16[4,2,131072]{2,1,0:T(2,128)(2,1)}), bf16[4,2,131072]{2,1,0:T(2,128)(2,1)}, u32[]{:S(2)}, u32[]{:S(2)}) async-start(bf16[4,2,131072]{2,1,0:T(2,128)(2,1)} %reshape.133), calls=%async_computation.3 | async-start | bytes 4194304 | tf_op jit(solution)/shard_map/all_to_all | solution.py:12
  149.0 6.9 copy-start.13
  149.0 187.2 %all-to-all-start.1 = ((bf16[8,1,2,128,2048]{4,3,2,1,0:T(8,128)(2,1)}), bf16[8,1,2,128,2048]{4,3,2,1,0:T(8,128)(2,1)}, u32[]{:S(2)}, u32[]{:S(2)}) async-start(bf16[8,1,2,128,2048]{4,3,2,1,0:T(8,128)(2,1)} %bitcast.146), calls=%async_computation.1 | async-start | bytes 16777216 | tf_op jit(solution)/shard_map/all_to_all | solution.py:21
  386.3 5.4 copy-start.2
  391.7 28.9 %copy-start.1 = (f32[8,16,64,128]{3,2,1,0:T(8,128)}, f32[8,16,64,128]{3,2,1,0:T(8,128)S(1)}, u32[]{:S(2)}) copy-start(f32[8,16,64,128]{3,2,1,0:T(8,128)S(1)} %get-tuple-element.31) | copy-start | bytes 12582916
  394.8 4.0 copy-start.7
  398.8 4.2 copy-start.9
  406.0 6.5 copy-start.6
  420.6 7.1 copy-start
  430.9 3.5 copy-start.12
  430.9 5.0 copy-start.16
  465.8 63.3 %all-to-all-start.2 = ((bf16[4,2,131072]{2,1,0:T(2,128)(2,1)}), bf16[4,2,131072]{2,1,0:T(2,128)(2,1)}, u32[]{:S(2)}, u32[]{:S(2)}) async-start(bf16[4,2,131072]{2,1,0:T(2,128)(2,1)} %reshape.131), calls=%async_computation.2 | async-start | bytes 4194304 | tf_op jit(solution)/shard_map/all_to_all | solution.py:16
  471.9 5.1 copy-start.3
  471.9 5.0 copy-start.4
  481.2 2.2 copy-start.11
  494.9 19.2 %copy-start.10 = (bf16[64,8,16,128]{3,2,1,0:T(8,128)(2,1)S(1)}, bf16[64,8,16,128]{3,2,1,0:T(8,128)(2,1)}, u32[]{:S(2)}) copy-start(bf16[64,8,16,128]{3,2,1,0:T(8,128)(2,1)} %copy.91) | copy-start | bytes 6291460
  529.1 43.7 %all-to-all-start.4 = ((bf16[4,2,131072]{2,1,0:T(2,128)(2,1)}), bf16[4,2,131072]{2,1,0:T(2,128)(2,1)S(1)}, u32[]{:S(2)}, u32[]{:S(2)}) async-start(bf16[4,2,131072]{2,1,0:T(2,128)(2,1)} %reshape.135), calls=%async_computation.4 | async-start | bytes 4194304 | tf_op jit(solution)/shard_map/all_to_all | solution.py:16
  533.0 4.9 copy-start.5
  537.8 4.8 copy-start.8
  572.8 190.0 %all-to-all-start.5 = ((bf16[8,1,2,128,2048]{4,3,2,1,0:T(8,128)(2,1)}), bf16[8,1,2,128,2048]{4,3,2,1,0:T(8,128)(2,1)}, u32[]{:S(2)}, u32[]{:S(2)}) async-start(bf16[8,1,2,128,2048]{4,3,2,1,0:T(8,128)(2,1)} %copy.77), calls=%async_computation.5 | async-start | bytes 16777216 | tf_op jit(solution)/shard_map/all_to_all | solution.py:126
  607.1 155.8 %copy-start.15 = (s32[1,8,1]{1,2,0:T(1,128)S(1)}, s32[1,8,1]{1,2,0:T(1,128)}, u32[]{:S(2)}) copy-start(s32[1,8,1]{1,2,0:T(1,128)} %param.7) | copy-start | bytes 100
where the time goes:
time: 793 us; the launch traced here: 777 us
  waiting for transfers between devices  317 us (40%)
  local copies, waits for them, and re-layouts  198 us (25%)
  other arithmetic  138 us (17%)
  matrix products  87.9 us (11%)
  starting transfers between devices  34.8 us (4%)
    all_to_all x1, waiting for transfers between devices, fetch_slots(): lax.all_to_all(outgoing, 'enc', split_axis=0, concat_axis=0, tiled=True)  152 us
    all_to_all x1, waiting for transfers between devices, local(): lax.all_to_all(slot_grads.reshape(entries.shape + slot_grads.shape[1:]),...  149 us
    unnamed x4, other arithmetic  121 us
    unnamed x58, local copies, waits for them, and re-layouts  85.6 us
    all_to_all x2, waiting for transfers between devices, to_heads(): lax.all_to_all(token_major, 'seq', split_axis=2, concat_axis=1, tiled=True)  16.4 us
  transfers between devices with their start and end apart: 6, of which 3 were waited for; matrix products, arithmetic and copies ran while one was open for 29% of the time, Pallas kernels for 0%

commit v1 on v0

v1 whole, which is shorter than its diff:
```python
import functools

import jax
import jax.numpy as jnp
from jax import lax
from jax.experimental import pallas as pl
from jax.experimental.pallas import tpu as pltpu
from jax.sharding import PartitionSpec as P

DH = 128
BLOCK = 64
NBLEN = 128
CHUNKS = 2
F32 = jnp.float32
BF16 = jnp.bfloat16
VMEM_BYTES = 40 * 1024 * 1024


def partner(index, step, count):
    if count & (count - 1) == 0:
        return index ^ step
    return (step - index) % count


def exchange(array, axis, step, count):
    pairs = [(i, partner(i, step, count)) for i in range(count)]
    return lax.ppermute(array, axis, pairs)


def pack_kernel(width, chunk, chunks, count, place, q_ref, g_ref, *rest):
    outs, sems = rest[:-1], rest[-1]
    copies = []
    for h in range(chunks):
        for step in range(1, count):
            peer = partner(place[1], step, count)
            cols = pl.ds(pl.multiple_of(peer * width + h * chunk, 128), chunk)
            out = outs[h * (count - 1) + step - 1]
            for n, ref in enumerate((q_ref, g_ref)):
                copy = pltpu.make_async_copy(ref.at[0, :, cols], out.at[n], sems.at[len(copies)])
                copy.start()
                copies.append(copy)
    for copy in copies:
        copy.wait()


def pack(place, queries, grads, width, chunk, chunks, count):
    rows = queries.shape[1]
    total = chunks * (count - 1)
    anywhere = pl.BlockSpec(memory_space=pl.ANY)
    outs = pl.pallas_call(
        functools.partial(pack_kernel, width, chunk, chunks, count),
        grid_spec=pltpu.PrefetchScalarGridSpec(
            num_scalar_prefetch=1,
            grid=(1,),
            in_specs=[anywhere, anywhere],
            out_specs=[anywhere] * total,
            scratch_shapes=[pltpu.SemaphoreType.DMA((2 * total,))],
        ),
        out_shape=[jax.ShapeDtypeStruct((2, rows, chunk), BF16)] * total,
        cost_estimate=pl.CostEstimate(
            flops=0, bytes_accessed=8 * total * rows * chunk, transcendentals=0
        ),
        name="pack_rows",
    )(place, queries, grads)
    return [outs[h * (count - 1) : (h + 1) * (count - 1)] for h in range(chunks)]


def unpack_kernel(width, chunk, chunks, count, place, *rest):
    ins, (ctx_ref, gq_ref), sems = rest[: chunks * count], rest[chunks * count : -1], rest[-1]
    copies = []
    for h in range(chunks):
        for step in range(count):
            peer = partner(place[1], step, count)
            cols = pl.ds(pl.multiple_of(peer * width + h * chunk, 128), chunk)
            src = ins[h * count + step]
            for n, ref in enumerate((ctx_ref, gq_ref)):
                copy = pltpu.make_async_copy(src.at[n], ref.at[0, :, cols], sems.at[len(copies)])
                copy.start()
                copies.append(copy)
    for copy in copies:
        copy.wait()


def unpack(place, parts, shape, width, chunk, chunks, count):
    flat = [array for part in parts for array in part]
    anywhere = pl.BlockSpec(memory_space=pl.ANY)
    return pl.pallas_call(
        functools.partial(unpack_kernel, width, chunk, chunks, count),
        grid_spec=pltpu.PrefetchScalarGridSpec(
            num_scalar_prefetch=1,
            grid=(1,),
            in_specs=[anywhere] * len(flat),
            out_specs=[anywhere, anywhere],
            scratch_shapes=[pltpu.SemaphoreType.DMA((2 * len(flat),))],
        ),
        out_shape=[jax.ShapeDtypeStruct(shape, BF16)] * 2,
        cost_estimate=pl.CostEstimate(
            flops=0, bytes_accessed=8 * shape[1] * shape[2], transcendentals=0
        ),
        name="unpack_rows",
    )(place, *flat)


def dot(left, right, left_dim, right_dim):
    return lax.dot_general(
        left, right, (((left_dim,), (right_dim,)), ((), ())), preferred_element_type=F32
    )


def attend_kernel(seqs, parts, uses, place, q_ref, g_ref, kv_ref, *rest):
    rows_in, rest = rest[: parts - 1], rest[parts - 1 :]
    kv_in, rest = rest[: seqs - 1], rest[seqs - 1 :]
    rows_out, rest = rest[:parts], rest[parts:]
    kv_out, rest = rest[:seqs], rest[seqs:]
    held, rows, made, sums = rest
    scale = DH ** (-0.5)
    me, mine = place[0], place[1]

    held[me] = kv_ref[0]
    for step in range(1, seqs):
        held[partner(me, step, seqs)] = kv_in[step - 1][...]
    for n, ref in enumerate((q_ref, g_ref)):
        rows[mine, n] = pltpu.roll(ref[0].astype(F32), 1, 0)
    for step in range(1, parts):
        for n in range(2):
            piece = rows_in[step - 1][n].astype(F32)
            rows[partner(mine, step, parts), n] = pltpu.roll(piece, 1, 0)
    rows[parts] = jnp.zeros(rows.shape[1:], F32)
    made[0, :, :BLOCK] = jnp.zeros((2, BLOCK, DH), F32)
    sums[...] = jnp.zeros_like(sums)
    first_row = lax.broadcasted_iota(jnp.int32, (BLOCK, DH), 0) == 0

    def one_block(block, q, g):
        first, second = uses[2 * block], uses[2 * block + 1]
        keys = jnp.concatenate([held[first, 0], held[second, 0]], axis=0)
        values = jnp.concatenate([held[first, 1], held[second, 1]], axis=0)
        scores = dot(q, keys, 1, 1) * scale
        weights = jnp.exp(scores - jnp.max(scores, axis=1, keepdims=True))
        probs = weights / jnp.sum(weights, axis=1, keepdims=True)
        probs_low = probs.astype(BF16)
        out = dot(probs_low, values, 1, 0)
        grad_probs = dot(g, values, 1, 1)
        inner = jnp.sum(probs * grad_probs, axis=1, keepdims=True)
        grad_scores = (probs * (grad_probs - inner) * scale).astype(BF16)
        grad_q = dot(grad_scores, keys, 1, 0)
        grad_keys = dot(grad_scores, q, 0, 0)
        grad_values = dot(probs_low, g, 0, 0)
        sums[first, 0] += grad_keys[:NBLEN]
        sums[second, 0] += grad_keys[NBLEN:]
        sums[first, 1] += grad_values[:NBLEN]
        sums[second, 1] += grad_values[NBLEN:]
        return out, grad_q

    def one_part(part, carry):
        q, g = (rows[part, n, BLOCK:].astype(BF16) for n in range(2))
        for n, result in enumerate(one_block(2 * part, q, g)):
            made[part, n, BLOCK:] = result
        q, g = (
            jnp.where(first_row, rows[part, n, :BLOCK], rows[part + 1, n, :BLOCK]).astype(BF16)
            for n in range(2)
        )
        for n, result in enumerate(one_block(2 * part + 1, q, g)):
            made[part + 1, n, :BLOCK] = result
            made[part, n, :1] = result[:1]
        return carry

    if parts <= 4:
        for part in range(parts):
            one_part(part, 0)
    else:
        lax.fori_loop(0, parts, one_part, 0)

    for step in range(parts):
        for n in range(2):
            piece = made[partner(mine, step, parts), n]
            rows_out[step][n] = pltpu.roll(piece, 2 * BLOCK - 1, 0).astype(BF16)
    for step in range(seqs):
        kv_out[step][...] = sums[partner(me, step, seqs)].astype(BF16)


def attend(h, uses, place, queries, grads, kv_pool, rows_in, kv_in, chunk, seqs, parts):
    heads = chunk // DH
    width = kv_pool.shape[-1]
    blocks = uses.shape[0] // 2
    first = h * heads
    per_part = width // DH
    own_rows = pl.BlockSpec(
        (1, 2 * BLOCK, DH), lambda i, uses, place: (0, 0, place[1] * per_part + first + i)
    )
    own_kv = pl.BlockSpec(
        (1, 2, NBLEN, DH), lambda i, uses, place: (place[2], 0, 0, first + i)
    )
    rows_spec = pl.BlockSpec((2, 2 * BLOCK, DH), lambda i, uses, place: (0, 0, i))
    kv_spec = pl.BlockSpec((2, NBLEN, DH), lambda i, uses, place: (0, 0, i))
    outs = pl.pallas_call(
        functools.partial(attend_kernel, seqs, parts),
        grid_spec=pltpu.PrefetchScalarGridSpec(
            num_scalar_prefetch=2,
            grid=(heads,),
            in_specs=[own_rows, own_rows, own_kv]
            + [rows_spec] * (parts - 1)
            + [kv_spec] * (seqs - 1),
            out_specs=[rows_spec] * parts + [kv_spec] * seqs,
            scratch_shapes=[
                pltpu.VMEM((seqs, 2, NBLEN, DH), BF16),
                pltpu.VMEM((parts + 1, 2, 2 * BLOCK, DH), F32),
                pltpu.VMEM((parts + 1, 2, 2 * BLOCK, DH), F32),
                pltpu.VMEM((seqs, 2, NBLEN, DH), F32),
            ],
        ),
        out_shape=[jax.ShapeDtypeStruct((2, 2 * BLOCK, chunk), BF16)] * parts
        + [jax.ShapeDtypeStruct((2, NBLEN, chunk), BF16)] * seqs,
        compiler_params=pltpu.CompilerParams(vmem_limit_bytes=VMEM_BYTES),
        cost_estimate=pl.CostEstimate(
            flops=12 * heads * blocks * BLOCK * 2 * NBLEN * DH,
            bytes_accessed=8 * (seqs + parts) * NBLEN * chunk,
            transcendentals=heads * blocks * BLOCK * 2 * NBLEN,
        ),
        name="attend_blocks",
    )(uses, place, queries, grads, kv_pool, *rows_in, *kv_in)
    return outs[:parts], outs[parts:]


def owner_kernel(seqs, aliased, names, *rest):
    ins, out_ref, acc = rest[:seqs], rest[-2], rest[-1]
    acc[...] = jnp.zeros_like(acc)
    for step in range(seqs):
        acc[names[step]] += ins[step][...].astype(F32)
    out_ref[...] = acc[...].astype(BF16)


def owner_sum(h, names, parts, shape, so_far, chunk):
    seqs = len(parts)
    wide = min(chunk, 256)
    steps = chunk // wide
    spec = pl.BlockSpec((2, NBLEN, wide), lambda i, names: (0, 0, i))
    out_spec = pl.BlockSpec(
        (shape[0], 2, NBLEN, wide), lambda i, names: (0, 0, 0, h * steps + i)
    )
    extra = [] if so_far is None else [so_far]
    return pl.pallas_call(
        functools.partial(owner_kernel, seqs, bool(extra)),
        grid_spec=pltpu.PrefetchScalarGridSpec(
            num_scalar_prefetch=1,
            grid=(steps,),
            in_specs=[spec] * seqs + [pl.BlockSpec(memory_space=pl.ANY)] * len(extra),
            out_specs=out_spec,
            scratch_shapes=[pltpu.VMEM((shape[0], 2, NBLEN, wide), F32)],
        ),
        out_shape=jax.ShapeDtypeStruct(shape, BF16),
        input_output_aliases={seqs + 1: 0} if extra else {},
        compiler_params=pltpu.CompilerParams(vmem_limit_bytes=VMEM_BYTES),
        cost_estimate=pl.CostEstimate(
            flops=seqs * 2 * NBLEN * chunk,
            bytes_accessed=4 * (seqs + shape[0]) * NBLEN * chunk,
            transcendentals=0,
        ),
        name="owner_sum",
    )(names, *parts, *extra)


def far_first(count):
    return sorted(range(1, count), reverse=True)


def local(seqs, parts, queries, kv_pool, send_lists, block_slots, grad_context):
    width = kv_pool.shape[-1]
    chunks = min(CHUNKS, width // DH)
    chunk = width // chunks
    me, mine = lax.axis_index("enc"), lax.axis_index("seq")
    entries = send_lists[0, :, 0]
    names = jnp.stack([entries[partner(me, step, seqs)] for step in range(seqs)])
    uses = block_slots[0].reshape(-1)
    place = jnp.stack([me, mine, names[0]]).astype(jnp.int32)

    def fetch(h, source):
        got = [None] * (seqs - 1)
        for step in far_first(seqs):
            piece = lax.dynamic_slice(
                source, (names[step], 0, 0, h * chunk), (1, 2, NBLEN, chunk)
            )[0]
            got[step - 1] = exchange(piece, "enc", step, seqs)
        return got

    fetched = [fetch(0, kv_pool)]
    packed = pack(place, queries, grad_context, width, chunk, chunks, parts)
    heads = [
        [exchange(packed[h][step - 1], "seq", step, parts) for step in range(1, parts)]
        for h in range(chunks)
    ]
    pool_grads = None
    token_parts, returns = [], []
    for h in range(chunks):
        if h + 1 < chunks:
            fetched[h], source = lax.optimization_barrier((fetched[h], kv_pool))
            fetched.append(fetch(h + 1, source))
        rows_out, kv_out = attend(
            h, uses, place, queries, grad_context, kv_pool, heads[h], fetched[h], chunk, seqs, parts
        )
        returns.append(
            [kv_out[0]] + [exchange(kv_out[step], "enc", step, seqs) for step in range(1, seqs)]
        )
        token_parts.append(
            [rows_out[0]] + [exchange(rows_out[step], "seq", step, parts) for step in range(1, parts)]
        )
    context, grad_queries = unpack(
        place, token_parts, queries.shape, width, chunk, chunks, parts
    )
    for h in range(chunks):
        pool_grads = owner_sum(h, names, returns[h], kv_pool.shape, pool_grads, chunk)
    return (context, grad_queries, pool_grads)


def solution(mesh):
    in_specs = (
        P("enc", "seq", None),
        P("enc", None, None, "seq"),
        P("enc", None, None),
        P("enc", None, None),
        P("enc", "seq", None),
    )
    out_specs = (P("enc", "seq", None), P("enc", "seq", None), P("enc", None, None, "seq"))
    body = functools.partial(local, mesh.shape["enc"], mesh.shape["seq"])
    return jax.shard_map(body, mesh=mesh, in_specs=in_specs, out_specs=out_specs, check_vma=False)
```

time: 793 us -> 584 us (0.74); the launches traced: 777 us -> 578 us
  Pallas kernels: 0 us -> 312 us
  local copies, waits for them, and re-layouts: 198 us -> 28.4 us
  waiting for transfers between devices: 317 us -> 174 us
  other arithmetic: 138 us -> 1.17 us
  matrix products: 87.9 us -> 0 us
  starting transfers between devices: 34.8 us -> 49.5 us
  between operations: 1.5 us -> 13.8 us
    all_to_all x6 -> x0, waiting for transfers between devices: 317 us -> none  [the longest x1 152 us: fetch_slots(): lax.all_to_all(outgoing, 'enc', split_axis=0, concat_axis=0, tiled=True)]
    pallas_call x0 -> x6, Pallas kernels: none -> 312 us  [the longest x1 129 us: unpack(): pl.pallas_call(functools.partial(unpack_kernel, width, chunk, chunks, cou...]
    ppermute x0 -> x40, waiting for transfers between devices: none -> 174 us  [exchange(): return lax.ppermute(array, axis, pairs)]
    unnamed x4 -> x0, other arithmetic: 121 us -> none
    dot_general x17 -> x0, matrix products: 87.9 us -> none  [the longest x2 14.2 us: local(): jnp.einsum('cs,chjd->shjd', picker, value_part, preferred_element_type=jn...]
    unnamed x58 -> x61, local copies, waits for them, and re-layouts: 85.6 us -> 17.2 us
    ppermute x0 -> x40, starting transfers between devices: none -> 49.5 us  [exchange(): return lax.ppermute(array, axis, pairs)]
    all_to_all x6 -> x0, starting transfers between devices: 34.8 us -> none  [the longest x2 9.92 us: to_tokens(): lax.all_to_all(head_major, 'seq', split_axis=1, concat_axis=2, tiled=True)]
  transfers between devices with their start and end apart: 6 -> 40, of which waited for: 3 -> 14; matrix products, arithmetic and copies ran while one was open for 29% -> 1% of each run, Pallas kernels for 0% -> 53%
where the time goes in v1:
time: 584 us; the launch traced here: 578 us
  Pallas kernels  312 us (53%)
  waiting for transfers between devices  174 us (30%)
  starting transfers between devices  49.5 us (8%)
  local copies, waits for them, and re-layouts  28.4 us (5%)
  between operations  13.8 us (2%)
    ppermute x40, waiting for transfers between devices, exchange(): return lax.ppermute(array, axis, pairs)  174 us
    pallas_call x1, Pallas kernels, unpack(): pl.pallas_call(functools.partial(unpack_kernel, width, chunk, chunks, cou...  129 us
    pallas_call x1, Pallas kernels, pack(): pl.pallas_call(functools.partial(pack_kernel, width, chunk, chunks, count...  97.3 us
    pallas_call x2, Pallas kernels, attend(): pl.pallas_call(functools.partial(attend_kernel, seqs, parts), grid_spec=p...  76.6 us
    ppermute x40, starting transfers between devices, exchange(): return lax.ppermute(array, axis, pairs)  49.5 us
    unnamed x61, local copies, waits for them, and re-layouts  17.2 us
  transfers between devices with their start and end apart: 40, of which 14 were waited for; matrix products, arithmetic and copies ran while one was open for 1% of the time, Pallas kernels for 53%

profile of v1, /device:TPU:15, one launch (start us, length us, event | category | flops | bytes accessed | tf_op | source)
XLA Modules:
  0.0 578.2 jit_solution(16761637131964947271)
XLA Ops:
  0.7 1.6 constant_dynamic-slice_fusion
  15.2 4.0 dynamic-slice_bitcast_fusion.7
  19.2 1.9 collective-permute-start.9
  21.3 4.1 collective-permute-start.7
  26.2 1.2 pad_add_fusion.place
  27.4 97.3 %pack_rows.1 = (bf16[2,128,1024]{2,1,0:T(8,128)(2,1)}, bf16[2,128,1024]{2,1,0:T(8,128)(2,1)}, bf16[2,128,1024]{2,1,0:T(8,128)(2,1)}, bf16[2,128,1024]{2,1,0:T(8,...) custom-call(s32[3]{0:T(128)} %pad_add_fusion.place, bf16[1,128,8192]{2,1,0:T(8,128)(2,1)} %q_ref.5, ...), custom_call_target="tpu_custom_call" | custom-call | bytes 6291456 | tf_op jit(solution)/shard_map/pack_rows/pallas_call | solution.py:50
  127.5 2.2 collective-permute-start.2
  129.8 8.7 %collective-permute-done.4.rest_4_ = bf16[2,128,1024]{2,1,0:T(8,128)(2,1)} collective-permute-done((bf16[2,128,1024]{2,1,0:T(8,128)(2,1)}, bf16[2,128,1024]{2,1,0:T(8,128)(2,1)}, u32[]{:S(2)}, u32[]{:S(2)}) %collective-permute-start.4) | collective-permute-done | bytes 524320 | tf_op jit(solution)/shard_map/ppermute | solution.py:27
  140.8 1.2 collective-permute-start.15
  141.9 10.1 %collective-permute-done.2.rest_2_ = bf16[2,128,1024]{2,1,0:T(8,128)(2,1)} collective-permute-done((bf16[2,128,1024]{2,1,0:T(8,128)(2,1)}, bf16[2,128,1024]{2,1,0:T(8,128)(2,1)}, u32[]{:S(2)}, u32[]{:S(2)}) %collective-permute-start.2) | collective-permute-done | bytes 524320 | tf_op jit(solution)/shard_map/ppermute | solution.py:27
  152.0 1.0 copy-done.18
  153.0 1.0 copy-done.20
  154.1 38.0 %attend_blocks.2 = (bf16[2,128,1024]{2,1,0:T(8,128)(2,1)S(1)}, bf16[2,128,1024]{2,1,0:T(8,128)(2,1)S(1)}, bf16[2,128,1024]{2,1,0:T(8,128)(2,1)S(1)}, bf16[2,128,...) custom-call(s32[16]{0:T(128)S(1)} %reshape_squeeze.3.uses, ...), custom_call_target="tpu_custom_call" | custom-call | flops 1610612736 | bytes 12582912 | tf_op jit(solution)/shard_map/attend_blocks/pallas_call | solution.py:195
  192.9 1.1 collective-permute-start.10
  194.9 1.2 collective-permute-start.12
  196.1 2.2 collective-permute-start.33
  198.8 6.1 %collective-permute-done.10.rest_1_ = bf16[2,128,1024]{2,1,0:T(8,128)(2,1)S(1)} collective-permute-done((bf16[2,128,1024]{2,1,0:T(8,128)(2,1)S(1)}, bf16[2,128,1024]{2,1,0:T(8,128)(2,1)S(1)}, u32[]{:S(2)}, u32[]{:S(2)}) %collective-permute-start.10) | collective-permute-done | bytes 524320 | tf_op jit(solution)/shard_map/ppermute | solution.py:27
  205.0 5.6 collective-permute-start.22
  210.6 6.7 %collective-permute-done.12.rest_3_ = bf16[2,128,1024]{2,1,0:T(8,128)(2,1)S(1)} collective-permute-done((bf16[2,128,1024]{2,1,0:T(8,128)(2,1)S(1)}, bf16[2,128,1024]{2,1,0:T(8,128)(2,1)S(1)}, u32[]{:S(2)}, u32[]{:S(2)}) %collective-permute-start.12) | collective-permute-done | bytes 524320 | tf_op jit(solution)/shard_map/ppermute | solution.py:27
  217.2 5.2 collective-permute-start.20
  223.6 44.6 %collective-permute-done.22.rest_9_ = bf16[2,128,1024]{2,1,0:T(8,128)(2,1)S(1)} collective-permute-done((bf16[2,128,1024]{2,1,0:T(8,128)(2,1)S(1)}, bf16[2,128,1024]{2,1,0:T(8,128)(2,1)S(1)}, u32[]{:S(2)}, u32[]{:S(2)}) %collective-permute-start.22) | collective-permute-done | bytes 524320 | tf_op jit(solution)/shard_map/ppermute | solution.py:27
  268.3 10.6 %collective-permute-done.21.rest_8_ = bf16[2,128,1024]{2,1,0:T(8,128)(2,1)S(1)} collective-permute-done((bf16[2,128,1024]{2,1,0:T(8,128)(2,1)S(1)}, bf16[2,128,1024]{2,1,0:T(8,128)(2,1)S(1)}, u32[]{:S(2)}, u32[]{:S(2)}) %collective-permute-start.21) | collective-permute-done | bytes 524320 | tf_op jit(solution)/shard_map/ppermute | solution.py:27
  278.8 1.0 collective-permute-start.16
  279.9 9.9 %collective-permute-done.20.rest_7_ = bf16[2,128,1024]{2,1,0:T(8,128)(2,1)S(1)} collective-permute-done((bf16[2,128,1024]{2,1,0:T(8,128)(2,1)S(1)}, bf16[2,128,1024]{2,1,0:T(8,128)(2,1)S(1)}, u32[]{:S(2)}, u32[]{:S(2)}) %collective-permute-start.20) | collective-permute-done | bytes 524320 | tf_op jit(solution)/shard_map/ppermute | solution.py:27
  289.8 1.9 collective-permute-start.35
  291.6 8.1 %collective-permute-done.19.rest_6_ = bf16[2,128,1024]{2,1,0:T(8,128)(2,1)S(1)} collective-permute-done((bf16[2,128,1024]{2,1,0:T(8,128)(2,1)S(1)}, bf16[2,128,1024]{2,1,0:T(8,128)(2,1)S(1)}, u32[]{:S(2)}, u32[]{:S(2)}) %collective-permute-start.19) | collective-permute-done | bytes 524320 | tf_op jit(solution)/shard_map/ppermute | solution.py:27
  299.8 2.9 collective-permute-start.36
  302.7 1.8 collective-permute-start.38
  304.8 38.5 %attend_blocks.3 = (bf16[2,128,1024]{2,1,0:T(8,128)(2,1)S(1)}, bf16[2,128,1024]{2,1,0:T(8,128)(2,1)S(1)}, bf16[2,128,1024]{2,1,0:T(8,128)(2,1)S(1)}, bf16[2,128,...) custom-call(s32[16]{0:T(128)S(1)} %reshape_squeeze.3.uses, ...), custom_call_target="tpu_custom_call" | custom-call | flops 1610612736 | bytes 12582912 | tf_op jit(solution)/shard_map/attend_blocks/pallas_call | solution.py:195
  345.8 1.7 collective-permute-start.23
  347.6 11.7 %collective-permute-done.36.rest_4_ = bf16[2,128,1024]{2,1,0:T(8,128)(2,1)S(1)} collective-permute-done((bf16[2,128,1024]{2,1,0:T(8,128)(2,1)S(1)}, bf16[2,128,1024]{2,1,0:T(8,128)(2,1)S(1)}, u32[]{:S(2)}, u32[]{:S(2)}) %collective-permute-start.36) | collective-permute-done | bytes 524320 | tf_op jit(solution)/shard_map/ppermute | solution.py:27
  360.0 1.2 collective-permute-start.24
  361.2 9.3 %collective-permute-done.37.rest_5_ = bf16[2,128,1024]{2,1,0:T(8,128)(2,1)S(1)} collective-permute-done((bf16[2,128,1024]{2,1,0:T(8,128)(2,1)S(1)}, bf16[2,128,1024]{2,1,0:T(8,128)(2,1)S(1)}, u32[]{:S(2)}, u32[]{:S(2)}) %collective-permute-start.37) | collective-permute-done | bytes 524320 | tf_op jit(solution)/shard_map/ppermute | solution.py:27
  371.3 1.1 collective-permute-start.25
  372.4 10.1 %collective-permute-done.38.rest_6_ = bf16[2,128,1024]{2,1,0:T(8,128)(2,1)S(1)} collective-permute-done((bf16[2,128,1024]{2,1,0:T(8,128)(2,1)S(1)}, bf16[2,128,1024]{2,1,0:T(8,128)(2,1)S(1)}, u32[]{:S(2)}, u32[]{:S(2)}) %collective-permute-start.38) | collective-permute-done | bytes 524320 | tf_op jit(solution)/shard_map/ppermute | solution.py:27
  383.9 9.9 %collective-permute-done.39.rest_7_ = bf16[2,128,1024]{2,1,0:T(8,128)(2,1)S(1)} collective-permute-done((bf16[2,128,1024]{2,1,0:T(8,128)(2,1)S(1)}, bf16[2,128,1024]{2,1,0:T(8,128)(2,1)S(1)}, u32[]{:S(2)}, u32[]{:S(2)}) %collective-permute-start.39) | collective-permute-done | bytes 524320 | tf_op jit(solution)/shard_map/ppermute | solution.py:27
  394.6 2.0 collective-permute-start.28
  397.4 1.5 collective-permute-start.30
  399.0 1.3 collective-permute-start.31
  400.3 26.9 %collective-permute-done.27.rest_2_ = bf16[2,128,1024]{2,1,0:T(8,128)(2,1)S(1)} collective-permute-done((bf16[2,128,1024]{2,1,0:T(8,128)(2,1)S(1)}, bf16[2,128,1024]{2,1,0:T(8,128)(2,1)S(1)}, u32[]{:S(2)}, u32[]{:S(2)}) %collective-permute-start.27) | collective-permute-done | bytes 524320 | tf_op jit(solution)/shard_map/ppermute | solution.py:27
  427.2 1.9 collective-permute-start.32
  429.1 5.0 stack.15.names
  434.1 1.0 copy-done.3
  435.1 1.0 copy-done.5
  437.2 1.0 copy-done.11
  440.3 3.6 owner_sum.2.rest_8_
  443.9 129.1 %unpack_rows.1 = (bf16[1,128,8192]{2,1,0:T(8,128)(2,1)}, bf16[1,128,8192]{2,1,0:T(8,128)(2,1)}) custom-call(s32[3]{0:T(128)} %pad_add_fusion.place, bf16[2,128,1024]{2,1,0:T(8,128)(2,1)} %copy-done.1, bf16[2,128,1024]{2,1,0:T(8,128)(2,1)} %copy-done.23, bf16[2,128,1024]{2,1,0:T(8,128)(2,1)} %copy-done.24, bf16[2,128,1024]{2,1,0:T(8,128)(2,1)} %copy-done.25, ...), custom_call_target="tpu_custom_call" | custom-call | bytes 8388608 | tf_op jit(solution)/shard_map/unpack_rows/pallas_call | solution.py:87
  573.0 5.1 owner_sum.3
  (105 shorter events, 20.2 us)
Async XLA Ops:
  15.2 114.4 %copy-start.29 = (s32[1,8,2]{1,2,0:T(2,128)S(1)}, s32[1,8,2]{1,2,0:T(2,128)}, u32[]{:S(2)}) copy-start(s32[1,8,2]{1,2,0:T(2,128)} %param.8) | copy-start | bytes 196
  15.2 136.8 %copy-start = (bf16[1,128,8192]{2,1,0:T(8,128)(2,1)S(1)}, bf16[1,128,8192]{2,1,0:T(8,128)(2,1)}, u32[]{:S(2)}) copy-start(bf16[1,128,8192]{2,1,0:T(8,128)(2,1)} %q_ref.5) | copy-start | bytes 6291460
  19.2 105.5 %collective-permute-start.9 = (bf16[2,128,1024]{2,1,0:T(8,128)(2,1)}, bf16[2,128,1024]{2,1,0:T(8,128)(2,1)S(1)}, u32[]{:S(2)}, u32[]{:S(2)}) collective-permute-start(bf16[2,128,1024]{2,1,0:T(8,128)(2,1)} %get-tuple-element.90), channel_id=1, source_target_pairs={{0,28},{4,24},{8,20},{12,16},{16,12},{20,8},{24,4},{28,0},{1,29},{... | collective-permute-start | bytes 1572872 | tf_op jit(solution)/shard_map/ppermute | solution.py:27
  21.1 104.6 %collective-permute-start.8 = (bf16[2,128,1024]{2,1,0:T(8,128)(2,1)}, bf16[2,128,1024]{2,1,0:T(8,128)(2,1)S(1)}, u32[]{:S(2)}, u32[]{:S(2)}) collective-permute-start(bf16[2,128,1024]{2,1,0:T(8,128)(2,1)} %get-tuple-element.91), channel_id=1, source_target_pairs={{0,24},{4,28},{8,16},{12,20},{16,8},{20,12},{24,0},{28,4},{1,25},{... | collective-permute-start | bytes 1572872 | tf_op jit(solution)/shard_map/ppermute | solution.py:27
  21.3 105.7 %collective-permute-start.7 = (bf16[2,128,1024]{2,1,0:T(8,128)(2,1)}, bf16[2,128,1024]{2,1,0:T(8,128)(2,1)}, u32[]{:S(2)}, u32[]{:S(2)}) collective-permute-start(bf16[2,128,1024]{2,1,0:T(8,128)(2,1)} %get-tuple-element.92), channel_id=1, source_target_pairs={{0,20},{4,16},{8,28},{12,24},{16,4},{20,0},{24,12},{28,8},{1,21},{... | collective-permute-start | bytes 1572872 | tf_op jit(solution)/shard_map/ppermute | solution.py:27
  25.4 101.9 %collective-permute-start.6 = (bf16[2,128,1024]{2,1,0:T(8,128)(2,1)}, bf16[2,128,1024]{2,1,0:T(8,128)(2,1)}, u32[]{:S(2)}, u32[]{:S(2)}) collective-permute-start(bf16[2,128,1024]{2,1,0:T(8,128)(2,1)} %get-tuple-element.93), channel_id=1, source_target_pairs={{0,16},{4,20},{8,24},{12,28},{16,0},{20,4},{24,8},{28,12},{1,17},{... | collective-permute-start | bytes 1572872 | tf_op jit(solution)/shard_map/ppermute | solution.py:27
  25.4 102.0 %collective-permute-start.5 = (bf16[2,128,1024]{2,1,0:T(8,128)(2,1)}, bf16[2,128,1024]{2,1,0:T(8,128)(2,1)}, u32[]{:S(2)}, u32[]{:S(2)}) collective-permute-start(bf16[2,128,1024]{2,1,0:T(8,128)(2,1)} %get-tuple-element.94), channel_id=1, source_target_pairs={{0,12},{4,8},{8,4},{12,0},{16,28},{20,24},{24,20},{28,16},{1,13},{... | collective-permute-start | bytes 1572872 | tf_op jit(solution)/shard_map/ppermute | solution.py:27
  27.4 124.6 %copy-start.21 = (s32[3]{0:T(128)S(1)}, s32[3]{0:T(128)}, u32[]{:S(2)}) copy-start(s32[3]{0:T(128)} %pad_add_fusion.place) | copy-start | bytes 40
  124.7 13.8 %collective-permute-start.4 = (bf16[2,128,1024]{2,1,0:T(8,128)(2,1)}, bf16[2,128,1024]{2,1,0:T(8,128)(2,1)}, u32[]{:S(2)}, u32[]{:S(2)}) collective-permute-start(bf16[2,128,1024]{2,1,0:T(8,128)(2,1)} %get-tuple-element.95), channel_id=1, source_target_pairs={{0,8},{4,12},{8,0},{12,4},{16,24},{20,28},{24,16},{28,20},{1,9},{5... | collective-permute-start | bytes 1572872 | tf_op jit(solution)/shard_map/ppermute | solution.py:27
  126.5 12.2 %collective-permute-start.3 = (bf16[2,128,1024]{2,1,0:T(8,128)(2,1)}, bf16[2,128,1024]{2,1,0:T(8,128)(2,1)S(1)}, u32[]{:S(2)}, u32[]{:S(2)}) collective-permute-start(bf16[2,128,1024]{2,1,0:T(8,128)(2,1)} %get-tuple-element.96), channel_id=1, source_target_pairs={{0,4},{4,0},{8,12},{12,8},{16,20},{20,16},{24,28},{28,24},{1,5},{5... | collective-permute-start | bytes 1572872 | tf_op jit(solution)/shard_map/ppermute | solution.py:27
  126.9 13.8 %collective-permute-start = (bf16[2,128,1024]{2,1,0:T(8,128)(2,1)}, bf16[2,128,1024]{2,1,0:T(8,128)(2,1)}, u32[]{:S(2)}, u32[]{:S(2)}) collective-permute-start(bf16[2,128,1024]{2,1,0:T(8,128)(2,1)} %get-tuple-element.43), channel_id=1, source_target_pairs={{0,1},{1,0},{2,3},{3,2},{4,5},{5,4},{6,7},{7,6},{8,9},{9,8},{10,11... | collective-permute-start | bytes 1572872 | tf_op jit(solution)/shard_map/ppermute | solution.py:27
  127.2 14.7 %collective-permute-start.1 = (bf16[2,128,1024]{2,1,0:T(8,128)(2,1)}, bf16[2,128,1024]{2,1,0:T(8,128)(2,1)}, u32[]{:S(2)}, u32[]{:S(2)}) collective-permute-start(bf16[2,128,1024]{2,1,0:T(8,128)(2,1)} %get-tuple-element.44), channel_id=1, source_target_pairs={{0,2},{1,3},{2,0},{3,1},{4,6},{5,7},{6,4},{7,5},{8,10},{9,11},{10,... | collective-permute-start | bytes 1572872 | tf_op jit(solution)/shard_map/ppermute | solution.py:27
  127.5 24.5 %collective-permute-start.2 = (bf16[2,128,1024]{2,1,0:T(8,128)(2,1)}, bf16[2,128,1024]{2,1,0:T(8,128)(2,1)}, u32[]{:S(2)}, u32[]{:S(2)}) collective-permute-start(bf16[2,128,1024]{2,1,0:T(8,128)(2,1)} %get-tuple-element.45), channel_id=1, source_target_pairs={{0,3},{1,2},{2,1},{3,0},{4,7},{5,6},{6,5},{7,4},{8,11},{9,10},{10,... | collective-permute-start | bytes 1572872 | tf_op jit(solution)/shard_map/ppermute | solution.py:27
  138.5 56.4 %collective-permute-start.13 = (bf16[2,128,1024]{2,1,0:T(8,128)(2,1)}, bf16[2,128,1024]{2,1,0:T(8,128)(2,1)S(1)}, u32[]{:S(2)}, u32[]{:S(2)}) collective-permute-start(bf16[2,128,1024]{2,1,0:T(8,128)(2,1)} %get-tuple-element.57), channel_id=1, source_target_pairs={{0,1},{1,0},{2,3},{3,2},{4,5},{5,4},{6,7},{7,6},{8,9},{9,8},{10,11... | collective-permute-start | bytes 1572872 | tf_op jit(solution)/shard_map/ppermute | solution.py:27
  139.5 56.6 %collective-permute-start.14 = (bf16[2,128,1024]{2,1,0:T(8,128)(2,1)}, bf16[2,128,1024]{2,1,0:T(8,128)(2,1)S(1)}, u32[]{:S(2)}, u32[]{:S(2)}) collective-permute-start(bf16[2,128,1024]{2,1,0:T(8,128)(2,1)} %get-tuple-element.58), channel_id=1, source_target_pairs={{0,2},{1,3},{2,0},{3,1},{4,6},{5,7},{6,4},{7,5},{8,10},{9,11},{10,... | collective-permute-start | bytes 1572872 | tf_op jit(solution)/shard_map/ppermute | solution.py:27
  140.8 57.6 %collective-permute-start.15 = (bf16[2,128,1024]{2,1,0:T(8,128)(2,1)}, bf16[2,128,1024]{2,1,0:T(8,128)(2,1)S(1)}, u32[]{:S(2)}, u32[]{:S(2)}) collective-permute-start(bf16[2,128,1024]{2,1,0:T(8,128)(2,1)} %get-tuple-element.59), channel_id=1, source_target_pairs={{0,3},{1,2},{2,1},{3,0},{4,7},{5,6},{6,5},{7,4},{8,11},{9,10},{10,... | collective-permute-start | bytes 1572872 | tf_op jit(solution)/shard_map/ppermute | solution.py:27
  154.1 40.3 %copy-start.22 = (bf16[4,2,128,2048]{3,2,1,0:T(8,128)(2,1)S(1)}, bf16[4,2,128,2048]{3,2,1,0:T(8,128)(2,1)}, u32[]{:S(2)}) copy-start(bf16[4,2,128,2048]{3,2,1,0:T(8,128)(2,1)} %kv_ref.3) | copy-start | bytes 12582916
  192.9 12.0 %collective-permute-start.10 = (bf16[2,128,1024]{2,1,0:T(8,128)(2,1)S(1)}, bf16[2,128,1024]{2,1,0:T(8,128)(2,1)S(1)}, u32[]{:S(2)}, u32[]{:S(2)}) collective-permute-start(bf16[2,128,1024]{2,1,0:T(8,128)(2,1)S(1)} %get-tuple-element.54), channel_id=1, source_target_pairs={{0,1},{1,0},{2,3},{3,2},{4,5},{5,4},{6,7},{7,6},{8,9},{9,8},{10,11... | collective-permute-start | bytes 1572872 | tf_op jit(solution)/shard_map/ppermute | solution.py:27
  194.1 16.5 %collective-permute-start.11 = (bf16[2,128,1024]{2,1,0:T(8,128)(2,1)S(1)}, bf16[2,128,1024]{2,1,0:T(8,128)(2,1)S(1)}, u32[]{:S(2)}, u32[]{:S(2)}) collective-permute-start(bf16[2,128,1024]{2,1,0:T(8,128)(2,1)S(1)} %get-tuple-element.55), channel_id=1, source_target_pairs={{0,2},{1,3},{2,0},{3,1},{4,6},{5,7},{6,4},{7,5},{8,10},{9,11},{10,... | collective-permute-start | bytes 1572872 | tf_op jit(solution)/shard_map/ppermute | solution.py:27
  194.9 22.4 %collective-permute-start.12 = (bf16[2,128,1024]{2,1,0:T(8,128)(2,1)S(1)}, bf16[2,128,1024]{2,1,0:T(8,128)(2,1)S(1)}, u32[]{:S(2)}, u32[]{:S(2)}) collective-permute-start(bf16[2,128,1024]{2,1,0:T(8,128)(2,1)S(1)} %get-tuple-element.56), channel_id=1, source_target_pairs={{0,3},{1,2},{2,1},{3,0},{4,7},{5,6},{6,5},{7,4},{8,11},{9,10},{10,... | collective-permute-start | bytes 1572872 | tf_op jit(solution)/shard_map/ppermute | solution.py:27
  196.1 26.3 %collective-permute-start.33 = (bf16[2,128,1024]{2,1,0:T(8,128)(2,1)S(1)}, bf16[2,128,1024]{2,1,0:T(8,128)(2,1)S(1)}, u32[]{:S(2)}, u32[]{:S(2)}) collective-permute-start(bf16[2,128,1024]{2,1,0:T(8,128)(2,1)S(1)} %get-tuple-element.76), channel_id=1, source_target_pairs={{0,4},{4,0},{8,12},{12,8},{16,20},{20,16},{24,28},{28,24},{1,5},{5... | collective-permute-start | bytes 1572872 | tf_op jit(solution)/shard_map/ppermute | solution.py:27
  198.3 24.1 %collective-permute-start.34 = (bf16[2,128,1024]{2,1,0:T(8,128)(2,1)S(1)}, bf16[2,128,1024]{2,1,0:T(8,128)(2,1)S(1)}, u32[]{:S(2)}, u32[]{:S(2)}) collective-permute-start(bf16[2,128,1024]{2,1,0:T(8,128)(2,1)S(1)} %get-tuple-element.77), channel_id=1, source_target_pairs={{0,8},{4,12},{8,0},{12,4},{16,24},{20,28},{24,16},{28,20},{1,9},{5... | collective-permute-start | bytes 1572872 | tf_op jit(solution)/shard_map/ppermute | solution.py:27
  205.0 224.1 %copy-start.23 = (bf16[2,128,1024]{2,1,0:T(8,128)(2,1)}, bf16[2,128,1024]{2,1,0:T(8,128)(2,1)S(1)}, u32[]{:S(2)}) copy-start(bf16[2,128,1024]{2,1,0:T(8,128)(2,1)S(1)} %collective-permute-done.10.rest_1_) | copy-start | bytes 1572868
  205.0 63.3 %collective-permute-start.22 = (bf16[2,128,1024]{2,1,0:T(8,128)(2,1)S(1)}, bf16[2,128,1024]{2,1,0:T(8,128)(2,1)S(1)}, u32[]{:S(2)}, u32[]{:S(2)}) collective-permute-start(bf16[2,128,1024]{2,1,0:T(8,128)(2,1)S(1)} %get-tuple-element.83), channel_id=1, source_target_pairs={{0,28},{4,24},{8,20},{12,16},{16,12},{20,8},{24,4},{28,0},{1,29},{... | collective-permute-start | bytes 1572872 | tf_op jit(solution)/shard_map/ppermute | solution.py:27
  210.6 68.3 %collective-permute-start.21 = (bf16[2,128,1024]{2,1,0:T(8,128)(2,1)S(1)}, bf16[2,128,1024]{2,1,0:T(8,128)(2,1)S(1)}, u32[]{:S(2)}, u32[]{:S(2)}) collective-permute-start(bf16[2,128,1024]{2,1,0:T(8,128)(2,1)S(1)} %get-tuple-element.84), channel_id=1, source_target_pairs={{0,24},{4,28},{8,16},{12,20},{16,8},{20,12},{24,0},{28,4},{1,25},{... | collective-permute-start | bytes 1572872 | tf_op jit(solution)/shard_map/ppermute | solution.py:27
  217.2 87.2 %copy-start.25 = (bf16[2,128,1024]{2,1,0:T(8,128)(2,1)}, bf16[2,128,1024]{2,1,0:T(8,128)(2,1)S(1)}, u32[]{:S(2)}) copy-start(bf16[2,128,1024]{2,1,0:T(8,128)(2,1)S(1)} %collective-permute-done.12.rest_3_) | copy-start | bytes 1572868
  217.2 72.5 %collective-permute-start.20 = (bf16[2,128,1024]{2,1,0:T(8,128)(2,1)S(1)}, bf16[2,128,1024]{2,1,0:T(8,128)(2,1)S(1)}, u32[]{:S(2)}, u32[]{:S(2)}) collective-permute-start(bf16[2,128,1024]{2,1,0:T(8,128)(2,1)S(1)} %get-tuple-element.85), channel_id=1, source_target_pairs={{0,20},{4,16},{8,28},{12,24},{16,4},{20,0},{24,12},{28,8},{1,21},{... | collective-permute-start | bytes 1572872 | tf_op jit(solution)/shard_map/ppermute | solution.py:27
  222.4 77.4 %collective-permute-start.19 = (bf16[2,128,1024]{2,1,0:T(8,128)(2,1)S(1)}, bf16[2,128,1024]{2,1,0:T(8,128)(2,1)S(1)}, u32[]{:S(2)}, u32[]{:S(2)}) collective-permute-start(bf16[2,128,1024]{2,1,0:T(8,128)(2,1)S(1)} %get-tuple-element.86), channel_id=1, source_target_pairs={{0,16},{4,20},{8,24},{12,28},{16,0},{20,4},{24,8},{28,12},{1,17},{... | collective-permute-start | bytes 1572872 | tf_op jit(solution)/shard_map/ppermute | solution.py:27
  223.2 79.4 %collective-permute-start.18 = (bf16[2,128,1024]{2,1,0:T(8,128)(2,1)S(1)}, bf16[2,128,1024]{2,1,0:T(8,128)(2,1)S(1)}, u32[]{:S(2)}, u32[]{:S(2)}) collective-permute-start(bf16[2,128,1024]{2,1,0:T(8,128)(2,1)S(1)} %get-tuple-element.87), channel_id=1, source_target_pairs={{0,12},{4,8},{8,4},{12,0},{16,28},{20,24},{24,20},{28,16},{1,13},{... | collective-permute-start | bytes 1572872 | tf_op jit(solution)/shard_map/ppermute | solution.py:27
  268.3 34.4 %collective-permute-start.17 = (bf16[2,128,1024]{2,1,0:T(8,128)(2,1)S(1)}, bf16[2,128,1024]{2,1,0:T(8,128)(2,1)S(1)}, u32[]{:S(2)}, u32[]{:S(2)}) collective-permute-start(bf16[2,128,1024]{2,1,0:T(8,128)(2,1)S(1)} %get-tuple-element.88), channel_id=1, source_target_pairs={{0,8},{4,12},{8,0},{12,4},{16,24},{20,28},{24,16},{28,20},{1,9},{5... | collective-permute-start | bytes 1572872 | tf_op jit(solution)/shard_map/ppermute | solution.py:27
  278.8 25.6 %collective-permute-start.16 = (bf16[2,128,1024]{2,1,0:T(8,128)(2,1)S(1)}, bf16[2,128,1024]{2,1,0:T(8,128)(2,1)S(1)}, u32[]{:S(2)}, u32[]{:S(2)}) collective-permute-start(bf16[2,128,1024]{2,1,0:T(8,128)(2,1)S(1)} %get-tuple-element.89), channel_id=1, source_target_pairs={{0,4},{4,0},{8,12},{12,8},{16,20},{20,16},{24,28},{28,24},{1,5},{5... | collective-permute-start | bytes 1572872 | tf_op jit(solution)/shard_map/ppermute | solution.py:27
  289.8 55.2 %collective-permute-start.35 = (bf16[2,128,1024]{2,1,0:T(8,128)(2,1)S(1)}, bf16[2,128,1024]{2,1,0:T(8,128)(2,1)S(1)}, u32[]{:S(2)}, u32[]{:S(2)}) collective-permute-start(bf16[2,128,1024]{2,1,0:T(8,128)(2,1)S(1)} %get-tuple-element.78), channel_id=1, source_target_pairs={{0,12},{4,8},{8,4},{12,0},{16,28},{20,24},{24,20},{28,16},{1,13},{... | collective-permute-start | bytes 1572872 | tf_op jit(solution)/shard_map/ppermute | solution.py:27
  299.8 59.4 %collective-permute-start.36 = (bf16[2,128,1024]{2,1,0:T(8,128)(2,1)S(1)}, bf16[2,128,1024]{2,1,0:T(8,128)(2,1)S(1)}, u32[]{:S(2)}, u32[]{:S(2)}) collective-permute-start(bf16[2,128,1024]{2,1,0:T(8,128)(2,1)S(1)} %get-tuple-element.79), channel_id=1, source_target_pairs={{0,16},{4,20},{8,24},{12,28},{16,0},{20,4},{24,8},{28,12},{1,17},{... | collective-permute-start | bytes 1572872 | tf_op jit(solution)/shard_map/ppermute | solution.py:27
  302.7 67.8 %collective-permute-start.37 = (bf16[2,128,1024]{2,1,0:T(8,128)(2,1)S(1)}, bf16[2,128,1024]{2,1,0:T(8,128)(2,1)S(1)}, u32[]{:S(2)}, u32[]{:S(2)}) collective-permute-start(bf16[2,128,1024]{2,1,0:T(8,128)(2,1)S(1)} %get-tuple-element.80), channel_id=1, source_target_pairs={{0,20},{4,16},{8,28},{12,24},{16,4},{20,0},{24,12},{28,8},{1,21},{... | collective-permute-start | bytes 1572872 | tf_op jit(solution)/shard_map/ppermute | solution.py:27
  302.7 79.9 %collective-permute-start.38 = (bf16[2,128,1024]{2,1,0:T(8,128)(2,1)S(1)}, bf16[2,128,1024]{2,1,0:T(8,128)(2,1)S(1)}, u32[]{:S(2)}, u32[]{:S(2)}) collective-permute-start(bf16[2,128,1024]{2,1,0:T(8,128)(2,1)S(1)} %get-tuple-element.81), channel_id=1, source_target_pairs={{0,24},{4,28},{8,16},{12,20},{16,8},{20,12},{24,0},{28,4},{1,25},{... | collective-permute-start | bytes 1572872 | tf_op jit(solution)/shard_map/ppermute | solution.py:27
  304.4 89.3 %collective-permute-start.39 = (bf16[2,128,1024]{2,1,0:T(8,128)(2,1)S(1)}, bf16[2,128,1024]{2,1,0:T(8,128)(2,1)S(1)}, u32[]{:S(2)}, u32[]{:S(2)}) collective-permute-start(bf16[2,128,1024]{2,1,0:T(8,128)(2,1)S(1)} %get-tuple-element.82), channel_id=1, source_target_pairs={{0,28},{4,24},{8,20},{12,16},{16,12},{20,8},{24,4},{28,0},{1,29},{... | collective-permute-start | bytes 1572872 | tf_op jit(solution)/shard_map/ppermute | solution.py:27
  345.8 48.8 %collective-permute-start.23 = (bf16[2,128,1024]{2,1,0:T(8,128)(2,1)S(1)}, bf16[2,128,1024]{2,1,0:T(8,128)(2,1)S(1)}, u32[]{:S(2)}, u32[]{:S(2)}) collective-permute-start(bf16[2,128,1024]{2,1,0:T(8,128)(2,1)S(1)} %get-tuple-element.62), channel_id=1, source_target_pairs={{0,1},{1,0},{2,3},{3,2},{4,5},{5,4},{6,7},{7,6},{8,9},{9,8},{10,11... | collective-permute-start | bytes 1572872 | tf_op jit(solution)/shard_map/ppermute | solution.py:27
  360.0 36.6 %collective-permute-start.24 = (bf16[2,128,1024]{2,1,0:T(8,128)(2,1)S(1)}, bf16[2,128,1024]{2,1,0:T(8,128)(2,1)S(1)}, u32[]{:S(2)}, u32[]{:S(2)}) collective-permute-start(bf16[2,128,1024]{2,1,0:T(8,128)(2,1)S(1)} %get-tuple-element.63), channel_id=1, source_target_pairs={{0,2},{1,3},{2,0},{3,1},{4,6},{5,7},{6,4},{7,5},{8,10},{9,11},{10,... | collective-permute-start | bytes 1572872 | tf_op jit(solution)/shard_map/ppermute | solution.py:27
  371.3 26.2 %collective-permute-start.25 = (bf16[2,128,1024]{2,1,0:T(8,128)(2,1)S(1)}, bf16[2,128,1024]{2,1,0:T(8,128)(2,1)S(1)}, u32[]{:S(2)}, u32[]{:S(2)}) collective-permute-start(bf16[2,128,1024]{2,1,0:T(8,128)(2,1)S(1)} %get-tuple-element.64), channel_id=1, source_target_pairs={{0,3},{1,2},{2,1},{3,0},{4,7},{5,6},{6,5},{7,4},{8,11},{9,10},{10,... | collective-permute-start | bytes 1572872 | tf_op jit(solution)/shard_map/ppermute | solution.py:27
  383.3 15.6 %collective-permute-start.26 = (bf16[2,128,1024]{2,1,0:T(8,128)(2,1)S(1)}, bf16[2,128,1024]{2,1,0:T(8,128)(2,1)S(1)}, u32[]{:S(2)}, u32[]{:S(2)}) collective-permute-start(bf16[2,128,1024]{2,1,0:T(8,128)(2,1)S(1)} %get-tuple-element.68), channel_id=1, source_target_pairs={{0,4},{4,0},{8,12},{12,8},{16,20},{20,16},{24,28},{28,24},{1,5},{5... | collective-permute-start | bytes 1572872 | tf_op jit(solution)/shard_map/ppermute | solution.py:27
  394.6 32.6 %collective-permute-start.27 = (bf16[2,128,1024]{2,1,0:T(8,128)(2,1)S(1)}, bf16[2,128,1024]{2,1,0:T(8,128)(2,1)S(1)}, u32[]{:S(2)}, u32[]{:S(2)}) collective-permute-start(bf16[2,128,1024]{2,1,0:T(8,128)(2,1)S(1)} %get-tuple-element.69), channel_id=1, source_target_pairs={{0,8},{4,12},{8,0},{12,4},{16,24},{20,28},{24,16},{28,20},{1,9},{5... | collective-permute-start | bytes 1572872 | tf_op jit(solution)/shard_map/ppermute | solution.py:27
  394.6 34.5 %copy-start.26 = (bf16[2,128,1024]{2,1,0:T(8,128)(2,1)}, bf16[2,128,1024]{2,1,0:T(8,128)(2,1)S(1)}, u32[]{:S(2)}) copy-start(bf16[2,128,1024]{2,1,0:T(8,128)(2,1)S(1)} %collective-permute-done.23.rest_5_) | copy-start | bytes 1572868
  394.6 178.4 %collective-permute-start.28 = (bf16[2,128,1024]{2,1,0:T(8,128)(2,1)}, bf16[2,128,1024]{2,1,0:T(8,128)(2,1)S(1)}, u32[]{:S(2)}, u32[]{:S(2)}) collective-permute-start(bf16[2,128,1024]{2,1,0:T(8,128)(2,1)} %get-tuple-element.70), channel_id=1, source_target_pairs={{0,12},{4,8},{8,4},{12,0},{16,28},{20,24},{24,20},{28,16},{1,13},{... | collective-permute-start | bytes 1572872 | tf_op jit(solution)/shard_map/ppermute | solution.py:27
  396.6 176.4 %collective-permute-start.29 = (bf16[2,128,1024]{2,1,0:T(8,128)(2,1)}, bf16[2,128,1024]{2,1,0:T(8,128)(2,1)}, u32[]{:S(2)}, u32[]{:S(2)}) collective-permute-start(bf16[2,128,1024]{2,1,0:T(8,128)(2,1)} %get-tuple-element.71), channel_id=1, source_target_pairs={{0,16},{4,20},{8,24},{12,28},{16,0},{20,4},{24,8},{28,12},{1,17},{... | collective-permute-start | bytes 1572872 | tf_op jit(solution)/shard_map/ppermute | solution.py:27
  397.4 175.6 %collective-permute-start.30 = (bf16[2,128,1024]{2,1,0:T(8,128)(2,1)}, bf16[2,128,1024]{2,1,0:T(8,128)(2,1)}, u32[]{:S(2)}, u32[]{:S(2)}) collective-permute-start(bf16[2,128,1024]{2,1,0:T(8,128)(2,1)} %get-tuple-element.72), channel_id=1, source_target_pairs={{0,20},{4,16},{8,28},{12,24},{16,4},{20,0},{24,12},{28,8},{1,21},{... | collective-permute-start | bytes 1572872 | tf_op jit(solution)/shard_map/ppermute | solution.py:27
  399.0 174.0 %collective-permute-start.31 = (bf16[2,128,1024]{2,1,0:T(8,128)(2,1)}, bf16[2,128,1024]{2,1,0:T(8,128)(2,1)}, u32[]{:S(2)}, u32[]{:S(2)}) collective-permute-start(bf16[2,128,1024]{2,1,0:T(8,128)(2,1)} %get-tuple-element.73), channel_id=1, source_target_pairs={{0,24},{4,28},{8,16},{12,20},{16,8},{20,12},{24,0},{28,4},{1,25},{... | collective-permute-start | bytes 1572872 | tf_op jit(solution)/shard_map/ppermute | solution.py:27
  427.2 145.8 %collective-permute-start.32 = (bf16[2,128,1024]{2,1,0:T(8,128)(2,1)}, bf16[2,128,1024]{2,1,0:T(8,128)(2,1)}, u32[]{:S(2)}, u32[]{:S(2)}) collective-permute-start(bf16[2,128,1024]{2,1,0:T(8,128)(2,1)} %get-tuple-element.74), channel_id=1, source_target_pairs={{0,28},{4,24},{8,20},{12,16},{16,12},{20,8},{24,4},{28,0},{1,29},{... | collective-permute-start | bytes 1572872 | tf_op jit(solution)/shard_map/ppermute | solution.py:27
  443.9 129.2 %copy-start.7 = (bf16[2,128,1024]{2,1,0:T(8,128)(2,1)S(1)}, bf16[2,128,1024]{2,1,0:T(8,128)(2,1)}, u32[]{:S(2)}) copy-start(bf16[2,128,1024]{2,1,0:T(8,128)(2,1)} %copy-done.6) | copy-start | bytes 1572868
  (22 other events, 93.1 us)

commit v2 on v1

--- a/solution.py
+++ b/solution.py
@@ -53,10 +53,11 @@
             num_scalar_prefetch=1,
             grid=(1,),
             in_specs=[anywhere, anywhere],
-            out_specs=[anywhere] * total,
+            out_specs=[pl.BlockSpec((2, rows, chunk), lambda i, place: (0, 0, 0))] * total,
             scratch_shapes=[pltpu.SemaphoreType.DMA((2 * total,))],
         ),
         out_shape=[jax.ShapeDtypeStruct((2, rows, chunk), BF16)] * total,
+        compiler_params=pltpu.CompilerParams(vmem_limit_bytes=VMEM_BYTES),
         cost_estimate=pl.CostEstimate(
             flops=0, bytes_accessed=8 * total * rows * chunk, transcendentals=0
         ),
@@ -89,11 +90,12 @@
         grid_spec=pltpu.PrefetchScalarGridSpec(
             num_scalar_prefetch=1,
             grid=(1,),
-            in_specs=[anywhere] * len(flat),
+            in_specs=[pl.BlockSpec(array.shape, lambda i, place: (0, 0, 0)) for array in flat],
             out_specs=[anywhere, anywhere],
             scratch_shapes=[pltpu.SemaphoreType.DMA((2 * len(flat),))],
         ),
         out_shape=[jax.ShapeDtypeStruct(shape, BF16)] * 2,
+        compiler_params=pltpu.CompilerParams(vmem_limit_bytes=VMEM_BYTES),
         cost_estimate=pl.CostEstimate(
             flops=0, bytes_accessed=8 * shape[1] * shape[2], transcendentals=0
         ),
@@ -107,18 +109,13 @@
     )
 
 
-def attend_kernel(seqs, parts, uses, place, q_ref, g_ref, kv_ref, *rest):
+def attend_kernel(seqs, parts, uses, place, q_ref, g_ref, held, *rest):
     rows_in, rest = rest[: parts - 1], rest[parts - 1 :]
-    kv_in, rest = rest[: seqs - 1], rest[seqs - 1 :]
     rows_out, rest = rest[:parts], rest[parts:]
-    kv_out, rest = rest[:seqs], rest[seqs:]
-    held, rows, made, sums = rest
+    kv_out, rows, made, sums = rest
     scale = DH ** (-0.5)
-    me, mine = place[0], place[1]
-
-    held[me] = kv_ref[0]
-    for step in range(1, seqs):
-        held[partner(me, step, seqs)] = kv_in[step - 1][...]
+    mine = place[1]
+
     for n, ref in enumerate((q_ref, g_ref)):
         rows[mine, n] = pltpu.roll(ref[0].astype(F32), 1, 0)
     for step in range(1, parts):
@@ -174,42 +171,34 @@
         for n in range(2):
             piece = made[partner(mine, step, parts), n]
             rows_out[step][n] = pltpu.roll(piece, 2 * BLOCK - 1, 0).astype(BF16)
-    for step in range(seqs):
-        kv_out[step][...] = sums[partner(me, step, seqs)].astype(BF16)
-
-
-def attend(h, uses, place, queries, grads, kv_pool, rows_in, kv_in, chunk, seqs, parts):
+    kv_out[...] = sums[...].astype(BF16)
+
+
+def attend(h, uses, place, queries, grads, rows_in, kv_in, width, chunk, seqs, parts):
     heads = chunk // DH
-    width = kv_pool.shape[-1]
     blocks = uses.shape[0] // 2
     first = h * heads
     per_part = width // DH
     own_rows = pl.BlockSpec(
         (1, 2 * BLOCK, DH), lambda i, uses, place: (0, 0, place[1] * per_part + first + i)
     )
-    own_kv = pl.BlockSpec(
-        (1, 2, NBLEN, DH), lambda i, uses, place: (place[2], 0, 0, first + i)
-    )
     rows_spec = pl.BlockSpec((2, 2 * BLOCK, DH), lambda i, uses, place: (0, 0, i))
-    kv_spec = pl.BlockSpec((2, NBLEN, DH), lambda i, uses, place: (0, 0, i))
+    kv_spec = pl.BlockSpec((seqs, 2, NBLEN, DH), lambda i, uses, place: (0, 0, 0, i))
     outs = pl.pallas_call(
         functools.partial(attend_kernel, seqs, parts),
         grid_spec=pltpu.PrefetchScalarGridSpec(
             num_scalar_prefetch=2,
             grid=(heads,),
-            in_specs=[own_rows, own_rows, own_kv]
-            + [rows_spec] * (parts - 1)
-            + [kv_spec] * (seqs - 1),
-            out_specs=[rows_spec] * parts + [kv_spec] * seqs,
+            in_specs=[own_rows, own_rows, kv_spec] + [rows_spec] * (parts - 1),
+            out_specs=[rows_spec] * parts + [kv_spec],
             scratch_shapes=[
-                pltpu.VMEM((seqs, 2, NBLEN, DH), BF16),
                 pltpu.VMEM((parts + 1, 2, 2 * BLOCK, DH), F32),
                 pltpu.VMEM((parts + 1, 2, 2 * BLOCK, DH), F32),
                 pltpu.VMEM((seqs, 2, NBLEN, DH), F32),
             ],
         ),
         out_shape=[jax.ShapeDtypeStruct((2, 2 * BLOCK, chunk), BF16)] * parts
-        + [jax.ShapeDtypeStruct((2, NBLEN, chunk), BF16)] * seqs,
+        + [jax.ShapeDtypeStruct((seqs, 2, NBLEN, chunk), BF16)],
         compiler_params=pltpu.CompilerParams(vmem_limit_bytes=VMEM_BYTES),
         cost_estimate=pl.CostEstimate(
             flops=12 * heads * blocks * BLOCK * 2 * NBLEN * DH,
@@ -217,38 +206,38 @@
             transcendentals=heads * blocks * BLOCK * 2 * NBLEN,
         ),
         name="attend_blocks",
-    )(uses, place, queries, grads, kv_pool, *rows_in, *kv_in)
-    return outs[:parts], outs[parts:]
-
-
-def owner_kernel(seqs, aliased, names, *rest):
-    ins, out_ref, acc = rest[:seqs], rest[-2], rest[-1]
+    )(uses, place, queries, grads, kv_in, *rows_in)
+    return outs[:parts], outs[parts]
+
+
+def owner_kernel(seqs, names, back_ref, *rest):
+    out_ref, acc = rest[-2], rest[-1]
     acc[...] = jnp.zeros_like(acc)
-    for step in range(seqs):
-        acc[names[step]] += ins[step][...].astype(F32)
+    for seq in range(seqs):
+        acc[names[seq]] += back_ref[seq].astype(F32)
     out_ref[...] = acc[...].astype(BF16)
 
 
-def owner_sum(h, names, parts, shape, so_far, chunk):
-    seqs = len(parts)
+def owner_sum(h, names, back, shape, so_far, chunk):
+    seqs = back.shape[0]
     wide = min(chunk, 256)
     steps = chunk // wide
-    spec = pl.BlockSpec((2, NBLEN, wide), lambda i, names: (0, 0, i))
+    spec = pl.BlockSpec((seqs, 2, NBLEN, wide), lambda i, names: (0, 0, 0, i))
     out_spec = pl.BlockSpec(
         (shape[0], 2, NBLEN, wide), lambda i, names: (0, 0, 0, h * steps + i)
     )
     extra = [] if so_far is None else [so_far]
     return pl.pallas_call(
-        functools.partial(owner_kernel, seqs, bool(extra)),
+        functools.partial(owner_kernel, seqs),
         grid_spec=pltpu.PrefetchScalarGridSpec(
             num_scalar_prefetch=1,
             grid=(steps,),
-            in_specs=[spec] * seqs + [pl.BlockSpec(memory_space=pl.ANY)] * len(extra),
+            in_specs=[spec] + [pl.BlockSpec(memory_space=pl.ANY)] * len(extra),
             out_specs=out_spec,
             scratch_shapes=[pltpu.VMEM((shape[0], 2, NBLEN, wide), F32)],
         ),
         out_shape=jax.ShapeDtypeStruct(shape, BF16),
-        input_output_aliases={seqs + 1: 0} if extra else {},
+        input_output_aliases={2: 0} if extra else {},
         compiler_params=pltpu.CompilerParams(vmem_limit_bytes=VMEM_BYTES),
         cost_estimate=pl.CostEstimate(
             flops=seqs * 2 * NBLEN * chunk,
@@ -256,33 +245,48 @@
             transcendentals=0,
         ),
         name="owner_sum",
-    )(names, *parts, *extra)
-
-
-def far_first(count):
-    return sorted(range(1, count), reverse=True)
+    )(names, back, *extra)
+
+
+def pick_kernel(names, pool_ref, out_ref):
+    out_ref[...] = pool_ref[...]
+
+
+def pick(h, names, kv_pool, chunk):
+    seqs = names.shape[0]
+    return pl.pallas_call(
+        pick_kernel,
+        grid_spec=pltpu.PrefetchScalarGridSpec(
+            num_scalar_prefetch=1,
+            grid=(seqs,),
+            in_specs=[
+                pl.BlockSpec((1, 2, NBLEN, chunk), lambda i, names: (names[i], 0, 0, h))
+            ],
+            out_specs=pl.BlockSpec((1, 2, NBLEN, chunk), lambda i, names: (i, 0, 0, 0)),
+        ),
+        out_shape=jax.ShapeDtypeStruct((seqs, 2, NBLEN, chunk), BF16),
+        compiler_params=pltpu.CompilerParams(vmem_limit_bytes=VMEM_BYTES),
+        cost_estimate=pl.CostEstimate(
+            flops=0, bytes_accessed=8 * seqs * NBLEN * chunk, transcendentals=0
+        ),
+        name="pick_entries",
+    )(names, kv_pool)
+
+
+def swap(array):
+    return lax.all_to_all(array, "enc", split_axis=0, concat_axis=0, tiled=True)
 
 
 def local(seqs, parts, queries, kv_pool, send_lists, block_slots, grad_context):
     width = kv_pool.shape[-1]
     chunks = min(CHUNKS, width // DH)
     chunk = width // chunks
-    me, mine = lax.axis_index("enc"), lax.axis_index("seq")
-    entries = send_lists[0, :, 0]
-    names = jnp.stack([entries[partner(me, step, seqs)] for step in range(seqs)])
-    uses = block_slots[0].reshape(-1)
-    place = jnp.stack([me, mine, names[0]]).astype(jnp.int32)
-
-    def fetch(h, source):
-        got = [None] * (seqs - 1)
-        for step in far_first(seqs):
-            piece = lax.dynamic_slice(
-                source, (names[step], 0, 0, h * chunk), (1, 2, NBLEN, chunk)
-            )[0]
-            got[step - 1] = exchange(piece, "enc", step, seqs)
-        return got
-
-    fetched = [fetch(0, kv_pool)]
+    mine = lax.axis_index("seq")
+    names = send_lists.reshape(-1)
+    uses = block_slots.reshape(-1)
+    place = jnp.stack([mine, mine]).astype(jnp.int32)
+
+    fetched = [swap(pick(h, names, kv_pool, chunk)) for h in range(chunks)]
     packed = pack(place, queries, grad_context, width, chunk, chunks, parts)
     heads = [
         [exchange(packed[h][step - 1], "seq", step, parts) for step in range(1, parts)]
@@ -291,15 +295,10 @@
     pool_grads = None
     token_parts, returns = [], []
     for h in range(chunks):
-        if h + 1 < chunks:
-            fetched[h], source = lax.optimization_barrier((fetched[h], kv_pool))
-            fetched.append(fetch(h + 1, source))
         rows_out, kv_out = attend(
-            h, uses, place, queries, grad_context, kv_pool, heads[h], fetched[h], chunk, seqs, parts
+            h, uses, place, queries, grad_context, heads[h], fetched[h], width, chunk, seqs, parts
         )
-        returns.append(
-            [kv_out[0]] + [exchange(kv_out[step], "enc", step, seqs) for step in range(1, seqs)]
-        )
+        returns.append(swap(kv_out))
         token_parts.append(
             [rows_out[0]] + [exchange(rows_out[step], "seq", step, parts) for step in range(1, parts)]
         )

time: 584 us -> 410 us (0.70)
  Pallas kernels: 312 us -> 91.9 us
  waiting for transfers between devices: 174 us -> 245 us
  between operations: 13.8 us -> 0.77 us
  starting transfers between devices: 49.5 us -> 39.1 us
    all_to_all x0 -> x4, waiting for transfers between devices: none -> 159 us  [swap(): return lax.all_to_all(array, 'enc', split_axis=0, concat_axis=0, tiled=True)]
    pallas_call x1, Pallas kernels: 129 us -> 2.67 us  [unpack(): pl.pallas_call(functools.partial(unpack_kernel, width, chunk, chunks, cou...]
    pallas_call x1, Pallas kernels: 97.3 us -> 2.06 us  [pack(): pl.pallas_call(functools.partial(pack_kernel, width, chunk, chunks, count...]
    ppermute x40 -> x12, waiting for transfers between devices: 174 us -> 86.8 us  [exchange(): return lax.ppermute(array, axis, pairs)]
    ppermute x40 -> x12, starting transfers between devices: 49.5 us -> 8.62 us  [exchange(): return lax.ppermute(array, axis, pairs)]
    all_to_all x0 -> x4, starting transfers between devices: none -> 30.5 us  [swap(): return lax.all_to_all(array, 'enc', split_axis=0, concat_axis=0, tiled=True)]
    unnamed x61 -> x59, local copies, waits for them, and re-layouts: 17.2 us -> 27 us
    pallas_call x2 -> x4, Pallas kernels: 8.69 us -> 13 us  [the longest x2 10.6 us: owner_sum(): pl.pallas_call(functools.partial(owner_kernel, seqs), grid_spec=pltpu.Pre...]
  transfers between devices with their start and end apart: 40 -> 16, of which waited for: 14 -> 12; matrix products, arithmetic and copies ran while one was open for 1% -> 0% of each run, Pallas kernels for 53% -> 21%
where the time goes in v2:
time: 410 us; the launch traced here: 404 us
  waiting for transfers between devices  245 us (60%)
  Pallas kernels  91.9 us (22%)
  starting transfers between devices  39.1 us (10%)
  local copies, waits for them, and re-layouts  27 us (7%)
    all_to_all x4, waiting for transfers between devices, swap(): return lax.all_to_all(array, 'enc', split_axis=0, concat_axis=0, tiled=True)  159 us
    ppermute x12, waiting for transfers between devices, exchange(): return lax.ppermute(array, axis, pairs)  86.8 us
    pallas_call x2, Pallas kernels, attend(): pl.pallas_call(functools.partial(attend_kernel, seqs, parts), grid_spec=p...  74.2 us
    all_to_all x4, starting transfers between devices, swap(): return lax.all_to_all(array, 'enc', split_axis=0, concat_axis=0, tiled=True)  30.5 us
    unnamed x59, local copies, waits for them, and re-layouts  27 us
    pallas_call x2, Pallas kernels, owner_sum(): pl.pallas_call(functools.partial(owner_kernel, seqs), grid_spec=pltpu.Pre...  10.6 us
    ppermute x12, starting transfers between devices, exchange(): return lax.ppermute(array, axis, pairs)  8.62 us
  transfers between devices with their start and end apart: 16, of which 12 were waited for; matrix products, arithmetic and copies ran while one was open for 0% of the time, Pallas kernels for 21%

profile of v2, /device:TPU:15, one launch (start us, length us, event | category | flops | bytes accessed | tf_op | source)
XLA Modules:
  0.0 404.3 jit_solution(3822165434142011812)
XLA Ops:
  0.6 2.2 copy-done.4
  2.8 0.7 copy-done.12
  3.5 1.2 pick_entries.2
  4.7 2.0 copy-done.7
  6.7 5.9 %all-to-all-start = ((bf16[8,2,128,1024]{3,2,1,0:T(8,128)(2,1)}), bf16[8,2,128,1024]{3,2,1,0:T(8,128)(2,1)}, u32[]{:S(2)}, u32[]{:S(2)}) async-start(bf16[8,2,128,1024]{3,2,1,0:T(8,128)(2,1)} %copy-done.7), calls=%async_computation | async-start | bytes 8388608 | tf_op jit(solution)/shard_map/all_to_all | solution.py:277
  12.6 2.2 copy-done.5
  14.8 1.2 pick_entries.3
  16.0 2.0 copy-done.6
  17.9 85.1 %all-to-all-done.held = bf16[8,2,128,1024]{3,2,1,0:T(8,128)(2,1)} async-done(((bf16[8,2,128,1024]{3,2,1,0:T(8,128)(2,1)}), bf16[8,2,128,1024]{3,2,1,0:T(8,128)(2,1)}, u32[]{:S(2)}, u32[]{:S(2)}) %all-to-all-start) | async-done | bytes 4194336 | tf_op jit(solution)/shard_map/all_to_all | solution.py:277
  103.0 8.1 %all-to-all-start.1 = ((bf16[8,2,128,1024]{3,2,1,0:T(8,128)(2,1)}), bf16[8,2,128,1024]{3,2,1,0:T(8,128)(2,1)}, u32[]{:S(2)}, u32[]{:S(2)}) async-start(bf16[8,2,128,1024]{3,2,1,0:T(8,128)(2,1)} %copy-done.6), calls=%async_computation.1 | async-start | bytes 8388608 | tf_op jit(solution)/shard_map/all_to_all | solution.py:277
  111.2 1.6 copy-done.1
  112.8 2.1 pack_rows.1
  114.9 0.8 copy-done.20
  115.7 0.8 copy-done.22
  116.5 0.8 copy-done.23
  117.8 2.2 collective-permute-start.2
  120.1 10.5 %collective-permute-done.rest_0_ = bf16[2,128,1024]{2,1,0:T(8,128)(2,1)S(1)} collective-permute-done((bf16[2,128,1024]{2,1,0:T(8,128)(2,1)}, bf16[2,128,1024]{2,1,0:T(8,128)(2,1)S(1)}, u32[]{:S(2)}, u32[]{:S(2)}) %collective-permute-start) | collective-permute-done | bytes 524320 | tf_op jit(solution)/shard_map/ppermute | solution.py:27
  130.7 0.8 copy-done.10
  131.4 10.5 %collective-permute-done.2.rest_2_ = bf16[2,128,1024]{2,1,0:T(8,128)(2,1)} collective-permute-done((bf16[2,128,1024]{2,1,0:T(8,128)(2,1)}, bf16[2,128,1024]{2,1,0:T(8,128)(2,1)}, u32[]{:S(2)}, u32[]{:S(2)}) %collective-permute-start.2) | collective-permute-done | bytes 524320 | tf_op jit(solution)/shard_map/ppermute | solution.py:27
  142.0 1.6 copy-done.2
  143.6 1.0 copy-done.11
  144.6 37.1 %attend_blocks.2 = (bf16[2,128,1024]{2,1,0:T(8,128)(2,1)S(1)}, bf16[2,128,1024]{2,1,0:T(8,128)(2,1)S(1)}, bf16[2,128,1024]{2,1,0:T(8,128)(2,1)S(1)}, bf16[2,128,...) custom-call(s32[16]{0:T(128)S(1)} %reshape.12.uses, s32[2]{0:T(128)S(1)} %pad_add_fusion.place, ...), custom_call_target="tpu_custom_call" | custom-call | flops 1610612736 | bytes 12582912 | tf_op jit(solution)/shard_map/attend_blocks/pallas_call | solution.py:187
  181.7 2.0 copy-done.9
  183.7 0.8 copy-done.14
  184.5 0.8 copy-done.16
  185.3 0.8 copy-done.18
  186.1 15.5 %all-to-all-done.1.held = bf16[8,2,128,1024]{3,2,1,0:T(8,128)(2,1)} async-done(((bf16[8,2,128,1024]{3,2,1,0:T(8,128)(2,1)}), bf16[8,2,128,1024]{3,2,1,0:T(8,128)(2,1)}, u32[]{:S(2)}, u32[]{:S(2)}) %all-to-all-start.1) | async-done | bytes 4194336 | tf_op jit(solution)/shard_map/all_to_all | solution.py:277
  201.6 8.2 %all-to-all-start.3 = ((bf16[8,2,128,1024]{3,2,1,0:T(8,128)(2,1)}), bf16[8,2,128,1024]{3,2,1,0:T(8,128)(2,1)}, u32[]{:S(2)}, u32[]{:S(2)}) async-start(bf16[8,2,128,1024]{3,2,1,0:T(8,128)(2,1)} %copy-done.9), calls=%async_computation.3 | async-start | bytes 8388608 | tf_op jit(solution)/shard_map/all_to_all | solution.py:277
  210.3 2.2 collective-permute-start.8
  212.5 10.8 %collective-permute-done.6.rest_0_ = bf16[2,128,1024]{2,1,0:T(8,128)(2,1)S(1)} collective-permute-done((bf16[2,128,1024]{2,1,0:T(8,128)(2,1)}, bf16[2,128,1024]{2,1,0:T(8,128)(2,1)S(1)}, u32[]{:S(2)}, u32[]{:S(2)}) %collective-permute-start.6) | collective-permute-done | bytes 524320 | tf_op jit(solution)/shard_map/ppermute | solution.py:27
  223.3 11.1 %collective-permute-done.8.rest_2_ = bf16[2,128,1024]{2,1,0:T(8,128)(2,1)S(1)} collective-permute-done((bf16[2,128,1024]{2,1,0:T(8,128)(2,1)S(1)}, bf16[2,128,1024]{2,1,0:T(8,128)(2,1)S(1)}, u32[]{:S(2)}, u32[]{:S(2)}) %collective-permute-start.8) | collective-permute-done | bytes 524320 | tf_op jit(solution)/shard_map/ppermute | solution.py:27
  234.4 1.6 copy-done.3
  236.0 37.2 %attend_blocks.3 = (bf16[2,128,1024]{2,1,0:T(8,128)(2,1)S(1)}, bf16[2,128,1024]{2,1,0:T(8,128)(2,1)S(1)}, bf16[2,128,1024]{2,1,0:T(8,128)(2,1)S(1)}, bf16[2,128,...) custom-call(s32[16]{0:T(128)S(1)} %reshape.12.uses, s32[2]{0:T(128)S(1)} %pad_add_fusion.place, ...), custom_call_target="tpu_custom_call" | custom-call | flops 1610612736 | bytes 12582912 | tf_op jit(solution)/shard_map/attend_blocks/pallas_call | solution.py:187
  273.2 2.0 copy-done.8
  275.2 0.8 copy-done.24
  276.0 0.8 copy-done.26
  276.8 0.8 copy-done.27
  277.6 22.7 %all-to-all-done.3.back_ref = bf16[8,2,128,1024]{3,2,1,0:T(8,128)(2,1)} async-done(((bf16[8,2,128,1024]{3,2,1,0:T(8,128)(2,1)}), bf16[8,2,128,1024]{3,2,1,0:T(8,128)(2,1)}, u32[]{:S(2)}, u32[]{:S(2)}) %all-to-all-start.3) | async-done | bytes 4194336 | tf_op jit(solution)/shard_map/all_to_all | solution.py:277
  300.3 8.3 %all-to-all-start.2 = ((bf16[8,2,128,1024]{3,2,1,0:T(8,128)(2,1)}), bf16[8,2,128,1024]{3,2,1,0:T(8,128)(2,1)}, u32[]{:S(2)}, u32[]{:S(2)}) async-start(bf16[8,2,128,1024]{3,2,1,0:T(8,128)(2,1)} %copy-done.8), calls=%async_computation.2 | async-start | bytes 8388608 | tf_op jit(solution)/shard_map/all_to_all | solution.py:277
  309.1 2.2 collective-permute-start.11
  311.7 10.3 %collective-permute-done.9.rest_5_ = bf16[2,128,1024]{2,1,0:T(8,128)(2,1)S(1)} collective-permute-done((bf16[2,128,1024]{2,1,0:T(8,128)(2,1)}, bf16[2,128,1024]{2,1,0:T(8,128)(2,1)S(1)}, u32[]{:S(2)}, u32[]{:S(2)}) %collective-permute-start.9) | collective-permute-done | bytes 524320 | tf_op jit(solution)/shard_map/ppermute | solution.py:27
  322.2 10.9 %collective-permute-done.11.rest_7_ = bf16[2,128,1024]{2,1,0:T(8,128)(2,1)S(1)} collective-permute-done((bf16[2,128,1024]{2,1,0:T(8,128)(2,1)S(1)}, bf16[2,128,1024]{2,1,0:T(8,128)(2,1)S(1)}, u32[]{:S(2)}, u32[]{:S(2)}) %collective-permute-start.11) | collective-permute-done | bytes 524320 | tf_op jit(solution)/shard_map/ppermute | solution.py:27
  333.2 11.4 %collective-permute-done.3.rest_1_ = bf16[2,128,1024]{2,1,0:T(8,128)(2,1)S(1)} collective-permute-done((bf16[2,128,1024]{2,1,0:T(8,128)(2,1)S(1)}, bf16[2,128,1024]{2,1,0:T(8,128)(2,1)S(1)}, u32[]{:S(2)}, u32[]{:S(2)}) %collective-permute-start.3) | collective-permute-done | bytes 524320 | tf_op jit(solution)/shard_map/ppermute | solution.py:27
  344.5 11.1 %collective-permute-done.5.rest_3_ = bf16[2,128,1024]{2,1,0:T(8,128)(2,1)S(1)} collective-permute-done((bf16[2,128,1024]{2,1,0:T(8,128)(2,1)S(1)}, bf16[2,128,1024]{2,1,0:T(8,128)(2,1)S(1)}, u32[]{:S(2)}, u32[]{:S(2)}) %collective-permute-start.5) | collective-permute-done | bytes 524320 | tf_op jit(solution)/shard_map/ppermute | solution.py:27
  355.7 2.7 unpack_rows.1
  358.3 5.3 %owner_sum.2.rest_0_ = bf16[4,2,128,2048]{3,2,1,0:T(8,128)(2,1)} custom-call(s32[8]{0:T(128)S(1)} %bitcast.4, bf16[8,2,128,1024]{3,2,1,0:T(8,128)(2,1)} %all-to-all-done.3.back_ref), custom_call_target="tpu_custom_call" | custom-call | flops 2097152 | bytes 6291456 | tf_op jit(solution)/shard_map/owner_sum/pallas_call | solution.py:230
  363.6 35.4 %all-to-all-done.2.back_ref = bf16[8,2,128,1024]{3,2,1,0:T(8,128)(2,1)} async-done(((bf16[8,2,128,1024]{3,2,1,0:T(8,128)(2,1)}), bf16[8,2,128,1024]{3,2,1,0:T(8,128)(2,1)}, u32[]{:S(2)}, u32[]{:S(2)}) %all-to-all-start.2) | async-done | bytes 4194336 | tf_op jit(solution)/shard_map/all_to_all | solution.py:277
  399.0 5.3 %owner_sum.3 = bf16[4,2,128,2048]{3,2,1,0:T(8,128)(2,1)} custom-call(s32[8]{0:T(128)S(1)} %bitcast.5, bf16[8,2,128,1024]{3,2,1,0:T(8,128)(2,1)} %all-to-all-done.2.back_ref, bf16[4,2,128,2048]{3,2,1,0:T(8,128)(2,1)} %owner_sum.2.rest_0_), custom_call_target="tpu_custom_call", output_to_operand_aliasing={{}: (2, {})} | custom-call | flops 2097152 | bytes 6291456 | tf_op jit(solution)/shard_map/owner_sum/pallas_call | solution.py:230
  (53 shorter events, 2.4 us)
Async XLA Ops:
  0.6 2.2 copy-start.4
  2.8 0.7 copy-start.12
  4.7 2.0 copy-start.7
  6.7 5.9 %copy-start.13 = (s32[1,8,1]{1,2,0:T(1,128)S(1)}, s32[1,8,1]{1,2,0:T(1,128)}, u32[]{:S(2)}) copy-start(s32[1,8,1]{1,2,0:T(1,128)} %param.7) | copy-start | bytes 100
  6.7 96.3 %all-to-all-start = ((bf16[8,2,128,1024]{3,2,1,0:T(8,128)(2,1)}), bf16[8,2,128,1024]{3,2,1,0:T(8,128)(2,1)}, u32[]{:S(2)}, u32[]{:S(2)}) async-start(bf16[8,2,128,1024]{3,2,1,0:T(8,128)(2,1)} %copy-done.7), calls=%async_computation | async-start | bytes 8388608 | tf_op jit(solution)/shard_map/all_to_all | solution.py:277
  12.6 2.2 copy-start.5
  16.0 2.0 copy-start.6
  17.9 93.3 %copy-start = (bf16[1,128,8192]{2,1,0:T(8,128)(2,1)S(1)}, bf16[1,128,8192]{2,1,0:T(8,128)(2,1)}, u32[]{:S(2)}) copy-start(bf16[1,128,8192]{2,1,0:T(8,128)(2,1)} %q_ref.5) | copy-start | bytes 6291460
  103.0 98.5 %all-to-all-start.1 = ((bf16[8,2,128,1024]{3,2,1,0:T(8,128)(2,1)}), bf16[8,2,128,1024]{3,2,1,0:T(8,128)(2,1)}, u32[]{:S(2)}, u32[]{:S(2)}) async-start(bf16[8,2,128,1024]{3,2,1,0:T(8,128)(2,1)} %copy-done.6), calls=%async_computation.1 | async-start | bytes 8388608 | tf_op jit(solution)/shard_map/all_to_all | solution.py:277
  111.1 8.8 %copy-start.28 = (s32[1,8,2]{1,2,0:T(2,128)S(1)}, s32[1,8,2]{1,2,0:T(2,128)}, u32[]{:S(2)}) copy-start(s32[1,8,2]{1,2,0:T(2,128)} %param.8) | copy-start | bytes 196
  111.2 1.6 copy-start.1
  114.9 0.8 copy-start.20
  115.7 0.8 copy-start.22
  116.5 0.8 copy-start.23
  117.3 13.4 %collective-permute-start = (bf16[2,128,1024]{2,1,0:T(8,128)(2,1)}, bf16[2,128,1024]{2,1,0:T(8,128)(2,1)S(1)}, u32[]{:S(2)}, u32[]{:S(2)}) collective-permute-start(bf16[2,128,1024]{2,1,0:T(8,128)(2,1)} %get-tuple-element.21), channel_id=1, source_target_pairs={{0,1},{1,0},{2,3},{3,2},{4,5},{5,4},{6,7},{7,6},{8,9},{9,8},{10,11... | collective-permute-start | bytes 1572872 | tf_op jit(solution)/shard_map/ppermute | solution.py:27
  117.5 13.1 %collective-permute-start.1 = (bf16[2,128,1024]{2,1,0:T(8,128)(2,1)}, bf16[2,128,1024]{2,1,0:T(8,128)(2,1)S(1)}, u32[]{:S(2)}, u32[]{:S(2)}) collective-permute-start(bf16[2,128,1024]{2,1,0:T(8,128)(2,1)} %get-tuple-element.22), channel_id=1, source_target_pairs={{0,2},{1,3},{2,0},{3,1},{4,6},{5,7},{6,4},{7,5},{8,10},{9,11},{10,... | collective-permute-start | bytes 1572872 | tf_op jit(solution)/shard_map/ppermute | solution.py:27
  117.8 24.2 %collective-permute-start.2 = (bf16[2,128,1024]{2,1,0:T(8,128)(2,1)}, bf16[2,128,1024]{2,1,0:T(8,128)(2,1)}, u32[]{:S(2)}, u32[]{:S(2)}) collective-permute-start(bf16[2,128,1024]{2,1,0:T(8,128)(2,1)} %get-tuple-element.23), channel_id=1, source_target_pairs={{0,3},{1,2},{2,1},{3,0},{4,7},{5,6},{6,5},{7,4},{8,11},{9,10},{10,... | collective-permute-start | bytes 1572872 | tf_op jit(solution)/shard_map/ppermute | solution.py:27
  130.7 0.8 copy-start.10
  142.0 1.6 copy-start.2
  143.6 1.0 copy-start.11
  181.7 2.0 copy-start.9
  183.7 0.8 copy-start.14
  184.5 0.8 copy-start.16
  185.3 0.8 copy-start.18
  201.6 8.7 %copy-start.21 = (bf16[2,128,1024]{2,1,0:T(8,128)(2,1)S(1)}, bf16[2,128,1024]{2,1,0:T(8,128)(2,1)}, u32[]{:S(2)}) copy-start(bf16[2,128,1024]{2,1,0:T(8,128)(2,1)} %copy-done.20) | copy-start | bytes 1572868
  201.6 98.7 %all-to-all-start.3 = ((bf16[8,2,128,1024]{3,2,1,0:T(8,128)(2,1)}), bf16[8,2,128,1024]{3,2,1,0:T(8,128)(2,1)}, u32[]{:S(2)}, u32[]{:S(2)}) async-start(bf16[8,2,128,1024]{3,2,1,0:T(8,128)(2,1)} %copy-done.9), calls=%async_computation.3 | async-start | bytes 8388608 | tf_op jit(solution)/shard_map/all_to_all | solution.py:277
  209.8 13.5 %collective-permute-start.6 = (bf16[2,128,1024]{2,1,0:T(8,128)(2,1)}, bf16[2,128,1024]{2,1,0:T(8,128)(2,1)S(1)}, u32[]{:S(2)}, u32[]{:S(2)}) collective-permute-start(bf16[2,128,1024]{2,1,0:T(8,128)(2,1)} %copy-done.23), channel_id=1, source_target_pairs={{0,1},{1,0},{2,3},{3,2},{4,5},{5,4},{6,7},{7,6},{8,9},{9,8},{10,11... | collective-permute-start | bytes 1572872 | tf_op jit(solution)/shard_map/ppermute | solution.py:27
  210.1 13.2 %collective-permute-start.7 = (bf16[2,128,1024]{2,1,0:T(8,128)(2,1)}, bf16[2,128,1024]{2,1,0:T(8,128)(2,1)S(1)}, u32[]{:S(2)}, u32[]{:S(2)}) collective-permute-start(bf16[2,128,1024]{2,1,0:T(8,128)(2,1)} %copy-done.22), channel_id=1, source_target_pairs={{0,2},{1,3},{2,0},{3,1},{4,6},{5,7},{6,4},{7,5},{8,10},{9,11},{10,... | collective-permute-start | bytes 1572872 | tf_op jit(solution)/shard_map/ppermute | solution.py:27
  210.3 24.1 %collective-permute-start.8 = (bf16[2,128,1024]{2,1,0:T(8,128)(2,1)S(1)}, bf16[2,128,1024]{2,1,0:T(8,128)(2,1)S(1)}, u32[]{:S(2)}, u32[]{:S(2)}) collective-permute-start(bf16[2,128,1024]{2,1,0:T(8,128)(2,1)S(1)} %copy-done.21), channel_id=1, source_target_pairs={{0,3},{1,2},{2,1},{3,0},{4,7},{5,6},{6,5},{7,4},{8,11},{9,10},{10,... | collective-permute-start | bytes 1572872 | tf_op jit(solution)/shard_map/ppermute | solution.py:27
  234.4 1.6 copy-start.3
  273.2 2.0 copy-start.8
  275.2 0.8 copy-start.24
  276.0 0.8 copy-start.26
  276.8 0.8 copy-start.27
  300.3 8.8 %copy-start.25 = (bf16[2,128,1024]{2,1,0:T(8,128)(2,1)S(1)}, bf16[2,128,1024]{2,1,0:T(8,128)(2,1)}, u32[]{:S(2)}) copy-start(bf16[2,128,1024]{2,1,0:T(8,128)(2,1)} %copy-done.24) | copy-start | bytes 1572868
  300.3 10.9 %copy-start.19 = (bf16[2,128,1024]{2,1,0:T(8,128)(2,1)S(1)}, bf16[2,128,1024]{2,1,0:T(8,128)(2,1)}, u32[]{:S(2)}) copy-start(bf16[2,128,1024]{2,1,0:T(8,128)(2,1)} %copy-done.18) | copy-start | bytes 1572868
  300.3 11.2 %copy-start.17 = (bf16[2,128,1024]{2,1,0:T(8,128)(2,1)S(1)}, bf16[2,128,1024]{2,1,0:T(8,128)(2,1)}, u32[]{:S(2)}) copy-start(bf16[2,128,1024]{2,1,0:T(8,128)(2,1)} %copy-done.16) | copy-start | bytes 1572868
  300.3 21.8 %copy-start.15 = (bf16[2,128,1024]{2,1,0:T(8,128)(2,1)S(1)}, bf16[2,128,1024]{2,1,0:T(8,128)(2,1)}, u32[]{:S(2)}) copy-start(bf16[2,128,1024]{2,1,0:T(8,128)(2,1)} %copy-done.14) | copy-start | bytes 1572868
  300.3 98.7 %all-to-all-start.2 = ((bf16[8,2,128,1024]{3,2,1,0:T(8,128)(2,1)}), bf16[8,2,128,1024]{3,2,1,0:T(8,128)(2,1)}, u32[]{:S(2)}, u32[]{:S(2)}) async-start(bf16[8,2,128,1024]{3,2,1,0:T(8,128)(2,1)} %copy-done.8), calls=%async_computation.2 | async-start | bytes 8388608 | tf_op jit(solution)/shard_map/all_to_all | solution.py:277
  308.6 13.5 %collective-permute-start.9 = (bf16[2,128,1024]{2,1,0:T(8,128)(2,1)}, bf16[2,128,1024]{2,1,0:T(8,128)(2,1)S(1)}, u32[]{:S(2)}, u32[]{:S(2)}) collective-permute-start(bf16[2,128,1024]{2,1,0:T(8,128)(2,1)} %copy-done.27), channel_id=1, source_target_pairs={{0,1},{1,0},{2,3},{3,2},{4,5},{5,4},{6,7},{7,6},{8,9},{9,8},{10,11... | collective-permute-start | bytes 1572872 | tf_op jit(solution)/shard_map/ppermute | solution.py:27
  308.8 13.4 %collective-permute-start.10 = (bf16[2,128,1024]{2,1,0:T(8,128)(2,1)}, bf16[2,128,1024]{2,1,0:T(8,128)(2,1)S(1)}, u32[]{:S(2)}, u32[]{:S(2)}) collective-permute-start(bf16[2,128,1024]{2,1,0:T(8,128)(2,1)} %copy-done.26), channel_id=1, source_target_pairs={{0,2},{1,3},{2,0},{3,1},{4,6},{5,7},{6,4},{7,5},{8,10},{9,11},{10,... | collective-permute-start | bytes 1572872 | tf_op jit(solution)/shard_map/ppermute | solution.py:27
  309.1 24.1 %collective-permute-start.11 = (bf16[2,128,1024]{2,1,0:T(8,128)(2,1)S(1)}, bf16[2,128,1024]{2,1,0:T(8,128)(2,1)S(1)}, u32[]{:S(2)}, u32[]{:S(2)}) collective-permute-start(bf16[2,128,1024]{2,1,0:T(8,128)(2,1)S(1)} %copy-done.25), channel_id=1, source_target_pairs={{0,3},{1,2},{2,1},{3,0},{4,7},{5,6},{6,5},{7,4},{8,11},{9,10},{10,... | collective-permute-start | bytes 1572872 | tf_op jit(solution)/shard_map/ppermute | solution.py:27
  311.2 33.3 %collective-permute-start.3 = (bf16[2,128,1024]{2,1,0:T(8,128)(2,1)S(1)}, bf16[2,128,1024]{2,1,0:T(8,128)(2,1)S(1)}, u32[]{:S(2)}, u32[]{:S(2)}) collective-permute-start(bf16[2,128,1024]{2,1,0:T(8,128)(2,1)S(1)} %copy-done.19), channel_id=1, source_target_pairs={{0,1},{1,0},{2,3},{3,2},{4,5},{5,4},{6,7},{7,6},{8,9},{9,8},{10,11... | collective-permute-start | bytes 1572872 | tf_op jit(solution)/shard_map/ppermute | solution.py:27
  311.5 33.1 %collective-permute-start.4 = (bf16[2,128,1024]{2,1,0:T(8,128)(2,1)S(1)}, bf16[2,128,1024]{2,1,0:T(8,128)(2,1)S(1)}, u32[]{:S(2)}, u32[]{:S(2)}) collective-permute-start(bf16[2,128,1024]{2,1,0:T(8,128)(2,1)S(1)} %copy-done.17), channel_id=1, source_target_pairs={{0,2},{1,3},{2,0},{3,1},{4,6},{5,7},{6,4},{7,5},{8,10},{9,11},{10,... | collective-permute-start | bytes 1572872 | tf_op jit(solution)/shard_map/ppermute | solution.py:27
  322.0 33.6 %collective-permute-start.5 = (bf16[2,128,1024]{2,1,0:T(8,128)(2,1)S(1)}, bf16[2,128,1024]{2,1,0:T(8,128)(2,1)S(1)}, u32[]{:S(2)}, u32[]{:S(2)}) collective-permute-start(bf16[2,128,1024]{2,1,0:T(8,128)(2,1)S(1)} %copy-done.15), channel_id=1, source_target_pairs={{0,3},{1,2},{2,1},{3,0},{4,7},{5,6},{6,5},{7,4},{8,11},{9,10},{10,... | collective-permute-start | bytes 1572872 | tf_op jit(solution)/shard_map/ppermute | solution.py:27

commit v3 on v1

v3 whole, which is shorter than its diff:
```python
import functools

import jax
import jax.numpy as jnp
from jax import lax
from jax.experimental import pallas as pl
from jax.experimental.pallas import tpu as pltpu
from jax.sharding import PartitionSpec as P

DH = 128
BLOCK = 64
NBLEN = 128
CHUNKS = 2
FAR_DEPTH = 4
F32 = jnp.float32
BF16 = jnp.bfloat16
VMEM_BYTES = 40 * 1024 * 1024


def partner(index, step, count):
    if count & (count - 1) == 0:
        return index ^ step
    return (step - index) % count


def exchange(array, step, count):
    pairs = [(i, partner(i, step, count)) for i in range(count)]
    return lax.ppermute(array, "enc", pairs)


def swap_rows(array):
    return lax.all_to_all(array, "seq", split_axis=0, concat_axis=0, tiled=True)


def after(array, earlier):
    return lax.optimization_barrier((array, earlier))[0]


def cost(moved, flops=0, exps=0):
    return pl.CostEstimate(flops=flops, bytes_accessed=moved, transcendentals=exps)


PARAMS = pltpu.CompilerParams(vmem_limit_bytes=VMEM_BYTES)
SCALARS = pl.BlockSpec(memory_space=pltpu.SMEM)
ANYWHERE = pl.BlockSpec(memory_space=pl.ANY)


def pack_kernel(q_ref, g_ref, out_ref):
    out_ref[0, 0] = q_ref[0]
    out_ref[0, 1] = g_ref[0]


def pack(h, queries, grads, chunk, chunks, parts):
    rows = queries.shape[1]
    spec = pl.BlockSpec((1, rows, chunk), lambda i: (0, 0, i * chunks + h))
    return pl.pallas_call(
        pack_kernel,
        grid=(parts,),
        in_specs=[spec, spec],
        out_specs=pl.BlockSpec((1, 2, rows, chunk), lambda i: (i, 0, 0, 0)),
        out_shape=jax.ShapeDtypeStruct((parts, 2, rows, chunk), BF16),
        compiler_params=PARAMS,
        cost_estimate=cost(8 * parts * rows * chunk),
        name="pack_rows",
    )(queries, grads)


def unpack_kernel(chunks, *refs):
    ins, (ctx_ref, gq_ref) = refs[:chunks], refs[chunks:]
    chunk = ins[0].shape[-1]
    for h, ref in enumerate(ins):
        ctx_ref[0, :, h * chunk : (h + 1) * chunk] = ref[0, 0]
        gq_ref[0, :, h * chunk : (h + 1) * chunk] = ref[0, 1]


def unpack(pieces, shape):
    parts, _, rows, chunk = pieces[0].shape
    chunks = len(pieces)
    out_spec = pl.BlockSpec((1, rows, chunks * chunk), lambda i: (0, 0, i))
    return pl.pallas_call(
        functools.partial(unpack_kernel, chunks),
        grid=(parts,),
        in_specs=[pl.BlockSpec((1, 2, rows, chunk), lambda i: (i, 0, 0, 0))] * chunks,
        out_specs=[out_spec, out_spec],
        out_shape=[jax.ShapeDtypeStruct(shape, BF16)] * 2,
        compiler_params=PARAMS,
        cost_estimate=cost(8 * rows * shape[2]),
        name="unpack_rows",
    )(*pieces)


def pick_kernel(h, steps, seqs, lists, pool_ref, *rest):
    outs, sems = rest[:-1], rest[-1]
    me = lax.axis_index("enc")
    chunk = outs[0].shape[-1]
    copies = []
    for n, step in enumerate(steps):
        entry = lists[0, partner(me, step, seqs), 0]
        source = pool_ref.at[entry, :, :, h * chunk : (h + 1) * chunk]
        copies.append(pltpu.make_async_copy(source, outs[n], sems.at[n]))
        copies[-1].start()
    for copy in copies:
        copy.wait()


def pick(h, steps, send_lists, kv_pool, chunk):
    seqs = send_lists.shape[1]
    shape = (2, NBLEN, chunk)
    return pl.pallas_call(
        functools.partial(pick_kernel, h, steps, seqs),
        grid=(1,),
        in_specs=[SCALARS, ANYWHERE],
        out_specs=[pl.BlockSpec(shape, lambda i: (0, 0, 0))] * len(steps),
        out_shape=[jax.ShapeDtypeStruct(shape, BF16)] * len(steps),
        scratch_shapes=[pltpu.SemaphoreType.DMA((len(steps),))],
        compiler_params=PARAMS,
        cost_estimate=cost(8 * len(steps) * NBLEN * chunk),
        name="pick_entries",
    )(send_lists, kv_pool)


def dot(left, right, left_dim, right_dim):
    return lax.dot_general(
        left, right, (((left_dim,), (right_dim,)), ((), ())), preferred_element_type=F32
    )


def attend_kernel(seqs, parts, uses, rows_in, *rest):
    kv_in, rest = rest[:seqs], rest[seqs:]
    rows_out, rest = rest[0], rest[1:]
    kv_out, rest = rest[:seqs], rest[seqs:]
    held, rows, made, sums = rest
    scale = DH ** (-0.5)
    me = lax.axis_index("enc")

    for step in range(seqs):
        held[partner(me, step, seqs)] = kv_in[step][...]
    for part in range(parts):
        for n in range(2):
            rows[part, n] = pltpu.roll(rows_in[part, n].astype(F32), 1, 0)
    rows[parts] = jnp.zeros(rows.shape[1:], F32)
    made[0, :, :BLOCK] = jnp.zeros((2, BLOCK, DH), F32)
    sums[...] = jnp.zeros_like(sums)
    first_row = lax.broadcasted_iota(jnp.int32, (BLOCK, DH), 0) == 0

    def one_block(block, q, g):
        first, second = uses[0, block, 0], uses[0, block, 1]
        keys = jnp.concatenate([held[first, 0], held[second, 0]], axis=0)
        values = jnp.concatenate([held[first, 1], held[second, 1]], axis=0)
        scores = dot(q, keys, 1, 1) * scale
        weights = jnp.exp(scores - jnp.max(scores, axis=1, keepdims=True))
        probs = weights / jnp.sum(weights, axis=1, keepdims=True)
        probs_low = probs.astype(BF16)
        out = dot(probs_low, values, 1, 0)
        grad_probs = dot(g, values, 1, 1)
        inner = jnp.sum(probs * grad_probs, axis=1, keepdims=True)
        grad_scores = (probs * (grad_probs - inner) * scale).astype(BF16)
        grad_q = dot(grad_scores, keys, 1, 0)
        grad_keys = dot(grad_scores, q, 0, 0)
        grad_values = dot(probs_low, g, 0, 0)
        sums[first, 0] += grad_keys[:NBLEN]
        sums[second, 0] += grad_keys[NBLEN:]
        sums[first, 1] += grad_values[:NBLEN]
        sums[second, 1] += grad_values[NBLEN:]
        return out, grad_q

    def one_part(part, carry):
        q, g = (rows[part, n, BLOCK:].astype(BF16) for n in range(2))
        for n, result in enumerate(one_block(2 * part, q, g)):
            made[part, n, BLOCK:] = result
        q, g = (
            jnp.where(first_row, rows[part, n, :BLOCK], rows[part + 1, n, :BLOCK]).astype(BF16)
            for n in range(2)
        )
        for n, result in enumerate(one_block(2 * part + 1, q, g)):
            made[part + 1, n, :BLOCK] = result
            made[part, n, :1] = result[:1]
        return carry

    if parts <= 4:
        for part in range(parts):
            one_part(part, 0)
    else:
        lax.fori_loop(0, parts, one_part, 0)

    for part in range(parts):
        for n in range(2):
            rows_out[part, n] = pltpu.roll(made[part, n], 2 * BLOCK - 1, 0).astype(BF16)
    for step in range(seqs):
        kv_out[step][...] = sums[partner(me, step, seqs)].astype(BF16)


def attend(uses, rows_in, kv_in):
    parts, _, part_rows, chunk = rows_in.shape
    seqs = len(kv_in)
    heads = chunk // DH
    rows_spec = pl.BlockSpec((parts, 2, part_rows, DH), lambda i: (0, 0, 0, i))
    kv_spec = pl.BlockSpec((2, NBLEN, DH), lambda i: (0, 0, i))
    pairs = heads * parts * part_rows * 2 * NBLEN
    outs = pl.pallas_call(
        functools.partial(attend_kernel, seqs, parts),
        grid=(heads,),
        in_specs=[SCALARS, rows_spec] + [kv_spec] * seqs,
        out_specs=[rows_spec] + [kv_spec] * seqs,
        scratch_shapes=[
            pltpu.VMEM((seqs, 2, NBLEN, DH), BF16),
            pltpu.VMEM((parts + 1, 2, part_rows, DH), F32),
            pltpu.VMEM((parts + 1, 2, part_rows, DH), F32),
            pltpu.VMEM((seqs, 2, NBLEN, DH), F32),
        ],
        out_shape=[jax.ShapeDtypeStruct(rows_in.shape, BF16)]
        + [jax.ShapeDtypeStruct((2, NBLEN, chunk), BF16)] * seqs,
        compiler_params=PARAMS,
        cost_estimate=cost(8 * (seqs + parts) * NBLEN * chunk, 12 * DH * pairs, pairs),
        name="attend_blocks",
    )(uses, rows_in, *kv_in)
    return outs[0], outs[1:]


def owner_kernel(seqs, lists, *rest):
    ins, out_ref, acc = rest[:seqs], rest[-2], rest[-1]
    me = lax.axis_index("enc")
    acc[...] = jnp.zeros_like(acc)
    for step in range(seqs):
        acc[lists[0, partner(me, step, seqs), 0]] += ins[step][...].astype(F32)
    out_ref[...] = acc[...].astype(BF16)


def owner_sum(h, send_lists, returned, shape, so_far):
    seqs = len(returned)
    chunk = returned[0].shape[-1]
    wide = min(chunk, 256)
    steps = chunk // wide
    extra = [] if so_far is None else [so_far]
    return pl.pallas_call(
        functools.partial(owner_kernel, seqs),
        grid=(steps,),
        in_specs=[SCALARS]
        + [pl.BlockSpec((2, NBLEN, wide), lambda i: (0, 0, i))] * seqs
        + [ANYWHERE] * len(extra),
        out_specs=pl.BlockSpec(
            (shape[0], 2, NBLEN, wide), lambda i: (0, 0, 0, h * steps + i)
        ),
        scratch_shapes=[pltpu.VMEM((shape[0], 2, NBLEN, wide), F32)],
        out_shape=jax.ShapeDtypeStruct(shape, BF16),
        input_output_aliases={seqs + 1: 0} if extra else {},
        compiler_params=PARAMS,
        cost_estimate=cost(4 * (seqs + shape[0]) * NBLEN * chunk, seqs * 2 * NBLEN * chunk),
        name="owner_sum",
    )(send_lists, *returned, *extra)


class Exchanges:
    def __init__(self, count, depth):
        self.count, self.depth = count, depth
        self.far, self.near = [], []
        half = count // 2
        self.far_steps = list(range(half, count))
        self.near_steps = list(range(1, half))

    def run(self, pieces):
        got = [pieces[0]] + [None] * (self.count - 1)
        for steps, done, depth in (
            (self.far_steps, self.far, self.depth),
            (self.near_steps, self.near, 1),
        ):
            for step in steps:
                piece = pieces[step]
                if len(done) >= depth:
                    piece = after(piece, done[-depth])
                got[step] = exchange(piece, step, self.count)
                done.append(got[step])
        return got


def local(seqs, parts, queries, kv_pool, send_lists, block_slots, grad_context):
    width = kv_pool.shape[-1]
    chunks = min(CHUNKS, width // DH)
    chunk = width // chunks
    links = Exchanges(seqs, FAR_DEPTH)
    half = seqs // 2

    fetched, arrived = [], []
    for h in range(chunks):
        far = pick(h, range(half, seqs), send_lists, kv_pool, chunk)
        send_lists = after(send_lists, far[0])
        near = pick(h, range(half), send_lists, kv_pool, chunk)
        queries = after(queries, near[0])
        fetched.append(links.run(list(near) + list(far)))
        packed = pack(h, queries, grad_context, chunk, chunks, parts)
        send_lists = after(send_lists, packed)
        arrived.append(swap_rows(packed))
    pool_grads = None
    token_parts, returns = [], []
    for h in range(chunks):
        rows_out, kv_out = attend(block_slots, arrived[h], fetched[h])
        returns.append(links.run(kv_out))
        token_parts.append(swap_rows(rows_out))
    context, grad_queries = unpack(token_parts, queries.shape)
    for h in range(chunks):
        pool_grads = owner_sum(h, send_lists, returns[h], kv_pool.shape, pool_grads)
    return (context, grad_queries, pool_grads)


def solution(mesh):
    in_specs = (
        P("enc", "seq", None),
        P("enc", None, None, "seq"),
        P("enc", None, None),
        P("enc", None, None),
        P("enc", "seq", None),
    )
    out_specs = (P("enc", "seq", None), P("enc", "seq", None), P("enc", None, None, "seq"))
    body = functools.partial(local, mesh.shape["enc"], mesh.shape["seq"])
    return jax.shard_map(body, mesh=mesh, in_specs=in_specs, out_specs=out_specs, check_vma=False)
```

time: 584 us -> 537 us (0.920)
  Pallas kernels: 312 us -> 93.4 us
  waiting for transfers between devices: 174 us -> 331 us
  local copies, waits for them, and re-layouts: 28.4 us -> 58.9 us
  between operations: 13.8 us -> 0.87 us
    pallas_call x6 -> x11, Pallas kernels: 312 us -> 93.4 us  [the longest x2 75.2 us: attend(): pl.pallas_call(functools.partial(attend_kernel, seqs, parts), grid=(heads...]
    ppermute x40 -> x28, waiting for transfers between devices: 174 us -> 331 us  [exchange(): return lax.ppermute(array, 'enc', pairs)]
    unnamed x61 -> x132, local copies, waits for them, and re-layouts: 17.2 us -> 58.6 us
    all_to_all x0 -> x4, starting transfers between devices: none -> 17 us  [swap_rows(): return lax.all_to_all(array, 'seq', split_axis=0, concat_axis=0, tiled=True)]
    ppermute x40 -> x28, starting transfers between devices: 49.5 us -> 34.2 us  [exchange(): return lax.ppermute(array, 'enc', pairs)]
  transfers between devices with their start and end apart: 40 -> 32, of which waited for: 14 -> 17; matrix products, arithmetic and copies ran while one was open for 1% -> 0% of each run, Pallas kernels for 53% -> 16%
where the time goes in v3:
time: 537 us; the launch traced here: 536 us
  waiting for transfers between devices  331 us (62%)
  Pallas kernels  93.4 us (17%)
  local copies, waits for them, and re-layouts  58.9 us (11%)
  starting transfers between devices  51.1 us (10%)
    ppermute x28, waiting for transfers between devices, exchange(): return lax.ppermute(array, 'enc', pairs)  331 us
    pallas_call x2, Pallas kernels, attend(): pl.pallas_call(functools.partial(attend_kernel, seqs, parts), grid=(heads...  75.2 us
    unnamed x132, local copies, waits for them, and re-layouts  58.6 us
    ppermute x28, starting transfers between devices, exchange(): return lax.ppermute(array, 'enc', pairs)  34.2 us
    all_to_all x4, starting transfers between devices, swap_rows(): return lax.all_to_all(array, 'seq', split_axis=0, concat_axis=0, tiled=True)  17 us
  transfers between devices with their start and end apart: 32, of which 17 were waited for; matrix products, arithmetic and copies ran while one was open for 0% of the time, Pallas kernels for 16%

profile of v3, /device:TPU:15, one launch (start us, length us, event | category | flops | bytes accessed | tf_op | source)
XLA Modules:
  0.0 535.6 jit_solution(5021105897084239903)
XLA Ops:
  1.4 2.2 copy-done
  7.7 2.2 copy-done.1
  9.8 1.8 pick_entries.5
  13.6 1.3 copy-done.8
  14.9 4.6 all-to-all-start
  19.6 13.2 %collective-permute-done.1.rest_2_ = bf16[2,128,1024]{2,1,0:T(8,128)(2,1)S(1)} collective-permute-done((bf16[2,128,1024]{2,1,0:T(8,128)(2,1)S(1)}, bf16[2,128,1024]{2,1,0:T(8,128)(2,1)S(1)}, u32[]{:S(2)}, u32[]{:S(2)}) %collective-permute-start.1) | collective-permute-done | bytes 524320 | tf_op jit(solution)/shard_map/ppermute | solution.py:28
  34.7 2.2 copy-done.2
  41.1 2.2 copy-done.3
  43.3 1.7 pick_entries.7
  46.6 1.6 collective-permute-done.2.rest_3_
  49.3 1.3 copy-done.7
  50.6 4.2 all-to-all-start.2
  54.8 2.4 collective-permute-start.3
  58.1 2.4 collective-permute-start.5
  60.6 16.3 %collective-permute-done.8.rest_2_ = bf16[2,128,1024]{2,1,0:T(8,128)(2,1)S(1)} collective-permute-done((bf16[2,128,1024]{2,1,0:T(8,128)(2,1)}, bf16[2,128,1024]{2,1,0:T(8,128)(2,1)S(1)}, u32[]{:S(2)}, u32[]{:S(2)}) %collective-permute-start.8) | collective-permute-done | bytes 524320 | tf_op jit(solution)/shard_map/ppermute | solution.py:28
  77.7 3.4 collective-permute-start.9
  81.1 43.1 %collective-permute-done.4.rest_5_ = bf16[2,128,1024]{2,1,0:T(8,128)(2,1)} collective-permute-done((bf16[2,128,1024]{2,1,0:T(8,128)(2,1)}, bf16[2,128,1024]{2,1,0:T(8,128)(2,1)}, u32[]{:S(2)}, u32[]{:S(2)}) %collective-permute-start.4) | collective-permute-done | bytes 524320 | tf_op jit(solution)/shard_map/ppermute | solution.py:28
  124.2 12.5 %collective-permute-done.5.rest_6_ = bf16[2,128,1024]{2,1,0:T(8,128)(2,1)} collective-permute-done((bf16[2,128,1024]{2,1,0:T(8,128)(2,1)}, bf16[2,128,1024]{2,1,0:T(8,128)(2,1)}, u32[]{:S(2)}, u32[]{:S(2)}) %collective-permute-start.5) | collective-permute-done | bytes 524320 | tf_op jit(solution)/shard_map/ppermute | solution.py:28
  136.7 12.0 %collective-permute-done.6.rest_7_ = bf16[2,128,1024]{2,1,0:T(8,128)(2,1)} collective-permute-done((bf16[2,128,1024]{2,1,0:T(8,128)(2,1)}, bf16[2,128,1024]{2,1,0:T(8,128)(2,1)}, u32[]{:S(2)}, u32[]{:S(2)}) %collective-permute-start.6) | collective-permute-done | bytes 524320 | tf_op jit(solution)/shard_map/ppermute | solution.py:28
  151.8 37.2 %attend_blocks.2 = (bf16[4,2,128,1024]{3,2,1,0:T(8,128)(2,1)S(1)}, bf16[2,128,1024]{2,1,0:T(8,128)(2,1)S(1)}, bf16[2,128,1024]{2,1,0:T(8,128)(2,1)}, bf16[2,128,...) custom-call(s32[1,8,2]{2,1,0:T(8,128)S(1)} %copy.11.uses, ...), custom_call_target="tpu_custom_call" | custom-call | flops 1610612736 | bytes 12582912 | tf_op jit(solution)/shard_map/attend_blocks/pallas_call | solution.py:200
  189.0 1.3 copy-done.11
  196.0 1.3 copy-done.9
  197.3 3.7 all-to-all-start.1
  201.8 2.4 collective-permute-start.10
  204.2 1.2 collective-permute-start.11
  207.4 16.3 %collective-permute-done.15.rest_2_ = bf16[2,128,1024]{2,1,0:T(8,128)(2,1)S(1)} collective-permute-done((bf16[2,128,1024]{2,1,0:T(8,128)(2,1)}, bf16[2,128,1024]{2,1,0:T(8,128)(2,1)S(1)}, u32[]{:S(2)}, u32[]{:S(2)}) %collective-permute-start.15) | collective-permute-done | bytes 524320 | tf_op jit(solution)/shard_map/ppermute | solution.py:28
  224.5 3.6 collective-permute-start.16
  228.1 42.6 %collective-permute-done.11.rest_5_ = bf16[2,128,1024]{2,1,0:T(8,128)(2,1)S(1)} collective-permute-done((bf16[2,128,1024]{2,1,0:T(8,128)(2,1)}, bf16[2,128,1024]{2,1,0:T(8,128)(2,1)S(1)}, u32[]{:S(2)}, u32[]{:S(2)}) %collective-permute-start.11) | collective-permute-done | bytes 524320 | tf_op jit(solution)/shard_map/ppermute | solution.py:28
  270.7 12.2 %collective-permute-done.12.rest_6_ = bf16[2,128,1024]{2,1,0:T(8,128)(2,1)S(1)} collective-permute-done((bf16[2,128,1024]{2,1,0:T(8,128)(2,1)}, bf16[2,128,1024]{2,1,0:T(8,128)(2,1)S(1)}, u32[]{:S(2)}, u32[]{:S(2)}) %collective-permute-start.12) | collective-permute-done | bytes 524320 | tf_op jit(solution)/shard_map/ppermute | solution.py:28
  282.9 12.7 %collective-permute-done.13.rest_7_ = bf16[2,128,1024]{2,1,0:T(8,128)(2,1)S(1)} collective-permute-done((bf16[2,128,1024]{2,1,0:T(8,128)(2,1)}, bf16[2,128,1024]{2,1,0:T(8,128)(2,1)S(1)}, u32[]{:S(2)}, u32[]{:S(2)}) %collective-permute-start.13) | collective-permute-done | bytes 524320 | tf_op jit(solution)/shard_map/ppermute | solution.py:28
  295.6 1.6 copy-done.10
  299.3 38.0 %attend_blocks.3 = (bf16[4,2,128,1024]{3,2,1,0:T(8,128)(2,1)S(1)}, bf16[2,128,1024]{2,1,0:T(8,128)(2,1)S(1)}, bf16[2,128,1024]{2,1,0:T(8,128)(2,1)}, bf16[2,128,...) custom-call(s32[1,8,2]{2,1,0:T(8,128)S(1)} %copy.11.uses, ...), custom_call_target="tpu_custom_call" | custom-call | flops 1610612736 | bytes 12582912 | tf_op jit(solution)/shard_map/attend_blocks/pallas_call | solution.py:200
  337.2 1.3 copy-done.12
  344.2 4.5 all-to-all-start.3
  348.7 3.2 collective-permute-start.22
  353.1 2.3 collective-permute-start.18
  355.5 49.4 %collective-permute-done.20.rest_4_ = bf16[2,128,1024]{2,1,0:T(8,128)(2,1)S(1)} collective-permute-done((bf16[2,128,1024]{2,1,0:T(8,128)(2,1)}, bf16[2,128,1024]{2,1,0:T(8,128)(2,1)S(1)}, u32[]{:S(2)}, u32[]{:S(2)}) %collective-permute-start.20) | collective-permute-done | bytes 524320 | tf_op jit(solution)/shard_map/ppermute | solution.py:28
  405.6 3.0 collective-permute-start.21
  408.6 18.7 %collective-permute-done.22.rest_5_ = bf16[2,128,1024]{2,1,0:T(8,128)(2,1)S(1)} collective-permute-done((bf16[2,128,1024]{2,1,0:T(8,128)(2,1)}, bf16[2,128,1024]{2,1,0:T(8,128)(2,1)S(1)}, u32[]{:S(2)}, u32[]{:S(2)}) %collective-permute-start.22) | collective-permute-done | bytes 524320 | tf_op jit(solution)/shard_map/ppermute | solution.py:28
  428.1 3.3 collective-permute-start.23
  431.4 42.7 %collective-permute-done.24.rest_6_ = bf16[2,128,1024]{2,1,0:T(8,128)(2,1)S(1)} collective-permute-done((bf16[2,128,1024]{2,1,0:T(8,128)(2,1)}, bf16[2,128,1024]{2,1,0:T(8,128)(2,1)S(1)}, u32[]{:S(2)}, u32[]{:S(2)}) %collective-permute-start.24) | collective-permute-done | bytes 524320 | tf_op jit(solution)/shard_map/ppermute | solution.py:28
  475.2 11.6 %collective-permute-done.26.rest_7_ = bf16[2,128,1024]{2,1,0:T(8,128)(2,1)S(1)} collective-permute-done((bf16[2,128,1024]{2,1,0:T(8,128)(2,1)}, bf16[2,128,1024]{2,1,0:T(8,128)(2,1)S(1)}, u32[]{:S(2)}, u32[]{:S(2)}) %collective-permute-start.26) | collective-permute-done | bytes 524320 | tf_op jit(solution)/shard_map/ppermute | solution.py:28
  496.8 3.4 owner_sum.2.rest_8_
  500.2 4.2 unpack_rows.1
  504.5 1.5 collective-permute-done.23.rest_5_
  506.0 13.1 %collective-permute-done.25.rest_6_ = bf16[2,128,1024]{2,1,0:T(8,128)(2,1)} collective-permute-done((bf16[2,128,1024]{2,1,0:T(8,128)(2,1)}, bf16[2,128,1024]{2,1,0:T(8,128)(2,1)}, u32[]{:S(2)}, u32[]{:S(2)}) %collective-permute-start.25) | collective-permute-done | bytes 524320 | tf_op jit(solution)/shard_map/ppermute | solution.py:28
  519.2 11.8 %collective-permute-done.27.rest_7_ = bf16[2,128,1024]{2,1,0:T(8,128)(2,1)} collective-permute-done((bf16[2,128,1024]{2,1,0:T(8,128)(2,1)}, bf16[2,128,1024]{2,1,0:T(8,128)(2,1)}, u32[]{:S(2)}, u32[]{:S(2)}) %collective-permute-start.27) | collective-permute-done | bytes 524320 | tf_op jit(solution)/shard_map/ppermute | solution.py:28
  531.0 4.7 owner_sum.3
  (163 shorter events, 51.6 us)
Async XLA Ops:
  1.4 2.2 copy-start
  3.5 4.0 copy-start.63
  7.7 2.2 copy-start.1
  9.8 3.3 copy-start.4
  9.8 3.3 copy-start.5
  12.5 7.0 %collective-permute-start = (bf16[2,128,1024]{2,1,0:T(8,128)(2,1)}, bf16[2,128,1024]{2,1,0:T(8,128)(2,1)S(1)}, u32[]{:S(2)}, u32[]{:S(2)}) collective-permute-start(bf16[2,128,1024]{2,1,0:T(8,128)(2,1)} %get-tuple-element.72), channel_id=1, source_target_pairs={{0,4},{4,0},{8,12},{12,8},{16,20},{20,16},{24,28},{28,24},{1,5},{5... | collective-permute-start | bytes 1572872 | tf_op jit(solution)/shard_map/ppermute | solution.py:28
  13.6 1.3 copy-start.8
  14.9 35.7 %all-to-all-start = ((bf16[4,2,128,1024]{3,2,1,0:T(8,128)(2,1)}), bf16[4,2,128,1024]{3,2,1,0:T(8,128)(2,1)}, u32[]{:S(2)}, u32[]{:S(2)}) async-start(bf16[4,2,128,1024]{3,2,1,0:T(8,128)(2,1)} %copy-done.8), calls=%async_computation | async-start | bytes 4194304 | tf_op jit(solution)/shard_map/all_to_all | solution.py:32
  19.5 18.3 %copy-start.21 = (bf16[2,128,1024]{2,1,0:T(8,128)(2,1)}, bf16[2,128,1024]{2,1,0:T(8,128)(2,1)S(1)}, u32[]{:S(2)}) copy-start(bf16[2,128,1024]{2,1,0:T(8,128)(2,1)S(1)} %collective-permute-done.rest_1_) | copy-start | bytes 1572868
  19.5 13.3 %collective-permute-start.1 = (bf16[2,128,1024]{2,1,0:T(8,128)(2,1)S(1)}, bf16[2,128,1024]{2,1,0:T(8,128)(2,1)S(1)}, u32[]{:S(2)}, u32[]{:S(2)}) collective-permute-start(bf16[2,128,1024]{2,1,0:T(8,128)(2,1)S(1)} %get-tuple-element.74), channel_id=1, source_target_pairs={{0,8},{4,12},{8,0},{12,4},{16,24},{20,28},{24,16},{28,20},{1,9},{5... | collective-permute-start | bytes 1572872 | tf_op jit(solution)/shard_map/ppermute | solution.py:28
  33.7 14.5 %collective-permute-start.2 = (bf16[2,128,1024]{2,1,0:T(8,128)(2,1)}, bf16[2,128,1024]{2,1,0:T(8,128)(2,1)}, u32[]{:S(2)}, u32[]{:S(2)}) collective-permute-start(bf16[2,128,1024]{2,1,0:T(8,128)(2,1)} %get-tuple-element.76), channel_id=1, source_target_pairs={{0,12},{4,8},{8,4},{12,0},{16,28},{20,24},{24,20},{28,16},{1,13},{... | collective-permute-start | bytes 1572872 | tf_op jit(solution)/shard_map/ppermute | solution.py:28
  34.7 2.2 copy-start.2
  41.1 2.2 copy-start.3
  43.3 5.6 %copy-start.6 = (bf16[1,128,8192]{2,1,0:T(8,128)(2,1)S(1)}, bf16[1,128,8192]{2,1,0:T(8,128)(2,1)}, u32[]{:S(2)}) copy-start(bf16[1,128,8192]{2,1,0:T(8,128)(2,1)} %g_ref.3) | copy-start | bytes 6291460
  48.2 6.6 %collective-permute-start.7 = (bf16[2,128,1024]{2,1,0:T(8,128)(2,1)}, bf16[2,128,1024]{2,1,0:T(8,128)(2,1)S(1)}, u32[]{:S(2)}, u32[]{:S(2)}) collective-permute-start(bf16[2,128,1024]{2,1,0:T(8,128)(2,1)} %get-tuple-element.87), channel_id=1, source_target_pairs={{0,4},{4,0},{8,12},{12,8},{16,20},{20,16},{24,28},{28,24},{1,5},{5... | collective-permute-start | bytes 1572872 | tf_op jit(solution)/shard_map/ppermute | solution.py:28
  49.3 1.3 copy-start.7
  50.6 30.4 %copy-start.64 = (s32[1,8,2]{1,2,0:T(2,128)S(1)}, s32[1,8,2]{1,2,0:T(2,128)}, u32[]{:S(2)}) copy-start(s32[1,8,2]{1,2,0:T(2,128)} %param.8) | copy-start | bytes 196
  50.6 145.4 %all-to-all-start.2 = ((bf16[4,2,128,1024]{3,2,1,0:T(8,128)(2,1)}), bf16[4,2,128,1024]{3,2,1,0:T(8,128)(2,1)S(1)}, u32[]{:S(2)}, u32[]{:S(2)}) async-start(bf16[4,2,128,1024]{3,2,1,0:T(8,128)(2,1)} %copy-done.7), calls=%async_computation.2 | async-start | bytes 4194304 | tf_op jit(solution)/shard_map/all_to_all | solution.py:32
  54.8 134.2 %copy-start.15 = (bf16[2,128,1024]{2,1,0:T(8,128)(2,1)}, bf16[2,128,1024]{2,1,0:T(8,128)(2,1)S(1)}, u32[]{:S(2)}) copy-start(bf16[2,128,1024]{2,1,0:T(8,128)(2,1)S(1)} %collective-permute-done.7.rest_1_) | copy-start | bytes 1572868
  54.8 22.0 %collective-permute-start.8 = (bf16[2,128,1024]{2,1,0:T(8,128)(2,1)}, bf16[2,128,1024]{2,1,0:T(8,128)(2,1)S(1)}, u32[]{:S(2)}, u32[]{:S(2)}) collective-permute-start(bf16[2,128,1024]{2,1,0:T(8,128)(2,1)} %copy-done.62), channel_id=1, source_target_pairs={{0,8},{4,12},{8,0},{12,4},{16,24},{20,28},{24,16},{28,20},{1,9},{5... | collective-permute-start | bytes 1572872 | tf_op jit(solution)/shard_map/ppermute | solution.py:28
  54.8 26.3 %collective-permute-start.3 = (bf16[2,128,1024]{2,1,0:T(8,128)(2,1)}, bf16[2,128,1024]{2,1,0:T(8,128)(2,1)}, u32[]{:S(2)}, u32[]{:S(2)}) collective-permute-start(bf16[2,128,1024]{2,1,0:T(8,128)(2,1)} %copy-done.57), channel_id=1, source_target_pairs={{0,16},{4,20},{8,24},{12,28},{16,0},{20,4},{24,8},{28,12},{1,17},{... | collective-permute-start | bytes 1572872 | tf_op jit(solution)/shard_map/ppermute | solution.py:28
  57.2 67.0 %collective-permute-start.4 = (bf16[2,128,1024]{2,1,0:T(8,128)(2,1)}, bf16[2,128,1024]{2,1,0:T(8,128)(2,1)}, u32[]{:S(2)}, u32[]{:S(2)}) collective-permute-start(bf16[2,128,1024]{2,1,0:T(8,128)(2,1)} %copy-done.56), channel_id=1, source_target_pairs={{0,20},{4,16},{8,28},{12,24},{16,4},{20,0},{24,12},{28,8},{1,21},{... | collective-permute-start | bytes 1572872 | tf_op jit(solution)/shard_map/ppermute | solution.py:28
  58.1 78.5 %collective-permute-start.5 = (bf16[2,128,1024]{2,1,0:T(8,128)(2,1)}, bf16[2,128,1024]{2,1,0:T(8,128)(2,1)}, u32[]{:S(2)}, u32[]{:S(2)}) collective-permute-start(bf16[2,128,1024]{2,1,0:T(8,128)(2,1)} %copy-done.55), channel_id=1, source_target_pairs={{0,24},{4,28},{8,16},{12,20},{16,8},{20,12},{24,0},{28,4},{1,25},{... | collective-permute-start | bytes 1572872 | tf_op jit(solution)/shard_map/ppermute | solution.py:28
  60.6 88.1 %collective-permute-start.6 = (bf16[2,128,1024]{2,1,0:T(8,128)(2,1)}, bf16[2,128,1024]{2,1,0:T(8,128)(2,1)}, u32[]{:S(2)}, u32[]{:S(2)}) collective-permute-start(bf16[2,128,1024]{2,1,0:T(8,128)(2,1)} %copy-done.54), channel_id=1, source_target_pairs={{0,28},{4,24},{8,20},{12,16},{16,12},{20,8},{24,4},{28,0},{1,29},{... | collective-permute-start | bytes 1572872 | tf_op jit(solution)/shard_map/ppermute | solution.py:28
  77.7 118.3 %collective-permute-start.9 = (bf16[2,128,1024]{2,1,0:T(8,128)(2,1)}, bf16[2,128,1024]{2,1,0:T(8,128)(2,1)}, u32[]{:S(2)}, u32[]{:S(2)}) collective-permute-start(bf16[2,128,1024]{2,1,0:T(8,128)(2,1)} %copy-done.60), channel_id=1, source_target_pairs={{0,12},{4,8},{8,4},{12,0},{16,28},{20,24},{24,20},{28,16},{1,13},{... | collective-permute-start | bytes 1572872 | tf_op jit(solution)/shard_map/ppermute | solution.py:28
  196.0 5.0 collective-permute-start.14
  196.0 1.3 copy-start.9
  197.3 146.8 %all-to-all-start.1 = ((bf16[4,2,128,1024]{3,2,1,0:T(8,128)(2,1)}), bf16[4,2,128,1024]{3,2,1,0:T(8,128)(2,1)S(1)}, u32[]{:S(2)}, u32[]{:S(2)}) async-start(bf16[4,2,128,1024]{3,2,1,0:T(8,128)(2,1)} %copy-done.11), calls=%async_computation.1 | async-start | bytes 4194304 | tf_op jit(solution)/shard_map/all_to_all | solution.py:32
  201.8 21.9 %collective-permute-start.15 = (bf16[2,128,1024]{2,1,0:T(8,128)(2,1)}, bf16[2,128,1024]{2,1,0:T(8,128)(2,1)S(1)}, u32[]{:S(2)}, u32[]{:S(2)}) collective-permute-start(bf16[2,128,1024]{2,1,0:T(8,128)(2,1)} %copy-done.61), channel_id=1, source_target_pairs={{0,8},{4,12},{8,0},{12,4},{16,24},{20,28},{24,16},{28,20},{1,9},{5... | collective-permute-start | bytes 1572872 | tf_op jit(solution)/shard_map/ppermute | solution.py:28
  201.8 26.3 %collective-permute-start.10 = (bf16[2,128,1024]{2,1,0:T(8,128)(2,1)}, bf16[2,128,1024]{2,1,0:T(8,128)(2,1)S(1)}, u32[]{:S(2)}, u32[]{:S(2)}) collective-permute-start(bf16[2,128,1024]{2,1,0:T(8,128)(2,1)} %copy-done.46), channel_id=1, source_target_pairs={{0,16},{4,20},{8,24},{12,28},{16,0},{20,4},{24,8},{28,12},{1,17},{... | collective-permute-start | bytes 1572872 | tf_op jit(solution)/shard_map/ppermute | solution.py:28
  204.2 66.5 %collective-permute-start.11 = (bf16[2,128,1024]{2,1,0:T(8,128)(2,1)}, bf16[2,128,1024]{2,1,0:T(8,128)(2,1)S(1)}, u32[]{:S(2)}, u32[]{:S(2)}) collective-permute-start(bf16[2,128,1024]{2,1,0:T(8,128)(2,1)} %copy-done.45), channel_id=1, source_target_pairs={{0,20},{4,16},{8,28},{12,24},{16,4},{20,0},{24,12},{28,8},{1,21},{... | collective-permute-start | bytes 1572872 | tf_op jit(solution)/shard_map/ppermute | solution.py:28
  205.4 77.5 %collective-permute-start.12 = (bf16[2,128,1024]{2,1,0:T(8,128)(2,1)}, bf16[2,128,1024]{2,1,0:T(8,128)(2,1)S(1)}, u32[]{:S(2)}, u32[]{:S(2)}) collective-permute-start(bf16[2,128,1024]{2,1,0:T(8,128)(2,1)} %copy-done.43), channel_id=1, source_target_pairs={{0,24},{4,28},{8,16},{12,20},{16,8},{20,12},{24,0},{28,4},{1,25},{... | collective-permute-start | bytes 1572872 | tf_op jit(solution)/shard_map/ppermute | solution.py:28
  206.6 89.0 %collective-permute-start.13 = (bf16[2,128,1024]{2,1,0:T(8,128)(2,1)}, bf16[2,128,1024]{2,1,0:T(8,128)(2,1)S(1)}, u32[]{:S(2)}, u32[]{:S(2)}) collective-permute-start(bf16[2,128,1024]{2,1,0:T(8,128)(2,1)} %copy-done.42), channel_id=1, source_target_pairs={{0,28},{4,24},{8,20},{12,16},{16,12},{20,8},{24,4},{28,0},{1,29},{... | collective-permute-start | bytes 1572872 | tf_op jit(solution)/shard_map/ppermute | solution.py:28
  224.5 118.8 %collective-permute-start.16 = (bf16[2,128,1024]{2,1,0:T(8,128)(2,1)}, bf16[2,128,1024]{2,1,0:T(8,128)(2,1)S(1)}, u32[]{:S(2)}, u32[]{:S(2)}) collective-permute-start(bf16[2,128,1024]{2,1,0:T(8,128)(2,1)} %copy-done.58), channel_id=1, source_target_pairs={{0,12},{4,8},{8,4},{12,0},{16,28},{20,24},{24,20},{28,16},{1,13},{... | collective-permute-start | bytes 1572872 | tf_op jit(solution)/shard_map/ppermute | solution.py:28
  295.6 1.6 copy-start.10
  344.2 9.0 %collective-permute-start.17 = (bf16[2,128,1024]{2,1,0:T(8,128)(2,1)}, bf16[2,128,1024]{2,1,0:T(8,128)(2,1)S(1)}, u32[]{:S(2)}, u32[]{:S(2)}) collective-permute-start(bf16[2,128,1024]{2,1,0:T(8,128)(2,1)} %get-tuple-element.111), channel_id=1, source_target_pairs={{0,4},{4,0},{8,12},{12,8},{16,20},{20,16},{24,28},{28,24},{1,5},{5... | collective-permute-start | bytes 1572872 | tf_op jit(solution)/shard_map/ppermute | solution.py:28
  344.2 156.1 %all-to-all-start.3 = ((bf16[4,2,128,1024]{3,2,1,0:T(8,128)(2,1)}), bf16[4,2,128,1024]{3,2,1,0:T(8,128)(2,1)}, u32[]{:S(2)}, u32[]{:S(2)}) async-start(bf16[4,2,128,1024]{3,2,1,0:T(8,128)(2,1)} %copy-done.12), calls=%async_computation.3 | async-start | bytes 4194304 | tf_op jit(solution)/shard_map/all_to_all | solution.py:32
  348.6 56.2 %collective-permute-start.20 = (bf16[2,128,1024]{2,1,0:T(8,128)(2,1)}, bf16[2,128,1024]{2,1,0:T(8,128)(2,1)S(1)}, u32[]{:S(2)}, u32[]{:S(2)}) collective-permute-start(bf16[2,128,1024]{2,1,0:T(8,128)(2,1)} %copy-done.48), channel_id=1, source_target_pairs={{0,16},{4,20},{8,24},{12,28},{16,0},{20,4},{24,8},{28,12},{1,17},{... | collective-permute-start | bytes 1572872 | tf_op jit(solution)/shard_map/ppermute | solution.py:28
  348.7 78.6 %collective-permute-start.22 = (bf16[2,128,1024]{2,1,0:T(8,128)(2,1)}, bf16[2,128,1024]{2,1,0:T(8,128)(2,1)S(1)}, u32[]{:S(2)}, u32[]{:S(2)}) collective-permute-start(bf16[2,128,1024]{2,1,0:T(8,128)(2,1)} %copy-done.47), channel_id=1, source_target_pairs={{0,20},{4,16},{8,28},{12,24},{16,4},{20,0},{24,12},{28,8},{1,21},{... | collective-permute-start | bytes 1572872 | tf_op jit(solution)/shard_map/ppermute | solution.py:28
  351.9 122.1 %collective-permute-start.24 = (bf16[2,128,1024]{2,1,0:T(8,128)(2,1)}, bf16[2,128,1024]{2,1,0:T(8,128)(2,1)S(1)}, u32[]{:S(2)}, u32[]{:S(2)}) collective-permute-start(bf16[2,128,1024]{2,1,0:T(8,128)(2,1)} %copy-done.44), channel_id=1, source_target_pairs={{0,24},{4,28},{8,16},{12,20},{16,8},{20,12},{24,0},{28,4},{1,25},{... | collective-permute-start | bytes 1572872 | tf_op jit(solution)/shard_map/ppermute | solution.py:28
  353.1 133.6 %collective-permute-start.26 = (bf16[2,128,1024]{2,1,0:T(8,128)(2,1)}, bf16[2,128,1024]{2,1,0:T(8,128)(2,1)S(1)}, u32[]{:S(2)}, u32[]{:S(2)}) collective-permute-start(bf16[2,128,1024]{2,1,0:T(8,128)(2,1)} %copy-done.41), channel_id=1, source_target_pairs={{0,28},{4,24},{8,20},{12,16},{16,12},{20,8},{24,4},{28,0},{1,29},{... | collective-permute-start | bytes 1572872 | tf_op jit(solution)/shard_map/ppermute | solution.py:28
  353.1 134.4 %collective-permute-start.18 = (bf16[2,128,1024]{2,1,0:T(8,128)(2,1)}, bf16[2,128,1024]{2,1,0:T(8,128)(2,1)S(1)}, u32[]{:S(2)}, u32[]{:S(2)}) collective-permute-start(bf16[2,128,1024]{2,1,0:T(8,128)(2,1)} %copy-done.59), channel_id=1, source_target_pairs={{0,8},{4,12},{8,0},{12,4},{16,24},{20,28},{24,16},{28,20},{1,9},{5... | collective-permute-start | bytes 1572872 | tf_op jit(solution)/shard_map/ppermute | solution.py:28
  405.6 98.8 %collective-permute-start.21 = (bf16[2,128,1024]{2,1,0:T(8,128)(2,1)}, bf16[2,128,1024]{2,1,0:T(8,128)(2,1)}, u32[]{:S(2)}, u32[]{:S(2)}) collective-permute-start(bf16[2,128,1024]{2,1,0:T(8,128)(2,1)} %copy-done.53), channel_id=1, source_target_pairs={{0,16},{4,20},{8,24},{12,28},{16,0},{20,4},{24,8},{28,12},{1,17},{... | collective-permute-start | bytes 1572872 | tf_op jit(solution)/shard_map/ppermute | solution.py:28
  428.1 77.9 %collective-permute-start.23 = (bf16[2,128,1024]{2,1,0:T(8,128)(2,1)}, bf16[2,128,1024]{2,1,0:T(8,128)(2,1)}, u32[]{:S(2)}, u32[]{:S(2)}) collective-permute-start(bf16[2,128,1024]{2,1,0:T(8,128)(2,1)} %copy-done.52), channel_id=1, source_target_pairs={{0,20},{4,16},{8,28},{12,24},{16,4},{20,0},{24,12},{28,8},{1,21},{... | collective-permute-start | bytes 1572872 | tf_op jit(solution)/shard_map/ppermute | solution.py:28
  474.9 44.3 %collective-permute-start.25 = (bf16[2,128,1024]{2,1,0:T(8,128)(2,1)}, bf16[2,128,1024]{2,1,0:T(8,128)(2,1)}, u32[]{:S(2)}, u32[]{:S(2)}) collective-permute-start(bf16[2,128,1024]{2,1,0:T(8,128)(2,1)} %copy-done.51), channel_id=1, source_target_pairs={{0,24},{4,28},{8,16},{12,20},{16,8},{20,12},{24,0},{28,4},{1,25},{... | collective-permute-start | bytes 1572872 | tf_op jit(solution)/shard_map/ppermute | solution.py:28
  487.5 43.4 %collective-permute-start.27 = (bf16[2,128,1024]{2,1,0:T(8,128)(2,1)}, bf16[2,128,1024]{2,1,0:T(8,128)(2,1)}, u32[]{:S(2)}, u32[]{:S(2)}) collective-permute-start(bf16[2,128,1024]{2,1,0:T(8,128)(2,1)} %copy-done.50), channel_id=1, source_target_pairs={{0,28},{4,24},{8,20},{12,16},{16,12},{20,8},{24,4},{28,0},{1,29},{... | collective-permute-start | bytes 1572872 | tf_op jit(solution)/shard_map/ppermute | solution.py:28
  488.4 42.6 %collective-permute-start.19 = (bf16[2,128,1024]{2,1,0:T(8,128)(2,1)}, bf16[2,128,1024]{2,1,0:T(8,128)(2,1)}, u32[]{:S(2)}, u32[]{:S(2)}) collective-permute-start(bf16[2,128,1024]{2,1,0:T(8,128)(2,1)} %copy-done.49), channel_id=1, source_target_pairs={{0,12},{4,8},{8,4},{12,0},{16,28},{20,24},{24,20},{28,16},{1,13},{... | collective-permute-start | bytes 1572872 | tf_op jit(solution)/shard_map/ppermute | solution.py:28
  500.2 30.7 %copy-start.14 = (bf16[2,128,1024]{2,1,0:T(8,128)(2,1)S(1)}, bf16[2,128,1024]{2,1,0:T(8,128)(2,1)}, u32[]{:S(2)}) copy-start(bf16[2,128,1024]{2,1,0:T(8,128)(2,1)} %copy-done.13) | copy-start | bytes 1572868
  (49 other events, 43.5 us)

commit v4 on v3

--- a/solution.py
+++ b/solution.py
@@ -18,14 +18,24 @@
 
 
 def partner(index, step, count):
-    if count & (count - 1) == 0:
-        return index ^ step
-    return (step - index) % count
+    half = count // 2
+    below = jnp.asarray(index) < half
+    return jnp.where(below, half + (index + step) % half, (index - step) % half)
 
 
 def exchange(array, step, count):
-    pairs = [(i, partner(i, step, count)) for i in range(count)]
+    half = count // 2
+    there = [half + (i + step) % half for i in range(half)]
+    pairs = list(enumerate(there)) + [(peer, i) for i, peer in enumerate(there)]
     return lax.ppermute(array, "enc", pairs)
+
+
+def swap_near(array, count):
+    half = count // 2
+    groups = [list(range(half)), list(range(half, count))]
+    return lax.all_to_all(
+        array, "enc", split_axis=0, concat_axis=0, axis_index_groups=groups, tiled=True
+    )
 
 
 def swap_rows(array):
@@ -34,6 +44,10 @@
 
 def after(array, earlier):
     return lax.optimization_barrier((array, earlier))[0]
+
+
+def in_hbm(shape):
+    return pltpu.HBM(shape, BF16)
 
 
 def cost(moved, flops=0, exps=0):
@@ -58,7 +72,7 @@
         grid=(parts,),
         in_specs=[spec, spec],
         out_specs=pl.BlockSpec((1, 2, rows, chunk), lambda i: (i, 0, 0, 0)),
-        out_shape=jax.ShapeDtypeStruct((parts, 2, rows, chunk), BF16),
+        out_shape=in_hbm((parts, 2, rows, chunk)),
         compiler_params=PARAMS,
         cost_estimate=cost(8 * parts * rows * chunk),
         name="pack_rows",
@@ -89,33 +103,38 @@
     )(*pieces)
 
 
-def pick_kernel(h, steps, seqs, lists, pool_ref, *rest):
+def pick_kernel(h, far, seqs, lists, pool_ref, *rest):
     outs, sems = rest[:-1], rest[-1]
+    half = seqs // 2
     me = lax.axis_index("enc")
-    chunk = outs[0].shape[-1]
     copies = []
-    for n, step in enumerate(steps):
-        entry = lists[0, partner(me, step, seqs), 0]
-        source = pool_ref.at[entry, :, :, h * chunk : (h + 1) * chunk]
-        copies.append(pltpu.make_async_copy(source, outs[n], sems.at[n]))
+    for step in range(half):
+        if far:
+            peer, out = partner(me, step, seqs), outs[step]
+        else:
+            peer, out = me - me % half + step, outs[0].at[step]
+        chunk = out.shape[-1]
+        source = pool_ref.at[lists[0, peer, 0], :, :, h * chunk : (h + 1) * chunk]
+        copies.append(pltpu.make_async_copy(source, out, sems.at[step]))
         copies[-1].start()
     for copy in copies:
         copy.wait()
 
 
-def pick(h, steps, send_lists, kv_pool, chunk):
+def pick(h, far, send_lists, kv_pool, chunk):
     seqs = send_lists.shape[1]
-    shape = (2, NBLEN, chunk)
+    half = seqs // 2
+    shapes = [(2, NBLEN, chunk)] * half if far else [(half, 2, NBLEN, chunk)]
     return pl.pallas_call(
-        functools.partial(pick_kernel, h, steps, seqs),
+        functools.partial(pick_kernel, h, far, seqs),
         grid=(1,),
         in_specs=[SCALARS, ANYWHERE],
-        out_specs=[pl.BlockSpec(shape, lambda i: (0, 0, 0))] * len(steps),
-        out_shape=[jax.ShapeDtypeStruct(shape, BF16)] * len(steps),
-        scratch_shapes=[pltpu.SemaphoreType.DMA((len(steps),))],
-        compiler_params=PARAMS,
-        cost_estimate=cost(8 * len(steps) * NBLEN * chunk),
-        name="pick_entries",
+        out_specs=[pl.BlockSpec(shape, lambda i, n=len(shape): (0,) * n) for shape in shapes],
+        out_shape=[in_hbm(shape) for shape in shapes],
+        scratch_shapes=[pltpu.SemaphoreType.DMA((half,))],
+        compiler_params=PARAMS,
+        cost_estimate=cost(8 * half * NBLEN * chunk),
+        name="pick_far" if far else "pick_near",
     )(send_lists, kv_pool)
 
 
@@ -126,15 +145,17 @@
 
 
 def attend_kernel(seqs, parts, uses, rows_in, *rest):
-    kv_in, rest = rest[:seqs], rest[seqs:]
-    rows_out, rest = rest[0], rest[1:]
-    kv_out, rest = rest[:seqs], rest[seqs:]
+    half = seqs // 2
+    near_in, far_in, rest = rest[0], rest[1 : 1 + half], rest[1 + half :]
+    rows_out, near_out, far_out, rest = rest[0], rest[1], rest[2 : 2 + half], rest[2 + half :]
     held, rows, made, sums = rest
     scale = DH ** (-0.5)
     me = lax.axis_index("enc")
 
-    for step in range(seqs):
-        held[partner(me, step, seqs)] = kv_in[step][...]
+    base = me - me % half
+    for step in range(half):
+        held[base + step] = near_in[step]
+        held[partner(me, step, seqs)] = far_in[step][...]
     for part in range(parts):
         for n in range(2):
             rows[part, n] = pltpu.roll(rows_in[part, n].astype(F32), 1, 0)
@@ -186,90 +207,87 @@
     for part in range(parts):
         for n in range(2):
             rows_out[part, n] = pltpu.roll(made[part, n], 2 * BLOCK - 1, 0).astype(BF16)
-    for step in range(seqs):
-        kv_out[step][...] = sums[partner(me, step, seqs)].astype(BF16)
-
-
-def attend(uses, rows_in, kv_in):
+    for step in range(half):
+        near_out[step] = sums[base + step].astype(BF16)
+        far_out[step][...] = sums[partner(me, step, seqs)].astype(BF16)
+
+
+def attend(uses, rows_in, near_in, far_in):
     parts, _, part_rows, chunk = rows_in.shape
-    seqs = len(kv_in)
+    half = len(far_in)
+    seqs = 2 * half
     heads = chunk // DH
     rows_spec = pl.BlockSpec((parts, 2, part_rows, DH), lambda i: (0, 0, 0, i))
-    kv_spec = pl.BlockSpec((2, NBLEN, DH), lambda i: (0, 0, i))
+    near_spec = pl.BlockSpec((half, 2, NBLEN, DH), lambda i: (0, 0, 0, i))
+    far_spec = pl.BlockSpec((2, NBLEN, DH), lambda i: (0, 0, i))
     pairs = heads * parts * part_rows * 2 * NBLEN
     outs = pl.pallas_call(
         functools.partial(attend_kernel, seqs, parts),
         grid=(heads,),
-        in_specs=[SCALARS, rows_spec] + [kv_spec] * seqs,
-        out_specs=[rows_spec] + [kv_spec] * seqs,
+        in_specs=[SCALARS, rows_spec, near_spec] + [far_spec] * half,
+        out_specs=[rows_spec, near_spec] + [far_spec] * half,
         scratch_shapes=[
             pltpu.VMEM((seqs, 2, NBLEN, DH), BF16),
             pltpu.VMEM((parts + 1, 2, part_rows, DH), F32),
             pltpu.VMEM((parts + 1, 2, part_rows, DH), F32),
             pltpu.VMEM((seqs, 2, NBLEN, DH), F32),
         ],
-        out_shape=[jax.ShapeDtypeStruct(rows_in.shape, BF16)]
-        + [jax.ShapeDtypeStruct((2, NBLEN, chunk), BF16)] * seqs,
+        out_shape=[in_hbm(rows_in.shape), in_hbm(near_in.shape)]
+        + [in_hbm(array.shape) for array in far_in],
         compiler_params=PARAMS,
         cost_estimate=cost(8 * (seqs + parts) * NBLEN * chunk, 12 * DH * pairs, pairs),
         name="attend_blocks",
-    )(uses, rows_in, *kv_in)
-    return outs[0], outs[1:]
-
-
-def owner_kernel(seqs, lists, *rest):
-    ins, out_ref, acc = rest[:seqs], rest[-2], rest[-1]
+    )(uses, rows_in, near_in, *far_in)
+    return outs[0], outs[1], outs[2:]
+
+
+def owner_kernel(seqs, lists, near_ref, *rest):
+    half = seqs // 2
+    far_refs, out_ref, acc = rest[:half], rest[-2], rest[-1]
     me = lax.axis_index("enc")
+    base = me - me % half
     acc[...] = jnp.zeros_like(acc)
-    for step in range(seqs):
-        acc[lists[0, partner(me, step, seqs), 0]] += ins[step][...].astype(F32)
+    for step in range(half):
+        acc[lists[0, base + step, 0]] += near_ref[step].astype(F32)
+        acc[lists[0, partner(me, step, seqs), 0]] += far_refs[step][...].astype(F32)
     out_ref[...] = acc[...].astype(BF16)
 
 
-def owner_sum(h, send_lists, returned, shape, so_far):
-    seqs = len(returned)
-    chunk = returned[0].shape[-1]
+def owner_sum(h, send_lists, near, far, shape, so_far):
+    half = len(far)
+    chunk = near.shape[-1]
     wide = min(chunk, 256)
     steps = chunk // wide
     extra = [] if so_far is None else [so_far]
     return pl.pallas_call(
-        functools.partial(owner_kernel, seqs),
+        functools.partial(owner_kernel, 2 * half),
         grid=(steps,),
-        in_specs=[SCALARS]
-        + [pl.BlockSpec((2, NBLEN, wide), lambda i: (0, 0, i))] * seqs
+        in_specs=[SCALARS, pl.BlockSpec((half, 2, NBLEN, wide), lambda i: (0, 0, 0, i))]
+        + [pl.BlockSpec((2, NBLEN, wide), lambda i: (0, 0, i))] * half
         + [ANYWHERE] * len(extra),
         out_specs=pl.BlockSpec(
             (shape[0], 2, NBLEN, wide), lambda i: (0, 0, 0, h * steps + i)
         ),
         scratch_shapes=[pltpu.VMEM((shape[0], 2, NBLEN, wide), F32)],
-        out_shape=jax.ShapeDtypeStruct(shape, BF16),
-        input_output_aliases={seqs + 1: 0} if extra else {},
-        compiler_params=PARAMS,
-        cost_estimate=cost(4 * (seqs + shape[0]) * NBLEN * chunk, seqs * 2 * NBLEN * chunk),
+        out_shape=in_hbm(shape),
+        input_output_aliases={half + 2: 0} if extra else {},
+        compiler_params=PARAMS,
+        cost_estimate=cost(4 * (2 * half + shape[0]) * NBLEN * chunk, 4 * half * NBLEN * chunk),
         name="owner_sum",
-    )(send_lists, *returned, *extra)
-
-
-class Exchanges:
+    )(send_lists, near, *far, *extra)
+
+
+class FarExchanges:
     def __init__(self, count, depth):
-        self.count, self.depth = count, depth
-        self.far, self.near = [], []
-        half = count // 2
-        self.far_steps = list(range(half, count))
-        self.near_steps = list(range(1, half))
+        self.count, self.depth, self.done = count, depth, []
 
     def run(self, pieces):
-        got = [pieces[0]] + [None] * (self.count - 1)
-        for steps, done, depth in (
-            (self.far_steps, self.far, self.depth),
-            (self.near_steps, self.near, 1),
-        ):
-            for step in steps:
-                piece = pieces[step]
-                if len(done) >= depth:
-                    piece = after(piece, done[-depth])
-                got[step] = exchange(piece, step, self.count)
-                done.append(got[step])
+        got = []
+        for step, piece in enumerate(pieces):
+            if len(self.done) >= self.depth:
+                piece = after(piece, self.done[-self.depth])
+            got.append(exchange(piece, step, self.count))
+            self.done.append(got[-1])
         return got
 
 
@@ -277,28 +295,25 @@
     width = kv_pool.shape[-1]
     chunks = min(CHUNKS, width // DH)
     chunk = width // chunks
-    links = Exchanges(seqs, FAR_DEPTH)
-    half = seqs // 2
-
-    fetched, arrived = [], []
+    links = FarExchanges(seqs, FAR_DEPTH)
+
+    arrived = []
     for h in range(chunks):
-        far = pick(h, range(half, seqs), send_lists, kv_pool, chunk)
-        send_lists = after(send_lists, far[0])
-        near = pick(h, range(half), send_lists, kv_pool, chunk)
-        queries = after(queries, near[0])
-        fetched.append(links.run(list(near) + list(far)))
-        packed = pack(h, queries, grad_context, chunk, chunks, parts)
-        send_lists = after(send_lists, packed)
-        arrived.append(swap_rows(packed))
+        far = links.run(pick(h, True, send_lists, kv_pool, chunk))
+        near = swap_near(pick(h, False, send_lists, kv_pool, chunk)[0], seqs)
+        rows = swap_rows(pack(h, queries, grad_context, chunk, chunks, parts))
+        arrived.append((rows, near, far))
     pool_grads = None
     token_parts, returns = [], []
     for h in range(chunks):
-        rows_out, kv_out = attend(block_slots, arrived[h], fetched[h])
-        returns.append(links.run(kv_out))
-        token_parts.append(swap_rows(rows_out))
+        rows, near, far = attend(block_slots, *arrived[h])
+        far = links.run(far)
+        near = swap_near(near, seqs)
+        returns.append((near, far))
+        token_parts.append(swap_rows(rows))
     context, grad_queries = unpack(token_parts, queries.shape)
     for h in range(chunks):
-        pool_grads = owner_sum(h, send_lists, returns[h], kv_pool.shape, pool_grads)
+        pool_grads = owner_sum(h, send_lists, *returns[h], kv_pool.shape, pool_grads)
     return (context, grad_queries, pool_grads)
 
 

time: 537 us -> 625 us (1.16)
  blocking collectives: 0 us -> 56.1 us
  waiting for transfers between devices: 331 us -> 385 us
  local copies, waits for them, and re-layouts: 58.9 us -> 23.7 us
  starting transfers between devices: 51.1 us -> 57.5 us
    all_to_all x0 -> x2, blocking collectives: none -> 56.1 us  [the longest x1 30.6 us: swap_near(): lax.all_to_all(array, 'enc', split_axis=0, concat_axis=0, axis_index_grou...]
    all_to_all x4 -> x3, waiting for transfers between devices: 0.01 us -> 37.5 us  [swap_rows(): return lax.all_to_all(array, 'seq', split_axis=0, concat_axis=0, tiled=True)]
    unnamed x132 -> x48, local copies, waits for them, and re-layouts: 58.6 us -> 23.7 us
    all_to_all x0 -> x3, waiting for transfers between devices: none -> 19.5 us  [swap_near(): lax.all_to_all(array, 'enc', split_axis=0, concat_axis=0, axis_index_grou...]
    all_to_all x0 -> x3, starting transfers between devices: none -> 18.7 us  [swap_near(): lax.all_to_all(array, 'enc', split_axis=0, concat_axis=0, axis_index_grou...]
    ppermute x28 -> x16, starting transfers between devices: 34.2 us -> 24.5 us  [exchange(): return lax.ppermute(array, 'enc', pairs)]
    ppermute x28 -> x16, waiting for transfers between devices: 331 us -> 328 us  [exchange(): return lax.ppermute(array, 'enc', pairs)]
    all_to_all x4 -> x3, starting transfers between devices: 17 us -> 14.3 us  [swap_rows(): return lax.all_to_all(array, 'seq', split_axis=0, concat_axis=0, tiled=True)]
  transfers between devices with their start and end apart: 32 -> 22, of which waited for: 17 -> 19; matrix products, arithmetic and copies ran while one was open for 0% -> 0% of each run, Pallas kernels for 16% -> 14%
where the time goes in v4:
time: 625 us; the launch traced here: 618 us
  waiting for transfers between devices  385 us (62%)
  Pallas kernels  95.3 us (15%)
  starting transfers between devices  57.5 us (9%)
  blocking collectives  56.1 us (9%)
  local copies, waits for them, and re-layouts  23.7 us (4%)
    ppermute x16, waiting for transfers between devices, exchange(): return lax.ppermute(array, 'enc', pairs)  328 us
    pallas_call x2, Pallas kernels, attend(): pl.pallas_call(functools.partial(attend_kernel, seqs, parts), grid=(heads...  72.5 us
    all_to_all x3, waiting for transfers between devices, swap_rows(): return lax.all_to_all(array, 'seq', split_axis=0, concat_axis=0, tiled=True)  37.5 us
    all_to_all x1, blocking collectives, swap_near(): lax.all_to_all(array, 'enc', split_axis=0, concat_axis=0, axis_index_grou...  30.6 us
    all_to_all x1, blocking collectives, swap_rows(): return lax.all_to_all(array, 'seq', split_axis=0, concat_axis=0, tiled=True)  25.5 us
    ppermute x16, starting transfers between devices, exchange(): return lax.ppermute(array, 'enc', pairs)  24.5 us
    unnamed x48, local copies, waits for them, and re-layouts  23.7 us
    all_to_all x3, waiting for transfers between devices, swap_near(): lax.all_to_all(array, 'enc', split_axis=0, concat_axis=0, axis_index_grou...  19.5 us
  transfers between devices with their start and end apart: 22, of which 19 were waited for; matrix products, arithmetic and copies ran while one was open for 0% of the time, Pallas kernels for 14%

profile of v4, /device:TPU:15, one launch (start us, length us, event | category | flops | bytes accessed | tf_op | source)
XLA Modules:
  0.0 618.3 jit_solution(14339723688212140329)
XLA Ops:
  3.8 2.0 pack_rows.3
  5.8 4.7 all-to-all-start.3
  12.1 2.0 pack_rows.2
  14.1 19.7 %all-to-all-done.3.rows_in = bf16[4,2,128,1024]{3,2,1,0:T(8,128)(2,1)} async-done(((bf16[4,2,128,1024]{3,2,1,0:T(8,128)(2,1)}), bf16[4,2,128,1024]{3,2,1,0:T(8,128)(2,1)}, u32[]{:S(2)}, u32[]{:S(2)}) %all-to-all-start.3) | async-done | bytes 2097184 | tf_op jit(solution)/shard_map/all_to_all | solution.py:42
  33.8 4.8 all-to-all-start
  38.7 2.2 copy-done
  40.8 2.2 pick_near.2
  43.0 17.8 %all-to-all-done.rows_in = bf16[4,2,128,1024]{3,2,1,0:T(8,128)(2,1)S(1)} async-done(((bf16[4,2,128,1024]{3,2,1,0:T(8,128)(2,1)}), bf16[4,2,128,1024]{3,2,1,0:T(8,128)(2,1)S(1)}, u32[]{:S(2)}, u32[]{:S(2)}) %all-to-all-start) | async-done | bytes 2097184 | tf_op jit(solution)/shard_map/all_to_all | solution.py:42
  62.2 6.8 %all-to-all-start.1 = ((bf16[4,2,128,1024]{3,2,1,0:T(8,128)(2,1)}), bf16[4,2,128,1024]{3,2,1,0:T(8,128)(2,1)}, u32[]{:S(2)}, u32[]{:S(2)}) async-start(bf16[4,2,128,1024]{3,2,1,0:T(8,128)(2,1)} %pick_near.2), calls=%async_computation.1 | async-start | bytes 4194304 | tf_op jit(solution)/shard_map/all_to_all | solution.py:36
  69.0 2.2 copy-done.1
  71.2 2.2 pick_near.3
  73.3 19.5 %all-to-all-done.1.rest_0_ = bf16[4,2,128,1024]{3,2,1,0:T(8,128)(2,1)} async-done(((bf16[4,2,128,1024]{3,2,1,0:T(8,128)(2,1)}), bf16[4,2,128,1024]{3,2,1,0:T(8,128)(2,1)}, u32[]{:S(2)}, u32[]{:S(2)}) %all-to-all-start.1) | async-done | bytes 2097184 | tf_op jit(solution)/shard_map/all_to_all | solution.py:36
  92.9 5.5 all-to-all-start.4
  98.4 2.2 copy-done.2
  100.6 2.2 pick_far.2
  102.7 2.4 collective-permute-start
  108.0 27.4 %collective-permute-done.rest_1_ = bf16[2,128,1024]{2,1,0:T(8,128)(2,1)S(1)} collective-permute-done((bf16[2,128,1024]{2,1,0:T(8,128)(2,1)}, bf16[2,128,1024]{2,1,0:T(8,128)(2,1)S(1)}, u32[]{:S(2)}, u32[]{:S(2)}) %collective-permute-start) | collective-permute-done | bytes 524320 | tf_op jit(solution)/shard_map/ppermute | solution.py:30
  135.4 37.7 %collective-permute-done.1.rest_2_ = bf16[2,128,1024]{2,1,0:T(8,128)(2,1)S(1)} collective-permute-done((bf16[2,128,1024]{2,1,0:T(8,128)(2,1)}, bf16[2,128,1024]{2,1,0:T(8,128)(2,1)S(1)}, u32[]{:S(2)}, u32[]{:S(2)}) %collective-permute-start.1) | collective-permute-done | bytes 524320 | tf_op jit(solution)/shard_map/ppermute | solution.py:30
  173.1 10.8 %collective-permute-done.2.rest_3_ = bf16[2,128,1024]{2,1,0:T(8,128)(2,1)} collective-permute-done((bf16[2,128,1024]{2,1,0:T(8,128)(2,1)}, bf16[2,128,1024]{2,1,0:T(8,128)(2,1)}, u32[]{:S(2)}, u32[]{:S(2)}) %collective-permute-start.2) | collective-permute-done | bytes 524320 | tf_op jit(solution)/shard_map/ppermute | solution.py:30
  183.9 11.2 %collective-permute-done.3.rest_4_ = bf16[2,128,1024]{2,1,0:T(8,128)(2,1)} collective-permute-done((bf16[2,128,1024]{2,1,0:T(8,128)(2,1)}, bf16[2,128,1024]{2,1,0:T(8,128)(2,1)}, u32[]{:S(2)}, u32[]{:S(2)}) %collective-permute-start.3) | collective-permute-done | bytes 524320 | tf_op jit(solution)/shard_map/ppermute | solution.py:30
  196.6 36.2 %attend_blocks.2 = (bf16[4,2,128,1024]{3,2,1,0:T(8,128)(2,1)}, bf16[4,2,128,1024]{3,2,1,0:T(8,128)(2,1)}, bf16[2,128,1024]{2,1,0:T(8,128)(2,1)}, bf16[2,128,1024...) custom-call(s32[1,8,2]{2,1,0:T(8,128)S(1)} %copy.11.uses, ...), custom_call_target="tpu_custom_call" | custom-call | flops 1610612736 | bytes 12582912 | tf_op jit(solution)/shard_map/attend_blocks/pallas_call | solution.py:224
  234.2 4.8 all-to-all-start.2
  239.0 2.2 copy-done.3
  241.2 2.2 pick_far.3
  243.8 2.6 collective-permute-start.6
  246.4 3.6 collective-permute-start.7
  250.0 48.5 %collective-permute-done.4.rest_1_ = bf16[2,128,1024]{2,1,0:T(8,128)(2,1)S(1)} collective-permute-done((bf16[2,128,1024]{2,1,0:T(8,128)(2,1)}, bf16[2,128,1024]{2,1,0:T(8,128)(2,1)S(1)}, u32[]{:S(2)}, u32[]{:S(2)}) %collective-permute-start.4) | collective-permute-done | bytes 524320 | tf_op jit(solution)/shard_map/ppermute | solution.py:30
  298.5 12.2 %collective-permute-done.5.rest_2_ = bf16[2,128,1024]{2,1,0:T(8,128)(2,1)S(1)} collective-permute-done((bf16[2,128,1024]{2,1,0:T(8,128)(2,1)}, bf16[2,128,1024]{2,1,0:T(8,128)(2,1)S(1)}, u32[]{:S(2)}, u32[]{:S(2)}) %collective-permute-start.5) | collective-permute-done | bytes 524320 | tf_op jit(solution)/shard_map/ppermute | solution.py:30
  310.7 15.1 %collective-permute-done.6.rest_3_ = bf16[2,128,1024]{2,1,0:T(8,128)(2,1)S(1)} collective-permute-done((bf16[2,128,1024]{2,1,0:T(8,128)(2,1)}, bf16[2,128,1024]{2,1,0:T(8,128)(2,1)S(1)}, u32[]{:S(2)}, u32[]{:S(2)}) %collective-permute-start.6) | collective-permute-done | bytes 524320 | tf_op jit(solution)/shard_map/ppermute | solution.py:30
  325.8 6.4 %collective-permute-done.7.rest_4_ = bf16[2,128,1024]{2,1,0:T(8,128)(2,1)S(1)} collective-permute-done((bf16[2,128,1024]{2,1,0:T(8,128)(2,1)}, bf16[2,128,1024]{2,1,0:T(8,128)(2,1)S(1)}, u32[]{:S(2)}, u32[]{:S(2)}) %collective-permute-start.7) | collective-permute-done | bytes 524320 | tf_op jit(solution)/shard_map/ppermute | solution.py:30
  332.2 36.3 %attend_blocks.3 = (bf16[4,2,128,1024]{3,2,1,0:T(8,128)(2,1)}, bf16[4,2,128,1024]{3,2,1,0:T(8,128)(2,1)}, bf16[2,128,1024]{2,1,0:T(8,128)(2,1)}, bf16[2,128,1024...) custom-call(s32[1,8,2]{2,1,0:T(8,128)S(1)} %copy.11.uses, ...), custom_call_target="tpu_custom_call" | custom-call | flops 1610612736 | bytes 12582912 | tf_op jit(solution)/shard_map/attend_blocks/pallas_call | solution.py:224
  368.5 25.5 %all_to_all.40.refs_1_ = bf16[4,2,128,1024]{3,2,1,0:T(8,128)(2,1)} all-to-all(bf16[4,2,128,1024]{3,2,1,0:T(8,128)(2,1)} %get-tuple-element.50), channel_id=1, replica_groups=mesh['enc'=8,'seq'=4] {'seq'}, dimensions={0} | all-to-all | bytes 4194304 | tf_op jit(solution)/shard_map/all_to_all | solution.py:42
  394.0 30.6 %all_to_all.41.near_ref = bf16[4,2,128,1024]{3,2,1,0:T(8,128)(2,1)} all-to-all(bf16[4,2,128,1024]{3,2,1,0:T(8,128)(2,1)S(1)} %copy-done.18), channel_id=1, replica_groups={{0,4,8,12},{16,20,24,28},{1,5,9,13},{17,21,25,29},{2,6,10,14},{18,22,26..., dimensions={0} | all-to-all | bytes 4194304 | tf_op jit(solution)/shard_map/all_to_all | solution.py:36
  424.6 6.4 %all-to-all-start.6 = ((bf16[4,2,128,1024]{3,2,1,0:T(8,128)(2,1)}), bf16[4,2,128,1024]{3,2,1,0:T(8,128)(2,1)}, u32[]{:S(2)}, u32[]{:S(2)}) async-start(bf16[4,2,128,1024]{3,2,1,0:T(8,128)(2,1)} %get-tuple-element.53), calls=%async_computation.6 | async-start | bytes 4194304 | tf_op jit(solution)/shard_map/all_to_all | solution.py:36
  432.6 3.5 collective-permute-start.14
  436.1 29.5 %collective-permute-done.8.rest_0_ = bf16[2,128,1024]{2,1,0:T(8,128)(2,1)S(1)} collective-permute-done((bf16[2,128,1024]{2,1,0:T(8,128)(2,1)}, bf16[2,128,1024]{2,1,0:T(8,128)(2,1)S(1)}, u32[]{:S(2)}, u32[]{:S(2)}) %collective-permute-start.8) | collective-permute-done | bytes 524320 | tf_op jit(solution)/shard_map/ppermute | solution.py:30
  465.6 35.9 %collective-permute-done.10.rest_1_ = bf16[2,128,1024]{2,1,0:T(8,128)(2,1)S(1)} collective-permute-done((bf16[2,128,1024]{2,1,0:T(8,128)(2,1)S(1)}, bf16[2,128,1024]{2,1,0:T(8,128)(2,1)S(1)}, u32[]{:S(2)}, u32[]{:S(2)}) %collective-permute-start.10) | collective-permute-done | bytes 524320 | tf_op jit(solution)/shard_map/ppermute | solution.py:30
  501.5 27.3 %collective-permute-done.12.rest_2_ = bf16[2,128,1024]{2,1,0:T(8,128)(2,1)S(1)} collective-permute-done((bf16[2,128,1024]{2,1,0:T(8,128)(2,1)S(1)}, bf16[2,128,1024]{2,1,0:T(8,128)(2,1)S(1)}, u32[]{:S(2)}, u32[]{:S(2)}) %collective-permute-start.12) | collective-permute-done | bytes 524320 | tf_op jit(solution)/shard_map/ppermute | solution.py:30
  528.9 3.0 collective-permute-start.11
  533.0 27.5 %collective-permute-done.14.rest_3_ = bf16[2,128,1024]{2,1,0:T(8,128)(2,1)S(1)} collective-permute-done((bf16[2,128,1024]{2,1,0:T(8,128)(2,1)}, bf16[2,128,1024]{2,1,0:T(8,128)(2,1)S(1)}, u32[]{:S(2)}, u32[]{:S(2)}) %collective-permute-start.14) | collective-permute-done | bytes 524320 | tf_op jit(solution)/shard_map/ppermute | solution.py:30
  560.5 3.3 collective-permute-start.15
  565.4 2.4 unpack_rows.1
  568.3 3.5 owner_sum.2.rest_4_
  571.8 7.5 %collective-permute-done.13.rest_2_ = bf16[2,128,1024]{2,1,0:T(8,128)(2,1)S(1)} collective-permute-done((bf16[2,128,1024]{2,1,0:T(8,128)(2,1)}, bf16[2,128,1024]{2,1,0:T(8,128)(2,1)S(1)}, u32[]{:S(2)}, u32[]{:S(2)}) %collective-permute-start.13) | collective-permute-done | bytes 524320 | tf_op jit(solution)/shard_map/ppermute | solution.py:30
  579.3 12.0 %collective-permute-done.11.rest_1_ = bf16[2,128,1024]{2,1,0:T(8,128)(2,1)S(1)} collective-permute-done((bf16[2,128,1024]{2,1,0:T(8,128)(2,1)}, bf16[2,128,1024]{2,1,0:T(8,128)(2,1)S(1)}, u32[]{:S(2)}, u32[]{:S(2)}) %collective-permute-start.11) | collective-permute-done | bytes 524320 | tf_op jit(solution)/shard_map/ppermute | solution.py:30
  591.4 8.5 %collective-permute-done.9.rest_0_ = bf16[2,128,1024]{2,1,0:T(8,128)(2,1)S(1)} collective-permute-done((bf16[2,128,1024]{2,1,0:T(8,128)(2,1)}, bf16[2,128,1024]{2,1,0:T(8,128)(2,1)S(1)}, u32[]{:S(2)}, u32[]{:S(2)}) %collective-permute-start.9) | collective-permute-done | bytes 524320 | tf_op jit(solution)/shard_map/ppermute | solution.py:30
  600.6 10.5 %collective-permute-done.15.rest_3_ = bf16[2,128,1024]{2,1,0:T(8,128)(2,1)S(1)} collective-permute-done((bf16[2,128,1024]{2,1,0:T(8,128)(2,1)}, bf16[2,128,1024]{2,1,0:T(8,128)(2,1)S(1)}, u32[]{:S(2)}, u32[]{:S(2)}) %collective-permute-start.15) | collective-permute-done | bytes 524320 | tf_op jit(solution)/shard_map/ppermute | solution.py:30
  614.0 4.3 owner_sum.3
  (57 shorter events, 21.1 us)
Async XLA Ops:
  0.6 1.6 copy-start.4
  2.2 1.6 copy-start.6
  5.8 4.7 copy-start.5
  5.8 28.0 %all-to-all-start.3 = ((bf16[4,2,128,1024]{3,2,1,0:T(8,128)(2,1)}), bf16[4,2,128,1024]{3,2,1,0:T(8,128)(2,1)}, u32[]{:S(2)}, u32[]{:S(2)}) async-start(bf16[4,2,128,1024]{3,2,1,0:T(8,128)(2,1)} %pack_rows.3), calls=%async_computation.3 | async-start | bytes 4194304 | tf_op jit(solution)/shard_map/all_to_all | solution.py:42
  10.5 1.6 copy-start.7
  14.1 24.5 %copy-start.20 = (s32[1,8,1]{1,2,0:T(1,128)S(1)}, s32[1,8,1]{1,2,0:T(1,128)}, u32[]{:S(2)}) copy-start(s32[1,8,1]{1,2,0:T(1,128)} %param.7) | copy-start | bytes 100
  33.8 27.1 %all-to-all-start = ((bf16[4,2,128,1024]{3,2,1,0:T(8,128)(2,1)}), bf16[4,2,128,1024]{3,2,1,0:T(8,128)(2,1)S(1)}, u32[]{:S(2)}, u32[]{:S(2)}) async-start(bf16[4,2,128,1024]{3,2,1,0:T(8,128)(2,1)} %pack_rows.2), calls=%async_computation | async-start | bytes 4194304 | tf_op jit(solution)/shard_map/all_to_all | solution.py:42
  38.6 2.2 copy-start
  60.8 1.3 copy-start.11
  62.2 30.7 %all-to-all-start.1 = ((bf16[4,2,128,1024]{3,2,1,0:T(8,128)(2,1)}), bf16[4,2,128,1024]{3,2,1,0:T(8,128)(2,1)}, u32[]{:S(2)}, u32[]{:S(2)}) async-start(bf16[4,2,128,1024]{3,2,1,0:T(8,128)(2,1)} %pick_near.2), calls=%async_computation.1 | async-start | bytes 4194304 | tf_op jit(solution)/shard_map/all_to_all | solution.py:36
  69.0 2.2 copy-start.1
  92.9 140.0 %all-to-all-start.4 = ((bf16[4,2,128,1024]{3,2,1,0:T(8,128)(2,1)}), bf16[4,2,128,1024]{3,2,1,0:T(8,128)(2,1)S(1)}, u32[]{:S(2)}, u32[]{:S(2)}) async-start(bf16[4,2,128,1024]{3,2,1,0:T(8,128)(2,1)} %pick_near.3), calls=%async_computation.4 | async-start | bytes 4194304 | tf_op jit(solution)/shard_map/all_to_all | solution.py:36
  98.4 2.2 copy-start.2
  100.6 7.3 %copy-start.19 = (s32[1,8,2]{1,2,0:T(2,128)S(1)}, s32[1,8,2]{1,2,0:T(2,128)}, u32[]{:S(2)}) copy-start(s32[1,8,2]{1,2,0:T(2,128)} %param.8) | copy-start | bytes 196
  102.7 32.7 %collective-permute-start = (bf16[2,128,1024]{2,1,0:T(8,128)(2,1)}, bf16[2,128,1024]{2,1,0:T(8,128)(2,1)S(1)}, u32[]{:S(2)}, u32[]{:S(2)}) collective-permute-start(bf16[2,128,1024]{2,1,0:T(8,128)(2,1)} %get-tuple-element.37), channel_id=1, source_target_pairs={{0,16},{4,20},{8,24},{12,28},{16,0},{20,4},{24,8},{28,12},{1,17},{... | collective-permute-start | bytes 1572872 | tf_op jit(solution)/shard_map/ppermute | solution.py:30
  105.1 68.0 %collective-permute-start.1 = (bf16[2,128,1024]{2,1,0:T(8,128)(2,1)}, bf16[2,128,1024]{2,1,0:T(8,128)(2,1)S(1)}, u32[]{:S(2)}, u32[]{:S(2)}) collective-permute-start(bf16[2,128,1024]{2,1,0:T(8,128)(2,1)} %get-tuple-element.38), channel_id=1, source_target_pairs={{0,20},{4,24},{8,28},{12,16},{20,0},{24,4},{28,8},{16,12},{1,21},{... | collective-permute-start | bytes 1572872 | tf_op jit(solution)/shard_map/ppermute | solution.py:30
  105.1 78.8 %collective-permute-start.2 = (bf16[2,128,1024]{2,1,0:T(8,128)(2,1)}, bf16[2,128,1024]{2,1,0:T(8,128)(2,1)}, u32[]{:S(2)}, u32[]{:S(2)}) collective-permute-start(bf16[2,128,1024]{2,1,0:T(8,128)(2,1)} %get-tuple-element.39), channel_id=1, source_target_pairs={{0,24},{4,28},{8,16},{12,20},{24,0},{28,4},{16,8},{20,12},{1,25},{... | collective-permute-start | bytes 1572872 | tf_op jit(solution)/shard_map/ppermute | solution.py:30
  106.6 88.5 %collective-permute-start.3 = (bf16[2,128,1024]{2,1,0:T(8,128)(2,1)}, bf16[2,128,1024]{2,1,0:T(8,128)(2,1)}, u32[]{:S(2)}, u32[]{:S(2)}) collective-permute-start(bf16[2,128,1024]{2,1,0:T(8,128)(2,1)} %get-tuple-element.40), channel_id=1, source_target_pairs={{0,28},{4,16},{8,20},{12,24},{28,0},{16,4},{20,8},{24,12},{1,29},{... | collective-permute-start | bytes 1572872 | tf_op jit(solution)/shard_map/ppermute | solution.py:30
  195.1 1.6 copy-start.12
  232.8 1.3 copy-start.9
  234.2 134.3 %all-to-all-start.2 = ((bf16[4,2,128,1024]{3,2,1,0:T(8,128)(2,1)}), bf16[4,2,128,1024]{3,2,1,0:T(8,128)(2,1)S(1)}, u32[]{:S(2)}, u32[]{:S(2)}) async-start(bf16[4,2,128,1024]{3,2,1,0:T(8,128)(2,1)} %get-tuple-element.41), calls=%async_computation.2 | async-start | bytes 4194304 | tf_op jit(solution)/shard_map/all_to_all | solution.py:42
  239.0 2.2 copy-start.3
  241.1 91.0 %copy-start.10 = (bf16[4,2,128,1024]{3,2,1,0:T(8,128)(2,1)S(1)}, bf16[4,2,128,1024]{3,2,1,0:T(8,128)(2,1)}, u32[]{:S(2)}) copy-start(bf16[4,2,128,1024]{3,2,1,0:T(8,128)(2,1)} %copy-done.9) | copy-start | bytes 6291460
  243.4 55.1 %collective-permute-start.4 = (bf16[2,128,1024]{2,1,0:T(8,128)(2,1)}, bf16[2,128,1024]{2,1,0:T(8,128)(2,1)S(1)}, u32[]{:S(2)}, u32[]{:S(2)}) collective-permute-start(bf16[2,128,1024]{2,1,0:T(8,128)(2,1)} %get-tuple-element.43), channel_id=1, source_target_pairs={{0,16},{4,20},{8,24},{12,28},{16,0},{20,4},{24,8},{28,12},{1,17},{... | collective-permute-start | bytes 1572872 | tf_op jit(solution)/shard_map/ppermute | solution.py:30
  243.4 67.2 %collective-permute-start.5 = (bf16[2,128,1024]{2,1,0:T(8,128)(2,1)}, bf16[2,128,1024]{2,1,0:T(8,128)(2,1)S(1)}, u32[]{:S(2)}, u32[]{:S(2)}) collective-permute-start(bf16[2,128,1024]{2,1,0:T(8,128)(2,1)} %get-tuple-element.45), channel_id=1, source_target_pairs={{0,20},{4,24},{8,28},{12,16},{20,0},{24,4},{28,8},{16,12},{1,21},{... | collective-permute-start | bytes 1572872 | tf_op jit(solution)/shard_map/ppermute | solution.py:30
  243.8 81.9 %collective-permute-start.6 = (bf16[2,128,1024]{2,1,0:T(8,128)(2,1)}, bf16[2,128,1024]{2,1,0:T(8,128)(2,1)S(1)}, u32[]{:S(2)}, u32[]{:S(2)}) collective-permute-start(bf16[2,128,1024]{2,1,0:T(8,128)(2,1)} %get-tuple-element.47), channel_id=1, source_target_pairs={{0,24},{4,28},{8,16},{12,20},{24,0},{28,4},{16,8},{20,12},{1,25},{... | collective-permute-start | bytes 1572872 | tf_op jit(solution)/shard_map/ppermute | solution.py:30
  246.4 85.8 %collective-permute-start.7 = (bf16[2,128,1024]{2,1,0:T(8,128)(2,1)}, bf16[2,128,1024]{2,1,0:T(8,128)(2,1)S(1)}, u32[]{:S(2)}, u32[]{:S(2)}) collective-permute-start(bf16[2,128,1024]{2,1,0:T(8,128)(2,1)} %get-tuple-element.49), channel_id=1, source_target_pairs={{0,28},{4,16},{8,20},{12,24},{28,0},{16,4},{20,8},{24,12},{1,29},{... | collective-permute-start | bytes 1572872 | tf_op jit(solution)/shard_map/ppermute | solution.py:30
  368.5 25.5 %copy-start.18 = (bf16[4,2,128,1024]{3,2,1,0:T(8,128)(2,1)S(1)}, bf16[4,2,128,1024]{3,2,1,0:T(8,128)(2,1)}, u32[]{:S(2)}) copy-start(bf16[4,2,128,1024]{3,2,1,0:T(8,128)(2,1)} %get-tuple-element.70) | copy-start | bytes 6291460
  424.6 6.4 %copy-start.22 = (bf16[2,128,1024]{2,1,0:T(8,128)(2,1)S(1)}, bf16[2,128,1024]{2,1,0:T(8,128)(2,1)}, u32[]{:S(2)}) copy-start(bf16[2,128,1024]{2,1,0:T(8,128)(2,1)} %get-tuple-element.60) | copy-start | bytes 1572868
  424.6 8.0 %copy-start.21 = (bf16[2,128,1024]{2,1,0:T(8,128)(2,1)S(1)}, bf16[2,128,1024]{2,1,0:T(8,128)(2,1)}, u32[]{:S(2)}) copy-start(bf16[2,128,1024]{2,1,0:T(8,128)(2,1)} %get-tuple-element.64) | copy-start | bytes 1572868
  424.6 187.3 %all-to-all-start.6 = ((bf16[4,2,128,1024]{3,2,1,0:T(8,128)(2,1)}), bf16[4,2,128,1024]{3,2,1,0:T(8,128)(2,1)}, u32[]{:S(2)}, u32[]{:S(2)}) async-start(bf16[4,2,128,1024]{3,2,1,0:T(8,128)(2,1)} %get-tuple-element.53), calls=%async_computation.6 | async-start | bytes 4194304 | tf_op jit(solution)/shard_map/all_to_all | solution.py:36
  431.1 34.6 %collective-permute-start.8 = (bf16[2,128,1024]{2,1,0:T(8,128)(2,1)}, bf16[2,128,1024]{2,1,0:T(8,128)(2,1)S(1)}, u32[]{:S(2)}, u32[]{:S(2)}) collective-permute-start(bf16[2,128,1024]{2,1,0:T(8,128)(2,1)} %get-tuple-element.56), channel_id=1, source_target_pairs={{0,16},{4,20},{8,24},{12,28},{16,0},{20,4},{24,8},{28,12},{1,17},{... | collective-permute-start | bytes 1572872 | tf_op jit(solution)/shard_map/ppermute | solution.py:30
  431.1 70.4 %collective-permute-start.10 = (bf16[2,128,1024]{2,1,0:T(8,128)(2,1)S(1)}, bf16[2,128,1024]{2,1,0:T(8,128)(2,1)S(1)}, u32[]{:S(2)}, u32[]{:S(2)}) collective-permute-start(bf16[2,128,1024]{2,1,0:T(8,128)(2,1)S(1)} %copy-done.22), channel_id=1, source_target_pairs={{0,20},{4,24},{8,28},{12,16},{20,0},{24,4},{28,8},{16,12},{1,21},{... | collective-permute-start | bytes 1572872 | tf_op jit(solution)/shard_map/ppermute | solution.py:30
  432.6 96.1 %collective-permute-start.12 = (bf16[2,128,1024]{2,1,0:T(8,128)(2,1)S(1)}, bf16[2,128,1024]{2,1,0:T(8,128)(2,1)S(1)}, u32[]{:S(2)}, u32[]{:S(2)}) collective-permute-start(bf16[2,128,1024]{2,1,0:T(8,128)(2,1)S(1)} %copy-done.21), channel_id=1, source_target_pairs={{0,24},{4,28},{8,16},{12,20},{24,0},{28,4},{16,8},{20,12},{1,25},{... | collective-permute-start | bytes 1572872 | tf_op jit(solution)/shard_map/ppermute | solution.py:30
  432.6 127.9 %collective-permute-start.14 = (bf16[2,128,1024]{2,1,0:T(8,128)(2,1)}, bf16[2,128,1024]{2,1,0:T(8,128)(2,1)S(1)}, u32[]{:S(2)}, u32[]{:S(2)}) collective-permute-start(bf16[2,128,1024]{2,1,0:T(8,128)(2,1)} %get-tuple-element.68), channel_id=1, source_target_pairs={{0,28},{4,16},{8,20},{12,24},{28,0},{16,4},{20,8},{24,12},{1,29},{... | collective-permute-start | bytes 1572872 | tf_op jit(solution)/shard_map/ppermute | solution.py:30
  528.8 50.6 %collective-permute-start.13 = (bf16[2,128,1024]{2,1,0:T(8,128)(2,1)}, bf16[2,128,1024]{2,1,0:T(8,128)(2,1)S(1)}, u32[]{:S(2)}, u32[]{:S(2)}) collective-permute-start(bf16[2,128,1024]{2,1,0:T(8,128)(2,1)} %get-tuple-element.65), channel_id=1, source_target_pairs={{0,24},{4,28},{8,16},{12,20},{24,0},{28,4},{16,8},{20,12},{1,25},{... | collective-permute-start | bytes 1572872 | tf_op jit(solution)/shard_map/ppermute | solution.py:30
  528.9 62.4 %collective-permute-start.11 = (bf16[2,128,1024]{2,1,0:T(8,128)(2,1)}, bf16[2,128,1024]{2,1,0:T(8,128)(2,1)S(1)}, u32[]{:S(2)}, u32[]{:S(2)}) collective-permute-start(bf16[2,128,1024]{2,1,0:T(8,128)(2,1)} %get-tuple-element.61), channel_id=1, source_target_pairs={{0,20},{4,24},{8,28},{12,16},{20,0},{24,4},{28,8},{16,12},{1,21},{... | collective-permute-start | bytes 1572872 | tf_op jit(solution)/shard_map/ppermute | solution.py:30
  531.9 68.0 %collective-permute-start.9 = (bf16[2,128,1024]{2,1,0:T(8,128)(2,1)}, bf16[2,128,1024]{2,1,0:T(8,128)(2,1)S(1)}, u32[]{:S(2)}, u32[]{:S(2)}) collective-permute-start(bf16[2,128,1024]{2,1,0:T(8,128)(2,1)} %get-tuple-element.57), channel_id=1, source_target_pairs={{0,16},{4,20},{8,24},{12,28},{16,0},{20,4},{24,8},{28,12},{1,17},{... | collective-permute-start | bytes 1572872 | tf_op jit(solution)/shard_map/ppermute | solution.py:30
  560.5 50.6 %collective-permute-start.15 = (bf16[2,128,1024]{2,1,0:T(8,128)(2,1)}, bf16[2,128,1024]{2,1,0:T(8,128)(2,1)S(1)}, u32[]{:S(2)}, u32[]{:S(2)}) collective-permute-start(bf16[2,128,1024]{2,1,0:T(8,128)(2,1)} %get-tuple-element.69), channel_id=1, source_target_pairs={{0,28},{4,16},{8,20},{12,24},{28,0},{16,4},{20,8},{24,12},{1,29},{... | collective-permute-start | bytes 1572872 | tf_op jit(solution)/shard_map/ppermute | solution.py:30
  563.8 1.6 copy-start.8
  565.4 2.9 copy-start.13
  599.9 0.8 copy-start.14
  611.1 0.8 copy-start.16
  611.9 1.0 copy-start.15
  612.9 1.0 copy-start.17

commit v5 on v3

v5 whole, which is shorter than its diff:
```python
import functools

import jax
import jax.numpy as jnp
from jax import lax
from jax.experimental import pallas as pl
from jax.experimental.pallas import tpu as pltpu
from jax.sharding import PartitionSpec as P

DH = 128
BLOCK = 64
NBLEN = 128
GROUPS = 4
DEPTH = 2
F32 = jnp.float32
BF16 = jnp.bfloat16
VMEM_BYTES = 40 * 1024 * 1024


def partner(index, step, count):
    if count & (count - 1) == 0:
        return index ^ step
    return (step - index) % count


def exchange(array, axis, step, count):
    pairs = [(i, partner(i, step, count)) for i in range(count)]
    return lax.ppermute(array, axis, pairs)


def swap_rows(pieces):
    count = len(pieces)
    return [pieces[0]] + [exchange(pieces[step], "seq", step, count) for step in range(1, count)]


def swap_pool(array):
    return lax.all_to_all(array, "enc", split_axis=0, concat_axis=0, tiled=True)


def after(array, earlier):
    return lax.optimization_barrier((array, earlier))[0]


def in_hbm(shape):
    return pltpu.HBM(shape, BF16)


def cost(moved, flops=0, exps=0):
    return pl.CostEstimate(flops=flops, bytes_accessed=moved, transcendentals=exps)


PARAMS = pltpu.CompilerParams(vmem_limit_bytes=VMEM_BYTES)
SCALARS = pl.BlockSpec(memory_space=pltpu.SMEM)
ANYWHERE = pl.BlockSpec(memory_space=pl.ANY)
IN_HBM = pl.BlockSpec(memory_space=pltpu.HBM)


def pack_kernel(first, width, q_ref, g_ref, *rest):
    outs, sems = rest[:-1], rest[-1]
    parts, chunk = len(outs), outs[0].shape[-1]
    me = lax.axis_index("seq")
    copies = []
    for step, out in enumerate(outs):
        start = pl.multiple_of(partner(me, step, parts) * width + first, DH)
        for n, ref in enumerate((q_ref, g_ref)):
            source = ref.at[0, :, pl.ds(start, chunk)]
            copies.append(pltpu.make_async_copy(source, out.at[n], sems.at[2 * step + n]))
            copies[-1].start()
    for copy in copies:
        copy.wait()


def pack(first, chunk, queries, grads, width, parts):
    shape = (2, queries.shape[1], chunk)
    return pl.pallas_call(
        functools.partial(pack_kernel, first, width),
        grid=(1,),
        in_specs=[IN_HBM, IN_HBM],
        out_specs=[pl.BlockSpec(shape, lambda i: (0, 0, 0))] * parts,
        out_shape=[in_hbm(shape)] * parts,
        scratch_shapes=[pltpu.SemaphoreType.DMA((2 * parts,))],
        compiler_params=PARAMS,
        cost_estimate=cost(8 * parts * queries.shape[1] * chunk),
        name="pack_rows",
    )(queries, grads)


def unpack_kernel(firsts, width, *refs):
    ins, (ctx_ref, gq_ref, sems) = refs[:-3], refs[-3:]
    parts = len(ins) // len(firsts)
    me = lax.axis_index("seq")
    copies = []
    for n, src in enumerate(ins):
        first, step = firsts[n // parts], n % parts
        start = pl.multiple_of(partner(me, step, parts) * width + first, DH)
        for k, ref in enumerate((ctx_ref, gq_ref)):
            target = ref.at[0, :, pl.ds(start, src.shape[-1])]
            copies.append(pltpu.make_async_copy(src.at[k], target, sems.at[2 * n + k]))
            copies[-1].start()
    for copy in copies:
        copy.wait()


def unpack(pieces, firsts, width, shape):
    flat = [array for piece in pieces for array in piece]
    return pl.pallas_call(
        functools.partial(unpack_kernel, firsts, width),
        grid=(1,),
        in_specs=[pl.BlockSpec(array.shape, lambda i: (0, 0, 0)) for array in flat],
        out_specs=[IN_HBM, IN_HBM],
        out_shape=[in_hbm(shape)] * 2,
        scratch_shapes=[pltpu.SemaphoreType.DMA((2 * len(flat),))],
        compiler_params=PARAMS,
        cost_estimate=cost(8 * shape[1] * shape[2]),
        name="unpack_rows",
    )(*flat)


def pick_kernel(first, split, seqs, lists, pool_ref, *rest):
    outs, sems = rest[:-1], rest[-1]
    me = lax.axis_index("enc")
    copies = []
    for step in range(seqs):
        if split:
            peer, out = partner(me, step, seqs), outs[step]
        else:
            peer, out = step, outs[0].at[step]
        chunk = out.shape[-1]
        source = pool_ref.at[lists[0, peer, 0], :, :, first : first + chunk]
        copies.append(pltpu.make_async_copy(source, out, sems.at[step]))
        copies[-1].start()
    for copy in copies:
        copy.wait()


def pick(first, chunk, split, send_lists, kv_pool):
    seqs = send_lists.shape[1]
    shapes = [(2, NBLEN, chunk)] * seqs if split else [(seqs, 2, NBLEN, chunk)]
    return pl.pallas_call(
        functools.partial(pick_kernel, first, split, seqs),
        grid=(1,),
        in_specs=[SCALARS, IN_HBM],
        out_specs=[pl.BlockSpec(shape, lambda i, n=len(shape): (0,) * n) for shape in shapes],
        out_shape=[in_hbm(shape) for shape in shapes],
        scratch_shapes=[pltpu.SemaphoreType.DMA((seqs,))],
        compiler_params=PARAMS,
        cost_estimate=cost(8 * seqs * NBLEN * chunk),
        name="pick_split" if split else "pick_whole",
    )(send_lists, kv_pool)


def dot(left, right, left_dim, right_dim):
    return lax.dot_general(
        left, right, (((left_dim,), (right_dim,)), ((), ())), preferred_element_type=F32
    )


def attend_kernel(seqs, parts, split, uses, *rest):
    pieces = seqs if split else 1
    rows_in, rest = rest[:parts], rest[parts:]
    kv_in, rest = rest[:pieces], rest[pieces:]
    rows_out, rest = rest[:parts], rest[parts:]
    kv_out, rest = rest[:pieces], rest[pieces:]
    held, rows, made, sums = rest if split else (kv_in[0], *rest)
    scale = DH ** (-0.5)
    me, mine = lax.axis_index("enc"), lax.axis_index("seq")

    if split:
        for step in range(seqs):
            held[partner(me, step, seqs)] = kv_in[step][...]
    for step in range(parts):
        for n in range(2):
            piece = rows_in[step][n].astype(F32)
            rows[partner(mine, step, parts), n] = pltpu.roll(piece, 1, 0)
    rows[parts] = jnp.zeros(rows.shape[1:], F32)
    made[0, :, :BLOCK] = jnp.zeros((2, BLOCK, DH), F32)
    sums[...] = jnp.zeros_like(sums)
    first_row = lax.broadcasted_iota(jnp.int32, (BLOCK, DH), 0) == 0

    def one_block(block, q, g):
        first, second = uses[0, block, 0], uses[0, block, 1]
        keys = jnp.concatenate([held[first, 0], held[second, 0]], axis=0)
        values = jnp.concatenate([held[first, 1], held[second, 1]], axis=0)
        scores = dot(q, keys, 1, 1) * scale
        weights = jnp.exp(scores - jnp.max(scores, axis=1, keepdims=True))
        probs = weights / jnp.sum(weights, axis=1, keepdims=True)
        probs_low = probs.astype(BF16)
        out = dot(probs_low, values, 1, 0)
        grad_probs = dot(g, values, 1, 1)
        inner = jnp.sum(probs * grad_probs, axis=1, keepdims=True)
        grad_scores = (probs * (grad_probs - inner) * scale).astype(BF16)
        grad_q = dot(grad_scores, keys, 1, 0)
        grad_keys = dot(grad_scores, q, 0, 0)
        grad_values = dot(probs_low, g, 0, 0)
        sums[first, 0] += grad_keys[:NBLEN]
        sums[second, 0] += grad_keys[NBLEN:]
        sums[first, 1] += grad_values[:NBLEN]
        sums[second, 1] += grad_values[NBLEN:]
        return out, grad_q

    def one_part(part, carry):
        q, g = (rows[part, n, BLOCK:].astype(BF16) for n in range(2))
        for n, result in enumerate(one_block(2 * part, q, g)):
            made[part, n, BLOCK:] = result
        q, g = (
            jnp.where(first_row, rows[part, n, :BLOCK], rows[part + 1, n, :BLOCK]).astype(BF16)
            for n in range(2)
        )
        for n, result in enumerate(one_block(2 * part + 1, q, g)):
            made[part + 1, n, :BLOCK] = result
            made[part, n, :1] = result[:1]
        return carry

    if parts <= 4:
        for part in range(parts):
            one_part(part, 0)
    else:
        lax.fori_loop(0, parts, one_part, 0)

    for step in range(parts):
        for n in range(2):
            piece = made[partner(mine, step, parts), n]
            rows_out[step][n] = pltpu.roll(piece, 2 * BLOCK - 1, 0).astype(BF16)
    if split:
        for step in range(seqs):
            kv_out[step][...] = sums[partner(me, step, seqs)].astype(BF16)
    else:
        kv_out[0][...] = sums[...].astype(BF16)


def attend(first, uses, rows_in, kv_in):
    parts, part_rows = len(rows_in), rows_in[0].shape[1]
    split = len(kv_in) > 1
    seqs = len(kv_in) if split else kv_in[0].shape[0]
    chunk = kv_in[0].shape[-1]
    heads = chunk // DH
    skip = first // DH
    rows_block = (2, part_rows, DH)
    if split:
        kv_spec = pl.BlockSpec((2, NBLEN, DH), lambda i: (0, 0, i))
    else:
        kv_spec = pl.BlockSpec((seqs, 2, NBLEN, DH), lambda i: (0, 0, 0, i))
    held = [pltpu.VMEM((seqs, 2, NBLEN, DH), BF16)] if split else []
    pairs = heads * parts * part_rows * 2 * NBLEN
    outs = pl.pallas_call(
        functools.partial(attend_kernel, seqs, parts, split),
        grid=(heads,),
        in_specs=[SCALARS]
        + [pl.BlockSpec(rows_block, lambda i: (0, 0, skip + i))] * parts
        + [kv_spec] * len(kv_in),
        out_specs=[pl.BlockSpec(rows_block, lambda i: (0, 0, i))] * parts
        + [kv_spec] * len(kv_in),
        scratch_shapes=held
        + [
            pltpu.VMEM((parts + 1, 2, part_rows, DH), F32),
            pltpu.VMEM((parts + 1, 2, part_rows, DH), F32),
            pltpu.VMEM((seqs, 2, NBLEN, DH), F32),
        ],
        out_shape=[in_hbm((2, part_rows, chunk))] * parts
        + [in_hbm(array.shape) for array in kv_in],
        compiler_params=PARAMS,
        cost_estimate=cost(8 * (seqs + parts) * NBLEN * chunk, 12 * DH * pairs, pairs),
        name="attend_blocks",
    )(uses, *rows_in, *kv_in)
    return outs[:parts], outs[parts:]


def owner_kernel(seqs, pieces, lists, *rest):
    ins, out_ref, acc = rest[:pieces], rest[-2], rest[-1]
    me = lax.axis_index("enc")
    acc[...] = jnp.zeros_like(acc)
    for step in range(seqs):
        if pieces > 1:
            acc[lists[0, partner(me, step, seqs), 0]] += ins[step][...].astype(F32)
        else:
            acc[lists[0, step, 0]] += ins[0][step].astype(F32)
    out_ref[...] = acc[...].astype(BF16)


def owner_sum(first, send_lists, back, shape, so_far):
    seqs = send_lists.shape[1]
    pieces, chunk = len(back), back[0].shape[-1]
    wide = min(chunk, 256)
    skip, steps = first // wide, chunk // wide
    extra = [] if so_far is None else [so_far]
    if pieces > 1:
        spec = pl.BlockSpec((2, NBLEN, wide), lambda i: (0, 0, i))
    else:
        spec = pl.BlockSpec((seqs, 2, NBLEN, wide), lambda i: (0, 0, 0, i))
    return pl.pallas_call(
        functools.partial(owner_kernel, seqs, pieces),
        grid=(steps,),
        in_specs=[SCALARS] + [spec] * pieces + [ANYWHERE] * len(extra),
        out_specs=pl.BlockSpec(
            (shape[0], 2, NBLEN, wide), lambda i: (0, 0, 0, skip + i)
        ),
        scratch_shapes=[pltpu.VMEM((shape[0], 2, NBLEN, wide), F32)],
        out_shape=in_hbm(shape),
        input_output_aliases={pieces + 1: 0} if extra else {},
        compiler_params=PARAMS,
        cost_estimate=cost(4 * (seqs + shape[0]) * NBLEN * chunk, seqs * 2 * NBLEN * chunk),
        name="owner_sum",
    )(send_lists, *back, *extra)


class Chain:
    def __init__(self, count):
        self.count, self.done = count, []

    def swap(self, pieces):
        got = [pieces[0]] + [None] * (self.count - 1)
        half = self.count // 2
        for step in list(range(half, self.count)) + list(range(1, half)):
            piece = pieces[step]
            if len(self.done) >= DEPTH:
                piece = after(piece, self.done[-DEPTH])
            got[step] = exchange(piece, "enc", step, self.count)
            self.done.append(got[step])
        return got


def local(seqs, parts, queries, kv_pool, send_lists, block_slots, grad_context):
    width = kv_pool.shape[-1]
    groups = min(GROUPS, width // DH)
    chunk = width // groups
    chain = Chain(seqs)

    def swap(split, pieces):
        return chain.swap(pieces) if split else [swap_pool(pieces[0])]

    fetched, rows = [], []
    for group in range(groups):
        split = group % 2 == 1
        picked = pick(group * chunk, chunk, split, send_lists, kv_pool)
        send_lists = after(send_lists, picked[0])
        if group == 3:
            picked = after(picked, fetched[0])
        fetched.append(swap(split, picked))
        rows.append(swap_rows(pack(group * chunk, chunk, queries, grad_context, width, parts)))
    pool_grads = None
    token_parts, returns = [], []
    for group in range(groups):
        rows_out, kv_out = attend(0, block_slots, rows[group], fetched[group])
        block_slots = after(block_slots, rows_out[0])
        returns.append(swap(group % 2 == 1, kv_out))
        token_parts.append(swap_rows(rows_out))
    firsts = [group * chunk for group in range(groups)]
    context, grad_queries = unpack(token_parts, firsts, width, queries.shape)
    for group in range(groups):
        pool_grads = owner_sum(
            group * chunk, send_lists, returns[group], kv_pool.shape, pool_grads
        )
    return (context, grad_queries, pool_grads)


def solution(mesh):
    in_specs = (
        P("enc", "seq", None),
        P("enc", None, None, "seq"),
        P("enc", None, None),
        P("enc", None, None),
        P("enc", "seq", None),
    )
    out_specs = (P("enc", "seq", None), P("enc", "seq", None), P("enc", None, None, "seq"))
    body = functools.partial(local, mesh.shape["enc"], mesh.shape["seq"])
    return jax.shard_map(body, mesh=mesh, in_specs=in_specs, out_specs=out_specs, check_vma=False)
```

time: 537 us -> 552 us (1.028); the launches traced: 536 us -> 545 us
  starting transfers between devices: 51.1 us -> 100 us
  waiting for transfers between devices: 331 us -> 289 us
  Pallas kernels: 93.4 us -> 102 us
  local copies, waits for them, and re-layouts: 58.9 us -> 51.8 us
    ppermute x28 -> x52, waiting for transfers between devices: 331 us -> 243 us  [exchange(): return lax.ppermute(array, axis, pairs)]
    all_to_all x4, waiting for transfers between devices: 0.01 us -> 46.1 us  [swap_pool(): return lax.all_to_all(array, 'enc', split_axis=0, concat_axis=0, tiled=True)]
    ppermute x28 -> x52, starting transfers between devices: 34.2 us -> 74.1 us  [exchange(): return lax.ppermute(array, axis, pairs)]
    all_to_all x4, starting transfers between devices: 17 us -> 26.1 us  [swap_pool(): return lax.all_to_all(array, 'enc', split_axis=0, concat_axis=0, tiled=True)]
    pallas_call x11 -> x17, Pallas kernels: 93.4 us -> 102 us  [the longest x4 75.3 us: attend(): pl.pallas_call(functools.partial(attend_kernel, seqs, parts, split), grid...]
    unnamed x132 -> x178, local copies, waits for them, and re-layouts: 58.6 us -> 51.2 us
  transfers between devices with their start and end apart: 32 -> 56, of which waited for: 17 -> 26; matrix products, arithmetic and copies ran while one was open for 0% -> 0% of each run, Pallas kernels for 16% -> 18%
where the time goes in v5:
time: 552 us; the launch traced here: 545 us
  waiting for transfers between devices  289 us (52%)
  Pallas kernels  102 us (18%)
  starting transfers between devices  100 us (18%)
  local copies, waits for them, and re-layouts  51.8 us (9%)
    ppermute x52, waiting for transfers between devices, exchange(): return lax.ppermute(array, axis, pairs)  243 us
    pallas_call x4, Pallas kernels, attend(): pl.pallas_call(functools.partial(attend_kernel, seqs, parts, split), grid...  75.3 us
    ppermute x52, starting transfers between devices, exchange(): return lax.ppermute(array, axis, pairs)  74.1 us
    unnamed x178, local copies, waits for them, and re-layouts  51.2 us
    all_to_all x4, waiting for transfers between devices, swap_pool(): return lax.all_to_all(array, 'enc', split_axis=0, concat_axis=0, tiled=True)  46.1 us
    all_to_all x4, starting transfers between devices, swap_pool(): return lax.all_to_all(array, 'enc', split_axis=0, concat_axis=0, tiled=True)  26.1 us
  transfers between devices with their start and end apart: 56, of which 26 were waited for; matrix products, arithmetic and copies ran while one was open for 0% of the time, Pallas kernels for 18%

profile of v5, /device:TPU:15, one launch (start us, length us, event | category | flops | bytes accessed | tf_op | source)
XLA Modules:
  0.0 545.0 jit_solution(4713420243901382683)
XLA Ops:
  5.8 5.6 %all-to-all-start = ((bf16[8,2,128,512]{3,2,1,0:T(8,128)(2,1)}), bf16[8,2,128,512]{3,2,1,0:T(8,128)(2,1)}, u32[]{:S(2)}, u32[]{:S(2)}) async-start(bf16[8,2,128,512]{3,2,1,0:T(8,128)(2,1)} %pick_whole.2), calls=%async_computation | async-start | bytes 4194304 | tf_op jit(solution)/shard_map/all_to_all | solution.py:37
  11.5 2.2 copy-done.1
  13.7 2.2 pick_split.2
  20.4 36.5 %all-to-all-done.rest_4_ = bf16[8,2,128,512]{3,2,1,0:T(8,128)(2,1)} async-done(((bf16[8,2,128,512]{3,2,1,0:T(8,128)(2,1)}), bf16[8,2,128,512]{3,2,1,0:T(8,128)(2,1)}, u32[]{:S(2)}, u32[]{:S(2)}) %all-to-all-start) | async-done | bytes 2097184 | tf_op jit(solution)/shard_map/all_to_all | solution.py:37
  56.9 7.9 %all-to-all-start.1 = ((bf16[8,2,128,512]{3,2,1,0:T(8,128)(2,1)}), bf16[8,2,128,512]{3,2,1,0:T(8,128)(2,1)}, u32[]{:S(2)}, u32[]{:S(2)}) async-start(bf16[8,2,128,512]{3,2,1,0:T(8,128)(2,1)} %pick_whole.3), calls=%async_computation.1 | async-start | bytes 4194304 | tf_op jit(solution)/shard_map/all_to_all | solution.py:37
  70.5 5.0 collective-permute-done.rest_1_
  75.5 5.6 %collective-permute-done.2.rest_3_ = bf16[2,128,512]{2,1,0:T(8,128)(2,1)S(1)} collective-permute-done((bf16[2,128,512]{2,1,0:T(8,128)(2,1)}, bf16[2,128,512]{2,1,0:T(8,128)(2,1)S(1)}, u32[]{:S(2)}, u32[]{:S(2)}) %collective-permute-start.2) | collective-permute-done | bytes 262176 | tf_op jit(solution)/shard_map/ppermute | solution.py:28
  82.0 18.7 %attend_blocks.4 = (bf16[2,128,512]{2,1,0:T(8,128)(2,1)}, bf16[2,128,512]{2,1,0:T(8,128)(2,1)}, bf16[2,128,512]{2,1,0:T(8,128)(2,1)}, bf16[2,128,512]{2,1,0:T(8,128)(2,1)}, bf16[8,2,128,512]{3,2,1,0:T(8,128)(2,1)}) custom-call(s32[1,8,2]{2,1,0:T(8,128)S(1)} %copy.12.uses, bf16[2,128,512]{2,1,0:T(8,128)(2,1)S(1)} %copy-done.69, ...), custom_call_target="tpu_custom_call" | custom-call | flops 805306368 | bytes 6291456 | tf_op jit(solution)/shard_map/attend_blocks/pallas_call | solution.py:245
  100.7 9.6 %all-to-all-done.1.rest_4_ = bf16[8,2,128,512]{3,2,1,0:T(8,128)(2,1)} async-done(((bf16[8,2,128,512]{3,2,1,0:T(8,128)(2,1)}), bf16[8,2,128,512]{3,2,1,0:T(8,128)(2,1)}, u32[]{:S(2)}, u32[]{:S(2)}) %all-to-all-start.1) | async-done | bytes 2097184 | tf_op jit(solution)/shard_map/all_to_all | solution.py:37
  110.3 8.1 %all-to-all-start.3 = ((bf16[8,2,128,512]{3,2,1,0:T(8,128)(2,1)}), bf16[8,2,128,512]{3,2,1,0:T(8,128)(2,1)}, u32[]{:S(2)}, u32[]{:S(2)}) async-start(bf16[8,2,128,512]{3,2,1,0:T(8,128)(2,1)} %get-tuple-element.220), calls=%async_computation.3 | async-start | bytes 4194304 | tf_op jit(solution)/shard_map/all_to_all | solution.py:37
  121.3 59.4 %collective-permute-done.9.rest_8_ = bf16[2,128,512]{2,1,0:T(8,128)(2,1)S(1)} collective-permute-done((bf16[2,128,512]{2,1,0:T(8,128)(2,1)S(1)}, bf16[2,128,512]{2,1,0:T(8,128)(2,1)S(1)}, u32[]{:S(2)}, u32[]{:S(2)}) %collective-permute-start.9) | collective-permute-done | bytes 262176 | tf_op jit(solution)/shard_map/ppermute | solution.py:28
  181.6 10.3 %collective-permute-done.12.rest_9_ = bf16[2,128,512]{2,1,0:T(8,128)(2,1)S(1)} collective-permute-done((bf16[2,128,512]{2,1,0:T(8,128)(2,1)S(1)}, bf16[2,128,512]{2,1,0:T(8,128)(2,1)S(1)}, u32[]{:S(2)}, u32[]{:S(2)}) %collective-permute-start.12) | collective-permute-done | bytes 262176 | tf_op jit(solution)/shard_map/ppermute | solution.py:28
  191.9 2.2 collective-permute-start.13
  194.1 10.7 %collective-permute-done.10.rest_10_ = bf16[2,128,512]{2,1,0:T(8,128)(2,1)S(1)} collective-permute-done((bf16[2,128,512]{2,1,0:T(8,128)(2,1)}, bf16[2,128,512]{2,1,0:T(8,128)(2,1)S(1)}, u32[]{:S(2)}, u32[]{:S(2)}) %collective-permute-start.10) | collective-permute-done | bytes 262176 | tf_op jit(solution)/shard_map/ppermute | solution.py:28
  212.4 2.5 collective-permute-start.15
  219.2 3.6 collective-permute-done.8.rest_3_
  223.5 3.2 collective-permute-start.21
  231.5 18.9 %attend_blocks.5 = (bf16[2,128,512]{2,1,0:T(8,128)(2,1)}, bf16[2,128,512]{2,1,0:T(8,128)(2,1)}, bf16[2,128,512]{2,1,0:T(8,128)(2,1)}, bf16[2,128,512]{2,1,0:T(8,...) custom-call(s32[1,8,2]{2,1,0:T(8,128)S(1)} %copy.14.uses, ...), custom_call_target="tpu_custom_call" | custom-call | flops 805306368 | bytes 6291456 | tf_op jit(solution)/shard_map/attend_blocks/pallas_call | solution.py:245
  251.5 18.8 %attend_blocks.6 = (bf16[2,128,512]{2,1,0:T(8,128)(2,1)}, bf16[2,128,512]{2,1,0:T(8,128)(2,1)}, bf16[2,128,512]{2,1,0:T(8,128)(2,1)}, bf16[2,128,512]{2,1,0:T(8,128)(2,1)}, bf16[8,2,128,512]{3,2,1,0:T(8,128)(2,1)}) custom-call(s32[1,8,2]{2,1,0:T(8,128)S(1)} %copy.16.uses, bf16[2,128,512]{2,1,0:T(8,128)(2,1)S(1)} %copy-done.57, ...), custom_call_target="tpu_custom_call" | custom-call | flops 805306368 | bytes 6291456 | tf_op jit(solution)/shard_map/attend_blocks/pallas_call | solution.py:245
  270.3 4.5 all-to-all-start.2
  277.1 2.2 pick_split.3
  283.4 53.7 %collective-permute-done.28.rest_8_ = bf16[2,128,512]{2,1,0:T(8,128)(2,1)S(1)} collective-permute-done((bf16[2,128,512]{2,1,0:T(8,128)(2,1)}, bf16[2,128,512]{2,1,0:T(8,128)(2,1)S(1)}, u32[]{:S(2)}, u32[]{:S(2)}) %collective-permute-start.28) | collective-permute-done | bytes 262176 | tf_op jit(solution)/shard_map/ppermute | solution.py:28
  338.1 10.2 %collective-permute-done.31.rest_9_ = bf16[2,128,512]{2,1,0:T(8,128)(2,1)S(1)} collective-permute-done((bf16[2,128,512]{2,1,0:T(8,128)(2,1)}, bf16[2,128,512]{2,1,0:T(8,128)(2,1)S(1)}, u32[]{:S(2)}, u32[]{:S(2)}) %collective-permute-start.31) | collective-permute-done | bytes 262176 | tf_op jit(solution)/shard_map/ppermute | solution.py:28
  348.3 2.2 collective-permute-start.32
  350.6 10.6 %collective-permute-done.29.rest_10_ = bf16[2,128,512]{2,1,0:T(8,128)(2,1)S(1)} collective-permute-done((bf16[2,128,512]{2,1,0:T(8,128)(2,1)}, bf16[2,128,512]{2,1,0:T(8,128)(2,1)S(1)}, u32[]{:S(2)}, u32[]{:S(2)}) %collective-permute-start.29) | collective-permute-done | bytes 262176 | tf_op jit(solution)/shard_map/ppermute | solution.py:28
  362.5 4.5 collective-permute-done.32.rest_11_
  368.9 6.0 %collective-permute-done.33.rest_6_ = bf16[2,128,512]{2,1,0:T(8,128)(2,1)S(1)} collective-permute-done((bf16[2,128,512]{2,1,0:T(8,128)(2,1)}, bf16[2,128,512]{2,1,0:T(8,128)(2,1)S(1)}, u32[]{:S(2)}, u32[]{:S(2)}) %collective-permute-start.33) | collective-permute-done | bytes 262176 | tf_op jit(solution)/shard_map/ppermute | solution.py:28
  375.0 7.3 %collective-permute-done.34.rest_7_ = bf16[2,128,512]{2,1,0:T(8,128)(2,1)S(1)} collective-permute-done((bf16[2,128,512]{2,1,0:T(8,128)(2,1)}, bf16[2,128,512]{2,1,0:T(8,128)(2,1)S(1)}, u32[]{:S(2)}, u32[]{:S(2)}) %collective-permute-start.34) | collective-permute-done | bytes 262176 | tf_op jit(solution)/shard_map/ppermute | solution.py:28
  382.3 3.3 collective-permute-start.38
  386.0 6.2 %collective-permute-start.45 = (bf16[2,128,512]{2,1,0:T(8,128)(2,1)S(1)}, bf16[2,128,512]{2,1,0:T(8,128)(2,1)S(1)}, u32[]{:S(2)}, u32[]{:S(2)}) collective-permute-start(bf16[2,128,512]{2,1,0:T(8,128)(2,1)S(1)} %copy-done.82), channel_id=1, source_target_pairs={{0,24},{4,28},{8,16},{12,20},{16,8},{20,12},{24,0},{28,4},{1,25},{... | collective-permute-start | bytes 786440 | tf_op jit(solution)/shard_map/ppermute | solution.py:28
  392.2 10.6 %collective-permute-done.38.rest_5_ = bf16[2,128,512]{2,1,0:T(8,128)(2,1)S(1)} collective-permute-done((bf16[2,128,512]{2,1,0:T(8,128)(2,1)S(1)}, bf16[2,128,512]{2,1,0:T(8,128)(2,1)S(1)}, u32[]{:S(2)}, u32[]{:S(2)}) %collective-permute-start.38) | collective-permute-done | bytes 262176 | tf_op jit(solution)/shard_map/ppermute | solution.py:28
  402.8 4.0 collective-permute-start.39
  408.6 2.3 collective-permute-start.27
  410.9 4.7 collective-permute-done.45.rest_6_
  415.5 3.4 collective-permute-start.46
  418.9 3.5 collective-permute-done.39.rest_7_
  431.8 18.9 %attend_blocks.7 = (bf16[2,128,512]{2,1,0:T(8,128)(2,1)}, bf16[2,128,512]{2,1,0:T(8,128)(2,1)}, bf16[2,128,512]{2,1,0:T(8,128)(2,1)}, bf16[2,128,512]{2,1,0:T(8,...) custom-call(s32[1,8,2]{2,1,0:T(8,128)S(1)} %copy.18.uses, ...), custom_call_target="tpu_custom_call" | custom-call | flops 805306368 | bytes 6291456 | tf_op jit(solution)/shard_map/attend_blocks/pallas_call | solution.py:245
  453.8 8.9 %collective-permute-done.47.rest_3_ = bf16[2,128,512]{2,1,0:T(8,128)(2,1)S(1)} collective-permute-done((bf16[2,128,512]{2,1,0:T(8,128)(2,1)S(1)}, bf16[2,128,512]{2,1,0:T(8,128)(2,1)S(1)}, u32[]{:S(2)}, u32[]{:S(2)}) %collective-permute-start.47) | collective-permute-done | bytes 262176 | tf_op jit(solution)/shard_map/ppermute | solution.py:28
  462.7 2.8 collective-permute-start.48
  469.7 12.6 %collective-permute-done.48.rest_5_ = bf16[2,128,512]{2,1,0:T(8,128)(2,1)S(1)} collective-permute-done((bf16[2,128,512]{2,1,0:T(8,128)(2,1)}, bf16[2,128,512]{2,1,0:T(8,128)(2,1)S(1)}, u32[]{:S(2)}, u32[]{:S(2)}) %collective-permute-start.48) | collective-permute-done | bytes 262176 | tf_op jit(solution)/shard_map/ppermute | solution.py:28
  482.6 6.7 %collective-permute-done.42.rest_6_ = bf16[2,128,512]{2,1,0:T(8,128)(2,1)S(1)} collective-permute-done((bf16[2,128,512]{2,1,0:T(8,128)(2,1)}, bf16[2,128,512]{2,1,0:T(8,128)(2,1)S(1)}, u32[]{:S(2)}, u32[]{:S(2)}) %collective-permute-start.42) | collective-permute-done | bytes 262176 | tf_op jit(solution)/shard_map/ppermute | solution.py:28
  499.4 3.7 collective-permute-done.3.refs_1_
  508.9 2.6 collective-permute-start.50
  512.3 5.8 %collective-permute-start.51 = (bf16[2,128,512]{2,1,0:T(8,128)(2,1)}, bf16[2,128,512]{2,1,0:T(8,128)(2,1)}, u32[]{:S(2)}, u32[]{:S(2)}) collective-permute-start(bf16[2,128,512]{2,1,0:T(8,128)(2,1)} %get-tuple-element.217), channel_id=1, source_target_pairs={{0,12},{4,8},{8,4},{12,0},{16,28},{20,24},{24,20},{28,16},{1,13},{... | collective-permute-start | bytes 786440 | tf_op jit(solution)/shard_map/ppermute | solution.py:28
  531.5 3.3 unpack_rows.1
  534.8 2.7 owner_sum.4.rest_8_
  539.7 2.8 owner_sum.6.rest_8_
  542.5 2.5 owner_sum.7
  (266 shorter events, 100.5 us)
Async XLA Ops:
  5.8 51.2 %all-to-all-start = ((bf16[8,2,128,512]{3,2,1,0:T(8,128)(2,1)}), bf16[8,2,128,512]{3,2,1,0:T(8,128)(2,1)}, u32[]{:S(2)}, u32[]{:S(2)}) async-start(bf16[8,2,128,512]{3,2,1,0:T(8,128)(2,1)} %pick_whole.2), calls=%async_computation | async-start | bytes 4194304 | tf_op jit(solution)/shard_map/all_to_all | solution.py:37
  56.9 53.4 %all-to-all-start.1 = ((bf16[8,2,128,512]{3,2,1,0:T(8,128)(2,1)}), bf16[8,2,128,512]{3,2,1,0:T(8,128)(2,1)}, u32[]{:S(2)}, u32[]{:S(2)}) async-start(bf16[8,2,128,512]{3,2,1,0:T(8,128)(2,1)} %pick_whole.3), calls=%async_computation.1 | async-start | bytes 4194304 | tf_op jit(solution)/shard_map/all_to_all | solution.py:37
  68.2 12.9 %collective-permute-start.2 = (bf16[2,128,512]{2,1,0:T(8,128)(2,1)}, bf16[2,128,512]{2,1,0:T(8,128)(2,1)S(1)}, u32[]{:S(2)}, u32[]{:S(2)}) collective-permute-start(bf16[2,128,512]{2,1,0:T(8,128)(2,1)} %get-tuple-element.115), channel_id=1, source_target_pairs={{0,3},{1,2},{2,1},{3,0},{4,7},{5,6},{6,5},{7,4},{8,11},{9,10},{10,... | collective-permute-start | bytes 786440 | tf_op jit(solution)/shard_map/ppermute | solution.py:28
  110.3 159.9 %all-to-all-start.3 = ((bf16[8,2,128,512]{3,2,1,0:T(8,128)(2,1)}), bf16[8,2,128,512]{3,2,1,0:T(8,128)(2,1)}, u32[]{:S(2)}, u32[]{:S(2)}) async-start(bf16[8,2,128,512]{3,2,1,0:T(8,128)(2,1)} %get-tuple-element.220), calls=%async_computation.3 | async-start | bytes 4194304 | tf_op jit(solution)/shard_map/all_to_all | solution.py:37
  118.4 62.2 %collective-permute-start.9 = (bf16[2,128,512]{2,1,0:T(8,128)(2,1)S(1)}, bf16[2,128,512]{2,1,0:T(8,128)(2,1)S(1)}, u32[]{:S(2)}, u32[]{:S(2)}) collective-permute-start(bf16[2,128,512]{2,1,0:T(8,128)(2,1)S(1)} %copy-done.87), channel_id=1, source_target_pairs={{0,16},{4,20},{8,24},{12,28},{16,0},{20,4},{24,8},{28,12},{1,17},{... | collective-permute-start | bytes 786440 | tf_op jit(solution)/shard_map/ppermute | solution.py:28
  120.5 71.4 %collective-permute-start.12 = (bf16[2,128,512]{2,1,0:T(8,128)(2,1)S(1)}, bf16[2,128,512]{2,1,0:T(8,128)(2,1)S(1)}, u32[]{:S(2)}, u32[]{:S(2)}) collective-permute-start(bf16[2,128,512]{2,1,0:T(8,128)(2,1)S(1)} %copy-done.86), channel_id=1, source_target_pairs={{0,20},{4,16},{8,28},{12,24},{16,4},{20,0},{24,12},{28,8},{1,21},{... | collective-permute-start | bytes 786440 | tf_op jit(solution)/shard_map/ppermute | solution.py:28
  180.6 24.2 %collective-permute-start.10 = (bf16[2,128,512]{2,1,0:T(8,128)(2,1)}, bf16[2,128,512]{2,1,0:T(8,128)(2,1)S(1)}, u32[]{:S(2)}, u32[]{:S(2)}) collective-permute-start(bf16[2,128,512]{2,1,0:T(8,128)(2,1)} %get-tuple-element.130), channel_id=1, source_target_pairs={{0,24},{4,28},{8,16},{12,20},{16,8},{20,12},{24,0},{28,4},{1,25},{... | collective-permute-start | bytes 786440 | tf_op jit(solution)/shard_map/ppermute | solution.py:28
  191.9 19.8 %collective-permute-start.13 = (bf16[2,128,512]{2,1,0:T(8,128)(2,1)}, bf16[2,128,512]{2,1,0:T(8,128)(2,1)S(1)}, u32[]{:S(2)}, u32[]{:S(2)}) collective-permute-start(bf16[2,128,512]{2,1,0:T(8,128)(2,1)} %get-tuple-element.135), channel_id=1, source_target_pairs={{0,28},{4,24},{8,20},{12,16},{16,12},{20,8},{24,4},{28,0},{1,29},{... | collective-permute-start | bytes 786440 | tf_op jit(solution)/shard_map/ppermute | solution.py:28
  209.5 13.3 %collective-permute-start.8 = (bf16[2,128,512]{2,1,0:T(8,128)(2,1)}, bf16[2,128,512]{2,1,0:T(8,128)(2,1)S(1)}, u32[]{:S(2)}, u32[]{:S(2)}) collective-permute-start(bf16[2,128,512]{2,1,0:T(8,128)(2,1)} %get-tuple-element.124), channel_id=1, source_target_pairs={{0,3},{1,2},{2,1},{3,0},{4,7},{5,6},{6,5},{7,4},{8,11},{9,10},{10,... | collective-permute-start | bytes 786440 | tf_op jit(solution)/shard_map/ppermute | solution.py:28
  211.7 15.0 %collective-permute-start.14 = (bf16[2,128,512]{2,1,0:T(8,128)(2,1)}, bf16[2,128,512]{2,1,0:T(8,128)(2,1)}, u32[]{:S(2)}, u32[]{:S(2)}) collective-permute-start(bf16[2,128,512]{2,1,0:T(8,128)(2,1)} %get-tuple-element.136), channel_id=1, source_target_pairs={{0,8},{4,12},{8,0},{12,4},{16,24},{20,28},{24,16},{28,20},{1,9},{5... | collective-permute-start | bytes 786440 | tf_op jit(solution)/shard_map/ppermute | solution.py:28
  212.4 14.3 %collective-permute-start.15 = (bf16[2,128,512]{2,1,0:T(8,128)(2,1)}, bf16[2,128,512]{2,1,0:T(8,128)(2,1)}, u32[]{:S(2)}, u32[]{:S(2)}) collective-permute-start(bf16[2,128,512]{2,1,0:T(8,128)(2,1)} %get-tuple-element.138), channel_id=1, source_target_pairs={{0,12},{4,8},{8,4},{12,0},{16,28},{20,24},{24,20},{28,16},{1,13},{... | collective-permute-start | bytes 786440 | tf_op jit(solution)/shard_map/ppermute | solution.py:28
  218.0 32.5 %collective-permute-start.19 = (bf16[2,128,512]{2,1,0:T(8,128)(2,1)}, bf16[2,128,512]{2,1,0:T(8,128)(2,1)}, u32[]{:S(2)}, u32[]{:S(2)}) collective-permute-start(bf16[2,128,512]{2,1,0:T(8,128)(2,1)} %get-tuple-element.145), channel_id=1, source_target_pairs={{0,1},{1,0},{2,3},{3,2},{4,5},{5,4},{6,7},{7,6},{8,9},{9,8},{10,11... | collective-permute-start | bytes 786440 | tf_op jit(solution)/shard_map/ppermute | solution.py:28
  219.0 31.5 %collective-permute-start.20 = (bf16[2,128,512]{2,1,0:T(8,128)(2,1)}, bf16[2,128,512]{2,1,0:T(8,128)(2,1)}, u32[]{:S(2)}, u32[]{:S(2)}) collective-permute-start(bf16[2,128,512]{2,1,0:T(8,128)(2,1)} %get-tuple-element.146), channel_id=1, source_target_pairs={{0,2},{1,3},{2,0},{3,1},{4,6},{5,7},{6,4},{7,5},{8,10},{9,11},{10,... | collective-permute-start | bytes 786440 | tf_op jit(solution)/shard_map/ppermute | solution.py:28
  223.5 27.0 %collective-permute-start.21 = (bf16[2,128,512]{2,1,0:T(8,128)(2,1)}, bf16[2,128,512]{2,1,0:T(8,128)(2,1)}, u32[]{:S(2)}, u32[]{:S(2)}) collective-permute-start(bf16[2,128,512]{2,1,0:T(8,128)(2,1)} %get-tuple-element.147), channel_id=1, source_target_pairs={{0,3},{1,2},{2,1},{3,0},{4,7},{5,6},{6,5},{7,4},{8,11},{9,10},{10,... | collective-permute-start | bytes 786440 | tf_op jit(solution)/shard_map/ppermute | solution.py:28
  270.3 269.4 %all-to-all-start.2 = ((bf16[8,2,128,512]{3,2,1,0:T(8,128)(2,1)}), bf16[8,2,128,512]{3,2,1,0:T(8,128)(2,1)}, u32[]{:S(2)}, u32[]{:S(2)}) async-start(bf16[8,2,128,512]{3,2,1,0:T(8,128)(2,1)} %get-tuple-element.218), calls=%async_computation.2 | async-start | bytes 4194304 | tf_op jit(solution)/shard_map/all_to_all | solution.py:37
  279.3 57.8 %collective-permute-start.28 = (bf16[2,128,512]{2,1,0:T(8,128)(2,1)}, bf16[2,128,512]{2,1,0:T(8,128)(2,1)S(1)}, u32[]{:S(2)}, u32[]{:S(2)}) collective-permute-start(bf16[2,128,512]{2,1,0:T(8,128)(2,1)} %get-tuple-element.171), channel_id=1, source_target_pairs={{0,16},{4,20},{8,24},{12,28},{16,0},{20,4},{24,8},{28,12},{1,17},{... | collective-permute-start | bytes 786440 | tf_op jit(solution)/shard_map/ppermute | solution.py:28
  281.4 66.9 %collective-permute-start.31 = (bf16[2,128,512]{2,1,0:T(8,128)(2,1)}, bf16[2,128,512]{2,1,0:T(8,128)(2,1)S(1)}, u32[]{:S(2)}, u32[]{:S(2)}) collective-permute-start(bf16[2,128,512]{2,1,0:T(8,128)(2,1)} %get-tuple-element.177), channel_id=1, source_target_pairs={{0,20},{4,16},{8,28},{12,24},{16,4},{20,0},{24,12},{28,8},{1,21},{... | collective-permute-start | bytes 786440 | tf_op jit(solution)/shard_map/ppermute | solution.py:28
  337.1 24.1 %collective-permute-start.29 = (bf16[2,128,512]{2,1,0:T(8,128)(2,1)}, bf16[2,128,512]{2,1,0:T(8,128)(2,1)S(1)}, u32[]{:S(2)}, u32[]{:S(2)}) collective-permute-start(bf16[2,128,512]{2,1,0:T(8,128)(2,1)} %get-tuple-element.172), channel_id=1, source_target_pairs={{0,24},{4,28},{8,16},{12,20},{16,8},{20,12},{24,0},{28,4},{1,25},{... | collective-permute-start | bytes 786440 | tf_op jit(solution)/shard_map/ppermute | solution.py:28
  348.3 18.7 %collective-permute-start.32 = (bf16[2,128,512]{2,1,0:T(8,128)(2,1)}, bf16[2,128,512]{2,1,0:T(8,128)(2,1)S(1)}, u32[]{:S(2)}, u32[]{:S(2)}) collective-permute-start(bf16[2,128,512]{2,1,0:T(8,128)(2,1)} %get-tuple-element.178), channel_id=1, source_target_pairs={{0,28},{4,24},{8,20},{12,16},{16,12},{20,8},{24,4},{28,0},{1,29},{... | collective-permute-start | bytes 786440 | tf_op jit(solution)/shard_map/ppermute | solution.py:28
  367.0 15.3 %collective-permute-start.34 = (bf16[2,128,512]{2,1,0:T(8,128)(2,1)}, bf16[2,128,512]{2,1,0:T(8,128)(2,1)S(1)}, u32[]{:S(2)}, u32[]{:S(2)}) collective-permute-start(bf16[2,128,512]{2,1,0:T(8,128)(2,1)} %get-tuple-element.181), channel_id=1, source_target_pairs={{0,12},{4,8},{8,4},{12,0},{16,28},{20,24},{24,20},{28,16},{1,13},{... | collective-permute-start | bytes 786440 | tf_op jit(solution)/shard_map/ppermute | solution.py:28
  374.9 11.1 %collective-permute-start.44 = (bf16[2,128,512]{2,1,0:T(8,128)(2,1)S(1)}, bf16[2,128,512]{2,1,0:T(8,128)(2,1)S(1)}, u32[]{:S(2)}, u32[]{:S(2)}) collective-permute-start(bf16[2,128,512]{2,1,0:T(8,128)(2,1)S(1)} %copy-done.84), channel_id=1, source_target_pairs={{0,16},{4,20},{8,24},{12,28},{16,0},{20,4},{24,8},{28,12},{1,17},{... | collective-permute-start | bytes 786440 | tf_op jit(solution)/shard_map/ppermute | solution.py:28
  382.3 20.5 %collective-permute-start.38 = (bf16[2,128,512]{2,1,0:T(8,128)(2,1)S(1)}, bf16[2,128,512]{2,1,0:T(8,128)(2,1)S(1)}, u32[]{:S(2)}, u32[]{:S(2)}) collective-permute-start(bf16[2,128,512]{2,1,0:T(8,128)(2,1)S(1)} %copy-done.83), channel_id=1, source_target_pairs={{0,20},{4,16},{8,28},{12,24},{16,4},{20,0},{24,12},{28,8},{1,21},{... | collective-permute-start | bytes 786440 | tf_op jit(solution)/shard_map/ppermute | solution.py:28
  386.0 29.6 %collective-permute-start.45 = (bf16[2,128,512]{2,1,0:T(8,128)(2,1)S(1)}, bf16[2,128,512]{2,1,0:T(8,128)(2,1)S(1)}, u32[]{:S(2)}, u32[]{:S(2)}) collective-permute-start(bf16[2,128,512]{2,1,0:T(8,128)(2,1)S(1)} %copy-done.82), channel_id=1, source_target_pairs={{0,24},{4,28},{8,16},{12,20},{16,8},{20,12},{24,0},{28,4},{1,25},{... | collective-permute-start | bytes 786440 | tf_op jit(solution)/shard_map/ppermute | solution.py:28
  402.8 19.6 %collective-permute-start.39 = (bf16[2,128,512]{2,1,0:T(8,128)(2,1)S(1)}, bf16[2,128,512]{2,1,0:T(8,128)(2,1)S(1)}, u32[]{:S(2)}, u32[]{:S(2)}) collective-permute-start(bf16[2,128,512]{2,1,0:T(8,128)(2,1)S(1)} %copy-done.81), channel_id=1, source_target_pairs={{0,28},{4,24},{8,20},{12,16},{16,12},{20,8},{24,4},{28,0},{1,29},{... | collective-permute-start | bytes 786440 | tf_op jit(solution)/shard_map/ppermute | solution.py:28
  408.1 14.3 %collective-permute-start.25 = (bf16[2,128,512]{2,1,0:T(8,128)(2,1)}, bf16[2,128,512]{2,1,0:T(8,128)(2,1)S(1)}, u32[]{:S(2)}, u32[]{:S(2)}) collective-permute-start(bf16[2,128,512]{2,1,0:T(8,128)(2,1)} %get-tuple-element.155), channel_id=1, source_target_pairs={{0,1},{1,0},{2,3},{3,2},{4,5},{5,4},{6,7},{7,6},{8,9},{9,8},{10,11... | collective-permute-start | bytes 786440 | tf_op jit(solution)/shard_map/ppermute | solution.py:28
  408.6 13.9 %collective-permute-start.26 = (bf16[2,128,512]{2,1,0:T(8,128)(2,1)}, bf16[2,128,512]{2,1,0:T(8,128)(2,1)S(1)}, u32[]{:S(2)}, u32[]{:S(2)}) collective-permute-start(bf16[2,128,512]{2,1,0:T(8,128)(2,1)} %get-tuple-element.156), channel_id=1, source_target_pairs={{0,2},{1,3},{2,0},{3,1},{4,6},{5,7},{6,4},{7,5},{8,10},{9,11},{10,... | collective-permute-start | bytes 786440 | tf_op jit(solution)/shard_map/ppermute | solution.py:28
  408.6 13.9 %collective-permute-start.27 = (bf16[2,128,512]{2,1,0:T(8,128)(2,1)}, bf16[2,128,512]{2,1,0:T(8,128)(2,1)S(1)}, u32[]{:S(2)}, u32[]{:S(2)}) collective-permute-start(bf16[2,128,512]{2,1,0:T(8,128)(2,1)} %get-tuple-element.157), channel_id=1, source_target_pairs={{0,3},{1,2},{2,1},{3,0},{4,7},{5,6},{6,5},{7,4},{8,11},{9,10},{10,... | collective-permute-start | bytes 786440 | tf_op jit(solution)/shard_map/ppermute | solution.py:28
  415.5 35.1 %collective-permute-start.46 = (bf16[2,128,512]{2,1,0:T(8,128)(2,1)}, bf16[2,128,512]{2,1,0:T(8,128)(2,1)S(1)}, u32[]{:S(2)}, u32[]{:S(2)}) collective-permute-start(bf16[2,128,512]{2,1,0:T(8,128)(2,1)} %get-tuple-element.211), channel_id=1, source_target_pairs={{0,4},{4,0},{8,12},{12,8},{16,20},{20,16},{24,28},{28,24},{1,5},{5... | collective-permute-start | bytes 786440 | tf_op jit(solution)/shard_map/ppermute | solution.py:28
  422.3 30.3 %collective-permute-start.40 = (bf16[2,128,512]{2,1,0:T(8,128)(2,1)}, bf16[2,128,512]{2,1,0:T(8,128)(2,1)S(1)}, u32[]{:S(2)}, u32[]{:S(2)}) collective-permute-start(bf16[2,128,512]{2,1,0:T(8,128)(2,1)} %get-tuple-element.198), channel_id=1, source_target_pairs={{0,8},{4,12},{8,0},{12,4},{16,24},{20,28},{24,16},{28,20},{1,9},{5... | collective-permute-start | bytes 786440 | tf_op jit(solution)/shard_map/ppermute | solution.py:28
  450.7 12.0 %collective-permute-start.47 = (bf16[2,128,512]{2,1,0:T(8,128)(2,1)S(1)}, bf16[2,128,512]{2,1,0:T(8,128)(2,1)S(1)}, u32[]{:S(2)}, u32[]{:S(2)}) collective-permute-start(bf16[2,128,512]{2,1,0:T(8,128)(2,1)S(1)} %copy-done.80), channel_id=1, source_target_pairs={{0,12},{4,8},{8,4},{12,0},{16,28},{20,24},{24,20},{28,16},{1,13},{... | collective-permute-start | bytes 786440 | tf_op jit(solution)/shard_map/ppermute | solution.py:28
  452.7 12.8 %collective-permute-start.41 = (bf16[2,128,512]{2,1,0:T(8,128)(2,1)}, bf16[2,128,512]{2,1,0:T(8,128)(2,1)S(1)}, u32[]{:S(2)}, u32[]{:S(2)}) collective-permute-start(bf16[2,128,512]{2,1,0:T(8,128)(2,1)} %get-tuple-element.199), channel_id=1, source_target_pairs={{0,16},{4,20},{8,24},{12,28},{16,0},{20,4},{24,8},{28,12},{1,17},{... | collective-permute-start | bytes 786440 | tf_op jit(solution)/shard_map/ppermute | solution.py:28
  452.7 16.1 %collective-permute-start.22 = (bf16[2,128,512]{2,1,0:T(8,128)(2,1)}, bf16[2,128,512]{2,1,0:T(8,128)(2,1)S(1)}, u32[]{:S(2)}, u32[]{:S(2)}) collective-permute-start(bf16[2,128,512]{2,1,0:T(8,128)(2,1)} %get-tuple-element.150), channel_id=1, source_target_pairs={{0,1},{1,0},{2,3},{3,2},{4,5},{5,4},{6,7},{7,6},{8,9},{9,8},{10,11... | collective-permute-start | bytes 786440 | tf_op jit(solution)/shard_map/ppermute | solution.py:28
  462.7 19.7 %collective-permute-start.48 = (bf16[2,128,512]{2,1,0:T(8,128)(2,1)}, bf16[2,128,512]{2,1,0:T(8,128)(2,1)S(1)}, u32[]{:S(2)}, u32[]{:S(2)}) collective-permute-start(bf16[2,128,512]{2,1,0:T(8,128)(2,1)} %get-tuple-element.213), channel_id=1, source_target_pairs={{0,20},{4,16},{8,28},{12,24},{16,4},{20,0},{24,12},{28,8},{1,21},{... | collective-permute-start | bytes 786440 | tf_op jit(solution)/shard_map/ppermute | solution.py:28
  465.4 23.9 %collective-permute-start.42 = (bf16[2,128,512]{2,1,0:T(8,128)(2,1)}, bf16[2,128,512]{2,1,0:T(8,128)(2,1)S(1)}, u32[]{:S(2)}, u32[]{:S(2)}) collective-permute-start(bf16[2,128,512]{2,1,0:T(8,128)(2,1)} %get-tuple-element.200), channel_id=1, source_target_pairs={{0,24},{4,28},{8,16},{12,20},{16,8},{20,12},{24,0},{28,4},{1,25},{... | collective-permute-start | bytes 786440 | tf_op jit(solution)/shard_map/ppermute | solution.py:28
  466.3 23.7 %collective-permute-start.23 = (bf16[2,128,512]{2,1,0:T(8,128)(2,1)S(1)}, bf16[2,128,512]{2,1,0:T(8,128)(2,1)S(1)}, u32[]{:S(2)}, u32[]{:S(2)}) collective-permute-start(bf16[2,128,512]{2,1,0:T(8,128)(2,1)S(1)} %copy-done.79), channel_id=1, source_target_pairs={{0,2},{1,3},{2,0},{3,1},{4,6},{5,7},{6,4},{7,5},{8,10},{9,11},{10,... | collective-permute-start | bytes 786440 | tf_op jit(solution)/shard_map/ppermute | solution.py:28
  467.3 24.9 %collective-permute-start.24 = (bf16[2,128,512]{2,1,0:T(8,128)(2,1)S(1)}, bf16[2,128,512]{2,1,0:T(8,128)(2,1)S(1)}, u32[]{:S(2)}, u32[]{:S(2)}) collective-permute-start(bf16[2,128,512]{2,1,0:T(8,128)(2,1)S(1)} %copy-done.78), channel_id=1, source_target_pairs={{0,3},{1,2},{2,1},{3,0},{4,7},{5,6},{6,5},{7,4},{8,11},{9,10},{10,... | collective-permute-start | bytes 786440 | tf_op jit(solution)/shard_map/ppermute | solution.py:28
  469.5 25.0 %collective-permute-start.16 = (bf16[2,128,512]{2,1,0:T(8,128)(2,1)S(1)}, bf16[2,128,512]{2,1,0:T(8,128)(2,1)S(1)}, u32[]{:S(2)}, u32[]{:S(2)}) collective-permute-start(bf16[2,128,512]{2,1,0:T(8,128)(2,1)S(1)} %copy-done.77), channel_id=1, source_target_pairs={{0,1},{1,0},{2,3},{3,2},{4,5},{5,4},{6,7},{7,6},{8,9},{9,8},{10,11... | collective-permute-start | bytes 786440 | tf_op jit(solution)/shard_map/ppermute | solution.py:28
  482.3 12.9 %collective-permute-start.17 = (bf16[2,128,512]{2,1,0:T(8,128)(2,1)S(1)}, bf16[2,128,512]{2,1,0:T(8,128)(2,1)S(1)}, u32[]{:S(2)}, u32[]{:S(2)}) collective-permute-start(bf16[2,128,512]{2,1,0:T(8,128)(2,1)S(1)} %copy-done.76), channel_id=1, source_target_pairs={{0,2},{1,3},{2,0},{3,1},{4,6},{5,7},{6,4},{7,5},{8,10},{9,11},{10,... | collective-permute-start | bytes 786440 | tf_op jit(solution)/shard_map/ppermute | solution.py:28
  490.8 12.4 %collective-permute-start.3 = (bf16[2,128,512]{2,1,0:T(8,128)(2,1)S(1)}, bf16[2,128,512]{2,1,0:T(8,128)(2,1)S(1)}, u32[]{:S(2)}, u32[]{:S(2)}) collective-permute-start(bf16[2,128,512]{2,1,0:T(8,128)(2,1)S(1)} %copy-done.74), channel_id=1, source_target_pairs={{0,1},{1,0},{2,3},{3,2},{4,5},{5,4},{6,7},{7,6},{8,9},{9,8},{10,11... | collective-permute-start | bytes 786440 | tf_op jit(solution)/shard_map/ppermute | solution.py:28
  492.9 12.1 %collective-permute-start.49 = (bf16[2,128,512]{2,1,0:T(8,128)(2,1)}, bf16[2,128,512]{2,1,0:T(8,128)(2,1)S(1)}, u32[]{:S(2)}, u32[]{:S(2)}) collective-permute-start(bf16[2,128,512]{2,1,0:T(8,128)(2,1)} %get-tuple-element.214), channel_id=1, source_target_pairs={{0,28},{4,24},{8,20},{12,16},{16,12},{20,8},{24,4},{28,0},{1,29},{... | collective-permute-start | bytes 786440 | tf_op jit(solution)/shard_map/ppermute | solution.py:28
  495.2 11.2 %collective-permute-start.43 = (bf16[2,128,512]{2,1,0:T(8,128)(2,1)}, bf16[2,128,512]{2,1,0:T(8,128)(2,1)S(1)}, u32[]{:S(2)}, u32[]{:S(2)}) collective-permute-start(bf16[2,128,512]{2,1,0:T(8,128)(2,1)} %get-tuple-element.201), channel_id=1, source_target_pairs={{0,4},{4,0},{8,12},{12,8},{16,20},{20,16},{24,28},{28,24},{1,5},{5... | collective-permute-start | bytes 786440 | tf_op jit(solution)/shard_map/ppermute | solution.py:28
  495.9 12.3 %collective-permute-start.4 = (bf16[2,128,512]{2,1,0:T(8,128)(2,1)S(1)}, bf16[2,128,512]{2,1,0:T(8,128)(2,1)S(1)}, u32[]{:S(2)}, u32[]{:S(2)}) collective-permute-start(bf16[2,128,512]{2,1,0:T(8,128)(2,1)S(1)} %copy-done.73), channel_id=1, source_target_pairs={{0,2},{1,3},{2,0},{3,1},{4,6},{5,7},{6,4},{7,5},{8,10},{9,11},{10,... | collective-permute-start | bytes 786440 | tf_op jit(solution)/shard_map/ppermute | solution.py:28
  499.1 12.5 %collective-permute-start.5 = (bf16[2,128,512]{2,1,0:T(8,128)(2,1)S(1)}, bf16[2,128,512]{2,1,0:T(8,128)(2,1)S(1)}, u32[]{:S(2)}, u32[]{:S(2)}) collective-permute-start(bf16[2,128,512]{2,1,0:T(8,128)(2,1)S(1)} %copy-done.72), channel_id=1, source_target_pairs={{0,3},{1,2},{2,1},{3,0},{4,7},{5,6},{6,5},{7,4},{8,11},{9,10},{10,... | collective-permute-start | bytes 786440 | tf_op jit(solution)/shard_map/ppermute | solution.py:28
  503.8 14.3 %collective-permute-start.35 = (bf16[2,128,512]{2,1,0:T(8,128)(2,1)}, bf16[2,128,512]{2,1,0:T(8,128)(2,1)}, u32[]{:S(2)}, u32[]{:S(2)}) collective-permute-start(bf16[2,128,512]{2,1,0:T(8,128)(2,1)} %get-tuple-element.183), channel_id=1, source_target_pairs={{0,1},{1,0},{2,3},{3,2},{4,5},{5,4},{6,7},{7,6},{8,9},{9,8},{10,11... | collective-permute-start | bytes 786440 | tf_op jit(solution)/shard_map/ppermute | solution.py:28
  505.7 12.4 %collective-permute-start.36 = (bf16[2,128,512]{2,1,0:T(8,128)(2,1)}, bf16[2,128,512]{2,1,0:T(8,128)(2,1)S(1)}, u32[]{:S(2)}, u32[]{:S(2)}) collective-permute-start(bf16[2,128,512]{2,1,0:T(8,128)(2,1)} %get-tuple-element.184), channel_id=1, source_target_pairs={{0,2},{1,3},{2,0},{3,1},{4,6},{5,7},{6,4},{7,5},{8,10},{9,11},{10,... | collective-permute-start | bytes 786440 | tf_op jit(solution)/shard_map/ppermute | solution.py:28
  507.1 13.9 %collective-permute-start.37 = (bf16[2,128,512]{2,1,0:T(8,128)(2,1)}, bf16[2,128,512]{2,1,0:T(8,128)(2,1)}, u32[]{:S(2)}, u32[]{:S(2)}) collective-permute-start(bf16[2,128,512]{2,1,0:T(8,128)(2,1)} %get-tuple-element.185), channel_id=1, source_target_pairs={{0,3},{1,2},{2,1},{3,0},{4,7},{5,6},{6,5},{7,4},{8,11},{9,10},{10,... | collective-permute-start | bytes 786440 | tf_op jit(solution)/shard_map/ppermute | solution.py:28
  508.9 33.5 %collective-permute-start.50 = (bf16[2,128,512]{2,1,0:T(8,128)(2,1)}, bf16[2,128,512]{2,1,0:T(8,128)(2,1)}, u32[]{:S(2)}, u32[]{:S(2)}) collective-permute-start(bf16[2,128,512]{2,1,0:T(8,128)(2,1)} %get-tuple-element.215), channel_id=1, source_target_pairs={{0,8},{4,12},{8,0},{12,4},{16,24},{20,28},{24,16},{28,20},{1,9},{5... | collective-permute-start | bytes 786440 | tf_op jit(solution)/shard_map/ppermute | solution.py:28
  512.3 30.2 %collective-permute-start.51 = (bf16[2,128,512]{2,1,0:T(8,128)(2,1)}, bf16[2,128,512]{2,1,0:T(8,128)(2,1)}, u32[]{:S(2)}, u32[]{:S(2)}) collective-permute-start(bf16[2,128,512]{2,1,0:T(8,128)(2,1)} %get-tuple-element.217), channel_id=1, source_target_pairs={{0,12},{4,8},{8,4},{12,0},{16,28},{20,24},{24,20},{28,16},{1,13},{... | collective-permute-start | bytes 786440 | tf_op jit(solution)/shard_map/ppermute | solution.py:28
  (96 other events, 1978.8 us)

commit v6 on v5

--- a/solution.py
+++ b/solution.py
@@ -1,4 +1,5 @@
 import functools
+import math
 
 import jax
 import jax.numpy as jnp
@@ -10,8 +11,6 @@
 DH = 128
 BLOCK = 64
 NBLEN = 128
-GROUPS = 4
-DEPTH = 2
 F32 = jnp.float32
 BF16 = jnp.bfloat16
 VMEM_BYTES = 40 * 1024 * 1024
@@ -280,7 +279,7 @@
 def owner_sum(first, send_lists, back, shape, so_far):
     seqs = send_lists.shape[1]
     pieces, chunk = len(back), back[0].shape[-1]
-    wide = min(chunk, 256)
+    wide = math.gcd(math.gcd(first, chunk), 256)
     skip, steps = first // wide, chunk // wide
     extra = [] if so_far is None else [so_far]
     if pieces > 1:
@@ -303,53 +302,58 @@
     )(send_lists, *back, *extra)
 
 
-class Chain:
-    def __init__(self, count):
-        self.count, self.done = count, []
-
-    def swap(self, pieces):
-        got = [pieces[0]] + [None] * (self.count - 1)
-        half = self.count // 2
-        for step in list(range(half, self.count)) + list(range(1, half)):
-            piece = pieces[step]
-            if len(self.done) >= DEPTH:
-                piece = after(piece, self.done[-DEPTH])
-            got[step] = exchange(piece, "enc", step, self.count)
-            self.done.append(got[step])
-        return got
+def swap_split(pieces, depth):
+    count = len(pieces)
+    half = count // 2
+    got = [pieces[0]] + [None] * (count - 1)
+    for step in list(range(half, count)) + list(range(1, half)):
+        piece = pieces[step]
+        if step >= half + depth:
+            piece = after(piece, got[step - depth])
+        got[step] = exchange(piece, "enc", step, count)
+    return got
 
 
 def local(seqs, parts, queries, kv_pool, send_lists, block_slots, grad_context):
     width = kv_pool.shape[-1]
-    groups = min(GROUPS, width // DH)
-    chunk = width // groups
-    chain = Chain(seqs)
-
-    def swap(split, pieces):
-        return chain.swap(pieces) if split else [swap_pool(pieces[0])]
-
-    fetched, rows = [], []
-    for group in range(groups):
-        split = group % 2 == 1
-        picked = pick(group * chunk, chunk, split, send_lists, kv_pool)
-        send_lists = after(send_lists, picked[0])
-        if group == 3:
-            picked = after(picked, fetched[0])
-        fetched.append(swap(split, picked))
-        rows.append(swap_rows(pack(group * chunk, chunk, queries, grad_context, width, parts)))
+    heads = width // DH
+    half = seqs // 2
+    cut = [heads // 4, heads // 4 + max(1, 3 * heads // 8)]
+    firsts = [0, cut[0] * DH, cut[1] * DH]
+    sizes = [cut[0] * DH, (cut[1] - cut[0]) * DH, width - cut[1] * DH]
+
+    def choose(group):
+        return pick(firsts[group], sizes[group], group == 1, send_lists, kv_pool)
+
+    def rows_of(group):
+        return swap_rows(pack(firsts[group], sizes[group], queries, grad_context, width, parts))
+
+    picked = choose(0)
+    send_lists = after(send_lists, picked[0])
+    early = [swap_pool(picked[0])]
+    picked = choose(1)
+    send_lists, queries = after((send_lists, queries), picked[0])
+    split = swap_split(picked, half)
+    rows = [rows_of(0), rows_of(1)]
+    late = [swap_pool(choose(2)[0])]
+    rows.append(rows_of(2))
+
+    early, split = lax.optimization_barrier((early, split))
+    early_rows, early_back = attend(0, block_slots, rows[0], early)
+    block_slots = after(block_slots, early_rows[0])
+    split_rows, split_back = attend(0, block_slots, rows[1], split)
+    block_slots = after(block_slots, split_rows[0])
+    early_back = [swap_pool(early_back[0])]
+    split_back = swap_split(split_back, 2)
+    late = after(late, split_back[half : half + 2])
+    late_rows, late_back = attend(0, block_slots, rows[2], late)
+    late_back = [swap_pool(late_back[0])]
+
+    token_parts = [swap_rows(piece) for piece in (early_rows, split_rows, late_rows)]
+    context, grad_queries = unpack(token_parts, firsts, width, queries.shape)
     pool_grads = None
-    token_parts, returns = [], []
-    for group in range(groups):
-        rows_out, kv_out = attend(0, block_slots, rows[group], fetched[group])
-        block_slots = after(block_slots, rows_out[0])
-        returns.append(swap(group % 2 == 1, kv_out))
-        token_parts.append(swap_rows(rows_out))
-    firsts = [group * chunk for group in range(groups)]
-    context, grad_queries = unpack(token_parts, firsts, width, queries.shape)
-    for group in range(groups):
-        pool_grads = owner_sum(
-            group * chunk, send_lists, returns[group], kv_pool.shape, pool_grads
-        )
+    for first, back in zip(firsts, (early_back, split_back, late_back)):
+        pool_grads = owner_sum(first, send_lists, back, kv_pool.shape, pool_grads)
     return (context, grad_queries, pool_grads)
 
 

time: 552 us -> 460 us (0.83); the launches traced: 545 us -> 459 us
  starting transfers between devices: 100 us -> 64.3 us
  local copies, waits for them, and re-layouts: 51.8 us -> 19.3 us
  waiting for transfers between devices: 289 us -> 278 us
  Pallas kernels: 102 us -> 96.1 us
    ppermute x52 -> x32, starting transfers between devices: 74.1 us -> 40.1 us  [exchange(): return lax.ppermute(array, axis, pairs)]
    unnamed x178 -> x54, local copies, waits for them, and re-layouts: 51.2 us -> 19 us
    all_to_all x4, waiting for transfers between devices: 46.1 us -> 35.6 us  [swap_pool(): return lax.all_to_all(array, 'enc', split_axis=0, concat_axis=0, tiled=True)]
    pallas_call x4 -> x3, Pallas kernels: 75.3 us -> 73.7 us  [attend(): pl.pallas_call(functools.partial(attend_kernel, seqs, parts, split), grid...]
    ppermute x52 -> x32, waiting for transfers between devices: 243 us -> 242 us  [exchange(): return lax.ppermute(array, axis, pairs)]
  transfers between devices with their start and end apart: 56 -> 36, of which waited for: 26 -> 19; matrix products, arithmetic and copies ran while one was open for 0% -> 0% of each run, Pallas kernels for 18% -> 20%
where the time goes in v6:
time: 460 us; the launch traced here: 459 us
  waiting for transfers between devices  278 us (60%)
  Pallas kernels  96.1 us (21%)
  starting transfers between devices  64.3 us (14%)
  local copies, waits for them, and re-layouts  19.3 us (4%)
    ppermute x32, waiting for transfers between devices, exchange(): return lax.ppermute(array, axis, pairs)  242 us
    pallas_call x3, Pallas kernels, attend(): pl.pallas_call(functools.partial(attend_kernel, seqs, parts, split), grid...  73.7 us
    ppermute x32, starting transfers between devices, exchange(): return lax.ppermute(array, axis, pairs)  40.1 us
    all_to_all x4, waiting for transfers between devices, swap_pool(): return lax.all_to_all(array, 'enc', split_axis=0, concat_axis=0, tiled=True)  35.6 us
    all_to_all x4, starting transfers between devices, swap_pool(): return lax.all_to_all(array, 'enc', split_axis=0, concat_axis=0, tiled=True)  24.2 us
    unnamed x54, local copies, waits for them, and re-layouts  19 us
  transfers between devices with their start and end apart: 36, of which 19 were waited for; matrix products, arithmetic and copies ran while one was open for 0% of the time, Pallas kernels for 20%

profile of v6, /device:TPU:15, one launch (start us, length us, event | category | flops | bytes accessed | tf_op | source)
XLA Modules:
  0.0 458.6 jit_solution(18340823828353234517)
XLA Ops:
  1.4 2.2 copy-done
  3.5 2.2 pick_whole.2
  5.8 5.6 %all-to-all-start = ((bf16[8,2,128,512]{3,2,1,0:T(8,128)(2,1)}), bf16[8,2,128,512]{3,2,1,0:T(8,128)(2,1)}, u32[]{:S(2)}, u32[]{:S(2)}) async-start(bf16[8,2,128,512]{3,2,1,0:T(8,128)(2,1)} %pick_whole.2), calls=%async_computation | async-start | bytes 4194304 | tf_op jit(solution)/shard_map/all_to_all | solution.py:36
  11.5 2.2 copy-done.1
  13.7 2.7 pick_split.1
  16.4 2.2 copy-done.2
  18.6 2.7 pick_whole.3
  21.3 35.6 %all-to-all-done.rest_4_ = bf16[8,2,128,512]{3,2,1,0:T(8,128)(2,1)} async-done(((bf16[8,2,128,512]{3,2,1,0:T(8,128)(2,1)}), bf16[8,2,128,512]{3,2,1,0:T(8,128)(2,1)}, u32[]{:S(2)}, u32[]{:S(2)}) %all-to-all-start) | async-done | bytes 2097184 | tf_op jit(solution)/shard_map/all_to_all | solution.py:36
  56.9 8.0 %all-to-all-start.1 = ((bf16[8,2,128,768]{3,2,1,0:T(8,128)(2,1)}), bf16[8,2,128,768]{3,2,1,0:T(8,128)(2,1)}, u32[]{:S(2)}, u32[]{:S(2)}) async-start(bf16[8,2,128,768]{3,2,1,0:T(8,128)(2,1)} %pick_whole.3), calls=%async_computation.1 | async-start | bytes 6291456 | tf_op jit(solution)/shard_map/all_to_all | solution.py:36
  65.3 1.8 collective-permute-start.5
  67.1 2.1 collective-permute-start.6
  70.9 54.5 %collective-permute-done.4.rest_6_ = bf16[2,128,768]{2,1,0:T(8,128)(2,1)S(1)} collective-permute-done((bf16[2,128,768]{2,1,0:T(8,128)(2,1)}, bf16[2,128,768]{2,1,0:T(8,128)(2,1)S(1)}, u32[]{:S(2)}, u32[]{:S(2)}) %collective-permute-start.4) | collective-permute-done | bytes 393248 | tf_op jit(solution)/shard_map/ppermute | solution.py:27
  125.4 3.2 collective-permute-start.9
  128.6 1.6 copy-done.4
  131.4 2.5 collective-permute-done.5.rest_7_
  134.1 40.9 %collective-permute-done.6.rest_8_ = bf16[2,128,768]{2,1,0:T(8,128)(2,1)S(1)} collective-permute-done((bf16[2,128,768]{2,1,0:T(8,128)(2,1)}, bf16[2,128,768]{2,1,0:T(8,128)(2,1)S(1)}, u32[]{:S(2)}, u32[]{:S(2)}) %collective-permute-start.6) | collective-permute-done | bytes 393248 | tf_op jit(solution)/shard_map/ppermute | solution.py:27
  176.1 7.4 %collective-permute-done.7.rest_9_ = bf16[2,128,768]{2,1,0:T(8,128)(2,1)S(1)} collective-permute-done((bf16[2,128,768]{2,1,0:T(8,128)(2,1)}, bf16[2,128,768]{2,1,0:T(8,128)(2,1)S(1)}, u32[]{:S(2)}, u32[]{:S(2)}) %collective-permute-start.7) | collective-permute-done | bytes 393248 | tf_op jit(solution)/shard_map/ppermute | solution.py:27
  184.5 9.1 %collective-permute-done.8.rest_10_ = bf16[2,128,768]{2,1,0:T(8,128)(2,1)} collective-permute-done((bf16[2,128,768]{2,1,0:T(8,128)(2,1)}, bf16[2,128,768]{2,1,0:T(8,128)(2,1)}, u32[]{:S(2)}, u32[]{:S(2)}) %collective-permute-start.8) | collective-permute-done | bytes 393248 | tf_op jit(solution)/shard_map/ppermute | solution.py:27
  193.6 8.6 %collective-permute-done.9.rest_11_ = bf16[2,128,768]{2,1,0:T(8,128)(2,1)} collective-permute-done((bf16[2,128,768]{2,1,0:T(8,128)(2,1)}, bf16[2,128,768]{2,1,0:T(8,128)(2,1)}, u32[]{:S(2)}, u32[]{:S(2)}) %collective-permute-start.9) | collective-permute-done | bytes 393248 | tf_op jit(solution)/shard_map/ppermute | solution.py:27
  203.2 18.7 %attend_blocks.3 = (bf16[2,128,512]{2,1,0:T(8,128)(2,1)}, bf16[2,128,512]{2,1,0:T(8,128)(2,1)}, bf16[2,128,512]{2,1,0:T(8,128)(2,1)}, bf16[2,128,512]{2,1,0:T(8,128)(2,1)}, bf16[8,2,128,512]{3,2,1,0:T(8,128)(2,1)}) custom-call(s32[1,8,2]{2,1,0:T(8,128)S(1)} %copy.12.uses, bf16[2,128,512]{2,1,0:T(8,128)(2,1)S(1)} %copy-done.23, ...), custom_call_target="tpu_custom_call" | custom-call | flops 805306368 | bytes 6291456 | tf_op jit(solution)/shard_map/attend_blocks/pallas_call | solution.py:244
  221.9 4.4 all-to-all-start.3
  226.3 1.6 copy-done.5
  227.9 1.4 pack_rows.4
  229.9 2.2 collective-permute-start.15
  232.0 1.5 pack_rows.5
  233.6 6.7 %collective-permute-done.13.rest_1_ = bf16[2,128,768]{2,1,0:T(8,128)(2,1)} collective-permute-done((bf16[2,128,768]{2,1,0:T(8,128)(2,1)}, bf16[2,128,768]{2,1,0:T(8,128)(2,1)}, u32[]{:S(2)}, u32[]{:S(2)}) %collective-permute-start.13) | collective-permute-done | bytes 393248 | tf_op jit(solution)/shard_map/ppermute | solution.py:27
  240.3 8.4 %collective-permute-done.15.rest_3_ = bf16[2,128,768]{2,1,0:T(8,128)(2,1)} collective-permute-done((bf16[2,128,768]{2,1,0:T(8,128)(2,1)}, bf16[2,128,768]{2,1,0:T(8,128)(2,1)}, u32[]{:S(2)}, u32[]{:S(2)}) %collective-permute-start.15) | collective-permute-done | bytes 393248 | tf_op jit(solution)/shard_map/ppermute | solution.py:27
  252.7 27.6 %attend_blocks.4 = (bf16[2,128,768]{2,1,0:T(8,128)(2,1)}, bf16[2,128,768]{2,1,0:T(8,128)(2,1)}, bf16[2,128,768]{2,1,0:T(8,128)(2,1)}, bf16[2,128,768]{2,1,0:T(8,...) custom-call(s32[1,8,2]{2,1,0:T(8,128)S(1)} %copy.13.uses, ...), custom_call_target="tpu_custom_call" | custom-call | flops 1207959552 | bytes 9437184 | tf_op jit(solution)/shard_map/attend_blocks/pallas_call | solution.py:244
  281.3 2.9 collective-permute-start.23
  286.8 20.4 %collective-permute-done.22.rest_4_ = bf16[2,128,768]{2,1,0:T(8,128)(2,1)S(1)} collective-permute-done((bf16[2,128,768]{2,1,0:T(8,128)(2,1)}, bf16[2,128,768]{2,1,0:T(8,128)(2,1)S(1)}, u32[]{:S(2)}, u32[]{:S(2)}) %collective-permute-start.22) | collective-permute-done | bytes 393248 | tf_op jit(solution)/shard_map/ppermute | solution.py:27
  307.2 8.4 %collective-permute-done.23.rest_5_ = bf16[2,128,768]{2,1,0:T(8,128)(2,1)S(1)} collective-permute-done((bf16[2,128,768]{2,1,0:T(8,128)(2,1)}, bf16[2,128,768]{2,1,0:T(8,128)(2,1)S(1)}, u32[]{:S(2)}, u32[]{:S(2)}) %collective-permute-start.23) | collective-permute-done | bytes 393248 | tf_op jit(solution)/shard_map/ppermute | solution.py:27
  315.7 27.3 %attend_blocks.5 = (bf16[2,128,768]{2,1,0:T(8,128)(2,1)}, bf16[2,128,768]{2,1,0:T(8,128)(2,1)}, bf16[2,128,768]{2,1,0:T(8,128)(2,1)}, bf16[2,128,768]{2,1,0:T(8,128)(2,1)}, bf16[8,2,128,768]{3,2,1,0:T(8,128)(2,1)}) custom-call(s32[1,8,2]{2,1,0:T(8,128)S(1)} %copy.15.uses, bf16[2,128,768]{2,1,0:T(8,128)(2,1)S(1)} %copy-done.20, ...), custom_call_target="tpu_custom_call" | custom-call | flops 1207959552 | bytes 9437184 | tf_op jit(solution)/shard_map/attend_blocks/pallas_call | solution.py:244
  343.0 6.2 %all-to-all-start.2 = ((bf16[8,2,128,768]{3,2,1,0:T(8,128)(2,1)}), bf16[8,2,128,768]{3,2,1,0:T(8,128)(2,1)S(1)}, u32[]{:S(2)}, u32[]{:S(2)}) async-start(bf16[8,2,128,768]{3,2,1,0:T(8,128)(2,1)} %get-tuple-element.115), calls=%async_computation.2 | async-start | bytes 6291456 | tf_op jit(solution)/shard_map/all_to_all | solution.py:36
  353.3 12.1 %collective-permute-done.10.refs_1_ = bf16[2,128,512]{2,1,0:T(8,128)(2,1)S(1)} collective-permute-done((bf16[2,128,512]{2,1,0:T(8,128)(2,1)}, bf16[2,128,512]{2,1,0:T(8,128)(2,1)S(1)}, u32[]{:S(2)}, u32[]{:S(2)}) %collective-permute-start.10) | collective-permute-done | bytes 262176 | tf_op jit(solution)/shard_map/ppermute | solution.py:27
  367.7 4.2 collective-permute-done.12.refs_3_
  373.4 9.2 %collective-permute-start.27 = (bf16[2,128,768]{2,1,0:T(8,128)(2,1)}, bf16[2,128,768]{2,1,0:T(8,128)(2,1)S(1)}, u32[]{:S(2)}, u32[]{:S(2)}) collective-permute-start(bf16[2,128,768]{2,1,0:T(8,128)(2,1)} %get-tuple-element.117), channel_id=1, source_target_pairs={{0,4},{4,0},{8,12},{12,8},{16,20},{20,16},{24,28},{28,24},{1,5},{5... | collective-permute-start | bytes 1179656 | tf_op jit(solution)/shard_map/ppermute | solution.py:27
  382.6 5.3 %collective-permute-done.24.refs_9_ = bf16[2,128,768]{2,1,0:T(8,128)(2,1)S(1)} collective-permute-done((bf16[2,128,768]{2,1,0:T(8,128)(2,1)}, bf16[2,128,768]{2,1,0:T(8,128)(2,1)S(1)}, u32[]{:S(2)}, u32[]{:S(2)}) %collective-permute-start.24) | collective-permute-done | bytes 393248 | tf_op jit(solution)/shard_map/ppermute | solution.py:27
  387.9 1.5 collective-permute-start.29
  389.5 8.7 %collective-permute-done.25.refs_10_ = bf16[2,128,768]{2,1,0:T(8,128)(2,1)S(1)} collective-permute-done((bf16[2,128,768]{2,1,0:T(8,128)(2,1)}, bf16[2,128,768]{2,1,0:T(8,128)(2,1)S(1)}, u32[]{:S(2)}, u32[]{:S(2)}) %collective-permute-start.25) | collective-permute-done | bytes 393248 | tf_op jit(solution)/shard_map/ppermute | solution.py:27
  399.3 1.3 collective-permute-start.31
  402.5 2.2 unpack_rows.1
  404.8 2.8 owner_sum.3.rest_8_
  407.6 2.0 collective-permute-done.28.rest_2_
  409.6 8.5 %collective-permute-done.29.rest_3_ = bf16[2,128,768]{2,1,0:T(8,128)(2,1)S(1)} collective-permute-done((bf16[2,128,768]{2,1,0:T(8,128)(2,1)}, bf16[2,128,768]{2,1,0:T(8,128)(2,1)S(1)}, u32[]{:S(2)}, u32[]{:S(2)}) %collective-permute-start.29) | collective-permute-done | bytes 393248 | tf_op jit(solution)/shard_map/ppermute | solution.py:27
  418.1 26.0 %collective-permute-done.30.rest_6_ = bf16[2,128,768]{2,1,0:T(8,128)(2,1)S(1)} collective-permute-done((bf16[2,128,768]{2,1,0:T(8,128)(2,1)}, bf16[2,128,768]{2,1,0:T(8,128)(2,1)S(1)}, u32[]{:S(2)}, u32[]{:S(2)}) %collective-permute-start.30) | collective-permute-done | bytes 393248 | tf_op jit(solution)/shard_map/ppermute | solution.py:27
  444.1 8.6 %collective-permute-done.31.rest_7_ = bf16[2,128,768]{2,1,0:T(8,128)(2,1)S(1)} collective-permute-done((bf16[2,128,768]{2,1,0:T(8,128)(2,1)}, bf16[2,128,768]{2,1,0:T(8,128)(2,1)S(1)}, u32[]{:S(2)}, u32[]{:S(2)}) %collective-permute-start.31) | collective-permute-done | bytes 393248 | tf_op jit(solution)/shard_map/ppermute | solution.py:27
  452.7 3.0 owner_sum.4.rest_1_
  455.7 2.9 owner_sum.5
  (95 shorter events, 26.8 us)
Async XLA Ops:
  5.7 5.7 %copy-start.25 = (s32[1,8,1]{1,2,0:T(1,128)S(1)}, s32[1,8,1]{1,2,0:T(1,128)}, u32[]{:S(2)}) copy-start(s32[1,8,1]{1,2,0:T(1,128)} %param.7) | copy-start | bytes 100
  5.8 51.2 %all-to-all-start = ((bf16[8,2,128,512]{3,2,1,0:T(8,128)(2,1)}), bf16[8,2,128,512]{3,2,1,0:T(8,128)(2,1)}, u32[]{:S(2)}, u32[]{:S(2)}) async-start(bf16[8,2,128,512]{3,2,1,0:T(8,128)(2,1)} %pick_whole.2), calls=%async_computation | async-start | bytes 4194304 | tf_op jit(solution)/shard_map/all_to_all | solution.py:36
  21.3 107.3 %copy-start.3 = (bf16[1,128,8192]{2,1,0:T(8,128)(2,1)S(1)}, bf16[1,128,8192]{2,1,0:T(8,128)(2,1)}, u32[]{:S(2)}) copy-start(bf16[1,128,8192]{2,1,0:T(8,128)(2,1)} %q_ref.2) | copy-start | bytes 6291460
  56.9 165.0 %all-to-all-start.1 = ((bf16[8,2,128,768]{3,2,1,0:T(8,128)(2,1)}), bf16[8,2,128,768]{3,2,1,0:T(8,128)(2,1)}, u32[]{:S(2)}, u32[]{:S(2)}) async-start(bf16[8,2,128,768]{3,2,1,0:T(8,128)(2,1)} %pick_whole.3), calls=%async_computation.1 | async-start | bytes 6291456 | tf_op jit(solution)/shard_map/all_to_all | solution.py:36
  64.9 119.5 %copy-start.24 = (s32[1,8,2]{1,2,0:T(2,128)S(1)}, s32[1,8,2]{1,2,0:T(2,128)}, u32[]{:S(2)}) copy-start(s32[1,8,2]{1,2,0:T(2,128)} %param.8) | copy-start | bytes 196
  64.9 4.8 %collective-permute-start.3 = (bf16[2,128,768]{2,1,0:T(8,128)(2,1)}, bf16[2,128,768]{2,1,0:T(8,128)(2,1)S(1)}, u32[]{:S(2)}, u32[]{:S(2)}) collective-permute-start(bf16[2,128,768]{2,1,0:T(8,128)(2,1)} %get-tuple-element.71), channel_id=1, source_target_pairs={{0,4},{4,0},{8,12},{12,8},{16,20},{20,16},{24,28},{28,24},{1,5},{5... | collective-permute-start | bytes 1179656 | tf_op jit(solution)/shard_map/ppermute | solution.py:27
  65.3 60.1 %collective-permute-start.4 = (bf16[2,128,768]{2,1,0:T(8,128)(2,1)}, bf16[2,128,768]{2,1,0:T(8,128)(2,1)S(1)}, u32[]{:S(2)}, u32[]{:S(2)}) collective-permute-start(bf16[2,128,768]{2,1,0:T(8,128)(2,1)} %get-tuple-element.72), channel_id=1, source_target_pairs={{0,8},{4,12},{8,0},{12,4},{16,24},{20,28},{24,16},{28,20},{1,9},{5... | collective-permute-start | bytes 1179656 | tf_op jit(solution)/shard_map/ppermute | solution.py:27
  65.3 68.6 %collective-permute-start.5 = (bf16[2,128,768]{2,1,0:T(8,128)(2,1)}, bf16[2,128,768]{2,1,0:T(8,128)(2,1)S(1)}, u32[]{:S(2)}, u32[]{:S(2)}) collective-permute-start(bf16[2,128,768]{2,1,0:T(8,128)(2,1)} %get-tuple-element.73), channel_id=1, source_target_pairs={{0,12},{4,8},{8,4},{12,0},{16,28},{20,24},{24,20},{28,16},{1,13},{... | collective-permute-start | bytes 1179656 | tf_op jit(solution)/shard_map/ppermute | solution.py:27
  67.1 108.0 %collective-permute-start.6 = (bf16[2,128,768]{2,1,0:T(8,128)(2,1)}, bf16[2,128,768]{2,1,0:T(8,128)(2,1)S(1)}, u32[]{:S(2)}, u32[]{:S(2)}) collective-permute-start(bf16[2,128,768]{2,1,0:T(8,128)(2,1)} %get-tuple-element.74), channel_id=1, source_target_pairs={{0,16},{4,20},{8,24},{12,28},{16,0},{20,4},{24,8},{28,12},{1,17},{... | collective-permute-start | bytes 1179656 | tf_op jit(solution)/shard_map/ppermute | solution.py:27
  69.2 114.3 %collective-permute-start.7 = (bf16[2,128,768]{2,1,0:T(8,128)(2,1)}, bf16[2,128,768]{2,1,0:T(8,128)(2,1)S(1)}, u32[]{:S(2)}, u32[]{:S(2)}) collective-permute-start(bf16[2,128,768]{2,1,0:T(8,128)(2,1)} %get-tuple-element.75), channel_id=1, source_target_pairs={{0,20},{4,16},{8,28},{12,24},{16,4},{20,0},{24,12},{28,8},{1,21},{... | collective-permute-start | bytes 1179656 | tf_op jit(solution)/shard_map/ppermute | solution.py:27
  69.7 123.9 %collective-permute-start.8 = (bf16[2,128,768]{2,1,0:T(8,128)(2,1)}, bf16[2,128,768]{2,1,0:T(8,128)(2,1)}, u32[]{:S(2)}, u32[]{:S(2)}) collective-permute-start(bf16[2,128,768]{2,1,0:T(8,128)(2,1)} %get-tuple-element.76), channel_id=1, source_target_pairs={{0,24},{4,28},{8,16},{12,20},{16,8},{20,12},{24,0},{28,4},{1,25},{... | collective-permute-start | bytes 1179656 | tf_op jit(solution)/shard_map/ppermute | solution.py:27
  125.4 76.8 %collective-permute-start.9 = (bf16[2,128,768]{2,1,0:T(8,128)(2,1)}, bf16[2,128,768]{2,1,0:T(8,128)(2,1)}, u32[]{:S(2)}, u32[]{:S(2)}) collective-permute-start(bf16[2,128,768]{2,1,0:T(8,128)(2,1)} %get-tuple-element.77), channel_id=1, source_target_pairs={{0,28},{4,24},{8,20},{12,16},{16,12},{20,8},{24,4},{28,0},{1,29},{... | collective-permute-start | bytes 1179656 | tf_op jit(solution)/shard_map/ppermute | solution.py:27
  133.9 88.0 %copy-start.14 = (bf16[2,128,768]{2,1,0:T(8,128)(2,1)}, bf16[2,128,768]{2,1,0:T(8,128)(2,1)S(1)}, u32[]{:S(2)}) copy-start(bf16[2,128,768]{2,1,0:T(8,128)(2,1)S(1)} %collective-permute-done.5.rest_7_) | copy-start | bytes 1179652
  133.9 68.3 %collective-permute-start = (bf16[2,128,512]{2,1,0:T(8,128)(2,1)}, bf16[2,128,512]{2,1,0:T(8,128)(2,1)S(1)}, u32[]{:S(2)}, u32[]{:S(2)}) collective-permute-start(bf16[2,128,512]{2,1,0:T(8,128)(2,1)} %get-tuple-element.68), channel_id=1, source_target_pairs={{0,1},{1,0},{2,3},{3,2},{4,5},{5,4},{6,7},{7,6},{8,9},{9,8},{10,11... | collective-permute-start | bytes 786440 | tf_op jit(solution)/shard_map/ppermute | solution.py:27
  175.9 26.4 %collective-permute-start.1 = (bf16[2,128,512]{2,1,0:T(8,128)(2,1)}, bf16[2,128,512]{2,1,0:T(8,128)(2,1)}, u32[]{:S(2)}, u32[]{:S(2)}) collective-permute-start(bf16[2,128,512]{2,1,0:T(8,128)(2,1)} %get-tuple-element.69), channel_id=1, source_target_pairs={{0,2},{1,3},{2,0},{3,1},{4,6},{5,7},{6,4},{7,5},{8,10},{9,11},{10,... | collective-permute-start | bytes 786440 | tf_op jit(solution)/shard_map/ppermute | solution.py:27
  184.3 18.0 %collective-permute-start.2 = (bf16[2,128,512]{2,1,0:T(8,128)(2,1)}, bf16[2,128,512]{2,1,0:T(8,128)(2,1)}, u32[]{:S(2)}, u32[]{:S(2)}) collective-permute-start(bf16[2,128,512]{2,1,0:T(8,128)(2,1)} %get-tuple-element.70), channel_id=1, source_target_pairs={{0,3},{1,2},{2,1},{3,0},{4,7},{5,6},{6,5},{7,4},{8,11},{9,10},{10,... | collective-permute-start | bytes 786440 | tf_op jit(solution)/shard_map/ppermute | solution.py:27
  221.9 121.1 %all-to-all-start.3 = ((bf16[8,2,128,512]{3,2,1,0:T(8,128)(2,1)}), bf16[8,2,128,512]{3,2,1,0:T(8,128)(2,1)}, u32[]{:S(2)}, u32[]{:S(2)}) async-start(bf16[8,2,128,512]{3,2,1,0:T(8,128)(2,1)} %get-tuple-element.124), calls=%async_computation.3 | async-start | bytes 4194304 | tf_op jit(solution)/shard_map/all_to_all | solution.py:36
  229.3 19.4 %copy-start.13 = (bf16[2,128,768]{2,1,0:T(8,128)(2,1)S(1)}, bf16[2,128,768]{2,1,0:T(8,128)(2,1)}, u32[]{:S(2)}) copy-start(bf16[2,128,768]{2,1,0:T(8,128)(2,1)} %get-tuple-element.88.rest_4_) | copy-start | bytes 1179652
  229.3 10.9 %collective-permute-start.13 = (bf16[2,128,768]{2,1,0:T(8,128)(2,1)}, bf16[2,128,768]{2,1,0:T(8,128)(2,1)}, u32[]{:S(2)}, u32[]{:S(2)}) collective-permute-start(bf16[2,128,768]{2,1,0:T(8,128)(2,1)} %get-tuple-element.85), channel_id=1, source_target_pairs={{0,1},{1,0},{2,3},{3,2},{4,5},{5,4},{6,7},{7,6},{8,9},{9,8},{10,11... | collective-permute-start | bytes 1179656 | tf_op jit(solution)/shard_map/ppermute | solution.py:27
  229.6 10.6 %collective-permute-start.14 = (bf16[2,128,768]{2,1,0:T(8,128)(2,1)}, bf16[2,128,768]{2,1,0:T(8,128)(2,1)}, u32[]{:S(2)}, u32[]{:S(2)}) collective-permute-start(bf16[2,128,768]{2,1,0:T(8,128)(2,1)} %get-tuple-element.86), channel_id=1, source_target_pairs={{0,2},{1,3},{2,0},{3,1},{4,6},{5,7},{6,4},{7,5},{8,10},{9,11},{10,... | collective-permute-start | bytes 1179656 | tf_op jit(solution)/shard_map/ppermute | solution.py:27
  229.9 18.8 %collective-permute-start.15 = (bf16[2,128,768]{2,1,0:T(8,128)(2,1)}, bf16[2,128,768]{2,1,0:T(8,128)(2,1)}, u32[]{:S(2)}, u32[]{:S(2)}) collective-permute-start(bf16[2,128,768]{2,1,0:T(8,128)(2,1)} %get-tuple-element.87), channel_id=1, source_target_pairs={{0,3},{1,2},{2,1},{3,0},{4,7},{5,6},{6,5},{7,4},{8,11},{9,10},{10,... | collective-permute-start | bytes 1179656 | tf_op jit(solution)/shard_map/ppermute | solution.py:27
  252.7 63.0 %copy-start.20 = (bf16[2,128,768]{2,1,0:T(8,128)(2,1)S(1)}, bf16[2,128,768]{2,1,0:T(8,128)(2,1)}, u32[]{:S(2)}) copy-start(bf16[2,128,768]{2,1,0:T(8,128)(2,1)} %get-tuple-element.101.rest_0_) | copy-start | bytes 1179652
  280.3 26.9 %collective-permute-start.22 = (bf16[2,128,768]{2,1,0:T(8,128)(2,1)}, bf16[2,128,768]{2,1,0:T(8,128)(2,1)S(1)}, u32[]{:S(2)}, u32[]{:S(2)}) collective-permute-start(bf16[2,128,768]{2,1,0:T(8,128)(2,1)} %get-tuple-element.106), channel_id=1, source_target_pairs={{0,16},{4,20},{8,24},{12,28},{16,0},{20,4},{24,8},{28,12},{1,17},{... | collective-permute-start | bytes 1179656 | tf_op jit(solution)/shard_map/ppermute | solution.py:27
  281.3 34.4 %collective-permute-start.23 = (bf16[2,128,768]{2,1,0:T(8,128)(2,1)}, bf16[2,128,768]{2,1,0:T(8,128)(2,1)S(1)}, u32[]{:S(2)}, u32[]{:S(2)}) collective-permute-start(bf16[2,128,768]{2,1,0:T(8,128)(2,1)} %get-tuple-element.107), channel_id=1, source_target_pairs={{0,20},{4,16},{8,28},{12,24},{16,4},{20,0},{24,12},{28,8},{1,21},{... | collective-permute-start | bytes 1179656 | tf_op jit(solution)/shard_map/ppermute | solution.py:27
  284.1 31.5 %collective-permute-start.19 = (bf16[2,128,768]{2,1,0:T(8,128)(2,1)}, bf16[2,128,768]{2,1,0:T(8,128)(2,1)S(1)}, u32[]{:S(2)}, u32[]{:S(2)}) collective-permute-start(bf16[2,128,768]{2,1,0:T(8,128)(2,1)} %get-tuple-element.102), channel_id=1, source_target_pairs={{0,1},{1,0},{2,3},{3,2},{4,5},{5,4},{6,7},{7,6},{8,9},{9,8},{10,11... | collective-permute-start | bytes 1179656 | tf_op jit(solution)/shard_map/ppermute | solution.py:27
  285.3 30.4 %collective-permute-start.20 = (bf16[2,128,768]{2,1,0:T(8,128)(2,1)}, bf16[2,128,768]{2,1,0:T(8,128)(2,1)S(1)}, u32[]{:S(2)}, u32[]{:S(2)}) collective-permute-start(bf16[2,128,768]{2,1,0:T(8,128)(2,1)} %get-tuple-element.103), channel_id=1, source_target_pairs={{0,2},{1,3},{2,0},{3,1},{4,6},{5,7},{6,4},{7,5},{8,10},{9,11},{10,... | collective-permute-start | bytes 1179656 | tf_op jit(solution)/shard_map/ppermute | solution.py:27
  285.5 30.2 %collective-permute-start.21 = (bf16[2,128,768]{2,1,0:T(8,128)(2,1)}, bf16[2,128,768]{2,1,0:T(8,128)(2,1)S(1)}, u32[]{:S(2)}, u32[]{:S(2)}) collective-permute-start(bf16[2,128,768]{2,1,0:T(8,128)(2,1)} %get-tuple-element.104), channel_id=1, source_target_pairs={{0,3},{1,2},{2,1},{3,0},{4,7},{5,6},{6,5},{7,4},{8,11},{9,10},{10,... | collective-permute-start | bytes 1179656 | tf_op jit(solution)/shard_map/ppermute | solution.py:27
  307.2 35.8 %copy-start.9 = (bf16[2,128,768]{2,1,0:T(8,128)(2,1)}, bf16[2,128,768]{2,1,0:T(8,128)(2,1)S(1)}, u32[]{:S(2)}) copy-start(bf16[2,128,768]{2,1,0:T(8,128)(2,1)S(1)} %collective-permute-done.22.rest_4_) | copy-start | bytes 1179652
  315.7 27.4 %copy-start.11 = (bf16[2,128,768]{2,1,0:T(8,128)(2,1)}, bf16[2,128,768]{2,1,0:T(8,128)(2,1)S(1)}, u32[]{:S(2)}) copy-start(bf16[2,128,768]{2,1,0:T(8,128)(2,1)S(1)} %collective-permute-done.23.rest_5_) | copy-start | bytes 1179652
  343.0 57.6 %copy-start.6 = (bf16[2,128,768]{2,1,0:T(8,128)(2,1)S(1)}, bf16[2,128,768]{2,1,0:T(8,128)(2,1)}, u32[]{:S(2)}) copy-start(bf16[2,128,768]{2,1,0:T(8,128)(2,1)} %get-tuple-element.96.refs_4_) | copy-start | bytes 1179652
  343.0 112.7 %all-to-all-start.2 = ((bf16[8,2,128,768]{3,2,1,0:T(8,128)(2,1)}), bf16[8,2,128,768]{3,2,1,0:T(8,128)(2,1)S(1)}, u32[]{:S(2)}, u32[]{:S(2)}) async-start(bf16[8,2,128,768]{3,2,1,0:T(8,128)(2,1)} %get-tuple-element.115), calls=%async_computation.2 | async-start | bytes 6291456 | tf_op jit(solution)/shard_map/all_to_all | solution.py:36
  349.2 23.0 %collective-permute-start.16 = (bf16[2,128,768]{2,1,0:T(8,128)(2,1)}, bf16[2,128,768]{2,1,0:T(8,128)(2,1)S(1)}, u32[]{:S(2)}, u32[]{:S(2)}) collective-permute-start(bf16[2,128,768]{2,1,0:T(8,128)(2,1)} %get-tuple-element.97), channel_id=1, source_target_pairs={{0,1},{1,0},{2,3},{3,2},{4,5},{5,4},{6,7},{7,6},{8,9},{9,8},{10,11... | collective-permute-start | bytes 1179656 | tf_op jit(solution)/shard_map/ppermute | solution.py:27
  349.5 15.9 %collective-permute-start.10 = (bf16[2,128,512]{2,1,0:T(8,128)(2,1)}, bf16[2,128,512]{2,1,0:T(8,128)(2,1)S(1)}, u32[]{:S(2)}, u32[]{:S(2)}) collective-permute-start(bf16[2,128,512]{2,1,0:T(8,128)(2,1)} %get-tuple-element.80), channel_id=1, source_target_pairs={{0,1},{1,0},{2,3},{3,2},{4,5},{5,4},{6,7},{7,6},{8,9},{9,8},{10,11... | collective-permute-start | bytes 786440 | tf_op jit(solution)/shard_map/ppermute | solution.py:27
  350.7 15.8 %collective-permute-start.11 = (bf16[2,128,512]{2,1,0:T(8,128)(2,1)}, bf16[2,128,512]{2,1,0:T(8,128)(2,1)S(1)}, u32[]{:S(2)}, u32[]{:S(2)}) collective-permute-start(bf16[2,128,512]{2,1,0:T(8,128)(2,1)} %get-tuple-element.81), channel_id=1, source_target_pairs={{0,2},{1,3},{2,0},{3,1},{4,6},{5,7},{6,4},{7,5},{8,10},{9,11},{10,... | collective-permute-start | bytes 786440 | tf_op jit(solution)/shard_map/ppermute | solution.py:27
  351.8 20.1 %collective-permute-start.12 = (bf16[2,128,512]{2,1,0:T(8,128)(2,1)}, bf16[2,128,512]{2,1,0:T(8,128)(2,1)S(1)}, u32[]{:S(2)}, u32[]{:S(2)}) collective-permute-start(bf16[2,128,512]{2,1,0:T(8,128)(2,1)} %get-tuple-element.82), channel_id=1, source_target_pairs={{0,3},{1,2},{2,1},{3,0},{4,7},{5,6},{6,5},{7,4},{8,11},{9,10},{10,... | collective-permute-start | bytes 786440 | tf_op jit(solution)/shard_map/ppermute | solution.py:27
  352.2 21.2 %collective-permute-start.17 = (bf16[2,128,768]{2,1,0:T(8,128)(2,1)}, bf16[2,128,768]{2,1,0:T(8,128)(2,1)S(1)}, u32[]{:S(2)}, u32[]{:S(2)}) collective-permute-start(bf16[2,128,768]{2,1,0:T(8,128)(2,1)} %get-tuple-element.98), channel_id=1, source_target_pairs={{0,2},{1,3},{2,0},{3,1},{4,6},{5,7},{6,4},{7,5},{8,10},{9,11},{10,... | collective-permute-start | bytes 1179656 | tf_op jit(solution)/shard_map/ppermute | solution.py:27
  365.4 17.1 %collective-permute-start.18 = (bf16[2,128,768]{2,1,0:T(8,128)(2,1)}, bf16[2,128,768]{2,1,0:T(8,128)(2,1)S(1)}, u32[]{:S(2)}, u32[]{:S(2)}) collective-permute-start(bf16[2,128,768]{2,1,0:T(8,128)(2,1)} %get-tuple-element.99), channel_id=1, source_target_pairs={{0,3},{1,2},{2,1},{3,0},{4,7},{5,6},{6,5},{7,4},{8,11},{9,10},{10,... | collective-permute-start | bytes 1179656 | tf_op jit(solution)/shard_map/ppermute | solution.py:27
  366.5 21.4 %collective-permute-start.24 = (bf16[2,128,768]{2,1,0:T(8,128)(2,1)}, bf16[2,128,768]{2,1,0:T(8,128)(2,1)S(1)}, u32[]{:S(2)}, u32[]{:S(2)}) collective-permute-start(bf16[2,128,768]{2,1,0:T(8,128)(2,1)} %get-tuple-element.110), channel_id=1, source_target_pairs={{0,1},{1,0},{2,3},{3,2},{4,5},{5,4},{6,7},{7,6},{8,9},{9,8},{10,11... | collective-permute-start | bytes 1179656 | tf_op jit(solution)/shard_map/ppermute | solution.py:27
  371.9 26.2 %collective-permute-start.25 = (bf16[2,128,768]{2,1,0:T(8,128)(2,1)}, bf16[2,128,768]{2,1,0:T(8,128)(2,1)S(1)}, u32[]{:S(2)}, u32[]{:S(2)}) collective-permute-start(bf16[2,128,768]{2,1,0:T(8,128)(2,1)} %get-tuple-element.111), channel_id=1, source_target_pairs={{0,2},{1,3},{2,0},{3,1},{4,6},{5,7},{6,4},{7,5},{8,10},{9,11},{10,... | collective-permute-start | bytes 1179656 | tf_op jit(solution)/shard_map/ppermute | solution.py:27
  372.3 27.0 %collective-permute-start.26 = (bf16[2,128,768]{2,1,0:T(8,128)(2,1)}, bf16[2,128,768]{2,1,0:T(8,128)(2,1)S(1)}, u32[]{:S(2)}, u32[]{:S(2)}) collective-permute-start(bf16[2,128,768]{2,1,0:T(8,128)(2,1)} %get-tuple-element.112), channel_id=1, source_target_pairs={{0,3},{1,2},{2,1},{3,0},{4,7},{5,6},{6,5},{7,4},{8,11},{9,10},{10,... | collective-permute-start | bytes 1179656 | tf_op jit(solution)/shard_map/ppermute | solution.py:27
  373.4 34.2 %collective-permute-start.27 = (bf16[2,128,768]{2,1,0:T(8,128)(2,1)}, bf16[2,128,768]{2,1,0:T(8,128)(2,1)S(1)}, u32[]{:S(2)}, u32[]{:S(2)}) collective-permute-start(bf16[2,128,768]{2,1,0:T(8,128)(2,1)} %get-tuple-element.117), channel_id=1, source_target_pairs={{0,4},{4,0},{8,12},{12,8},{16,20},{20,16},{24,28},{28,24},{1,5},{5... | collective-permute-start | bytes 1179656 | tf_op jit(solution)/shard_map/ppermute | solution.py:27
  382.6 27.1 %collective-permute-start.28 = (bf16[2,128,768]{2,1,0:T(8,128)(2,1)}, bf16[2,128,768]{2,1,0:T(8,128)(2,1)S(1)}, u32[]{:S(2)}, u32[]{:S(2)}) collective-permute-start(bf16[2,128,768]{2,1,0:T(8,128)(2,1)} %get-tuple-element.118), channel_id=1, source_target_pairs={{0,8},{4,12},{8,0},{12,4},{16,24},{20,28},{24,16},{28,20},{1,9},{5... | collective-permute-start | bytes 1179656 | tf_op jit(solution)/shard_map/ppermute | solution.py:27
  387.9 30.2 %collective-permute-start.29 = (bf16[2,128,768]{2,1,0:T(8,128)(2,1)}, bf16[2,128,768]{2,1,0:T(8,128)(2,1)S(1)}, u32[]{:S(2)}, u32[]{:S(2)}) collective-permute-start(bf16[2,128,768]{2,1,0:T(8,128)(2,1)} %get-tuple-element.119), channel_id=1, source_target_pairs={{0,12},{4,8},{8,4},{12,0},{16,28},{20,24},{24,20},{28,16},{1,13},{... | collective-permute-start | bytes 1179656 | tf_op jit(solution)/shard_map/ppermute | solution.py:27
  398.1 46.0 %collective-permute-start.30 = (bf16[2,128,768]{2,1,0:T(8,128)(2,1)}, bf16[2,128,768]{2,1,0:T(8,128)(2,1)S(1)}, u32[]{:S(2)}, u32[]{:S(2)}) collective-permute-start(bf16[2,128,768]{2,1,0:T(8,128)(2,1)} %get-tuple-element.121), channel_id=1, source_target_pairs={{0,24},{4,28},{8,16},{12,20},{16,8},{20,12},{24,0},{28,4},{1,25},{... | collective-permute-start | bytes 1179656 | tf_op jit(solution)/shard_map/ppermute | solution.py:27
  399.3 53.4 %collective-permute-start.31 = (bf16[2,128,768]{2,1,0:T(8,128)(2,1)}, bf16[2,128,768]{2,1,0:T(8,128)(2,1)S(1)}, u32[]{:S(2)}, u32[]{:S(2)}) collective-permute-start(bf16[2,128,768]{2,1,0:T(8,128)(2,1)} %get-tuple-element.123), channel_id=1, source_target_pairs={{0,28},{4,24},{8,20},{12,16},{16,12},{20,8},{24,4},{28,0},{1,29},{... | collective-permute-start | bytes 1179656 | tf_op jit(solution)/shard_map/ppermute | solution.py:27
  404.7 48.0 %copy-start.8 = (bf16[2,128,768]{2,1,0:T(8,128)(2,1)S(1)}, bf16[2,128,768]{2,1,0:T(8,128)(2,1)}, u32[]{:S(2)}) copy-start(bf16[2,128,768]{2,1,0:T(8,128)(2,1)} %get-tuple-element.116.rest_0_) | copy-start | bytes 1179652
  404.8 48.0 %copy-start.10 = (bf16[2,128,768]{2,1,0:T(8,128)(2,1)S(1)}, bf16[2,128,768]{2,1,0:T(8,128)(2,1)}, u32[]{:S(2)}) copy-start(bf16[2,128,768]{2,1,0:T(8,128)(2,1)} %copy-done.9) | copy-start | bytes 1179652
  404.8 48.0 %copy-start.12 = (bf16[2,128,768]{2,1,0:T(8,128)(2,1)S(1)}, bf16[2,128,768]{2,1,0:T(8,128)(2,1)}, u32[]{:S(2)}) copy-start(bf16[2,128,768]{2,1,0:T(8,128)(2,1)} %copy-done.11) | copy-start | bytes 1179652
  (14 other events, 18.2 us)

commit v7 on v6

v7 whole, which is shorter than its diff:
```python
import functools

import jax
import jax.numpy as jnp
from jax import lax
from jax.experimental import pallas as pl
from jax.experimental.pallas import tpu as pltpu
from jax.sharding import PartitionSpec as P

DH = 128
BLOCK = 64
NBLEN = 128
CHUNKS = 2
DEPTH = 4
ATTEND_WEIGHT = 24
F32 = jnp.float32
BF16 = jnp.bfloat16
VMEM_BYTES = 40 * 1024 * 1024


def partner(index, step, count):
    if count & (count - 1) == 0:
        return index ^ step
    return (step - index) % count


def exchange(array, axis, step, count):
    pairs = [(i, partner(i, step, count)) for i in range(count)]
    return lax.ppermute(array, axis, pairs)


def across(index, step, count):
    half = count // 2
    there = half + (index + step) % half
    return jnp.where(index < half, there, (index - step) % half)


def swap_near(array, count):
    half = count // 2
    groups = [list(range(half)), list(range(half, count))]
    return lax.all_to_all(
        array, "enc", split_axis=0, concat_axis=0, axis_index_groups=groups, tiled=True
    )


def swap_rows(pieces):
    count = len(pieces)
    return [pieces[0]] + [exchange(pieces[step], "seq", step, count) for step in range(1, count)]


def swap_pool(array):
    return lax.all_to_all(array, "enc", split_axis=0, concat_axis=0, tiled=True)


def after(array, earlier):
    return lax.optimization_barrier((array, earlier))[0]


def in_hbm(shape):
    return pltpu.HBM(shape, BF16)


def cost(moved, flops=0, exps=0):
    return pl.CostEstimate(flops=flops, bytes_accessed=moved, transcendentals=exps)


PARAMS = pltpu.CompilerParams(vmem_limit_bytes=VMEM_BYTES)
SCALARS = pl.BlockSpec(memory_space=pltpu.SMEM)
ANYWHERE = pl.BlockSpec(memory_space=pl.ANY)
IN_HBM = pl.BlockSpec(memory_space=pltpu.HBM)


def pack_kernel(first, width, q_ref, g_ref, *rest):
    outs, sems = rest[:-1], rest[-1]
    parts, chunk = len(outs), outs[0].shape[-1]
    me = lax.axis_index("seq")
    copies = []
    for step, out in enumerate(outs):
        start = pl.multiple_of(partner(me, step, parts) * width + first, DH)
        for n, ref in enumerate((q_ref, g_ref)):
            source = ref.at[0, :, pl.ds(start, chunk)]
            copies.append(pltpu.make_async_copy(source, out.at[n], sems.at[2 * step + n]))
            copies[-1].start()
    for copy in copies:
        copy.wait()


def pack(first, chunk, queries, grads, width, parts):
    shape = (2, queries.shape[1], chunk)
    return pl.pallas_call(
        functools.partial(pack_kernel, first, width),
        grid=(1,),
        in_specs=[IN_HBM, IN_HBM],
        out_specs=[pl.BlockSpec(shape, lambda i: (0, 0, 0))] * parts,
        out_shape=[in_hbm(shape)] * parts,
        scratch_shapes=[pltpu.SemaphoreType.DMA((2 * parts,))],
        compiler_params=PARAMS,
        cost_estimate=cost(8 * parts * queries.shape[1] * chunk),
        name="pack_rows",
    )(queries, grads)


def unpack_kernel(firsts, width, *refs):
    ins, (ctx_ref, gq_ref, sems) = refs[:-3], refs[-3:]
    parts = len(ins) // len(firsts)
    me = lax.axis_index("seq")
    copies = []
    for n, src in enumerate(ins):
        first, step = firsts[n // parts], n % parts
        start = pl.multiple_of(partner(me, step, parts) * width + first, DH)
        for k, ref in enumerate((ctx_ref, gq_ref)):
            target = ref.at[0, :, pl.ds(start, src.shape[-1])]
            copies.append(pltpu.make_async_copy(src.at[k], target, sems.at[2 * n + k]))
            copies[-1].start()
    for copy in copies:
        copy.wait()


def unpack(pieces, firsts, width, shape):
    flat = [array for piece in pieces for array in piece]
    return pl.pallas_call(
        functools.partial(unpack_kernel, firsts, width),
        grid=(1,),
        in_specs=[pl.BlockSpec(array.shape, lambda i: (0, 0, 0)) for array in flat],
        out_specs=[IN_HBM, IN_HBM],
        out_shape=[in_hbm(shape)] * 2,
        scratch_shapes=[pltpu.SemaphoreType.DMA((2 * len(flat),))],
        compiler_params=PARAMS,
        cost_estimate=cost(8 * shape[1] * shape[2]),
        name="unpack_rows",
    )(*flat)


def pick_kernel(first, lists, pool_ref, out_ref, sems):
    copies = []
    for seq in range(out_ref.shape[0]):
        source = pool_ref.at[lists[0, seq, 0], :, :, first : first + out_ref.shape[-1]]
        copies.append(pltpu.make_async_copy(source, out_ref.at[seq], sems.at[seq]))
        copies[-1].start()
    for copy in copies:
        copy.wait()


def pick(first, chunk, send_lists, kv_pool):
    shape = (send_lists.shape[1], 2, NBLEN, chunk)
    return pl.pallas_call(
        functools.partial(pick_kernel, first),
        grid=(1,),
        in_specs=[SCALARS, IN_HBM],
        out_specs=pl.BlockSpec(shape, lambda i: (0, 0, 0, 0)),
        out_shape=in_hbm(shape),
        scratch_shapes=[pltpu.SemaphoreType.DMA((shape[0],))],
        compiler_params=PARAMS,
        cost_estimate=cost(8 * shape[0] * NBLEN * chunk),
        name="pick_entries",
    )(send_lists, kv_pool)


def dot(left, right, left_dim, right_dim):
    return lax.dot_general(
        left, right, (((left_dim,), (right_dim,)), ((), ())), preferred_element_type=F32
    )


def attend_kernel(seqs, parts, uses, *rest):
    half = seqs // 2
    rows_in, held, rest = rest[:parts], rest[parts], rest[parts + 1 :]
    rows_out, near_out, rest = rest[:parts], rest[parts], rest[parts + 1 :]
    far_out, (rows, made, sums) = rest[:half], rest[half:]
    scale = DH ** (-0.5)
    me, mine = lax.axis_index("enc"), lax.axis_index("seq")

    for step in range(parts):
        for n in range(2):
            piece = rows_in[step][n].astype(F32)
            rows[partner(mine, step, parts), n] = pltpu.roll(piece, 1, 0)
    rows[parts] = jnp.zeros(rows.shape[1:], F32)
    made[0, :, :BLOCK] = jnp.zeros((2, BLOCK, DH), F32)
    sums[...] = jnp.zeros_like(sums)
    first_row = lax.broadcasted_iota(jnp.int32, (BLOCK, DH), 0) == 0

    def one_block(block, q, g):
        first, second = uses[0, block, 0], uses[0, block, 1]
        keys = jnp.concatenate([held[first, 0], held[second, 0]], axis=0)
        values = jnp.concatenate([held[first, 1], held[second, 1]], axis=0)
        scores = dot(q, keys, 1, 1) * scale
        weights = jnp.exp(scores - jnp.max(scores, axis=1, keepdims=True))
        probs = weights / jnp.sum(weights, axis=1, keepdims=True)
        probs_low = probs.astype(BF16)
        out = dot(probs_low, values, 1, 0)
        grad_probs = dot(g, values, 1, 1)
        inner = jnp.sum(probs * grad_probs, axis=1, keepdims=True)
        grad_scores = (probs * (grad_probs - inner) * scale).astype(BF16)
        grad_q = dot(grad_scores, keys, 1, 0)
        grad_keys = dot(grad_scores, q, 0, 0)
        grad_values = dot(probs_low, g, 0, 0)
        sums[first, 0] += grad_keys[:NBLEN]
        sums[second, 0] += grad_keys[NBLEN:]
        sums[first, 1] += grad_values[:NBLEN]
        sums[second, 1] += grad_values[NBLEN:]
        return out, grad_q

    def one_part(part, carry):
        q, g = (rows[part, n, BLOCK:].astype(BF16) for n in range(2))
        for n, result in enumerate(one_block(2 * part, q, g)):
            made[part, n, BLOCK:] = result
        q, g = (
            jnp.where(first_row, rows[part, n, :BLOCK], rows[part + 1, n, :BLOCK]).astype(BF16)
            for n in range(2)
        )
        for n, result in enumerate(one_block(2 * part + 1, q, g)):
            made[part + 1, n, :BLOCK] = result
            made[part, n, :1] = result[:1]
        return carry

    if parts <= 4:
        for part in range(parts):
            one_part(part, 0)
    else:
        lax.fori_loop(0, parts, one_part, 0)

    for step in range(parts):
        for n in range(2):
            piece = made[partner(mine, step, parts), n]
            rows_out[step][n] = pltpu.roll(piece, 2 * BLOCK - 1, 0).astype(BF16)
    base = me - me % half
    for step in range(half):
        near_out[step] = sums[base + step].astype(BF16)
        far_out[step][...] = sums[across(me, step, seqs)].astype(BF16)


def attend(uses, rows_in, arrived):
    parts, part_rows = len(rows_in), rows_in[0].shape[1]
    seqs, _, _, chunk = arrived.shape
    half, heads = seqs // 2, chunk // DH
    rows_spec = pl.BlockSpec((2, part_rows, DH), lambda i: (0, 0, i))
    far_spec = pl.BlockSpec((2, NBLEN, DH), lambda i: (0, 0, i))
    pairs = heads * parts * part_rows * 2 * NBLEN
    outs = pl.pallas_call(
        functools.partial(attend_kernel, seqs, parts),
        grid=(heads,),
        in_specs=[SCALARS]
        + [rows_spec] * parts
        + [pl.BlockSpec((seqs, 2, NBLEN, DH), lambda i: (0, 0, 0, i))],
        out_specs=[rows_spec] * parts
        + [pl.BlockSpec((half, 2, NBLEN, DH), lambda i: (0, 0, 0, i))]
        + [far_spec] * half,
        scratch_shapes=[
            pltpu.VMEM((parts + 1, 2, part_rows, DH), F32),
            pltpu.VMEM((parts + 1, 2, part_rows, DH), F32),
            pltpu.VMEM((seqs, 2, NBLEN, DH), F32),
        ],
        out_shape=[in_hbm((2, part_rows, chunk))] * parts
        + [in_hbm((half, 2, NBLEN, chunk))]
        + [in_hbm((2, NBLEN, chunk))] * half,
        compiler_params=PARAMS,
        cost_estimate=cost(
            8 * (seqs + parts) * NBLEN * chunk, ATTEND_WEIGHT * 12 * DH * pairs, pairs
        ),
        name="attend_blocks",
    )(uses, *rows_in, arrived)
    return outs[:parts], outs[parts], outs[parts + 1 :]


def owner_kernel(seqs, lists, near_ref, *rest):
    half = seqs // 2
    far_refs, out_ref, acc = rest[:half], rest[-2], rest[-1]
    me = lax.axis_index("enc")
    base = me - me % half
    acc[...] = jnp.zeros_like(acc)
    for step in range(half):
        acc[lists[0, base + step, 0]] += near_ref[step].astype(F32)
        acc[lists[0, across(me, step, seqs), 0]] += far_refs[step][...].astype(F32)
    out_ref[...] = acc[...].astype(BF16)


def owner_sum(h, send_lists, near, far, shape, so_far):
    half = len(far)
    chunk = near.shape[-1]
    wide = min(chunk, 256)
    steps = chunk // wide
    extra = [] if so_far is None else [so_far]
    return pl.pallas_call(
        functools.partial(owner_kernel, 2 * half),
        grid=(steps,),
        in_specs=[SCALARS, pl.BlockSpec((half, 2, NBLEN, wide), lambda i: (0, 0, 0, i))]
        + [pl.BlockSpec((2, NBLEN, wide), lambda i: (0, 0, i))] * half
        + [ANYWHERE] * len(extra),
        out_specs=pl.BlockSpec(
            (shape[0], 2, NBLEN, wide), lambda i: (0, 0, 0, h * steps + i)
        ),
        scratch_shapes=[pltpu.VMEM((shape[0], 2, NBLEN, wide), F32)],
        out_shape=in_hbm(shape),
        input_output_aliases={half + 2: 0} if extra else {},
        compiler_params=PARAMS,
        cost_estimate=cost(4 * (2 * half + shape[0]) * NBLEN * chunk, 4 * half * NBLEN * chunk),
        name="owner_sum",
    )(send_lists, near, *far, *extra)


def swap_far(pieces, done):
    half = len(pieces)
    there = [[half + (i + step) % half for i in range(half)] for step in range(half)]
    got = []
    for step, piece in enumerate(pieces):
        if len(done) >= DEPTH:
            piece = after(piece, done[-DEPTH])
        pairs = list(enumerate(there[step])) + [(peer, i) for i, peer in enumerate(there[step])]
        got.append(lax.ppermute(piece, "enc", pairs))
        done.append(got[-1])
    return got


def local(seqs, parts, queries, kv_pool, send_lists, block_slots, grad_context):
    width = kv_pool.shape[-1]
    chunks = min(CHUNKS, width // DH)
    chunk = width // chunks
    firsts = [h * chunk for h in range(chunks)]

    arrived, rows = [], []
    for first in firsts:
        picked = pick(first, chunk, send_lists, kv_pool)
        send_lists, queries = after((send_lists, queries), picked)
        arrived.append(swap_pool(picked))
        rows.append(swap_rows(pack(first, chunk, queries, grad_context, width, parts)))
    done, returns, token_parts = [], [], []
    for h in range(chunks):
        rows_out, near, far = attend(block_slots, rows[h], arrived[h])
        far = swap_far(far, done)
        if h > 0:
            near, rows_out = after((near, rows_out), done[:DEPTH])
        returns.append((swap_near(near, seqs), far))
        token_parts.append(swap_rows(rows_out))
    context, grad_queries = unpack(token_parts, firsts, width, queries.shape)
    pool_grads = None
    for h in range(chunks):
        pool_grads = owner_sum(h, send_lists, *returns[h], kv_pool.shape, pool_grads)
    return (context, grad_queries, pool_grads)


def solution(mesh):
    in_specs = (
        P("enc", "seq", None),
        P("enc", None, None, "seq"),
        P("enc", None, None),
        P("enc", None, None),
        P("enc", "seq", None),
    )
    out_specs = (P("enc", "seq", None), P("enc", "seq", None), P("enc", None, None, "seq"))
    body = functools.partial(local, mesh.shape["enc"], mesh.shape["seq"])
    return jax.shard_map(body, mesh=mesh, in_specs=in_specs, out_specs=out_specs, check_vma=False)
```

time: 460 us -> 425 us (0.924)
  the two profiles are of different devices: /device:TPU:15 before, /device:TPU:5 now
where the time goes in v7:
time: 425 us; the launch traced here: 423 us
  waiting for transfers between devices  260 us (61%)
  Pallas kernels  93 us (22%)
  starting transfers between devices  47 us (11%)
  local copies, waits for them, and re-layouts  23 us (5%)
    all_to_all x2, waiting for transfers between devices, swap_pool(): return lax.all_to_all(array, 'enc', split_axis=0, concat_axis=0, tiled=True)  152 us
    pallas_call x2, Pallas kernels, attend(): pl.pallas_call(functools.partial(attend_kernel, seqs, parts), grid=(heads...  71.5 us
    ppermute x8, waiting for transfers between devices, swap_far(): got.append(lax.ppermute(piece, 'enc', pairs))  56 us
    ppermute x12, waiting for transfers between devices, exchange(): return lax.ppermute(array, axis, pairs)  51.9 us
    unnamed x58, local copies, waits for them, and re-layouts  22.8 us
    ppermute x8, starting transfers between devices, swap_far(): got.append(lax.ppermute(piece, 'enc', pairs))  16.1 us
    all_to_all x2, starting transfers between devices, swap_pool(): return lax.all_to_all(array, 'enc', split_axis=0, concat_axis=0, tiled=True)  10.9 us
    ppermute x12, starting transfers between devices, exchange(): return lax.ppermute(array, axis, pairs)  10.7 us
  transfers between devices with their start and end apart: 24, of which 11 were waited for; matrix products, arithmetic and copies ran while one was open for 0% of the time, Pallas kernels for 20%

profile of v7, /device:TPU:5, one launch (start us, length us, event | category | flops | bytes accessed | tf_op | source)
XLA Modules:
  0.0 423.3 jit_solution(9085380966900637509)
XLA Ops:
  1.4 2.2 copy-done
  3.5 3.1 pick_entries.2
  6.6 5.6 %all-to-all-start = ((bf16[8,2,128,1024]{3,2,1,0:T(8,128)(2,1)}), bf16[8,2,128,1024]{3,2,1,0:T(8,128)(2,1)}, u32[]{:S(2)}, u32[]{:S(2)}) async-start(bf16[8,2,128,1024]{3,2,1,0:T(8,128)(2,1)} %pick_entries.2), calls=%async_computation | async-start | bytes 8388608 | tf_op jit(solution)/shard_map/all_to_all | solution.py:52
  12.3 2.2 copy-done.1
  14.5 3.1 pick_entries.3
  17.5 87.9 %all-to-all-done.rest_4_ = bf16[8,2,128,1024]{3,2,1,0:T(8,128)(2,1)} async-done(((bf16[8,2,128,1024]{3,2,1,0:T(8,128)(2,1)}), bf16[8,2,128,1024]{3,2,1,0:T(8,128)(2,1)}, u32[]{:S(2)}, u32[]{:S(2)}) %all-to-all-start) | async-done | bytes 4194336 | tf_op jit(solution)/shard_map/all_to_all | solution.py:52
  105.5 5.3 %all-to-all-start.1 = ((bf16[8,2,128,1024]{3,2,1,0:T(8,128)(2,1)}), bf16[8,2,128,1024]{3,2,1,0:T(8,128)(2,1)}, u32[]{:S(2)}, u32[]{:S(2)}) async-start(bf16[8,2,128,1024]{3,2,1,0:T(8,128)(2,1)} %pick_entries.3), calls=%async_computation.1 | async-start | bytes 8388608 | tf_op jit(solution)/shard_map/all_to_all | solution.py:52
  110.8 1.6 copy-done.3
  112.4 1.6 pack_rows.2
  113.9 1.3 collective-permute-start
  115.4 1.2 collective-permute-start.2
  116.6 1.6 pack_rows.3
  118.2 1.3 collective-permute-start.6
  119.8 7.9 %collective-permute-done.rest_1_ = bf16[2,128,1024]{2,1,0:T(8,128)(2,1)S(1)} collective-permute-done((bf16[2,128,1024]{2,1,0:T(8,128)(2,1)}, bf16[2,128,1024]{2,1,0:T(8,128)(2,1)S(1)}, u32[]{:S(2)}, u32[]{:S(2)}) %collective-permute-start) | collective-permute-done | bytes 524320 | tf_op jit(solution)/shard_map/ppermute | solution.py:29
  127.7 1.2 collective-permute-start.8
  128.8 10.7 %collective-permute-done.1.rest_2_ = bf16[2,128,1024]{2,1,0:T(8,128)(2,1)} collective-permute-done((bf16[2,128,1024]{2,1,0:T(8,128)(2,1)}, bf16[2,128,1024]{2,1,0:T(8,128)(2,1)}, u32[]{:S(2)}, u32[]{:S(2)}) %collective-permute-start.1) | collective-permute-done | bytes 524320 | tf_op jit(solution)/shard_map/ppermute | solution.py:29
  139.6 35.7 %attend_blocks.2 = (bf16[2,128,1024]{2,1,0:T(8,128)(2,1)}, bf16[2,128,1024]{2,1,0:T(8,128)(2,1)}, bf16[2,128,1024]{2,1,0:T(8,128)(2,1)}, bf16[2,128,1024]{2,1,0:...) custom-call(s32[1,8,2]{2,1,0:T(8,128)S(1)} %copy.10.uses, ...), custom_call_target="tpu_custom_call" | custom-call | flops 38654705664 | bytes 12582912 | tf_op jit(solution)/shard_map/attend_blocks/pallas_call | solution.py:239
  175.3 1.7 collective-permute-start.9
  176.9 4.6 %collective-permute-start.10 = (bf16[2,128,1024]{2,1,0:T(8,128)(2,1)}, bf16[2,128,1024]{2,1,0:T(8,128)(2,1)S(1)}, u32[]{:S(2)}, u32[]{:S(2)}) collective-permute-start(bf16[2,128,1024]{2,1,0:T(8,128)(2,1)} %get-tuple-element.65), channel_id=1, source_target_pairs={{0,20},{4,24},{8,28},{12,16},{20,0},{24,4},{28,8},{16,12},{1,21},{... | collective-permute-start | bytes 1572872 | tf_op jit(solution)/shard_map/ppermute | solution.py:309
  182.4 2.1 collective-permute-start.11
  185.3 63.7 %all-to-all-done.1.rest_4_ = bf16[8,2,128,1024]{3,2,1,0:T(8,128)(2,1)} async-done(((bf16[8,2,128,1024]{3,2,1,0:T(8,128)(2,1)}), bf16[8,2,128,1024]{3,2,1,0:T(8,128)(2,1)}, u32[]{:S(2)}, u32[]{:S(2)}) %all-to-all-start.1) | async-done | bytes 4194336 | tf_op jit(solution)/shard_map/all_to_all | solution.py:52
  249.0 4.9 %all-to-all-start.3 = ((bf16[4,2,128,1024]{3,2,1,0:T(8,128)(2,1)}), bf16[4,2,128,1024]{3,2,1,0:T(8,128)(2,1)S(1)}, u32[]{:S(2)}, u32[]{:S(2)}) async-start(bf16[4,2,128,1024]{3,2,1,0:T(8,128)(2,1)} %get-tuple-element.84), calls=%async_computation.3 | async-start | bytes 4194304 | tf_op jit(solution)/shard_map/all_to_all | solution.py:41
  253.9 1.0 copy-done.20
  254.9 1.0 copy-done.22
  256.0 1.0 copy-done.24
  257.0 35.9 %attend_blocks.3 = (bf16[2,128,1024]{2,1,0:T(8,128)(2,1)}, bf16[2,128,1024]{2,1,0:T(8,128)(2,1)}, bf16[2,128,1024]{2,1,0:T(8,128)(2,1)}, bf16[2,128,1024]{2,1,0:...) custom-call(s32[1,8,2]{2,1,0:T(8,128)S(1)} %copy.10.uses, ...), custom_call_target="tpu_custom_call" | custom-call | flops 38654705664 | bytes 12582912 | tf_op jit(solution)/shard_map/attend_blocks/pallas_call | solution.py:239
  293.0 1.2 collective-permute-done.12.rest_3_
  294.2 4.4 %all-to-all-start.2 = ((bf16[4,2,128,1024]{3,2,1,0:T(8,128)(2,1)}), bf16[4,2,128,1024]{3,2,1,0:T(8,128)(2,1)}, u32[]{:S(2)}, u32[]{:S(2)}) async-start(bf16[4,2,128,1024]{3,2,1,0:T(8,128)(2,1)} %get-tuple-element.75), calls=%async_computation.2 | async-start | bytes 4194304 | tf_op jit(solution)/shard_map/all_to_all | solution.py:41
  298.6 1.3 collective-permute-start.3
  300.1 1.2 collective-permute-start.5
  301.3 1.2 collective-permute-start.13
  302.8 9.6 %collective-permute-done.3.refs_1_ = bf16[2,128,1024]{2,1,0:T(8,128)(2,1)S(1)} collective-permute-done((bf16[2,128,1024]{2,1,0:T(8,128)(2,1)}, bf16[2,128,1024]{2,1,0:T(8,128)(2,1)S(1)}, u32[]{:S(2)}, u32[]{:S(2)}) %collective-permute-start.3) | collective-permute-done | bytes 524320 | tf_op jit(solution)/shard_map/ppermute | solution.py:29
  313.2 1.2 collective-permute-start.15
  314.3 10.2 %collective-permute-done.4.refs_2_ = bf16[2,128,1024]{2,1,0:T(8,128)(2,1)S(1)} collective-permute-done((bf16[2,128,1024]{2,1,0:T(8,128)(2,1)}, bf16[2,128,1024]{2,1,0:T(8,128)(2,1)S(1)}, u32[]{:S(2)}, u32[]{:S(2)}) %collective-permute-start.4) | collective-permute-done | bytes 524320 | tf_op jit(solution)/shard_map/ppermute | solution.py:29
  326.3 5.6 %collective-permute-start.17 = (bf16[2,128,1024]{2,1,0:T(8,128)(2,1)}, bf16[2,128,1024]{2,1,0:T(8,128)(2,1)S(1)}, u32[]{:S(2)}, u32[]{:S(2)}) collective-permute-start(bf16[2,128,1024]{2,1,0:T(8,128)(2,1)} %get-tuple-element.79), channel_id=1, source_target_pairs={{0,20},{4,24},{8,28},{12,16},{20,0},{24,4},{28,8},{16,12},{1,21},{... | collective-permute-start | bytes 1572872 | tf_op jit(solution)/shard_map/ppermute | solution.py:309
  331.9 3.0 collective-permute-done.13.refs_5_
  336.4 10.5 %collective-permute-done.14.refs_6_ = bf16[2,128,1024]{2,1,0:T(8,128)(2,1)S(1)} collective-permute-done((bf16[2,128,1024]{2,1,0:T(8,128)(2,1)}, bf16[2,128,1024]{2,1,0:T(8,128)(2,1)S(1)}, u32[]{:S(2)}, u32[]{:S(2)}) %collective-permute-start.14) | collective-permute-done | bytes 524320 | tf_op jit(solution)/shard_map/ppermute | solution.py:29
  347.8 1.1 collective-permute-start.19
  349.0 1.0 copy-done.4
  351.1 1.0 copy-done.7
  352.1 1.0 copy-done.9
  354.2 1.0 copy-done.13
  355.2 1.0 copy-done.15
  356.3 3.3 unpack_rows.1
  359.6 4.4 %owner_sum.2.rest_4_ = bf16[4,2,128,2048]{3,2,1,0:T(8,128)(2,1)} custom-call(s32[1,8,1]{2,1,0:T(8,128)S(1)} %copy.14.lists, bf16[4,2,128,1024]{3,2,1,0:T(8,128)(2,1)S(1)} %all-to-all-done.3.near_ref, bf16[2,128,1024]{2,1,0:T(8,128)(2,1)S(1)} %copy-done.17, bf16[2,128,1024]{2,1,0:T(8,128)(2,1)S(1)} %copy-done.19, ...), custom_call_target="tpu_custom_call" | custom-call | flops 2097152 | bytes 6291456 | tf_op jit(solution)/shard_map/owner_sum/pallas_call | solution.py:283
  364.0 21.2 %collective-permute-done.16.rest_0_ = bf16[2,128,1024]{2,1,0:T(8,128)(2,1)S(1)} collective-permute-done((bf16[2,128,1024]{2,1,0:T(8,128)(2,1)}, bf16[2,128,1024]{2,1,0:T(8,128)(2,1)S(1)}, u32[]{:S(2)}, u32[]{:S(2)}) %collective-permute-start.16) | collective-permute-done | bytes 524320 | tf_op jit(solution)/shard_map/ppermute | solution.py:309
  385.2 33.6 %collective-permute-done.19.rest_3_ = bf16[2,128,1024]{2,1,0:T(8,128)(2,1)} collective-permute-done((bf16[2,128,1024]{2,1,0:T(8,128)(2,1)}, bf16[2,128,1024]{2,1,0:T(8,128)(2,1)}, u32[]{:S(2)}, u32[]{:S(2)}) %collective-permute-start.19) | collective-permute-done | bytes 524320 | tf_op jit(solution)/shard_map/ppermute | solution.py:309
  418.8 4.5 %owner_sum.3 = bf16[4,2,128,2048]{3,2,1,0:T(8,128)(2,1)} custom-call(s32[1,8,1]{2,1,0:T(8,128)S(1)} %copy.14.lists, bf16[4,2,128,1024]{3,2,1,0:T(8,128)(2,1)} %all-to-all-done.2.near_ref, bf16[2,128,1024]{2,1,0:T(8,128)(2,1)S(1)} %collective-permute-done.16.rest_0_, ...), custom_call_target="tpu_custom_call", output_to_operand_aliasing={{}: (6, {})} | custom-call | flops 2097152 | bytes 6291456 | tf_op jit(solution)/shard_map/owner_sum/pallas_call | solution.py:283
  (69 shorter events, 10.6 us)
Async XLA Ops:
  1.4 2.2 copy-start
  6.6 5.6 %copy-start.26 = (s32[1,8,1]{1,2,0:T(1,128)S(1)}, s32[1,8,1]{1,2,0:T(1,128)}, u32[]{:S(2)}) copy-start(s32[1,8,1]{1,2,0:T(1,128)} %param.7) | copy-start | bytes 100
  6.6 98.8 %all-to-all-start = ((bf16[8,2,128,1024]{3,2,1,0:T(8,128)(2,1)}), bf16[8,2,128,1024]{3,2,1,0:T(8,128)(2,1)}, u32[]{:S(2)}, u32[]{:S(2)}) async-start(bf16[8,2,128,1024]{3,2,1,0:T(8,128)(2,1)} %pick_entries.2), calls=%async_computation | async-start | bytes 8388608 | tf_op jit(solution)/shard_map/all_to_all | solution.py:52
  12.3 2.2 copy-start.1
  17.5 93.2 %copy-start.2 = (bf16[1,128,8192]{2,1,0:T(8,128)(2,1)S(1)}, bf16[1,128,8192]{2,1,0:T(8,128)(2,1)}, u32[]{:S(2)}) copy-start(bf16[1,128,8192]{2,1,0:T(8,128)(2,1)} %q_ref.1) | copy-start | bytes 6291460
  105.5 143.5 %all-to-all-start.1 = ((bf16[8,2,128,1024]{3,2,1,0:T(8,128)(2,1)}), bf16[8,2,128,1024]{3,2,1,0:T(8,128)(2,1)}, u32[]{:S(2)}, u32[]{:S(2)}) async-start(bf16[8,2,128,1024]{3,2,1,0:T(8,128)(2,1)} %pick_entries.3), calls=%async_computation.1 | async-start | bytes 8388608 | tf_op jit(solution)/shard_map/all_to_all | solution.py:52
  110.8 1.6 copy-start.3
  113.9 13.8 %collective-permute-start = (bf16[2,128,1024]{2,1,0:T(8,128)(2,1)}, bf16[2,128,1024]{2,1,0:T(8,128)(2,1)S(1)}, u32[]{:S(2)}, u32[]{:S(2)}) collective-permute-start(bf16[2,128,1024]{2,1,0:T(8,128)(2,1)} %get-tuple-element.46), channel_id=1, source_target_pairs={{0,1},{1,0},{2,3},{3,2},{4,5},{5,4},{6,7},{7,6},{8,9},{9,8},{10,11... | collective-permute-start | bytes 1572872 | tf_op jit(solution)/shard_map/ppermute | solution.py:29
  115.2 24.4 %collective-permute-start.1 = (bf16[2,128,1024]{2,1,0:T(8,128)(2,1)}, bf16[2,128,1024]{2,1,0:T(8,128)(2,1)}, u32[]{:S(2)}, u32[]{:S(2)}) collective-permute-start(bf16[2,128,1024]{2,1,0:T(8,128)(2,1)} %get-tuple-element.47), channel_id=1, source_target_pairs={{0,2},{1,3},{2,0},{3,1},{4,6},{5,7},{6,4},{7,5},{8,10},{9,11},{10,... | collective-permute-start | bytes 1572872 | tf_op jit(solution)/shard_map/ppermute | solution.py:29
  115.4 4.3 %copy-start.27 = (s32[1,8,2]{1,2,0:T(2,128)S(1)}, s32[1,8,2]{1,2,0:T(2,128)}, u32[]{:S(2)}) copy-start(s32[1,8,2]{1,2,0:T(2,128)} %param.8) | copy-start | bytes 196
  115.4 24.2 %copy-start.25 = (bf16[2,128,1024]{2,1,0:T(8,128)(2,1)S(1)}, bf16[2,128,1024]{2,1,0:T(8,128)(2,1)}, u32[]{:S(2)}) copy-start(bf16[2,128,1024]{2,1,0:T(8,128)(2,1)} %get-tuple-element.45.rest_0_) | copy-start | bytes 1572868
  115.4 24.2 %collective-permute-start.2 = (bf16[2,128,1024]{2,1,0:T(8,128)(2,1)}, bf16[2,128,1024]{2,1,0:T(8,128)(2,1)}, u32[]{:S(2)}, u32[]{:S(2)}) collective-permute-start(bf16[2,128,1024]{2,1,0:T(8,128)(2,1)} %get-tuple-element.48), channel_id=1, source_target_pairs={{0,3},{1,2},{2,1},{3,0},{4,7},{5,6},{6,5},{7,4},{8,11},{9,10},{10,... | collective-permute-start | bytes 1572872 | tf_op jit(solution)/shard_map/ppermute | solution.py:29
  118.2 63.3 %collective-permute-start.6 = (bf16[2,128,1024]{2,1,0:T(8,128)(2,1)}, bf16[2,128,1024]{2,1,0:T(8,128)(2,1)S(1)}, u32[]{:S(2)}, u32[]{:S(2)}) collective-permute-start(bf16[2,128,1024]{2,1,0:T(8,128)(2,1)} %get-tuple-element.56), channel_id=1, source_target_pairs={{0,1},{1,0},{2,3},{3,2},{4,5},{5,4},{6,7},{7,6},{8,9},{9,8},{10,11... | collective-permute-start | bytes 1572872 | tf_op jit(solution)/shard_map/ppermute | solution.py:29
  119.5 65.0 %collective-permute-start.7 = (bf16[2,128,1024]{2,1,0:T(8,128)(2,1)}, bf16[2,128,1024]{2,1,0:T(8,128)(2,1)S(1)}, u32[]{:S(2)}, u32[]{:S(2)}) collective-permute-start(bf16[2,128,1024]{2,1,0:T(8,128)(2,1)} %get-tuple-element.57), channel_id=1, source_target_pairs={{0,2},{1,3},{2,0},{3,1},{4,6},{5,7},{6,4},{7,5},{8,10},{9,11},{10,... | collective-permute-start | bytes 1572872 | tf_op jit(solution)/shard_map/ppermute | solution.py:29
  127.7 126.2 %collective-permute-start.8 = (bf16[2,128,1024]{2,1,0:T(8,128)(2,1)}, bf16[2,128,1024]{2,1,0:T(8,128)(2,1)}, u32[]{:S(2)}, u32[]{:S(2)}) collective-permute-start(bf16[2,128,1024]{2,1,0:T(8,128)(2,1)} %get-tuple-element.58), channel_id=1, source_target_pairs={{0,3},{1,2},{2,1},{3,0},{4,7},{5,6},{6,5},{7,4},{8,11},{9,10},{10,... | collective-permute-start | bytes 1572872 | tf_op jit(solution)/shard_map/ppermute | solution.py:29
  175.3 117.7 %collective-permute-start.9 = (bf16[2,128,1024]{2,1,0:T(8,128)(2,1)}, bf16[2,128,1024]{2,1,0:T(8,128)(2,1)S(1)}, u32[]{:S(2)}, u32[]{:S(2)}) collective-permute-start(bf16[2,128,1024]{2,1,0:T(8,128)(2,1)} %get-tuple-element.64), channel_id=1, source_target_pairs={{0,16},{4,20},{8,24},{12,28},{16,0},{20,4},{24,8},{28,12},{1,17},{... | collective-permute-start | bytes 1572872 | tf_op jit(solution)/shard_map/ppermute | solution.py:309
  176.9 116.0 %collective-permute-start.10 = (bf16[2,128,1024]{2,1,0:T(8,128)(2,1)}, bf16[2,128,1024]{2,1,0:T(8,128)(2,1)S(1)}, u32[]{:S(2)}, u32[]{:S(2)}) collective-permute-start(bf16[2,128,1024]{2,1,0:T(8,128)(2,1)} %get-tuple-element.65), channel_id=1, source_target_pairs={{0,20},{4,24},{8,28},{12,16},{20,0},{24,4},{28,8},{16,12},{1,21},{... | collective-permute-start | bytes 1572872 | tf_op jit(solution)/shard_map/ppermute | solution.py:309
  181.6 0.8 copy-start.21
  182.4 110.6 %collective-permute-start.11 = (bf16[2,128,1024]{2,1,0:T(8,128)(2,1)}, bf16[2,128,1024]{2,1,0:T(8,128)(2,1)}, u32[]{:S(2)}, u32[]{:S(2)}) collective-permute-start(bf16[2,128,1024]{2,1,0:T(8,128)(2,1)} %get-tuple-element.66), channel_id=1, source_target_pairs={{0,24},{4,28},{8,16},{12,20},{24,0},{28,4},{16,8},{20,12},{1,25},{... | collective-permute-start | bytes 1572872 | tf_op jit(solution)/shard_map/ppermute | solution.py:309
  185.3 108.8 %collective-permute-start.12 = (bf16[2,128,1024]{2,1,0:T(8,128)(2,1)}, bf16[2,128,1024]{2,1,0:T(8,128)(2,1)}, u32[]{:S(2)}, u32[]{:S(2)}) collective-permute-start(bf16[2,128,1024]{2,1,0:T(8,128)(2,1)} %get-tuple-element.67), channel_id=1, source_target_pairs={{0,28},{4,16},{8,20},{12,24},{28,0},{16,4},{20,8},{24,12},{1,29},{... | collective-permute-start | bytes 1572872 | tf_op jit(solution)/shard_map/ppermute | solution.py:309
  249.0 45.2 %all-to-all-start.3 = ((bf16[4,2,128,1024]{3,2,1,0:T(8,128)(2,1)}), bf16[4,2,128,1024]{3,2,1,0:T(8,128)(2,1)S(1)}, u32[]{:S(2)}, u32[]{:S(2)}) async-start(bf16[4,2,128,1024]{3,2,1,0:T(8,128)(2,1)} %get-tuple-element.84), calls=%async_computation.3 | async-start | bytes 4194304 | tf_op jit(solution)/shard_map/all_to_all | solution.py:41
  253.9 1.0 copy-start.20
  254.9 1.0 copy-start.22
  256.0 1.0 copy-start.24
  292.9 1.2 copy-start.16
  293.0 1.2 copy-start.18
  294.2 124.7 %all-to-all-start.2 = ((bf16[4,2,128,1024]{3,2,1,0:T(8,128)(2,1)}), bf16[4,2,128,1024]{3,2,1,0:T(8,128)(2,1)}, u32[]{:S(2)}, u32[]{:S(2)}) async-start(bf16[4,2,128,1024]{3,2,1,0:T(8,128)(2,1)} %get-tuple-element.75), calls=%async_computation.2 | async-start | bytes 4194304 | tf_op jit(solution)/shard_map/all_to_all | solution.py:41
  298.6 13.8 %collective-permute-start.3 = (bf16[2,128,1024]{2,1,0:T(8,128)(2,1)}, bf16[2,128,1024]{2,1,0:T(8,128)(2,1)S(1)}, u32[]{:S(2)}, u32[]{:S(2)}) collective-permute-start(bf16[2,128,1024]{2,1,0:T(8,128)(2,1)} %get-tuple-element.50), channel_id=1, source_target_pairs={{0,1},{1,0},{2,3},{3,2},{4,5},{5,4},{6,7},{7,6},{8,9},{9,8},{10,11... | collective-permute-start | bytes 1572872 | tf_op jit(solution)/shard_map/ppermute | solution.py:29
  299.9 24.6 %collective-permute-start.4 = (bf16[2,128,1024]{2,1,0:T(8,128)(2,1)}, bf16[2,128,1024]{2,1,0:T(8,128)(2,1)S(1)}, u32[]{:S(2)}, u32[]{:S(2)}) collective-permute-start(bf16[2,128,1024]{2,1,0:T(8,128)(2,1)} %get-tuple-element.51), channel_id=1, source_target_pairs={{0,2},{1,3},{2,0},{3,1},{4,6},{5,7},{6,4},{7,5},{8,10},{9,11},{10,... | collective-permute-start | bytes 1572872 | tf_op jit(solution)/shard_map/ppermute | solution.py:29
  300.1 25.4 %collective-permute-start.5 = (bf16[2,128,1024]{2,1,0:T(8,128)(2,1)}, bf16[2,128,1024]{2,1,0:T(8,128)(2,1)S(1)}, u32[]{:S(2)}, u32[]{:S(2)}) collective-permute-start(bf16[2,128,1024]{2,1,0:T(8,128)(2,1)} %get-tuple-element.52), channel_id=1, source_target_pairs={{0,3},{1,2},{2,1},{3,0},{4,7},{5,6},{6,5},{7,4},{8,11},{9,10},{10,... | collective-permute-start | bytes 1572872 | tf_op jit(solution)/shard_map/ppermute | solution.py:29
  301.3 33.6 %collective-permute-start.13 = (bf16[2,128,1024]{2,1,0:T(8,128)(2,1)}, bf16[2,128,1024]{2,1,0:T(8,128)(2,1)S(1)}, u32[]{:S(2)}, u32[]{:S(2)}) collective-permute-start(bf16[2,128,1024]{2,1,0:T(8,128)(2,1)} %get-tuple-element.69), channel_id=1, source_target_pairs={{0,1},{1,0},{2,3},{3,2},{4,5},{5,4},{6,7},{7,6},{8,9},{9,8},{10,11... | collective-permute-start | bytes 1572872 | tf_op jit(solution)/shard_map/ppermute | solution.py:29
  302.5 44.5 %collective-permute-start.14 = (bf16[2,128,1024]{2,1,0:T(8,128)(2,1)}, bf16[2,128,1024]{2,1,0:T(8,128)(2,1)S(1)}, u32[]{:S(2)}, u32[]{:S(2)}) collective-permute-start(bf16[2,128,1024]{2,1,0:T(8,128)(2,1)} %get-tuple-element.70), channel_id=1, source_target_pairs={{0,2},{1,3},{2,0},{3,1},{4,6},{5,7},{6,4},{7,5},{8,10},{9,11},{10,... | collective-permute-start | bytes 1572872 | tf_op jit(solution)/shard_map/ppermute | solution.py:29
  313.2 35.8 %collective-permute-start.15 = (bf16[2,128,1024]{2,1,0:T(8,128)(2,1)}, bf16[2,128,1024]{2,1,0:T(8,128)(2,1)}, u32[]{:S(2)}, u32[]{:S(2)}) collective-permute-start(bf16[2,128,1024]{2,1,0:T(8,128)(2,1)} %get-tuple-element.71), channel_id=1, source_target_pairs={{0,3},{1,2},{2,1},{3,0},{4,7},{5,6},{6,5},{7,4},{8,11},{9,10},{10,... | collective-permute-start | bytes 1572872 | tf_op jit(solution)/shard_map/ppermute | solution.py:29
  325.3 59.9 %collective-permute-start.16 = (bf16[2,128,1024]{2,1,0:T(8,128)(2,1)}, bf16[2,128,1024]{2,1,0:T(8,128)(2,1)S(1)}, u32[]{:S(2)}, u32[]{:S(2)}) collective-permute-start(bf16[2,128,1024]{2,1,0:T(8,128)(2,1)} %get-tuple-element.77), channel_id=1, source_target_pairs={{0,16},{4,20},{8,24},{12,28},{16,0},{20,4},{24,8},{28,12},{1,17},{... | collective-permute-start | bytes 1572872 | tf_op jit(solution)/shard_map/ppermute | solution.py:309
  325.5 0.8 copy-start.10
  326.3 58.9 %collective-permute-start.17 = (bf16[2,128,1024]{2,1,0:T(8,128)(2,1)}, bf16[2,128,1024]{2,1,0:T(8,128)(2,1)S(1)}, u32[]{:S(2)}, u32[]{:S(2)}) collective-permute-start(bf16[2,128,1024]{2,1,0:T(8,128)(2,1)} %get-tuple-element.79), channel_id=1, source_target_pairs={{0,20},{4,24},{8,28},{12,16},{20,0},{24,4},{28,8},{16,12},{1,21},{... | collective-permute-start | bytes 1572872 | tf_op jit(solution)/shard_map/ppermute | solution.py:309
  335.7 49.5 %collective-permute-start.18 = (bf16[2,128,1024]{2,1,0:T(8,128)(2,1)}, bf16[2,128,1024]{2,1,0:T(8,128)(2,1)}, u32[]{:S(2)}, u32[]{:S(2)}) collective-permute-start(bf16[2,128,1024]{2,1,0:T(8,128)(2,1)} %get-tuple-element.81), channel_id=1, source_target_pairs={{0,24},{4,28},{8,16},{12,20},{24,0},{28,4},{16,8},{20,12},{1,25},{... | collective-permute-start | bytes 1572872 | tf_op jit(solution)/shard_map/ppermute | solution.py:309
  347.0 0.8 copy-start.14
  347.8 71.0 %collective-permute-start.19 = (bf16[2,128,1024]{2,1,0:T(8,128)(2,1)}, bf16[2,128,1024]{2,1,0:T(8,128)(2,1)}, u32[]{:S(2)}, u32[]{:S(2)}) collective-permute-start(bf16[2,128,1024]{2,1,0:T(8,128)(2,1)} %get-tuple-element.83), channel_id=1, source_target_pairs={{0,28},{4,16},{8,20},{12,24},{28,0},{16,4},{20,8},{24,12},{1,29},{... | collective-permute-start | bytes 1572872 | tf_op jit(solution)/shard_map/ppermute | solution.py:309
  349.0 1.0 copy-start.4
  350.0 1.0 copy-start.5
  351.1 1.0 copy-start.7
  352.1 1.0 copy-start.9
  353.2 1.0 copy-start.11
  354.2 1.0 copy-start.13
  355.2 1.0 copy-start.15
  356.3 3.3 copy-start.17
  356.3 3.3 copy-start.19
  (4 other events, 3.2 us)

commit v8 on v7

--- a/solution.py
+++ b/solution.py
@@ -45,7 +45,13 @@
 
 def swap_rows(pieces):
     count = len(pieces)
-    return [pieces[0]] + [exchange(pieces[step], "seq", step, count) for step in range(1, count)]
+    got = [pieces[0]]
+    for step in range(1, count):
+        piece = pieces[step]
+        if step > 1:
+            piece = after(piece, got[-1])
+        got.append(exchange(piece, "seq", step, count))
+    return got
 
 
 def swap_pool(array):
@@ -321,16 +327,22 @@
     for first in firsts:
         picked = pick(first, chunk, send_lists, kv_pool)
         send_lists, queries = after((send_lists, queries), picked)
+        if rows:
+            picked = after(picked, rows)
         arrived.append(swap_pool(picked))
-        rows.append(swap_rows(pack(first, chunk, queries, grad_context, width, parts)))
+        if not rows:
+            for start in firsts:
+                packed = pack(start, chunk, queries, grad_context, width, parts)
+                rows.append(swap_rows(packed))
     done, returns, token_parts = [], [], []
     for h in range(chunks):
         rows_out, near, far = attend(block_slots, rows[h], arrived[h])
         far = swap_far(far, done)
         if h > 0:
-            near, rows_out = after((near, rows_out), done[:DEPTH])
+            near = after(near, done[:DEPTH])
         returns.append((swap_near(near, seqs), far))
         token_parts.append(swap_rows(rows_out))
+        block_slots = after(block_slots, token_parts[-1])
     context, grad_queries = unpack(token_parts, firsts, width, queries.shape)
     pool_grads = None
     for h in range(chunks):

time: 425 us -> 416 us (0.979)
  the two profiles are of different devices: /device:TPU:5 before, /device:TPU:15 now
where the time goes in v8:
time: 416 us; the launch traced here: 409 us
  waiting for transfers between devices  253 us (61%)
  Pallas kernels  93.4 us (22%)
  starting transfers between devices  42.2 us (10%)
  local copies, waits for them, and re-layouts  19.9 us (5%)
    ppermute x12, waiting for transfers between devices, exchange(): return lax.ppermute(array, axis, pairs)  109 us
    all_to_all x2, waiting for transfers between devices, swap_pool(): return lax.all_to_all(array, 'enc', split_axis=0, concat_axis=0, tiled=True)  82.5 us
    pallas_call x2, Pallas kernels, attend(): pl.pallas_call(functools.partial(attend_kernel, seqs, parts), grid=(heads...  71.8 us
    ppermute x8, waiting for transfers between devices, swap_far(): got.append(lax.ppermute(piece, 'enc', pairs))  61.3 us
    unnamed x66, local copies, waits for them, and re-layouts  19.7 us
    all_to_all x2, starting transfers between devices, swap_pool(): return lax.all_to_all(array, 'enc', split_axis=0, concat_axis=0, tiled=True)  13.9 us
    all_to_all x2, starting transfers between devices, swap_near(): lax.all_to_all(array, 'enc', split_axis=0, concat_axis=0, axis_index_grou...  12.2 us
    ppermute x8, starting transfers between devices, swap_far(): got.append(lax.ppermute(piece, 'enc', pairs))  12.2 us
  transfers between devices with their start and end apart: 24, of which 17 were waited for; matrix products, arithmetic and copies ran while one was open for 0% of the time, Pallas kernels for 21%

profile of v8, /device:TPU:15, one launch (start us, length us, event | category | flops | bytes accessed | tf_op | source)
XLA Modules:
  0.0 409.0 jit_solution(12216355266814785050)
XLA Ops:
  1.4 2.2 copy-done
  3.5 3.1 pick_entries.2
  6.6 5.8 %all-to-all-start = ((bf16[8,2,128,1024]{3,2,1,0:T(8,128)(2,1)}), bf16[8,2,128,1024]{3,2,1,0:T(8,128)(2,1)}, u32[]{:S(2)}, u32[]{:S(2)}) async-start(bf16[8,2,128,1024]{3,2,1,0:T(8,128)(2,1)} %pick_entries.2), calls=%async_computation | async-start | bytes 8388608 | tf_op jit(solution)/shard_map/all_to_all | solution.py:58
  12.4 1.6 copy-done.3
  14.0 1.6 pack_rows.3
  16.0 1.5 pack_rows.2
  17.5 1.3 collective-permute-start
  18.8 10.3 %collective-permute-done.6.rest_1_ = bf16[2,128,1024]{2,1,0:T(8,128)(2,1)S(1)} collective-permute-done((bf16[2,128,1024]{2,1,0:T(8,128)(2,1)}, bf16[2,128,1024]{2,1,0:T(8,128)(2,1)S(1)}, u32[]{:S(2)}, u32[]{:S(2)}) %collective-permute-start.6) | collective-permute-done | bytes 524320 | tf_op jit(solution)/shard_map/ppermute | solution.py:29
  30.1 10.3 %collective-permute-done.rest_1_ = bf16[2,128,1024]{2,1,0:T(8,128)(2,1)S(1)} collective-permute-done((bf16[2,128,1024]{2,1,0:T(8,128)(2,1)}, bf16[2,128,1024]{2,1,0:T(8,128)(2,1)S(1)}, u32[]{:S(2)}, u32[]{:S(2)}) %collective-permute-start) | collective-permute-done | bytes 524320 | tf_op jit(solution)/shard_map/ppermute | solution.py:29
  41.4 0.8 copy-done.23
  42.7 22.6 %collective-permute-done.1.rest_2_ = bf16[2,128,1024]{2,1,0:T(8,128)(2,1)S(1)} collective-permute-done((bf16[2,128,1024]{2,1,0:T(8,128)(2,1)}, bf16[2,128,1024]{2,1,0:T(8,128)(2,1)S(1)}, u32[]{:S(2)}, u32[]{:S(2)}) %collective-permute-start.1) | collective-permute-done | bytes 524320 | tf_op jit(solution)/shard_map/ppermute | solution.py:29
  65.5 2.2 copy-done.1
  67.7 3.1 pick_entries.3
  70.9 7.6 %collective-permute-done.2.rest_3_ = bf16[2,128,1024]{2,1,0:T(8,128)(2,1)S(1)} collective-permute-done((bf16[2,128,1024]{2,1,0:T(8,128)(2,1)}, bf16[2,128,1024]{2,1,0:T(8,128)(2,1)S(1)}, u32[]{:S(2)}, u32[]{:S(2)}) %collective-permute-start.2) | collective-permute-done | bytes 524320 | tf_op jit(solution)/shard_map/ppermute | solution.py:29
  78.4 24.4 %all-to-all-done.rest_4_ = bf16[8,2,128,1024]{3,2,1,0:T(8,128)(2,1)} async-done(((bf16[8,2,128,1024]{3,2,1,0:T(8,128)(2,1)}), bf16[8,2,128,1024]{3,2,1,0:T(8,128)(2,1)}, u32[]{:S(2)}, u32[]{:S(2)}) %all-to-all-start) | async-done | bytes 4194336 | tf_op jit(solution)/shard_map/all_to_all | solution.py:58
  102.9 8.1 %all-to-all-start.1 = ((bf16[8,2,128,1024]{3,2,1,0:T(8,128)(2,1)}), bf16[8,2,128,1024]{3,2,1,0:T(8,128)(2,1)}, u32[]{:S(2)}, u32[]{:S(2)}) async-start(bf16[8,2,128,1024]{3,2,1,0:T(8,128)(2,1)} %pick_entries.3), calls=%async_computation.1 | async-start | bytes 8388608 | tf_op jit(solution)/shard_map/all_to_all | solution.py:58
  111.1 35.9 %attend_blocks.2 = (bf16[2,128,1024]{2,1,0:T(8,128)(2,1)}, bf16[2,128,1024]{2,1,0:T(8,128)(2,1)}, bf16[2,128,1024]{2,1,0:T(8,128)(2,1)}, bf16[2,128,1024]{2,1,0:...) custom-call(s32[1,8,2]{2,1,0:T(8,128)S(1)} %copy.10.uses, ...), custom_call_target="tpu_custom_call" | custom-call | flops 38654705664 | bytes 12582912 | tf_op jit(solution)/shard_map/attend_blocks/pallas_call | solution.py:245
  147.3 13.2 %collective-permute-done.3.refs_1_ = bf16[2,128,1024]{2,1,0:T(8,128)(2,1)S(1)} collective-permute-done((bf16[2,128,1024]{2,1,0:T(8,128)(2,1)}, bf16[2,128,1024]{2,1,0:T(8,128)(2,1)S(1)}, u32[]{:S(2)}, u32[]{:S(2)}) %collective-permute-start.3) | collective-permute-done | bytes 524320 | tf_op jit(solution)/shard_map/ppermute | solution.py:29
  161.5 12.5 %collective-permute-done.4.refs_2_ = bf16[2,128,1024]{2,1,0:T(8,128)(2,1)S(1)} collective-permute-done((bf16[2,128,1024]{2,1,0:T(8,128)(2,1)}, bf16[2,128,1024]{2,1,0:T(8,128)(2,1)S(1)}, u32[]{:S(2)}, u32[]{:S(2)}) %collective-permute-start.4) | collective-permute-done | bytes 524320 | tf_op jit(solution)/shard_map/ppermute | solution.py:29
  173.9 0.8 copy-done.7
  174.9 2.0 collective-permute-start.12
  177.0 1.8 collective-permute-start.13
  178.8 2.1 collective-permute-start.14
  180.9 1.2 collective-permute-start.15
  182.0 5.4 %collective-permute-done.5.refs_3_ = bf16[2,128,1024]{2,1,0:T(8,128)(2,1)S(1)} collective-permute-done((bf16[2,128,1024]{2,1,0:T(8,128)(2,1)}, bf16[2,128,1024]{2,1,0:T(8,128)(2,1)S(1)}, u32[]{:S(2)}, u32[]{:S(2)}) %collective-permute-start.5) | collective-permute-done | bytes 524320 | tf_op jit(solution)/shard_map/ppermute | solution.py:29
  187.4 0.8 copy-done.9
  188.3 58.1 %all-to-all-done.1.rest_4_ = bf16[8,2,128,1024]{3,2,1,0:T(8,128)(2,1)} async-done(((bf16[8,2,128,1024]{3,2,1,0:T(8,128)(2,1)}), bf16[8,2,128,1024]{3,2,1,0:T(8,128)(2,1)}, u32[]{:S(2)}, u32[]{:S(2)}) %all-to-all-start.1) | async-done | bytes 4194336 | tf_op jit(solution)/shard_map/all_to_all | solution.py:58
  246.4 7.7 %all-to-all-start.3 = ((bf16[4,2,128,1024]{3,2,1,0:T(8,128)(2,1)}), bf16[4,2,128,1024]{3,2,1,0:T(8,128)(2,1)S(1)}, u32[]{:S(2)}, u32[]{:S(2)}) async-start(bf16[4,2,128,1024]{3,2,1,0:T(8,128)(2,1)} %get-tuple-element.94), calls=%async_computation.3 | async-start | bytes 4194304 | tf_op jit(solution)/shard_map/all_to_all | solution.py:41
  254.1 1.0 copy-done.20
  255.2 1.0 copy-done.22
  256.2 1.0 copy-done.24
  257.3 1.0 copy-done.26
  258.3 35.9 %attend_blocks.3 = (bf16[2,128,1024]{2,1,0:T(8,128)(2,1)}, bf16[2,128,1024]{2,1,0:T(8,128)(2,1)}, bf16[2,128,1024]{2,1,0:T(8,128)(2,1)}, bf16[2,128,1024]{2,1,0:...) custom-call(s32[1,8,2]{2,1,0:T(8,128)S(1)} %copy.12.uses, ...), custom_call_target="tpu_custom_call" | custom-call | flops 38654705664 | bytes 12582912 | tf_op jit(solution)/shard_map/attend_blocks/pallas_call | solution.py:245
  295.2 4.5 %all-to-all-start.2 = ((bf16[4,2,128,1024]{3,2,1,0:T(8,128)(2,1)}), bf16[4,2,128,1024]{3,2,1,0:T(8,128)(2,1)}, u32[]{:S(2)}, u32[]{:S(2)}) async-start(bf16[4,2,128,1024]{3,2,1,0:T(8,128)(2,1)} %get-tuple-element.85), calls=%async_computation.2 | async-start | bytes 4194304 | tf_op jit(solution)/shard_map/all_to_all | solution.py:41
  299.9 13.3 %collective-permute-done.9.refs_5_ = bf16[2,128,1024]{2,1,0:T(8,128)(2,1)S(1)} collective-permute-done((bf16[2,128,1024]{2,1,0:T(8,128)(2,1)}, bf16[2,128,1024]{2,1,0:T(8,128)(2,1)S(1)}, u32[]{:S(2)}, u32[]{:S(2)}) %collective-permute-start.9) | collective-permute-done | bytes 524320 | tf_op jit(solution)/shard_map/ppermute | solution.py:29
  314.7 11.8 %collective-permute-done.10.refs_6_ = bf16[2,128,1024]{2,1,0:T(8,128)(2,1)S(1)} collective-permute-done((bf16[2,128,1024]{2,1,0:T(8,128)(2,1)}, bf16[2,128,1024]{2,1,0:T(8,128)(2,1)S(1)}, u32[]{:S(2)}, u32[]{:S(2)}) %collective-permute-start.10) | collective-permute-done | bytes 524320 | tf_op jit(solution)/shard_map/ppermute | solution.py:29
  326.5 0.8 copy-done.14
  327.5 3.9 collective-permute-start.17
  332.1 1.0 copy-done.17
  333.2 1.0 copy-done.19
  334.2 4.6 %owner_sum.2.rest_4_ = bf16[4,2,128,2048]{3,2,1,0:T(8,128)(2,1)} custom-call(s32[1,8,1]{2,1,0:T(8,128)S(1)} %copy.14.lists, bf16[4,2,128,1024]{3,2,1,0:T(8,128)(2,1)S(1)} %all-to-all-done.3.near_ref, bf16[2,128,1024]{2,1,0:T(8,128)(2,1)S(1)} %copy-done.17, bf16[2,128,1024]{2,1,0:T(8,128)(2,1)S(1)} %copy-done.19, ...), custom_call_target="tpu_custom_call" | custom-call | flops 2097152 | bytes 6291456 | tf_op jit(solution)/shard_map/owner_sum/pallas_call | solution.py:289
  338.8 1.2 collective-permute-done.11.refs_7_
  340.0 3.2 unpack_rows.1
  343.2 27.6 %collective-permute-done.19.rest_3_ = bf16[2,128,1024]{2,1,0:T(8,128)(2,1)S(1)} collective-permute-done((bf16[2,128,1024]{2,1,0:T(8,128)(2,1)}, bf16[2,128,1024]{2,1,0:T(8,128)(2,1)S(1)}, u32[]{:S(2)}, u32[]{:S(2)}) %collective-permute-start.19) | collective-permute-done | bytes 524320 | tf_op jit(solution)/shard_map/ppermute | solution.py:315
  370.8 14.6 %collective-permute-done.18.rest_2_ = bf16[2,128,1024]{2,1,0:T(8,128)(2,1)S(1)} collective-permute-done((bf16[2,128,1024]{2,1,0:T(8,128)(2,1)}, bf16[2,128,1024]{2,1,0:T(8,128)(2,1)S(1)}, u32[]{:S(2)}, u32[]{:S(2)}) %collective-permute-start.18) | collective-permute-done | bytes 524320 | tf_op jit(solution)/shard_map/ppermute | solution.py:315
  385.4 10.2 %collective-permute-done.17.rest_1_ = bf16[2,128,1024]{2,1,0:T(8,128)(2,1)} collective-permute-done((bf16[2,128,1024]{2,1,0:T(8,128)(2,1)}, bf16[2,128,1024]{2,1,0:T(8,128)(2,1)}, u32[]{:S(2)}, u32[]{:S(2)}) %collective-permute-start.17) | collective-permute-done | bytes 524320 | tf_op jit(solution)/shard_map/ppermute | solution.py:315
  395.6 8.9 %collective-permute-done.16.rest_0_ = bf16[2,128,1024]{2,1,0:T(8,128)(2,1)} collective-permute-done((bf16[2,128,1024]{2,1,0:T(8,128)(2,1)}, bf16[2,128,1024]{2,1,0:T(8,128)(2,1)}, u32[]{:S(2)}, u32[]{:S(2)}) %collective-permute-start.16) | collective-permute-done | bytes 524320 | tf_op jit(solution)/shard_map/ppermute | solution.py:315
  404.5 4.5 %owner_sum.3 = bf16[4,2,128,2048]{3,2,1,0:T(8,128)(2,1)} custom-call(s32[1,8,1]{2,1,0:T(8,128)S(1)} %copy.14.lists, bf16[4,2,128,1024]{3,2,1,0:T(8,128)(2,1)} %all-to-all-done.2.near_ref, bf16[2,128,1024]{2,1,0:T(8,128)(2,1)} %collective-permute-done.16.rest_0_, ...), custom_call_target="tpu_custom_call", output_to_operand_aliasing={{}: (6, {})} | custom-call | flops 2097152 | bytes 6291456 | tf_op jit(solution)/shard_map/owner_sum/pallas_call | solution.py:289
  (78 shorter events, 9.0 us)
Async XLA Ops:
  1.4 2.2 copy-start
  6.6 5.8 %copy-start.2 = (bf16[1,128,8192]{2,1,0:T(8,128)(2,1)S(1)}, bf16[1,128,8192]{2,1,0:T(8,128)(2,1)}, u32[]{:S(2)}) copy-start(bf16[1,128,8192]{2,1,0:T(8,128)(2,1)} %q_ref.1) | copy-start | bytes 6291460
  6.6 96.2 %all-to-all-start = ((bf16[8,2,128,1024]{3,2,1,0:T(8,128)(2,1)}), bf16[8,2,128,1024]{3,2,1,0:T(8,128)(2,1)}, u32[]{:S(2)}, u32[]{:S(2)}) async-start(bf16[8,2,128,1024]{3,2,1,0:T(8,128)(2,1)} %pick_entries.2), calls=%async_computation | async-start | bytes 8388608 | tf_op jit(solution)/shard_map/all_to_all | solution.py:58
  12.4 1.6 copy-start.3
  15.6 14.2 %copy-start.31 = (bf16[2,128,1024]{2,1,0:T(8,128)(2,1)S(1)}, bf16[2,128,1024]{2,1,0:T(8,128)(2,1)}, u32[]{:S(2)}) copy-start(bf16[2,128,1024]{2,1,0:T(8,128)(2,1)} %get-tuple-element.66) | copy-start | bytes 1572868
  15.6 26.6 %copy-start.30 = (bf16[2,128,1024]{2,1,0:T(8,128)(2,1)S(1)}, bf16[2,128,1024]{2,1,0:T(8,128)(2,1)}, u32[]{:S(2)}) copy-start(bf16[2,128,1024]{2,1,0:T(8,128)(2,1)} %get-tuple-element.68) | copy-start | bytes 1572868
  15.6 49.8 %copy-start.28 = (s32[1,8,1]{1,2,0:T(1,128)S(1)}, s32[1,8,1]{1,2,0:T(1,128)}, u32[]{:S(2)}) copy-start(s32[1,8,1]{1,2,0:T(1,128)} %param.7) | copy-start | bytes 100
  15.6 13.4 %collective-permute-start.6 = (bf16[2,128,1024]{2,1,0:T(8,128)(2,1)}, bf16[2,128,1024]{2,1,0:T(8,128)(2,1)S(1)}, u32[]{:S(2)}, u32[]{:S(2)}) collective-permute-start(bf16[2,128,1024]{2,1,0:T(8,128)(2,1)} %get-tuple-element.64), channel_id=1, source_target_pairs={{0,1},{1,0},{2,3},{3,2},{4,5},{5,4},{6,7},{7,6},{8,9},{9,8},{10,11... | collective-permute-start | bytes 1572872 | tf_op jit(solution)/shard_map/ppermute | solution.py:29
  17.5 22.9 %collective-permute-start = (bf16[2,128,1024]{2,1,0:T(8,128)(2,1)}, bf16[2,128,1024]{2,1,0:T(8,128)(2,1)S(1)}, u32[]{:S(2)}, u32[]{:S(2)}) collective-permute-start(bf16[2,128,1024]{2,1,0:T(8,128)(2,1)} %get-tuple-element.51), channel_id=1, source_target_pairs={{0,1},{1,0},{2,3},{3,2},{4,5},{5,4},{6,7},{7,6},{8,9},{9,8},{10,11... | collective-permute-start | bytes 1572872 | tf_op jit(solution)/shard_map/ppermute | solution.py:29
  29.8 11.5 %collective-permute-start.7 = (bf16[2,128,1024]{2,1,0:T(8,128)(2,1)S(1)}, bf16[2,128,1024]{2,1,0:T(8,128)(2,1)S(1)}, u32[]{:S(2)}, u32[]{:S(2)}) collective-permute-start(bf16[2,128,1024]{2,1,0:T(8,128)(2,1)S(1)} %copy-done.31), channel_id=1, source_target_pairs={{0,2},{1,3},{2,0},{3,1},{4,6},{5,7},{6,4},{7,5},{8,10},{9,11},{10,... | collective-permute-start | bytes 1572872 | tf_op jit(solution)/shard_map/ppermute | solution.py:29
  40.4 24.8 %collective-permute-start.1 = (bf16[2,128,1024]{2,1,0:T(8,128)(2,1)}, bf16[2,128,1024]{2,1,0:T(8,128)(2,1)S(1)}, u32[]{:S(2)}, u32[]{:S(2)}) collective-permute-start(bf16[2,128,1024]{2,1,0:T(8,128)(2,1)} %get-tuple-element.53), channel_id=1, source_target_pairs={{0,2},{1,3},{2,0},{3,1},{4,6},{5,7},{6,4},{7,5},{8,10},{9,11},{10,... | collective-permute-start | bytes 1572872 | tf_op jit(solution)/shard_map/ppermute | solution.py:29
  42.2 28.6 %collective-permute-start.8 = (bf16[2,128,1024]{2,1,0:T(8,128)(2,1)S(1)}, bf16[2,128,1024]{2,1,0:T(8,128)(2,1)S(1)}, u32[]{:S(2)}, u32[]{:S(2)}) collective-permute-start(bf16[2,128,1024]{2,1,0:T(8,128)(2,1)S(1)} %copy-done.30), channel_id=1, source_target_pairs={{0,3},{1,2},{2,1},{3,0},{4,7},{5,6},{6,5},{7,4},{8,11},{9,10},{10,... | collective-permute-start | bytes 1572872 | tf_op jit(solution)/shard_map/ppermute | solution.py:29
  65.2 13.2 %collective-permute-start.2 = (bf16[2,128,1024]{2,1,0:T(8,128)(2,1)}, bf16[2,128,1024]{2,1,0:T(8,128)(2,1)S(1)}, u32[]{:S(2)}, u32[]{:S(2)}) collective-permute-start(bf16[2,128,1024]{2,1,0:T(8,128)(2,1)} %get-tuple-element.55), channel_id=1, source_target_pairs={{0,3},{1,2},{2,1},{3,0},{4,7},{5,6},{6,5},{7,4},{8,11},{9,10},{10,... | collective-permute-start | bytes 1572872 | tf_op jit(solution)/shard_map/ppermute | solution.py:29
  65.5 2.2 copy-start.1
  70.8 32.0 %copy-start.25 = (bf16[2,128,1024]{2,1,0:T(8,128)(2,1)}, bf16[2,128,1024]{2,1,0:T(8,128)(2,1)S(1)}, u32[]{:S(2)}) copy-start(bf16[2,128,1024]{2,1,0:T(8,128)(2,1)S(1)} %collective-permute-done.8.rest_3_) | copy-start | bytes 1572868
  78.4 32.6 %copy-start.29 = (s32[1,8,2]{1,2,0:T(2,128)S(1)}, s32[1,8,2]{1,2,0:T(2,128)}, u32[]{:S(2)}) copy-start(s32[1,8,2]{1,2,0:T(2,128)} %param.8) | copy-start | bytes 196
  78.4 32.7 %copy-start.27 = (bf16[2,128,1024]{2,1,0:T(8,128)(2,1)S(1)}, bf16[2,128,1024]{2,1,0:T(8,128)(2,1)}, u32[]{:S(2)}) copy-start(bf16[2,128,1024]{2,1,0:T(8,128)(2,1)} %get-tuple-element.50.rest_0_) | copy-start | bytes 1572868
  102.9 143.5 %all-to-all-start.1 = ((bf16[8,2,128,1024]{3,2,1,0:T(8,128)(2,1)}), bf16[8,2,128,1024]{3,2,1,0:T(8,128)(2,1)}, u32[]{:S(2)}, u32[]{:S(2)}) async-start(bf16[8,2,128,1024]{3,2,1,0:T(8,128)(2,1)} %pick_entries.3), calls=%async_computation.1 | async-start | bytes 8388608 | tf_op jit(solution)/shard_map/all_to_all | solution.py:58
  147.0 13.5 %collective-permute-start.3 = (bf16[2,128,1024]{2,1,0:T(8,128)(2,1)}, bf16[2,128,1024]{2,1,0:T(8,128)(2,1)S(1)}, u32[]{:S(2)}, u32[]{:S(2)}) collective-permute-start(bf16[2,128,1024]{2,1,0:T(8,128)(2,1)} %get-tuple-element.57), channel_id=1, source_target_pairs={{0,1},{1,0},{2,3},{3,2},{4,5},{5,4},{6,7},{7,6},{8,9},{9,8},{10,11... | collective-permute-start | bytes 1572872 | tf_op jit(solution)/shard_map/ppermute | solution.py:29
  161.3 12.6 %collective-permute-start.4 = (bf16[2,128,1024]{2,1,0:T(8,128)(2,1)}, bf16[2,128,1024]{2,1,0:T(8,128)(2,1)S(1)}, u32[]{:S(2)}, u32[]{:S(2)}) collective-permute-start(bf16[2,128,1024]{2,1,0:T(8,128)(2,1)} %get-tuple-element.59), channel_id=1, source_target_pairs={{0,2},{1,3},{2,0},{3,1},{4,6},{5,7},{6,4},{7,5},{8,10},{9,11},{10,... | collective-permute-start | bytes 1572872 | tf_op jit(solution)/shard_map/ppermute | solution.py:29
  174.8 12.6 %collective-permute-start.5 = (bf16[2,128,1024]{2,1,0:T(8,128)(2,1)}, bf16[2,128,1024]{2,1,0:T(8,128)(2,1)S(1)}, u32[]{:S(2)}, u32[]{:S(2)}) collective-permute-start(bf16[2,128,1024]{2,1,0:T(8,128)(2,1)} %get-tuple-element.61), channel_id=1, source_target_pairs={{0,3},{1,2},{2,1},{3,0},{4,7},{5,6},{6,5},{7,4},{8,11},{9,10},{10,... | collective-permute-start | bytes 1572872 | tf_op jit(solution)/shard_map/ppermute | solution.py:29
  174.9 119.3 %collective-permute-start.12 = (bf16[2,128,1024]{2,1,0:T(8,128)(2,1)}, bf16[2,128,1024]{2,1,0:T(8,128)(2,1)S(1)}, u32[]{:S(2)}, u32[]{:S(2)}) collective-permute-start(bf16[2,128,1024]{2,1,0:T(8,128)(2,1)} %get-tuple-element.81), channel_id=1, source_target_pairs={{0,16},{4,20},{8,24},{12,28},{16,0},{20,4},{24,8},{28,12},{1,17},{... | collective-permute-start | bytes 1572872 | tf_op jit(solution)/shard_map/ppermute | solution.py:315
  177.0 117.3 %collective-permute-start.13 = (bf16[2,128,1024]{2,1,0:T(8,128)(2,1)}, bf16[2,128,1024]{2,1,0:T(8,128)(2,1)S(1)}, u32[]{:S(2)}, u32[]{:S(2)}) collective-permute-start(bf16[2,128,1024]{2,1,0:T(8,128)(2,1)} %get-tuple-element.82), channel_id=1, source_target_pairs={{0,20},{4,24},{8,28},{12,16},{20,0},{24,4},{28,8},{16,12},{1,21},{... | collective-permute-start | bytes 1572872 | tf_op jit(solution)/shard_map/ppermute | solution.py:315
  178.8 115.5 %collective-permute-start.14 = (bf16[2,128,1024]{2,1,0:T(8,128)(2,1)}, bf16[2,128,1024]{2,1,0:T(8,128)(2,1)}, u32[]{:S(2)}, u32[]{:S(2)}) collective-permute-start(bf16[2,128,1024]{2,1,0:T(8,128)(2,1)} %get-tuple-element.83), channel_id=1, source_target_pairs={{0,24},{4,28},{8,16},{12,20},{24,0},{28,4},{16,8},{20,12},{1,25},{... | collective-permute-start | bytes 1572872 | tf_op jit(solution)/shard_map/ppermute | solution.py:315
  180.9 113.4 %collective-permute-start.15 = (bf16[2,128,1024]{2,1,0:T(8,128)(2,1)}, bf16[2,128,1024]{2,1,0:T(8,128)(2,1)}, u32[]{:S(2)}, u32[]{:S(2)}) collective-permute-start(bf16[2,128,1024]{2,1,0:T(8,128)(2,1)} %get-tuple-element.84), channel_id=1, source_target_pairs={{0,28},{4,16},{8,20},{12,24},{28,0},{16,4},{20,8},{24,12},{1,29},{... | collective-permute-start | bytes 1572872 | tf_op jit(solution)/shard_map/ppermute | solution.py:315
  246.4 47.9 %all-to-all-start.3 = ((bf16[4,2,128,1024]{3,2,1,0:T(8,128)(2,1)}), bf16[4,2,128,1024]{3,2,1,0:T(8,128)(2,1)S(1)}, u32[]{:S(2)}, u32[]{:S(2)}) async-start(bf16[4,2,128,1024]{3,2,1,0:T(8,128)(2,1)} %get-tuple-element.94), calls=%async_computation.3 | async-start | bytes 4194304 | tf_op jit(solution)/shard_map/all_to_all | solution.py:41
  254.1 1.0 copy-start.20
  255.2 1.0 copy-start.22
  256.2 1.0 copy-start.24
  257.2 1.0 copy-start.26
  294.2 1.0 copy-start.18
  295.2 109.3 %all-to-all-start.2 = ((bf16[4,2,128,1024]{3,2,1,0:T(8,128)(2,1)}), bf16[4,2,128,1024]{3,2,1,0:T(8,128)(2,1)}, u32[]{:S(2)}, u32[]{:S(2)}) async-start(bf16[4,2,128,1024]{3,2,1,0:T(8,128)(2,1)} %get-tuple-element.85), calls=%async_computation.2 | async-start | bytes 4194304 | tf_op jit(solution)/shard_map/all_to_all | solution.py:41
  299.6 13.5 %collective-permute-start.9 = (bf16[2,128,1024]{2,1,0:T(8,128)(2,1)}, bf16[2,128,1024]{2,1,0:T(8,128)(2,1)S(1)}, u32[]{:S(2)}, u32[]{:S(2)}) collective-permute-start(bf16[2,128,1024]{2,1,0:T(8,128)(2,1)} %get-tuple-element.72), channel_id=1, source_target_pairs={{0,1},{1,0},{2,3},{3,2},{4,5},{5,4},{6,7},{7,6},{8,9},{9,8},{10,11... | collective-permute-start | bytes 1572872 | tf_op jit(solution)/shard_map/ppermute | solution.py:29
  314.0 12.6 %collective-permute-start.10 = (bf16[2,128,1024]{2,1,0:T(8,128)(2,1)}, bf16[2,128,1024]{2,1,0:T(8,128)(2,1)S(1)}, u32[]{:S(2)}, u32[]{:S(2)}) collective-permute-start(bf16[2,128,1024]{2,1,0:T(8,128)(2,1)} %get-tuple-element.74), channel_id=1, source_target_pairs={{0,2},{1,3},{2,0},{3,1},{4,6},{5,7},{6,4},{7,5},{8,10},{9,11},{10,... | collective-permute-start | bytes 1572872 | tf_op jit(solution)/shard_map/ppermute | solution.py:29
  314.2 56.6 %collective-permute-start.19 = (bf16[2,128,1024]{2,1,0:T(8,128)(2,1)}, bf16[2,128,1024]{2,1,0:T(8,128)(2,1)S(1)}, u32[]{:S(2)}, u32[]{:S(2)}) collective-permute-start(bf16[2,128,1024]{2,1,0:T(8,128)(2,1)} %get-tuple-element.93), channel_id=1, source_target_pairs={{0,28},{4,16},{8,20},{12,24},{28,0},{16,4},{20,8},{24,12},{1,29},{... | collective-permute-start | bytes 1572872 | tf_op jit(solution)/shard_map/ppermute | solution.py:315
  327.3 12.6 %collective-permute-start.11 = (bf16[2,128,1024]{2,1,0:T(8,128)(2,1)}, bf16[2,128,1024]{2,1,0:T(8,128)(2,1)}, u32[]{:S(2)}, u32[]{:S(2)}) collective-permute-start(bf16[2,128,1024]{2,1,0:T(8,128)(2,1)} %get-tuple-element.76), channel_id=1, source_target_pairs={{0,3},{1,2},{2,1},{3,0},{4,7},{5,6},{6,5},{7,4},{8,11},{9,10},{10,... | collective-permute-start | bytes 1572872 | tf_op jit(solution)/shard_map/ppermute | solution.py:29
  327.5 57.9 %collective-permute-start.18 = (bf16[2,128,1024]{2,1,0:T(8,128)(2,1)}, bf16[2,128,1024]{2,1,0:T(8,128)(2,1)S(1)}, u32[]{:S(2)}, u32[]{:S(2)}) collective-permute-start(bf16[2,128,1024]{2,1,0:T(8,128)(2,1)} %get-tuple-element.91), channel_id=1, source_target_pairs={{0,24},{4,28},{8,16},{12,20},{24,0},{28,4},{16,8},{20,12},{1,25},{... | collective-permute-start | bytes 1572872 | tf_op jit(solution)/shard_map/ppermute | solution.py:315
  327.5 68.0 %collective-permute-start.17 = (bf16[2,128,1024]{2,1,0:T(8,128)(2,1)}, bf16[2,128,1024]{2,1,0:T(8,128)(2,1)}, u32[]{:S(2)}, u32[]{:S(2)}) collective-permute-start(bf16[2,128,1024]{2,1,0:T(8,128)(2,1)} %get-tuple-element.89), channel_id=1, source_target_pairs={{0,20},{4,24},{8,28},{12,16},{20,0},{24,4},{28,8},{16,12},{1,21},{... | collective-permute-start | bytes 1572872 | tf_op jit(solution)/shard_map/ppermute | solution.py:315
  331.4 73.1 %collective-permute-start.16 = (bf16[2,128,1024]{2,1,0:T(8,128)(2,1)}, bf16[2,128,1024]{2,1,0:T(8,128)(2,1)}, u32[]{:S(2)}, u32[]{:S(2)}) collective-permute-start(bf16[2,128,1024]{2,1,0:T(8,128)(2,1)} %get-tuple-element.87), channel_id=1, source_target_pairs={{0,16},{4,20},{8,24},{12,28},{16,0},{20,4},{24,8},{28,12},{1,17},{... | collective-permute-start | bytes 1572872 | tf_op jit(solution)/shard_map/ppermute | solution.py:315
  332.1 1.0 copy-start.17
  333.2 1.0 copy-start.19
  334.2 5.8 %copy-start.4 = (bf16[2,128,1024]{2,1,0:T(8,128)(2,1)S(1)}, bf16[2,128,1024]{2,1,0:T(8,128)(2,1)}, u32[]{:S(2)}) copy-start(bf16[2,128,1024]{2,1,0:T(8,128)(2,1)} %get-tuple-element.56.refs_0_) | copy-start | bytes 1572868
  334.2 5.8 %copy-start.6 = (bf16[2,128,1024]{2,1,0:T(8,128)(2,1)S(1)}, bf16[2,128,1024]{2,1,0:T(8,128)(2,1)}, u32[]{:S(2)}) copy-start(bf16[2,128,1024]{2,1,0:T(8,128)(2,1)} %copy-done.5) | copy-start | bytes 1572868
  334.2 5.8 %copy-start.8 = (bf16[2,128,1024]{2,1,0:T(8,128)(2,1)S(1)}, bf16[2,128,1024]{2,1,0:T(8,128)(2,1)}, u32[]{:S(2)}) copy-start(bf16[2,128,1024]{2,1,0:T(8,128)(2,1)} %copy-done.7) | copy-start | bytes 1572868
  334.2 5.8 %copy-start.10 = (bf16[2,128,1024]{2,1,0:T(8,128)(2,1)S(1)}, bf16[2,128,1024]{2,1,0:T(8,128)(2,1)}, u32[]{:S(2)}) copy-start(bf16[2,128,1024]{2,1,0:T(8,128)(2,1)} %copy-done.9) | copy-start | bytes 1572868
  334.2 5.8 %copy-start.11 = (bf16[2,128,1024]{2,1,0:T(8,128)(2,1)S(1)}, bf16[2,128,1024]{2,1,0:T(8,128)(2,1)}, u32[]{:S(2)}) copy-start(bf16[2,128,1024]{2,1,0:T(8,128)(2,1)} %get-tuple-element.71.refs_4_) | copy-start | bytes 1572868
  334.2 5.8 %copy-start.13 = (bf16[2,128,1024]{2,1,0:T(8,128)(2,1)S(1)}, bf16[2,128,1024]{2,1,0:T(8,128)(2,1)}, u32[]{:S(2)}) copy-start(bf16[2,128,1024]{2,1,0:T(8,128)(2,1)} %copy-done.12) | copy-start | bytes 1572868
  334.2 5.8 %copy-start.15 = (bf16[2,128,1024]{2,1,0:T(8,128)(2,1)S(1)}, bf16[2,128,1024]{2,1,0:T(8,128)(2,1)}, u32[]{:S(2)}) copy-start(bf16[2,128,1024]{2,1,0:T(8,128)(2,1)} %copy-done.14) | copy-start | bytes 1572868
  (8 other events, 6.5 us)

commit v9 on v7

--- a/solution.py
+++ b/solution.py
@@ -11,7 +11,7 @@
 BLOCK = 64
 NBLEN = 128
 CHUNKS = 2
-DEPTH = 4
+DEPTH = 2
 ATTEND_WEIGHT = 24
 F32 = jnp.float32
 BF16 = jnp.bfloat16
@@ -321,16 +321,20 @@
     for first in firsts:
         picked = pick(first, chunk, send_lists, kv_pool)
         send_lists, queries = after((send_lists, queries), picked)
+        if rows:
+            picked = after(picked, rows)
         arrived.append(swap_pool(picked))
-        rows.append(swap_rows(pack(first, chunk, queries, grad_context, width, parts)))
+        if not rows:
+            for start in firsts:
+                packed = pack(start, chunk, queries, grad_context, width, parts)
+                rows.append(swap_rows(packed))
     done, returns, token_parts = [], [], []
     for h in range(chunks):
         rows_out, near, far = attend(block_slots, rows[h], arrived[h])
         far = swap_far(far, done)
-        if h > 0:
-            near, rows_out = after((near, rows_out), done[:DEPTH])
         returns.append((swap_near(near, seqs), far))
         token_parts.append(swap_rows(rows_out))
+        block_slots = after(block_slots, (token_parts[-1], far[:DEPTH]))
     context, grad_queries = unpack(token_parts, firsts, width, queries.shape)
     pool_grads = None
     for h in range(chunks):

time: 425 us -> 439 us (1.033)
  the two profiles are of different devices: /device:TPU:5 before, /device:TPU:15 now
where the time goes in v9:
time: 439 us; the launch traced here: 438 us
  waiting for transfers between devices  286 us (65%)
  Pallas kernels  92.7 us (21%)
  starting transfers between devices  38 us (9%)
  local copies, waits for them, and re-layouts  20.9 us (5%)
    ppermute x8, waiting for transfers between devices, swap_far(): got.append(lax.ppermute(piece, 'enc', pairs))  192 us
    pallas_call x2, Pallas kernels, attend(): pl.pallas_call(functools.partial(attend_kernel, seqs, parts), grid=(heads...  71.8 us
    ppermute x12, waiting for transfers between devices, exchange(): return lax.ppermute(array, axis, pairs)  54.7 us
    all_to_all x2, waiting for transfers between devices, swap_pool(): return lax.all_to_all(array, 'enc', split_axis=0, concat_axis=0, tiled=True)  39.3 us
    unnamed x60, local copies, waits for them, and re-layouts  20.7 us
    all_to_all x2, starting transfers between devices, swap_pool(): return lax.all_to_all(array, 'enc', split_axis=0, concat_axis=0, tiled=True)  13.9 us
    all_to_all x2, starting transfers between devices, swap_near(): lax.all_to_all(array, 'enc', split_axis=0, concat_axis=0, axis_index_grou...  9.64 us
    ppermute x12, starting transfers between devices, exchange(): return lax.ppermute(array, axis, pairs)  8.81 us
  transfers between devices with their start and end apart: 24, of which 15 were waited for; matrix products, arithmetic and copies ran while one was open for 0% of the time, Pallas kernels for 19%

profile of v9, /device:TPU:15, one launch (start us, length us, event | category | flops | bytes accessed | tf_op | source)
XLA Modules:
  0.0 438.2 jit_solution(12137931787890887246)
XLA Ops:
  1.4 2.2 copy-done
  3.5 3.1 pick_entries.2
  6.6 5.8 %all-to-all-start = ((bf16[8,2,128,1024]{3,2,1,0:T(8,128)(2,1)}), bf16[8,2,128,1024]{3,2,1,0:T(8,128)(2,1)}, u32[]{:S(2)}, u32[]{:S(2)}) async-start(bf16[8,2,128,1024]{3,2,1,0:T(8,128)(2,1)} %pick_entries.2), calls=%async_computation | async-start | bytes 8388608 | tf_op jit(solution)/shard_map/all_to_all | solution.py:52
  12.4 1.6 copy-done.3
  14.0 1.6 pack_rows.3
  16.2 2.2 collective-permute-start.10
  18.3 1.6 pack_rows.2
  20.4 8.6 %collective-permute-done.8.rest_1_ = bf16[2,128,1024]{2,1,0:T(8,128)(2,1)S(1)} collective-permute-done((bf16[2,128,1024]{2,1,0:T(8,128)(2,1)}, bf16[2,128,1024]{2,1,0:T(8,128)(2,1)S(1)}, u32[]{:S(2)}, u32[]{:S(2)}) %collective-permute-start.8) | collective-permute-done | bytes 524320 | tf_op jit(solution)/shard_map/ppermute | solution.py:29
  29.3 2.2 copy-done.1
  31.5 3.1 pick_entries.3
  34.7 5.7 %collective-permute-done.10.rest_3_ = bf16[2,128,1024]{2,1,0:T(8,128)(2,1)} collective-permute-done((bf16[2,128,1024]{2,1,0:T(8,128)(2,1)}, bf16[2,128,1024]{2,1,0:T(8,128)(2,1)}, u32[]{:S(2)}, u32[]{:S(2)}) %collective-permute-start.10) | collective-permute-done | bytes 524320 | tf_op jit(solution)/shard_map/ppermute | solution.py:29
  40.4 11.3 %collective-permute-done.rest_1_ = bf16[2,128,1024]{2,1,0:T(8,128)(2,1)S(1)} collective-permute-done((bf16[2,128,1024]{2,1,0:T(8,128)(2,1)}, bf16[2,128,1024]{2,1,0:T(8,128)(2,1)S(1)}, u32[]{:S(2)}, u32[]{:S(2)}) %collective-permute-start) | collective-permute-done | bytes 524320 | tf_op jit(solution)/shard_map/ppermute | solution.py:29
  51.7 11.1 %collective-permute-done.2.rest_3_ = bf16[2,128,1024]{2,1,0:T(8,128)(2,1)S(1)} collective-permute-done((bf16[2,128,1024]{2,1,0:T(8,128)(2,1)}, bf16[2,128,1024]{2,1,0:T(8,128)(2,1)S(1)}, u32[]{:S(2)}, u32[]{:S(2)}) %collective-permute-start.2) | collective-permute-done | bytes 524320 | tf_op jit(solution)/shard_map/ppermute | solution.py:29
  63.6 39.3 %all-to-all-done.rest_4_ = bf16[8,2,128,1024]{3,2,1,0:T(8,128)(2,1)} async-done(((bf16[8,2,128,1024]{3,2,1,0:T(8,128)(2,1)}), bf16[8,2,128,1024]{3,2,1,0:T(8,128)(2,1)}, u32[]{:S(2)}, u32[]{:S(2)}) %all-to-all-start) | async-done | bytes 4194336 | tf_op jit(solution)/shard_map/all_to_all | solution.py:52
  102.9 8.1 %all-to-all-start.1 = ((bf16[8,2,128,1024]{3,2,1,0:T(8,128)(2,1)}), bf16[8,2,128,1024]{3,2,1,0:T(8,128)(2,1)}, u32[]{:S(2)}, u32[]{:S(2)}) async-start(bf16[8,2,128,1024]{3,2,1,0:T(8,128)(2,1)} %pick_entries.3), calls=%async_computation.1 | async-start | bytes 8388608 | tf_op jit(solution)/shard_map/all_to_all | solution.py:52
  111.1 1.0 copy-done.25
  112.1 35.9 %attend_blocks.2 = (bf16[2,128,1024]{2,1,0:T(8,128)(2,1)}, bf16[2,128,1024]{2,1,0:T(8,128)(2,1)}, bf16[2,128,1024]{2,1,0:T(8,128)(2,1)}, bf16[2,128,1024]{2,1,0:...) custom-call(s32[1,8,2]{2,1,0:T(8,128)S(1)} %copy.10.uses, ...), custom_call_target="tpu_custom_call" | custom-call | flops 38654705664 | bytes 12582912 | tf_op jit(solution)/shard_map/attend_blocks/pallas_call | solution.py:239
  148.5 2.2 collective-permute-start.5
  150.7 2.1 collective-permute-start.6
  153.1 8.4 %collective-permute-done.3.refs_1_ = bf16[2,128,1024]{2,1,0:T(8,128)(2,1)S(1)} collective-permute-done((bf16[2,128,1024]{2,1,0:T(8,128)(2,1)}, bf16[2,128,1024]{2,1,0:T(8,128)(2,1)S(1)}, u32[]{:S(2)}, u32[]{:S(2)}) %collective-permute-start.3) | collective-permute-done | bytes 524320 | tf_op jit(solution)/shard_map/ppermute | solution.py:29
  162.3 0.9 copy-done.7
  163.2 9.5 %collective-permute-done.5.refs_3_ = bf16[2,128,1024]{2,1,0:T(8,128)(2,1)S(1)} collective-permute-done((bf16[2,128,1024]{2,1,0:T(8,128)(2,1)}, bf16[2,128,1024]{2,1,0:T(8,128)(2,1)S(1)}, u32[]{:S(2)}, u32[]{:S(2)}) %collective-permute-start.5) | collective-permute-done | bytes 524320 | tf_op jit(solution)/shard_map/ppermute | solution.py:29
  172.7 0.9 copy-done.9
  173.6 61.6 %collective-permute-done.6.rest_0_ = bf16[2,128,1024]{2,1,0:T(8,128)(2,1)S(1)} collective-permute-done((bf16[2,128,1024]{2,1,0:T(8,128)(2,1)}, bf16[2,128,1024]{2,1,0:T(8,128)(2,1)S(1)}, u32[]{:S(2)}, u32[]{:S(2)}) %collective-permute-start.6) | collective-permute-done | bytes 524320 | tf_op jit(solution)/shard_map/ppermute | solution.py:309
  235.9 12.2 %collective-permute-done.7.rest_1_ = bf16[2,128,1024]{2,1,0:T(8,128)(2,1)S(1)} collective-permute-done((bf16[2,128,1024]{2,1,0:T(8,128)(2,1)}, bf16[2,128,1024]{2,1,0:T(8,128)(2,1)S(1)}, u32[]{:S(2)}, u32[]{:S(2)}) %collective-permute-start.7) | collective-permute-done | bytes 524320 | tf_op jit(solution)/shard_map/ppermute | solution.py:309
  248.2 0.8 copy-done.14
  249.1 5.0 %all-to-all-start.3 = ((bf16[4,2,128,1024]{3,2,1,0:T(8,128)(2,1)}), bf16[4,2,128,1024]{3,2,1,0:T(8,128)(2,1)S(1)}, u32[]{:S(2)}, u32[]{:S(2)}) async-start(bf16[4,2,128,1024]{3,2,1,0:T(8,128)(2,1)} %get-tuple-element.80), calls=%async_computation.3 | async-start | bytes 4194304 | tf_op jit(solution)/shard_map/all_to_all | solution.py:41
  254.1 1.0 copy-done.22
  255.1 35.9 %attend_blocks.3 = (bf16[2,128,1024]{2,1,0:T(8,128)(2,1)}, bf16[2,128,1024]{2,1,0:T(8,128)(2,1)}, bf16[2,128,1024]{2,1,0:T(8,128)(2,1)}, bf16[2,128,1024]{2,1,0:...) custom-call(s32[1,8,2]{2,1,0:T(8,128)S(1)} %copy.12.uses, ...), custom_call_target="tpu_custom_call" | custom-call | flops 38654705664 | bytes 12582912 | tf_op jit(solution)/shard_map/attend_blocks/pallas_call | solution.py:239
  291.0 4.6 %all-to-all-start.2 = ((bf16[4,2,128,1024]{3,2,1,0:T(8,128)(2,1)}), bf16[4,2,128,1024]{3,2,1,0:T(8,128)(2,1)}, u32[]{:S(2)}, u32[]{:S(2)}) async-start(bf16[4,2,128,1024]{3,2,1,0:T(8,128)(2,1)} %get-tuple-element.67), calls=%async_computation.2 | async-start | bytes 4194304 | tf_op jit(solution)/shard_map/all_to_all | solution.py:41
  296.4 1.0 collective-permute-start.14
  297.4 34.2 %collective-permute-done.16.rest_3_ = bf16[2,128,1024]{2,1,0:T(8,128)(2,1)S(1)} collective-permute-done((bf16[2,128,1024]{2,1,0:T(8,128)(2,1)}, bf16[2,128,1024]{2,1,0:T(8,128)(2,1)S(1)}, u32[]{:S(2)}, u32[]{:S(2)}) %collective-permute-start.16) | collective-permute-done | bytes 524320 | tf_op jit(solution)/shard_map/ppermute | solution.py:309
  333.0 21.9 %collective-permute-done.14.rest_2_ = bf16[2,128,1024]{2,1,0:T(8,128)(2,1)S(1)} collective-permute-done((bf16[2,128,1024]{2,1,0:T(8,128)(2,1)S(1)}, bf16[2,128,1024]{2,1,0:T(8,128)(2,1)S(1)}, u32[]{:S(2)}, u32[]{:S(2)}) %collective-permute-start.14) | collective-permute-done | bytes 524320 | tf_op jit(solution)/shard_map/ppermute | solution.py:309
  354.9 0.8 copy-done.18
  356.2 2.2 collective-permute-start.13
  358.4 19.3 %collective-permute-done.17.rest_1_ = bf16[2,128,1024]{2,1,0:T(8,128)(2,1)S(1)} collective-permute-done((bf16[2,128,1024]{2,1,0:T(8,128)(2,1)}, bf16[2,128,1024]{2,1,0:T(8,128)(2,1)S(1)}, u32[]{:S(2)}, u32[]{:S(2)}) %collective-permute-start.17) | collective-permute-done | bytes 524320 | tf_op jit(solution)/shard_map/ppermute | solution.py:309
  377.7 20.6 %collective-permute-done.15.rest_0_ = bf16[2,128,1024]{2,1,0:T(8,128)(2,1)S(1)} collective-permute-done((bf16[2,128,1024]{2,1,0:T(8,128)(2,1)}, bf16[2,128,1024]{2,1,0:T(8,128)(2,1)S(1)}, u32[]{:S(2)}, u32[]{:S(2)}) %collective-permute-start.15) | collective-permute-done | bytes 524320 | tf_op jit(solution)/shard_map/ppermute | solution.py:309
  398.4 0.9 collective-permute-start.18
  399.3 1.0 copy-done.4
  400.4 1.0 copy-done.6
  401.4 1.0 copy-done.8
  402.4 1.0 copy-done.10
  403.5 1.0 copy-done.11
  404.5 3.6 unpack_rows.1
  408.2 3.5 owner_sum.2.rest_4_
  411.7 9.2 %collective-permute-done.19.rest_3_ = bf16[2,128,1024]{2,1,0:T(8,128)(2,1)} collective-permute-done((bf16[2,128,1024]{2,1,0:T(8,128)(2,1)}, bf16[2,128,1024]{2,1,0:T(8,128)(2,1)}, u32[]{:S(2)}, u32[]{:S(2)}) %collective-permute-start.19) | collective-permute-done | bytes 524320 | tf_op jit(solution)/shard_map/ppermute | solution.py:309
  420.8 12.8 %collective-permute-done.18.rest_2_ = bf16[2,128,1024]{2,1,0:T(8,128)(2,1)} collective-permute-done((bf16[2,128,1024]{2,1,0:T(8,128)(2,1)}, bf16[2,128,1024]{2,1,0:T(8,128)(2,1)}, u32[]{:S(2)}, u32[]{:S(2)}) %collective-permute-start.18) | collective-permute-done | bytes 524320 | tf_op jit(solution)/shard_map/ppermute | solution.py:309
  433.7 4.5 %owner_sum.3 = bf16[4,2,128,2048]{3,2,1,0:T(8,128)(2,1)} custom-call(s32[1,8,1]{2,1,0:T(8,128)S(1)} %copy.14.lists, bf16[4,2,128,1024]{3,2,1,0:T(8,128)(2,1)} %all-to-all-done.2.near_ref, bf16[2,128,1024]{2,1,0:T(8,128)(2,1)S(1)} %collective-permute-done.15.rest_0_, ...), custom_call_target="tpu_custom_call", output_to_operand_aliasing={{}: (6, {})} | custom-call | flops 2097152 | bytes 6291456 | tf_op jit(solution)/shard_map/owner_sum/pallas_call | solution.py:283
  (72 shorter events, 8.3 us)
Async XLA Ops:
  1.4 2.2 copy-start
  6.6 5.8 %copy-start.2 = (bf16[1,128,8192]{2,1,0:T(8,128)(2,1)S(1)}, bf16[1,128,8192]{2,1,0:T(8,128)(2,1)}, u32[]{:S(2)}) copy-start(bf16[1,128,8192]{2,1,0:T(8,128)(2,1)} %q_ref.1) | copy-start | bytes 6291460
  6.6 96.2 %all-to-all-start = ((bf16[8,2,128,1024]{3,2,1,0:T(8,128)(2,1)}), bf16[8,2,128,1024]{3,2,1,0:T(8,128)(2,1)}, u32[]{:S(2)}, u32[]{:S(2)}) async-start(bf16[8,2,128,1024]{3,2,1,0:T(8,128)(2,1)} %pick_entries.2), calls=%async_computation | async-start | bytes 8388608 | tf_op jit(solution)/shard_map/all_to_all | solution.py:52
  12.4 1.6 copy-start.3
  15.6 13.4 %collective-permute-start.8 = (bf16[2,128,1024]{2,1,0:T(8,128)(2,1)}, bf16[2,128,1024]{2,1,0:T(8,128)(2,1)S(1)}, u32[]{:S(2)}, u32[]{:S(2)}) collective-permute-start(bf16[2,128,1024]{2,1,0:T(8,128)(2,1)} %get-tuple-element.55), channel_id=1, source_target_pairs={{0,1},{1,0},{2,3},{3,2},{4,5},{5,4},{6,7},{7,6},{8,9},{9,8},{10,11... | collective-permute-start | bytes 1572872 | tf_op jit(solution)/shard_map/ppermute | solution.py:29
  15.9 18.7 %collective-permute-start.9 = (bf16[2,128,1024]{2,1,0:T(8,128)(2,1)}, bf16[2,128,1024]{2,1,0:T(8,128)(2,1)S(1)}, u32[]{:S(2)}, u32[]{:S(2)}) collective-permute-start(bf16[2,128,1024]{2,1,0:T(8,128)(2,1)} %get-tuple-element.56), channel_id=1, source_target_pairs={{0,2},{1,3},{2,0},{3,1},{4,6},{5,7},{6,4},{7,5},{8,10},{9,11},{10,... | collective-permute-start | bytes 1572872 | tf_op jit(solution)/shard_map/ppermute | solution.py:29
  16.2 13.1 %copy-start.26 = (s32[1,8,1]{1,2,0:T(1,128)S(1)}, s32[1,8,1]{1,2,0:T(1,128)}, u32[]{:S(2)}) copy-start(s32[1,8,1]{1,2,0:T(1,128)} %param.7) | copy-start | bytes 100
  16.2 24.2 %collective-permute-start.10 = (bf16[2,128,1024]{2,1,0:T(8,128)(2,1)}, bf16[2,128,1024]{2,1,0:T(8,128)(2,1)}, u32[]{:S(2)}, u32[]{:S(2)}) collective-permute-start(bf16[2,128,1024]{2,1,0:T(8,128)(2,1)} %get-tuple-element.57), channel_id=1, source_target_pairs={{0,3},{1,2},{2,1},{3,0},{4,7},{5,6},{6,5},{7,4},{8,11},{9,10},{10,... | collective-permute-start | bytes 1572872 | tf_op jit(solution)/shard_map/ppermute | solution.py:29
  19.9 31.8 %collective-permute-start = (bf16[2,128,1024]{2,1,0:T(8,128)(2,1)}, bf16[2,128,1024]{2,1,0:T(8,128)(2,1)S(1)}, u32[]{:S(2)}, u32[]{:S(2)}) collective-permute-start(bf16[2,128,1024]{2,1,0:T(8,128)(2,1)} %get-tuple-element.44), channel_id=1, source_target_pairs={{0,1},{1,0},{2,3},{3,2},{4,5},{5,4},{6,7},{7,6},{8,9},{9,8},{10,11... | collective-permute-start | bytes 1572872 | tf_op jit(solution)/shard_map/ppermute | solution.py:29
  20.2 31.4 %collective-permute-start.1 = (bf16[2,128,1024]{2,1,0:T(8,128)(2,1)}, bf16[2,128,1024]{2,1,0:T(8,128)(2,1)S(1)}, u32[]{:S(2)}, u32[]{:S(2)}) collective-permute-start(bf16[2,128,1024]{2,1,0:T(8,128)(2,1)} %get-tuple-element.45), channel_id=1, source_target_pairs={{0,2},{1,3},{2,0},{3,1},{4,6},{5,7},{6,4},{7,5},{8,10},{9,11},{10,... | collective-permute-start | bytes 1572872 | tf_op jit(solution)/shard_map/ppermute | solution.py:29
  29.0 33.7 %collective-permute-start.2 = (bf16[2,128,1024]{2,1,0:T(8,128)(2,1)}, bf16[2,128,1024]{2,1,0:T(8,128)(2,1)S(1)}, u32[]{:S(2)}, u32[]{:S(2)}) collective-permute-start(bf16[2,128,1024]{2,1,0:T(8,128)(2,1)} %get-tuple-element.46), channel_id=1, source_target_pairs={{0,3},{1,2},{2,1},{3,0},{4,7},{5,6},{6,5},{7,4},{8,11},{9,10},{10,... | collective-permute-start | bytes 1572872 | tf_op jit(solution)/shard_map/ppermute | solution.py:29
  29.3 2.2 copy-start.1
  34.7 68.2 %copy-start.21 = (bf16[2,128,1024]{2,1,0:T(8,128)(2,1)}, bf16[2,128,1024]{2,1,0:T(8,128)(2,1)S(1)}, u32[]{:S(2)}) copy-start(bf16[2,128,1024]{2,1,0:T(8,128)(2,1)S(1)} %collective-permute-done.9.rest_2_) | copy-start | bytes 1572868
  63.6 47.4 %copy-start.27 = (s32[1,8,2]{1,2,0:T(2,128)S(1)}, s32[1,8,2]{1,2,0:T(2,128)}, u32[]{:S(2)}) copy-start(s32[1,8,2]{1,2,0:T(2,128)} %param.8) | copy-start | bytes 196
  63.6 47.5 %copy-start.23 = (bf16[2,128,1024]{2,1,0:T(8,128)(2,1)S(1)}, bf16[2,128,1024]{2,1,0:T(8,128)(2,1)}, u32[]{:S(2)}) copy-start(bf16[2,128,1024]{2,1,0:T(8,128)(2,1)} %get-tuple-element.43.rest_0_) | copy-start | bytes 1572868
  102.9 146.2 %all-to-all-start.1 = ((bf16[8,2,128,1024]{3,2,1,0:T(8,128)(2,1)}), bf16[8,2,128,1024]{3,2,1,0:T(8,128)(2,1)}, u32[]{:S(2)}, u32[]{:S(2)}) async-start(bf16[8,2,128,1024]{3,2,1,0:T(8,128)(2,1)} %pick_entries.3), calls=%async_computation.1 | async-start | bytes 8388608 | tf_op jit(solution)/shard_map/all_to_all | solution.py:52
  111.1 1.0 copy-start.25
  148.0 13.5 %collective-permute-start.3 = (bf16[2,128,1024]{2,1,0:T(8,128)(2,1)}, bf16[2,128,1024]{2,1,0:T(8,128)(2,1)S(1)}, u32[]{:S(2)}, u32[]{:S(2)}) collective-permute-start(bf16[2,128,1024]{2,1,0:T(8,128)(2,1)} %get-tuple-element.48), channel_id=1, source_target_pairs={{0,1},{1,0},{2,3},{3,2},{4,5},{5,4},{6,7},{7,6},{8,9},{9,8},{10,11... | collective-permute-start | bytes 1572872 | tf_op jit(solution)/shard_map/ppermute | solution.py:29
  148.3 14.0 %collective-permute-start.4 = (bf16[2,128,1024]{2,1,0:T(8,128)(2,1)}, bf16[2,128,1024]{2,1,0:T(8,128)(2,1)S(1)}, u32[]{:S(2)}, u32[]{:S(2)}) collective-permute-start(bf16[2,128,1024]{2,1,0:T(8,128)(2,1)} %get-tuple-element.49), channel_id=1, source_target_pairs={{0,2},{1,3},{2,0},{3,1},{4,6},{5,7},{6,4},{7,5},{8,10},{9,11},{10,... | collective-permute-start | bytes 1572872 | tf_op jit(solution)/shard_map/ppermute | solution.py:29
  148.5 24.2 %collective-permute-start.5 = (bf16[2,128,1024]{2,1,0:T(8,128)(2,1)}, bf16[2,128,1024]{2,1,0:T(8,128)(2,1)S(1)}, u32[]{:S(2)}, u32[]{:S(2)}) collective-permute-start(bf16[2,128,1024]{2,1,0:T(8,128)(2,1)} %get-tuple-element.50), channel_id=1, source_target_pairs={{0,3},{1,2},{2,1},{3,0},{4,7},{5,6},{6,5},{7,4},{8,11},{9,10},{10,... | collective-permute-start | bytes 1572872 | tf_op jit(solution)/shard_map/ppermute | solution.py:29
  150.7 84.4 %collective-permute-start.6 = (bf16[2,128,1024]{2,1,0:T(8,128)(2,1)}, bf16[2,128,1024]{2,1,0:T(8,128)(2,1)S(1)}, u32[]{:S(2)}, u32[]{:S(2)}) collective-permute-start(bf16[2,128,1024]{2,1,0:T(8,128)(2,1)} %get-tuple-element.51), channel_id=1, source_target_pairs={{0,16},{4,20},{8,24},{12,28},{16,0},{20,4},{24,8},{28,12},{1,17},{... | collective-permute-start | bytes 1572872 | tf_op jit(solution)/shard_map/ppermute | solution.py:309
  152.8 95.4 %collective-permute-start.7 = (bf16[2,128,1024]{2,1,0:T(8,128)(2,1)}, bf16[2,128,1024]{2,1,0:T(8,128)(2,1)S(1)}, u32[]{:S(2)}, u32[]{:S(2)}) collective-permute-start(bf16[2,128,1024]{2,1,0:T(8,128)(2,1)} %get-tuple-element.52), channel_id=1, source_target_pairs={{0,20},{4,24},{8,28},{12,16},{20,0},{24,4},{28,8},{16,12},{1,21},{... | collective-permute-start | bytes 1572872 | tf_op jit(solution)/shard_map/ppermute | solution.py:309
  162.3 0.9 copy-start.7
  172.7 0.9 copy-start.9
  249.1 5.0 %copy-start.20 = (bf16[2,128,1024]{2,1,0:T(8,128)(2,1)S(1)}, bf16[2,128,1024]{2,1,0:T(8,128)(2,1)}, u32[]{:S(2)}) copy-start(bf16[2,128,1024]{2,1,0:T(8,128)(2,1)} %get-tuple-element.54.rest_0_) | copy-start | bytes 1572868
  249.1 42.0 %all-to-all-start.3 = ((bf16[4,2,128,1024]{3,2,1,0:T(8,128)(2,1)}), bf16[4,2,128,1024]{3,2,1,0:T(8,128)(2,1)S(1)}, u32[]{:S(2)}, u32[]{:S(2)}) async-start(bf16[4,2,128,1024]{3,2,1,0:T(8,128)(2,1)} %get-tuple-element.80), calls=%async_computation.3 | async-start | bytes 4194304 | tf_op jit(solution)/shard_map/all_to_all | solution.py:41
  254.1 1.0 copy-start.22
  291.0 5.4 %copy-start.28 = (bf16[2,128,1024]{2,1,0:T(8,128)(2,1)S(1)}, bf16[2,128,1024]{2,1,0:T(8,128)(2,1)}, u32[]{:S(2)}) copy-start(bf16[2,128,1024]{2,1,0:T(8,128)(2,1)} %get-tuple-element.70) | copy-start | bytes 1572868
  291.0 142.6 %all-to-all-start.2 = ((bf16[4,2,128,1024]{3,2,1,0:T(8,128)(2,1)}), bf16[4,2,128,1024]{3,2,1,0:T(8,128)(2,1)}, u32[]{:S(2)}, u32[]{:S(2)}) async-start(bf16[4,2,128,1024]{3,2,1,0:T(8,128)(2,1)} %get-tuple-element.67), calls=%async_computation.2 | async-start | bytes 4194304 | tf_op jit(solution)/shard_map/all_to_all | solution.py:41
  295.7 35.9 %collective-permute-start.16 = (bf16[2,128,1024]{2,1,0:T(8,128)(2,1)}, bf16[2,128,1024]{2,1,0:T(8,128)(2,1)S(1)}, u32[]{:S(2)}, u32[]{:S(2)}) collective-permute-start(bf16[2,128,1024]{2,1,0:T(8,128)(2,1)} %get-tuple-element.74), channel_id=1, source_target_pairs={{0,28},{4,16},{8,20},{12,24},{28,0},{16,4},{20,8},{24,12},{1,29},{... | collective-permute-start | bytes 1572872 | tf_op jit(solution)/shard_map/ppermute | solution.py:309
  296.4 58.5 %collective-permute-start.14 = (bf16[2,128,1024]{2,1,0:T(8,128)(2,1)S(1)}, bf16[2,128,1024]{2,1,0:T(8,128)(2,1)S(1)}, u32[]{:S(2)}, u32[]{:S(2)}) collective-permute-start(bf16[2,128,1024]{2,1,0:T(8,128)(2,1)S(1)} %copy-done.28), channel_id=1, source_target_pairs={{0,24},{4,28},{8,16},{12,20},{24,0},{28,4},{16,8},{20,12},{1,25},{... | collective-permute-start | bytes 1572872 | tf_op jit(solution)/shard_map/ppermute | solution.py:309
  332.4 45.4 %collective-permute-start.17 = (bf16[2,128,1024]{2,1,0:T(8,128)(2,1)}, bf16[2,128,1024]{2,1,0:T(8,128)(2,1)S(1)}, u32[]{:S(2)}, u32[]{:S(2)}) collective-permute-start(bf16[2,128,1024]{2,1,0:T(8,128)(2,1)} %get-tuple-element.75), channel_id=1, source_target_pairs={{0,20},{4,24},{8,28},{12,16},{20,0},{24,4},{28,8},{16,12},{1,21},{... | collective-permute-start | bytes 1572872 | tf_op jit(solution)/shard_map/ppermute | solution.py:309
  354.9 0.8 copy-start.18
  355.8 42.6 %collective-permute-start.15 = (bf16[2,128,1024]{2,1,0:T(8,128)(2,1)}, bf16[2,128,1024]{2,1,0:T(8,128)(2,1)S(1)}, u32[]{:S(2)}, u32[]{:S(2)}) collective-permute-start(bf16[2,128,1024]{2,1,0:T(8,128)(2,1)} %get-tuple-element.71), channel_id=1, source_target_pairs={{0,16},{4,20},{8,24},{12,28},{16,0},{20,4},{24,8},{28,12},{1,17},{... | collective-permute-start | bytes 1572872 | tf_op jit(solution)/shard_map/ppermute | solution.py:309
  355.8 43.5 %collective-permute-start.11 = (bf16[2,128,1024]{2,1,0:T(8,128)(2,1)}, bf16[2,128,1024]{2,1,0:T(8,128)(2,1)}, u32[]{:S(2)}, u32[]{:S(2)}) collective-permute-start(bf16[2,128,1024]{2,1,0:T(8,128)(2,1)} %get-tuple-element.61), channel_id=1, source_target_pairs={{0,1},{1,0},{2,3},{3,2},{4,5},{5,4},{6,7},{7,6},{8,9},{9,8},{10,11... | collective-permute-start | bytes 1572872 | tf_op jit(solution)/shard_map/ppermute | solution.py:29
  356.0 43.3 %collective-permute-start.12 = (bf16[2,128,1024]{2,1,0:T(8,128)(2,1)}, bf16[2,128,1024]{2,1,0:T(8,128)(2,1)}, u32[]{:S(2)}, u32[]{:S(2)}) collective-permute-start(bf16[2,128,1024]{2,1,0:T(8,128)(2,1)} %get-tuple-element.62), channel_id=1, source_target_pairs={{0,2},{1,3},{2,0},{3,1},{4,6},{5,7},{6,4},{7,5},{8,10},{9,11},{10,... | collective-permute-start | bytes 1572872 | tf_op jit(solution)/shard_map/ppermute | solution.py:29
  356.2 43.1 %collective-permute-start.13 = (bf16[2,128,1024]{2,1,0:T(8,128)(2,1)}, bf16[2,128,1024]{2,1,0:T(8,128)(2,1)}, u32[]{:S(2)}, u32[]{:S(2)}) collective-permute-start(bf16[2,128,1024]{2,1,0:T(8,128)(2,1)} %get-tuple-element.63), channel_id=1, source_target_pairs={{0,3},{1,2},{2,1},{3,0},{4,7},{5,6},{6,5},{7,4},{8,11},{9,10},{10,... | collective-permute-start | bytes 1572872 | tf_op jit(solution)/shard_map/ppermute | solution.py:29
  377.7 43.1 %collective-permute-start.19 = (bf16[2,128,1024]{2,1,0:T(8,128)(2,1)}, bf16[2,128,1024]{2,1,0:T(8,128)(2,1)}, u32[]{:S(2)}, u32[]{:S(2)}) collective-permute-start(bf16[2,128,1024]{2,1,0:T(8,128)(2,1)} %get-tuple-element.79), channel_id=1, source_target_pairs={{0,28},{4,16},{8,20},{12,24},{28,0},{16,4},{20,8},{24,12},{1,29},{... | collective-permute-start | bytes 1572872 | tf_op jit(solution)/shard_map/ppermute | solution.py:309
  398.4 35.3 %collective-permute-start.18 = (bf16[2,128,1024]{2,1,0:T(8,128)(2,1)}, bf16[2,128,1024]{2,1,0:T(8,128)(2,1)}, u32[]{:S(2)}, u32[]{:S(2)}) collective-permute-start(bf16[2,128,1024]{2,1,0:T(8,128)(2,1)} %get-tuple-element.77), channel_id=1, source_target_pairs={{0,24},{4,28},{8,16},{12,20},{24,0},{28,4},{16,8},{20,12},{1,25},{... | collective-permute-start | bytes 1572872 | tf_op jit(solution)/shard_map/ppermute | solution.py:309
  399.3 1.0 copy-start.4
  400.4 1.0 copy-start.6
  401.4 1.0 copy-start.8
  402.4 1.0 copy-start.10
  403.5 1.0 copy-start.11
  404.5 3.7 copy-start.13
  404.5 3.7 copy-start.15
  404.5 3.7 copy-start.17
  404.5 3.7 copy-start.19
  (5 other events, 4.0 us)

commit v10 on v9

--- a/solution.py
+++ b/solution.py
@@ -332,6 +332,8 @@
     for h in range(chunks):
         rows_out, near, far = attend(block_slots, rows[h], arrived[h])
         far = swap_far(far, done)
+        if h > 0:
+            near = after(near, done[: seqs // 2])
         returns.append((swap_near(near, seqs), far))
         token_parts.append(swap_rows(rows_out))
         block_slots = after(block_slots, (token_parts[-1], far[:DEPTH]))

time: 439 us -> 413 us (0.941)
  waiting for transfers between devices: 286 us -> 232 us
  starting transfers between devices: 38 us -> 61.4 us
    ppermute x8, waiting for transfers between devices: 192 us -> 157 us  [swap_far(): got.append(lax.ppermute(piece, 'enc', pairs))]
    ppermute x8, starting transfers between devices: 5.68 us -> 28.7 us  [swap_far(): got.append(lax.ppermute(piece, 'enc', pairs))]
    ppermute x12, waiting for transfers between devices: 54.7 us -> 35.9 us  [exchange(): return lax.ppermute(array, axis, pairs)]
    unnamed x60 -> x66, local copies, waits for them, and re-layouts: 20.7 us -> 23.9 us
  transfers between devices with their start and end apart: 24 -> 24, of which waited for: 15 -> 11; matrix products, arithmetic and copies ran while one was open for 0% -> 0% of each run, Pallas kernels for 19% -> 21%
where the time goes in v10:
time: 413 us; the launch traced here: 411 us
  waiting for transfers between devices  232 us (56%)
  Pallas kernels  92.8 us (22%)
  starting transfers between devices  61.4 us (15%)
  local copies, waits for them, and re-layouts  24.1 us (6%)
    ppermute x8, waiting for transfers between devices, swap_far(): got.append(lax.ppermute(piece, 'enc', pairs))  157 us
    pallas_call x2, Pallas kernels, attend(): pl.pallas_call(functools.partial(attend_kernel, seqs, parts), grid=(heads...  71.8 us
    all_to_all x2, waiting for transfers between devices, swap_pool(): return lax.all_to_all(array, 'enc', split_axis=0, concat_axis=0, tiled=True)  39.3 us
    ppermute x12, waiting for transfers between devices, exchange(): return lax.ppermute(array, axis, pairs)  35.9 us
    ppermute x8, starting transfers between devices, swap_far(): got.append(lax.ppermute(piece, 'enc', pairs))  28.7 us
    unnamed x66, local copies, waits for them, and re-layouts  23.9 us
    all_to_all x2, starting transfers between devices, swap_pool(): return lax.all_to_all(array, 'enc', split_axis=0, concat_axis=0, tiled=True)  13.9 us
    all_to_all x2, starting transfers between devices, swap_near(): lax.all_to_all(array, 'enc', split_axis=0, concat_axis=0, axis_index_grou...  10.1 us
  transfers between devices with their start and end apart: 24, of which 11 were waited for; matrix products, arithmetic and copies ran while one was open for 0% of the time, Pallas kernels for 21%

profile of v10, /device:TPU:15, one launch (start us, length us, event | category | flops | bytes accessed | tf_op | source)
XLA Modules:
  0.0 411.5 jit_solution(17984558763763105714)
XLA Ops:
  1.4 2.2 copy-done
  3.5 3.1 pick_entries.2
  6.6 5.8 %all-to-all-start = ((bf16[8,2,128,1024]{3,2,1,0:T(8,128)(2,1)}), bf16[8,2,128,1024]{3,2,1,0:T(8,128)(2,1)}, u32[]{:S(2)}, u32[]{:S(2)}) async-start(bf16[8,2,128,1024]{3,2,1,0:T(8,128)(2,1)} %pick_entries.2), calls=%async_computation | async-start | bytes 8388608 | tf_op jit(solution)/shard_map/all_to_all | solution.py:52
  12.4 1.6 copy-done.3
  14.0 1.6 pack_rows.3
  16.2 2.2 collective-permute-start.10
  18.4 1.6 pack_rows.2
  20.5 8.6 %collective-permute-done.8.rest_1_ = bf16[2,128,1024]{2,1,0:T(8,128)(2,1)S(1)} collective-permute-done((bf16[2,128,1024]{2,1,0:T(8,128)(2,1)}, bf16[2,128,1024]{2,1,0:T(8,128)(2,1)S(1)}, u32[]{:S(2)}, u32[]{:S(2)}) %collective-permute-start.8) | collective-permute-done | bytes 524320 | tf_op jit(solution)/shard_map/ppermute | solution.py:29
  29.1 0.8 copy-done.21
  30.2 2.2 copy-done.1
  32.4 3.1 pick_entries.3
  35.5 4.8 %collective-permute-done.10.rest_3_ = bf16[2,128,1024]{2,1,0:T(8,128)(2,1)S(1)} collective-permute-done((bf16[2,128,1024]{2,1,0:T(8,128)(2,1)}, bf16[2,128,1024]{2,1,0:T(8,128)(2,1)S(1)}, u32[]{:S(2)}, u32[]{:S(2)}) %collective-permute-start.10) | collective-permute-done | bytes 524320 | tf_op jit(solution)/shard_map/ppermute | solution.py:29
  40.3 11.4 %collective-permute-done.rest_1_ = bf16[2,128,1024]{2,1,0:T(8,128)(2,1)S(1)} collective-permute-done((bf16[2,128,1024]{2,1,0:T(8,128)(2,1)}, bf16[2,128,1024]{2,1,0:T(8,128)(2,1)S(1)}, u32[]{:S(2)}, u32[]{:S(2)}) %collective-permute-start) | collective-permute-done | bytes 524320 | tf_op jit(solution)/shard_map/ppermute | solution.py:29
  51.7 11.1 %collective-permute-done.2.rest_3_ = bf16[2,128,1024]{2,1,0:T(8,128)(2,1)S(1)} collective-permute-done((bf16[2,128,1024]{2,1,0:T(8,128)(2,1)}, bf16[2,128,1024]{2,1,0:T(8,128)(2,1)S(1)}, u32[]{:S(2)}, u32[]{:S(2)}) %collective-permute-start.2) | collective-permute-done | bytes 524320 | tf_op jit(solution)/shard_map/ppermute | solution.py:29
  63.6 39.3 %all-to-all-done.rest_4_ = bf16[8,2,128,1024]{3,2,1,0:T(8,128)(2,1)} async-done(((bf16[8,2,128,1024]{3,2,1,0:T(8,128)(2,1)}), bf16[8,2,128,1024]{3,2,1,0:T(8,128)(2,1)}, u32[]{:S(2)}, u32[]{:S(2)}) %all-to-all-start) | async-done | bytes 4194336 | tf_op jit(solution)/shard_map/all_to_all | solution.py:52
  102.9 8.1 %all-to-all-start.1 = ((bf16[8,2,128,1024]{3,2,1,0:T(8,128)(2,1)}), bf16[8,2,128,1024]{3,2,1,0:T(8,128)(2,1)}, u32[]{:S(2)}, u32[]{:S(2)}) async-start(bf16[8,2,128,1024]{3,2,1,0:T(8,128)(2,1)} %pick_entries.3), calls=%async_computation.1 | async-start | bytes 8388608 | tf_op jit(solution)/shard_map/all_to_all | solution.py:52
  111.1 1.0 copy-done.29
  112.1 35.9 %attend_blocks.2 = (bf16[2,128,1024]{2,1,0:T(8,128)(2,1)}, bf16[2,128,1024]{2,1,0:T(8,128)(2,1)}, bf16[2,128,1024]{2,1,0:T(8,128)(2,1)}, bf16[2,128,1024]{2,1,0:...) custom-call(s32[1,8,2]{2,1,0:T(8,128)S(1)} %copy.10.uses, ...), custom_call_target="tpu_custom_call" | custom-call | flops 38654705664 | bytes 12582912 | tf_op jit(solution)/shard_map/attend_blocks/pallas_call | solution.py:239
  148.0 2.2 collective-permute-start.6
  150.6 2.2 collective-permute-start.5
  152.8 82.3 %collective-permute-done.6.rest_0_ = bf16[2,128,1024]{2,1,0:T(8,128)(2,1)S(1)} collective-permute-done((bf16[2,128,1024]{2,1,0:T(8,128)(2,1)}, bf16[2,128,1024]{2,1,0:T(8,128)(2,1)S(1)}, u32[]{:S(2)}, u32[]{:S(2)}) %collective-permute-start.6) | collective-permute-done | bytes 524320 | tf_op jit(solution)/shard_map/ppermute | solution.py:309
  235.9 1.0 collective-permute-start.14
  236.9 23.0 %collective-permute-done.7.rest_1_ = bf16[2,128,1024]{2,1,0:T(8,128)(2,1)S(1)} collective-permute-done((bf16[2,128,1024]{2,1,0:T(8,128)(2,1)}, bf16[2,128,1024]{2,1,0:T(8,128)(2,1)S(1)}, u32[]{:S(2)}, u32[]{:S(2)}) %collective-permute-start.7) | collective-permute-done | bytes 524320 | tf_op jit(solution)/shard_map/ppermute | solution.py:309
  259.9 0.8 copy-done.14
  261.5 0.8 copy-done.7
  262.4 0.9 copy-done.9
  263.3 5.6 %all-to-all-start.3 = ((bf16[4,2,128,1024]{3,2,1,0:T(8,128)(2,1)}), bf16[4,2,128,1024]{3,2,1,0:T(8,128)(2,1)S(1)}, u32[]{:S(2)}, u32[]{:S(2)}) async-start(bf16[4,2,128,1024]{3,2,1,0:T(8,128)(2,1)} %get-tuple-element.82), calls=%async_computation.3 | async-start | bytes 4194304 | tf_op jit(solution)/shard_map/all_to_all | solution.py:41
  268.9 1.0 copy-done.20
  270.0 1.0 copy-done.22
  271.0 1.0 copy-done.24
  272.0 1.0 copy-done.26
  273.1 36.0 %attend_blocks.3 = (bf16[2,128,1024]{2,1,0:T(8,128)(2,1)}, bf16[2,128,1024]{2,1,0:T(8,128)(2,1)}, bf16[2,128,1024]{2,1,0:T(8,128)(2,1)}, bf16[2,128,1024]{2,1,0:...) custom-call(s32[1,8,2]{2,1,0:T(8,128)S(1)} %copy.12.uses, ...), custom_call_target="tpu_custom_call" | custom-call | flops 38654705664 | bytes 12582912 | tf_op jit(solution)/shard_map/attend_blocks/pallas_call | solution.py:239
  310.0 4.5 %all-to-all-start.2 = ((bf16[4,2,128,1024]{3,2,1,0:T(8,128)(2,1)}), bf16[4,2,128,1024]{3,2,1,0:T(8,128)(2,1)}, u32[]{:S(2)}, u32[]{:S(2)}) async-start(bf16[4,2,128,1024]{3,2,1,0:T(8,128)(2,1)} %get-tuple-element.73), calls=%async_computation.2 | async-start | bytes 4194304 | tf_op jit(solution)/shard_map/all_to_all | solution.py:41
  314.6 2.6 collective-permute-start.16
  317.6 2.2 collective-permute-start.13
  319.8 9.6 %collective-permute-done.17.rest_1_ = bf16[2,128,1024]{2,1,0:T(8,128)(2,1)S(1)} collective-permute-done((bf16[2,128,1024]{2,1,0:T(8,128)(2,1)}, bf16[2,128,1024]{2,1,0:T(8,128)(2,1)S(1)}, u32[]{:S(2)}, u32[]{:S(2)}) %collective-permute-start.17) | collective-permute-done | bytes 524320 | tf_op jit(solution)/shard_map/ppermute | solution.py:309
  329.4 22.6 %collective-permute-start.19 = (bf16[2,128,1024]{2,1,0:T(8,128)(2,1)}, bf16[2,128,1024]{2,1,0:T(8,128)(2,1)}, u32[]{:S(2)}, u32[]{:S(2)}) collective-permute-start(bf16[2,128,1024]{2,1,0:T(8,128)(2,1)} %get-tuple-element.81), channel_id=1, source_target_pairs={{0,28},{4,16},{8,20},{12,24},{28,0},{16,4},{20,8},{24,12},{1,29},{... | collective-permute-start | bytes 1572872 | tf_op jit(solution)/shard_map/ppermute | solution.py:309
  352.0 9.8 %collective-permute-done.16.rest_0_ = bf16[2,128,1024]{2,1,0:T(8,128)(2,1)S(1)} collective-permute-done((bf16[2,128,1024]{2,1,0:T(8,128)(2,1)}, bf16[2,128,1024]{2,1,0:T(8,128)(2,1)S(1)}, u32[]{:S(2)}, u32[]{:S(2)}) %collective-permute-start.16) | collective-permute-done | bytes 524320 | tf_op jit(solution)/shard_map/ppermute | solution.py:309
  362.1 1.0 copy-done.4
  363.1 1.0 copy-done.6
  364.2 1.0 copy-done.8
  365.2 1.0 copy-done.10
  366.3 1.0 copy-done.11
  367.3 3.6 unpack_rows.1
  371.0 3.5 owner_sum.2.rest_4_
  374.4 19.5 %collective-permute-done.19.rest_3_ = bf16[2,128,1024]{2,1,0:T(8,128)(2,1)} collective-permute-done((bf16[2,128,1024]{2,1,0:T(8,128)(2,1)}, bf16[2,128,1024]{2,1,0:T(8,128)(2,1)}, u32[]{:S(2)}, u32[]{:S(2)}) %collective-permute-start.19) | collective-permute-done | bytes 524320 | tf_op jit(solution)/shard_map/ppermute | solution.py:309
  393.9 13.0 %collective-permute-done.18.rest_2_ = bf16[2,128,1024]{2,1,0:T(8,128)(2,1)} collective-permute-done((bf16[2,128,1024]{2,1,0:T(8,128)(2,1)}, bf16[2,128,1024]{2,1,0:T(8,128)(2,1)}, u32[]{:S(2)}, u32[]{:S(2)}) %collective-permute-start.18) | collective-permute-done | bytes 524320 | tf_op jit(solution)/shard_map/ppermute | solution.py:309
  407.0 4.5 %owner_sum.3 = bf16[4,2,128,2048]{3,2,1,0:T(8,128)(2,1)} custom-call(s32[1,8,1]{2,1,0:T(8,128)S(1)} %copy.14.lists, bf16[4,2,128,1024]{3,2,1,0:T(8,128)(2,1)} %all-to-all-done.2.near_ref, bf16[2,128,1024]{2,1,0:T(8,128)(2,1)S(1)} %collective-permute-done.16.rest_0_, ...), custom_call_target="tpu_custom_call", output_to_operand_aliasing={{}: (6, {})} | custom-call | flops 2097152 | bytes 6291456 | tf_op jit(solution)/shard_map/owner_sum/pallas_call | solution.py:283
  (78 shorter events, 7.0 us)
Async XLA Ops:
  1.4 2.2 copy-start
  6.6 5.8 %copy-start.2 = (bf16[1,128,8192]{2,1,0:T(8,128)(2,1)S(1)}, bf16[1,128,8192]{2,1,0:T(8,128)(2,1)}, u32[]{:S(2)}) copy-start(bf16[1,128,8192]{2,1,0:T(8,128)(2,1)} %q_ref.1) | copy-start | bytes 6291460
  6.6 96.2 %all-to-all-start = ((bf16[8,2,128,1024]{3,2,1,0:T(8,128)(2,1)}), bf16[8,2,128,1024]{3,2,1,0:T(8,128)(2,1)}, u32[]{:S(2)}, u32[]{:S(2)}) async-start(bf16[8,2,128,1024]{3,2,1,0:T(8,128)(2,1)} %pick_entries.2), calls=%async_computation | async-start | bytes 8388608 | tf_op jit(solution)/shard_map/all_to_all | solution.py:52
  12.4 1.6 copy-start.3
  15.6 13.4 %collective-permute-start.8 = (bf16[2,128,1024]{2,1,0:T(8,128)(2,1)}, bf16[2,128,1024]{2,1,0:T(8,128)(2,1)S(1)}, u32[]{:S(2)}, u32[]{:S(2)}) collective-permute-start(bf16[2,128,1024]{2,1,0:T(8,128)(2,1)} %get-tuple-element.56), channel_id=1, source_target_pairs={{0,1},{1,0},{2,3},{3,2},{4,5},{5,4},{6,7},{7,6},{8,9},{9,8},{10,11... | collective-permute-start | bytes 1572872 | tf_op jit(solution)/shard_map/ppermute | solution.py:29
  16.0 19.5 %collective-permute-start.9 = (bf16[2,128,1024]{2,1,0:T(8,128)(2,1)}, bf16[2,128,1024]{2,1,0:T(8,128)(2,1)S(1)}, u32[]{:S(2)}, u32[]{:S(2)}) collective-permute-start(bf16[2,128,1024]{2,1,0:T(8,128)(2,1)} %get-tuple-element.57), channel_id=1, source_target_pairs={{0,2},{1,3},{2,0},{3,1},{4,6},{5,7},{6,4},{7,5},{8,10},{9,11},{10,... | collective-permute-start | bytes 1572872 | tf_op jit(solution)/shard_map/ppermute | solution.py:29
  16.2 13.9 %copy-start.30 = (s32[1,8,1]{1,2,0:T(1,128)S(1)}, s32[1,8,1]{1,2,0:T(1,128)}, u32[]{:S(2)}) copy-start(s32[1,8,1]{1,2,0:T(1,128)} %param.7) | copy-start | bytes 100
  16.2 24.1 %collective-permute-start.10 = (bf16[2,128,1024]{2,1,0:T(8,128)(2,1)}, bf16[2,128,1024]{2,1,0:T(8,128)(2,1)S(1)}, u32[]{:S(2)}, u32[]{:S(2)}) collective-permute-start(bf16[2,128,1024]{2,1,0:T(8,128)(2,1)} %get-tuple-element.58), channel_id=1, source_target_pairs={{0,3},{1,2},{2,1},{3,0},{4,7},{5,6},{6,5},{7,4},{8,11},{9,10},{10,... | collective-permute-start | bytes 1572872 | tf_op jit(solution)/shard_map/ppermute | solution.py:29
  19.9 31.7 %collective-permute-start = (bf16[2,128,1024]{2,1,0:T(8,128)(2,1)}, bf16[2,128,1024]{2,1,0:T(8,128)(2,1)S(1)}, u32[]{:S(2)}, u32[]{:S(2)}) collective-permute-start(bf16[2,128,1024]{2,1,0:T(8,128)(2,1)} %get-tuple-element.45), channel_id=1, source_target_pairs={{0,1},{1,0},{2,3},{3,2},{4,5},{5,4},{6,7},{7,6},{8,9},{9,8},{10,11... | collective-permute-start | bytes 1572872 | tf_op jit(solution)/shard_map/ppermute | solution.py:29
  20.3 31.4 %collective-permute-start.1 = (bf16[2,128,1024]{2,1,0:T(8,128)(2,1)}, bf16[2,128,1024]{2,1,0:T(8,128)(2,1)S(1)}, u32[]{:S(2)}, u32[]{:S(2)}) collective-permute-start(bf16[2,128,1024]{2,1,0:T(8,128)(2,1)} %get-tuple-element.46), channel_id=1, source_target_pairs={{0,2},{1,3},{2,0},{3,1},{4,6},{5,7},{6,4},{7,5},{8,10},{9,11},{10,... | collective-permute-start | bytes 1572872 | tf_op jit(solution)/shard_map/ppermute | solution.py:29
  29.9 32.9 %collective-permute-start.2 = (bf16[2,128,1024]{2,1,0:T(8,128)(2,1)}, bf16[2,128,1024]{2,1,0:T(8,128)(2,1)S(1)}, u32[]{:S(2)}, u32[]{:S(2)}) collective-permute-start(bf16[2,128,1024]{2,1,0:T(8,128)(2,1)} %get-tuple-element.47), channel_id=1, source_target_pairs={{0,3},{1,2},{2,1},{3,0},{4,7},{5,6},{6,5},{7,4},{8,11},{9,10},{10,... | collective-permute-start | bytes 1572872 | tf_op jit(solution)/shard_map/ppermute | solution.py:29
  30.2 2.2 copy-start.1
  35.5 67.4 %copy-start.23 = (bf16[2,128,1024]{2,1,0:T(8,128)(2,1)}, bf16[2,128,1024]{2,1,0:T(8,128)(2,1)S(1)}, u32[]{:S(2)}) copy-start(bf16[2,128,1024]{2,1,0:T(8,128)(2,1)S(1)} %collective-permute-done.9.rest_2_) | copy-start | bytes 1572868
  40.3 62.6 %copy-start.25 = (bf16[2,128,1024]{2,1,0:T(8,128)(2,1)}, bf16[2,128,1024]{2,1,0:T(8,128)(2,1)S(1)}, u32[]{:S(2)}) copy-start(bf16[2,128,1024]{2,1,0:T(8,128)(2,1)S(1)} %collective-permute-done.10.rest_3_) | copy-start | bytes 1572868
  63.6 47.4 %copy-start.31 = (s32[1,8,2]{1,2,0:T(2,128)S(1)}, s32[1,8,2]{1,2,0:T(2,128)}, u32[]{:S(2)}) copy-start(s32[1,8,2]{1,2,0:T(2,128)} %param.8) | copy-start | bytes 196
  63.6 47.5 %copy-start.27 = (bf16[2,128,1024]{2,1,0:T(8,128)(2,1)S(1)}, bf16[2,128,1024]{2,1,0:T(8,128)(2,1)}, u32[]{:S(2)}) copy-start(bf16[2,128,1024]{2,1,0:T(8,128)(2,1)} %get-tuple-element.44.rest_0_) | copy-start | bytes 1572868
  102.9 160.4 %all-to-all-start.1 = ((bf16[8,2,128,1024]{3,2,1,0:T(8,128)(2,1)}), bf16[8,2,128,1024]{3,2,1,0:T(8,128)(2,1)}, u32[]{:S(2)}, u32[]{:S(2)}) async-start(bf16[8,2,128,1024]{3,2,1,0:T(8,128)(2,1)} %pick_entries.3), calls=%async_computation.1 | async-start | bytes 8388608 | tf_op jit(solution)/shard_map/all_to_all | solution.py:52
  111.1 1.0 copy-start.29
  148.0 87.1 %collective-permute-start.6 = (bf16[2,128,1024]{2,1,0:T(8,128)(2,1)}, bf16[2,128,1024]{2,1,0:T(8,128)(2,1)S(1)}, u32[]{:S(2)}, u32[]{:S(2)}) collective-permute-start(bf16[2,128,1024]{2,1,0:T(8,128)(2,1)} %get-tuple-element.52), channel_id=1, source_target_pairs={{0,16},{4,20},{8,24},{12,28},{16,0},{20,4},{24,8},{28,12},{1,17},{... | collective-permute-start | bytes 1572872 | tf_op jit(solution)/shard_map/ppermute | solution.py:309
  150.2 109.7 %collective-permute-start.7 = (bf16[2,128,1024]{2,1,0:T(8,128)(2,1)}, bf16[2,128,1024]{2,1,0:T(8,128)(2,1)S(1)}, u32[]{:S(2)}, u32[]{:S(2)}) collective-permute-start(bf16[2,128,1024]{2,1,0:T(8,128)(2,1)} %get-tuple-element.53), channel_id=1, source_target_pairs={{0,20},{4,24},{8,28},{12,16},{20,0},{24,4},{28,8},{16,12},{1,21},{... | collective-permute-start | bytes 1572872 | tf_op jit(solution)/shard_map/ppermute | solution.py:309
  150.2 110.5 %collective-permute-start.3 = (bf16[2,128,1024]{2,1,0:T(8,128)(2,1)}, bf16[2,128,1024]{2,1,0:T(8,128)(2,1)S(1)}, u32[]{:S(2)}, u32[]{:S(2)}) collective-permute-start(bf16[2,128,1024]{2,1,0:T(8,128)(2,1)} %get-tuple-element.49), channel_id=1, source_target_pairs={{0,1},{1,0},{2,3},{3,2},{4,5},{5,4},{6,7},{7,6},{8,9},{9,8},{10,11... | collective-permute-start | bytes 1572872 | tf_op jit(solution)/shard_map/ppermute | solution.py:29
  150.4 111.1 %collective-permute-start.4 = (bf16[2,128,1024]{2,1,0:T(8,128)(2,1)}, bf16[2,128,1024]{2,1,0:T(8,128)(2,1)S(1)}, u32[]{:S(2)}, u32[]{:S(2)}) collective-permute-start(bf16[2,128,1024]{2,1,0:T(8,128)(2,1)} %get-tuple-element.50), channel_id=1, source_target_pairs={{0,2},{1,3},{2,0},{3,1},{4,6},{5,7},{6,4},{7,5},{8,10},{9,11},{10,... | collective-permute-start | bytes 1572872 | tf_op jit(solution)/shard_map/ppermute | solution.py:29
  150.6 111.7 %collective-permute-start.5 = (bf16[2,128,1024]{2,1,0:T(8,128)(2,1)}, bf16[2,128,1024]{2,1,0:T(8,128)(2,1)S(1)}, u32[]{:S(2)}, u32[]{:S(2)}) collective-permute-start(bf16[2,128,1024]{2,1,0:T(8,128)(2,1)} %get-tuple-element.51), channel_id=1, source_target_pairs={{0,3},{1,2},{2,1},{3,0},{4,7},{5,6},{6,5},{7,4},{8,11},{9,10},{10,... | collective-permute-start | bytes 1572872 | tf_op jit(solution)/shard_map/ppermute | solution.py:29
  235.9 73.1 %collective-permute-start.14 = (bf16[2,128,1024]{2,1,0:T(8,128)(2,1)}, bf16[2,128,1024]{2,1,0:T(8,128)(2,1)S(1)}, u32[]{:S(2)}, u32[]{:S(2)}) collective-permute-start(bf16[2,128,1024]{2,1,0:T(8,128)(2,1)} %get-tuple-element.70), channel_id=1, source_target_pairs={{0,24},{4,28},{8,16},{12,20},{24,0},{28,4},{16,8},{20,12},{1,25},{... | collective-permute-start | bytes 1572872 | tf_op jit(solution)/shard_map/ppermute | solution.py:309
  263.3 45.8 %collective-permute-start.15 = (bf16[2,128,1024]{2,1,0:T(8,128)(2,1)}, bf16[2,128,1024]{2,1,0:T(8,128)(2,1)S(1)}, u32[]{:S(2)}, u32[]{:S(2)}) collective-permute-start(bf16[2,128,1024]{2,1,0:T(8,128)(2,1)} %get-tuple-element.72), channel_id=1, source_target_pairs={{0,28},{4,16},{8,20},{12,24},{28,0},{16,4},{20,8},{24,12},{1,29},{... | collective-permute-start | bytes 1572872 | tf_op jit(solution)/shard_map/ppermute | solution.py:309
  263.3 45.8 %all-to-all-start.3 = ((bf16[4,2,128,1024]{3,2,1,0:T(8,128)(2,1)}), bf16[4,2,128,1024]{3,2,1,0:T(8,128)(2,1)S(1)}, u32[]{:S(2)}, u32[]{:S(2)}) async-start(bf16[4,2,128,1024]{3,2,1,0:T(8,128)(2,1)} %get-tuple-element.82), calls=%async_computation.3 | async-start | bytes 4194304 | tf_op jit(solution)/shard_map/all_to_all | solution.py:41
  268.9 1.0 copy-start.20
  270.0 1.0 copy-start.22
  271.0 1.0 copy-start.24
  272.0 1.0 copy-start.26
  309.1 1.0 copy-start.18
  310.0 96.9 %all-to-all-start.2 = ((bf16[4,2,128,1024]{3,2,1,0:T(8,128)(2,1)}), bf16[4,2,128,1024]{3,2,1,0:T(8,128)(2,1)}, u32[]{:S(2)}, u32[]{:S(2)}) async-start(bf16[4,2,128,1024]{3,2,1,0:T(8,128)(2,1)} %get-tuple-element.73), calls=%async_computation.2 | async-start | bytes 4194304 | tf_op jit(solution)/shard_map/all_to_all | solution.py:41
  314.5 14.9 %collective-permute-start.17 = (bf16[2,128,1024]{2,1,0:T(8,128)(2,1)}, bf16[2,128,1024]{2,1,0:T(8,128)(2,1)S(1)}, u32[]{:S(2)}, u32[]{:S(2)}) collective-permute-start(bf16[2,128,1024]{2,1,0:T(8,128)(2,1)} %get-tuple-element.77), channel_id=1, source_target_pairs={{0,20},{4,24},{8,28},{12,16},{20,0},{24,4},{28,8},{16,12},{1,21},{... | collective-permute-start | bytes 1572872 | tf_op jit(solution)/shard_map/ppermute | solution.py:309
  314.6 47.2 %collective-permute-start.16 = (bf16[2,128,1024]{2,1,0:T(8,128)(2,1)}, bf16[2,128,1024]{2,1,0:T(8,128)(2,1)S(1)}, u32[]{:S(2)}, u32[]{:S(2)}) collective-permute-start(bf16[2,128,1024]{2,1,0:T(8,128)(2,1)} %get-tuple-element.75), channel_id=1, source_target_pairs={{0,16},{4,20},{8,24},{12,28},{16,0},{20,4},{24,8},{28,12},{1,17},{... | collective-permute-start | bytes 1572872 | tf_op jit(solution)/shard_map/ppermute | solution.py:309
  317.2 44.9 %collective-permute-start.11 = (bf16[2,128,1024]{2,1,0:T(8,128)(2,1)}, bf16[2,128,1024]{2,1,0:T(8,128)(2,1)}, u32[]{:S(2)}, u32[]{:S(2)}) collective-permute-start(bf16[2,128,1024]{2,1,0:T(8,128)(2,1)} %get-tuple-element.62), channel_id=1, source_target_pairs={{0,1},{1,0},{2,3},{3,2},{4,5},{5,4},{6,7},{7,6},{8,9},{9,8},{10,11... | collective-permute-start | bytes 1572872 | tf_op jit(solution)/shard_map/ppermute | solution.py:29
  317.4 44.7 %collective-permute-start.12 = (bf16[2,128,1024]{2,1,0:T(8,128)(2,1)}, bf16[2,128,1024]{2,1,0:T(8,128)(2,1)}, u32[]{:S(2)}, u32[]{:S(2)}) collective-permute-start(bf16[2,128,1024]{2,1,0:T(8,128)(2,1)} %get-tuple-element.63), channel_id=1, source_target_pairs={{0,2},{1,3},{2,0},{3,1},{4,6},{5,7},{6,4},{7,5},{8,10},{9,11},{10,... | collective-permute-start | bytes 1572872 | tf_op jit(solution)/shard_map/ppermute | solution.py:29
  317.6 44.5 %collective-permute-start.13 = (bf16[2,128,1024]{2,1,0:T(8,128)(2,1)}, bf16[2,128,1024]{2,1,0:T(8,128)(2,1)}, u32[]{:S(2)}, u32[]{:S(2)}) collective-permute-start(bf16[2,128,1024]{2,1,0:T(8,128)(2,1)} %get-tuple-element.64), channel_id=1, source_target_pairs={{0,3},{1,2},{2,1},{3,0},{4,7},{5,6},{6,5},{7,4},{8,11},{9,10},{10,... | collective-permute-start | bytes 1572872 | tf_op jit(solution)/shard_map/ppermute | solution.py:29
  329.4 64.6 %collective-permute-start.19 = (bf16[2,128,1024]{2,1,0:T(8,128)(2,1)}, bf16[2,128,1024]{2,1,0:T(8,128)(2,1)}, u32[]{:S(2)}, u32[]{:S(2)}) collective-permute-start(bf16[2,128,1024]{2,1,0:T(8,128)(2,1)} %get-tuple-element.81), channel_id=1, source_target_pairs={{0,28},{4,16},{8,20},{12,24},{28,0},{16,4},{20,8},{24,12},{1,29},{... | collective-permute-start | bytes 1572872 | tf_op jit(solution)/shard_map/ppermute | solution.py:309
  361.7 45.2 %collective-permute-start.18 = (bf16[2,128,1024]{2,1,0:T(8,128)(2,1)}, bf16[2,128,1024]{2,1,0:T(8,128)(2,1)}, u32[]{:S(2)}, u32[]{:S(2)}) collective-permute-start(bf16[2,128,1024]{2,1,0:T(8,128)(2,1)} %get-tuple-element.79), channel_id=1, source_target_pairs={{0,24},{4,28},{8,16},{12,20},{24,0},{28,4},{16,8},{20,12},{1,25},{... | collective-permute-start | bytes 1572872 | tf_op jit(solution)/shard_map/ppermute | solution.py:309
  362.1 1.0 copy-start.4
  363.1 1.0 copy-start.6
  364.2 1.0 copy-start.8
  365.2 1.0 copy-start.10
  366.3 1.0 copy-start.11
  367.3 3.7 copy-start.13
  367.3 3.7 copy-start.15
  367.3 3.7 copy-start.17
  367.3 3.7 copy-start.19
  (8 other events, 6.5 us)

commit v11 on v10

--- a/solution.py
+++ b/solution.py
@@ -1,4 +1,5 @@
 import functools
+import math
 
 import jax
 import jax.numpy as jnp
@@ -10,7 +11,6 @@
 DH = 128
 BLOCK = 64
 NBLEN = 128
-CHUNKS = 2
 DEPTH = 2
 ATTEND_WEIGHT = 24
 F32 = jnp.float32
@@ -274,11 +274,11 @@
     out_ref[...] = acc[...].astype(BF16)
 
 
-def owner_sum(h, send_lists, near, far, shape, so_far):
+def owner_sum(first, send_lists, near, far, shape, so_far):
     half = len(far)
     chunk = near.shape[-1]
-    wide = min(chunk, 256)
-    steps = chunk // wide
+    wide = math.gcd(math.gcd(first, chunk), 256)
+    skip, steps = first // wide, chunk // wide
     extra = [] if so_far is None else [so_far]
     return pl.pallas_call(
         functools.partial(owner_kernel, 2 * half),
@@ -287,7 +287,7 @@
         + [pl.BlockSpec((2, NBLEN, wide), lambda i: (0, 0, i))] * half
         + [ANYWHERE] * len(extra),
         out_specs=pl.BlockSpec(
-            (shape[0], 2, NBLEN, wide), lambda i: (0, 0, 0, h * steps + i)
+            (shape[0], 2, NBLEN, wide), lambda i: (0, 0, 0, skip + i)
         ),
         scratch_shapes=[pltpu.VMEM((shape[0], 2, NBLEN, wide), F32)],
         out_shape=in_hbm(shape),
@@ -313,23 +313,24 @@
 
 def local(seqs, parts, queries, kv_pool, send_lists, block_slots, grad_context):
     width = kv_pool.shape[-1]
-    chunks = min(CHUNKS, width // DH)
-    chunk = width // chunks
-    firsts = [h * chunk for h in range(chunks)]
+    heads = width // DH
+    cut = (5 * heads // 8) * DH
+    bounds = [(0, cut), (cut, width - cut)]
+    firsts = [first for first, _ in bounds]
 
     arrived, rows = [], []
-    for first in firsts:
+    for first, chunk in bounds:
         picked = pick(first, chunk, send_lists, kv_pool)
         send_lists, queries = after((send_lists, queries), picked)
         if rows:
             picked = after(picked, rows)
         arrived.append(swap_pool(picked))
         if not rows:
-            for start in firsts:
-                packed = pack(start, chunk, queries, grad_context, width, parts)
+            for start, size in bounds:
+                packed = pack(start, size, queries, grad_context, width, parts)
                 rows.append(swap_rows(packed))
     done, returns, token_parts = [], [], []
-    for h in range(chunks):
+    for h in range(2):
         rows_out, near, far = attend(block_slots, rows[h], arrived[h])
         far = swap_far(far, done)
         if h > 0:
@@ -339,8 +340,8 @@
         block_slots = after(block_slots, (token_parts[-1], far[:DEPTH]))
     context, grad_queries = unpack(token_parts, firsts, width, queries.shape)
     pool_grads = None
-    for h in range(chunks):
-        pool_grads = owner_sum(h, send_lists, *returns[h], kv_pool.shape, pool_grads)
+    for h, first in enumerate(firsts):
+        pool_grads = owner_sum(first, send_lists, *returns[h], kv_pool.shape, pool_grads)
     return (context, grad_queries, pool_grads)
 
 

time: 413 us -> 407 us (0.985)
  waiting for transfers between devices: 232 us -> 212 us
  local copies, waits for them, and re-layouts: 24.1 us -> 36.9 us
    ppermute x8, waiting for transfers between devices: 157 us -> 98.1 us  [swap_far(): got.append(lax.ppermute(piece, 'enc', pairs))]
    all_to_all x2, waiting for transfers between devices: 39.3 us -> 75.2 us  [swap_pool(): return lax.all_to_all(array, 'enc', split_axis=0, concat_axis=0, tiled=True)]
    unnamed x66 -> x80, local copies, waits for them, and re-layouts: 23.9 us -> 36.7 us
where the time goes in v11:
time: 407 us; the launch traced here: 406 us
  waiting for transfers between devices  212 us (52%)
  Pallas kernels  93.4 us (23%)
  starting transfers between devices  62.6 us (15%)
  local copies, waits for them, and re-layouts  36.9 us (9%)
    ppermute x8, waiting for transfers between devices, swap_far(): got.append(lax.ppermute(piece, 'enc', pairs))  98.1 us
    all_to_all x2, waiting for transfers between devices, swap_pool(): return lax.all_to_all(array, 'enc', split_axis=0, concat_axis=0, tiled=True)  75.2 us
    pallas_call x2, Pallas kernels, attend(): pl.pallas_call(functools.partial(attend_kernel, seqs, parts), grid=(heads...  71.6 us
    ppermute x12, waiting for transfers between devices, exchange(): return lax.ppermute(array, axis, pairs)  39 us
    unnamed x80, local copies, waits for them, and re-layouts  36.7 us
    ppermute x8, starting transfers between devices, swap_far(): got.append(lax.ppermute(piece, 'enc', pairs))  28.8 us
    all_to_all x2, starting transfers between devices, swap_pool(): return lax.all_to_all(array, 'enc', split_axis=0, concat_axis=0, tiled=True)  13 us
    all_to_all x2, starting transfers between devices, swap_near(): lax.all_to_all(array, 'enc', split_axis=0, concat_axis=0, axis_index_grou...  12.1 us
  transfers between devices with their start and end apart: 24, of which 11 were waited for; matrix products, arithmetic and copies ran while one was open for 0% of the time, Pallas kernels for 21%

profile of v11, /device:TPU:15, one launch (start us, length us, event | category | flops | bytes accessed | tf_op | source)
XLA Modules:
  0.0 406.0 jit_solution(15934375371172637590)
XLA Ops:
  1.4 2.2 copy-done
  3.5 3.6 pick_entries.2
  7.1 5.8 %all-to-all-start = ((bf16[8,2,128,1280]{3,2,1,0:T(8,128)(2,1)}), bf16[8,2,128,1280]{3,2,1,0:T(8,128)(2,1)}, u32[]{:S(2)}, u32[]{:S(2)}) async-start(bf16[8,2,128,1280]{3,2,1,0:T(8,128)(2,1)} %pick_entries.2), calls=%async_computation | async-start | bytes 10485760 | tf_op jit(solution)/shard_map/all_to_all | solution.py:52
  12.9 1.6 copy-done.3
  14.5 1.4 pack_rows.3
  16.3 1.8 pack_rows.2
  18.1 1.3 collective-permute-start
  19.6 1.2 collective-permute-start.2
  21.0 5.7 %collective-permute-done.8.rest_1_ = bf16[2,128,768]{2,1,0:T(8,128)(2,1)S(1)} collective-permute-done((bf16[2,128,768]{2,1,0:T(8,128)(2,1)}, bf16[2,128,768]{2,1,0:T(8,128)(2,1)S(1)}, u32[]{:S(2)}, u32[]{:S(2)}) %collective-permute-start.8) | collective-permute-done | bytes 393248 | tf_op jit(solution)/shard_map/ppermute | solution.py:29
  27.8 2.2 copy-done.1
  29.9 2.7 pick_entries.3
  32.6 33.3 %collective-permute-done.9.rest_2_ = bf16[2,128,768]{2,1,0:T(8,128)(2,1)S(1)} collective-permute-done((bf16[2,128,768]{2,1,0:T(8,128)(2,1)}, bf16[2,128,768]{2,1,0:T(8,128)(2,1)S(1)}, u32[]{:S(2)}, u32[]{:S(2)}) %collective-permute-start.9) | collective-permute-done | bytes 393248 | tf_op jit(solution)/shard_map/ppermute | solution.py:29
  70.0 55.9 %all-to-all-done.rest_4_ = bf16[8,2,128,1280]{3,2,1,0:T(8,128)(2,1)} async-done(((bf16[8,2,128,1280]{3,2,1,0:T(8,128)(2,1)}), bf16[8,2,128,1280]{3,2,1,0:T(8,128)(2,1)}, u32[]{:S(2)}, u32[]{:S(2)}) %all-to-all-start) | async-done | bytes 5242912 | tf_op jit(solution)/shard_map/all_to_all | solution.py:52
  125.8 7.2 %all-to-all-start.1 = ((bf16[8,2,128,768]{3,2,1,0:T(8,128)(2,1)}), bf16[8,2,128,768]{3,2,1,0:T(8,128)(2,1)S(1)}, u32[]{:S(2)}, u32[]{:S(2)}) async-start(bf16[8,2,128,768]{3,2,1,0:T(8,128)(2,1)} %pick_entries.3), calls=%async_computation.1 | async-start | bytes 6291456 | tf_op jit(solution)/shard_map/all_to_all | solution.py:52
  133.1 1.1 copy-done.22
  134.2 1.1 copy-done.24
  135.3 1.1 copy-done.26
  136.4 1.1 copy-done.28
  137.5 44.2 %attend_blocks.2 = (bf16[2,128,1280]{2,1,0:T(8,128)(2,1)}, bf16[2,128,1280]{2,1,0:T(8,128)(2,1)}, bf16[2,128,1280]{2,1,0:T(8,128)(2,1)}, bf16[2,128,1280]{2,1,0:...) custom-call(s32[1,8,2]{2,1,0:T(8,128)S(1)} %copy.10.uses, ...), custom_call_target="tpu_custom_call" | custom-call | flops 48318382080 | bytes 15728640 | tf_op jit(solution)/shard_map/attend_blocks/pallas_call | solution.py:239
  181.7 19.3 %all-to-all-done.1.rest_4_ = bf16[8,2,128,768]{3,2,1,0:T(8,128)(2,1)S(1)} async-done(((bf16[8,2,128,768]{3,2,1,0:T(8,128)(2,1)}), bf16[8,2,128,768]{3,2,1,0:T(8,128)(2,1)S(1)}, u32[]{:S(2)}, u32[]{:S(2)}) %all-to-all-start.1) | async-done | bytes 3145760 | tf_op jit(solution)/shard_map/all_to_all | solution.py:52
  201.0 1.7 copy-done.4
  202.7 7.2 %all-to-all-start.3 = ((bf16[4,2,128,1280]{3,2,1,0:T(8,128)(2,1)}), bf16[4,2,128,1280]{3,2,1,0:T(8,128)(2,1)S(1)}, u32[]{:S(2)}, u32[]{:S(2)}) async-start(bf16[4,2,128,1280]{3,2,1,0:T(8,128)(2,1)} %get-tuple-element.82), calls=%async_computation.3 | async-start | bytes 5242880 | tf_op jit(solution)/shard_map/all_to_all | solution.py:41
  209.9 1.5 collective-permute-start.7
  211.9 2.2 collective-permute-start.5
  214.1 38.3 %collective-permute-done.6.rest_0_ = bf16[2,128,1280]{2,1,0:T(8,128)(2,1)S(1)} collective-permute-done((bf16[2,128,1280]{2,1,0:T(8,128)(2,1)}, bf16[2,128,1280]{2,1,0:T(8,128)(2,1)S(1)}, u32[]{:S(2)}, u32[]{:S(2)}) %collective-permute-start.6) | collective-permute-done | bytes 655392 | tf_op jit(solution)/shard_map/ppermute | solution.py:309
  252.4 2.2 collective-permute-start.14
  254.6 28.5 %collective-permute-done.7.rest_1_ = bf16[2,128,1280]{2,1,0:T(8,128)(2,1)S(1)} collective-permute-done((bf16[2,128,1280]{2,1,0:T(8,128)(2,1)}, bf16[2,128,1280]{2,1,0:T(8,128)(2,1)S(1)}, u32[]{:S(2)}, u32[]{:S(2)}) %collective-permute-start.7) | collective-permute-done | bytes 655392 | tf_op jit(solution)/shard_map/ppermute | solution.py:309
  286.6 1.9 copy-done.5
  292.5 27.4 %attend_blocks.3 = (bf16[2,128,768]{2,1,0:T(8,128)(2,1)}, bf16[2,128,768]{2,1,0:T(8,128)(2,1)}, bf16[2,128,768]{2,1,0:T(8,128)(2,1)}, bf16[2,128,768]{2,1,0:T(8,...) custom-call(s32[1,8,2]{2,1,0:T(8,128)S(1)} %copy.12.uses, ...), custom_call_target="tpu_custom_call" | custom-call | flops 28991029248 | bytes 9437184 | tf_op jit(solution)/shard_map/attend_blocks/pallas_call | solution.py:239
  319.9 3.1 collective-permute-done.15.rest_3_
  323.9 4.9 %all-to-all-start.2 = ((bf16[4,2,128,768]{3,2,1,0:T(8,128)(2,1)}), bf16[4,2,128,768]{3,2,1,0:T(8,128)(2,1)}, u32[]{:S(2)}, u32[]{:S(2)}) async-start(bf16[4,2,128,768]{3,2,1,0:T(8,128)(2,1)} %get-tuple-element.73), calls=%async_computation.2 | async-start | bytes 3145728 | tf_op jit(solution)/shard_map/all_to_all | solution.py:41
  328.8 1.2 collective-permute-start.17
  330.0 2.5 collective-permute-start.16
  333.0 2.2 collective-permute-start.13
  335.1 5.6 %collective-permute-done.17.rest_1_ = bf16[2,128,768]{2,1,0:T(8,128)(2,1)S(1)} collective-permute-done((bf16[2,128,768]{2,1,0:T(8,128)(2,1)}, bf16[2,128,768]{2,1,0:T(8,128)(2,1)S(1)}, u32[]{:S(2)}, u32[]{:S(2)}) %collective-permute-start.17) | collective-permute-done | bytes 393248 | tf_op jit(solution)/shard_map/ppermute | solution.py:309
  341.5 19.6 %collective-permute-start.19 = (bf16[2,128,768]{2,1,0:T(8,128)(2,1)}, bf16[2,128,768]{2,1,0:T(8,128)(2,1)}, u32[]{:S(2)}, u32[]{:S(2)}) collective-permute-start(bf16[2,128,768]{2,1,0:T(8,128)(2,1)} %get-tuple-element.81), channel_id=1, source_target_pairs={{0,28},{4,16},{8,20},{12,24},{28,0},{16,4},{20,8},{24,12},{1,29},{... | collective-permute-start | bytes 1179656 | tf_op jit(solution)/shard_map/ppermute | solution.py:309
  361.1 4.6 %collective-permute-done.16.rest_0_ = bf16[2,128,768]{2,1,0:T(8,128)(2,1)S(1)} collective-permute-done((bf16[2,128,768]{2,1,0:T(8,128)(2,1)}, bf16[2,128,768]{2,1,0:T(8,128)(2,1)S(1)}, u32[]{:S(2)}, u32[]{:S(2)}) %collective-permute-start.16) | collective-permute-done | bytes 393248 | tf_op jit(solution)/shard_map/ppermute | solution.py:309
  366.4 1.6 collective-permute-start.18
  368.2 1.2 copy-done.10
  369.4 1.1 copy-done.12
  370.5 1.1 copy-done.14
  371.6 1.1 copy-done.16
  373.6 3.4 unpack_rows.1
  377.0 4.9 %owner_sum.2.rest_4_ = bf16[4,2,128,2048]{3,2,1,0:T(8,128)(2,1)} custom-call(s32[1,8,1]{2,1,0:T(8,128)S(1)} %copy.14.lists, bf16[4,2,128,1280]{3,2,1,0:T(8,128)(2,1)S(1)} %all-to-all-done.3.near_ref, bf16[2,128,1280]{2,1,0:T(8,128)(2,1)S(1)} %collective-permute-done.6.rest_0_, bf16[2,128,1280]{2,1,0:T(8,128)(2,1)S(1)} %copy-done.7, ...), custom_call_target="tpu_custom_call" | custom-call | flops 2621440 | bytes 7864320 | tf_op jit(solution)/shard_map/owner_sum/pallas_call | solution.py:283
  382.0 2.5 collective-permute-done.19.rest_3_
  384.5 15.5 %collective-permute-done.18.rest_2_ = bf16[2,128,768]{2,1,0:T(8,128)(2,1)} collective-permute-done((bf16[2,128,768]{2,1,0:T(8,128)(2,1)}, bf16[2,128,768]{2,1,0:T(8,128)(2,1)}, u32[]{:S(2)}, u32[]{:S(2)}) %collective-permute-start.18) | collective-permute-done | bytes 393248 | tf_op jit(solution)/shard_map/ppermute | solution.py:309
  400.0 1.0 copy-done.19
  402.0 4.0 owner_sum.3
  (92 shorter events, 19.6 us)
Async XLA Ops:
  1.4 2.2 copy-start
  7.1 5.8 %copy-start.2 = (bf16[1,128,8192]{2,1,0:T(8,128)(2,1)S(1)}, bf16[1,128,8192]{2,1,0:T(8,128)(2,1)}, u32[]{:S(2)}) copy-start(bf16[1,128,8192]{2,1,0:T(8,128)(2,1)} %q_ref.1) | copy-start | bytes 6291460
  7.1 118.7 %all-to-all-start = ((bf16[8,2,128,1280]{3,2,1,0:T(8,128)(2,1)}), bf16[8,2,128,1280]{3,2,1,0:T(8,128)(2,1)}, u32[]{:S(2)}, u32[]{:S(2)}) async-start(bf16[8,2,128,1280]{3,2,1,0:T(8,128)(2,1)} %pick_entries.2), calls=%async_computation | async-start | bytes 10485760 | tf_op jit(solution)/shard_map/all_to_all | solution.py:52
  12.9 1.6 copy-start.3
  16.0 11.5 %copy-start.38 = (bf16[2,128,768]{2,1,0:T(8,128)(2,1)S(1)}, bf16[2,128,768]{2,1,0:T(8,128)(2,1)}, u32[]{:S(2)}) copy-start(bf16[2,128,768]{2,1,0:T(8,128)(2,1)} %get-tuple-element.58) | copy-start | bytes 1179652
  16.0 11.7 %copy-start.36 = (s32[1,8,1]{1,2,0:T(1,128)S(1)}, s32[1,8,1]{1,2,0:T(1,128)}, u32[]{:S(2)}) copy-start(s32[1,8,1]{1,2,0:T(1,128)} %param.7) | copy-start | bytes 100
  16.0 10.7 %collective-permute-start.8 = (bf16[2,128,768]{2,1,0:T(8,128)(2,1)}, bf16[2,128,768]{2,1,0:T(8,128)(2,1)S(1)}, u32[]{:S(2)}, u32[]{:S(2)}) collective-permute-start(bf16[2,128,768]{2,1,0:T(8,128)(2,1)} %get-tuple-element.56), channel_id=1, source_target_pairs={{0,1},{1,0},{2,3},{3,2},{4,5},{5,4},{6,7},{7,6},{8,9},{9,8},{10,11... | collective-permute-start | bytes 1179656 | tf_op jit(solution)/shard_map/ppermute | solution.py:29
  18.1 49.3 %collective-permute-start = (bf16[2,128,1280]{2,1,0:T(8,128)(2,1)}, bf16[2,128,1280]{2,1,0:T(8,128)(2,1)S(1)}, u32[]{:S(2)}, u32[]{:S(2)}) collective-permute-start(bf16[2,128,1280]{2,1,0:T(8,128)(2,1)} %get-tuple-element.45), channel_id=1, source_target_pairs={{0,1},{1,0},{2,3},{3,2},{4,5},{5,4},{6,7},{7,6},{8,9},{9,8},{10,11... | collective-permute-start | bytes 1966088 | tf_op jit(solution)/shard_map/ppermute | solution.py:29
  19.4 48.9 %collective-permute-start.1 = (bf16[2,128,1280]{2,1,0:T(8,128)(2,1)}, bf16[2,128,1280]{2,1,0:T(8,128)(2,1)S(1)}, u32[]{:S(2)}, u32[]{:S(2)}) collective-permute-start(bf16[2,128,1280]{2,1,0:T(8,128)(2,1)} %get-tuple-element.46), channel_id=1, source_target_pairs={{0,2},{1,3},{2,0},{3,1},{4,6},{5,7},{6,4},{7,5},{8,10},{9,11},{10,... | collective-permute-start | bytes 1966088 | tf_op jit(solution)/shard_map/ppermute | solution.py:29
  19.6 49.5 %collective-permute-start.2 = (bf16[2,128,1280]{2,1,0:T(8,128)(2,1)}, bf16[2,128,1280]{2,1,0:T(8,128)(2,1)S(1)}, u32[]{:S(2)}, u32[]{:S(2)}) collective-permute-start(bf16[2,128,1280]{2,1,0:T(8,128)(2,1)} %get-tuple-element.47), channel_id=1, source_target_pairs={{0,3},{1,2},{2,1},{3,0},{4,7},{5,6},{6,5},{7,4},{8,11},{9,10},{10,... | collective-permute-start | bytes 1966088 | tf_op jit(solution)/shard_map/ppermute | solution.py:29
  20.8 45.1 %collective-permute-start.9 = (bf16[2,128,768]{2,1,0:T(8,128)(2,1)}, bf16[2,128,768]{2,1,0:T(8,128)(2,1)S(1)}, u32[]{:S(2)}, u32[]{:S(2)}) collective-permute-start(bf16[2,128,768]{2,1,0:T(8,128)(2,1)} %get-tuple-element.57), channel_id=1, source_target_pairs={{0,2},{1,3},{2,0},{3,1},{4,6},{5,7},{6,4},{7,5},{8,10},{9,11},{10,... | collective-permute-start | bytes 1179656 | tf_op jit(solution)/shard_map/ppermute | solution.py:29
  27.5 39.2 %collective-permute-start.10 = (bf16[2,128,768]{2,1,0:T(8,128)(2,1)S(1)}, bf16[2,128,768]{2,1,0:T(8,128)(2,1)S(1)}, u32[]{:S(2)}, u32[]{:S(2)}) collective-permute-start(bf16[2,128,768]{2,1,0:T(8,128)(2,1)S(1)} %copy-done.38), channel_id=1, source_target_pairs={{0,3},{1,2},{2,1},{3,0},{4,7},{5,6},{6,5},{7,4},{8,11},{9,10},{10,... | collective-permute-start | bytes 1179656 | tf_op jit(solution)/shard_map/ppermute | solution.py:29
  27.8 2.2 copy-start.1
  70.0 63.1 %copy-start.37 = (s32[1,8,2]{1,2,0:T(2,128)S(1)}, s32[1,8,2]{1,2,0:T(2,128)}, u32[]{:S(2)}) copy-start(s32[1,8,2]{1,2,0:T(2,128)} %param.8) | copy-start | bytes 196
  125.8 75.2 %all-to-all-start.1 = ((bf16[8,2,128,768]{3,2,1,0:T(8,128)(2,1)}), bf16[8,2,128,768]{3,2,1,0:T(8,128)(2,1)S(1)}, u32[]{:S(2)}, u32[]{:S(2)}) async-start(bf16[8,2,128,768]{3,2,1,0:T(8,128)(2,1)} %pick_entries.3), calls=%async_computation.1 | async-start | bytes 6291456 | tf_op jit(solution)/shard_map/all_to_all | solution.py:52
  133.1 1.1 copy-start.22
  134.2 1.1 copy-start.24
  135.3 1.1 copy-start.26
  136.4 1.1 copy-start.28
  201.0 1.7 copy-start.4
  202.7 121.2 %all-to-all-start.3 = ((bf16[4,2,128,1280]{3,2,1,0:T(8,128)(2,1)}), bf16[4,2,128,1280]{3,2,1,0:T(8,128)(2,1)S(1)}, u32[]{:S(2)}, u32[]{:S(2)}) async-start(bf16[4,2,128,1280]{3,2,1,0:T(8,128)(2,1)} %get-tuple-element.82), calls=%async_computation.3 | async-start | bytes 5242880 | tf_op jit(solution)/shard_map/all_to_all | solution.py:41
  209.9 42.5 %collective-permute-start.6 = (bf16[2,128,1280]{2,1,0:T(8,128)(2,1)}, bf16[2,128,1280]{2,1,0:T(8,128)(2,1)S(1)}, u32[]{:S(2)}, u32[]{:S(2)}) collective-permute-start(bf16[2,128,1280]{2,1,0:T(8,128)(2,1)} %get-tuple-element.52), channel_id=1, source_target_pairs={{0,16},{4,20},{8,24},{12,28},{16,0},{20,4},{24,8},{28,12},{1,17},{... | collective-permute-start | bytes 1966088 | tf_op jit(solution)/shard_map/ppermute | solution.py:309
  209.9 73.2 %collective-permute-start.7 = (bf16[2,128,1280]{2,1,0:T(8,128)(2,1)}, bf16[2,128,1280]{2,1,0:T(8,128)(2,1)S(1)}, u32[]{:S(2)}, u32[]{:S(2)}) collective-permute-start(bf16[2,128,1280]{2,1,0:T(8,128)(2,1)} %get-tuple-element.53), channel_id=1, source_target_pairs={{0,20},{4,24},{8,28},{12,16},{20,0},{24,4},{28,8},{16,12},{1,21},{... | collective-permute-start | bytes 1966088 | tf_op jit(solution)/shard_map/ppermute | solution.py:309
  211.4 72.5 %collective-permute-start.3 = (bf16[2,128,1280]{2,1,0:T(8,128)(2,1)}, bf16[2,128,1280]{2,1,0:T(8,128)(2,1)S(1)}, u32[]{:S(2)}, u32[]{:S(2)}) collective-permute-start(bf16[2,128,1280]{2,1,0:T(8,128)(2,1)} %get-tuple-element.49), channel_id=1, source_target_pairs={{0,1},{1,0},{2,3},{3,2},{4,5},{5,4},{6,7},{7,6},{8,9},{9,8},{10,11... | collective-permute-start | bytes 1966088 | tf_op jit(solution)/shard_map/ppermute | solution.py:29
  211.7 73.1 %collective-permute-start.4 = (bf16[2,128,1280]{2,1,0:T(8,128)(2,1)}, bf16[2,128,1280]{2,1,0:T(8,128)(2,1)S(1)}, u32[]{:S(2)}, u32[]{:S(2)}) collective-permute-start(bf16[2,128,1280]{2,1,0:T(8,128)(2,1)} %get-tuple-element.50), channel_id=1, source_target_pairs={{0,2},{1,3},{2,0},{3,1},{4,6},{5,7},{6,4},{7,5},{8,10},{9,11},{10,... | collective-permute-start | bytes 1966088 | tf_op jit(solution)/shard_map/ppermute | solution.py:29
  211.9 73.8 %collective-permute-start.5 = (bf16[2,128,1280]{2,1,0:T(8,128)(2,1)}, bf16[2,128,1280]{2,1,0:T(8,128)(2,1)S(1)}, u32[]{:S(2)}, u32[]{:S(2)}) collective-permute-start(bf16[2,128,1280]{2,1,0:T(8,128)(2,1)} %get-tuple-element.51), channel_id=1, source_target_pairs={{0,3},{1,2},{2,1},{3,0},{4,7},{5,6},{6,5},{7,4},{8,11},{9,10},{10,... | collective-permute-start | bytes 1966088 | tf_op jit(solution)/shard_map/ppermute | solution.py:29
  252.4 67.5 %collective-permute-start.14 = (bf16[2,128,1280]{2,1,0:T(8,128)(2,1)}, bf16[2,128,1280]{2,1,0:T(8,128)(2,1)}, u32[]{:S(2)}, u32[]{:S(2)}) collective-permute-start(bf16[2,128,1280]{2,1,0:T(8,128)(2,1)} %get-tuple-element.70), channel_id=1, source_target_pairs={{0,24},{4,28},{8,16},{12,20},{24,0},{28,4},{16,8},{20,12},{1,25},{... | collective-permute-start | bytes 1966088 | tf_op jit(solution)/shard_map/ppermute | solution.py:309
  286.6 36.4 %collective-permute-start.15 = (bf16[2,128,1280]{2,1,0:T(8,128)(2,1)}, bf16[2,128,1280]{2,1,0:T(8,128)(2,1)S(1)}, u32[]{:S(2)}, u32[]{:S(2)}) collective-permute-start(bf16[2,128,1280]{2,1,0:T(8,128)(2,1)} %get-tuple-element.72), channel_id=1, source_target_pairs={{0,28},{4,16},{8,20},{12,24},{28,0},{16,4},{20,8},{24,12},{1,29},{... | collective-permute-start | bytes 1966088 | tf_op jit(solution)/shard_map/ppermute | solution.py:309
  286.6 1.9 copy-start.5
  288.5 1.0 copy-start.29
  289.5 1.0 copy-start.31
  290.5 1.0 copy-start.33
  291.5 1.0 copy-start.35
  323.9 76.1 %all-to-all-start.2 = ((bf16[4,2,128,768]{3,2,1,0:T(8,128)(2,1)}), bf16[4,2,128,768]{3,2,1,0:T(8,128)(2,1)}, u32[]{:S(2)}, u32[]{:S(2)}) async-start(bf16[4,2,128,768]{3,2,1,0:T(8,128)(2,1)} %get-tuple-element.73), calls=%async_computation.2 | async-start | bytes 3145728 | tf_op jit(solution)/shard_map/all_to_all | solution.py:41
  328.8 12.0 %collective-permute-start.17 = (bf16[2,128,768]{2,1,0:T(8,128)(2,1)}, bf16[2,128,768]{2,1,0:T(8,128)(2,1)S(1)}, u32[]{:S(2)}, u32[]{:S(2)}) collective-permute-start(bf16[2,128,768]{2,1,0:T(8,128)(2,1)} %get-tuple-element.77), channel_id=1, source_target_pairs={{0,20},{4,24},{8,28},{12,16},{20,0},{24,4},{28,8},{16,12},{1,21},{... | collective-permute-start | bytes 1179656 | tf_op jit(solution)/shard_map/ppermute | solution.py:309
  330.0 35.7 %collective-permute-start.16 = (bf16[2,128,768]{2,1,0:T(8,128)(2,1)}, bf16[2,128,768]{2,1,0:T(8,128)(2,1)S(1)}, u32[]{:S(2)}, u32[]{:S(2)}) collective-permute-start(bf16[2,128,768]{2,1,0:T(8,128)(2,1)} %get-tuple-element.75), channel_id=1, source_target_pairs={{0,16},{4,20},{8,24},{12,28},{16,0},{20,4},{24,8},{28,12},{1,17},{... | collective-permute-start | bytes 1179656 | tf_op jit(solution)/shard_map/ppermute | solution.py:309
  332.5 35.7 %collective-permute-start.11 = (bf16[2,128,768]{2,1,0:T(8,128)(2,1)}, bf16[2,128,768]{2,1,0:T(8,128)(2,1)}, u32[]{:S(2)}, u32[]{:S(2)}) collective-permute-start(bf16[2,128,768]{2,1,0:T(8,128)(2,1)} %get-tuple-element.62), channel_id=1, source_target_pairs={{0,1},{1,0},{2,3},{3,2},{4,5},{5,4},{6,7},{7,6},{8,9},{9,8},{10,11... | collective-permute-start | bytes 1179656 | tf_op jit(solution)/shard_map/ppermute | solution.py:29
  332.7 35.4 %collective-permute-start.12 = (bf16[2,128,768]{2,1,0:T(8,128)(2,1)}, bf16[2,128,768]{2,1,0:T(8,128)(2,1)}, u32[]{:S(2)}, u32[]{:S(2)}) collective-permute-start(bf16[2,128,768]{2,1,0:T(8,128)(2,1)} %get-tuple-element.63), channel_id=1, source_target_pairs={{0,2},{1,3},{2,0},{3,1},{4,6},{5,7},{6,4},{7,5},{8,10},{9,11},{10,... | collective-permute-start | bytes 1179656 | tf_op jit(solution)/shard_map/ppermute | solution.py:29
  333.0 35.2 %collective-permute-start.13 = (bf16[2,128,768]{2,1,0:T(8,128)(2,1)}, bf16[2,128,768]{2,1,0:T(8,128)(2,1)}, u32[]{:S(2)}, u32[]{:S(2)}) collective-permute-start(bf16[2,128,768]{2,1,0:T(8,128)(2,1)} %get-tuple-element.64), channel_id=1, source_target_pairs={{0,3},{1,2},{2,1},{3,0},{4,7},{5,6},{6,5},{7,4},{8,11},{9,10},{10,... | collective-permute-start | bytes 1179656 | tf_op jit(solution)/shard_map/ppermute | solution.py:29
  341.5 43.0 %collective-permute-start.19 = (bf16[2,128,768]{2,1,0:T(8,128)(2,1)}, bf16[2,128,768]{2,1,0:T(8,128)(2,1)}, u32[]{:S(2)}, u32[]{:S(2)}) collective-permute-start(bf16[2,128,768]{2,1,0:T(8,128)(2,1)} %get-tuple-element.81), channel_id=1, source_target_pairs={{0,28},{4,16},{8,20},{12,24},{28,0},{16,4},{20,8},{24,12},{1,29},{... | collective-permute-start | bytes 1179656 | tf_op jit(solution)/shard_map/ppermute | solution.py:309
  366.4 33.5 %collective-permute-start.18 = (bf16[2,128,768]{2,1,0:T(8,128)(2,1)}, bf16[2,128,768]{2,1,0:T(8,128)(2,1)}, u32[]{:S(2)}, u32[]{:S(2)}) collective-permute-start(bf16[2,128,768]{2,1,0:T(8,128)(2,1)} %get-tuple-element.79), channel_id=1, source_target_pairs={{0,24},{4,28},{8,16},{12,20},{24,0},{28,4},{16,8},{20,12},{1,25},{... | collective-permute-start | bytes 1179656 | tf_op jit(solution)/shard_map/ppermute | solution.py:309
  368.2 8.8 %copy-start.7 = (bf16[2,128,1280]{2,1,0:T(8,128)(2,1)S(1)}, bf16[2,128,1280]{2,1,0:T(8,128)(2,1)}, u32[]{:S(2)}) copy-start(bf16[2,128,1280]{2,1,0:T(8,128)(2,1)} %copy-done.6) | copy-start | bytes 1966084
  368.2 8.9 %copy-start.9 = (bf16[2,128,1280]{2,1,0:T(8,128)(2,1)S(1)}, bf16[2,128,1280]{2,1,0:T(8,128)(2,1)}, u32[]{:S(2)}) copy-start(bf16[2,128,1280]{2,1,0:T(8,128)(2,1)} %copy-done.8) | copy-start | bytes 1966084
  368.2 1.2 copy-start.10
  369.4 1.1 copy-start.12
  370.5 1.1 copy-start.14
  371.6 1.1 copy-start.16
  400.0 1.0 copy-start.19
  (15 other events, 12.6 us)

commit v12 on v10

--- a/solution.py
+++ b/solution.py
@@ -15,6 +15,7 @@
 ATTEND_WEIGHT = 24
 F32 = jnp.float32
 BF16 = jnp.bfloat16
+LOG2E = 1.4426950408889634
 VMEM_BYTES = 40 * 1024 * 1024
 
 
@@ -153,7 +154,7 @@
         compiler_params=PARAMS,
         cost_estimate=cost(8 * shape[0] * NBLEN * chunk),
         name="pick_entries",
-    )(send_lists, kv_pool)
+    )(send_lists, pltpu.with_memory_space_constraint(kv_pool, pltpu.HBM))
 
 
 def dot(left, right, left_dim, right_dim):
@@ -179,38 +180,42 @@
     sums[...] = jnp.zeros_like(sums)
     first_row = lax.broadcasted_iota(jnp.int32, (BLOCK, DH), 0) == 0
 
-    def one_block(block, q, g):
-        first, second = uses[0, block, 0], uses[0, block, 1]
-        keys = jnp.concatenate([held[first, 0], held[second, 0]], axis=0)
-        values = jnp.concatenate([held[first, 1], held[second, 1]], axis=0)
-        scores = dot(q, keys, 1, 1) * scale
-        weights = jnp.exp(scores - jnp.max(scores, axis=1, keepdims=True))
-        probs = weights / jnp.sum(weights, axis=1, keepdims=True)
-        probs_low = probs.astype(BF16)
-        out = dot(probs_low, values, 1, 0)
-        grad_probs = dot(g, values, 1, 1)
-        inner = jnp.sum(probs * grad_probs, axis=1, keepdims=True)
-        grad_scores = (probs * (grad_probs - inner) * scale).astype(BF16)
-        grad_q = dot(grad_scores, keys, 1, 0)
-        grad_keys = dot(grad_scores, q, 0, 0)
-        grad_values = dot(probs_low, g, 0, 0)
-        sums[first, 0] += grad_keys[:NBLEN]
-        sums[second, 0] += grad_keys[NBLEN:]
-        sums[first, 1] += grad_values[:NBLEN]
-        sums[second, 1] += grad_values[NBLEN:]
+    def blocks_of(first, qs, gs):
+        several = range(len(qs))
+        slots = [(uses[0, first + n, 0], uses[0, first + n, 1]) for n in several]
+        keys = [jnp.concatenate([held[a, 0], held[b, 0]], axis=0) for a, b in slots]
+        values = [jnp.concatenate([held[a, 1], held[b, 1]], axis=0) for a, b in slots]
+        scores = [dot(qs[n], keys[n], 1, 1) for n in several]
+        grad_probs = [dot(gs[n], values[n], 1, 1) for n in several]
+        peaks = [jnp.max(scores[n], axis=1, keepdims=True) for n in several]
+        weights = [jnp.exp2((scores[n] - peaks[n]) * (scale * LOG2E)) for n in several]
+        shares = [1.0 / jnp.sum(weights[n], axis=1, keepdims=True) for n in several]
+        probs = [weights[n] * shares[n] for n in several]
+        probs_low = [probs[n].astype(BF16) for n in several]
+        inner = [jnp.sum(probs[n] * grad_probs[n], axis=1, keepdims=True) for n in several]
+        out = [dot(probs_low[n], values[n], 1, 0) for n in several]
+        grad_values = [dot(probs_low[n], gs[n], 0, 0) for n in several]
+        grad_scores = [
+            (probs[n] * ((grad_probs[n] - inner[n]) * scale)).astype(BF16) for n in several
+        ]
+        grad_q = [dot(grad_scores[n], keys[n], 1, 0) for n in several]
+        grad_keys = [dot(grad_scores[n], qs[n], 0, 0) for n in several]
+        for n, (a, b) in enumerate(slots):
+            sums[a, 0] += grad_keys[n][:NBLEN]
+            sums[b, 0] += grad_keys[n][NBLEN:]
+            sums[a, 1] += grad_values[n][:NBLEN]
+            sums[b, 1] += grad_values[n][NBLEN:]
         return out, grad_q
 
     def one_part(part, carry):
-        q, g = (rows[part, n, BLOCK:].astype(BF16) for n in range(2))
-        for n, result in enumerate(one_block(2 * part, q, g)):
-            made[part, n, BLOCK:] = result
-        q, g = (
-            jnp.where(first_row, rows[part, n, :BLOCK], rows[part + 1, n, :BLOCK]).astype(BF16)
-            for n in range(2)
-        )
-        for n, result in enumerate(one_block(2 * part + 1, q, g)):
-            made[part + 1, n, :BLOCK] = result
-            made[part, n, :1] = result[:1]
+        inputs = []
+        for n in range(2):
+            later = jnp.where(first_row, rows[part, n, :BLOCK], rows[part + 1, n, :BLOCK])
+            inputs.append([rows[part, n, BLOCK:].astype(BF16), later.astype(BF16)])
+        for n, (even, odd) in enumerate(blocks_of(2 * part, *inputs)):
+            made[part, n, BLOCK:] = even
+            made[part + 1, n, :BLOCK] = odd
+            made[part, n, :1] = odd[:1]
         return carry
 
     if parts <= 4:

time: 413 us -> 407 us (0.985)
  Pallas kernels: 92.8 us -> 70.4 us
  starting transfers between devices: 61.4 us -> 76.3 us
  waiting for transfers between devices: 232 us -> 239 us
  local copies, waits for them, and re-layouts: 24.1 us -> 18.8 us
    pallas_call x2, Pallas kernels: 71.8 us -> 45.3 us  [attend(): pl.pallas_call(functools.partial(attend_kernel, seqs, parts), grid=(heads...]
    ppermute x8, starting transfers between devices: 28.7 us -> 40.9 us  [swap_far(): got.append(lax.ppermute(piece, 'enc', pairs))]
    all_to_all x2, waiting for transfers between devices: 0.01 us -> 5.91 us  [swap_near(): lax.all_to_all(array, 'enc', split_axis=0, concat_axis=0, axis_index_grou...]
    unnamed x66 -> x62, local copies, waits for them, and re-layouts: 23.9 us -> 18.6 us
  transfers between devices with their start and end apart: 24 -> 24, of which waited for: 11 -> 12; matrix products, arithmetic and copies ran while one was open for 0% -> 0% of each run, Pallas kernels for 21% -> 15%
where the time goes in v12:
time: 407 us; the launch traced here: 405 us
  waiting for transfers between devices  239 us (59%)
  starting transfers between devices  76.3 us (19%)
  Pallas kernels  70.4 us (17%)
  local copies, waits for them, and re-layouts  18.8 us (5%)
    ppermute x8, waiting for transfers between devices, swap_far(): got.append(lax.ppermute(piece, 'enc', pairs))  158 us
    pallas_call x2, Pallas kernels, attend(): pl.pallas_call(functools.partial(attend_kernel, seqs, parts), grid=(heads...  45.3 us
    ppermute x8, starting transfers between devices, swap_far(): got.append(lax.ppermute(piece, 'enc', pairs))  40.9 us
    all_to_all x2, waiting for transfers between devices, swap_pool(): return lax.all_to_all(array, 'enc', split_axis=0, concat_axis=0, tiled=True)  39.3 us
    ppermute x12, waiting for transfers between devices, exchange(): return lax.ppermute(array, axis, pairs)  36.1 us
    unnamed x62, local copies, waits for them, and re-layouts  18.6 us
    all_to_all x2, starting transfers between devices, swap_pool(): return lax.all_to_all(array, 'enc', split_axis=0, concat_axis=0, tiled=True)  14 us
    all_to_all x2, starting transfers between devices, swap_near(): lax.all_to_all(array, 'enc', split_axis=0, concat_axis=0, axis_index_grou...  12.7 us
  transfers between devices with their start and end apart: 24, of which 12 were waited for; matrix products, arithmetic and copies ran while one was open for 0% of the time, Pallas kernels for 15%

profile of v12, /device:TPU:15, one launch (start us, length us, event | category | flops | bytes accessed | tf_op | source)
XLA Modules:
  0.0 405.3 jit_solution(1902453040001612315)
XLA Ops:
  1.4 5.2 %pick_entries.2 = bf16[8,2,128,1024]{3,2,1,0:T(8,128)(2,1)} custom-call(s32[1,8,1]{2,1,0:T(8,128)S(1)} %copy.9.lists, bf16[4,2,128,2048]{3,2,1,0:T(8,128)(2,1)} %pool_ref.3), custom_call_target="tpu_custom_call" | custom-call | bytes 8388608 | tf_op jit(solution)/shard_map/pick_entries/pallas_call | solution.py:147
  6.6 5.9 %all-to-all-start = ((bf16[8,2,128,1024]{3,2,1,0:T(8,128)(2,1)}), bf16[8,2,128,1024]{3,2,1,0:T(8,128)(2,1)}, u32[]{:S(2)}, u32[]{:S(2)}) async-start(bf16[8,2,128,1024]{3,2,1,0:T(8,128)(2,1)} %pick_entries.2), calls=%async_computation | async-start | bytes 8388608 | tf_op jit(solution)/shard_map/all_to_all | solution.py:53
  12.4 1.6 copy-done.1
  14.0 1.6 pack_rows.3
  16.2 2.2 collective-permute-start.10
  18.4 1.6 pack_rows.2
  20.5 8.6 %collective-permute-done.8.rest_1_ = bf16[2,128,1024]{2,1,0:T(8,128)(2,1)S(1)} collective-permute-done((bf16[2,128,1024]{2,1,0:T(8,128)(2,1)}, bf16[2,128,1024]{2,1,0:T(8,128)(2,1)S(1)}, u32[]{:S(2)}, u32[]{:S(2)}) %collective-permute-start.8) | collective-permute-done | bytes 524320 | tf_op jit(solution)/shard_map/ppermute | solution.py:30
  29.1 0.8 copy-done.19
  30.2 5.1 %pick_entries.3 = bf16[8,2,128,1024]{3,2,1,0:T(8,128)(2,1)} custom-call(s32[1,8,1]{2,1,0:T(8,128)S(1)} %copy.11.lists, bf16[4,2,128,2048]{3,2,1,0:T(8,128)(2,1)} %pool_ref.3), custom_call_target="tpu_custom_call" | custom-call | bytes 8388608 | tf_op jit(solution)/shard_map/pick_entries/pallas_call | solution.py:147
  35.3 5.0 %collective-permute-done.10.rest_3_ = bf16[2,128,1024]{2,1,0:T(8,128)(2,1)S(1)} collective-permute-done((bf16[2,128,1024]{2,1,0:T(8,128)(2,1)}, bf16[2,128,1024]{2,1,0:T(8,128)(2,1)S(1)}, u32[]{:S(2)}, u32[]{:S(2)}) %collective-permute-start.10) | collective-permute-done | bytes 524320 | tf_op jit(solution)/shard_map/ppermute | solution.py:30
  40.3 11.4 %collective-permute-done.rest_1_ = bf16[2,128,1024]{2,1,0:T(8,128)(2,1)S(1)} collective-permute-done((bf16[2,128,1024]{2,1,0:T(8,128)(2,1)}, bf16[2,128,1024]{2,1,0:T(8,128)(2,1)S(1)}, u32[]{:S(2)}, u32[]{:S(2)}) %collective-permute-start) | collective-permute-done | bytes 524320 | tf_op jit(solution)/shard_map/ppermute | solution.py:30
  51.7 11.1 %collective-permute-done.2.rest_3_ = bf16[2,128,1024]{2,1,0:T(8,128)(2,1)S(1)} collective-permute-done((bf16[2,128,1024]{2,1,0:T(8,128)(2,1)}, bf16[2,128,1024]{2,1,0:T(8,128)(2,1)S(1)}, u32[]{:S(2)}, u32[]{:S(2)}) %collective-permute-start.2) | collective-permute-done | bytes 524320 | tf_op jit(solution)/shard_map/ppermute | solution.py:30
  63.6 39.3 %all-to-all-done.rest_4_ = bf16[8,2,128,1024]{3,2,1,0:T(8,128)(2,1)} async-done(((bf16[8,2,128,1024]{3,2,1,0:T(8,128)(2,1)}), bf16[8,2,128,1024]{3,2,1,0:T(8,128)(2,1)}, u32[]{:S(2)}, u32[]{:S(2)}) %all-to-all-start) | async-done | bytes 4194336 | tf_op jit(solution)/shard_map/all_to_all | solution.py:53
  102.9 8.1 %all-to-all-start.1 = ((bf16[8,2,128,1024]{3,2,1,0:T(8,128)(2,1)}), bf16[8,2,128,1024]{3,2,1,0:T(8,128)(2,1)}, u32[]{:S(2)}, u32[]{:S(2)}) async-start(bf16[8,2,128,1024]{3,2,1,0:T(8,128)(2,1)} %pick_entries.3), calls=%async_computation.1 | async-start | bytes 8388608 | tf_op jit(solution)/shard_map/all_to_all | solution.py:53
  111.1 1.0 copy-done.27
  112.1 22.6 %attend_blocks.2 = (bf16[2,128,1024]{2,1,0:T(8,128)(2,1)}, bf16[2,128,1024]{2,1,0:T(8,128)(2,1)}, bf16[2,128,1024]{2,1,0:T(8,128)(2,1)}, bf16[2,128,1024]{2,1,0:...) custom-call(s32[1,8,2]{2,1,0:T(8,128)S(1)} %copy.10.uses, ...), custom_call_target="tpu_custom_call" | custom-call | flops 38654705664 | bytes 12582912 | tf_op jit(solution)/shard_map/attend_blocks/pallas_call | solution.py:244
  134.7 2.1 collective-permute-start.6
  137.4 2.2 collective-permute-start.5
  139.5 95.6 %collective-permute-done.6.rest_0_ = bf16[2,128,1024]{2,1,0:T(8,128)(2,1)S(1)} collective-permute-done((bf16[2,128,1024]{2,1,0:T(8,128)(2,1)}, bf16[2,128,1024]{2,1,0:T(8,128)(2,1)S(1)}, u32[]{:S(2)}, u32[]{:S(2)}) %collective-permute-start.6) | collective-permute-done | bytes 524320 | tf_op jit(solution)/shard_map/ppermute | solution.py:314
  235.9 1.0 collective-permute-start.14
  236.9 23.0 %collective-permute-done.7.rest_1_ = bf16[2,128,1024]{2,1,0:T(8,128)(2,1)S(1)} collective-permute-done((bf16[2,128,1024]{2,1,0:T(8,128)(2,1)}, bf16[2,128,1024]{2,1,0:T(8,128)(2,1)S(1)}, u32[]{:S(2)}, u32[]{:S(2)}) %collective-permute-start.7) | collective-permute-done | bytes 524320 | tf_op jit(solution)/shard_map/ppermute | solution.py:314
  259.9 0.8 copy-done.12
  261.5 0.9 copy-done.5
  262.4 0.9 copy-done.7
  263.3 5.6 %all-to-all-start.3 = ((bf16[4,2,128,1024]{3,2,1,0:T(8,128)(2,1)}), bf16[4,2,128,1024]{3,2,1,0:T(8,128)(2,1)S(1)}, u32[]{:S(2)}, u32[]{:S(2)}) async-start(bf16[4,2,128,1024]{3,2,1,0:T(8,128)(2,1)} %get-tuple-element.82), calls=%async_computation.3 | async-start | bytes 4194304 | tf_op jit(solution)/shard_map/all_to_all | solution.py:42
  268.9 1.0 copy-done.18
  270.0 1.0 copy-done.20
  271.0 1.0 copy-done.22
  272.1 1.0 copy-done.24
  273.1 22.7 %attend_blocks.3 = (bf16[2,128,1024]{2,1,0:T(8,128)(2,1)}, bf16[2,128,1024]{2,1,0:T(8,128)(2,1)}, bf16[2,128,1024]{2,1,0:T(8,128)(2,1)}, bf16[2,128,1024]{2,1,0:...) custom-call(s32[1,8,2]{2,1,0:T(8,128)S(1)} %copy.12.uses, ...), custom_call_target="tpu_custom_call" | custom-call | flops 38654705664 | bytes 12582912 | tf_op jit(solution)/shard_map/attend_blocks/pallas_call | solution.py:244
  295.8 5.9 %all-to-all-done.3.near_ref = bf16[4,2,128,1024]{3,2,1,0:T(8,128)(2,1)S(1)} async-done(((bf16[4,2,128,1024]{3,2,1,0:T(8,128)(2,1)}), bf16[4,2,128,1024]{3,2,1,0:T(8,128)(2,1)S(1)}, u32[]{:S(2)}, u32[]{:S(2)}) %all-to-all-start.3) | async-done | bytes 2097184 | tf_op jit(solution)/shard_map/all_to_all | solution.py:42
  301.7 7.1 %all-to-all-start.2 = ((bf16[4,2,128,1024]{3,2,1,0:T(8,128)(2,1)}), bf16[4,2,128,1024]{3,2,1,0:T(8,128)(2,1)}, u32[]{:S(2)}, u32[]{:S(2)}) async-start(bf16[4,2,128,1024]{3,2,1,0:T(8,128)(2,1)} %get-tuple-element.73), calls=%async_computation.2 | async-start | bytes 4194304 | tf_op jit(solution)/shard_map/all_to_all | solution.py:42
  308.8 2.6 collective-permute-start.16
  311.9 2.2 collective-permute-start.13
  314.1 9.5 %collective-permute-done.17.rest_1_ = bf16[2,128,1024]{2,1,0:T(8,128)(2,1)S(1)} collective-permute-done((bf16[2,128,1024]{2,1,0:T(8,128)(2,1)}, bf16[2,128,1024]{2,1,0:T(8,128)(2,1)S(1)}, u32[]{:S(2)}, u32[]{:S(2)}) %collective-permute-start.17) | collective-permute-done | bytes 524320 | tf_op jit(solution)/shard_map/ppermute | solution.py:314
  323.6 22.7 %collective-permute-start.19 = (bf16[2,128,1024]{2,1,0:T(8,128)(2,1)}, bf16[2,128,1024]{2,1,0:T(8,128)(2,1)}, u32[]{:S(2)}, u32[]{:S(2)}) collective-permute-start(bf16[2,128,1024]{2,1,0:T(8,128)(2,1)} %get-tuple-element.81), channel_id=1, source_target_pairs={{0,28},{4,16},{8,20},{12,24},{28,0},{16,4},{20,8},{24,12},{1,29},{... | collective-permute-start | bytes 1572872 | tf_op jit(solution)/shard_map/ppermute | solution.py:314
  346.3 7.6 %collective-permute-done.16.rest_0_ = bf16[2,128,1024]{2,1,0:T(8,128)(2,1)S(1)} collective-permute-done((bf16[2,128,1024]{2,1,0:T(8,128)(2,1)}, bf16[2,128,1024]{2,1,0:T(8,128)(2,1)S(1)}, u32[]{:S(2)}, u32[]{:S(2)}) %collective-permute-start.16) | collective-permute-done | bytes 524320 | tf_op jit(solution)/shard_map/ppermute | solution.py:314
  353.9 12.5 %collective-permute-start.18 = (bf16[2,128,1024]{2,1,0:T(8,128)(2,1)}, bf16[2,128,1024]{2,1,0:T(8,128)(2,1)}, u32[]{:S(2)}, u32[]{:S(2)}) collective-permute-start(bf16[2,128,1024]{2,1,0:T(8,128)(2,1)} %get-tuple-element.79), channel_id=1, source_target_pairs={{0,24},{4,28},{8,16},{12,20},{24,0},{28,4},{16,8},{20,12},{1,25},{... | collective-permute-start | bytes 1572872 | tf_op jit(solution)/shard_map/ppermute | solution.py:314
  366.4 1.0 copy-done.2
  367.5 1.0 copy-done.4
  368.5 1.0 copy-done.6
  369.6 1.0 copy-done.8
  370.6 1.0 copy-done.9
  371.7 3.6 unpack_rows.1
  375.3 3.5 owner_sum.2.rest_4_
  378.8 9.4 %collective-permute-done.19.rest_3_ = bf16[2,128,1024]{2,1,0:T(8,128)(2,1)} collective-permute-done((bf16[2,128,1024]{2,1,0:T(8,128)(2,1)}, bf16[2,128,1024]{2,1,0:T(8,128)(2,1)}, u32[]{:S(2)}, u32[]{:S(2)}) %collective-permute-start.19) | collective-permute-done | bytes 524320 | tf_op jit(solution)/shard_map/ppermute | solution.py:314
  388.2 12.5 %collective-permute-done.18.rest_2_ = bf16[2,128,1024]{2,1,0:T(8,128)(2,1)} collective-permute-done((bf16[2,128,1024]{2,1,0:T(8,128)(2,1)}, bf16[2,128,1024]{2,1,0:T(8,128)(2,1)}, u32[]{:S(2)}, u32[]{:S(2)}) %collective-permute-start.18) | collective-permute-done | bytes 524320 | tf_op jit(solution)/shard_map/ppermute | solution.py:314
  400.8 4.5 %owner_sum.3 = bf16[4,2,128,2048]{3,2,1,0:T(8,128)(2,1)} custom-call(s32[1,8,1]{2,1,0:T(8,128)S(1)} %copy.14.lists, bf16[4,2,128,1024]{3,2,1,0:T(8,128)(2,1)} %all-to-all-done.2.near_ref, bf16[2,128,1024]{2,1,0:T(8,128)(2,1)S(1)} %collective-permute-done.16.rest_0_, ...), custom_call_target="tpu_custom_call", output_to_operand_aliasing={{}: (6, {})} | custom-call | flops 2097152 | bytes 6291456 | tf_op jit(solution)/shard_map/owner_sum/pallas_call | solution.py:288
  (74 shorter events, 5.8 us)
Async XLA Ops:
  6.6 5.9 %copy-start = (bf16[1,128,8192]{2,1,0:T(8,128)(2,1)S(1)}, bf16[1,128,8192]{2,1,0:T(8,128)(2,1)}, u32[]{:S(2)}) copy-start(bf16[1,128,8192]{2,1,0:T(8,128)(2,1)} %q_ref.1) | copy-start | bytes 6291460
  6.6 96.3 %all-to-all-start = ((bf16[8,2,128,1024]{3,2,1,0:T(8,128)(2,1)}), bf16[8,2,128,1024]{3,2,1,0:T(8,128)(2,1)}, u32[]{:S(2)}, u32[]{:S(2)}) async-start(bf16[8,2,128,1024]{3,2,1,0:T(8,128)(2,1)} %pick_entries.2), calls=%async_computation | async-start | bytes 8388608 | tf_op jit(solution)/shard_map/all_to_all | solution.py:53
  12.4 1.6 copy-start.1
  15.7 13.4 %collective-permute-start.8 = (bf16[2,128,1024]{2,1,0:T(8,128)(2,1)}, bf16[2,128,1024]{2,1,0:T(8,128)(2,1)S(1)}, u32[]{:S(2)}, u32[]{:S(2)}) collective-permute-start(bf16[2,128,1024]{2,1,0:T(8,128)(2,1)} %get-tuple-element.56), channel_id=1, source_target_pairs={{0,1},{1,0},{2,3},{3,2},{4,5},{5,4},{6,7},{7,6},{8,9},{9,8},{10,11... | collective-permute-start | bytes 1572872 | tf_op jit(solution)/shard_map/ppermute | solution.py:30
  16.0 19.3 %collective-permute-start.9 = (bf16[2,128,1024]{2,1,0:T(8,128)(2,1)}, bf16[2,128,1024]{2,1,0:T(8,128)(2,1)S(1)}, u32[]{:S(2)}, u32[]{:S(2)}) collective-permute-start(bf16[2,128,1024]{2,1,0:T(8,128)(2,1)} %get-tuple-element.57), channel_id=1, source_target_pairs={{0,2},{1,3},{2,0},{3,1},{4,6},{5,7},{6,4},{7,5},{8,10},{9,11},{10,... | collective-permute-start | bytes 1572872 | tf_op jit(solution)/shard_map/ppermute | solution.py:30
  16.2 13.9 %copy-start.28 = (s32[1,8,1]{1,2,0:T(1,128)S(1)}, s32[1,8,1]{1,2,0:T(1,128)}, u32[]{:S(2)}) copy-start(s32[1,8,1]{1,2,0:T(1,128)} %param.7) | copy-start | bytes 100
  16.2 24.1 %collective-permute-start.10 = (bf16[2,128,1024]{2,1,0:T(8,128)(2,1)}, bf16[2,128,1024]{2,1,0:T(8,128)(2,1)S(1)}, u32[]{:S(2)}, u32[]{:S(2)}) collective-permute-start(bf16[2,128,1024]{2,1,0:T(8,128)(2,1)} %get-tuple-element.58), channel_id=1, source_target_pairs={{0,3},{1,2},{2,1},{3,0},{4,7},{5,6},{6,5},{7,4},{8,11},{9,10},{10,... | collective-permute-start | bytes 1572872 | tf_op jit(solution)/shard_map/ppermute | solution.py:30
  20.0 31.7 %collective-permute-start = (bf16[2,128,1024]{2,1,0:T(8,128)(2,1)}, bf16[2,128,1024]{2,1,0:T(8,128)(2,1)S(1)}, u32[]{:S(2)}, u32[]{:S(2)}) collective-permute-start(bf16[2,128,1024]{2,1,0:T(8,128)(2,1)} %get-tuple-element.45), channel_id=1, source_target_pairs={{0,1},{1,0},{2,3},{3,2},{4,5},{5,4},{6,7},{7,6},{8,9},{9,8},{10,11... | collective-permute-start | bytes 1572872 | tf_op jit(solution)/shard_map/ppermute | solution.py:30
  20.3 31.4 %collective-permute-start.1 = (bf16[2,128,1024]{2,1,0:T(8,128)(2,1)}, bf16[2,128,1024]{2,1,0:T(8,128)(2,1)S(1)}, u32[]{:S(2)}, u32[]{:S(2)}) collective-permute-start(bf16[2,128,1024]{2,1,0:T(8,128)(2,1)} %get-tuple-element.46), channel_id=1, source_target_pairs={{0,2},{1,3},{2,0},{3,1},{4,6},{5,7},{6,4},{7,5},{8,10},{9,11},{10,... | collective-permute-start | bytes 1572872 | tf_op jit(solution)/shard_map/ppermute | solution.py:30
  29.9 32.9 %collective-permute-start.2 = (bf16[2,128,1024]{2,1,0:T(8,128)(2,1)}, bf16[2,128,1024]{2,1,0:T(8,128)(2,1)S(1)}, u32[]{:S(2)}, u32[]{:S(2)}) collective-permute-start(bf16[2,128,1024]{2,1,0:T(8,128)(2,1)} %get-tuple-element.47), channel_id=1, source_target_pairs={{0,3},{1,2},{2,1},{3,0},{4,7},{5,6},{6,5},{7,4},{8,11},{9,10},{10,... | collective-permute-start | bytes 1572872 | tf_op jit(solution)/shard_map/ppermute | solution.py:30
  35.3 67.6 %copy-start.21 = (bf16[2,128,1024]{2,1,0:T(8,128)(2,1)}, bf16[2,128,1024]{2,1,0:T(8,128)(2,1)S(1)}, u32[]{:S(2)}) copy-start(bf16[2,128,1024]{2,1,0:T(8,128)(2,1)S(1)} %collective-permute-done.9.rest_2_) | copy-start | bytes 1572868
  40.3 62.6 %copy-start.23 = (bf16[2,128,1024]{2,1,0:T(8,128)(2,1)}, bf16[2,128,1024]{2,1,0:T(8,128)(2,1)S(1)}, u32[]{:S(2)}) copy-start(bf16[2,128,1024]{2,1,0:T(8,128)(2,1)S(1)} %collective-permute-done.10.rest_3_) | copy-start | bytes 1572868
  63.6 47.4 %copy-start.29 = (s32[1,8,2]{1,2,0:T(2,128)S(1)}, s32[1,8,2]{1,2,0:T(2,128)}, u32[]{:S(2)}) copy-start(s32[1,8,2]{1,2,0:T(2,128)} %param.8) | copy-start | bytes 196
  63.6 47.5 %copy-start.25 = (bf16[2,128,1024]{2,1,0:T(8,128)(2,1)S(1)}, bf16[2,128,1024]{2,1,0:T(8,128)(2,1)}, u32[]{:S(2)}) copy-start(bf16[2,128,1024]{2,1,0:T(8,128)(2,1)} %get-tuple-element.44.rest_0_) | copy-start | bytes 1572868
  102.9 160.4 %all-to-all-start.1 = ((bf16[8,2,128,1024]{3,2,1,0:T(8,128)(2,1)}), bf16[8,2,128,1024]{3,2,1,0:T(8,128)(2,1)}, u32[]{:S(2)}, u32[]{:S(2)}) async-start(bf16[8,2,128,1024]{3,2,1,0:T(8,128)(2,1)} %pick_entries.3), calls=%async_computation.1 | async-start | bytes 8388608 | tf_op jit(solution)/shard_map/all_to_all | solution.py:53
  111.1 1.0 copy-start.27
  134.7 100.4 %collective-permute-start.6 = (bf16[2,128,1024]{2,1,0:T(8,128)(2,1)}, bf16[2,128,1024]{2,1,0:T(8,128)(2,1)S(1)}, u32[]{:S(2)}, u32[]{:S(2)}) collective-permute-start(bf16[2,128,1024]{2,1,0:T(8,128)(2,1)} %get-tuple-element.52), channel_id=1, source_target_pairs={{0,16},{4,20},{8,24},{12,28},{16,0},{20,4},{24,8},{28,12},{1,17},{... | collective-permute-start | bytes 1572872 | tf_op jit(solution)/shard_map/ppermute | solution.py:314
  136.9 123.0 %collective-permute-start.7 = (bf16[2,128,1024]{2,1,0:T(8,128)(2,1)}, bf16[2,128,1024]{2,1,0:T(8,128)(2,1)S(1)}, u32[]{:S(2)}, u32[]{:S(2)}) collective-permute-start(bf16[2,128,1024]{2,1,0:T(8,128)(2,1)} %get-tuple-element.53), channel_id=1, source_target_pairs={{0,20},{4,24},{8,28},{12,16},{20,0},{24,4},{28,8},{16,12},{1,21},{... | collective-permute-start | bytes 1572872 | tf_op jit(solution)/shard_map/ppermute | solution.py:314
  136.9 123.8 %collective-permute-start.3 = (bf16[2,128,1024]{2,1,0:T(8,128)(2,1)}, bf16[2,128,1024]{2,1,0:T(8,128)(2,1)S(1)}, u32[]{:S(2)}, u32[]{:S(2)}) collective-permute-start(bf16[2,128,1024]{2,1,0:T(8,128)(2,1)} %get-tuple-element.49), channel_id=1, source_target_pairs={{0,1},{1,0},{2,3},{3,2},{4,5},{5,4},{6,7},{7,6},{8,9},{9,8},{10,11... | collective-permute-start | bytes 1572872 | tf_op jit(solution)/shard_map/ppermute | solution.py:30
  137.1 124.4 %collective-permute-start.4 = (bf16[2,128,1024]{2,1,0:T(8,128)(2,1)}, bf16[2,128,1024]{2,1,0:T(8,128)(2,1)S(1)}, u32[]{:S(2)}, u32[]{:S(2)}) collective-permute-start(bf16[2,128,1024]{2,1,0:T(8,128)(2,1)} %get-tuple-element.50), channel_id=1, source_target_pairs={{0,2},{1,3},{2,0},{3,1},{4,6},{5,7},{6,4},{7,5},{8,10},{9,11},{10,... | collective-permute-start | bytes 1572872 | tf_op jit(solution)/shard_map/ppermute | solution.py:30
  137.4 125.0 %collective-permute-start.5 = (bf16[2,128,1024]{2,1,0:T(8,128)(2,1)}, bf16[2,128,1024]{2,1,0:T(8,128)(2,1)S(1)}, u32[]{:S(2)}, u32[]{:S(2)}) collective-permute-start(bf16[2,128,1024]{2,1,0:T(8,128)(2,1)} %get-tuple-element.51), channel_id=1, source_target_pairs={{0,3},{1,2},{2,1},{3,0},{4,7},{5,6},{6,5},{7,4},{8,11},{9,10},{10,... | collective-permute-start | bytes 1572872 | tf_op jit(solution)/shard_map/ppermute | solution.py:30
  235.9 59.8 %collective-permute-start.14 = (bf16[2,128,1024]{2,1,0:T(8,128)(2,1)}, bf16[2,128,1024]{2,1,0:T(8,128)(2,1)S(1)}, u32[]{:S(2)}, u32[]{:S(2)}) collective-permute-start(bf16[2,128,1024]{2,1,0:T(8,128)(2,1)} %get-tuple-element.70), channel_id=1, source_target_pairs={{0,24},{4,28},{8,16},{12,20},{24,0},{28,4},{16,8},{20,12},{1,25},{... | collective-permute-start | bytes 1572872 | tf_op jit(solution)/shard_map/ppermute | solution.py:314
  262.4 0.9 copy-start.7
  263.3 32.5 %collective-permute-start.15 = (bf16[2,128,1024]{2,1,0:T(8,128)(2,1)}, bf16[2,128,1024]{2,1,0:T(8,128)(2,1)S(1)}, u32[]{:S(2)}, u32[]{:S(2)}) collective-permute-start(bf16[2,128,1024]{2,1,0:T(8,128)(2,1)} %get-tuple-element.72), channel_id=1, source_target_pairs={{0,28},{4,16},{8,20},{12,24},{28,0},{16,4},{20,8},{24,12},{1,29},{... | collective-permute-start | bytes 1572872 | tf_op jit(solution)/shard_map/ppermute | solution.py:314
  263.3 38.4 %all-to-all-start.3 = ((bf16[4,2,128,1024]{3,2,1,0:T(8,128)(2,1)}), bf16[4,2,128,1024]{3,2,1,0:T(8,128)(2,1)S(1)}, u32[]{:S(2)}, u32[]{:S(2)}) async-start(bf16[4,2,128,1024]{3,2,1,0:T(8,128)(2,1)} %get-tuple-element.82), calls=%async_computation.3 | async-start | bytes 4194304 | tf_op jit(solution)/shard_map/all_to_all | solution.py:42
  268.9 1.0 copy-start.18
  270.0 1.0 copy-start.20
  271.0 1.0 copy-start.22
  272.1 1.0 copy-start.24
  295.8 5.9 %copy-start.14 = (bf16[2,128,1024]{2,1,0:T(8,128)(2,1)}, bf16[2,128,1024]{2,1,0:T(8,128)(2,1)S(1)}, u32[]{:S(2)}) copy-start(bf16[2,128,1024]{2,1,0:T(8,128)(2,1)S(1)} %collective-permute-done.14.rest_2_) | copy-start | bytes 1572868
  295.8 5.9 %copy-start.16 = (bf16[2,128,1024]{2,1,0:T(8,128)(2,1)}, bf16[2,128,1024]{2,1,0:T(8,128)(2,1)S(1)}, u32[]{:S(2)}) copy-start(bf16[2,128,1024]{2,1,0:T(8,128)(2,1)S(1)} %collective-permute-done.15.rest_3_) | copy-start | bytes 1572868
  301.7 99.1 %all-to-all-start.2 = ((bf16[4,2,128,1024]{3,2,1,0:T(8,128)(2,1)}), bf16[4,2,128,1024]{3,2,1,0:T(8,128)(2,1)}, u32[]{:S(2)}, u32[]{:S(2)}) async-start(bf16[4,2,128,1024]{3,2,1,0:T(8,128)(2,1)} %get-tuple-element.73), calls=%async_computation.2 | async-start | bytes 4194304 | tf_op jit(solution)/shard_map/all_to_all | solution.py:42
  308.8 14.8 %collective-permute-start.17 = (bf16[2,128,1024]{2,1,0:T(8,128)(2,1)}, bf16[2,128,1024]{2,1,0:T(8,128)(2,1)S(1)}, u32[]{:S(2)}, u32[]{:S(2)}) collective-permute-start(bf16[2,128,1024]{2,1,0:T(8,128)(2,1)} %get-tuple-element.77), channel_id=1, source_target_pairs={{0,20},{4,24},{8,28},{12,16},{20,0},{24,4},{28,8},{16,12},{1,21},{... | collective-permute-start | bytes 1572872 | tf_op jit(solution)/shard_map/ppermute | solution.py:314
  308.8 45.1 %collective-permute-start.16 = (bf16[2,128,1024]{2,1,0:T(8,128)(2,1)}, bf16[2,128,1024]{2,1,0:T(8,128)(2,1)S(1)}, u32[]{:S(2)}, u32[]{:S(2)}) collective-permute-start(bf16[2,128,1024]{2,1,0:T(8,128)(2,1)} %get-tuple-element.75), channel_id=1, source_target_pairs={{0,16},{4,20},{8,24},{12,28},{16,0},{20,4},{24,8},{28,12},{1,17},{... | collective-permute-start | bytes 1572872 | tf_op jit(solution)/shard_map/ppermute | solution.py:314
  311.4 55.0 %collective-permute-start.11 = (bf16[2,128,1024]{2,1,0:T(8,128)(2,1)}, bf16[2,128,1024]{2,1,0:T(8,128)(2,1)}, u32[]{:S(2)}, u32[]{:S(2)}) collective-permute-start(bf16[2,128,1024]{2,1,0:T(8,128)(2,1)} %get-tuple-element.62), channel_id=1, source_target_pairs={{0,1},{1,0},{2,3},{3,2},{4,5},{5,4},{6,7},{7,6},{8,9},{9,8},{10,11... | collective-permute-start | bytes 1572872 | tf_op jit(solution)/shard_map/ppermute | solution.py:30
  311.7 54.7 %collective-permute-start.12 = (bf16[2,128,1024]{2,1,0:T(8,128)(2,1)}, bf16[2,128,1024]{2,1,0:T(8,128)(2,1)}, u32[]{:S(2)}, u32[]{:S(2)}) collective-permute-start(bf16[2,128,1024]{2,1,0:T(8,128)(2,1)} %get-tuple-element.63), channel_id=1, source_target_pairs={{0,2},{1,3},{2,0},{3,1},{4,6},{5,7},{6,4},{7,5},{8,10},{9,11},{10,... | collective-permute-start | bytes 1572872 | tf_op jit(solution)/shard_map/ppermute | solution.py:30
  311.9 54.5 %collective-permute-start.13 = (bf16[2,128,1024]{2,1,0:T(8,128)(2,1)}, bf16[2,128,1024]{2,1,0:T(8,128)(2,1)}, u32[]{:S(2)}, u32[]{:S(2)}) collective-permute-start(bf16[2,128,1024]{2,1,0:T(8,128)(2,1)} %get-tuple-element.64), channel_id=1, source_target_pairs={{0,3},{1,2},{2,1},{3,0},{4,7},{5,6},{6,5},{7,4},{8,11},{9,10},{10,... | collective-permute-start | bytes 1572872 | tf_op jit(solution)/shard_map/ppermute | solution.py:30
  323.6 64.6 %collective-permute-start.19 = (bf16[2,128,1024]{2,1,0:T(8,128)(2,1)}, bf16[2,128,1024]{2,1,0:T(8,128)(2,1)}, u32[]{:S(2)}, u32[]{:S(2)}) collective-permute-start(bf16[2,128,1024]{2,1,0:T(8,128)(2,1)} %get-tuple-element.81), channel_id=1, source_target_pairs={{0,28},{4,16},{8,20},{12,24},{28,0},{16,4},{20,8},{24,12},{1,29},{... | collective-permute-start | bytes 1572872 | tf_op jit(solution)/shard_map/ppermute | solution.py:314
  353.9 46.9 %collective-permute-start.18 = (bf16[2,128,1024]{2,1,0:T(8,128)(2,1)}, bf16[2,128,1024]{2,1,0:T(8,128)(2,1)}, u32[]{:S(2)}, u32[]{:S(2)}) collective-permute-start(bf16[2,128,1024]{2,1,0:T(8,128)(2,1)} %get-tuple-element.79), channel_id=1, source_target_pairs={{0,24},{4,28},{8,16},{12,20},{24,0},{28,4},{16,8},{20,12},{1,25},{... | collective-permute-start | bytes 1572872 | tf_op jit(solution)/shard_map/ppermute | solution.py:314
  366.4 1.0 copy-start.2
  367.5 1.0 copy-start.4
  368.5 1.0 copy-start.6
  369.6 1.0 copy-start.8
  370.6 1.0 copy-start.9
  371.6 3.7 copy-start.11
  371.6 3.7 copy-start.13
  371.6 3.7 copy-start.15
  371.6 3.7 copy-start.17
  (6 other events, 4.9 us)

commit v13 on v12

--- a/solution.py
+++ b/solution.py
@@ -132,14 +132,19 @@
     )(*flat)
 
 
-def pick_kernel(first, lists, pool_ref, out_ref, sems):
-    copies = []
-    for seq in range(out_ref.shape[0]):
-        source = pool_ref.at[lists[0, seq, 0], :, :, first : first + out_ref.shape[-1]]
-        copies.append(pltpu.make_async_copy(source, out_ref.at[seq], sems.at[seq]))
-        copies[-1].start()
-    for copy in copies:
-        copy.wait()
+def pick_kernel(first, lists, pool_ref, out_ref, held, sems):
+    seqs, chunk = held.shape[0], held.shape[-1]
+    arriving, leaving = [], []
+    for seq in range(seqs):
+        source = pool_ref.at[lists[0, seq, 0], :, :, first : first + chunk]
+        arriving.append(pltpu.make_async_copy(source, held.at[seq], sems.at[0, seq]))
+        leaving.append(pltpu.make_async_copy(held.at[seq], out_ref.at[seq], sems.at[1, seq]))
+        arriving[seq].start()
+    for seq in range(seqs):
+        arriving[seq].wait()
+        leaving[seq].start()
+    for seq in range(seqs):
+        leaving[seq].wait()
 
 
 def pick(first, chunk, send_lists, kv_pool):
@@ -148,9 +153,9 @@
         functools.partial(pick_kernel, first),
         grid=(1,),
         in_specs=[SCALARS, IN_HBM],
-        out_specs=pl.BlockSpec(shape, lambda i: (0, 0, 0, 0)),
+        out_specs=IN_HBM,
         out_shape=in_hbm(shape),
-        scratch_shapes=[pltpu.SemaphoreType.DMA((shape[0],))],
+        scratch_shapes=[pltpu.VMEM(shape, BF16), pltpu.SemaphoreType.DMA((2, shape[0]))],
         compiler_params=PARAMS,
         cost_estimate=cost(8 * shape[0] * NBLEN * chunk),
         name="pick_entries",
@@ -338,7 +343,7 @@
         rows_out, near, far = attend(block_slots, rows[h], arrived[h])
         far = swap_far(far, done)
         if h > 0:
-            near = after(near, done[: seqs // 2])
+            near = after(near, done[seqs // 2])
         returns.append((swap_near(near, seqs), far))
         token_parts.append(swap_rows(rows_out))
         block_slots = after(block_slots, (token_parts[-1], far[:DEPTH]))

time: 407 us -> 436 us (1.071)
  waiting for transfers between devices: 239 us -> 304 us
  starting transfers between devices: 76.3 us -> 41 us
    ppermute x8, waiting for transfers between devices: 158 us -> 228 us  [swap_far(): got.append(lax.ppermute(piece, 'enc', pairs))]
    ppermute x8, starting transfers between devices: 40.9 us -> 6.01 us  [swap_far(): got.append(lax.ppermute(piece, 'enc', pairs))]
    all_to_all x2, waiting for transfers between devices: 5.91 us -> 0.01 us  [swap_near(): lax.all_to_all(array, 'enc', split_axis=0, concat_axis=0, axis_index_grou...]
    unnamed x62 -> x64, local copies, waits for them, and re-layouts: 18.6 us -> 19.1 us
  transfers between devices with their start and end apart: 24 -> 24, of which waited for: 12 -> 12; matrix products, arithmetic and copies ran while one was open for 0% -> 0% of each run, Pallas kernels for 15% -> 14%
where the time goes in v13:
time: 436 us; the launch traced here: 434 us
  waiting for transfers between devices  304 us (70%)
  Pallas kernels  68.4 us (16%)
  starting transfers between devices  41 us (9%)
  local copies, waits for them, and re-layouts  19.4 us (4%)
    ppermute x8, waiting for transfers between devices, swap_far(): got.append(lax.ppermute(piece, 'enc', pairs))  228 us
    pallas_call x2, Pallas kernels, attend(): pl.pallas_call(functools.partial(attend_kernel, seqs, parts), grid=(heads...  45.2 us
    all_to_all x2, waiting for transfers between devices, swap_pool(): return lax.all_to_all(array, 'enc', split_axis=0, concat_axis=0, tiled=True)  39.3 us
    ppermute x12, waiting for transfers between devices, exchange(): return lax.ppermute(array, axis, pairs)  37 us
    unnamed x64, local copies, waits for them, and re-layouts  19.1 us
    all_to_all x2, starting transfers between devices, swap_pool(): return lax.all_to_all(array, 'enc', split_axis=0, concat_axis=0, tiled=True)  13.9 us
    all_to_all x2, starting transfers between devices, swap_near(): lax.all_to_all(array, 'enc', split_axis=0, concat_axis=0, axis_index_grou...  12.3 us
    ppermute x12, starting transfers between devices, exchange(): return lax.ppermute(array, axis, pairs)  8.75 us
  transfers between devices with their start and end apart: 24, of which 12 were waited for; matrix products, arithmetic and copies ran while one was open for 0% of the time, Pallas kernels for 14%

profile of v13, /device:TPU:15, one launch (start us, length us, event | category | flops | bytes accessed | tf_op | source)
XLA Modules:
  0.0 433.7 jit_solution(17502969292177307674)
XLA Ops:
  1.4 4.2 pick_entries.2
  5.6 5.8 %all-to-all-start = ((bf16[8,2,128,1024]{3,2,1,0:T(8,128)(2,1)}), bf16[8,2,128,1024]{3,2,1,0:T(8,128)(2,1)}, u32[]{:S(2)}, u32[]{:S(2)}) async-start(bf16[8,2,128,1024]{3,2,1,0:T(8,128)(2,1)} %pick_entries.2), calls=%async_computation | async-start | bytes 8388608 | tf_op jit(solution)/shard_map/all_to_all | solution.py:53
  11.3 1.6 copy-done.1
  12.9 1.6 pack_rows.3
  15.1 2.2 collective-permute-start.10
  17.3 1.6 pack_rows.2
  19.4 8.6 %collective-permute-done.8.rest_1_ = bf16[2,128,1024]{2,1,0:T(8,128)(2,1)S(1)} collective-permute-done((bf16[2,128,1024]{2,1,0:T(8,128)(2,1)}, bf16[2,128,1024]{2,1,0:T(8,128)(2,1)S(1)}, u32[]{:S(2)}, u32[]{:S(2)}) %collective-permute-start.8) | collective-permute-done | bytes 524320 | tf_op jit(solution)/shard_map/ppermute | solution.py:30
  28.0 0.8 copy-done.19
  29.1 4.2 pick_entries.3
  33.4 5.9 %collective-permute-done.10.rest_3_ = bf16[2,128,1024]{2,1,0:T(8,128)(2,1)S(1)} collective-permute-done((bf16[2,128,1024]{2,1,0:T(8,128)(2,1)}, bf16[2,128,1024]{2,1,0:T(8,128)(2,1)S(1)}, u32[]{:S(2)}, u32[]{:S(2)}) %collective-permute-start.10) | collective-permute-done | bytes 524320 | tf_op jit(solution)/shard_map/ppermute | solution.py:30
  39.2 11.4 %collective-permute-done.rest_1_ = bf16[2,128,1024]{2,1,0:T(8,128)(2,1)S(1)} collective-permute-done((bf16[2,128,1024]{2,1,0:T(8,128)(2,1)}, bf16[2,128,1024]{2,1,0:T(8,128)(2,1)S(1)}, u32[]{:S(2)}, u32[]{:S(2)}) %collective-permute-start) | collective-permute-done | bytes 524320 | tf_op jit(solution)/shard_map/ppermute | solution.py:30
  50.6 11.1 %collective-permute-done.2.rest_3_ = bf16[2,128,1024]{2,1,0:T(8,128)(2,1)S(1)} collective-permute-done((bf16[2,128,1024]{2,1,0:T(8,128)(2,1)}, bf16[2,128,1024]{2,1,0:T(8,128)(2,1)S(1)}, u32[]{:S(2)}, u32[]{:S(2)}) %collective-permute-start.2) | collective-permute-done | bytes 524320 | tf_op jit(solution)/shard_map/ppermute | solution.py:30
  61.7 0.8 copy-done.26
  62.5 39.3 %all-to-all-done.rest_4_ = bf16[8,2,128,1024]{3,2,1,0:T(8,128)(2,1)} async-done(((bf16[8,2,128,1024]{3,2,1,0:T(8,128)(2,1)}), bf16[8,2,128,1024]{3,2,1,0:T(8,128)(2,1)}, u32[]{:S(2)}, u32[]{:S(2)}) %all-to-all-start) | async-done | bytes 4194336 | tf_op jit(solution)/shard_map/all_to_all | solution.py:53
  101.8 8.1 %all-to-all-start.1 = ((bf16[8,2,128,1024]{3,2,1,0:T(8,128)(2,1)}), bf16[8,2,128,1024]{3,2,1,0:T(8,128)(2,1)}, u32[]{:S(2)}, u32[]{:S(2)}) async-start(bf16[8,2,128,1024]{3,2,1,0:T(8,128)(2,1)} %pick_entries.3), calls=%async_computation.1 | async-start | bytes 8388608 | tf_op jit(solution)/shard_map/all_to_all | solution.py:53
  110.0 1.0 copy-done.27
  111.0 22.6 %attend_blocks.2 = (bf16[2,128,1024]{2,1,0:T(8,128)(2,1)}, bf16[2,128,1024]{2,1,0:T(8,128)(2,1)}, bf16[2,128,1024]{2,1,0:T(8,128)(2,1)}, bf16[2,128,1024]{2,1,0:...) custom-call(s32[1,8,2]{2,1,0:T(8,128)S(1)} %copy.10.uses, ...), custom_call_target="tpu_custom_call" | custom-call | flops 38654705664 | bytes 12582912 | tf_op jit(solution)/shard_map/attend_blocks/pallas_call | solution.py:249
  133.6 2.2 collective-permute-start.6
  136.3 2.2 collective-permute-start.5
  138.8 95.3 %collective-permute-done.6.rest_0_ = bf16[2,128,1024]{2,1,0:T(8,128)(2,1)S(1)} collective-permute-done((bf16[2,128,1024]{2,1,0:T(8,128)(2,1)}, bf16[2,128,1024]{2,1,0:T(8,128)(2,1)S(1)}, u32[]{:S(2)}, u32[]{:S(2)}) %collective-permute-start.6) | collective-permute-done | bytes 524320 | tf_op jit(solution)/shard_map/ppermute | solution.py:319
  234.9 1.0 collective-permute-start.14
  235.8 0.8 copy-done.3
  236.6 0.8 copy-done.5
  237.5 0.9 copy-done.7
  238.4 20.4 %collective-permute-done.7.rest_1_ = bf16[2,128,1024]{2,1,0:T(8,128)(2,1)S(1)} collective-permute-done((bf16[2,128,1024]{2,1,0:T(8,128)(2,1)}, bf16[2,128,1024]{2,1,0:T(8,128)(2,1)S(1)}, u32[]{:S(2)}, u32[]{:S(2)}) %collective-permute-start.7) | collective-permute-done | bytes 524320 | tf_op jit(solution)/shard_map/ppermute | solution.py:319
  258.8 0.8 copy-done.12
  259.7 4.6 %all-to-all-start.3 = ((bf16[4,2,128,1024]{3,2,1,0:T(8,128)(2,1)}), bf16[4,2,128,1024]{3,2,1,0:T(8,128)(2,1)S(1)}, u32[]{:S(2)}, u32[]{:S(2)}) async-start(bf16[4,2,128,1024]{3,2,1,0:T(8,128)(2,1)} %get-tuple-element.82), calls=%async_computation.3 | async-start | bytes 4194304 | tf_op jit(solution)/shard_map/all_to_all | solution.py:42
  264.3 1.0 copy-done.20
  265.3 1.0 copy-done.22
  266.3 1.0 copy-done.24
  267.4 22.7 %attend_blocks.3 = (bf16[2,128,1024]{2,1,0:T(8,128)(2,1)}, bf16[2,128,1024]{2,1,0:T(8,128)(2,1)}, bf16[2,128,1024]{2,1,0:T(8,128)(2,1)}, bf16[2,128,1024]{2,1,0:...) custom-call(s32[1,8,2]{2,1,0:T(8,128)S(1)} %copy.12.uses, ...), custom_call_target="tpu_custom_call" | custom-call | flops 38654705664 | bytes 12582912 | tf_op jit(solution)/shard_map/attend_blocks/pallas_call | solution.py:249
  291.3 23.0 %collective-permute-done.15.rest_0_ = bf16[2,128,1024]{2,1,0:T(8,128)(2,1)S(1)} collective-permute-done((bf16[2,128,1024]{2,1,0:T(8,128)(2,1)}, bf16[2,128,1024]{2,1,0:T(8,128)(2,1)S(1)}, u32[]{:S(2)}, u32[]{:S(2)}) %collective-permute-start.15) | collective-permute-done | bytes 524320 | tf_op jit(solution)/shard_map/ppermute | solution.py:319
  314.3 7.7 %all-to-all-start.2 = ((bf16[4,2,128,1024]{3,2,1,0:T(8,128)(2,1)}), bf16[4,2,128,1024]{3,2,1,0:T(8,128)(2,1)}, u32[]{:S(2)}, u32[]{:S(2)}) async-start(bf16[4,2,128,1024]{3,2,1,0:T(8,128)(2,1)} %get-tuple-element.73), calls=%async_computation.2 | async-start | bytes 4194304 | tf_op jit(solution)/shard_map/all_to_all | solution.py:42
  322.3 34.4 %collective-permute-done.16.rest_3_ = bf16[2,128,1024]{2,1,0:T(8,128)(2,1)S(1)} collective-permute-done((bf16[2,128,1024]{2,1,0:T(8,128)(2,1)S(1)}, bf16[2,128,1024]{2,1,0:T(8,128)(2,1)S(1)}, u32[]{:S(2)}, u32[]{:S(2)}) %collective-permute-start.16) | collective-permute-done | bytes 524320 | tf_op jit(solution)/shard_map/ppermute | solution.py:319
  356.8 0.8 copy-done.16
  357.6 1.8 collective-permute-start.17
  359.9 2.2 collective-permute-start.13
  362.0 21.5 %collective-permute-done.17.rest_1_ = bf16[2,128,1024]{2,1,0:T(8,128)(2,1)S(1)} collective-permute-done((bf16[2,128,1024]{2,1,0:T(8,128)(2,1)}, bf16[2,128,1024]{2,1,0:T(8,128)(2,1)S(1)}, u32[]{:S(2)}, u32[]{:S(2)}) %collective-permute-start.17) | collective-permute-done | bytes 524320 | tf_op jit(solution)/shard_map/ppermute | solution.py:319
  383.6 1.0 copy-done.2
  384.6 1.0 copy-done.4
  385.7 1.0 copy-done.6
  386.7 1.0 copy-done.8
  387.8 1.0 copy-done.9
  388.8 3.6 unpack_rows.1
  392.5 3.5 owner_sum.2.rest_4_
  396.0 22.0 %collective-permute-done.19.rest_3_ = bf16[2,128,1024]{2,1,0:T(8,128)(2,1)} collective-permute-done((bf16[2,128,1024]{2,1,0:T(8,128)(2,1)}, bf16[2,128,1024]{2,1,0:T(8,128)(2,1)}, u32[]{:S(2)}, u32[]{:S(2)}) %collective-permute-start.19) | collective-permute-done | bytes 524320 | tf_op jit(solution)/shard_map/ppermute | solution.py:319
  418.0 11.2 %collective-permute-done.18.rest_2_ = bf16[2,128,1024]{2,1,0:T(8,128)(2,1)} collective-permute-done((bf16[2,128,1024]{2,1,0:T(8,128)(2,1)}, bf16[2,128,1024]{2,1,0:T(8,128)(2,1)}, u32[]{:S(2)}, u32[]{:S(2)}) %collective-permute-start.18) | collective-permute-done | bytes 524320 | tf_op jit(solution)/shard_map/ppermute | solution.py:319
  429.2 4.5 %owner_sum.3 = bf16[4,2,128,2048]{3,2,1,0:T(8,128)(2,1)} custom-call(s32[1,8,1]{2,1,0:T(8,128)S(1)} %copy.14.lists, bf16[4,2,128,1024]{3,2,1,0:T(8,128)(2,1)} %all-to-all-done.2.near_ref, bf16[2,128,1024]{2,1,0:T(8,128)(2,1)S(1)} %collective-permute-done.15.rest_0_, ...), custom_call_target="tpu_custom_call", output_to_operand_aliasing={{}: (6, {})} | custom-call | flops 2097152 | bytes 6291456 | tf_op jit(solution)/shard_map/owner_sum/pallas_call | solution.py:293
  (76 shorter events, 6.0 us)
Async XLA Ops:
  5.5 5.8 %copy-start = (bf16[1,128,8192]{2,1,0:T(8,128)(2,1)S(1)}, bf16[1,128,8192]{2,1,0:T(8,128)(2,1)}, u32[]{:S(2)}) copy-start(bf16[1,128,8192]{2,1,0:T(8,128)(2,1)} %q_ref.1) | copy-start | bytes 6291460
  5.6 96.2 %all-to-all-start = ((bf16[8,2,128,1024]{3,2,1,0:T(8,128)(2,1)}), bf16[8,2,128,1024]{3,2,1,0:T(8,128)(2,1)}, u32[]{:S(2)}, u32[]{:S(2)}) async-start(bf16[8,2,128,1024]{3,2,1,0:T(8,128)(2,1)} %pick_entries.2), calls=%async_computation | async-start | bytes 8388608 | tf_op jit(solution)/shard_map/all_to_all | solution.py:53
  11.3 1.6 copy-start.1
  14.6 13.4 %collective-permute-start.8 = (bf16[2,128,1024]{2,1,0:T(8,128)(2,1)}, bf16[2,128,1024]{2,1,0:T(8,128)(2,1)S(1)}, u32[]{:S(2)}, u32[]{:S(2)}) collective-permute-start(bf16[2,128,1024]{2,1,0:T(8,128)(2,1)} %get-tuple-element.56), channel_id=1, source_target_pairs={{0,1},{1,0},{2,3},{3,2},{4,5},{5,4},{6,7},{7,6},{8,9},{9,8},{10,11... | collective-permute-start | bytes 1572872 | tf_op jit(solution)/shard_map/ppermute | solution.py:30
  14.9 18.4 %collective-permute-start.9 = (bf16[2,128,1024]{2,1,0:T(8,128)(2,1)}, bf16[2,128,1024]{2,1,0:T(8,128)(2,1)S(1)}, u32[]{:S(2)}, u32[]{:S(2)}) collective-permute-start(bf16[2,128,1024]{2,1,0:T(8,128)(2,1)} %get-tuple-element.57), channel_id=1, source_target_pairs={{0,2},{1,3},{2,0},{3,1},{4,6},{5,7},{6,4},{7,5},{8,10},{9,11},{10,... | collective-permute-start | bytes 1572872 | tf_op jit(solution)/shard_map/ppermute | solution.py:30
  15.1 13.9 %copy-start.28 = (s32[1,8,1]{1,2,0:T(1,128)S(1)}, s32[1,8,1]{1,2,0:T(1,128)}, u32[]{:S(2)}) copy-start(s32[1,8,1]{1,2,0:T(1,128)} %param.7) | copy-start | bytes 100
  15.1 24.1 %collective-permute-start.10 = (bf16[2,128,1024]{2,1,0:T(8,128)(2,1)}, bf16[2,128,1024]{2,1,0:T(8,128)(2,1)S(1)}, u32[]{:S(2)}, u32[]{:S(2)}) collective-permute-start(bf16[2,128,1024]{2,1,0:T(8,128)(2,1)} %get-tuple-element.58), channel_id=1, source_target_pairs={{0,3},{1,2},{2,1},{3,0},{4,7},{5,6},{6,5},{7,4},{8,11},{9,10},{10,... | collective-permute-start | bytes 1572872 | tf_op jit(solution)/shard_map/ppermute | solution.py:30
  18.9 31.8 %collective-permute-start = (bf16[2,128,1024]{2,1,0:T(8,128)(2,1)}, bf16[2,128,1024]{2,1,0:T(8,128)(2,1)S(1)}, u32[]{:S(2)}, u32[]{:S(2)}) collective-permute-start(bf16[2,128,1024]{2,1,0:T(8,128)(2,1)} %get-tuple-element.45), channel_id=1, source_target_pairs={{0,1},{1,0},{2,3},{3,2},{4,5},{5,4},{6,7},{7,6},{8,9},{9,8},{10,11... | collective-permute-start | bytes 1572872 | tf_op jit(solution)/shard_map/ppermute | solution.py:30
  19.2 31.4 %collective-permute-start.1 = (bf16[2,128,1024]{2,1,0:T(8,128)(2,1)}, bf16[2,128,1024]{2,1,0:T(8,128)(2,1)S(1)}, u32[]{:S(2)}, u32[]{:S(2)}) collective-permute-start(bf16[2,128,1024]{2,1,0:T(8,128)(2,1)} %get-tuple-element.46), channel_id=1, source_target_pairs={{0,2},{1,3},{2,0},{3,1},{4,6},{5,7},{6,4},{7,5},{8,10},{9,11},{10,... | collective-permute-start | bytes 1572872 | tf_op jit(solution)/shard_map/ppermute | solution.py:30
  28.8 32.9 %collective-permute-start.2 = (bf16[2,128,1024]{2,1,0:T(8,128)(2,1)}, bf16[2,128,1024]{2,1,0:T(8,128)(2,1)S(1)}, u32[]{:S(2)}, u32[]{:S(2)}) collective-permute-start(bf16[2,128,1024]{2,1,0:T(8,128)(2,1)} %get-tuple-element.47), channel_id=1, source_target_pairs={{0,3},{1,2},{2,1},{3,0},{4,7},{5,6},{6,5},{7,4},{8,11},{9,10},{10,... | collective-permute-start | bytes 1572872 | tf_op jit(solution)/shard_map/ppermute | solution.py:30
  33.3 68.4 %copy-start.21 = (bf16[2,128,1024]{2,1,0:T(8,128)(2,1)}, bf16[2,128,1024]{2,1,0:T(8,128)(2,1)S(1)}, u32[]{:S(2)}) copy-start(bf16[2,128,1024]{2,1,0:T(8,128)(2,1)S(1)} %collective-permute-done.9.rest_2_) | copy-start | bytes 1572868
  39.2 62.6 %copy-start.23 = (bf16[2,128,1024]{2,1,0:T(8,128)(2,1)}, bf16[2,128,1024]{2,1,0:T(8,128)(2,1)S(1)}, u32[]{:S(2)}) copy-start(bf16[2,128,1024]{2,1,0:T(8,128)(2,1)S(1)} %collective-permute-done.10.rest_3_) | copy-start | bytes 1572868
  62.5 47.4 %copy-start.29 = (s32[1,8,2]{1,2,0:T(2,128)S(1)}, s32[1,8,2]{1,2,0:T(2,128)}, u32[]{:S(2)}) copy-start(s32[1,8,2]{1,2,0:T(2,128)} %param.8) | copy-start | bytes 196
  62.5 47.5 %copy-start.25 = (bf16[2,128,1024]{2,1,0:T(8,128)(2,1)S(1)}, bf16[2,128,1024]{2,1,0:T(8,128)(2,1)}, u32[]{:S(2)}) copy-start(bf16[2,128,1024]{2,1,0:T(8,128)(2,1)} %get-tuple-element.44.rest_0_) | copy-start | bytes 1572868
  101.8 157.9 %all-to-all-start.1 = ((bf16[8,2,128,1024]{3,2,1,0:T(8,128)(2,1)}), bf16[8,2,128,1024]{3,2,1,0:T(8,128)(2,1)}, u32[]{:S(2)}, u32[]{:S(2)}) async-start(bf16[8,2,128,1024]{3,2,1,0:T(8,128)(2,1)} %pick_entries.3), calls=%async_computation.1 | async-start | bytes 8388608 | tf_op jit(solution)/shard_map/all_to_all | solution.py:53
  110.0 1.0 copy-start.27
  133.6 100.4 %collective-permute-start.6 = (bf16[2,128,1024]{2,1,0:T(8,128)(2,1)}, bf16[2,128,1024]{2,1,0:T(8,128)(2,1)S(1)}, u32[]{:S(2)}, u32[]{:S(2)}) collective-permute-start(bf16[2,128,1024]{2,1,0:T(8,128)(2,1)} %get-tuple-element.52), channel_id=1, source_target_pairs={{0,16},{4,20},{8,24},{12,28},{16,0},{20,4},{24,8},{28,12},{1,17},{... | collective-permute-start | bytes 1572872 | tf_op jit(solution)/shard_map/ppermute | solution.py:319
  135.8 100.0 %collective-permute-start.3 = (bf16[2,128,1024]{2,1,0:T(8,128)(2,1)}, bf16[2,128,1024]{2,1,0:T(8,128)(2,1)S(1)}, u32[]{:S(2)}, u32[]{:S(2)}) collective-permute-start(bf16[2,128,1024]{2,1,0:T(8,128)(2,1)} %get-tuple-element.49), channel_id=1, source_target_pairs={{0,1},{1,0},{2,3},{3,2},{4,5},{5,4},{6,7},{7,6},{8,9},{9,8},{10,11... | collective-permute-start | bytes 1572872 | tf_op jit(solution)/shard_map/ppermute | solution.py:30
  136.1 100.6 %collective-permute-start.4 = (bf16[2,128,1024]{2,1,0:T(8,128)(2,1)}, bf16[2,128,1024]{2,1,0:T(8,128)(2,1)S(1)}, u32[]{:S(2)}, u32[]{:S(2)}) collective-permute-start(bf16[2,128,1024]{2,1,0:T(8,128)(2,1)} %get-tuple-element.50), channel_id=1, source_target_pairs={{0,2},{1,3},{2,0},{3,1},{4,6},{5,7},{6,4},{7,5},{8,10},{9,11},{10,... | collective-permute-start | bytes 1572872 | tf_op jit(solution)/shard_map/ppermute | solution.py:30
  136.3 101.2 %collective-permute-start.5 = (bf16[2,128,1024]{2,1,0:T(8,128)(2,1)}, bf16[2,128,1024]{2,1,0:T(8,128)(2,1)S(1)}, u32[]{:S(2)}, u32[]{:S(2)}) collective-permute-start(bf16[2,128,1024]{2,1,0:T(8,128)(2,1)} %get-tuple-element.51), channel_id=1, source_target_pairs={{0,3},{1,2},{2,1},{3,0},{4,7},{5,6},{6,5},{7,4},{8,11},{9,10},{10,... | collective-permute-start | bytes 1572872 | tf_op jit(solution)/shard_map/ppermute | solution.py:30
  138.5 120.3 %collective-permute-start.7 = (bf16[2,128,1024]{2,1,0:T(8,128)(2,1)}, bf16[2,128,1024]{2,1,0:T(8,128)(2,1)S(1)}, u32[]{:S(2)}, u32[]{:S(2)}) collective-permute-start(bf16[2,128,1024]{2,1,0:T(8,128)(2,1)} %get-tuple-element.53), channel_id=1, source_target_pairs={{0,20},{4,24},{8,28},{12,16},{20,0},{24,4},{28,8},{16,12},{1,21},{... | collective-permute-start | bytes 1572872 | tf_op jit(solution)/shard_map/ppermute | solution.py:319
  234.9 55.2 %collective-permute-start.14 = (bf16[2,128,1024]{2,1,0:T(8,128)(2,1)}, bf16[2,128,1024]{2,1,0:T(8,128)(2,1)S(1)}, u32[]{:S(2)}, u32[]{:S(2)}) collective-permute-start(bf16[2,128,1024]{2,1,0:T(8,128)(2,1)} %get-tuple-element.71), channel_id=1, source_target_pairs={{0,24},{4,28},{8,16},{12,20},{24,0},{28,4},{16,8},{20,12},{1,25},{... | collective-permute-start | bytes 1572872 | tf_op jit(solution)/shard_map/ppermute | solution.py:319
  236.6 0.8 copy-start.5
  237.5 0.9 copy-start.7
  259.7 4.6 %copy-start.18 = (bf16[2,128,1024]{2,1,0:T(8,128)(2,1)S(1)}, bf16[2,128,1024]{2,1,0:T(8,128)(2,1)}, u32[]{:S(2)}) copy-start(bf16[2,128,1024]{2,1,0:T(8,128)(2,1)} %get-tuple-element.55.rest_0_) | copy-start | bytes 1572868
  259.7 54.6 %all-to-all-start.3 = ((bf16[4,2,128,1024]{3,2,1,0:T(8,128)(2,1)}), bf16[4,2,128,1024]{3,2,1,0:T(8,128)(2,1)S(1)}, u32[]{:S(2)}, u32[]{:S(2)}) async-start(bf16[4,2,128,1024]{3,2,1,0:T(8,128)(2,1)} %get-tuple-element.82), calls=%async_computation.3 | async-start | bytes 4194304 | tf_op jit(solution)/shard_map/all_to_all | solution.py:42
  264.3 1.0 copy-start.20
  265.3 1.0 copy-start.22
  266.3 1.0 copy-start.24
  290.8 23.5 %collective-permute-start.15 = (bf16[2,128,1024]{2,1,0:T(8,128)(2,1)}, bf16[2,128,1024]{2,1,0:T(8,128)(2,1)S(1)}, u32[]{:S(2)}, u32[]{:S(2)}) collective-permute-start(bf16[2,128,1024]{2,1,0:T(8,128)(2,1)} %get-tuple-element.72), channel_id=1, source_target_pairs={{0,16},{4,20},{8,24},{12,28},{16,0},{20,4},{24,8},{28,12},{1,17},{... | collective-permute-start | bytes 1572872 | tf_op jit(solution)/shard_map/ppermute | solution.py:319
  314.3 7.8 %copy-start.30 = (bf16[2,128,1024]{2,1,0:T(8,128)(2,1)S(1)}, bf16[2,128,1024]{2,1,0:T(8,128)(2,1)}, u32[]{:S(2)}) copy-start(bf16[2,128,1024]{2,1,0:T(8,128)(2,1)} %get-tuple-element.76) | copy-start | bytes 1572868
  314.3 114.9 %all-to-all-start.2 = ((bf16[4,2,128,1024]{3,2,1,0:T(8,128)(2,1)}), bf16[4,2,128,1024]{3,2,1,0:T(8,128)(2,1)}, u32[]{:S(2)}, u32[]{:S(2)}) async-start(bf16[4,2,128,1024]{3,2,1,0:T(8,128)(2,1)} %get-tuple-element.73), calls=%async_computation.2 | async-start | bytes 4194304 | tf_op jit(solution)/shard_map/all_to_all | solution.py:42
  322.1 34.7 %collective-permute-start.16 = (bf16[2,128,1024]{2,1,0:T(8,128)(2,1)S(1)}, bf16[2,128,1024]{2,1,0:T(8,128)(2,1)S(1)}, u32[]{:S(2)}, u32[]{:S(2)}) collective-permute-start(bf16[2,128,1024]{2,1,0:T(8,128)(2,1)S(1)} %copy-done.30), channel_id=1, source_target_pairs={{0,28},{4,16},{8,20},{12,24},{28,0},{16,4},{20,8},{24,12},{1,29},{... | collective-permute-start | bytes 1572872 | tf_op jit(solution)/shard_map/ppermute | solution.py:319
  357.6 25.9 %collective-permute-start.17 = (bf16[2,128,1024]{2,1,0:T(8,128)(2,1)}, bf16[2,128,1024]{2,1,0:T(8,128)(2,1)S(1)}, u32[]{:S(2)}, u32[]{:S(2)}) collective-permute-start(bf16[2,128,1024]{2,1,0:T(8,128)(2,1)} %get-tuple-element.77), channel_id=1, source_target_pairs={{0,20},{4,24},{8,28},{12,16},{20,0},{24,4},{28,8},{16,12},{1,21},{... | collective-permute-start | bytes 1572872 | tf_op jit(solution)/shard_map/ppermute | solution.py:319
  359.4 24.2 %collective-permute-start.11 = (bf16[2,128,1024]{2,1,0:T(8,128)(2,1)}, bf16[2,128,1024]{2,1,0:T(8,128)(2,1)}, u32[]{:S(2)}, u32[]{:S(2)}) collective-permute-start(bf16[2,128,1024]{2,1,0:T(8,128)(2,1)} %get-tuple-element.62), channel_id=1, source_target_pairs={{0,1},{1,0},{2,3},{3,2},{4,5},{5,4},{6,7},{7,6},{8,9},{9,8},{10,11... | collective-permute-start | bytes 1572872 | tf_op jit(solution)/shard_map/ppermute | solution.py:30
  359.6 24.0 %collective-permute-start.12 = (bf16[2,128,1024]{2,1,0:T(8,128)(2,1)}, bf16[2,128,1024]{2,1,0:T(8,128)(2,1)}, u32[]{:S(2)}, u32[]{:S(2)}) collective-permute-start(bf16[2,128,1024]{2,1,0:T(8,128)(2,1)} %get-tuple-element.63), channel_id=1, source_target_pairs={{0,2},{1,3},{2,0},{3,1},{4,6},{5,7},{6,4},{7,5},{8,10},{9,11},{10,... | collective-permute-start | bytes 1572872 | tf_op jit(solution)/shard_map/ppermute | solution.py:30
  359.9 23.7 %collective-permute-start.13 = (bf16[2,128,1024]{2,1,0:T(8,128)(2,1)}, bf16[2,128,1024]{2,1,0:T(8,128)(2,1)}, u32[]{:S(2)}, u32[]{:S(2)}) collective-permute-start(bf16[2,128,1024]{2,1,0:T(8,128)(2,1)} %get-tuple-element.64), channel_id=1, source_target_pairs={{0,3},{1,2},{2,1},{3,0},{4,7},{5,6},{6,5},{7,4},{8,11},{9,10},{10,... | collective-permute-start | bytes 1572872 | tf_op jit(solution)/shard_map/ppermute | solution.py:30
  383.5 34.5 %collective-permute-start.19 = (bf16[2,128,1024]{2,1,0:T(8,128)(2,1)}, bf16[2,128,1024]{2,1,0:T(8,128)(2,1)}, u32[]{:S(2)}, u32[]{:S(2)}) collective-permute-start(bf16[2,128,1024]{2,1,0:T(8,128)(2,1)} %get-tuple-element.81), channel_id=1, source_target_pairs={{0,28},{4,16},{8,20},{12,24},{28,0},{16,4},{20,8},{24,12},{1,29},{... | collective-permute-start | bytes 1572872 | tf_op jit(solution)/shard_map/ppermute | solution.py:319
  383.5 45.7 %collective-permute-start.18 = (bf16[2,128,1024]{2,1,0:T(8,128)(2,1)}, bf16[2,128,1024]{2,1,0:T(8,128)(2,1)}, u32[]{:S(2)}, u32[]{:S(2)}) collective-permute-start(bf16[2,128,1024]{2,1,0:T(8,128)(2,1)} %get-tuple-element.79), channel_id=1, source_target_pairs={{0,24},{4,28},{8,16},{12,20},{24,0},{28,4},{16,8},{20,12},{1,25},{... | collective-permute-start | bytes 1572872 | tf_op jit(solution)/shard_map/ppermute | solution.py:319
  383.6 1.0 copy-start.2
  384.6 1.0 copy-start.4
  385.7 1.0 copy-start.6
  386.7 1.0 copy-start.8
  387.8 1.0 copy-start.9
  388.8 3.7 copy-start.11
  388.8 3.7 copy-start.13
  388.8 3.7 copy-start.15
  388.8 3.7 copy-start.17
  (7 other events, 5.6 us)

commit v14 on v13

--- a/solution.py
+++ b/solution.py
@@ -1,4 +1,5 @@
 import functools
+import math
 
 import jax
 import jax.numpy as jnp
@@ -10,9 +11,8 @@
 DH = 128
 BLOCK = 64
 NBLEN = 128
-CHUNKS = 2
-DEPTH = 2
 ATTEND_WEIGHT = 24
+SHARE = 8
 F32 = jnp.float32
 BF16 = jnp.bfloat16
 LOG2E = 1.4426950408889634
@@ -168,11 +168,10 @@
     )
 
 
-def attend_kernel(seqs, parts, uses, *rest):
+def attend_kernel(seqs, parts, split, uses, *rest):
     half = seqs // 2
     rows_in, held, rest = rest[:parts], rest[parts], rest[parts + 1 :]
-    rows_out, near_out, rest = rest[:parts], rest[parts], rest[parts + 1 :]
-    far_out, (rows, made, sums) = rest[:half], rest[half:]
+    rows_out, kv_out, (rows, made, sums) = rest[:parts], rest[parts:-3], rest[-3:]
     scale = DH ** (-0.5)
     me, mine = lax.axis_index("enc"), lax.axis_index("seq")
 
@@ -233,124 +232,133 @@
         for n in range(2):
             piece = made[partner(mine, step, parts), n]
             rows_out[step][n] = pltpu.roll(piece, 2 * BLOCK - 1, 0).astype(BF16)
-    base = me - me % half
-    for step in range(half):
-        near_out[step] = sums[base + step].astype(BF16)
-        far_out[step][...] = sums[across(me, step, seqs)].astype(BF16)
-
-
-def attend(uses, rows_in, arrived):
+    if split:
+        base = me - me % half
+        for step in range(half):
+            kv_out[0][step] = sums[base + step].astype(BF16)
+            kv_out[1 + step][...] = sums[across(me, step, seqs)].astype(BF16)
+    else:
+        kv_out[0][...] = sums[...].astype(BF16)
+
+
+def attend(uses, rows_in, arrived, split):
     parts, part_rows = len(rows_in), rows_in[0].shape[1]
     seqs, _, _, chunk = arrived.shape
     half, heads = seqs // 2, chunk // DH
     rows_spec = pl.BlockSpec((2, part_rows, DH), lambda i: (0, 0, i))
-    far_spec = pl.BlockSpec((2, NBLEN, DH), lambda i: (0, 0, i))
+    shapes = [(seqs, 2, NBLEN)]
+    if split:
+        shapes = [(half, 2, NBLEN)] + [(2, NBLEN)] * half
+    kv_specs = [
+        pl.BlockSpec((*shape, DH), lambda i, n=len(shape): (0,) * n + (i,)) for shape in shapes
+    ]
     pairs = heads * parts * part_rows * 2 * NBLEN
     outs = pl.pallas_call(
-        functools.partial(attend_kernel, seqs, parts),
+        functools.partial(attend_kernel, seqs, parts, split),
         grid=(heads,),
         in_specs=[SCALARS]
         + [rows_spec] * parts
         + [pl.BlockSpec((seqs, 2, NBLEN, DH), lambda i: (0, 0, 0, i))],
-        out_specs=[rows_spec] * parts
-        + [pl.BlockSpec((half, 2, NBLEN, DH), lambda i: (0, 0, 0, i))]
-        + [far_spec] * half,
+        out_specs=[rows_spec] * parts + kv_specs,
         scratch_shapes=[
             pltpu.VMEM((parts + 1, 2, part_rows, DH), F32),
             pltpu.VMEM((parts + 1, 2, part_rows, DH), F32),
             pltpu.VMEM((seqs, 2, NBLEN, DH), F32),
         ],
         out_shape=[in_hbm((2, part_rows, chunk))] * parts
-        + [in_hbm((half, 2, NBLEN, chunk))]
-        + [in_hbm((2, NBLEN, chunk))] * half,
+        + [in_hbm((*shape, chunk)) for shape in shapes],
         compiler_params=PARAMS,
         cost_estimate=cost(
             8 * (seqs + parts) * NBLEN * chunk, ATTEND_WEIGHT * 12 * DH * pairs, pairs
         ),
         name="attend_blocks",
     )(uses, *rows_in, arrived)
-    return outs[:parts], outs[parts], outs[parts + 1 :]
-
-
-def owner_kernel(seqs, lists, near_ref, *rest):
+    return outs[:parts], outs[parts:]
+
+
+def owner_kernel(seqs, lists, *rest):
     half = seqs // 2
-    far_refs, out_ref, acc = rest[:half], rest[-2], rest[-1]
+    first_ref, out_ref, acc = rest[0], rest[-2], rest[-1]
     me = lax.axis_index("enc")
     base = me - me % half
     acc[...] = jnp.zeros_like(acc)
-    for step in range(half):
-        acc[lists[0, base + step, 0]] += near_ref[step].astype(F32)
-        acc[lists[0, across(me, step, seqs), 0]] += far_refs[step][...].astype(F32)
+    if first_ref.shape[0] == seqs:
+        for seq in range(seqs):
+            acc[lists[0, seq, 0]] += first_ref[seq].astype(F32)
+    else:
+        for step in range(half):
+            acc[lists[0, base + step, 0]] += first_ref[step].astype(F32)
+            acc[lists[0, across(me, step, seqs), 0]] += rest[1 + step][...].astype(F32)
     out_ref[...] = acc[...].astype(BF16)
 
 
-def owner_sum(h, send_lists, near, far, shape, so_far):
-    half = len(far)
-    chunk = near.shape[-1]
-    wide = min(chunk, 256)
-    steps = chunk // wide
+def owner_sum(first, send_lists, back, shape, so_far):
+    seqs = send_lists.shape[1]
+    chunk = back[0].shape[-1]
+    wide = math.gcd(math.gcd(first, chunk), 256)
+    skip, steps = first // wide, chunk // wide
     extra = [] if so_far is None else [so_far]
+    specs = [
+        pl.BlockSpec((*array.shape[:-1], wide), lambda i, n=array.ndim - 1: (0,) * n + (i,))
+        for array in back
+    ]
     return pl.pallas_call(
-        functools.partial(owner_kernel, 2 * half),
+        functools.partial(owner_kernel, seqs),
         grid=(steps,),
-        in_specs=[SCALARS, pl.BlockSpec((half, 2, NBLEN, wide), lambda i: (0, 0, 0, i))]
-        + [pl.BlockSpec((2, NBLEN, wide), lambda i: (0, 0, i))] * half
-        + [ANYWHERE] * len(extra),
+        in_specs=[SCALARS] + specs + [ANYWHERE] * len(extra),
         out_specs=pl.BlockSpec(
-            (shape[0], 2, NBLEN, wide), lambda i: (0, 0, 0, h * steps + i)
+            (shape[0], 2, NBLEN, wide), lambda i: (0, 0, 0, skip + i)
         ),
         scratch_shapes=[pltpu.VMEM((shape[0], 2, NBLEN, wide), F32)],
         out_shape=in_hbm(shape),
-        input_output_aliases={half + 2: 0} if extra else {},
-        compiler_params=PARAMS,
-        cost_estimate=cost(4 * (2 * half + shape[0]) * NBLEN * chunk, 4 * half * NBLEN * chunk),
+        input_output_aliases={len(back) + 1: 0} if extra else {},
+        compiler_params=PARAMS,
+        cost_estimate=cost(4 * (seqs + shape[0]) * NBLEN * chunk, 2 * seqs * NBLEN * chunk),
         name="owner_sum",
-    )(send_lists, near, *far, *extra)
-
-
-def swap_far(pieces, done):
+    )(send_lists, *back, *extra)
+
+
+def swap_far(pieces):
     half = len(pieces)
-    there = [[half + (i + step) % half for i in range(half)] for step in range(half)]
     got = []
     for step, piece in enumerate(pieces):
-        if len(done) >= DEPTH:
-            piece = after(piece, done[-DEPTH])
-        pairs = list(enumerate(there[step])) + [(peer, i) for i, peer in enumerate(there[step])]
+        there = [half + (i + step) % half for i in range(half)]
+        pairs = list(enumerate(there)) + [(peer, i) for i, peer in enumerate(there)]
         got.append(lax.ppermute(piece, "enc", pairs))
-        done.append(got[-1])
     return got
 
 
 def local(seqs, parts, queries, kv_pool, send_lists, block_slots, grad_context):
     width = kv_pool.shape[-1]
-    chunks = min(CHUNKS, width // DH)
-    chunk = width // chunks
-    firsts = [h * chunk for h in range(chunks)]
+    cut = (SHARE * width // DH // 16) * DH
+    bounds = [(0, cut), (cut, width - cut)]
+    firsts = [first for first, _ in bounds]
 
     arrived, rows = [], []
-    for first in firsts:
+    for first, chunk in bounds:
         picked = pick(first, chunk, send_lists, kv_pool)
         send_lists, queries = after((send_lists, queries), picked)
         if rows:
             picked = after(picked, rows)
         arrived.append(swap_pool(picked))
         if not rows:
-            for start in firsts:
-                packed = pack(start, chunk, queries, grad_context, width, parts)
+            for start, size in bounds:
+                packed = pack(start, size, queries, grad_context, width, parts)
                 rows.append(swap_rows(packed))
-    done, returns, token_parts = [], [], []
-    for h in range(chunks):
-        rows_out, near, far = attend(block_slots, rows[h], arrived[h])
-        far = swap_far(far, done)
-        if h > 0:
-            near = after(near, done[seqs // 2])
-        returns.append((swap_near(near, seqs), far))
-        token_parts.append(swap_rows(rows_out))
-        block_slots = after(block_slots, (token_parts[-1], far[:DEPTH]))
+
+    rows_out, (near, *far) = attend(block_slots, rows[0], arrived[0], True)
+    far = swap_far(far)
+    returns = [[swap_near(near, seqs), *far]]
+    token_parts = [swap_rows(rows_out)]
+    block_slots = after(block_slots, token_parts[0])
+    rows_out, (whole,) = attend(block_slots, rows[1], arrived[1], False)
+    token_parts.append(swap_rows(rows_out))
+    returns.append([swap_pool(after(whole, far))])
+
     context, grad_queries = unpack(token_parts, firsts, width, queries.shape)
     pool_grads = None
-    for h in range(chunks):
-        pool_grads = owner_sum(h, send_lists, *returns[h], kv_pool.shape, pool_grads)
+    for first, back in zip(firsts, returns):
+        pool_grads = owner_sum(first, send_lists, back, kv_pool.shape, pool_grads)
     return (context, grad_queries, pool_grads)
 
 

time: 436 us -> 398 us (0.913)
  waiting for transfers between devices: 304 us -> 253 us
  starting transfers between devices: 41 us -> 54.9 us
    ppermute x8 -> x4, waiting for transfers between devices: 228 us -> 9.64 us  [swap_far(): got.append(lax.ppermute(piece, 'enc', pairs))]
    all_to_all x2 -> x3, waiting for transfers between devices: 39.3 us -> 176 us  [swap_pool(): return lax.all_to_all(array, 'enc', split_axis=0, concat_axis=0, tiled=True)]
    ppermute x12, waiting for transfers between devices: 37 us -> 67.3 us  [exchange(): return lax.ppermute(array, axis, pairs)]
    ppermute x8 -> x4, starting transfers between devices: 6.01 us -> 17 us  [swap_far(): got.append(lax.ppermute(piece, 'enc', pairs))]
    all_to_all x2 -> x3, starting transfers between devices: 13.9 us -> 21.3 us  [swap_pool(): return lax.all_to_all(array, 'enc', split_axis=0, concat_axis=0, tiled=True)]
    all_to_all x2 -> x1, starting transfers between devices: 12.3 us -> 7.74 us  [swap_near(): lax.all_to_all(array, 'enc', split_axis=0, concat_axis=0, axis_index_grou...]
    unnamed x64 -> x46, local copies, waits for them, and re-layouts: 19.1 us -> 14.8 us
  transfers between devices with their start and end apart: 24 -> 20, of which waited for: 12 -> 12; matrix products, arithmetic and copies ran while one was open for 0% -> 0% of each run, Pallas kernels for 14% -> 15%
where the time goes in v14:
time: 398 us; the launch traced here: 393 us
  waiting for transfers between devices  253 us (64%)
  Pallas kernels  69.5 us (17%)
  starting transfers between devices  54.9 us (14%)
  local copies, waits for them, and re-layouts  15.1 us (4%)
    all_to_all x3, waiting for transfers between devices, swap_pool(): return lax.all_to_all(array, 'enc', split_axis=0, concat_axis=0, tiled=True)  176 us
    ppermute x12, waiting for transfers between devices, exchange(): return lax.ppermute(array, axis, pairs)  67.3 us
    pallas_call x2, Pallas kernels, attend(): pl.pallas_call(functools.partial(attend_kernel, seqs, parts, split), grid...  45.2 us
    all_to_all x3, starting transfers between devices, swap_pool(): return lax.all_to_all(array, 'enc', split_axis=0, concat_axis=0, tiled=True)  21.3 us
    ppermute x4, starting transfers between devices, swap_far(): got.append(lax.ppermute(piece, 'enc', pairs))  17 us
    unnamed x46, local copies, waits for them, and re-layouts  14.8 us
    ppermute x4, waiting for transfers between devices, swap_far(): got.append(lax.ppermute(piece, 'enc', pairs))  9.64 us
    pallas_call x2, Pallas kernels, owner_sum(): pl.pallas_call(functools.partial(owner_kernel, seqs), grid=(steps,), in_s...  9.25 us
  transfers between devices with their start and end apart: 20, of which 12 were waited for; matrix products, arithmetic and copies ran while one was open for 0% of the time, Pallas kernels for 15%

profile of v14, /device:TPU:15, one launch (start us, length us, event | category | flops | bytes accessed | tf_op | source)
XLA Modules:
  0.0 393.1 jit_solution(5870391675783260787)
XLA Ops:
  0.6 0.7 copy.9.lists
  1.4 4.2 %pick_entries.2 = bf16[8,2,128,1024]{3,2,1,0:T(8,128)(2,1)} custom-call(s32[1,8,1]{2,1,0:T(8,128)S(1)} %copy.9.lists, bf16[4,2,128,2048]{3,2,1,0:T(8,128)(2,1)} %pool_ref.3), custom_call_target="tpu_custom_call" | custom-call | bytes 8388608 | tf_op jit(solution)/shard_map/pick_entries/pallas_call | solution.py:152
  5.6 5.8 %all-to-all-start = ((bf16[8,2,128,1024]{3,2,1,0:T(8,128)(2,1)}), bf16[8,2,128,1024]{3,2,1,0:T(8,128)(2,1)}, u32[]{:S(2)}, u32[]{:S(2)}) async-start(bf16[8,2,128,1024]{3,2,1,0:T(8,128)(2,1)} %pick_entries.2), calls=%async_computation | async-start | bytes 8388608 | tf_op jit(solution)/shard_map/all_to_all | solution.py:53
  11.3 1.6 copy-done.1
  12.9 1.5 pack_rows.3
  14.5 0.3 collective-permute-start.6
  15.0 2.2 collective-permute-start.8
  17.2 1.6 pack_rows.2
  18.8 0.3 collective-permute-start
  19.3 8.6 %collective-permute-done.6.rest_1_ = bf16[2,128,1024]{2,1,0:T(8,128)(2,1)S(1)} collective-permute-done((bf16[2,128,1024]{2,1,0:T(8,128)(2,1)}, bf16[2,128,1024]{2,1,0:T(8,128)(2,1)S(1)}, u32[]{:S(2)}, u32[]{:S(2)}) %collective-permute-start.6) | collective-permute-done | bytes 524320 | tf_op jit(solution)/shard_map/ppermute | solution.py:30
  27.9 0.8 copy-done.11
  29.0 4.2 %pick_entries.3 = bf16[8,2,128,1024]{3,2,1,0:T(8,128)(2,1)} custom-call(s32[1,8,1]{2,1,0:T(8,128)S(1)} %copy.11.lists, bf16[4,2,128,2048]{3,2,1,0:T(8,128)(2,1)} %pool_ref.3), custom_call_target="tpu_custom_call" | custom-call | bytes 8388608 | tf_op jit(solution)/shard_map/pick_entries/pallas_call | solution.py:152
  33.3 5.9 %collective-permute-done.8.rest_3_ = bf16[2,128,1024]{2,1,0:T(8,128)(2,1)S(1)} collective-permute-done((bf16[2,128,1024]{2,1,0:T(8,128)(2,1)}, bf16[2,128,1024]{2,1,0:T(8,128)(2,1)S(1)}, u32[]{:S(2)}, u32[]{:S(2)}) %collective-permute-start.8) | collective-permute-done | bytes 524320 | tf_op jit(solution)/shard_map/ppermute | solution.py:30
  39.1 11.4 %collective-permute-done.rest_1_ = bf16[2,128,1024]{2,1,0:T(8,128)(2,1)S(1)} collective-permute-done((bf16[2,128,1024]{2,1,0:T(8,128)(2,1)}, bf16[2,128,1024]{2,1,0:T(8,128)(2,1)S(1)}, u32[]{:S(2)}, u32[]{:S(2)}) %collective-permute-start) | collective-permute-done | bytes 524320 | tf_op jit(solution)/shard_map/ppermute | solution.py:30
  50.5 11.1 %collective-permute-done.2.rest_3_ = bf16[2,128,1024]{2,1,0:T(8,128)(2,1)S(1)} collective-permute-done((bf16[2,128,1024]{2,1,0:T(8,128)(2,1)}, bf16[2,128,1024]{2,1,0:T(8,128)(2,1)S(1)}, u32[]{:S(2)}, u32[]{:S(2)}) %collective-permute-start.2) | collective-permute-done | bytes 524320 | tf_op jit(solution)/shard_map/ppermute | solution.py:30
  61.7 0.8 copy-done.18
  62.5 39.3 %all-to-all-done.rest_4_ = bf16[8,2,128,1024]{3,2,1,0:T(8,128)(2,1)} async-done(((bf16[8,2,128,1024]{3,2,1,0:T(8,128)(2,1)}), bf16[8,2,128,1024]{3,2,1,0:T(8,128)(2,1)}, u32[]{:S(2)}, u32[]{:S(2)}) %all-to-all-start) | async-done | bytes 4194336 | tf_op jit(solution)/shard_map/all_to_all | solution.py:53
  101.8 8.1 %all-to-all-start.1 = ((bf16[8,2,128,1024]{3,2,1,0:T(8,128)(2,1)}), bf16[8,2,128,1024]{3,2,1,0:T(8,128)(2,1)}, u32[]{:S(2)}, u32[]{:S(2)}) async-start(bf16[8,2,128,1024]{3,2,1,0:T(8,128)(2,1)} %pick_entries.3), calls=%async_computation.1 | async-start | bytes 8388608 | tf_op jit(solution)/shard_map/all_to_all | solution.py:53
  110.0 1.0 copy-done.19
  111.0 22.6 %attend_blocks.2 = (bf16[2,128,1024]{2,1,0:T(8,128)(2,1)}, bf16[2,128,1024]{2,1,0:T(8,128)(2,1)}, bf16[2,128,1024]{2,1,0:T(8,128)(2,1)}, bf16[2,128,1024]{2,1,0:...) custom-call(s32[1,8,2]{2,1,0:T(8,128)S(1)} %copy.10.uses, ...), custom_call_target="tpu_custom_call" | custom-call | flops 38654705664 | bytes 12582912 | tf_op jit(solution)/shard_map/attend_blocks/pallas_call | solution.py:256
  133.6 0.3 collective-permute-start.3
  134.2 2.2 collective-permute-start.5
  136.3 2.1 collective-permute-start.12
  138.8 8.4 %collective-permute-done.3.refs_1_ = bf16[2,128,1024]{2,1,0:T(8,128)(2,1)S(1)} collective-permute-done((bf16[2,128,1024]{2,1,0:T(8,128)(2,1)}, bf16[2,128,1024]{2,1,0:T(8,128)(2,1)S(1)}, u32[]{:S(2)}, u32[]{:S(2)}) %collective-permute-start.3) | collective-permute-done | bytes 524320 | tf_op jit(solution)/shard_map/ppermute | solution.py:30
  147.2 1.2 collective-permute-start.14
  148.4 0.8 copy-done.3
  149.2 13.4 %collective-permute-start.15 = (bf16[2,128,1024]{2,1,0:T(8,128)(2,1)}, bf16[2,128,1024]{2,1,0:T(8,128)(2,1)}, u32[]{:S(2)}, u32[]{:S(2)}) collective-permute-start(bf16[2,128,1024]{2,1,0:T(8,128)(2,1)} %get-tuple-element.60), channel_id=1, source_target_pairs={{0,28},{4,16},{8,20},{12,24},{28,0},{16,4},{20,8},{24,12},{1,29},{... | collective-permute-start | bytes 1572872 | tf_op jit(solution)/shard_map/ppermute | solution.py:327
  162.5 0.8 copy-done.5
  163.4 81.8 %all-to-all-done.1.rest_4_ = bf16[8,2,128,1024]{3,2,1,0:T(8,128)(2,1)} async-done(((bf16[8,2,128,1024]{3,2,1,0:T(8,128)(2,1)}), bf16[8,2,128,1024]{3,2,1,0:T(8,128)(2,1)}, u32[]{:S(2)}, u32[]{:S(2)}) %all-to-all-start.1) | async-done | bytes 4194336 | tf_op jit(solution)/shard_map/all_to_all | solution.py:53
  245.3 7.7 %all-to-all-start.3 = ((bf16[4,2,128,1024]{3,2,1,0:T(8,128)(2,1)}), bf16[4,2,128,1024]{3,2,1,0:T(8,128)(2,1)S(1)}, u32[]{:S(2)}, u32[]{:S(2)}) async-start(bf16[4,2,128,1024]{3,2,1,0:T(8,128)(2,1)} %get-tuple-element.62), calls=%async_computation.3 | async-start | bytes 4194304 | tf_op jit(solution)/shard_map/all_to_all | solution.py:42
  253.0 1.0 copy-done.10
  254.1 1.0 copy-done.12
  255.1 1.0 copy-done.14
  256.2 1.0 copy-done.16
  257.2 22.6 %attend_blocks.3 = (bf16[2,128,1024]{2,1,0:T(8,128)(2,1)}, bf16[2,128,1024]{2,1,0:T(8,128)(2,1)}, bf16[2,128,1024]{2,1,0:T(8,128)(2,1)}, bf16[2,128,1024]{2,1,0:T(8,128)(2,1)}, bf16[8,2,128,1024]{3,2,1,0:T(8,128)(2,1)}) custom-call(s32[1,8,2]{2,1,0:T(8,128)S(1)} %copy.12.uses, bf16[2,128,1024]{2,1,0:T(8,128)(2,1)S(1)} %copy-done.10, ...), custom_call_target="tpu_custom_call" | custom-call | flops 38654705664 | bytes 12582912 | tf_op jit(solution)/shard_map/attend_blocks/pallas_call | solution.py:256
  279.8 0.8 copy-done.8
  280.8 9.5 %collective-permute-done.15.rest_4_ = bf16[2,128,1024]{2,1,0:T(8,128)(2,1)} collective-permute-done((bf16[2,128,1024]{2,1,0:T(8,128)(2,1)}, bf16[2,128,1024]{2,1,0:T(8,128)(2,1)}, u32[]{:S(2)}, u32[]{:S(2)}) %collective-permute-start.15) | collective-permute-done | bytes 524320 | tf_op jit(solution)/shard_map/ppermute | solution.py:327
  290.3 7.4 %all-to-all-start.2 = ((bf16[8,2,128,1024]{3,2,1,0:T(8,128)(2,1)}), bf16[8,2,128,1024]{3,2,1,0:T(8,128)(2,1)}, u32[]{:S(2)}, u32[]{:S(2)}) async-start(bf16[8,2,128,1024]{3,2,1,0:T(8,128)(2,1)} %get-tuple-element.61), calls=%async_computation.2 | async-start | bytes 8388608 | tf_op jit(solution)/shard_map/all_to_all | solution.py:53
  298.2 2.2 collective-permute-start.11
  300.5 10.7 %collective-permute-done.9.refs_5_ = bf16[2,128,1024]{2,1,0:T(8,128)(2,1)} collective-permute-done((bf16[2,128,1024]{2,1,0:T(8,128)(2,1)}, bf16[2,128,1024]{2,1,0:T(8,128)(2,1)}, u32[]{:S(2)}, u32[]{:S(2)}) %collective-permute-start.9) | collective-permute-done | bytes 524320 | tf_op jit(solution)/shard_map/ppermute | solution.py:30
  311.2 11.2 %collective-permute-done.11.refs_7_ = bf16[2,128,1024]{2,1,0:T(8,128)(2,1)} collective-permute-done((bf16[2,128,1024]{2,1,0:T(8,128)(2,1)}, bf16[2,128,1024]{2,1,0:T(8,128)(2,1)}, u32[]{:S(2)}, u32[]{:S(2)}) %collective-permute-start.11) | collective-permute-done | bytes 524320 | tf_op jit(solution)/shard_map/ppermute | solution.py:30
  322.4 1.0 copy-done.4
  323.5 1.0 copy-done.6
  324.5 1.0 copy-done.7
  325.6 3.5 unpack_rows.1
  329.1 4.5 %owner_sum.2.rest_1_ = bf16[4,2,128,2048]{3,2,1,0:T(8,128)(2,1)} custom-call(s32[1,8,1]{2,1,0:T(8,128)S(1)} %copy.14.lists, bf16[4,2,128,1024]{3,2,1,0:T(8,128)(2,1)S(1)} %all-to-all-done.3.rest_0_, bf16[2,128,1024]{2,1,0:T(8,128)(2,1)S(1)} %copy-done.9, bf16[2,128,1024]{2,1,0:T(8,128)(2,1)} %collective-permute-done.13.rest_2_, ...), custom_call_target="tpu_custom_call" | custom-call | flops 2097152 | bytes 6291456 | tf_op jit(solution)/shard_map/owner_sum/pallas_call | solution.py:305
  333.6 54.7 %all-to-all-done.2.rest_0_ = bf16[8,2,128,1024]{3,2,1,0:T(8,128)(2,1)} async-done(((bf16[8,2,128,1024]{3,2,1,0:T(8,128)(2,1)}), bf16[8,2,128,1024]{3,2,1,0:T(8,128)(2,1)}, u32[]{:S(2)}, u32[]{:S(2)}) %all-to-all-start.2) | async-done | bytes 4194336 | tf_op jit(solution)/shard_map/all_to_all | solution.py:53
  388.3 4.7 %owner_sum.3 = bf16[4,2,128,2048]{3,2,1,0:T(8,128)(2,1)} custom-call(s32[1,8,1]{2,1,0:T(8,128)S(1)} %copy.14.lists, bf16[8,2,128,1024]{3,2,1,0:T(8,128)(2,1)} %all-to-all-done.2.rest_0_, bf16[4,2,128,2048]{3,2,1,0:T(8,128)(2,1)} %owner_sum.2.rest_1_), custom_call_target="tpu_custom_call", output_to_operand_aliasing={{}: (2, {})} | custom-call | flops 2097152 | bytes 6291456 | tf_op jit(solution)/shard_map/owner_sum/pallas_call | solution.py:305
  (50 shorter events, 2.2 us)
Async XLA Ops:
  5.5 5.8 %copy-start = (bf16[1,128,8192]{2,1,0:T(8,128)(2,1)S(1)}, bf16[1,128,8192]{2,1,0:T(8,128)(2,1)}, u32[]{:S(2)}) copy-start(bf16[1,128,8192]{2,1,0:T(8,128)(2,1)} %q_ref.1) | copy-start | bytes 6291460
  5.6 96.2 %all-to-all-start = ((bf16[8,2,128,1024]{3,2,1,0:T(8,128)(2,1)}), bf16[8,2,128,1024]{3,2,1,0:T(8,128)(2,1)}, u32[]{:S(2)}, u32[]{:S(2)}) async-start(bf16[8,2,128,1024]{3,2,1,0:T(8,128)(2,1)} %pick_entries.2), calls=%async_computation | async-start | bytes 8388608 | tf_op jit(solution)/shard_map/all_to_all | solution.py:53
  11.3 1.6 copy-start.1
  12.9 16.0 %copy-start.20 = (s32[1,8,1]{1,2,0:T(1,128)S(1)}, s32[1,8,1]{1,2,0:T(1,128)}, u32[]{:S(2)}) copy-start(s32[1,8,1]{1,2,0:T(1,128)} %param.7) | copy-start | bytes 100
  14.5 13.4 %collective-permute-start.6 = (bf16[2,128,1024]{2,1,0:T(8,128)(2,1)}, bf16[2,128,1024]{2,1,0:T(8,128)(2,1)S(1)}, u32[]{:S(2)}, u32[]{:S(2)}) collective-permute-start(bf16[2,128,1024]{2,1,0:T(8,128)(2,1)} %get-tuple-element.44), channel_id=1, source_target_pairs={{0,1},{1,0},{2,3},{3,2},{4,5},{5,4},{6,7},{7,6},{8,9},{9,8},{10,11... | collective-permute-start | bytes 1572872 | tf_op jit(solution)/shard_map/ppermute | solution.py:30
  14.8 18.4 %collective-permute-start.7 = (bf16[2,128,1024]{2,1,0:T(8,128)(2,1)}, bf16[2,128,1024]{2,1,0:T(8,128)(2,1)S(1)}, u32[]{:S(2)}, u32[]{:S(2)}) collective-permute-start(bf16[2,128,1024]{2,1,0:T(8,128)(2,1)} %get-tuple-element.45), channel_id=1, source_target_pairs={{0,2},{1,3},{2,0},{3,1},{4,6},{5,7},{6,4},{7,5},{8,10},{9,11},{10,... | collective-permute-start | bytes 1572872 | tf_op jit(solution)/shard_map/ppermute | solution.py:30
  15.0 24.1 %collective-permute-start.8 = (bf16[2,128,1024]{2,1,0:T(8,128)(2,1)}, bf16[2,128,1024]{2,1,0:T(8,128)(2,1)S(1)}, u32[]{:S(2)}, u32[]{:S(2)}) collective-permute-start(bf16[2,128,1024]{2,1,0:T(8,128)(2,1)} %get-tuple-element.46), channel_id=1, source_target_pairs={{0,3},{1,2},{2,1},{3,0},{4,7},{5,6},{6,5},{7,4},{8,11},{9,10},{10,... | collective-permute-start | bytes 1572872 | tf_op jit(solution)/shard_map/ppermute | solution.py:30
  18.8 31.8 %collective-permute-start = (bf16[2,128,1024]{2,1,0:T(8,128)(2,1)}, bf16[2,128,1024]{2,1,0:T(8,128)(2,1)S(1)}, u32[]{:S(2)}, u32[]{:S(2)}) collective-permute-start(bf16[2,128,1024]{2,1,0:T(8,128)(2,1)} %get-tuple-element.35), channel_id=1, source_target_pairs={{0,1},{1,0},{2,3},{3,2},{4,5},{5,4},{6,7},{7,6},{8,9},{9,8},{10,11... | collective-permute-start | bytes 1572872 | tf_op jit(solution)/shard_map/ppermute | solution.py:30
  19.1 31.4 %collective-permute-start.1 = (bf16[2,128,1024]{2,1,0:T(8,128)(2,1)}, bf16[2,128,1024]{2,1,0:T(8,128)(2,1)S(1)}, u32[]{:S(2)}, u32[]{:S(2)}) collective-permute-start(bf16[2,128,1024]{2,1,0:T(8,128)(2,1)} %get-tuple-element.36), channel_id=1, source_target_pairs={{0,2},{1,3},{2,0},{3,1},{4,6},{5,7},{6,4},{7,5},{8,10},{9,11},{10,... | collective-permute-start | bytes 1572872 | tf_op jit(solution)/shard_map/ppermute | solution.py:30
  27.9 0.8 copy-start.11
  28.7 32.9 %collective-permute-start.2 = (bf16[2,128,1024]{2,1,0:T(8,128)(2,1)}, bf16[2,128,1024]{2,1,0:T(8,128)(2,1)S(1)}, u32[]{:S(2)}, u32[]{:S(2)}) collective-permute-start(bf16[2,128,1024]{2,1,0:T(8,128)(2,1)} %get-tuple-element.37), channel_id=1, source_target_pairs={{0,3},{1,2},{2,1},{3,0},{4,7},{5,6},{6,5},{7,4},{8,11},{9,10},{10,... | collective-permute-start | bytes 1572872 | tf_op jit(solution)/shard_map/ppermute | solution.py:30
  33.3 68.5 %copy-start.13 = (bf16[2,128,1024]{2,1,0:T(8,128)(2,1)}, bf16[2,128,1024]{2,1,0:T(8,128)(2,1)S(1)}, u32[]{:S(2)}) copy-start(bf16[2,128,1024]{2,1,0:T(8,128)(2,1)S(1)} %collective-permute-done.7.rest_2_) | copy-start | bytes 1572868
  39.1 62.7 %copy-start.15 = (bf16[2,128,1024]{2,1,0:T(8,128)(2,1)}, bf16[2,128,1024]{2,1,0:T(8,128)(2,1)S(1)}, u32[]{:S(2)}) copy-start(bf16[2,128,1024]{2,1,0:T(8,128)(2,1)S(1)} %collective-permute-done.8.rest_3_) | copy-start | bytes 1572868
  61.7 0.8 copy-start.18
  62.5 47.5 %copy-start.21 = (s32[1,8,2]{1,2,0:T(2,128)S(1)}, s32[1,8,2]{1,2,0:T(2,128)}, u32[]{:S(2)}) copy-start(s32[1,8,2]{1,2,0:T(2,128)} %param.8) | copy-start | bytes 196
  62.5 47.5 %copy-start.17 = (bf16[2,128,1024]{2,1,0:T(8,128)(2,1)S(1)}, bf16[2,128,1024]{2,1,0:T(8,128)(2,1)}, u32[]{:S(2)}) copy-start(bf16[2,128,1024]{2,1,0:T(8,128)(2,1)} %get-tuple-element.34.rest_0_) | copy-start | bytes 1572868
  101.8 143.5 %all-to-all-start.1 = ((bf16[8,2,128,1024]{3,2,1,0:T(8,128)(2,1)}), bf16[8,2,128,1024]{3,2,1,0:T(8,128)(2,1)}, u32[]{:S(2)}, u32[]{:S(2)}) async-start(bf16[8,2,128,1024]{3,2,1,0:T(8,128)(2,1)} %pick_entries.3), calls=%async_computation.1 | async-start | bytes 8388608 | tf_op jit(solution)/shard_map/all_to_all | solution.py:53
  110.0 1.0 copy-start.19
  133.6 13.5 %collective-permute-start.3 = (bf16[2,128,1024]{2,1,0:T(8,128)(2,1)}, bf16[2,128,1024]{2,1,0:T(8,128)(2,1)S(1)}, u32[]{:S(2)}, u32[]{:S(2)}) collective-permute-start(bf16[2,128,1024]{2,1,0:T(8,128)(2,1)} %get-tuple-element.39), channel_id=1, source_target_pairs={{0,1},{1,0},{2,3},{3,2},{4,5},{5,4},{6,7},{7,6},{8,9},{9,8},{10,11... | collective-permute-start | bytes 1572872 | tf_op jit(solution)/shard_map/ppermute | solution.py:30
  134.0 14.4 %collective-permute-start.4 = (bf16[2,128,1024]{2,1,0:T(8,128)(2,1)}, bf16[2,128,1024]{2,1,0:T(8,128)(2,1)S(1)}, u32[]{:S(2)}, u32[]{:S(2)}) collective-permute-start(bf16[2,128,1024]{2,1,0:T(8,128)(2,1)} %get-tuple-element.40), channel_id=1, source_target_pairs={{0,2},{1,3},{2,0},{3,1},{4,6},{5,7},{6,4},{7,5},{8,10},{9,11},{10,... | collective-permute-start | bytes 1572872 | tf_op jit(solution)/shard_map/ppermute | solution.py:30
  134.2 28.4 %collective-permute-start.5 = (bf16[2,128,1024]{2,1,0:T(8,128)(2,1)}, bf16[2,128,1024]{2,1,0:T(8,128)(2,1)S(1)}, u32[]{:S(2)}, u32[]{:S(2)}) collective-permute-start(bf16[2,128,1024]{2,1,0:T(8,128)(2,1)} %get-tuple-element.41), channel_id=1, source_target_pairs={{0,3},{1,2},{2,1},{3,0},{4,7},{5,6},{6,5},{7,4},{8,11},{9,10},{10,... | collective-permute-start | bytes 1572872 | tf_op jit(solution)/shard_map/ppermute | solution.py:30
  136.3 143.5 %collective-permute-start.12 = (bf16[2,128,1024]{2,1,0:T(8,128)(2,1)}, bf16[2,128,1024]{2,1,0:T(8,128)(2,1)S(1)}, u32[]{:S(2)}, u32[]{:S(2)}) collective-permute-start(bf16[2,128,1024]{2,1,0:T(8,128)(2,1)} %get-tuple-element.57), channel_id=1, source_target_pairs={{0,16},{4,20},{8,24},{12,28},{16,0},{20,4},{24,8},{28,12},{1,17},{... | collective-permute-start | bytes 1572872 | tf_op jit(solution)/shard_map/ppermute | solution.py:327
  138.5 142.2 %collective-permute-start.13 = (bf16[2,128,1024]{2,1,0:T(8,128)(2,1)}, bf16[2,128,1024]{2,1,0:T(8,128)(2,1)}, u32[]{:S(2)}, u32[]{:S(2)}) collective-permute-start(bf16[2,128,1024]{2,1,0:T(8,128)(2,1)} %get-tuple-element.58), channel_id=1, source_target_pairs={{0,20},{4,24},{8,28},{12,16},{20,0},{24,4},{28,8},{16,12},{1,21},{... | collective-permute-start | bytes 1572872 | tf_op jit(solution)/shard_map/ppermute | solution.py:327
  147.2 133.6 %collective-permute-start.14 = (bf16[2,128,1024]{2,1,0:T(8,128)(2,1)}, bf16[2,128,1024]{2,1,0:T(8,128)(2,1)}, u32[]{:S(2)}, u32[]{:S(2)}) collective-permute-start(bf16[2,128,1024]{2,1,0:T(8,128)(2,1)} %get-tuple-element.59), channel_id=1, source_target_pairs={{0,24},{4,28},{8,16},{12,20},{24,0},{28,4},{16,8},{20,12},{1,25},{... | collective-permute-start | bytes 1572872 | tf_op jit(solution)/shard_map/ppermute | solution.py:327
  148.4 0.8 copy-start.3
  149.2 141.1 %collective-permute-start.15 = (bf16[2,128,1024]{2,1,0:T(8,128)(2,1)}, bf16[2,128,1024]{2,1,0:T(8,128)(2,1)}, u32[]{:S(2)}, u32[]{:S(2)}) collective-permute-start(bf16[2,128,1024]{2,1,0:T(8,128)(2,1)} %get-tuple-element.60), channel_id=1, source_target_pairs={{0,28},{4,16},{8,20},{12,24},{28,0},{16,4},{20,8},{24,12},{1,29},{... | collective-permute-start | bytes 1572872 | tf_op jit(solution)/shard_map/ppermute | solution.py:327
  162.5 0.8 copy-start.5
  245.3 45.0 %all-to-all-start.3 = ((bf16[4,2,128,1024]{3,2,1,0:T(8,128)(2,1)}), bf16[4,2,128,1024]{3,2,1,0:T(8,128)(2,1)S(1)}, u32[]{:S(2)}, u32[]{:S(2)}) async-start(bf16[4,2,128,1024]{3,2,1,0:T(8,128)(2,1)} %get-tuple-element.62), calls=%async_computation.3 | async-start | bytes 4194304 | tf_op jit(solution)/shard_map/all_to_all | solution.py:42
  253.0 1.0 copy-start.10
  254.1 1.0 copy-start.12
  255.1 1.0 copy-start.14
  256.2 1.0 copy-start.16
  279.8 0.8 copy-start.8
  290.3 32.1 %copy-start.2 = (bf16[2,128,1024]{2,1,0:T(8,128)(2,1)S(1)}, bf16[2,128,1024]{2,1,0:T(8,128)(2,1)}, u32[]{:S(2)}) copy-start(bf16[2,128,1024]{2,1,0:T(8,128)(2,1)} %get-tuple-element.38.refs_0_) | copy-start | bytes 1572868
  290.3 98.0 %all-to-all-start.2 = ((bf16[8,2,128,1024]{3,2,1,0:T(8,128)(2,1)}), bf16[8,2,128,1024]{3,2,1,0:T(8,128)(2,1)}, u32[]{:S(2)}, u32[]{:S(2)}) async-start(bf16[8,2,128,1024]{3,2,1,0:T(8,128)(2,1)} %get-tuple-element.61), calls=%async_computation.2 | async-start | bytes 8388608 | tf_op jit(solution)/shard_map/all_to_all | solution.py:53
  297.7 13.5 %collective-permute-start.9 = (bf16[2,128,1024]{2,1,0:T(8,128)(2,1)}, bf16[2,128,1024]{2,1,0:T(8,128)(2,1)}, u32[]{:S(2)}, u32[]{:S(2)}) collective-permute-start(bf16[2,128,1024]{2,1,0:T(8,128)(2,1)} %get-tuple-element.50), channel_id=1, source_target_pairs={{0,1},{1,0},{2,3},{3,2},{4,5},{5,4},{6,7},{7,6},{8,9},{9,8},{10,11... | collective-permute-start | bytes 1572872 | tf_op jit(solution)/shard_map/ppermute | solution.py:30
  298.0 13.2 %collective-permute-start.10 = (bf16[2,128,1024]{2,1,0:T(8,128)(2,1)}, bf16[2,128,1024]{2,1,0:T(8,128)(2,1)}, u32[]{:S(2)}, u32[]{:S(2)}) collective-permute-start(bf16[2,128,1024]{2,1,0:T(8,128)(2,1)} %get-tuple-element.51), channel_id=1, source_target_pairs={{0,2},{1,3},{2,0},{3,1},{4,6},{5,7},{6,4},{7,5},{8,10},{9,11},{10,... | collective-permute-start | bytes 1572872 | tf_op jit(solution)/shard_map/ppermute | solution.py:30
  298.2 24.2 %collective-permute-start.11 = (bf16[2,128,1024]{2,1,0:T(8,128)(2,1)}, bf16[2,128,1024]{2,1,0:T(8,128)(2,1)}, u32[]{:S(2)}, u32[]{:S(2)}) collective-permute-start(bf16[2,128,1024]{2,1,0:T(8,128)(2,1)} %get-tuple-element.52), channel_id=1, source_target_pairs={{0,3},{1,2},{2,1},{3,0},{4,7},{5,6},{6,5},{7,4},{8,11},{9,10},{10,... | collective-permute-start | bytes 1572872 | tf_op jit(solution)/shard_map/ppermute | solution.py:30
  322.4 1.0 copy-start.4
  323.5 1.0 copy-start.6
  324.5 1.0 copy-start.7
  325.6 3.6 copy-start.9

commit v15 on v14

--- a/solution.py
+++ b/solution.py
@@ -132,32 +132,53 @@
     )(*flat)
 
 
-def pick_kernel(first, lists, pool_ref, out_ref, held, sems):
-    seqs, chunk = held.shape[0], held.shape[-1]
+def kv_shapes(seqs, chunk, split):
+    half = seqs // 2
+    if split:
+        return [(half, 2, NBLEN, chunk)] + [(2, NBLEN, chunk)] * half
+    return [(seqs, 2, NBLEN, chunk)]
+
+
+def kv_views(refs, seqs, split):
+    if not split:
+        return [(seq, refs[0].at[seq]) for seq in range(seqs)]
+    half = seqs // 2
+    me = lax.axis_index("enc")
+    near = [(me - me % half + step, refs[0].at[step]) for step in range(half)]
+    return near + [(across(me, step, seqs), refs[1 + step]) for step in range(half)]
+
+
+def pick_kernel(first, split, seqs, lists, pool_ref, *rest):
+    outs, held, sems = rest[:-2], rest[-2], rest[-1]
+    chunk = held.shape[-1]
     arriving, leaving = [], []
-    for seq in range(seqs):
+    for n, (seq, out) in enumerate(kv_views(outs, seqs, split)):
         source = pool_ref.at[lists[0, seq, 0], :, :, first : first + chunk]
-        arriving.append(pltpu.make_async_copy(source, held.at[seq], sems.at[0, seq]))
-        leaving.append(pltpu.make_async_copy(held.at[seq], out_ref.at[seq], sems.at[1, seq]))
-        arriving[seq].start()
-    for seq in range(seqs):
-        arriving[seq].wait()
-        leaving[seq].start()
-    for seq in range(seqs):
-        leaving[seq].wait()
-
-
-def pick(first, chunk, send_lists, kv_pool):
-    shape = (send_lists.shape[1], 2, NBLEN, chunk)
+        arriving.append(pltpu.make_async_copy(source, held.at[n], sems.at[0, n]))
+        leaving.append(pltpu.make_async_copy(held.at[n], out, sems.at[1, n]))
+        arriving[n].start()
+    for n in range(seqs):
+        arriving[n].wait()
+        leaving[n].start()
+    for n in range(seqs):
+        leaving[n].wait()
+
+
+def pick(first, chunk, split, send_lists, kv_pool):
+    seqs = send_lists.shape[1]
+    shapes = kv_shapes(seqs, chunk, split)
     return pl.pallas_call(
-        functools.partial(pick_kernel, first),
+        functools.partial(pick_kernel, first, split, seqs),
         grid=(1,),
         in_specs=[SCALARS, IN_HBM],
-        out_specs=IN_HBM,
-        out_shape=in_hbm(shape),
-        scratch_shapes=[pltpu.VMEM(shape, BF16), pltpu.SemaphoreType.DMA((2, shape[0]))],
-        compiler_params=PARAMS,
-        cost_estimate=cost(8 * shape[0] * NBLEN * chunk),
+        out_specs=[IN_HBM] * len(shapes),
+        out_shape=[in_hbm(shape) for shape in shapes],
+        scratch_shapes=[
+            pltpu.VMEM((seqs, 2, NBLEN, chunk), BF16),
+            pltpu.SemaphoreType.DMA((2, seqs)),
+        ],
+        compiler_params=PARAMS,
+        cost_estimate=cost(8 * seqs * NBLEN * chunk),
         name="pick_entries",
     )(send_lists, pltpu.with_memory_space_constraint(kv_pool, pltpu.HBM))
 
@@ -169,12 +190,18 @@
 
 
 def attend_kernel(seqs, parts, split, uses, *rest):
-    half = seqs // 2
-    rows_in, held, rest = rest[:parts], rest[parts], rest[parts + 1 :]
-    rows_out, kv_out, (rows, made, sums) = rest[:parts], rest[parts:-3], rest[-3:]
+    pieces = 1 + seqs // 2 if split else 1
+    rows_in, rest = rest[:parts], rest[parts:]
+    kv_in, rest = rest[:pieces], rest[pieces:]
+    rows_out, rest = rest[:parts], rest[parts:]
+    kv_out, rest = rest[:pieces], rest[pieces:]
+    held, rows, made, sums = rest if split else (kv_in[0], *rest)
     scale = DH ** (-0.5)
-    me, mine = lax.axis_index("enc"), lax.axis_index("seq")
-
+    mine = lax.axis_index("seq")
+
+    if split:
+        for slot, piece in kv_views(kv_in, seqs, split):
+            held[slot] = piece[...]
     for step in range(parts):
         for n in range(2):
             piece = rows_in[step][n].astype(F32)
@@ -232,63 +259,50 @@
         for n in range(2):
             piece = made[partner(mine, step, parts), n]
             rows_out[step][n] = pltpu.roll(piece, 2 * BLOCK - 1, 0).astype(BF16)
-    if split:
-        base = me - me % half
-        for step in range(half):
-            kv_out[0][step] = sums[base + step].astype(BF16)
-            kv_out[1 + step][...] = sums[across(me, step, seqs)].astype(BF16)
-    else:
-        kv_out[0][...] = sums[...].astype(BF16)
-
-
-def attend(uses, rows_in, arrived, split):
+    for slot, piece in kv_views(kv_out, seqs, split):
+        piece[...] = sums[slot].astype(BF16)
+
+
+def heads_spec(shape, wide):
+    return pl.BlockSpec((*shape[:-1], wide), lambda i, n=len(shape) - 1: (0,) * n + (i,))
+
+
+def attend(uses, rows_in, kv_in):
     parts, part_rows = len(rows_in), rows_in[0].shape[1]
-    seqs, _, _, chunk = arrived.shape
-    half, heads = seqs // 2, chunk // DH
-    rows_spec = pl.BlockSpec((2, part_rows, DH), lambda i: (0, 0, i))
-    shapes = [(seqs, 2, NBLEN)]
-    if split:
-        shapes = [(half, 2, NBLEN)] + [(2, NBLEN)] * half
-    kv_specs = [
-        pl.BlockSpec((*shape, DH), lambda i, n=len(shape): (0,) * n + (i,)) for shape in shapes
-    ]
+    split = len(kv_in) > 1
+    seqs = 2 * kv_in[0].shape[0] if split else kv_in[0].shape[0]
+    chunk = kv_in[0].shape[-1]
+    heads = chunk // DH
+    shapes = [array.shape for array in (*rows_in, *kv_in)]
+    specs = [heads_spec(shape, DH) for shape in shapes]
     pairs = heads * parts * part_rows * 2 * NBLEN
+    held = [pltpu.VMEM((seqs, 2, NBLEN, DH), BF16)] if split else []
     outs = pl.pallas_call(
         functools.partial(attend_kernel, seqs, parts, split),
         grid=(heads,),
-        in_specs=[SCALARS]
-        + [rows_spec] * parts
-        + [pl.BlockSpec((seqs, 2, NBLEN, DH), lambda i: (0, 0, 0, i))],
-        out_specs=[rows_spec] * parts + kv_specs,
-        scratch_shapes=[
+        in_specs=[SCALARS] + specs,
+        out_specs=specs,
+        scratch_shapes=held
+        + [
             pltpu.VMEM((parts + 1, 2, part_rows, DH), F32),
             pltpu.VMEM((parts + 1, 2, part_rows, DH), F32),
             pltpu.VMEM((seqs, 2, NBLEN, DH), F32),
         ],
-        out_shape=[in_hbm((2, part_rows, chunk))] * parts
-        + [in_hbm((*shape, chunk)) for shape in shapes],
+        out_shape=[in_hbm(shape) for shape in shapes],
         compiler_params=PARAMS,
         cost_estimate=cost(
             8 * (seqs + parts) * NBLEN * chunk, ATTEND_WEIGHT * 12 * DH * pairs, pairs
         ),
         name="attend_blocks",
-    )(uses, *rows_in, arrived)
+    )(uses, *rows_in, *kv_in)
     return outs[:parts], outs[parts:]
 
 
-def owner_kernel(seqs, lists, *rest):
-    half = seqs // 2
-    first_ref, out_ref, acc = rest[0], rest[-2], rest[-1]
-    me = lax.axis_index("enc")
-    base = me - me % half
+def owner_kernel(seqs, pieces, lists, *rest):
+    out_ref, acc = rest[-2], rest[-1]
     acc[...] = jnp.zeros_like(acc)
-    if first_ref.shape[0] == seqs:
-        for seq in range(seqs):
-            acc[lists[0, seq, 0]] += first_ref[seq].astype(F32)
-    else:
-        for step in range(half):
-            acc[lists[0, base + step, 0]] += first_ref[step].astype(F32)
-            acc[lists[0, across(me, step, seqs), 0]] += rest[1 + step][...].astype(F32)
+    for seq, piece in kv_views(rest[:pieces], seqs, pieces > 1):
+        acc[lists[0, seq, 0]] += piece[...].astype(F32)
     out_ref[...] = acc[...].astype(BF16)
 
 
@@ -298,12 +312,9 @@
     wide = math.gcd(math.gcd(first, chunk), 256)
     skip, steps = first // wide, chunk // wide
     extra = [] if so_far is None else [so_far]
-    specs = [
-        pl.BlockSpec((*array.shape[:-1], wide), lambda i, n=array.ndim - 1: (0,) * n + (i,))
-        for array in back
-    ]
+    specs = [heads_spec(array.shape, wide) for array in back]
     return pl.pallas_call(
-        functools.partial(owner_kernel, seqs),
+        functools.partial(owner_kernel, seqs, len(back)),
         grid=(steps,),
         in_specs=[SCALARS] + specs + [ANYWHERE] * len(extra),
         out_specs=pl.BlockSpec(
@@ -324,6 +335,8 @@
     for step, piece in enumerate(pieces):
         there = [half + (i + step) % half for i in range(half)]
         pairs = list(enumerate(there)) + [(peer, i) for i, peer in enumerate(there)]
+        if step >= 2:
+            piece = after(piece, got[step - 2])
         got.append(lax.ppermute(piece, "enc", pairs))
     return got
 
@@ -334,26 +347,27 @@
     bounds = [(0, cut), (cut, width - cut)]
     firsts = [first for first, _ in bounds]
 
-    arrived, rows = [], []
-    for first, chunk in bounds:
-        picked = pick(first, chunk, send_lists, kv_pool)
-        send_lists, queries = after((send_lists, queries), picked)
-        if rows:
-            picked = after(picked, rows)
-        arrived.append(swap_pool(picked))
-        if not rows:
-            for start, size in bounds:
-                packed = pack(start, size, queries, grad_context, width, parts)
-                rows.append(swap_rows(packed))
-
-    rows_out, (near, *far) = attend(block_slots, rows[0], arrived[0], True)
+    picked = pick(*bounds[0], False, send_lists, kv_pool)
+    send_lists, queries = after((send_lists, queries), picked[0])
+    early = swap_pool(picked[0])
+    near, *far = pick(*bounds[1], True, send_lists, kv_pool)
+    queries = after(queries, near)
+    rows = [
+        swap_rows(pack(first, chunk, queries, grad_context, width, parts))
+        for first, chunk in bounds
+    ]
+    far = swap_far(after(far, rows))
+    near = swap_near(near, seqs)
+
+    early = after(early, (far[:2], rows))
+    rows_out, whole = attend(block_slots, rows[0], [early])
+    token_parts = [swap_rows(rows_out)]
+    returns = [[swap_pool(after(whole[0], far))]]
+    block_slots = after(block_slots, token_parts[0])
+    rows_out, (near, *far) = attend(block_slots, rows[1], [near, *far])
     far = swap_far(far)
-    returns = [[swap_near(near, seqs), *far]]
-    token_parts = [swap_rows(rows_out)]
-    block_slots = after(block_slots, token_parts[0])
-    rows_out, (whole,) = attend(block_slots, rows[1], arrived[1], False)
     token_parts.append(swap_rows(rows_out))
-    returns.append([swap_pool(after(whole, far))])
+    returns.append([swap_near(after(near, far[:2]), seqs), *far])
 
     context, grad_queries = unpack(token_parts, firsts, width, queries.shape)
     pool_grads = None

time: 398 us -> 408 us (1.025)
  local copies, waits for them, and re-layouts: 15.1 us -> 27.5 us
  starting transfers between devices: 54.9 us -> 43.8 us
  waiting for transfers between devices: 253 us -> 261 us
    all_to_all x3 -> x2, waiting for transfers between devices: 176 us -> 0.01 us  [swap_pool(): return lax.all_to_all(array, 'enc', split_axis=0, concat_axis=0, tiled=True)]
    ppermute x4 -> x8, waiting for transfers between devices: 9.64 us -> 178 us  [swap_far(): got.append(lax.ppermute(piece, 'enc', pairs))]
    unnamed x46 -> x78, local copies, waits for them, and re-layouts: 14.8 us -> 27.4 us
    ppermute x12, waiting for transfers between devices: 67.3 us -> 77 us  [exchange(): return lax.ppermute(array, axis, pairs)]
    all_to_all x3 -> x2, starting transfers between devices: 21.3 us -> 12.8 us  [swap_pool(): return lax.all_to_all(array, 'enc', split_axis=0, concat_axis=0, tiled=True)]
    all_to_all x1 -> x2, waiting for transfers between devices: 0.01 us -> 5.94 us  [swap_near(): lax.all_to_all(array, 'enc', split_axis=0, concat_axis=0, axis_index_grou...]
    ppermute x4 -> x8, starting transfers between devices: 17 us -> 11.6 us  [swap_far(): got.append(lax.ppermute(piece, 'enc', pairs))]
    all_to_all x1 -> x2, starting transfers between devices: 7.74 us -> 10.5 us  [swap_near(): lax.all_to_all(array, 'enc', split_axis=0, concat_axis=0, axis_index_grou...]
  transfers between devices with their start and end apart: 20 -> 24, of which waited for: 12 -> 14; matrix products, arithmetic and copies ran while one was open for 0% -> 0% of each run, Pallas kernels for 15% -> 15%
where the time goes in v15:
time: 408 us; the launch traced here: 402 us
  waiting for transfers between devices  261 us (64%)
  Pallas kernels  68.5 us (17%)
  starting transfers between devices  43.8 us (11%)
  local copies, waits for them, and re-layouts  27.5 us (7%)
    ppermute x8, waiting for transfers between devices, swap_far(): got.append(lax.ppermute(piece, 'enc', pairs))  178 us
    ppermute x12, waiting for transfers between devices, exchange(): return lax.ppermute(array, axis, pairs)  77 us
    pallas_call x2, Pallas kernels, attend(): pl.pallas_call(functools.partial(attend_kernel, seqs, parts, split), grid...  46.3 us
    unnamed x78, local copies, waits for them, and re-layouts  27.4 us
    all_to_all x2, starting transfers between devices, swap_pool(): return lax.all_to_all(array, 'enc', split_axis=0, concat_axis=0, tiled=True)  12.8 us
    ppermute x8, starting transfers between devices, swap_far(): got.append(lax.ppermute(piece, 'enc', pairs))  11.6 us
    all_to_all x2, starting transfers between devices, swap_near(): lax.all_to_all(array, 'enc', split_axis=0, concat_axis=0, axis_index_grou...  10.5 us
    ppermute x12, starting transfers between devices, exchange(): return lax.ppermute(array, axis, pairs)  8.82 us
  transfers between devices with their start and end apart: 24, of which 14 were waited for; matrix products, arithmetic and copies ran while one was open for 0% of the time, Pallas kernels for 15%

profile of v15, /device:TPU:15, one launch (start us, length us, event | category | flops | bytes accessed | tf_op | source)
XLA Modules:
  0.0 401.8 jit_solution(1264966073323452250)
XLA Ops:
  1.4 4.2 %pick_entries.2 = bf16[8,2,128,1024]{3,2,1,0:T(8,128)(2,1)} custom-call(s32[1,8,1]{2,1,0:T(8,128)S(1)} %copy.9.lists, bf16[4,2,128,2048]{3,2,1,0:T(8,128)(2,1)} %pool_ref.3), custom_call_target="tpu_custom_call" | custom-call | bytes 8388608 | tf_op jit(solution)/shard_map/pick_entries/pallas_call | solution.py:170
  5.6 5.6 %all-to-all-start = ((bf16[8,2,128,1024]{3,2,1,0:T(8,128)(2,1)}), bf16[8,2,128,1024]{3,2,1,0:T(8,128)(2,1)}, u32[]{:S(2)}, u32[]{:S(2)}) async-start(bf16[8,2,128,1024]{3,2,1,0:T(8,128)(2,1)} %pick_entries.2), calls=%async_computation | async-start | bytes 8388608 | tf_op jit(solution)/shard_map/all_to_all | solution.py:53
  11.3 4.6 %pick_entries.3 = (bf16[4,2,128,1024]{3,2,1,0:T(8,128)(2,1)}, bf16[2,128,1024]{2,1,0:T(8,128)(2,1)}, bf16[2,128,1024]{2,1,0:T(8,128)(2,1)}, bf16[2,128,1024]{2,1,0:T(8,128)(2,1)}, bf16[2,128,1024]{2,1,0:T(8,128)(2,1)}) custom-call(s32[1,8,1]{2,1,0:T(8,128)S(1)} %copy.10.lists, bf16[4,2,128,2048]{3,2,1,0:T(8,128)(2,1)} %pool_ref.3), custom_call_target="tpu_custom_call" | custom-call | bytes 8388608 | tf_op jit(solution)/shard_map/pick_entries/pallas_call | solution.py:170
  16.1 1.6 pack_rows.3
  18.3 2.2 collective-permute-start.5
  20.5 1.5 pack_rows.2
  22.6 8.5 %collective-permute-done.3.rest_1_ = bf16[2,128,1024]{2,1,0:T(8,128)(2,1)S(1)} collective-permute-done((bf16[2,128,1024]{2,1,0:T(8,128)(2,1)}, bf16[2,128,1024]{2,1,0:T(8,128)(2,1)S(1)}, u32[]{:S(2)}, u32[]{:S(2)}) %collective-permute-start.3) | collective-permute-done | bytes 524320 | tf_op jit(solution)/shard_map/ppermute | solution.py:30
  32.9 9.4 %collective-permute-done.5.rest_3_ = bf16[2,128,1024]{2,1,0:T(8,128)(2,1)S(1)} collective-permute-done((bf16[2,128,1024]{2,1,0:T(8,128)(2,1)}, bf16[2,128,1024]{2,1,0:T(8,128)(2,1)S(1)}, u32[]{:S(2)}, u32[]{:S(2)}) %collective-permute-start.5) | collective-permute-done | bytes 524320 | tf_op jit(solution)/shard_map/ppermute | solution.py:30
  43.2 10.6 %collective-permute-done.rest_1_ = bf16[2,128,1024]{2,1,0:T(8,128)(2,1)S(1)} collective-permute-done((bf16[2,128,1024]{2,1,0:T(8,128)(2,1)}, bf16[2,128,1024]{2,1,0:T(8,128)(2,1)S(1)}, u32[]{:S(2)}, u32[]{:S(2)}) %collective-permute-start) | collective-permute-done | bytes 524320 | tf_op jit(solution)/shard_map/ppermute | solution.py:30
  55.3 9.5 %collective-permute-done.2.rest_3_ = bf16[2,128,1024]{2,1,0:T(8,128)(2,1)S(1)} collective-permute-done((bf16[2,128,1024]{2,1,0:T(8,128)(2,1)}, bf16[2,128,1024]{2,1,0:T(8,128)(2,1)S(1)}, u32[]{:S(2)}, u32[]{:S(2)}) %collective-permute-start.2) | collective-permute-done | bytes 524320 | tf_op jit(solution)/shard_map/ppermute | solution.py:30
  65.7 2.1 collective-permute-start.6
  67.7 1.6 collective-permute-start.7
  69.4 65.9 %collective-permute-done.6.rest_5_ = bf16[2,128,1024]{2,1,0:T(8,128)(2,1)S(1)} collective-permute-done((bf16[2,128,1024]{2,1,0:T(8,128)(2,1)S(1)}, bf16[2,128,1024]{2,1,0:T(8,128)(2,1)S(1)}, u32[]{:S(2)}, u32[]{:S(2)}) %collective-permute-start.6) | collective-permute-done | bytes 524320 | tf_op jit(solution)/shard_map/ppermute | solution.py:340
  136.2 23.9 %collective-permute-done.7.rest_6_ = bf16[2,128,1024]{2,1,0:T(8,128)(2,1)S(1)} collective-permute-done((bf16[2,128,1024]{2,1,0:T(8,128)(2,1)S(1)}, bf16[2,128,1024]{2,1,0:T(8,128)(2,1)S(1)}, u32[]{:S(2)}, u32[]{:S(2)}) %collective-permute-start.7) | collective-permute-done | bytes 524320 | tf_op jit(solution)/shard_map/ppermute | solution.py:340
  160.9 5.6 %all-to-all-start.1 = ((bf16[4,2,128,1024]{3,2,1,0:T(8,128)(2,1)}), bf16[4,2,128,1024]{3,2,1,0:T(8,128)(2,1)S(1)}, u32[]{:S(2)}, u32[]{:S(2)}) async-start(bf16[4,2,128,1024]{3,2,1,0:T(8,128)(2,1)} %get-tuple-element.49), calls=%async_computation.1 | async-start | bytes 4194304 | tf_op jit(solution)/shard_map/all_to_all | solution.py:42
  166.5 1.0 copy-done.25
  167.6 1.0 copy-done.27
  168.6 1.0 copy-done.29
  169.7 1.0 copy-done.31
  170.7 22.5 %attend_blocks.2 = (bf16[2,128,1024]{2,1,0:T(8,128)(2,1)}, bf16[2,128,1024]{2,1,0:T(8,128)(2,1)}, bf16[2,128,1024]{2,1,0:T(8,128)(2,1)}, bf16[2,128,1024]{2,1,0:T(8,128)(2,1)}, bf16[8,2,128,1024]{3,2,1,0:T(8,128)(2,1)}) custom-call(s32[1,8,2]{2,1,0:T(8,128)S(1)} %copy.11.uses, bf16[2,128,1024]{2,1,0:T(8,128)(2,1)S(1)} %copy-done.25, ...), custom_call_target="tpu_custom_call" | custom-call | flops 38654705664 | bytes 12582912 | tf_op jit(solution)/shard_map/attend_blocks/pallas_call | solution.py:280
  193.3 5.9 %all-to-all-done.1.rest_4_ = bf16[4,2,128,1024]{3,2,1,0:T(8,128)(2,1)S(1)} async-done(((bf16[4,2,128,1024]{3,2,1,0:T(8,128)(2,1)}), bf16[4,2,128,1024]{3,2,1,0:T(8,128)(2,1)S(1)}, u32[]{:S(2)}, u32[]{:S(2)}) %all-to-all-start.1) | async-done | bytes 2097184 | tf_op jit(solution)/shard_map/all_to_all | solution.py:42
  199.2 7.1 %all-to-all-start.3 = ((bf16[8,2,128,1024]{3,2,1,0:T(8,128)(2,1)}), bf16[8,2,128,1024]{3,2,1,0:T(8,128)(2,1)}, u32[]{:S(2)}, u32[]{:S(2)}) async-start(bf16[8,2,128,1024]{3,2,1,0:T(8,128)(2,1)} %get-tuple-element.90), calls=%async_computation.3 | async-start | bytes 8388608 | tf_op jit(solution)/shard_map/all_to_all | solution.py:53
  206.8 2.2 collective-permute-start.10
  209.0 10.8 %collective-permute-done.8.refs_1_ = bf16[2,128,1024]{2,1,0:T(8,128)(2,1)S(1)} collective-permute-done((bf16[2,128,1024]{2,1,0:T(8,128)(2,1)}, bf16[2,128,1024]{2,1,0:T(8,128)(2,1)S(1)}, u32[]{:S(2)}, u32[]{:S(2)}) %collective-permute-start.8) | collective-permute-done | bytes 524320 | tf_op jit(solution)/shard_map/ppermute | solution.py:30
  221.4 9.5 %collective-permute-done.10.refs_3_ = bf16[2,128,1024]{2,1,0:T(8,128)(2,1)S(1)} collective-permute-done((bf16[2,128,1024]{2,1,0:T(8,128)(2,1)S(1)}, bf16[2,128,1024]{2,1,0:T(8,128)(2,1)S(1)}, u32[]{:S(2)}, u32[]{:S(2)}) %collective-permute-start.10) | collective-permute-done | bytes 524320 | tf_op jit(solution)/shard_map/ppermute | solution.py:30
  231.8 1.0 copy-done.16
  232.8 1.0 copy-done.18
  233.9 1.0 copy-done.20
  236.0 1.0 copy-done.24
  237.0 23.8 %attend_blocks.3 = (bf16[2,128,1024]{2,1,0:T(8,128)(2,1)}, bf16[2,128,1024]{2,1,0:T(8,128)(2,1)}, bf16[2,128,1024]{2,1,0:T(8,128)(2,1)}, bf16[2,128,1024]{2,1,0:...) custom-call(s32[1,8,2]{2,1,0:T(8,128)S(1)} %copy.12.uses, ...), custom_call_target="tpu_custom_call" | custom-call | flops 38654705664 | bytes 12582912 | tf_op jit(solution)/shard_map/attend_blocks/pallas_call | solution.py:280
  260.8 2.3 collective-permute-start.16
  263.1 1.5 collective-permute-start.17
  264.6 65.9 %collective-permute-done.16.rest_1_ = bf16[2,128,1024]{2,1,0:T(8,128)(2,1)S(1)} collective-permute-done((bf16[2,128,1024]{2,1,0:T(8,128)(2,1)}, bf16[2,128,1024]{2,1,0:T(8,128)(2,1)S(1)}, u32[]{:S(2)}, u32[]{:S(2)}) %collective-permute-start.16) | collective-permute-done | bytes 524320 | tf_op jit(solution)/shard_map/ppermute | solution.py:340
  330.5 13.0 %collective-permute-done.17.rest_2_ = bf16[2,128,1024]{2,1,0:T(8,128)(2,1)S(1)} collective-permute-done((bf16[2,128,1024]{2,1,0:T(8,128)(2,1)}, bf16[2,128,1024]{2,1,0:T(8,128)(2,1)S(1)}, u32[]{:S(2)}, u32[]{:S(2)}) %collective-permute-start.17) | collective-permute-done | bytes 524320 | tf_op jit(solution)/shard_map/ppermute | solution.py:340
  343.5 4.9 %all-to-all-start.2 = ((bf16[4,2,128,1024]{3,2,1,0:T(8,128)(2,1)}), bf16[4,2,128,1024]{3,2,1,0:T(8,128)(2,1)S(1)}, u32[]{:S(2)}, u32[]{:S(2)}) async-start(bf16[4,2,128,1024]{3,2,1,0:T(8,128)(2,1)} %get-tuple-element.84), calls=%async_computation.2 | async-start | bytes 4194304 | tf_op jit(solution)/shard_map/all_to_all | solution.py:42
  348.9 2.2 collective-permute-start.15
  351.1 3.3 collective-permute-start.19
  354.3 7.4 %collective-permute-done.13.refs_5_ = bf16[2,128,1024]{2,1,0:T(8,128)(2,1)S(1)} collective-permute-done((bf16[2,128,1024]{2,1,0:T(8,128)(2,1)}, bf16[2,128,1024]{2,1,0:T(8,128)(2,1)S(1)}, u32[]{:S(2)}, u32[]{:S(2)}) %collective-permute-start.13) | collective-permute-done | bytes 524320 | tf_op jit(solution)/shard_map/ppermute | solution.py:30
  361.8 11.2 %collective-permute-done.15.refs_7_ = bf16[2,128,1024]{2,1,0:T(8,128)(2,1)S(1)} collective-permute-done((bf16[2,128,1024]{2,1,0:T(8,128)(2,1)}, bf16[2,128,1024]{2,1,0:T(8,128)(2,1)S(1)}, u32[]{:S(2)}, u32[]{:S(2)}) %collective-permute-start.15) | collective-permute-done | bytes 524320 | tf_op jit(solution)/shard_map/ppermute | solution.py:30
  373.0 1.0 copy-done.6
  374.0 1.0 copy-done.8
  375.1 1.0 copy-done.10
  377.2 1.0 copy-done.13
  378.2 2.1 unpack_rows.1
  380.3 4.8 %owner_sum.2.rest_5_ = bf16[4,2,128,2048]{3,2,1,0:T(8,128)(2,1)} custom-call(s32[1,8,1]{2,1,0:T(8,128)S(1)} %copy.10.lists, bf16[8,2,128,1024]{3,2,1,0:T(8,128)(2,1)} %all-to-all-done.3.rest_0_), custom_call_target="tpu_custom_call" | custom-call | flops 2097152 | bytes 6291456 | tf_op jit(solution)/shard_map/owner_sum/pallas_call | solution.py:316
  385.9 9.5 %collective-permute-done.19.rest_4_ = bf16[2,128,1024]{2,1,0:T(8,128)(2,1)S(1)} collective-permute-done((bf16[2,128,1024]{2,1,0:T(8,128)(2,1)}, bf16[2,128,1024]{2,1,0:T(8,128)(2,1)S(1)}, u32[]{:S(2)}, u32[]{:S(2)}) %collective-permute-start.19) | collective-permute-done | bytes 524320 | tf_op jit(solution)/shard_map/ppermute | solution.py:340
  396.2 1.0 copy-done.3
  398.3 3.5 owner_sum.3
  (89 shorter events, 17.3 us)
Async XLA Ops:
  5.5 5.7 %copy-start.33 = (s32[1,8,1]{1,2,0:T(1,128)S(1)}, s32[1,8,1]{1,2,0:T(1,128)}, u32[]{:S(2)}) copy-start(s32[1,8,1]{1,2,0:T(1,128)} %param.7) | copy-start | bytes 100
  5.6 155.4 %all-to-all-start = ((bf16[8,2,128,1024]{3,2,1,0:T(8,128)(2,1)}), bf16[8,2,128,1024]{3,2,1,0:T(8,128)(2,1)}, u32[]{:S(2)}, u32[]{:S(2)}) async-start(bf16[8,2,128,1024]{3,2,1,0:T(8,128)(2,1)} %pick_entries.2), calls=%async_computation | async-start | bytes 8388608 | tf_op jit(solution)/shard_map/all_to_all | solution.py:53
  11.3 4.6 %copy-start = (bf16[1,128,8192]{2,1,0:T(8,128)(2,1)S(1)}, bf16[1,128,8192]{2,1,0:T(8,128)(2,1)}, u32[]{:S(2)}) copy-start(bf16[1,128,8192]{2,1,0:T(8,128)(2,1)} %q_ref.1) | copy-start | bytes 6291460
  11.3 4.8 %copy-start.1 = (bf16[1,128,8192]{2,1,0:T(8,128)(2,1)S(1)}, bf16[1,128,8192]{2,1,0:T(8,128)(2,1)}, u32[]{:S(2)}) copy-start(bf16[1,128,8192]{2,1,0:T(8,128)(2,1)} %g_ref.3) | copy-start | bytes 6291460
  17.7 13.4 %collective-permute-start.3 = (bf16[2,128,1024]{2,1,0:T(8,128)(2,1)}, bf16[2,128,1024]{2,1,0:T(8,128)(2,1)S(1)}, u32[]{:S(2)}, u32[]{:S(2)}) collective-permute-start(bf16[2,128,1024]{2,1,0:T(8,128)(2,1)} %get-tuple-element.60), channel_id=1, source_target_pairs={{0,1},{1,0},{2,3},{3,2},{4,5},{5,4},{6,7},{7,6},{8,9},{9,8},{10,11... | collective-permute-start | bytes 1572872 | tf_op jit(solution)/shard_map/ppermute | solution.py:30
  18.0 14.1 %collective-permute-start.4 = (bf16[2,128,1024]{2,1,0:T(8,128)(2,1)}, bf16[2,128,1024]{2,1,0:T(8,128)(2,1)S(1)}, u32[]{:S(2)}, u32[]{:S(2)}) collective-permute-start(bf16[2,128,1024]{2,1,0:T(8,128)(2,1)} %get-tuple-element.61), channel_id=1, source_target_pairs={{0,2},{1,3},{2,0},{3,1},{4,6},{5,7},{6,4},{7,5},{8,10},{9,11},{10,... | collective-permute-start | bytes 1572872 | tf_op jit(solution)/shard_map/ppermute | solution.py:30
  18.2 47.4 %copy-start.36 = (bf16[2,128,1024]{2,1,0:T(8,128)(2,1)S(1)}, bf16[2,128,1024]{2,1,0:T(8,128)(2,1)}, u32[]{:S(2)}) copy-start(bf16[2,128,1024]{2,1,0:T(8,128)(2,1)} %get-tuple-element.63) | copy-start | bytes 1572868
  18.3 49.5 %copy-start.35 = (bf16[2,128,1024]{2,1,0:T(8,128)(2,1)S(1)}, bf16[2,128,1024]{2,1,0:T(8,128)(2,1)}, u32[]{:S(2)}) copy-start(bf16[2,128,1024]{2,1,0:T(8,128)(2,1)} %get-tuple-element.64) | copy-start | bytes 1572868
  18.3 51.1 %copy-start.32 = (s32[1,8,2]{1,2,0:T(2,128)S(1)}, s32[1,8,2]{1,2,0:T(2,128)}, u32[]{:S(2)}) copy-start(s32[1,8,2]{1,2,0:T(2,128)} %param.8) | copy-start | bytes 196
  18.3 142.7 %copy-start.34 = (bf16[2,128,1024]{2,1,0:T(8,128)(2,1)S(1)}, bf16[2,128,1024]{2,1,0:T(8,128)(2,1)}, u32[]{:S(2)}) copy-start(bf16[2,128,1024]{2,1,0:T(8,128)(2,1)} %get-tuple-element.74) | copy-start | bytes 1572868
  18.3 24.1 %collective-permute-start.5 = (bf16[2,128,1024]{2,1,0:T(8,128)(2,1)}, bf16[2,128,1024]{2,1,0:T(8,128)(2,1)S(1)}, u32[]{:S(2)}, u32[]{:S(2)}) collective-permute-start(bf16[2,128,1024]{2,1,0:T(8,128)(2,1)} %get-tuple-element.62), channel_id=1, source_target_pairs={{0,3},{1,2},{2,1},{3,0},{4,7},{5,6},{6,5},{7,4},{8,11},{9,10},{10,... | collective-permute-start | bytes 1572872 | tf_op jit(solution)/shard_map/ppermute | solution.py:30
  22.0 31.7 %collective-permute-start = (bf16[2,128,1024]{2,1,0:T(8,128)(2,1)}, bf16[2,128,1024]{2,1,0:T(8,128)(2,1)S(1)}, u32[]{:S(2)}, u32[]{:S(2)}) collective-permute-start(bf16[2,128,1024]{2,1,0:T(8,128)(2,1)} %get-tuple-element.52), channel_id=1, source_target_pairs={{0,1},{1,0},{2,3},{3,2},{4,5},{5,4},{6,7},{7,6},{8,9},{9,8},{10,11... | collective-permute-start | bytes 1572872 | tf_op jit(solution)/shard_map/ppermute | solution.py:30
  22.4 32.2 %collective-permute-start.1 = (bf16[2,128,1024]{2,1,0:T(8,128)(2,1)}, bf16[2,128,1024]{2,1,0:T(8,128)(2,1)S(1)}, u32[]{:S(2)}, u32[]{:S(2)}) collective-permute-start(bf16[2,128,1024]{2,1,0:T(8,128)(2,1)} %get-tuple-element.53), channel_id=1, source_target_pairs={{0,2},{1,3},{2,0},{3,1},{4,6},{5,7},{6,4},{7,5},{8,10},{9,11},{10,... | collective-permute-start | bytes 1572872 | tf_op jit(solution)/shard_map/ppermute | solution.py:30
  31.9 32.9 %collective-permute-start.2 = (bf16[2,128,1024]{2,1,0:T(8,128)(2,1)}, bf16[2,128,1024]{2,1,0:T(8,128)(2,1)S(1)}, u32[]{:S(2)}, u32[]{:S(2)}) collective-permute-start(bf16[2,128,1024]{2,1,0:T(8,128)(2,1)} %get-tuple-element.54), channel_id=1, source_target_pairs={{0,3},{1,2},{2,1},{3,0},{4,7},{5,6},{6,5},{7,4},{8,11},{9,10},{10,... | collective-permute-start | bytes 1572872 | tf_op jit(solution)/shard_map/ppermute | solution.py:30
  65.7 69.6 %collective-permute-start.6 = (bf16[2,128,1024]{2,1,0:T(8,128)(2,1)S(1)}, bf16[2,128,1024]{2,1,0:T(8,128)(2,1)S(1)}, u32[]{:S(2)}, u32[]{:S(2)}) collective-permute-start(bf16[2,128,1024]{2,1,0:T(8,128)(2,1)S(1)} %copy-done.36), channel_id=1, source_target_pairs={{0,16},{4,20},{8,24},{12,28},{16,0},{20,4},{24,8},{28,12},{1,17},{... | collective-permute-start | bytes 1572872 | tf_op jit(solution)/shard_map/ppermute | solution.py:340
  67.7 92.3 %collective-permute-start.7 = (bf16[2,128,1024]{2,1,0:T(8,128)(2,1)S(1)}, bf16[2,128,1024]{2,1,0:T(8,128)(2,1)S(1)}, u32[]{:S(2)}, u32[]{:S(2)}) collective-permute-start(bf16[2,128,1024]{2,1,0:T(8,128)(2,1)S(1)} %copy-done.35), channel_id=1, source_target_pairs={{0,20},{4,24},{8,28},{12,16},{20,0},{24,4},{28,8},{16,12},{1,21},{... | collective-permute-start | bytes 1572872 | tf_op jit(solution)/shard_map/ppermute | solution.py:340
  135.3 25.7 %copy-start.21 = (bf16[2,128,1024]{2,1,0:T(8,128)(2,1)}, bf16[2,128,1024]{2,1,0:T(8,128)(2,1)S(1)}, u32[]{:S(2)}) copy-start(bf16[2,128,1024]{2,1,0:T(8,128)(2,1)S(1)} %collective-permute-done.6.rest_5_) | copy-start | bytes 1572868
  135.3 58.0 %collective-permute-start.11 = (bf16[2,128,1024]{2,1,0:T(8,128)(2,1)}, bf16[2,128,1024]{2,1,0:T(8,128)(2,1)}, u32[]{:S(2)}, u32[]{:S(2)}) collective-permute-start(bf16[2,128,1024]{2,1,0:T(8,128)(2,1)} %get-tuple-element.72), channel_id=1, source_target_pairs={{0,24},{4,28},{8,16},{12,20},{24,0},{28,4},{16,8},{20,12},{1,25},{... | collective-permute-start | bytes 1572872 | tf_op jit(solution)/shard_map/ppermute | solution.py:340
  160.9 32.3 %collective-permute-start.12 = (bf16[2,128,1024]{2,1,0:T(8,128)(2,1)S(1)}, bf16[2,128,1024]{2,1,0:T(8,128)(2,1)}, u32[]{:S(2)}, u32[]{:S(2)}) collective-permute-start(bf16[2,128,1024]{2,1,0:T(8,128)(2,1)S(1)} %copy-done.34), channel_id=1, source_target_pairs={{0,28},{4,16},{8,20},{12,24},{28,0},{16,4},{20,8},{24,12},{1,29},{... | collective-permute-start | bytes 1572872 | tf_op jit(solution)/shard_map/ppermute | solution.py:340
  160.9 38.3 %all-to-all-start.1 = ((bf16[4,2,128,1024]{3,2,1,0:T(8,128)(2,1)}), bf16[4,2,128,1024]{3,2,1,0:T(8,128)(2,1)S(1)}, u32[]{:S(2)}, u32[]{:S(2)}) async-start(bf16[4,2,128,1024]{3,2,1,0:T(8,128)(2,1)} %get-tuple-element.49), calls=%async_computation.1 | async-start | bytes 4194304 | tf_op jit(solution)/shard_map/all_to_all | solution.py:42
  166.5 1.0 copy-start.25
  167.6 1.0 copy-start.27
  168.6 1.0 copy-start.29
  169.7 1.0 copy-start.31
  193.2 13.6 %copy-start.37 = (bf16[2,128,1024]{2,1,0:T(8,128)(2,1)S(1)}, bf16[2,128,1024]{2,1,0:T(8,128)(2,1)}, u32[]{:S(2)}) copy-start(bf16[2,128,1024]{2,1,0:T(8,128)(2,1)} %get-tuple-element.69) | copy-start | bytes 1572868
  193.3 38.5 %copy-start.14 = (bf16[2,128,1024]{2,1,0:T(8,128)(2,1)S(1)}, bf16[2,128,1024]{2,1,0:T(8,128)(2,1)}, u32[]{:S(2)}) copy-start(bf16[2,128,1024]{2,1,0:T(8,128)(2,1)} %get-tuple-element.59.rest_0_) | copy-start | bytes 1572868
  199.2 144.3 %all-to-all-start.3 = ((bf16[8,2,128,1024]{3,2,1,0:T(8,128)(2,1)}), bf16[8,2,128,1024]{3,2,1,0:T(8,128)(2,1)}, u32[]{:S(2)}, u32[]{:S(2)}) async-start(bf16[8,2,128,1024]{3,2,1,0:T(8,128)(2,1)} %get-tuple-element.90), calls=%async_computation.3 | async-start | bytes 8388608 | tf_op jit(solution)/shard_map/all_to_all | solution.py:53
  206.3 13.5 %collective-permute-start.8 = (bf16[2,128,1024]{2,1,0:T(8,128)(2,1)}, bf16[2,128,1024]{2,1,0:T(8,128)(2,1)S(1)}, u32[]{:S(2)}, u32[]{:S(2)}) collective-permute-start(bf16[2,128,1024]{2,1,0:T(8,128)(2,1)} %get-tuple-element.67), channel_id=1, source_target_pairs={{0,1},{1,0},{2,3},{3,2},{4,5},{5,4},{6,7},{7,6},{8,9},{9,8},{10,11... | collective-permute-start | bytes 1572872 | tf_op jit(solution)/shard_map/ppermute | solution.py:30
  206.6 14.0 %collective-permute-start.9 = (bf16[2,128,1024]{2,1,0:T(8,128)(2,1)}, bf16[2,128,1024]{2,1,0:T(8,128)(2,1)S(1)}, u32[]{:S(2)}, u32[]{:S(2)}) collective-permute-start(bf16[2,128,1024]{2,1,0:T(8,128)(2,1)} %get-tuple-element.68), channel_id=1, source_target_pairs={{0,2},{1,3},{2,0},{3,1},{4,6},{5,7},{6,4},{7,5},{8,10},{9,11},{10,... | collective-permute-start | bytes 1572872 | tf_op jit(solution)/shard_map/ppermute | solution.py:30
  206.8 24.1 %collective-permute-start.10 = (bf16[2,128,1024]{2,1,0:T(8,128)(2,1)S(1)}, bf16[2,128,1024]{2,1,0:T(8,128)(2,1)S(1)}, u32[]{:S(2)}, u32[]{:S(2)}) collective-permute-start(bf16[2,128,1024]{2,1,0:T(8,128)(2,1)S(1)} %copy-done.37), channel_id=1, source_target_pairs={{0,3},{1,2},{2,1},{3,0},{4,7},{5,6},{6,5},{7,4},{8,11},{9,10},{10,... | collective-permute-start | bytes 1572872 | tf_op jit(solution)/shard_map/ppermute | solution.py:30
  231.8 1.0 copy-start.16
  232.8 1.0 copy-start.18
  233.9 1.0 copy-start.20
  236.0 1.0 copy-start.24
  260.8 69.7 %collective-permute-start.16 = (bf16[2,128,1024]{2,1,0:T(8,128)(2,1)}, bf16[2,128,1024]{2,1,0:T(8,128)(2,1)S(1)}, u32[]{:S(2)}, u32[]{:S(2)}) collective-permute-start(bf16[2,128,1024]{2,1,0:T(8,128)(2,1)} %get-tuple-element.82), channel_id=1, source_target_pairs={{0,16},{4,20},{8,24},{12,28},{16,0},{20,4},{24,8},{28,12},{1,17},{... | collective-permute-start | bytes 1572872 | tf_op jit(solution)/shard_map/ppermute | solution.py:340
  263.1 80.5 %collective-permute-start.17 = (bf16[2,128,1024]{2,1,0:T(8,128)(2,1)}, bf16[2,128,1024]{2,1,0:T(8,128)(2,1)S(1)}, u32[]{:S(2)}, u32[]{:S(2)}) collective-permute-start(bf16[2,128,1024]{2,1,0:T(8,128)(2,1)} %get-tuple-element.83), channel_id=1, source_target_pairs={{0,20},{4,24},{8,28},{12,16},{20,0},{24,4},{28,8},{16,12},{1,21},{... | collective-permute-start | bytes 1572872 | tf_op jit(solution)/shard_map/ppermute | solution.py:340
  343.5 52.7 %all-to-all-start.2 = ((bf16[4,2,128,1024]{3,2,1,0:T(8,128)(2,1)}), bf16[4,2,128,1024]{3,2,1,0:T(8,128)(2,1)S(1)}, u32[]{:S(2)}, u32[]{:S(2)}) async-start(bf16[4,2,128,1024]{3,2,1,0:T(8,128)(2,1)} %get-tuple-element.84), calls=%async_computation.2 | async-start | bytes 4194304 | tf_op jit(solution)/shard_map/all_to_all | solution.py:42
  348.4 13.4 %collective-permute-start.13 = (bf16[2,128,1024]{2,1,0:T(8,128)(2,1)}, bf16[2,128,1024]{2,1,0:T(8,128)(2,1)S(1)}, u32[]{:S(2)}, u32[]{:S(2)}) collective-permute-start(bf16[2,128,1024]{2,1,0:T(8,128)(2,1)} %get-tuple-element.76), channel_id=1, source_target_pairs={{0,1},{1,0},{2,3},{3,2},{4,5},{5,4},{6,7},{7,6},{8,9},{9,8},{10,11... | collective-permute-start | bytes 1572872 | tf_op jit(solution)/shard_map/ppermute | solution.py:30
  348.7 13.1 %collective-permute-start.14 = (bf16[2,128,1024]{2,1,0:T(8,128)(2,1)}, bf16[2,128,1024]{2,1,0:T(8,128)(2,1)S(1)}, u32[]{:S(2)}, u32[]{:S(2)}) collective-permute-start(bf16[2,128,1024]{2,1,0:T(8,128)(2,1)} %get-tuple-element.77), channel_id=1, source_target_pairs={{0,2},{1,3},{2,0},{3,1},{4,6},{5,7},{6,4},{7,5},{8,10},{9,11},{10,... | collective-permute-start | bytes 1572872 | tf_op jit(solution)/shard_map/ppermute | solution.py:30
  348.9 24.1 %collective-permute-start.15 = (bf16[2,128,1024]{2,1,0:T(8,128)(2,1)}, bf16[2,128,1024]{2,1,0:T(8,128)(2,1)S(1)}, u32[]{:S(2)}, u32[]{:S(2)}) collective-permute-start(bf16[2,128,1024]{2,1,0:T(8,128)(2,1)} %get-tuple-element.78), channel_id=1, source_target_pairs={{0,3},{1,2},{2,1},{3,0},{4,7},{5,6},{6,5},{7,4},{8,11},{9,10},{10,... | collective-permute-start | bytes 1572872 | tf_op jit(solution)/shard_map/ppermute | solution.py:30
  351.1 34.1 %collective-permute-start.18 = (bf16[2,128,1024]{2,1,0:T(8,128)(2,1)}, bf16[2,128,1024]{2,1,0:T(8,128)(2,1)S(1)}, u32[]{:S(2)}, u32[]{:S(2)}) collective-permute-start(bf16[2,128,1024]{2,1,0:T(8,128)(2,1)} %get-tuple-element.86), channel_id=1, source_target_pairs={{0,24},{4,28},{8,16},{12,20},{24,0},{28,4},{16,8},{20,12},{1,25},{... | collective-permute-start | bytes 1572872 | tf_op jit(solution)/shard_map/ppermute | solution.py:340
  351.1 44.3 %collective-permute-start.19 = (bf16[2,128,1024]{2,1,0:T(8,128)(2,1)}, bf16[2,128,1024]{2,1,0:T(8,128)(2,1)S(1)}, u32[]{:S(2)}, u32[]{:S(2)}) collective-permute-start(bf16[2,128,1024]{2,1,0:T(8,128)(2,1)} %get-tuple-element.88), channel_id=1, source_target_pairs={{0,28},{4,16},{8,20},{12,24},{28,0},{16,4},{20,8},{24,12},{1,29},{... | collective-permute-start | bytes 1572872 | tf_op jit(solution)/shard_map/ppermute | solution.py:340
  373.0 1.0 copy-start.6
  374.0 1.0 copy-start.8
  375.1 1.0 copy-start.10
  376.1 1.0 copy-start.12
  377.2 1.0 copy-start.13
  396.2 1.0 copy-start.3
  (14 other events, 11.7 us)

commit v16 on v15

--- a/solution.py
+++ b/solution.py
@@ -42,6 +42,15 @@
     return lax.all_to_all(
         array, "enc", split_axis=0, concat_axis=0, axis_index_groups=groups, tiled=True
     )
+
+
+def swap_half(pieces, count):
+    half = count // 2
+    got = [pieces[0]]
+    for step in range(1, half):
+        pairs = [(i, i - i % half + partner(i % half, step, half)) for i in range(count)]
+        got.append(lax.ppermute(pieces[step], "enc", pairs))
+    return got
 
 
 def swap_rows(pieces):
@@ -132,27 +141,30 @@
     )(*flat)
 
 
-def kv_shapes(seqs, chunk, split):
+def kv_shapes(seqs, chunk, form):
     half = seqs // 2
-    if split:
-        return [(half, 2, NBLEN, chunk)] + [(2, NBLEN, chunk)] * half
-    return [(seqs, 2, NBLEN, chunk)]
-
-
-def kv_views(refs, seqs, split):
-    if not split:
+    one = (2, NBLEN, chunk)
+    return [[(seqs, *one)], [(half, *one)] + [one] * half, [one] * seqs][form]
+
+
+def kv_views(refs, seqs, form):
+    if form == 0:
         return [(seq, refs[0].at[seq]) for seq in range(seqs)]
     half = seqs // 2
     me = lax.axis_index("enc")
-    near = [(me - me % half + step, refs[0].at[step]) for step in range(half)]
-    return near + [(across(me, step, seqs), refs[1 + step]) for step in range(half)]
-
-
-def pick_kernel(first, split, seqs, lists, pool_ref, *rest):
+    base = me - me % half
+    if form == 1:
+        near = [(base + step, refs[0].at[step]) for step in range(half)]
+    else:
+        near = [(base + partner(me % half, step, half), refs[step]) for step in range(half)]
+    return near + [(across(me, step, seqs), refs[step - half]) for step in range(half)]
+
+
+def pick_kernel(first, form, seqs, lists, pool_ref, *rest):
     outs, held, sems = rest[:-2], rest[-2], rest[-1]
     chunk = held.shape[-1]
     arriving, leaving = [], []
-    for n, (seq, out) in enumerate(kv_views(outs, seqs, split)):
+    for n, (seq, out) in enumerate(kv_views(outs, seqs, form)):
         source = pool_ref.at[lists[0, seq, 0], :, :, first : first + chunk]
         arriving.append(pltpu.make_async_copy(source, held.at[n], sems.at[0, n]))
         leaving.append(pltpu.make_async_copy(held.at[n], out, sems.at[1, n]))
@@ -164,11 +176,11 @@
         leaving[n].wait()
 
 
-def pick(first, chunk, split, send_lists, kv_pool):
+def pick(first, chunk, form, send_lists, kv_pool):
     seqs = send_lists.shape[1]
-    shapes = kv_shapes(seqs, chunk, split)
+    shapes = kv_shapes(seqs, chunk, form)
     return pl.pallas_call(
-        functools.partial(pick_kernel, first, split, seqs),
+        functools.partial(pick_kernel, first, form, seqs),
         grid=(1,),
         in_specs=[SCALARS, IN_HBM],
         out_specs=[IN_HBM] * len(shapes),
@@ -189,18 +201,17 @@
     )
 
 
-def attend_kernel(seqs, parts, split, uses, *rest):
-    pieces = 1 + seqs // 2 if split else 1
+def attend_kernel(seqs, parts, forms, pieces, uses, *rest):
     rows_in, rest = rest[:parts], rest[parts:]
-    kv_in, rest = rest[:pieces], rest[pieces:]
+    kv_in, rest = rest[: pieces[0]], rest[pieces[0] :]
     rows_out, rest = rest[:parts], rest[parts:]
-    kv_out, rest = rest[:pieces], rest[pieces:]
-    held, rows, made, sums = rest if split else (kv_in[0], *rest)
+    kv_out, rest = rest[: pieces[1]], rest[pieces[1] :]
+    held, rows, made, sums = rest if forms[0] else (kv_in[0], *rest)
     scale = DH ** (-0.5)
     mine = lax.axis_index("seq")
 
-    if split:
-        for slot, piece in kv_views(kv_in, seqs, split):
+    if forms[0]:
+        for slot, piece in kv_views(kv_in, seqs, forms[0]):
             held[slot] = piece[...]
     for step in range(parts):
         for n in range(2):
@@ -259,7 +270,7 @@
         for n in range(2):
             piece = made[partner(mine, step, parts), n]
             rows_out[step][n] = pltpu.roll(piece, 2 * BLOCK - 1, 0).astype(BF16)
-    for slot, piece in kv_views(kv_out, seqs, split):
+    for slot, piece in kv_views(kv_out, seqs, forms[1]):
         piece[...] = sums[slot].astype(BF16)
 
 
@@ -267,28 +278,27 @@
     return pl.BlockSpec((*shape[:-1], wide), lambda i, n=len(shape) - 1: (0,) * n + (i,))
 
 
-def attend(uses, rows_in, kv_in):
+def attend(seqs, forms, uses, rows_in, kv_in):
     parts, part_rows = len(rows_in), rows_in[0].shape[1]
-    split = len(kv_in) > 1
-    seqs = 2 * kv_in[0].shape[0] if split else kv_in[0].shape[0]
     chunk = kv_in[0].shape[-1]
     heads = chunk // DH
-    shapes = [array.shape for array in (*rows_in, *kv_in)]
-    specs = [heads_spec(shape, DH) for shape in shapes]
+    rows_shapes = [array.shape for array in rows_in]
+    in_shapes, out_shapes = (kv_shapes(seqs, chunk, form) for form in forms)
     pairs = heads * parts * part_rows * 2 * NBLEN
-    held = [pltpu.VMEM((seqs, 2, NBLEN, DH), BF16)] if split else []
+    held = [pltpu.VMEM((seqs, 2, NBLEN, DH), BF16)] if forms[0] else []
+    pieces = (len(in_shapes), len(out_shapes))
     outs = pl.pallas_call(
-        functools.partial(attend_kernel, seqs, parts, split),
+        functools.partial(attend_kernel, seqs, parts, forms, pieces),
         grid=(heads,),
-        in_specs=[SCALARS] + specs,
-        out_specs=specs,
+        in_specs=[SCALARS] + [heads_spec(shape, DH) for shape in rows_shapes + in_shapes],
+        out_specs=[heads_spec(shape, DH) for shape in rows_shapes + out_shapes],
         scratch_shapes=held
         + [
             pltpu.VMEM((parts + 1, 2, part_rows, DH), F32),
             pltpu.VMEM((parts + 1, 2, part_rows, DH), F32),
             pltpu.VMEM((seqs, 2, NBLEN, DH), F32),
         ],
-        out_shape=[in_hbm(shape) for shape in shapes],
+        out_shape=[in_hbm(shape) for shape in rows_shapes + out_shapes],
         compiler_params=PARAMS,
         cost_estimate=cost(
             8 * (seqs + parts) * NBLEN * chunk, ATTEND_WEIGHT * 12 * DH * pairs, pairs
@@ -298,15 +308,15 @@
     return outs[:parts], outs[parts:]
 
 
-def owner_kernel(seqs, pieces, lists, *rest):
+def owner_kernel(seqs, form, pieces, lists, *rest):
     out_ref, acc = rest[-2], rest[-1]
     acc[...] = jnp.zeros_like(acc)
-    for seq, piece in kv_views(rest[:pieces], seqs, pieces > 1):
+    for seq, piece in kv_views(rest[:pieces], seqs, form):
         acc[lists[0, seq, 0]] += piece[...].astype(F32)
     out_ref[...] = acc[...].astype(BF16)
 
 
-def owner_sum(first, send_lists, back, shape, so_far):
+def owner_sum(first, form, send_lists, back, shape, so_far):
     seqs = send_lists.shape[1]
     chunk = back[0].shape[-1]
     wide = math.gcd(math.gcd(first, chunk), 256)
@@ -314,7 +324,7 @@
     extra = [] if so_far is None else [so_far]
     specs = [heads_spec(array.shape, wide) for array in back]
     return pl.pallas_call(
-        functools.partial(owner_kernel, seqs, len(back)),
+        functools.partial(owner_kernel, seqs, form, len(back)),
         grid=(steps,),
         in_specs=[SCALARS] + specs + [ANYWHERE] * len(extra),
         out_specs=pl.BlockSpec(
@@ -329,14 +339,14 @@
     )(send_lists, *back, *extra)
 
 
-def swap_far(pieces):
+def swap_far(pieces, depth):
     half = len(pieces)
     got = []
     for step, piece in enumerate(pieces):
         there = [half + (i + step) % half for i in range(half)]
         pairs = list(enumerate(there)) + [(peer, i) for i, peer in enumerate(there)]
-        if step >= 2:
-            piece = after(piece, got[step - 2])
+        if step >= depth:
+            piece = after(piece, got[step - depth])
         got.append(lax.ppermute(piece, "enc", pairs))
     return got
 
@@ -347,32 +357,34 @@
     bounds = [(0, cut), (cut, width - cut)]
     firsts = [first for first, _ in bounds]
 
-    picked = pick(*bounds[0], False, send_lists, kv_pool)
+    picked = pick(*bounds[0], 0, send_lists, kv_pool)
     send_lists, queries = after((send_lists, queries), picked[0])
     early = swap_pool(picked[0])
-    near, *far = pick(*bounds[1], True, send_lists, kv_pool)
+    near, *far = pick(*bounds[1], 1, send_lists, kv_pool)
     queries = after(queries, near)
     rows = [
         swap_rows(pack(first, chunk, queries, grad_context, width, parts))
         for first, chunk in bounds
     ]
-    far = swap_far(after(far, rows))
+    far = swap_far(after(far, rows), seqs)
     near = swap_near(near, seqs)
 
-    early = after(early, (far[:2], rows))
-    rows_out, whole = attend(block_slots, rows[0], [early])
+    early = after(early, far[0])
+    rows_out, whole = attend(seqs, (0, 0), block_slots, rows[0], [early])
     token_parts = [swap_rows(rows_out)]
     returns = [[swap_pool(after(whole[0], far))]]
     block_slots = after(block_slots, token_parts[0])
-    rows_out, (near, *far) = attend(block_slots, rows[1], [near, *far])
-    far = swap_far(far)
+    rows_out, back = attend(seqs, (1, 2), block_slots, rows[1], [near, *far])
+    near, far = back[: seqs // 2], back[seqs // 2 :]
+    far = swap_far(far, 2)
     token_parts.append(swap_rows(rows_out))
-    returns.append([swap_near(after(near, far[:2]), seqs), *far])
+    near = swap_half(after(near, token_parts[1]), seqs)
+    returns.append([*near, *far])
 
     context, grad_queries = unpack(token_parts, firsts, width, queries.shape)
     pool_grads = None
-    for first, back in zip(firsts, returns):
-        pool_grads = owner_sum(first, send_lists, back, kv_pool.shape, pool_grads)
+    for first, form, back in zip(firsts, (0, 2), returns):
+        pool_grads = owner_sum(first, form, send_lists, back, kv_pool.shape, pool_grads)
     return (context, grad_queries, pool_grads)
 
 

time: 408 us -> 389 us (0.953)
  local copies, waits for them, and re-layouts: 27.5 us -> 15.9 us
  waiting for transfers between devices: 261 us -> 250 us
    ppermute x8, waiting for transfers between devices: 178 us -> 100 us  [swap_far(): got.append(lax.ppermute(piece, 'enc', pairs))]
    all_to_all x2, waiting for transfers between devices: 0.01 us -> 73.9 us  [swap_pool(): return lax.all_to_all(array, 'enc', split_axis=0, concat_axis=0, tiled=True)]
    unnamed x78 -> x58, local copies, waits for them, and re-layouts: 27.4 us -> 15.8 us
    all_to_all x2 -> x1, waiting for transfers between devices: 5.94 us -> 0.1 us  [swap_near(): lax.all_to_all(array, 'enc', split_axis=0, concat_axis=0, axis_index_grou...]
    ppermute x0 -> x3, starting transfers between devices: none -> 4.95 us  [swap_half(): got.append(lax.ppermute(pieces[step], 'enc', pairs))]
    all_to_all x2 -> x1, starting transfers between devices: 10.5 us -> 7.72 us  [swap_near(): lax.all_to_all(array, 'enc', split_axis=0, concat_axis=0, axis_index_grou...]
  transfers between devices with their start and end apart: 24 -> 26, of which waited for: 14 -> 17; matrix products, arithmetic and copies ran while one was open for 0% -> 0% of each run, Pallas kernels for 15% -> 16%
where the time goes in v16:
time: 389 us; the launch traced here: 384 us
  waiting for transfers between devices  250 us (64%)
  Pallas kernels  69.6 us (18%)
  starting transfers between devices  47.3 us (12%)
  local copies, waits for them, and re-layouts  15.9 us (4%)
    ppermute x8, waiting for transfers between devices, swap_far(): got.append(lax.ppermute(piece, 'enc', pairs))  100 us
    ppermute x12, waiting for transfers between devices, exchange(): return lax.ppermute(array, axis, pairs)  76.3 us
    all_to_all x2, waiting for transfers between devices, swap_pool(): return lax.all_to_all(array, 'enc', split_axis=0, concat_axis=0, tiled=True)  73.9 us
    pallas_call x2, Pallas kernels, attend(): pl.pallas_call(functools.partial(attend_kernel, seqs, parts, forms, piece...  46.3 us
    unnamed x58, local copies, waits for them, and re-layouts  15.8 us
    all_to_all x2, starting transfers between devices, swap_pool(): return lax.all_to_all(array, 'enc', split_axis=0, concat_axis=0, tiled=True)  13.1 us
    ppermute x8, starting transfers between devices, swap_far(): got.append(lax.ppermute(piece, 'enc', pairs))  12.1 us
    ppermute x12, starting transfers between devices, exchange(): return lax.ppermute(array, axis, pairs)  9.51 us
  transfers between devices with their start and end apart: 26, of which 17 were waited for; matrix products, arithmetic and copies ran while one was open for 0% of the time, Pallas kernels for 16%

profile of v16, /device:TPU:15, one launch (start us, length us, event | category | flops | bytes accessed | tf_op | source)
XLA Modules:
  0.0 384.0 jit_solution(13735772986411731391)
XLA Ops:
  1.4 4.2 %pick_entries.2 = bf16[8,2,128,1024]{3,2,1,0:T(8,128)(2,1)} custom-call(s32[1,8,1]{2,1,0:T(8,128)S(1)} %copy.9.lists, bf16[4,2,128,2048]{3,2,1,0:T(8,128)(2,1)} %pool_ref.3), custom_call_target="tpu_custom_call" | custom-call | bytes 8388608 | tf_op jit(solution)/shard_map/pick_entries/pallas_call | solution.py:182
  5.6 5.6 %all-to-all-start = ((bf16[8,2,128,1024]{3,2,1,0:T(8,128)(2,1)}), bf16[8,2,128,1024]{3,2,1,0:T(8,128)(2,1)}, u32[]{:S(2)}, u32[]{:S(2)}) async-start(bf16[8,2,128,1024]{3,2,1,0:T(8,128)(2,1)} %pick_entries.2), calls=%async_computation | async-start | bytes 8388608 | tf_op jit(solution)/shard_map/all_to_all | solution.py:62
  11.3 4.5 %pick_entries.3 = (bf16[4,2,128,1024]{3,2,1,0:T(8,128)(2,1)}, bf16[2,128,1024]{2,1,0:T(8,128)(2,1)}, bf16[2,128,1024]{2,1,0:T(8,128)(2,1)}, bf16[2,128,1024]{2,1,0:T(8,128)(2,1)}, bf16[2,128,1024]{2,1,0:T(8,128)(2,1)}) custom-call(s32[1,8,1]{2,1,0:T(8,128)S(1)} %copy.10.lists, bf16[4,2,128,2048]{3,2,1,0:T(8,128)(2,1)} %pool_ref.3), custom_call_target="tpu_custom_call" | custom-call | bytes 8388608 | tf_op jit(solution)/shard_map/pick_entries/pallas_call | solution.py:182
  15.9 1.6 pack_rows.3
  18.1 2.2 collective-permute-start.5
  20.2 1.6 pack_rows.2
  22.3 8.6 %collective-permute-done.3.rest_1_ = bf16[2,128,1024]{2,1,0:T(8,128)(2,1)S(1)} collective-permute-done((bf16[2,128,1024]{2,1,0:T(8,128)(2,1)}, bf16[2,128,1024]{2,1,0:T(8,128)(2,1)S(1)}, u32[]{:S(2)}, u32[]{:S(2)}) %collective-permute-start.3) | collective-permute-done | bytes 524320 | tf_op jit(solution)/shard_map/ppermute | solution.py:30
  30.9 0.9 copy-done.12
  32.0 10.1 %collective-permute-done.5.rest_3_ = bf16[2,128,1024]{2,1,0:T(8,128)(2,1)S(1)} collective-permute-done((bf16[2,128,1024]{2,1,0:T(8,128)(2,1)}, bf16[2,128,1024]{2,1,0:T(8,128)(2,1)S(1)}, u32[]{:S(2)}, u32[]{:S(2)}) %collective-permute-start.5) | collective-permute-done | bytes 524320 | tf_op jit(solution)/shard_map/ppermute | solution.py:30
  43.0 10.6 %collective-permute-done.rest_1_ = bf16[2,128,1024]{2,1,0:T(8,128)(2,1)S(1)} collective-permute-done((bf16[2,128,1024]{2,1,0:T(8,128)(2,1)}, bf16[2,128,1024]{2,1,0:T(8,128)(2,1)S(1)}, u32[]{:S(2)}, u32[]{:S(2)}) %collective-permute-start) | collective-permute-done | bytes 524320 | tf_op jit(solution)/shard_map/ppermute | solution.py:30
  55.2 9.5 %collective-permute-done.2.rest_3_ = bf16[2,128,1024]{2,1,0:T(8,128)(2,1)S(1)} collective-permute-done((bf16[2,128,1024]{2,1,0:T(8,128)(2,1)}, bf16[2,128,1024]{2,1,0:T(8,128)(2,1)S(1)}, u32[]{:S(2)}, u32[]{:S(2)}) %collective-permute-start.2) | collective-permute-done | bytes 524320 | tf_op jit(solution)/shard_map/ppermute | solution.py:30
  65.5 2.1 collective-permute-start.6
  67.7 1.6 collective-permute-start.10
  69.2 2.3 collective-permute-start.11
  71.5 1.2 collective-permute-start.12
  72.8 73.9 %all-to-all-done.rest_4_ = bf16[8,2,128,1024]{3,2,1,0:T(8,128)(2,1)} async-done(((bf16[8,2,128,1024]{3,2,1,0:T(8,128)(2,1)}), bf16[8,2,128,1024]{3,2,1,0:T(8,128)(2,1)}, u32[]{:S(2)}, u32[]{:S(2)}) %all-to-all-start) | async-done | bytes 4194336 | tf_op jit(solution)/shard_map/all_to_all | solution.py:62
  146.6 7.7 %all-to-all-start.1 = ((bf16[4,2,128,1024]{3,2,1,0:T(8,128)(2,1)}), bf16[4,2,128,1024]{3,2,1,0:T(8,128)(2,1)S(1)}, u32[]{:S(2)}, u32[]{:S(2)}) async-start(bf16[4,2,128,1024]{3,2,1,0:T(8,128)(2,1)} %get-tuple-element.53), calls=%async_computation.1 | async-start | bytes 4194304 | tf_op jit(solution)/shard_map/all_to_all | solution.py:42
  154.3 3.6 collective-permute-done.6.rest_5_
  157.9 1.0 copy-done.18
  158.9 1.0 copy-done.20
  160.0 1.0 copy-done.22
  161.0 1.0 copy-done.24
  162.1 22.6 %attend_blocks.2 = (bf16[2,128,1024]{2,1,0:T(8,128)(2,1)}, bf16[2,128,1024]{2,1,0:T(8,128)(2,1)}, bf16[2,128,1024]{2,1,0:T(8,128)(2,1)}, bf16[2,128,1024]{2,1,0:T(8,128)(2,1)}, bf16[8,2,128,1024]{3,2,1,0:T(8,128)(2,1)}) custom-call(s32[1,8,2]{2,1,0:T(8,128)S(1)} %copy.11.uses, bf16[2,128,1024]{2,1,0:T(8,128)(2,1)S(1)} %copy-done.18, ...), custom_call_target="tpu_custom_call" | custom-call | flops 38654705664 | bytes 12582912 | tf_op jit(solution)/shard_map/attend_blocks/pallas_call | solution.py:290
  184.7 6.8 %collective-permute-done.12.rest_8_ = bf16[2,128,1024]{2,1,0:T(8,128)(2,1)} collective-permute-done((bf16[2,128,1024]{2,1,0:T(8,128)(2,1)S(1)}, bf16[2,128,1024]{2,1,0:T(8,128)(2,1)}, u32[]{:S(2)}, u32[]{:S(2)}) %collective-permute-start.12) | collective-permute-done | bytes 524320 | tf_op jit(solution)/shard_map/ppermute | solution.py:350
  191.6 7.4 %all-to-all-start.2 = ((bf16[8,2,128,1024]{3,2,1,0:T(8,128)(2,1)}), bf16[8,2,128,1024]{3,2,1,0:T(8,128)(2,1)}, u32[]{:S(2)}, u32[]{:S(2)}) async-start(bf16[8,2,128,1024]{3,2,1,0:T(8,128)(2,1)} %get-tuple-element.98), calls=%async_computation.2 | async-start | bytes 8388608 | tf_op jit(solution)/shard_map/all_to_all | solution.py:62
  199.5 2.2 collective-permute-start.9
  201.7 10.8 %collective-permute-done.7.refs_1_ = bf16[2,128,1024]{2,1,0:T(8,128)(2,1)S(1)} collective-permute-done((bf16[2,128,1024]{2,1,0:T(8,128)(2,1)}, bf16[2,128,1024]{2,1,0:T(8,128)(2,1)S(1)}, u32[]{:S(2)}, u32[]{:S(2)}) %collective-permute-start.7) | collective-permute-done | bytes 524320 | tf_op jit(solution)/shard_map/ppermute | solution.py:30
  214.1 9.5 %collective-permute-done.9.refs_3_ = bf16[2,128,1024]{2,1,0:T(8,128)(2,1)S(1)} collective-permute-done((bf16[2,128,1024]{2,1,0:T(8,128)(2,1)}, bf16[2,128,1024]{2,1,0:T(8,128)(2,1)S(1)}, u32[]{:S(2)}, u32[]{:S(2)}) %collective-permute-start.9) | collective-permute-done | bytes 524320 | tf_op jit(solution)/shard_map/ppermute | solution.py:30
  224.6 1.0 copy-done.13
  225.6 1.0 copy-done.15
  226.6 1.0 copy-done.17
  227.7 23.8 %attend_blocks.3 = (bf16[2,128,1024]{2,1,0:T(8,128)(2,1)}, bf16[2,128,1024]{2,1,0:T(8,128)(2,1)}, bf16[2,128,1024]{2,1,0:T(8,128)(2,1)}, bf16[2,128,1024]{2,1,0:...) custom-call(s32[1,8,2]{2,1,0:T(8,128)S(1)} %copy.12.uses, ...), custom_call_target="tpu_custom_call" | custom-call | flops 38654705664 | bytes 12582912 | tf_op jit(solution)/shard_map/attend_blocks/pallas_call | solution.py:290
  251.5 2.1 collective-permute-start.13
  253.6 1.3 collective-permute-start.15
  254.9 2.1 collective-permute-start.19
  257.0 2.0 collective-permute-start.20
  259.0 5.2 %collective-permute-done.13.refs_5_ = bf16[2,128,1024]{2,1,0:T(8,128)(2,1)S(1)} collective-permute-done((bf16[2,128,1024]{2,1,0:T(8,128)(2,1)}, bf16[2,128,1024]{2,1,0:T(8,128)(2,1)S(1)}, u32[]{:S(2)}, u32[]{:S(2)}) %collective-permute-start.13) | collective-permute-done | bytes 524320 | tf_op jit(solution)/shard_map/ppermute | solution.py:30
  264.2 2.2 collective-permute-done.14.refs_6_
  266.4 9.7 %collective-permute-done.15.refs_7_ = bf16[2,128,1024]{2,1,0:T(8,128)(2,1)S(1)} collective-permute-done((bf16[2,128,1024]{2,1,0:T(8,128)(2,1)}, bf16[2,128,1024]{2,1,0:T(8,128)(2,1)S(1)}, u32[]{:S(2)}, u32[]{:S(2)}) %collective-permute-start.15) | collective-permute-done | bytes 524320 | tf_op jit(solution)/shard_map/ppermute | solution.py:30
  276.1 3.3 collective-permute-start.16
  281.0 42.4 %collective-permute-done.19.rest_4_ = bf16[2,128,1024]{2,1,0:T(8,128)(2,1)S(1)} collective-permute-done((bf16[2,128,1024]{2,1,0:T(8,128)(2,1)}, bf16[2,128,1024]{2,1,0:T(8,128)(2,1)S(1)}, u32[]{:S(2)}, u32[]{:S(2)}) %collective-permute-start.19) | collective-permute-done | bytes 524320 | tf_op jit(solution)/shard_map/ppermute | solution.py:350
  324.2 23.8 %collective-permute-done.20.rest_5_ = bf16[2,128,1024]{2,1,0:T(8,128)(2,1)S(1)} collective-permute-done((bf16[2,128,1024]{2,1,0:T(8,128)(2,1)}, bf16[2,128,1024]{2,1,0:T(8,128)(2,1)S(1)}, u32[]{:S(2)}, u32[]{:S(2)}) %collective-permute-start.20) | collective-permute-done | bytes 524320 | tf_op jit(solution)/shard_map/ppermute | solution.py:350
  348.0 1.0 copy-done.10
  349.0 2.1 unpack_rows.1
  351.1 4.8 %owner_sum.2.rest_8_ = bf16[4,2,128,2048]{3,2,1,0:T(8,128)(2,1)} custom-call(s32[1,8,1]{2,1,0:T(8,128)S(1)} %copy.10.lists, bf16[8,2,128,1024]{3,2,1,0:T(8,128)(2,1)} %all-to-all-done.2.rest_0_), custom_call_target="tpu_custom_call" | custom-call | flops 2097152 | bytes 6291456 | tf_op jit(solution)/shard_map/owner_sum/pallas_call | solution.py:326
  356.0 13.9 %collective-permute-done.21.rest_6_ = bf16[2,128,1024]{2,1,0:T(8,128)(2,1)} collective-permute-done((bf16[2,128,1024]{2,1,0:T(8,128)(2,1)}, bf16[2,128,1024]{2,1,0:T(8,128)(2,1)}, u32[]{:S(2)}, u32[]{:S(2)}) %collective-permute-start.21) | collective-permute-done | bytes 524320 | tf_op jit(solution)/shard_map/ppermute | solution.py:350
  369.8 9.7 %collective-permute-done.22.rest_7_ = bf16[2,128,1024]{2,1,0:T(8,128)(2,1)} collective-permute-done((bf16[2,128,1024]{2,1,0:T(8,128)(2,1)}, bf16[2,128,1024]{2,1,0:T(8,128)(2,1)}, u32[]{:S(2)}, u32[]{:S(2)}) %collective-permute-start.22) | collective-permute-done | bytes 524320 | tf_op jit(solution)/shard_map/ppermute | solution.py:350
  379.6 4.5 %owner_sum.3 = bf16[4,2,128,2048]{3,2,1,0:T(8,128)(2,1)} custom-call(s32[1,8,1]{2,1,0:T(8,128)S(1)} %copy.10.lists, bf16[2,128,1024]{2,1,0:T(8,128)(2,1)S(1)} %copy-done.2, bf16[2,128,1024]{2,1,0:T(8,128)(2,1)S(1)} %collective-permute-done.16.rest_1_, bf16[2,128,1024]{2,1,0:T(8,128)(2,1)S(1)} %collective-permute-done.17.rest_2_, ...), custom_call_target="tpu_custom_call", output_to_operand_aliasing={{}: (9, {})} | custom-call | flops 2097152 | bytes 6291456 | tf_op jit(solution)/shard_map/owner_sum/pallas_call | solution.py:326
  (73 shorter events, 11.0 us)
Async XLA Ops:
  5.5 5.7 %copy-start.26 = (s32[1,8,1]{1,2,0:T(1,128)S(1)}, s32[1,8,1]{1,2,0:T(1,128)}, u32[]{:S(2)}) copy-start(s32[1,8,1]{1,2,0:T(1,128)} %param.7) | copy-start | bytes 100
  5.6 141.0 %all-to-all-start = ((bf16[8,2,128,1024]{3,2,1,0:T(8,128)(2,1)}), bf16[8,2,128,1024]{3,2,1,0:T(8,128)(2,1)}, u32[]{:S(2)}, u32[]{:S(2)}) async-start(bf16[8,2,128,1024]{3,2,1,0:T(8,128)(2,1)} %pick_entries.2), calls=%async_computation | async-start | bytes 8388608 | tf_op jit(solution)/shard_map/all_to_all | solution.py:62
  11.2 4.6 %copy-start = (bf16[1,128,8192]{2,1,0:T(8,128)(2,1)S(1)}, bf16[1,128,8192]{2,1,0:T(8,128)(2,1)}, u32[]{:S(2)}) copy-start(bf16[1,128,8192]{2,1,0:T(8,128)(2,1)} %q_ref.1) | copy-start | bytes 6291460
  11.3 4.6 %copy-start.1 = (bf16[1,128,8192]{2,1,0:T(8,128)(2,1)S(1)}, bf16[1,128,8192]{2,1,0:T(8,128)(2,1)}, u32[]{:S(2)}) copy-start(bf16[1,128,8192]{2,1,0:T(8,128)(2,1)} %g_ref.3) | copy-start | bytes 6291460
  15.9 51.7 %copy-start.25 = (s32[1,8,2]{1,2,0:T(2,128)S(1)}, s32[1,8,2]{1,2,0:T(2,128)}, u32[]{:S(2)}) copy-start(s32[1,8,2]{1,2,0:T(2,128)} %param.8) | copy-start | bytes 196
  15.9 55.6 %copy-start.27 = (bf16[2,128,1024]{2,1,0:T(8,128)(2,1)S(1)}, bf16[2,128,1024]{2,1,0:T(8,128)(2,1)}, u32[]{:S(2)}) copy-start(bf16[2,128,1024]{2,1,0:T(8,128)(2,1)} %get-tuple-element.76) | copy-start | bytes 1572868
  17.5 13.4 %collective-permute-start.3 = (bf16[2,128,1024]{2,1,0:T(8,128)(2,1)}, bf16[2,128,1024]{2,1,0:T(8,128)(2,1)S(1)}, u32[]{:S(2)}, u32[]{:S(2)}) collective-permute-start(bf16[2,128,1024]{2,1,0:T(8,128)(2,1)} %get-tuple-element.64), channel_id=1, source_target_pairs={{0,1},{1,0},{2,3},{3,2},{4,5},{5,4},{6,7},{7,6},{8,9},{9,8},{10,11... | collective-permute-start | bytes 1572872 | tf_op jit(solution)/shard_map/ppermute | solution.py:30
  17.8 14.2 %collective-permute-start.4 = (bf16[2,128,1024]{2,1,0:T(8,128)(2,1)}, bf16[2,128,1024]{2,1,0:T(8,128)(2,1)S(1)}, u32[]{:S(2)}, u32[]{:S(2)}) collective-permute-start(bf16[2,128,1024]{2,1,0:T(8,128)(2,1)} %get-tuple-element.65), channel_id=1, source_target_pairs={{0,2},{1,3},{2,0},{3,1},{4,6},{5,7},{6,4},{7,5},{8,10},{9,11},{10,... | collective-permute-start | bytes 1572872 | tf_op jit(solution)/shard_map/ppermute | solution.py:30
  18.1 24.1 %collective-permute-start.5 = (bf16[2,128,1024]{2,1,0:T(8,128)(2,1)}, bf16[2,128,1024]{2,1,0:T(8,128)(2,1)S(1)}, u32[]{:S(2)}, u32[]{:S(2)}) collective-permute-start(bf16[2,128,1024]{2,1,0:T(8,128)(2,1)} %get-tuple-element.66), channel_id=1, source_target_pairs={{0,3},{1,2},{2,1},{3,0},{4,7},{5,6},{6,5},{7,4},{8,11},{9,10},{10,... | collective-permute-start | bytes 1572872 | tf_op jit(solution)/shard_map/ppermute | solution.py:30
  21.8 31.8 %collective-permute-start = (bf16[2,128,1024]{2,1,0:T(8,128)(2,1)}, bf16[2,128,1024]{2,1,0:T(8,128)(2,1)S(1)}, u32[]{:S(2)}, u32[]{:S(2)}) collective-permute-start(bf16[2,128,1024]{2,1,0:T(8,128)(2,1)} %get-tuple-element.56), channel_id=1, source_target_pairs={{0,1},{1,0},{2,3},{3,2},{4,5},{5,4},{6,7},{7,6},{8,9},{9,8},{10,11... | collective-permute-start | bytes 1572872 | tf_op jit(solution)/shard_map/ppermute | solution.py:30
  22.1 32.3 %collective-permute-start.1 = (bf16[2,128,1024]{2,1,0:T(8,128)(2,1)}, bf16[2,128,1024]{2,1,0:T(8,128)(2,1)S(1)}, u32[]{:S(2)}, u32[]{:S(2)}) collective-permute-start(bf16[2,128,1024]{2,1,0:T(8,128)(2,1)} %get-tuple-element.57), channel_id=1, source_target_pairs={{0,2},{1,3},{2,0},{3,1},{4,6},{5,7},{6,4},{7,5},{8,10},{9,11},{10,... | collective-permute-start | bytes 1572872 | tf_op jit(solution)/shard_map/ppermute | solution.py:30
  30.9 0.9 copy-start.12
  31.8 32.9 %collective-permute-start.2 = (bf16[2,128,1024]{2,1,0:T(8,128)(2,1)}, bf16[2,128,1024]{2,1,0:T(8,128)(2,1)S(1)}, u32[]{:S(2)}, u32[]{:S(2)}) collective-permute-start(bf16[2,128,1024]{2,1,0:T(8,128)(2,1)} %get-tuple-element.58), channel_id=1, source_target_pairs={{0,3},{1,2},{2,1},{3,0},{4,7},{5,6},{6,5},{7,4},{8,11},{9,10},{10,... | collective-permute-start | bytes 1572872 | tf_op jit(solution)/shard_map/ppermute | solution.py:30
  32.0 152.6 %copy-start.14 = (bf16[2,128,1024]{2,1,0:T(8,128)(2,1)}, bf16[2,128,1024]{2,1,0:T(8,128)(2,1)S(1)}, u32[]{:S(2)}) copy-start(bf16[2,128,1024]{2,1,0:T(8,128)(2,1)S(1)} %collective-permute-done.4.rest_2_) | copy-start | bytes 1572868
  65.5 92.4 %collective-permute-start.6 = (bf16[2,128,1024]{2,1,0:T(8,128)(2,1)}, bf16[2,128,1024]{2,1,0:T(8,128)(2,1)}, u32[]{:S(2)}, u32[]{:S(2)}) collective-permute-start(bf16[2,128,1024]{2,1,0:T(8,128)(2,1)} %get-tuple-element.67), channel_id=1, source_target_pairs={{0,16},{4,20},{8,24},{12,28},{16,0},{20,4},{24,8},{28,12},{1,17},{... | collective-permute-start | bytes 1572872 | tf_op jit(solution)/shard_map/ppermute | solution.py:350
  67.7 117.0 %collective-permute-start.10 = (bf16[2,128,1024]{2,1,0:T(8,128)(2,1)}, bf16[2,128,1024]{2,1,0:T(8,128)(2,1)}, u32[]{:S(2)}, u32[]{:S(2)}) collective-permute-start(bf16[2,128,1024]{2,1,0:T(8,128)(2,1)} %get-tuple-element.74), channel_id=1, source_target_pairs={{0,20},{4,24},{8,28},{12,16},{20,0},{24,4},{28,8},{16,12},{1,21},{... | collective-permute-start | bytes 1572872 | tf_op jit(solution)/shard_map/ppermute | solution.py:350
  69.2 115.4 %collective-permute-start.11 = (bf16[2,128,1024]{2,1,0:T(8,128)(2,1)}, bf16[2,128,1024]{2,1,0:T(8,128)(2,1)}, u32[]{:S(2)}, u32[]{:S(2)}) collective-permute-start(bf16[2,128,1024]{2,1,0:T(8,128)(2,1)} %get-tuple-element.75), channel_id=1, source_target_pairs={{0,24},{4,28},{8,16},{12,20},{24,0},{28,4},{16,8},{20,12},{1,25},{... | collective-permute-start | bytes 1572872 | tf_op jit(solution)/shard_map/ppermute | solution.py:350
  71.5 120.0 %collective-permute-start.12 = (bf16[2,128,1024]{2,1,0:T(8,128)(2,1)S(1)}, bf16[2,128,1024]{2,1,0:T(8,128)(2,1)}, u32[]{:S(2)}, u32[]{:S(2)}) collective-permute-start(bf16[2,128,1024]{2,1,0:T(8,128)(2,1)S(1)} %copy-done.27), channel_id=1, source_target_pairs={{0,28},{4,16},{8,20},{12,24},{28,0},{16,4},{20,8},{24,12},{1,29},{... | collective-permute-start | bytes 1572872 | tf_op jit(solution)/shard_map/ppermute | solution.py:350
  146.6 45.0 %all-to-all-start.1 = ((bf16[4,2,128,1024]{3,2,1,0:T(8,128)(2,1)}), bf16[4,2,128,1024]{3,2,1,0:T(8,128)(2,1)S(1)}, u32[]{:S(2)}, u32[]{:S(2)}) async-start(bf16[4,2,128,1024]{3,2,1,0:T(8,128)(2,1)} %get-tuple-element.53), calls=%async_computation.1 | async-start | bytes 4194304 | tf_op jit(solution)/shard_map/all_to_all | solution.py:42
  157.9 1.0 copy-start.18
  158.9 1.0 copy-start.20
  160.0 1.0 copy-start.22
  161.0 1.0 copy-start.24
  191.5 33.1 %copy-start.11 = (bf16[2,128,1024]{2,1,0:T(8,128)(2,1)S(1)}, bf16[2,128,1024]{2,1,0:T(8,128)(2,1)}, u32[]{:S(2)}) copy-start(bf16[2,128,1024]{2,1,0:T(8,128)(2,1)} %get-tuple-element.63.rest_0_) | copy-start | bytes 1572868
  191.6 159.6 %all-to-all-start.2 = ((bf16[8,2,128,1024]{3,2,1,0:T(8,128)(2,1)}), bf16[8,2,128,1024]{3,2,1,0:T(8,128)(2,1)}, u32[]{:S(2)}, u32[]{:S(2)}) async-start(bf16[8,2,128,1024]{3,2,1,0:T(8,128)(2,1)} %get-tuple-element.98), calls=%async_computation.2 | async-start | bytes 8388608 | tf_op jit(solution)/shard_map/all_to_all | solution.py:62
  199.0 13.5 %collective-permute-start.7 = (bf16[2,128,1024]{2,1,0:T(8,128)(2,1)}, bf16[2,128,1024]{2,1,0:T(8,128)(2,1)S(1)}, u32[]{:S(2)}, u32[]{:S(2)}) collective-permute-start(bf16[2,128,1024]{2,1,0:T(8,128)(2,1)} %get-tuple-element.70), channel_id=1, source_target_pairs={{0,1},{1,0},{2,3},{3,2},{4,5},{5,4},{6,7},{7,6},{8,9},{9,8},{10,11... | collective-permute-start | bytes 1572872 | tf_op jit(solution)/shard_map/ppermute | solution.py:30
  199.3 14.0 %collective-permute-start.8 = (bf16[2,128,1024]{2,1,0:T(8,128)(2,1)}, bf16[2,128,1024]{2,1,0:T(8,128)(2,1)S(1)}, u32[]{:S(2)}, u32[]{:S(2)}) collective-permute-start(bf16[2,128,1024]{2,1,0:T(8,128)(2,1)} %get-tuple-element.71), channel_id=1, source_target_pairs={{0,2},{1,3},{2,0},{3,1},{4,6},{5,7},{6,4},{7,5},{8,10},{9,11},{10,... | collective-permute-start | bytes 1572872 | tf_op jit(solution)/shard_map/ppermute | solution.py:30
  199.5 24.1 %collective-permute-start.9 = (bf16[2,128,1024]{2,1,0:T(8,128)(2,1)}, bf16[2,128,1024]{2,1,0:T(8,128)(2,1)S(1)}, u32[]{:S(2)}, u32[]{:S(2)}) collective-permute-start(bf16[2,128,1024]{2,1,0:T(8,128)(2,1)} %get-tuple-element.72), channel_id=1, source_target_pairs={{0,3},{1,2},{2,1},{3,0},{4,7},{5,6},{6,5},{7,4},{8,11},{9,10},{10,... | collective-permute-start | bytes 1572872 | tf_op jit(solution)/shard_map/ppermute | solution.py:30
  223.6 0.9 copy-start.8
  224.6 1.0 copy-start.13
  225.6 1.0 copy-start.15
  226.6 1.0 copy-start.17
  227.7 120.2 %copy-start.3 = (bf16[2,128,1024]{2,1,0:T(8,128)(2,1)S(1)}, bf16[2,128,1024]{2,1,0:T(8,128)(2,1)}, u32[]{:S(2)}) copy-start(bf16[2,128,1024]{2,1,0:T(8,128)(2,1)} %get-tuple-element.69.refs_0_) | copy-start | bytes 1572868
  227.7 120.2 %copy-start.5 = (bf16[2,128,1024]{2,1,0:T(8,128)(2,1)S(1)}, bf16[2,128,1024]{2,1,0:T(8,128)(2,1)}, u32[]{:S(2)}) copy-start(bf16[2,128,1024]{2,1,0:T(8,128)(2,1)} %copy-done.4) | copy-start | bytes 1572868
  227.7 120.2 %copy-start.7 = (bf16[2,128,1024]{2,1,0:T(8,128)(2,1)S(1)}, bf16[2,128,1024]{2,1,0:T(8,128)(2,1)}, u32[]{:S(2)}) copy-start(bf16[2,128,1024]{2,1,0:T(8,128)(2,1)} %copy-done.6) | copy-start | bytes 1572868
  227.7 120.2 %copy-start.9 = (bf16[2,128,1024]{2,1,0:T(8,128)(2,1)S(1)}, bf16[2,128,1024]{2,1,0:T(8,128)(2,1)}, u32[]{:S(2)}) copy-start(bf16[2,128,1024]{2,1,0:T(8,128)(2,1)} %copy-done.8) | copy-start | bytes 1572868
  251.5 12.8 %collective-permute-start.13 = (bf16[2,128,1024]{2,1,0:T(8,128)(2,1)}, bf16[2,128,1024]{2,1,0:T(8,128)(2,1)S(1)}, u32[]{:S(2)}, u32[]{:S(2)}) collective-permute-start(bf16[2,128,1024]{2,1,0:T(8,128)(2,1)} %get-tuple-element.78), channel_id=1, source_target_pairs={{0,1},{1,0},{2,3},{3,2},{4,5},{5,4},{6,7},{7,6},{8,9},{9,8},{10,11... | collective-permute-start | bytes 1572872 | tf_op jit(solution)/shard_map/ppermute | solution.py:30
  253.6 12.8 %collective-permute-start.14 = (bf16[2,128,1024]{2,1,0:T(8,128)(2,1)}, bf16[2,128,1024]{2,1,0:T(8,128)(2,1)S(1)}, u32[]{:S(2)}, u32[]{:S(2)}) collective-permute-start(bf16[2,128,1024]{2,1,0:T(8,128)(2,1)} %get-tuple-element.79), channel_id=1, source_target_pairs={{0,2},{1,3},{2,0},{3,1},{4,6},{5,7},{6,4},{7,5},{8,10},{9,11},{10,... | collective-permute-start | bytes 1572872 | tf_op jit(solution)/shard_map/ppermute | solution.py:30
  253.6 22.5 %collective-permute-start.15 = (bf16[2,128,1024]{2,1,0:T(8,128)(2,1)}, bf16[2,128,1024]{2,1,0:T(8,128)(2,1)S(1)}, u32[]{:S(2)}, u32[]{:S(2)}) collective-permute-start(bf16[2,128,1024]{2,1,0:T(8,128)(2,1)} %get-tuple-element.80), channel_id=1, source_target_pairs={{0,3},{1,2},{2,1},{3,0},{4,7},{5,6},{6,5},{7,4},{8,11},{9,10},{10,... | collective-permute-start | bytes 1572872 | tf_op jit(solution)/shard_map/ppermute | solution.py:30
  254.9 68.5 %collective-permute-start.19 = (bf16[2,128,1024]{2,1,0:T(8,128)(2,1)}, bf16[2,128,1024]{2,1,0:T(8,128)(2,1)S(1)}, u32[]{:S(2)}, u32[]{:S(2)}) collective-permute-start(bf16[2,128,1024]{2,1,0:T(8,128)(2,1)} %get-tuple-element.91), channel_id=1, source_target_pairs={{0,16},{4,20},{8,24},{12,28},{16,0},{20,4},{24,8},{28,12},{1,17},{... | collective-permute-start | bytes 1572872 | tf_op jit(solution)/shard_map/ppermute | solution.py:350
  257.0 90.9 %collective-permute-start.20 = (bf16[2,128,1024]{2,1,0:T(8,128)(2,1)}, bf16[2,128,1024]{2,1,0:T(8,128)(2,1)S(1)}, u32[]{:S(2)}, u32[]{:S(2)}) collective-permute-start(bf16[2,128,1024]{2,1,0:T(8,128)(2,1)} %get-tuple-element.92), channel_id=1, source_target_pairs={{0,20},{4,24},{8,28},{12,16},{20,0},{24,4},{28,8},{16,12},{1,21},{... | collective-permute-start | bytes 1572872 | tf_op jit(solution)/shard_map/ppermute | solution.py:350
  276.1 79.9 %collective-permute-start.16 = (bf16[2,128,1024]{2,1,0:T(8,128)(2,1)}, bf16[2,128,1024]{2,1,0:T(8,128)(2,1)S(1)}, u32[]{:S(2)}, u32[]{:S(2)}) collective-permute-start(bf16[2,128,1024]{2,1,0:T(8,128)(2,1)} %get-tuple-element.88), channel_id=1, source_target_pairs={{0,4},{4,0},{8,12},{12,8},{16,20},{20,16},{24,28},{28,24},{1,5},{5... | collective-permute-start | bytes 1572872 | tf_op jit(solution)/shard_map/ppermute | solution.py:52
  279.4 76.6 %collective-permute-start.17 = (bf16[2,128,1024]{2,1,0:T(8,128)(2,1)}, bf16[2,128,1024]{2,1,0:T(8,128)(2,1)S(1)}, u32[]{:S(2)}, u32[]{:S(2)}) collective-permute-start(bf16[2,128,1024]{2,1,0:T(8,128)(2,1)} %get-tuple-element.89), channel_id=1, source_target_pairs={{0,8},{4,12},{8,0},{12,4},{16,24},{20,28},{24,16},{28,20},{1,9},{5... | collective-permute-start | bytes 1572872 | tf_op jit(solution)/shard_map/ppermute | solution.py:52
  280.2 75.7 %collective-permute-start.18 = (bf16[2,128,1024]{2,1,0:T(8,128)(2,1)}, bf16[2,128,1024]{2,1,0:T(8,128)(2,1)S(1)}, u32[]{:S(2)}, u32[]{:S(2)}) collective-permute-start(bf16[2,128,1024]{2,1,0:T(8,128)(2,1)} %get-tuple-element.90), channel_id=1, source_target_pairs={{0,12},{4,8},{8,4},{12,0},{16,28},{20,24},{24,20},{28,16},{1,13},{... | collective-permute-start | bytes 1572872 | tf_op jit(solution)/shard_map/ppermute | solution.py:52
  323.4 46.5 %collective-permute-start.21 = (bf16[2,128,1024]{2,1,0:T(8,128)(2,1)}, bf16[2,128,1024]{2,1,0:T(8,128)(2,1)}, u32[]{:S(2)}, u32[]{:S(2)}) collective-permute-start(bf16[2,128,1024]{2,1,0:T(8,128)(2,1)} %get-tuple-element.94), channel_id=1, source_target_pairs={{0,24},{4,28},{8,16},{12,20},{24,0},{28,4},{16,8},{20,12},{1,25},{... | collective-permute-start | bytes 1572872 | tf_op jit(solution)/shard_map/ppermute | solution.py:350
  347.9 31.6 %collective-permute-start.22 = (bf16[2,128,1024]{2,1,0:T(8,128)(2,1)}, bf16[2,128,1024]{2,1,0:T(8,128)(2,1)}, u32[]{:S(2)}, u32[]{:S(2)}) collective-permute-start(bf16[2,128,1024]{2,1,0:T(8,128)(2,1)} %get-tuple-element.96), channel_id=1, source_target_pairs={{0,28},{4,16},{8,20},{12,24},{28,0},{16,4},{20,8},{24,12},{1,29},{... | collective-permute-start | bytes 1572872 | tf_op jit(solution)/shard_map/ppermute | solution.py:350
  347.9 1.0 copy-start.10
  351.1 28.4 %copy-start.2 = (bf16[2,128,1024]{2,1,0:T(8,128)(2,1)S(1)}, bf16[2,128,1024]{2,1,0:T(8,128)(2,1)}, u32[]{:S(2)}) copy-start(bf16[2,128,1024]{2,1,0:T(8,128)(2,1)} %get-tuple-element.87.rest_0_) | copy-start | bytes 1572868
  (6 other events, 4.8 us)

commit v17 on v16

--- a/solution.py
+++ b/solution.py
@@ -13,6 +13,7 @@
 NBLEN = 128
 ATTEND_WEIGHT = 24
 SHARE = 8
+READS = 3
 F32 = jnp.float32
 BF16 = jnp.bfloat16
 LOG2E = 1.4426950408889634
@@ -34,14 +35,6 @@
     half = count // 2
     there = half + (index + step) % half
     return jnp.where(index < half, there, (index - step) % half)
-
-
-def swap_near(array, count):
-    half = count // 2
-    groups = [list(range(half)), list(range(half, count))]
-    return lax.all_to_all(
-        array, "enc", split_axis=0, concat_axis=0, axis_index_groups=groups, tiled=True
-    )
 
 
 def swap_half(pieces, count):
@@ -142,9 +135,8 @@
 
 
 def kv_shapes(seqs, chunk, form):
-    half = seqs // 2
     one = (2, NBLEN, chunk)
-    return [[(seqs, *one)], [(half, *one)] + [one] * half, [one] * seqs][form]
+    return [one] * seqs if form else [(seqs, *one)]
 
 
 def kv_views(refs, seqs, form):
@@ -153,10 +145,7 @@
     half = seqs // 2
     me = lax.axis_index("enc")
     base = me - me % half
-    if form == 1:
-        near = [(base + step, refs[0].at[step]) for step in range(half)]
-    else:
-        near = [(base + partner(me % half, step, half), refs[step]) for step in range(half)]
+    near = [(base + partner(me % half, step, half), refs[step]) for step in range(half)]
     return near + [(across(me, step, seqs), refs[step - half]) for step in range(half)]
 
 
@@ -168,10 +157,13 @@
         source = pool_ref.at[lists[0, seq, 0], :, :, first : first + chunk]
         arriving.append(pltpu.make_async_copy(source, held.at[n], sems.at[0, n]))
         leaving.append(pltpu.make_async_copy(held.at[n], out, sems.at[1, n]))
+    for n in range(READS):
         arriving[n].start()
     for n in range(seqs):
         arriving[n].wait()
         leaving[n].start()
+        if n + READS < seqs:
+            arriving[n + READS].start()
     for n in range(seqs):
         leaving[n].wait()
 
@@ -360,21 +352,22 @@
     picked = pick(*bounds[0], 0, send_lists, kv_pool)
     send_lists, queries = after((send_lists, queries), picked[0])
     early = swap_pool(picked[0])
-    near, *far = pick(*bounds[1], 1, send_lists, kv_pool)
-    queries = after(queries, near)
+    picked = pick(*bounds[1], 1, send_lists, kv_pool)
+    near, far = picked[: seqs // 2], picked[seqs // 2 :]
+    queries = after(queries, near[0])
     rows = [
         swap_rows(pack(first, chunk, queries, grad_context, width, parts))
         for first, chunk in bounds
     ]
-    far = swap_far(after(far, rows), seqs)
-    near = swap_near(near, seqs)
+    near = swap_half(after(near, rows), seqs)
+    far = swap_far(after(far, near), seqs)
 
     early = after(early, far[0])
     rows_out, whole = attend(seqs, (0, 0), block_slots, rows[0], [early])
     token_parts = [swap_rows(rows_out)]
     returns = [[swap_pool(after(whole[0], far))]]
     block_slots = after(block_slots, token_parts[0])
-    rows_out, back = attend(seqs, (1, 2), block_slots, rows[1], [near, *far])
+    rows_out, back = attend(seqs, (1, 1), block_slots, rows[1], [*near, *far])
     near, far = back[: seqs // 2], back[seqs // 2 :]
     far = swap_far(far, 2)
     token_parts.append(swap_rows(rows_out))
@@ -383,7 +376,7 @@
 
     context, grad_queries = unpack(token_parts, firsts, width, queries.shape)
     pool_grads = None
-    for first, form, back in zip(firsts, (0, 2), returns):
+    for first, form, back in zip(firsts, (0, 1), returns):
         pool_grads = owner_sum(first, form, send_lists, back, kv_pool.shape, pool_grads)
     return (context, grad_queries, pool_grads)
 

time: 389 us -> 402 us (1.033)
  waiting for transfers between devices: 250 us -> 261 us
  starting transfers between devices: 47.3 us -> 42.4 us
    all_to_all x2, waiting for transfers between devices: 73.9 us -> 0.01 us  [swap_pool(): return lax.all_to_all(array, 'enc', split_axis=0, concat_axis=0, tiled=True)]
    ppermute x8, waiting for transfers between devices: 100 us -> 144 us  [swap_far(): got.append(lax.ppermute(piece, 'enc', pairs))]
    ppermute x3 -> x6, waiting for transfers between devices: 0.01 us -> 38.1 us  [swap_half(): got.append(lax.ppermute(pieces[step], 'enc', pairs))]
    all_to_all x1 -> x0, starting transfers between devices: 7.72 us -> none  [swap_near(): lax.all_to_all(array, 'enc', split_axis=0, concat_axis=0, axis_index_grou...]
    ppermute x3 -> x6, starting transfers between devices: 4.95 us -> 9.56 us  [swap_half(): got.append(lax.ppermute(pieces[step], 'enc', pairs))]
    unnamed x58 -> x70, local copies, waits for them, and re-layouts: 15.8 us -> 18.7 us
  transfers between devices with their start and end apart: 26 -> 28, of which waited for: 17 -> 18; matrix products, arithmetic and copies ran while one was open for 0% -> 0% of each run, Pallas kernels for 16% -> 16%
where the time goes in v17:
time: 402 us; the launch traced here: 396 us
  waiting for transfers between devices  261 us (65%)
  Pallas kernels  73.3 us (18%)
  starting transfers between devices  42.4 us (11%)
  local copies, waits for them, and re-layouts  18.8 us (5%)
    ppermute x8, waiting for transfers between devices, swap_far(): got.append(lax.ppermute(piece, 'enc', pairs))  144 us
    ppermute x12, waiting for transfers between devices, exchange(): return lax.ppermute(array, axis, pairs)  78.9 us
    pallas_call x2, Pallas kernels, attend(): pl.pallas_call(functools.partial(attend_kernel, seqs, parts, forms, piece...  46.7 us
    ppermute x6, waiting for transfers between devices, swap_half(): got.append(lax.ppermute(pieces[step], 'enc', pairs))  38.1 us
    unnamed x70, local copies, waits for them, and re-layouts  18.7 us
    pallas_call x2, Pallas kernels, pick(): pl.pallas_call(functools.partial(pick_kernel, first, form, seqs), grid=(1...  12.1 us
    ppermute x8, starting transfers between devices, swap_far(): got.append(lax.ppermute(piece, 'enc', pairs))  12.1 us
    all_to_all x2, starting transfers between devices, swap_pool(): return lax.all_to_all(array, 'enc', split_axis=0, concat_axis=0, tiled=True)  11.9 us
  transfers between devices with their start and end apart: 28, of which 18 were waited for; matrix products, arithmetic and copies ran while one was open for 0% of the time, Pallas kernels for 16%

profile of v17, /device:TPU:15, one launch (start us, length us, event | category | flops | bytes accessed | tf_op | source)
XLA Modules:
  0.0 396.3 jit_solution(7249902333516675091)
XLA Ops:
  1.4 5.9 %pick_entries.2 = bf16[8,2,128,1024]{3,2,1,0:T(8,128)(2,1)} custom-call(s32[1,8,1]{2,1,0:T(8,128)S(1)} %copy.9.lists, bf16[4,2,128,2048]{3,2,1,0:T(8,128)(2,1)} %pool_ref.3), custom_call_target="tpu_custom_call" | custom-call | bytes 8388608 | tf_op jit(solution)/shard_map/pick_entries/pallas_call | solution.py:174
  7.2 5.6 %all-to-all-start = ((bf16[8,2,128,1024]{3,2,1,0:T(8,128)(2,1)}), bf16[8,2,128,1024]{3,2,1,0:T(8,128)(2,1)}, u32[]{:S(2)}, u32[]{:S(2)}) async-start(bf16[8,2,128,1024]{3,2,1,0:T(8,128)(2,1)} %pick_entries.2), calls=%async_computation | async-start | bytes 8388608 | tf_op jit(solution)/shard_map/all_to_all | solution.py:55
  13.0 6.3 %pick_entries.3 = (bf16[2,128,1024]{2,1,0:T(8,128)(2,1)}, bf16[2,128,1024]{2,1,0:T(8,128)(2,1)}, bf16[2,128,1024]{2,1,0:T(8,128)(2,1)}, bf16[2,128,1024]{2,1,0:T...) custom-call(s32[1,8,1]{2,1,0:T(8,128)S(1)} %copy.10.lists, ...), custom_call_target="tpu_custom_call" | custom-call | bytes 8388608 | tf_op jit(solution)/shard_map/pick_entries/pallas_call | solution.py:174
  19.3 1.6 pack_rows.3
  21.5 2.2 collective-permute-start.5
  23.6 1.5 pack_rows.2
  25.7 8.6 %collective-permute-done.3.rest_1_ = bf16[2,128,1024]{2,1,0:T(8,128)(2,1)S(1)} collective-permute-done((bf16[2,128,1024]{2,1,0:T(8,128)(2,1)}, bf16[2,128,1024]{2,1,0:T(8,128)(2,1)S(1)}, u32[]{:S(2)}, u32[]{:S(2)}) %collective-permute-start.3) | collective-permute-done | bytes 524320 | tf_op jit(solution)/shard_map/ppermute | solution.py:31
  34.5 11.0 %collective-permute-done.5.rest_3_ = bf16[2,128,1024]{2,1,0:T(8,128)(2,1)S(1)} collective-permute-done((bf16[2,128,1024]{2,1,0:T(8,128)(2,1)}, bf16[2,128,1024]{2,1,0:T(8,128)(2,1)S(1)}, u32[]{:S(2)}, u32[]{:S(2)}) %collective-permute-start.5) | collective-permute-done | bytes 524320 | tf_op jit(solution)/shard_map/ppermute | solution.py:31
  46.4 10.6 %collective-permute-done.rest_1_ = bf16[2,128,1024]{2,1,0:T(8,128)(2,1)S(1)} collective-permute-done((bf16[2,128,1024]{2,1,0:T(8,128)(2,1)}, bf16[2,128,1024]{2,1,0:T(8,128)(2,1)S(1)}, u32[]{:S(2)}, u32[]{:S(2)}) %collective-permute-start) | collective-permute-done | bytes 524320 | tf_op jit(solution)/shard_map/ppermute | solution.py:31
  57.7 10.3 %collective-permute-done.2.rest_3_ = bf16[2,128,1024]{2,1,0:T(8,128)(2,1)S(1)} collective-permute-done((bf16[2,128,1024]{2,1,0:T(8,128)(2,1)}, bf16[2,128,1024]{2,1,0:T(8,128)(2,1)S(1)}, u32[]{:S(2)}, u32[]{:S(2)}) %collective-permute-start.2) | collective-permute-done | bytes 524320 | tf_op jit(solution)/shard_map/ppermute | solution.py:31
  68.9 2.2 collective-permute-start.6
  71.1 1.6 collective-permute-start.8
  73.5 19.5 %collective-permute-done.7.rest_6_ = bf16[2,128,1024]{2,1,0:T(8,128)(2,1)S(1)} collective-permute-done((bf16[2,128,1024]{2,1,0:T(8,128)(2,1)S(1)}, bf16[2,128,1024]{2,1,0:T(8,128)(2,1)S(1)}, u32[]{:S(2)}, u32[]{:S(2)}) %collective-permute-start.7) | collective-permute-done | bytes 524320 | tf_op jit(solution)/shard_map/ppermute | solution.py:45
  93.8 16.4 %collective-permute-done.8.rest_7_ = bf16[2,128,1024]{2,1,0:T(8,128)(2,1)S(1)} collective-permute-done((bf16[2,128,1024]{2,1,0:T(8,128)(2,1)S(1)}, bf16[2,128,1024]{2,1,0:T(8,128)(2,1)S(1)}, u32[]{:S(2)}, u32[]{:S(2)}) %collective-permute-start.8) | collective-permute-done | bytes 524320 | tf_op jit(solution)/shard_map/ppermute | solution.py:45
  111.0 4.7 %collective-permute-start.9 = (bf16[2,128,1024]{2,1,0:T(8,128)(2,1)}, bf16[2,128,1024]{2,1,0:T(8,128)(2,1)S(1)}, u32[]{:S(2)}, u32[]{:S(2)}) collective-permute-start(bf16[2,128,1024]{2,1,0:T(8,128)(2,1)} %get-tuple-element.81), channel_id=1, source_target_pairs={{0,16},{4,20},{8,24},{12,28},{16,0},{20,4},{24,8},{28,12},{1,17},{... | collective-permute-start | bytes 1572872 | tf_op jit(solution)/shard_map/ppermute | solution.py:342
  115.8 1.3 collective-permute-start.14
  117.1 1.4 collective-permute-start.15
  118.5 52.9 %collective-permute-done.9.rest_8_ = bf16[2,128,1024]{2,1,0:T(8,128)(2,1)S(1)} collective-permute-done((bf16[2,128,1024]{2,1,0:T(8,128)(2,1)}, bf16[2,128,1024]{2,1,0:T(8,128)(2,1)S(1)}, u32[]{:S(2)}, u32[]{:S(2)}) %collective-permute-start.9) | collective-permute-done | bytes 524320 | tf_op jit(solution)/shard_map/ppermute | solution.py:342
  171.4 1.2 copy-done.21
  172.7 1.0 copy-done.25
  173.7 1.0 copy-done.27
  174.7 22.6 %attend_blocks.2 = (bf16[2,128,1024]{2,1,0:T(8,128)(2,1)}, bf16[2,128,1024]{2,1,0:T(8,128)(2,1)}, bf16[2,128,1024]{2,1,0:T(8,128)(2,1)}, bf16[2,128,1024]{2,1,0:T(8,128)(2,1)}, bf16[8,2,128,1024]{3,2,1,0:T(8,128)(2,1)}) custom-call(s32[1,8,2]{2,1,0:T(8,128)S(1)} %copy.11.uses, bf16[2,128,1024]{2,1,0:T(8,128)(2,1)S(1)} %copy-done.21, ...), custom_call_target="tpu_custom_call" | custom-call | flops 38654705664 | bytes 12582912 | tf_op jit(solution)/shard_map/attend_blocks/pallas_call | solution.py:282
  198.2 6.9 %collective-permute-done.15.rest_11_ = bf16[2,128,1024]{2,1,0:T(8,128)(2,1)} collective-permute-done((bf16[2,128,1024]{2,1,0:T(8,128)(2,1)}, bf16[2,128,1024]{2,1,0:T(8,128)(2,1)}, u32[]{:S(2)}, u32[]{:S(2)}) %collective-permute-start.15) | collective-permute-done | bytes 524320 | tf_op jit(solution)/shard_map/ppermute | solution.py:342
  205.1 6.3 %all-to-all-start.1 = ((bf16[8,2,128,1024]{3,2,1,0:T(8,128)(2,1)}), bf16[8,2,128,1024]{3,2,1,0:T(8,128)(2,1)}, u32[]{:S(2)}, u32[]{:S(2)}) async-start(bf16[8,2,128,1024]{3,2,1,0:T(8,128)(2,1)} %get-tuple-element.112), calls=%async_computation.1 | async-start | bytes 8388608 | tf_op jit(solution)/shard_map/all_to_all | solution.py:55
  211.4 1.2 collective-permute-start.10
  212.9 1.2 collective-permute-start.12
  214.1 10.8 %collective-permute-done.10.refs_1_ = bf16[2,128,1024]{2,1,0:T(8,128)(2,1)S(1)} collective-permute-done((bf16[2,128,1024]{2,1,0:T(8,128)(2,1)}, bf16[2,128,1024]{2,1,0:T(8,128)(2,1)S(1)}, u32[]{:S(2)}, u32[]{:S(2)}) %collective-permute-start.10) | collective-permute-done | bytes 524320 | tf_op jit(solution)/shard_map/ppermute | solution.py:31
  224.9 12.1 %collective-permute-done.11.refs_2_ = bf16[2,128,1024]{2,1,0:T(8,128)(2,1)S(1)} collective-permute-done((bf16[2,128,1024]{2,1,0:T(8,128)(2,1)}, bf16[2,128,1024]{2,1,0:T(8,128)(2,1)S(1)}, u32[]{:S(2)}, u32[]{:S(2)}) %collective-permute-start.11) | collective-permute-done | bytes 524320 | tf_op jit(solution)/shard_map/ppermute | solution.py:31
  238.7 1.0 copy-done.12
  239.7 1.0 copy-done.14
  240.8 1.0 copy-done.16
  241.8 1.0 copy-done.18
  243.9 1.0 copy-done.23
  244.9 24.1 %attend_blocks.3 = (bf16[2,128,1024]{2,1,0:T(8,128)(2,1)}, bf16[2,128,1024]{2,1,0:T(8,128)(2,1)}, bf16[2,128,1024]{2,1,0:T(8,128)(2,1)}, bf16[2,128,1024]{2,1,0:...) custom-call(s32[1,8,2]{2,1,0:T(8,128)S(1)} %copy.12.uses, ...), custom_call_target="tpu_custom_call" | custom-call | flops 38654705664 | bytes 12582912 | tf_op jit(solution)/shard_map/attend_blocks/pallas_call | solution.py:282
  269.7 2.1 collective-permute-start.18
  271.7 2.1 collective-permute-start.22
  273.8 1.7 collective-permute-start.23
  275.5 5.9 %collective-permute-done.16.refs_5_ = bf16[2,128,1024]{2,1,0:T(8,128)(2,1)S(1)} collective-permute-done((bf16[2,128,1024]{2,1,0:T(8,128)(2,1)}, bf16[2,128,1024]{2,1,0:T(8,128)(2,1)S(1)}, u32[]{:S(2)}, u32[]{:S(2)}) %collective-permute-start.16) | collective-permute-done | bytes 524320 | tf_op jit(solution)/shard_map/ppermute | solution.py:31
  282.2 8.7 %collective-permute-done.18.refs_7_ = bf16[2,128,1024]{2,1,0:T(8,128)(2,1)S(1)} collective-permute-done((bf16[2,128,1024]{2,1,0:T(8,128)(2,1)}, bf16[2,128,1024]{2,1,0:T(8,128)(2,1)S(1)}, u32[]{:S(2)}, u32[]{:S(2)}) %collective-permute-start.18) | collective-permute-done | bytes 524320 | tf_op jit(solution)/shard_map/ppermute | solution.py:31
  290.9 4.0 %collective-permute-start.19 = (bf16[2,128,1024]{2,1,0:T(8,128)(2,1)}, bf16[2,128,1024]{2,1,0:T(8,128)(2,1)S(1)}, u32[]{:S(2)}, u32[]{:S(2)}) collective-permute-start(bf16[2,128,1024]{2,1,0:T(8,128)(2,1)} %get-tuple-element.102), channel_id=1, source_target_pairs={{0,4},{4,0},{8,12},{12,8},{16,20},{20,16},{24,28},{28,24},{1,5},{5... | collective-permute-start | bytes 1572872 | tf_op jit(solution)/shard_map/ppermute | solution.py:45
  296.6 39.0 %collective-permute-done.22.rest_4_ = bf16[2,128,1024]{2,1,0:T(8,128)(2,1)S(1)} collective-permute-done((bf16[2,128,1024]{2,1,0:T(8,128)(2,1)}, bf16[2,128,1024]{2,1,0:T(8,128)(2,1)S(1)}, u32[]{:S(2)}, u32[]{:S(2)}) %collective-permute-start.22) | collective-permute-done | bytes 524320 | tf_op jit(solution)/shard_map/ppermute | solution.py:342
  336.5 23.8 %collective-permute-done.23.rest_5_ = bf16[2,128,1024]{2,1,0:T(8,128)(2,1)S(1)} collective-permute-done((bf16[2,128,1024]{2,1,0:T(8,128)(2,1)}, bf16[2,128,1024]{2,1,0:T(8,128)(2,1)S(1)}, u32[]{:S(2)}, u32[]{:S(2)}) %collective-permute-start.23) | collective-permute-done | bytes 524320 | tf_op jit(solution)/shard_map/ppermute | solution.py:342
  361.4 2.1 unpack_rows.1
  363.5 4.8 %owner_sum.2.rest_8_ = bf16[4,2,128,2048]{3,2,1,0:T(8,128)(2,1)} custom-call(s32[1,8,1]{2,1,0:T(8,128)S(1)} %copy.10.lists, bf16[8,2,128,1024]{3,2,1,0:T(8,128)(2,1)} %all-to-all-done.1.rest_0_), custom_call_target="tpu_custom_call" | custom-call | flops 2097152 | bytes 6291456 | tf_op jit(solution)/shard_map/owner_sum/pallas_call | solution.py:318
  368.3 2.2 collective-permute-done.21.rest_3_
  370.6 11.7 %collective-permute-done.24.rest_6_ = bf16[2,128,1024]{2,1,0:T(8,128)(2,1)} collective-permute-done((bf16[2,128,1024]{2,1,0:T(8,128)(2,1)}, bf16[2,128,1024]{2,1,0:T(8,128)(2,1)}, u32[]{:S(2)}, u32[]{:S(2)}) %collective-permute-start.24) | collective-permute-done | bytes 524320 | tf_op jit(solution)/shard_map/ppermute | solution.py:342
  382.2 9.6 %collective-permute-done.25.rest_7_ = bf16[2,128,1024]{2,1,0:T(8,128)(2,1)} collective-permute-done((bf16[2,128,1024]{2,1,0:T(8,128)(2,1)}, bf16[2,128,1024]{2,1,0:T(8,128)(2,1)}, u32[]{:S(2)}, u32[]{:S(2)}) %collective-permute-start.25) | collective-permute-done | bytes 524320 | tf_op jit(solution)/shard_map/ppermute | solution.py:342
  391.8 4.5 %owner_sum.3 = bf16[4,2,128,2048]{3,2,1,0:T(8,128)(2,1)} custom-call(s32[1,8,1]{2,1,0:T(8,128)S(1)} %copy.10.lists, bf16[2,128,1024]{2,1,0:T(8,128)(2,1)S(1)} %copy-done.2, bf16[2,128,1024]{2,1,0:T(8,128)(2,1)S(1)} %collective-permute-done.19.rest_1_, bf16[2,128,1024]{2,1,0:T(8,128)(2,1)S(1)} %collective-permute-done.20.rest_2_, ...), custom_call_target="tpu_custom_call", output_to_operand_aliasing={{}: (9, {})} | custom-call | flops 2097152 | bytes 6291456 | tf_op jit(solution)/shard_map/owner_sum/pallas_call | solution.py:318
  (89 shorter events, 16.0 us)
Async XLA Ops:
  7.2 5.6 %copy-start.29 = (s32[1,8,1]{1,2,0:T(1,128)S(1)}, s32[1,8,1]{1,2,0:T(1,128)}, u32[]{:S(2)}) copy-start(s32[1,8,1]{1,2,0:T(1,128)} %param.7) | copy-start | bytes 100
  7.2 164.2 %all-to-all-start = ((bf16[8,2,128,1024]{3,2,1,0:T(8,128)(2,1)}), bf16[8,2,128,1024]{3,2,1,0:T(8,128)(2,1)}, u32[]{:S(2)}, u32[]{:S(2)}) async-start(bf16[8,2,128,1024]{3,2,1,0:T(8,128)(2,1)} %pick_entries.2), calls=%async_computation | async-start | bytes 8388608 | tf_op jit(solution)/shard_map/all_to_all | solution.py:55
  12.9 6.4 %copy-start = (bf16[1,128,8192]{2,1,0:T(8,128)(2,1)S(1)}, bf16[1,128,8192]{2,1,0:T(8,128)(2,1)}, u32[]{:S(2)}) copy-start(bf16[1,128,8192]{2,1,0:T(8,128)(2,1)} %q_ref.1) | copy-start | bytes 6291460
  13.0 6.3 %copy-start.1 = (bf16[1,128,8192]{2,1,0:T(8,128)(2,1)S(1)}, bf16[1,128,8192]{2,1,0:T(8,128)(2,1)}, u32[]{:S(2)}) copy-start(bf16[1,128,8192]{2,1,0:T(8,128)(2,1)} %g_ref.3) | copy-start | bytes 6291460
  19.3 49.6 %copy-start.32 = (bf16[2,128,1024]{2,1,0:T(8,128)(2,1)S(1)}, bf16[2,128,1024]{2,1,0:T(8,128)(2,1)}, u32[]{:S(2)}) copy-start(bf16[2,128,1024]{2,1,0:T(8,128)(2,1)} %get-tuple-element.78) | copy-start | bytes 1572868
  19.3 51.8 %copy-start.31 = (bf16[2,128,1024]{2,1,0:T(8,128)(2,1)S(1)}, bf16[2,128,1024]{2,1,0:T(8,128)(2,1)}, u32[]{:S(2)}) copy-start(bf16[2,128,1024]{2,1,0:T(8,128)(2,1)} %get-tuple-element.79) | copy-start | bytes 1572868
  19.3 51.9 %copy-start.30 = (bf16[2,128,1024]{2,1,0:T(8,128)(2,1)S(1)}, bf16[2,128,1024]{2,1,0:T(8,128)(2,1)}, u32[]{:S(2)}) copy-start(bf16[2,128,1024]{2,1,0:T(8,128)(2,1)} %get-tuple-element.80) | copy-start | bytes 1572868
  19.3 96.4 %copy-start.28 = (s32[1,8,2]{1,2,0:T(2,128)S(1)}, s32[1,8,2]{1,2,0:T(2,128)}, u32[]{:S(2)}) copy-start(s32[1,8,2]{1,2,0:T(2,128)} %param.8) | copy-start | bytes 196
  20.9 13.4 %collective-permute-start.3 = (bf16[2,128,1024]{2,1,0:T(8,128)(2,1)}, bf16[2,128,1024]{2,1,0:T(8,128)(2,1)S(1)}, u32[]{:S(2)}, u32[]{:S(2)}) collective-permute-start(bf16[2,128,1024]{2,1,0:T(8,128)(2,1)} %get-tuple-element.74), channel_id=1, source_target_pairs={{0,1},{1,0},{2,3},{3,2},{4,5},{5,4},{6,7},{7,6},{8,9},{9,8},{10,11... | collective-permute-start | bytes 1572872 | tf_op jit(solution)/shard_map/ppermute | solution.py:31
  21.2 13.3 %collective-permute-start.4 = (bf16[2,128,1024]{2,1,0:T(8,128)(2,1)}, bf16[2,128,1024]{2,1,0:T(8,128)(2,1)S(1)}, u32[]{:S(2)}, u32[]{:S(2)}) collective-permute-start(bf16[2,128,1024]{2,1,0:T(8,128)(2,1)} %get-tuple-element.75), channel_id=1, source_target_pairs={{0,2},{1,3},{2,0},{3,1},{4,6},{5,7},{6,4},{7,5},{8,10},{9,11},{10,... | collective-permute-start | bytes 1572872 | tf_op jit(solution)/shard_map/ppermute | solution.py:31
  21.5 24.1 %collective-permute-start.5 = (bf16[2,128,1024]{2,1,0:T(8,128)(2,1)}, bf16[2,128,1024]{2,1,0:T(8,128)(2,1)S(1)}, u32[]{:S(2)}, u32[]{:S(2)}) collective-permute-start(bf16[2,128,1024]{2,1,0:T(8,128)(2,1)} %get-tuple-element.76), channel_id=1, source_target_pairs={{0,3},{1,2},{2,1},{3,0},{4,7},{5,6},{6,5},{7,4},{8,11},{9,10},{10,... | collective-permute-start | bytes 1572872 | tf_op jit(solution)/shard_map/ppermute | solution.py:31
  25.2 31.8 %collective-permute-start = (bf16[2,128,1024]{2,1,0:T(8,128)(2,1)}, bf16[2,128,1024]{2,1,0:T(8,128)(2,1)S(1)}, u32[]{:S(2)}, u32[]{:S(2)}) collective-permute-start(bf16[2,128,1024]{2,1,0:T(8,128)(2,1)} %get-tuple-element.63), channel_id=1, source_target_pairs={{0,1},{1,0},{2,3},{3,2},{4,5},{5,4},{6,7},{7,6},{8,9},{9,8},{10,11... | collective-permute-start | bytes 1572872 | tf_op jit(solution)/shard_map/ppermute | solution.py:31
  25.5 31.5 %collective-permute-start.1 = (bf16[2,128,1024]{2,1,0:T(8,128)(2,1)}, bf16[2,128,1024]{2,1,0:T(8,128)(2,1)S(1)}, u32[]{:S(2)}, u32[]{:S(2)}) collective-permute-start(bf16[2,128,1024]{2,1,0:T(8,128)(2,1)} %get-tuple-element.64), channel_id=1, source_target_pairs={{0,2},{1,3},{2,0},{3,1},{4,6},{5,7},{6,4},{7,5},{8,10},{9,11},{10,... | collective-permute-start | bytes 1572872 | tf_op jit(solution)/shard_map/ppermute | solution.py:31
  34.3 33.7 %collective-permute-start.2 = (bf16[2,128,1024]{2,1,0:T(8,128)(2,1)}, bf16[2,128,1024]{2,1,0:T(8,128)(2,1)S(1)}, u32[]{:S(2)}, u32[]{:S(2)}) collective-permute-start(bf16[2,128,1024]{2,1,0:T(8,128)(2,1)} %get-tuple-element.65), channel_id=1, source_target_pairs={{0,3},{1,2},{2,1},{3,0},{4,7},{5,6},{6,5},{7,4},{8,11},{9,10},{10,... | collective-permute-start | bytes 1572872 | tf_op jit(solution)/shard_map/ppermute | solution.py:31
  68.9 3.9 collective-permute-start.6
  71.1 22.0 %collective-permute-start.7 = (bf16[2,128,1024]{2,1,0:T(8,128)(2,1)S(1)}, bf16[2,128,1024]{2,1,0:T(8,128)(2,1)S(1)}, u32[]{:S(2)}, u32[]{:S(2)}) collective-permute-start(bf16[2,128,1024]{2,1,0:T(8,128)(2,1)S(1)} %copy-done.31), channel_id=1, source_target_pairs={{0,8},{4,12},{8,0},{12,4},{16,24},{20,28},{24,16},{28,20},{1,9},{5... | collective-permute-start | bytes 1572872 | tf_op jit(solution)/shard_map/ppermute | solution.py:45
  71.1 39.1 %collective-permute-start.8 = (bf16[2,128,1024]{2,1,0:T(8,128)(2,1)S(1)}, bf16[2,128,1024]{2,1,0:T(8,128)(2,1)S(1)}, u32[]{:S(2)}, u32[]{:S(2)}) collective-permute-start(bf16[2,128,1024]{2,1,0:T(8,128)(2,1)S(1)} %copy-done.30), channel_id=1, source_target_pairs={{0,12},{4,8},{8,4},{12,0},{16,28},{20,24},{24,20},{28,16},{1,13},{... | collective-permute-start | bytes 1572872 | tf_op jit(solution)/shard_map/ppermute | solution.py:45
  111.0 60.4 %collective-permute-start.9 = (bf16[2,128,1024]{2,1,0:T(8,128)(2,1)}, bf16[2,128,1024]{2,1,0:T(8,128)(2,1)S(1)}, u32[]{:S(2)}, u32[]{:S(2)}) collective-permute-start(bf16[2,128,1024]{2,1,0:T(8,128)(2,1)} %get-tuple-element.81), channel_id=1, source_target_pairs={{0,16},{4,20},{8,24},{12,28},{16,0},{20,4},{24,8},{28,12},{1,17},{... | collective-permute-start | bytes 1572872 | tf_op jit(solution)/shard_map/ppermute | solution.py:342
  115.8 81.6 %collective-permute-start.13 = (bf16[2,128,1024]{2,1,0:T(8,128)(2,1)}, bf16[2,128,1024]{2,1,0:T(8,128)(2,1)S(1)}, u32[]{:S(2)}, u32[]{:S(2)}) collective-permute-start(bf16[2,128,1024]{2,1,0:T(8,128)(2,1)} %get-tuple-element.88), channel_id=1, source_target_pairs={{0,20},{4,24},{8,28},{12,16},{20,0},{24,4},{28,8},{16,12},{1,21},{... | collective-permute-start | bytes 1572872 | tf_op jit(solution)/shard_map/ppermute | solution.py:342
  115.8 82.4 %collective-permute-start.14 = (bf16[2,128,1024]{2,1,0:T(8,128)(2,1)}, bf16[2,128,1024]{2,1,0:T(8,128)(2,1)}, u32[]{:S(2)}, u32[]{:S(2)}) collective-permute-start(bf16[2,128,1024]{2,1,0:T(8,128)(2,1)} %get-tuple-element.89), channel_id=1, source_target_pairs={{0,24},{4,28},{8,16},{12,20},{24,0},{28,4},{16,8},{20,12},{1,25},{... | collective-permute-start | bytes 1572872 | tf_op jit(solution)/shard_map/ppermute | solution.py:342
  117.1 88.1 %collective-permute-start.15 = (bf16[2,128,1024]{2,1,0:T(8,128)(2,1)}, bf16[2,128,1024]{2,1,0:T(8,128)(2,1)}, u32[]{:S(2)}, u32[]{:S(2)}) collective-permute-start(bf16[2,128,1024]{2,1,0:T(8,128)(2,1)} %get-tuple-element.90), channel_id=1, source_target_pairs={{0,28},{4,16},{8,20},{12,24},{28,0},{16,4},{20,8},{24,12},{1,29},{... | collective-permute-start | bytes 1572872 | tf_op jit(solution)/shard_map/ppermute | solution.py:342
  171.4 25.9 %copy-start.19 = (bf16[2,128,1024]{2,1,0:T(8,128)(2,1)}, bf16[2,128,1024]{2,1,0:T(8,128)(2,1)S(1)}, u32[]{:S(2)}) copy-start(bf16[2,128,1024]{2,1,0:T(8,128)(2,1)S(1)} %collective-permute-done.9.rest_8_) | copy-start | bytes 1572868
  171.4 1.2 copy-start.21
  172.7 1.0 copy-start.25
  173.7 1.0 copy-start.27
  205.1 7.7 %copy-start.33 = (bf16[2,128,1024]{2,1,0:T(8,128)(2,1)S(1)}, bf16[2,128,1024]{2,1,0:T(8,128)(2,1)}, u32[]{:S(2)}) copy-start(bf16[2,128,1024]{2,1,0:T(8,128)(2,1)} %get-tuple-element.86) | copy-start | bytes 1572868
  205.1 33.5 %copy-start.9 = (bf16[2,128,1024]{2,1,0:T(8,128)(2,1)S(1)}, bf16[2,128,1024]{2,1,0:T(8,128)(2,1)}, u32[]{:S(2)}) copy-start(bf16[2,128,1024]{2,1,0:T(8,128)(2,1)} %get-tuple-element.77.rest_4_) | copy-start | bytes 1572868
  205.1 33.5 %copy-start.10 = (bf16[2,128,1024]{2,1,0:T(8,128)(2,1)S(1)}, bf16[2,128,1024]{2,1,0:T(8,128)(2,1)}, u32[]{:S(2)}) copy-start(bf16[2,128,1024]{2,1,0:T(8,128)(2,1)} %get-tuple-element.73.rest_0_) | copy-start | bytes 1572868
  205.1 158.4 %all-to-all-start.1 = ((bf16[8,2,128,1024]{3,2,1,0:T(8,128)(2,1)}), bf16[8,2,128,1024]{3,2,1,0:T(8,128)(2,1)}, u32[]{:S(2)}, u32[]{:S(2)}) async-start(bf16[8,2,128,1024]{3,2,1,0:T(8,128)(2,1)} %get-tuple-element.112), calls=%async_computation.1 | async-start | bytes 8388608 | tf_op jit(solution)/shard_map/all_to_all | solution.py:55
  211.4 13.5 %collective-permute-start.10 = (bf16[2,128,1024]{2,1,0:T(8,128)(2,1)}, bf16[2,128,1024]{2,1,0:T(8,128)(2,1)S(1)}, u32[]{:S(2)}, u32[]{:S(2)}) collective-permute-start(bf16[2,128,1024]{2,1,0:T(8,128)(2,1)} %get-tuple-element.84), channel_id=1, source_target_pairs={{0,1},{1,0},{2,3},{3,2},{4,5},{5,4},{6,7},{7,6},{8,9},{9,8},{10,11... | collective-permute-start | bytes 1572872 | tf_op jit(solution)/shard_map/ppermute | solution.py:31
  212.6 24.4 %collective-permute-start.11 = (bf16[2,128,1024]{2,1,0:T(8,128)(2,1)}, bf16[2,128,1024]{2,1,0:T(8,128)(2,1)S(1)}, u32[]{:S(2)}, u32[]{:S(2)}) collective-permute-start(bf16[2,128,1024]{2,1,0:T(8,128)(2,1)} %get-tuple-element.85), channel_id=1, source_target_pairs={{0,2},{1,3},{2,0},{3,1},{4,6},{5,7},{6,4},{7,5},{8,10},{9,11},{10,... | collective-permute-start | bytes 1572872 | tf_op jit(solution)/shard_map/ppermute | solution.py:31
  212.9 24.9 %collective-permute-start.12 = (bf16[2,128,1024]{2,1,0:T(8,128)(2,1)S(1)}, bf16[2,128,1024]{2,1,0:T(8,128)(2,1)S(1)}, u32[]{:S(2)}, u32[]{:S(2)}) collective-permute-start(bf16[2,128,1024]{2,1,0:T(8,128)(2,1)S(1)} %copy-done.33), channel_id=1, source_target_pairs={{0,3},{1,2},{2,1},{3,0},{4,7},{5,6},{6,5},{7,4},{8,11},{9,10},{10,... | collective-permute-start | bytes 1572872 | tf_op jit(solution)/shard_map/ppermute | solution.py:31
  238.7 1.0 copy-start.12
  244.9 115.4 %copy-start.3 = (bf16[2,128,1024]{2,1,0:T(8,128)(2,1)S(1)}, bf16[2,128,1024]{2,1,0:T(8,128)(2,1)}, u32[]{:S(2)}) copy-start(bf16[2,128,1024]{2,1,0:T(8,128)(2,1)} %get-tuple-element.83.refs_0_) | copy-start | bytes 1572868
  244.9 115.4 %copy-start.5 = (bf16[2,128,1024]{2,1,0:T(8,128)(2,1)S(1)}, bf16[2,128,1024]{2,1,0:T(8,128)(2,1)}, u32[]{:S(2)}) copy-start(bf16[2,128,1024]{2,1,0:T(8,128)(2,1)} %copy-done.4) | copy-start | bytes 1572868
  244.9 115.4 %copy-start.7 = (bf16[2,128,1024]{2,1,0:T(8,128)(2,1)S(1)}, bf16[2,128,1024]{2,1,0:T(8,128)(2,1)}, u32[]{:S(2)}) copy-start(bf16[2,128,1024]{2,1,0:T(8,128)(2,1)} %copy-done.6) | copy-start | bytes 1572868
  269.0 12.4 %collective-permute-start.16 = (bf16[2,128,1024]{2,1,0:T(8,128)(2,1)}, bf16[2,128,1024]{2,1,0:T(8,128)(2,1)S(1)}, u32[]{:S(2)}, u32[]{:S(2)}) collective-permute-start(bf16[2,128,1024]{2,1,0:T(8,128)(2,1)} %get-tuple-element.92), channel_id=1, source_target_pairs={{0,1},{1,0},{2,3},{3,2},{4,5},{5,4},{6,7},{7,6},{8,9},{9,8},{10,11... | collective-permute-start | bytes 1572872 | tf_op jit(solution)/shard_map/ppermute | solution.py:31
  269.1 13.2 %collective-permute-start.17 = (bf16[2,128,1024]{2,1,0:T(8,128)(2,1)}, bf16[2,128,1024]{2,1,0:T(8,128)(2,1)S(1)}, u32[]{:S(2)}, u32[]{:S(2)}) collective-permute-start(bf16[2,128,1024]{2,1,0:T(8,128)(2,1)} %get-tuple-element.93), channel_id=1, source_target_pairs={{0,2},{1,3},{2,0},{3,1},{4,6},{5,7},{6,4},{7,5},{8,10},{9,11},{10,... | collective-permute-start | bytes 1572872 | tf_op jit(solution)/shard_map/ppermute | solution.py:31
  269.7 21.3 %collective-permute-start.18 = (bf16[2,128,1024]{2,1,0:T(8,128)(2,1)}, bf16[2,128,1024]{2,1,0:T(8,128)(2,1)S(1)}, u32[]{:S(2)}, u32[]{:S(2)}) collective-permute-start(bf16[2,128,1024]{2,1,0:T(8,128)(2,1)} %get-tuple-element.94), channel_id=1, source_target_pairs={{0,3},{1,2},{2,1},{3,0},{4,7},{5,6},{6,5},{7,4},{8,11},{9,10},{10,... | collective-permute-start | bytes 1572872 | tf_op jit(solution)/shard_map/ppermute | solution.py:31
  271.7 63.9 %collective-permute-start.22 = (bf16[2,128,1024]{2,1,0:T(8,128)(2,1)}, bf16[2,128,1024]{2,1,0:T(8,128)(2,1)S(1)}, u32[]{:S(2)}, u32[]{:S(2)}) collective-permute-start(bf16[2,128,1024]{2,1,0:T(8,128)(2,1)} %get-tuple-element.105), channel_id=1, source_target_pairs={{0,16},{4,20},{8,24},{12,28},{16,0},{20,4},{24,8},{28,12},{1,17},{... | collective-permute-start | bytes 1572872 | tf_op jit(solution)/shard_map/ppermute | solution.py:342
  273.8 86.5 %collective-permute-start.23 = (bf16[2,128,1024]{2,1,0:T(8,128)(2,1)}, bf16[2,128,1024]{2,1,0:T(8,128)(2,1)S(1)}, u32[]{:S(2)}, u32[]{:S(2)}) collective-permute-start(bf16[2,128,1024]{2,1,0:T(8,128)(2,1)} %get-tuple-element.106), channel_id=1, source_target_pairs={{0,20},{4,24},{8,28},{12,16},{20,0},{24,4},{28,8},{16,12},{1,21},{... | collective-permute-start | bytes 1572872 | tf_op jit(solution)/shard_map/ppermute | solution.py:342
  290.9 77.4 %collective-permute-start.19 = (bf16[2,128,1024]{2,1,0:T(8,128)(2,1)}, bf16[2,128,1024]{2,1,0:T(8,128)(2,1)S(1)}, u32[]{:S(2)}, u32[]{:S(2)}) collective-permute-start(bf16[2,128,1024]{2,1,0:T(8,128)(2,1)} %get-tuple-element.102), channel_id=1, source_target_pairs={{0,4},{4,0},{8,12},{12,8},{16,20},{20,16},{24,28},{28,24},{1,5},{5... | collective-permute-start | bytes 1572872 | tf_op jit(solution)/shard_map/ppermute | solution.py:45
  294.9 73.4 %collective-permute-start.20 = (bf16[2,128,1024]{2,1,0:T(8,128)(2,1)}, bf16[2,128,1024]{2,1,0:T(8,128)(2,1)S(1)}, u32[]{:S(2)}, u32[]{:S(2)}) collective-permute-start(bf16[2,128,1024]{2,1,0:T(8,128)(2,1)} %get-tuple-element.103), channel_id=1, source_target_pairs={{0,8},{4,12},{8,0},{12,4},{16,24},{20,28},{24,16},{28,20},{1,9},{5... | collective-permute-start | bytes 1572872 | tf_op jit(solution)/shard_map/ppermute | solution.py:45
  295.7 74.9 %collective-permute-start.21 = (bf16[2,128,1024]{2,1,0:T(8,128)(2,1)}, bf16[2,128,1024]{2,1,0:T(8,128)(2,1)S(1)}, u32[]{:S(2)}, u32[]{:S(2)}) collective-permute-start(bf16[2,128,1024]{2,1,0:T(8,128)(2,1)} %get-tuple-element.104), channel_id=1, source_target_pairs={{0,12},{4,8},{8,4},{12,0},{16,28},{20,24},{24,20},{28,16},{1,13},{... | collective-permute-start | bytes 1572872 | tf_op jit(solution)/shard_map/ppermute | solution.py:45
  335.6 46.6 %collective-permute-start.24 = (bf16[2,128,1024]{2,1,0:T(8,128)(2,1)}, bf16[2,128,1024]{2,1,0:T(8,128)(2,1)}, u32[]{:S(2)}, u32[]{:S(2)}) collective-permute-start(bf16[2,128,1024]{2,1,0:T(8,128)(2,1)} %get-tuple-element.108), channel_id=1, source_target_pairs={{0,24},{4,28},{8,16},{12,20},{24,0},{28,4},{16,8},{20,12},{1,25},{... | collective-permute-start | bytes 1572872 | tf_op jit(solution)/shard_map/ppermute | solution.py:342
  360.3 31.5 %collective-permute-start.25 = (bf16[2,128,1024]{2,1,0:T(8,128)(2,1)}, bf16[2,128,1024]{2,1,0:T(8,128)(2,1)}, u32[]{:S(2)}, u32[]{:S(2)}) collective-permute-start(bf16[2,128,1024]{2,1,0:T(8,128)(2,1)} %get-tuple-element.110), channel_id=1, source_target_pairs={{0,28},{4,16},{8,20},{12,24},{28,0},{16,4},{20,8},{24,12},{1,29},{... | collective-permute-start | bytes 1572872 | tf_op jit(solution)/shard_map/ppermute | solution.py:342
  360.3 1.0 copy-start.8
  363.5 28.3 %copy-start.2 = (bf16[2,128,1024]{2,1,0:T(8,128)(2,1)S(1)}, bf16[2,128,1024]{2,1,0:T(8,128)(2,1)}, u32[]{:S(2)}) copy-start(bf16[2,128,1024]{2,1,0:T(8,128)(2,1)} %get-tuple-element.101.rest_0_) | copy-start | bytes 1572868
  (14 other events, 12.4 us)

commit v18 on v16

--- a/solution.py
+++ b/solution.py
@@ -165,15 +165,17 @@
     chunk = held.shape[-1]
     arriving, leaving = [], []
     for n, (seq, out) in enumerate(kv_views(outs, seqs, form)):
-        source = pool_ref.at[lists[0, seq, 0], :, :, first : first + chunk]
-        arriving.append(pltpu.make_async_copy(source, held.at[n], sems.at[0, n]))
-        leaving.append(pltpu.make_async_copy(held.at[n], out, sems.at[1, n]))
-        arriving[n].start()
-    for n in range(seqs):
-        arriving[n].wait()
-        leaving[n].start()
-    for n in range(seqs):
-        leaving[n].wait()
+        entry = lists[0, seq, 0]
+        for k in range(2):
+            source = pool_ref.at[entry, k, :, first : first + chunk]
+            arriving.append(pltpu.make_async_copy(source, held.at[n, k], sems.at[0, n, k]))
+            leaving.append(pltpu.make_async_copy(held.at[n, k], out.at[k], sems.at[1, n, k]))
+            arriving[-1].start()
+    for arrival, departure in zip(arriving, leaving):
+        arrival.wait()
+        departure.start()
+    for departure in leaving:
+        departure.wait()
 
 
 def pick(first, chunk, form, send_lists, kv_pool):
@@ -187,7 +189,7 @@
         out_shape=[in_hbm(shape) for shape in shapes],
         scratch_shapes=[
             pltpu.VMEM((seqs, 2, NBLEN, chunk), BF16),
-            pltpu.SemaphoreType.DMA((2, seqs)),
+            pltpu.SemaphoreType.DMA((2, seqs, 2)),
         ],
         compiler_params=PARAMS,
         cost_estimate=cost(8 * seqs * NBLEN * chunk),
@@ -366,7 +368,8 @@
         swap_rows(pack(first, chunk, queries, grad_context, width, parts))
         for first, chunk in bounds
     ]
-    far = swap_far(after(far, rows), seqs)
+    far = after(far, rows)
+    far = swap_far(far[:1] + after(far[1:], early), seqs)
     near = swap_near(near, seqs)
 
     early = after(early, far[0])

time: 389 us -> 388 us (level)
  local copies, waits for them, and re-layouts: 15.9 us -> 21.3 us
    all_to_all x2, waiting for transfers between devices: 73.9 us -> 45 us  [swap_pool(): return lax.all_to_all(array, 'enc', split_axis=0, concat_axis=0, tiled=True)]
    ppermute x8, waiting for transfers between devices: 100 us -> 122 us  [swap_far(): got.append(lax.ppermute(piece, 'enc', pairs))]
    unnamed x58 -> x70, local copies, waits for them, and re-layouts: 15.8 us -> 21.1 us
where the time goes in v18:
time: 388 us; the launch traced here: 384 us
  waiting for transfers between devices  247 us (64%)
  Pallas kernels  70.5 us (18%)
  starting transfers between devices  43.8 us (11%)
  local copies, waits for them, and re-layouts  21.3 us (5%)
    ppermute x8, waiting for transfers between devices, swap_far(): got.append(lax.ppermute(piece, 'enc', pairs))  122 us
    ppermute x12, waiting for transfers between devices, exchange(): return lax.ppermute(array, axis, pairs)  76.5 us
    pallas_call x2, Pallas kernels, attend(): pl.pallas_call(functools.partial(attend_kernel, seqs, parts, forms, piece...  46.6 us
    all_to_all x2, waiting for transfers between devices, swap_pool(): return lax.all_to_all(array, 'enc', split_axis=0, concat_axis=0, tiled=True)  45 us
    unnamed x70, local copies, waits for them, and re-layouts  21.1 us
    all_to_all x2, starting transfers between devices, swap_pool(): return lax.all_to_all(array, 'enc', split_axis=0, concat_axis=0, tiled=True)  11.9 us
    ppermute x8, starting transfers between devices, swap_far(): got.append(lax.ppermute(piece, 'enc', pairs))  9.73 us
    pallas_call x2, Pallas kernels, owner_sum(): pl.pallas_call(functools.partial(owner_kernel, seqs, form, len(back)), gr...  9.28 us
  transfers between devices with their start and end apart: 26, of which 17 were waited for; matrix products, arithmetic and copies ran while one was open for 0% of the time, Pallas kernels for 16%

profile of v18, /device:TPU:15, one launch (start us, length us, event | category | flops | bytes accessed | tf_op | source)
XLA Modules:
  0.0 383.8 jit_solution(12178906380455909944)
XLA Ops:
  1.4 4.5 %pick_entries.2 = bf16[8,2,128,1024]{3,2,1,0:T(8,128)(2,1)} custom-call(s32[1,8,1]{2,1,0:T(8,128)S(1)} %copy.9.lists, bf16[4,2,128,2048]{3,2,1,0:T(8,128)(2,1)} %pool_ref.3), custom_call_target="tpu_custom_call" | custom-call | bytes 8388608 | tf_op jit(solution)/shard_map/pick_entries/pallas_call | solution.py:184
  5.8 5.6 %all-to-all-start = ((bf16[8,2,128,1024]{3,2,1,0:T(8,128)(2,1)}), bf16[8,2,128,1024]{3,2,1,0:T(8,128)(2,1)}, u32[]{:S(2)}, u32[]{:S(2)}) async-start(bf16[8,2,128,1024]{3,2,1,0:T(8,128)(2,1)} %pick_entries.2), calls=%async_computation | async-start | bytes 8388608 | tf_op jit(solution)/shard_map/all_to_all | solution.py:62
  11.6 4.8 %pick_entries.3 = (bf16[4,2,128,1024]{3,2,1,0:T(8,128)(2,1)}, bf16[2,128,1024]{2,1,0:T(8,128)(2,1)}, bf16[2,128,1024]{2,1,0:T(8,128)(2,1)}, bf16[2,128,1024]{2,1,0:T(8,128)(2,1)}, bf16[2,128,1024]{2,1,0:T(8,128)(2,1)}) custom-call(s32[1,8,1]{2,1,0:T(8,128)S(1)} %copy.10.lists, bf16[4,2,128,2048]{3,2,1,0:T(8,128)(2,1)} %pool_ref.3), custom_call_target="tpu_custom_call" | custom-call | bytes 8388608 | tf_op jit(solution)/shard_map/pick_entries/pallas_call | solution.py:184
  16.4 1.6 pack_rows.3
  18.6 2.2 collective-permute-start.5
  20.7 1.6 pack_rows.2
  22.9 8.6 %collective-permute-done.3.rest_1_ = bf16[2,128,1024]{2,1,0:T(8,128)(2,1)S(1)} collective-permute-done((bf16[2,128,1024]{2,1,0:T(8,128)(2,1)}, bf16[2,128,1024]{2,1,0:T(8,128)(2,1)S(1)}, u32[]{:S(2)}, u32[]{:S(2)}) %collective-permute-start.3) | collective-permute-done | bytes 524320 | tf_op jit(solution)/shard_map/ppermute | solution.py:30
  32.5 10.2 %collective-permute-done.5.rest_3_ = bf16[2,128,1024]{2,1,0:T(8,128)(2,1)S(1)} collective-permute-done((bf16[2,128,1024]{2,1,0:T(8,128)(2,1)}, bf16[2,128,1024]{2,1,0:T(8,128)(2,1)S(1)}, u32[]{:S(2)}, u32[]{:S(2)}) %collective-permute-start.5) | collective-permute-done | bytes 524320 | tf_op jit(solution)/shard_map/ppermute | solution.py:30
  43.5 10.6 %collective-permute-done.rest_1_ = bf16[2,128,1024]{2,1,0:T(8,128)(2,1)S(1)} collective-permute-done((bf16[2,128,1024]{2,1,0:T(8,128)(2,1)}, bf16[2,128,1024]{2,1,0:T(8,128)(2,1)S(1)}, u32[]{:S(2)}, u32[]{:S(2)}) %collective-permute-start) | collective-permute-done | bytes 524320 | tf_op jit(solution)/shard_map/ppermute | solution.py:30
  55.7 9.5 %collective-permute-done.2.rest_3_ = bf16[2,128,1024]{2,1,0:T(8,128)(2,1)S(1)} collective-permute-done((bf16[2,128,1024]{2,1,0:T(8,128)(2,1)}, bf16[2,128,1024]{2,1,0:T(8,128)(2,1)S(1)}, u32[]{:S(2)}, u32[]{:S(2)}) %collective-permute-start.2) | collective-permute-done | bytes 524320 | tf_op jit(solution)/shard_map/ppermute | solution.py:30
  66.0 2.1 collective-permute-start.6
  68.2 45.0 %all-to-all-done.rest_4_ = bf16[8,2,128,1024]{3,2,1,0:T(8,128)(2,1)} async-done(((bf16[8,2,128,1024]{3,2,1,0:T(8,128)(2,1)}), bf16[8,2,128,1024]{3,2,1,0:T(8,128)(2,1)}, u32[]{:S(2)}, u32[]{:S(2)}) %all-to-all-start) | async-done | bytes 4194336 | tf_op jit(solution)/shard_map/all_to_all | solution.py:62
  113.2 7.7 %all-to-all-start.1 = ((bf16[4,2,128,1024]{3,2,1,0:T(8,128)(2,1)}), bf16[4,2,128,1024]{3,2,1,0:T(8,128)(2,1)S(1)}, u32[]{:S(2)}, u32[]{:S(2)}) async-start(bf16[4,2,128,1024]{3,2,1,0:T(8,128)(2,1)} %get-tuple-element.56), calls=%async_computation.1 | async-start | bytes 4194304 | tf_op jit(solution)/shard_map/all_to_all | solution.py:42
  120.9 1.2 collective-permute-start.11
  122.1 1.3 collective-permute-start.12
  123.4 1.0 collective-permute-done.6.rest_5_
  124.5 1.0 copy-done.24
  125.5 1.0 copy-done.26
  127.6 1.0 copy-done.30
  128.6 22.6 %attend_blocks.2 = (bf16[2,128,1024]{2,1,0:T(8,128)(2,1)}, bf16[2,128,1024]{2,1,0:T(8,128)(2,1)}, bf16[2,128,1024]{2,1,0:T(8,128)(2,1)}, bf16[2,128,1024]{2,1,0:T(8,128)(2,1)}, bf16[8,2,128,1024]{3,2,1,0:T(8,128)(2,1)}) custom-call(s32[1,8,2]{2,1,0:T(8,128)S(1)} %copy.11.uses, bf16[2,128,1024]{2,1,0:T(8,128)(2,1)S(1)} %copy-done.24, ...), custom_call_target="tpu_custom_call" | custom-call | flops 38654705664 | bytes 12582912 | tf_op jit(solution)/shard_map/attend_blocks/pallas_call | solution.py:292
  152.1 30.2 %collective-permute-done.11.rest_7_ = bf16[2,128,1024]{2,1,0:T(8,128)(2,1)S(1)} collective-permute-done((bf16[2,128,1024]{2,1,0:T(8,128)(2,1)}, bf16[2,128,1024]{2,1,0:T(8,128)(2,1)S(1)}, u32[]{:S(2)}, u32[]{:S(2)}) %collective-permute-start.11) | collective-permute-done | bytes 524320 | tf_op jit(solution)/shard_map/ppermute | solution.py:352
  183.0 8.8 %collective-permute-done.12.rest_8_ = bf16[2,128,1024]{2,1,0:T(8,128)(2,1)S(1)} collective-permute-done((bf16[2,128,1024]{2,1,0:T(8,128)(2,1)S(1)}, bf16[2,128,1024]{2,1,0:T(8,128)(2,1)S(1)}, u32[]{:S(2)}, u32[]{:S(2)}) %collective-permute-start.12) | collective-permute-done | bytes 524320 | tf_op jit(solution)/shard_map/ppermute | solution.py:352
  192.5 6.3 %all-to-all-start.2 = ((bf16[8,2,128,1024]{3,2,1,0:T(8,128)(2,1)}), bf16[8,2,128,1024]{3,2,1,0:T(8,128)(2,1)}, u32[]{:S(2)}, u32[]{:S(2)}) async-start(bf16[8,2,128,1024]{3,2,1,0:T(8,128)(2,1)} %get-tuple-element.104), calls=%async_computation.2 | async-start | bytes 8388608 | tf_op jit(solution)/shard_map/all_to_all | solution.py:62
  199.3 2.2 collective-permute-start.9
  201.5 10.6 %collective-permute-done.7.refs_1_ = bf16[2,128,1024]{2,1,0:T(8,128)(2,1)S(1)} collective-permute-done((bf16[2,128,1024]{2,1,0:T(8,128)(2,1)}, bf16[2,128,1024]{2,1,0:T(8,128)(2,1)S(1)}, u32[]{:S(2)}, u32[]{:S(2)}) %collective-permute-start.7) | collective-permute-done | bytes 524320 | tf_op jit(solution)/shard_map/ppermute | solution.py:30
  213.7 9.5 %collective-permute-done.9.refs_3_ = bf16[2,128,1024]{2,1,0:T(8,128)(2,1)S(1)} collective-permute-done((bf16[2,128,1024]{2,1,0:T(8,128)(2,1)}, bf16[2,128,1024]{2,1,0:T(8,128)(2,1)S(1)}, u32[]{:S(2)}, u32[]{:S(2)}) %collective-permute-start.9) | collective-permute-done | bytes 524320 | tf_op jit(solution)/shard_map/ppermute | solution.py:30
  224.2 1.0 copy-done.13
  225.2 1.0 copy-done.15
  226.3 1.0 copy-done.17
  228.3 1.0 copy-done.21
  229.4 1.0 copy-done.23
  230.4 24.0 %attend_blocks.3 = (bf16[2,128,1024]{2,1,0:T(8,128)(2,1)}, bf16[2,128,1024]{2,1,0:T(8,128)(2,1)}, bf16[2,128,1024]{2,1,0:T(8,128)(2,1)}, bf16[2,128,1024]{2,1,0:...) custom-call(s32[1,8,2]{2,1,0:T(8,128)S(1)} %copy.12.uses, ...), custom_call_target="tpu_custom_call" | custom-call | flops 38654705664 | bytes 12582912 | tf_op jit(solution)/shard_map/attend_blocks/pallas_call | solution.py:292
  254.8 1.2 collective-permute-start.14
  256.0 1.2 collective-permute-start.15
  257.2 2.9 collective-permute-start.19
  260.1 1.4 collective-permute-start.20
  261.6 4.3 %collective-permute-done.13.refs_5_ = bf16[2,128,1024]{2,1,0:T(8,128)(2,1)S(1)} collective-permute-done((bf16[2,128,1024]{2,1,0:T(8,128)(2,1)}, bf16[2,128,1024]{2,1,0:T(8,128)(2,1)S(1)}, u32[]{:S(2)}, u32[]{:S(2)}) %collective-permute-start.13) | collective-permute-done | bytes 524320 | tf_op jit(solution)/shard_map/ppermute | solution.py:30
  265.9 13.1 %collective-permute-done.15.refs_7_ = bf16[2,128,1024]{2,1,0:T(8,128)(2,1)S(1)} collective-permute-done((bf16[2,128,1024]{2,1,0:T(8,128)(2,1)}, bf16[2,128,1024]{2,1,0:T(8,128)(2,1)S(1)}, u32[]{:S(2)}, u32[]{:S(2)}) %collective-permute-start.15) | collective-permute-done | bytes 524320 | tf_op jit(solution)/shard_map/ppermute | solution.py:30
  278.9 2.3 collective-permute-start.16
  281.2 3.3 collective-permute-start.17
  284.5 38.7 %collective-permute-done.19.rest_4_ = bf16[2,128,1024]{2,1,0:T(8,128)(2,1)S(1)} collective-permute-done((bf16[2,128,1024]{2,1,0:T(8,128)(2,1)}, bf16[2,128,1024]{2,1,0:T(8,128)(2,1)S(1)}, u32[]{:S(2)}, u32[]{:S(2)}) %collective-permute-start.19) | collective-permute-done | bytes 524320 | tf_op jit(solution)/shard_map/ppermute | solution.py:352
  323.9 23.8 %collective-permute-done.20.rest_5_ = bf16[2,128,1024]{2,1,0:T(8,128)(2,1)S(1)} collective-permute-done((bf16[2,128,1024]{2,1,0:T(8,128)(2,1)}, bf16[2,128,1024]{2,1,0:T(8,128)(2,1)S(1)}, u32[]{:S(2)}, u32[]{:S(2)}) %collective-permute-start.20) | collective-permute-done | bytes 524320 | tf_op jit(solution)/shard_map/ppermute | solution.py:352
  348.8 2.1 unpack_rows.1
  350.9 4.8 %owner_sum.2.rest_8_ = bf16[4,2,128,2048]{3,2,1,0:T(8,128)(2,1)} custom-call(s32[1,8,1]{2,1,0:T(8,128)S(1)} %copy.10.lists, bf16[8,2,128,1024]{3,2,1,0:T(8,128)(2,1)} %all-to-all-done.2.rest_0_), custom_call_target="tpu_custom_call" | custom-call | flops 2097152 | bytes 6291456 | tf_op jit(solution)/shard_map/owner_sum/pallas_call | solution.py:328
  355.8 3.6 collective-permute-done.18.rest_3_
  359.4 10.2 %collective-permute-done.21.rest_6_ = bf16[2,128,1024]{2,1,0:T(8,128)(2,1)} collective-permute-done((bf16[2,128,1024]{2,1,0:T(8,128)(2,1)}, bf16[2,128,1024]{2,1,0:T(8,128)(2,1)}, u32[]{:S(2)}, u32[]{:S(2)}) %collective-permute-start.21) | collective-permute-done | bytes 524320 | tf_op jit(solution)/shard_map/ppermute | solution.py:352
  369.6 9.7 %collective-permute-done.22.rest_7_ = bf16[2,128,1024]{2,1,0:T(8,128)(2,1)} collective-permute-done((bf16[2,128,1024]{2,1,0:T(8,128)(2,1)}, bf16[2,128,1024]{2,1,0:T(8,128)(2,1)}, u32[]{:S(2)}, u32[]{:S(2)}) %collective-permute-start.22) | collective-permute-done | bytes 524320 | tf_op jit(solution)/shard_map/ppermute | solution.py:352
  379.3 4.5 %owner_sum.3 = bf16[4,2,128,2048]{3,2,1,0:T(8,128)(2,1)} custom-call(s32[1,8,1]{2,1,0:T(8,128)S(1)} %copy.10.lists, bf16[2,128,1024]{2,1,0:T(8,128)(2,1)S(1)} %copy-done.2, bf16[2,128,1024]{2,1,0:T(8,128)(2,1)S(1)} %collective-permute-done.16.rest_1_, bf16[2,128,1024]{2,1,0:T(8,128)(2,1)S(1)} %collective-permute-done.17.rest_2_, ...), custom_call_target="tpu_custom_call", output_to_operand_aliasing={{}: (9, {})} | custom-call | flops 2097152 | bytes 6291456 | tf_op jit(solution)/shard_map/owner_sum/pallas_call | solution.py:328
  (85 shorter events, 15.9 us)
Async XLA Ops:
  5.8 5.7 %copy-start.32 = (s32[1,8,1]{1,2,0:T(1,128)S(1)}, s32[1,8,1]{1,2,0:T(1,128)}, u32[]{:S(2)}) copy-start(s32[1,8,1]{1,2,0:T(1,128)} %param.7) | copy-start | bytes 100
  5.8 107.3 %all-to-all-start = ((bf16[8,2,128,1024]{3,2,1,0:T(8,128)(2,1)}), bf16[8,2,128,1024]{3,2,1,0:T(8,128)(2,1)}, u32[]{:S(2)}, u32[]{:S(2)}) async-start(bf16[8,2,128,1024]{3,2,1,0:T(8,128)(2,1)} %pick_entries.2), calls=%async_computation | async-start | bytes 8388608 | tf_op jit(solution)/shard_map/all_to_all | solution.py:62
  11.5 4.9 %copy-start = (bf16[1,128,8192]{2,1,0:T(8,128)(2,1)S(1)}, bf16[1,128,8192]{2,1,0:T(8,128)(2,1)}, u32[]{:S(2)}) copy-start(bf16[1,128,8192]{2,1,0:T(8,128)(2,1)} %q_ref.1) | copy-start | bytes 6291460
  11.6 4.8 %copy-start.1 = (bf16[1,128,8192]{2,1,0:T(8,128)(2,1)S(1)}, bf16[1,128,8192]{2,1,0:T(8,128)(2,1)}, u32[]{:S(2)}) copy-start(bf16[1,128,8192]{2,1,0:T(8,128)(2,1)} %g_ref.3) | copy-start | bytes 6291460
  16.4 51.7 %copy-start.31 = (s32[1,8,2]{1,2,0:T(2,128)S(1)}, s32[1,8,2]{1,2,0:T(2,128)}, u32[]{:S(2)}) copy-start(s32[1,8,2]{1,2,0:T(2,128)} %param.8) | copy-start | bytes 196
  18.0 13.4 %collective-permute-start.3 = (bf16[2,128,1024]{2,1,0:T(8,128)(2,1)}, bf16[2,128,1024]{2,1,0:T(8,128)(2,1)S(1)}, u32[]{:S(2)}, u32[]{:S(2)}) collective-permute-start(bf16[2,128,1024]{2,1,0:T(8,128)(2,1)} %get-tuple-element.67), channel_id=1, source_target_pairs={{0,1},{1,0},{2,3},{3,2},{4,5},{5,4},{6,7},{7,6},{8,9},{9,8},{10,11... | collective-permute-start | bytes 1572872 | tf_op jit(solution)/shard_map/ppermute | solution.py:30
  18.3 14.1 %collective-permute-start.4 = (bf16[2,128,1024]{2,1,0:T(8,128)(2,1)}, bf16[2,128,1024]{2,1,0:T(8,128)(2,1)S(1)}, u32[]{:S(2)}, u32[]{:S(2)}) collective-permute-start(bf16[2,128,1024]{2,1,0:T(8,128)(2,1)} %get-tuple-element.68), channel_id=1, source_target_pairs={{0,2},{1,3},{2,0},{3,1},{4,6},{5,7},{6,4},{7,5},{8,10},{9,11},{10,... | collective-permute-start | bytes 1572872 | tf_op jit(solution)/shard_map/ppermute | solution.py:30
  18.6 103.6 %copy-start.33 = (bf16[2,128,1024]{2,1,0:T(8,128)(2,1)S(1)}, bf16[2,128,1024]{2,1,0:T(8,128)(2,1)}, u32[]{:S(2)}) copy-start(bf16[2,128,1024]{2,1,0:T(8,128)(2,1)} %get-tuple-element.82) | copy-start | bytes 1572868
  18.6 24.1 %collective-permute-start.5 = (bf16[2,128,1024]{2,1,0:T(8,128)(2,1)}, bf16[2,128,1024]{2,1,0:T(8,128)(2,1)S(1)}, u32[]{:S(2)}, u32[]{:S(2)}) collective-permute-start(bf16[2,128,1024]{2,1,0:T(8,128)(2,1)} %get-tuple-element.69), channel_id=1, source_target_pairs={{0,3},{1,2},{2,1},{3,0},{4,7},{5,6},{6,5},{7,4},{8,11},{9,10},{10,... | collective-permute-start | bytes 1572872 | tf_op jit(solution)/shard_map/ppermute | solution.py:30
  22.3 31.8 %collective-permute-start = (bf16[2,128,1024]{2,1,0:T(8,128)(2,1)}, bf16[2,128,1024]{2,1,0:T(8,128)(2,1)S(1)}, u32[]{:S(2)}, u32[]{:S(2)}) collective-permute-start(bf16[2,128,1024]{2,1,0:T(8,128)(2,1)} %get-tuple-element.59), channel_id=1, source_target_pairs={{0,1},{1,0},{2,3},{3,2},{4,5},{5,4},{6,7},{7,6},{8,9},{9,8},{10,11... | collective-permute-start | bytes 1572872 | tf_op jit(solution)/shard_map/ppermute | solution.py:30
  22.6 32.2 %collective-permute-start.1 = (bf16[2,128,1024]{2,1,0:T(8,128)(2,1)}, bf16[2,128,1024]{2,1,0:T(8,128)(2,1)S(1)}, u32[]{:S(2)}, u32[]{:S(2)}) collective-permute-start(bf16[2,128,1024]{2,1,0:T(8,128)(2,1)} %get-tuple-element.60), channel_id=1, source_target_pairs={{0,2},{1,3},{2,0},{3,1},{4,6},{5,7},{6,4},{7,5},{8,10},{9,11},{10,... | collective-permute-start | bytes 1572872 | tf_op jit(solution)/shard_map/ppermute | solution.py:30
  32.3 32.9 %collective-permute-start.2 = (bf16[2,128,1024]{2,1,0:T(8,128)(2,1)}, bf16[2,128,1024]{2,1,0:T(8,128)(2,1)S(1)}, u32[]{:S(2)}, u32[]{:S(2)}) collective-permute-start(bf16[2,128,1024]{2,1,0:T(8,128)(2,1)} %get-tuple-element.61), channel_id=1, source_target_pairs={{0,3},{1,2},{2,1},{3,0},{4,7},{5,6},{6,5},{7,4},{8,11},{9,10},{10,... | collective-permute-start | bytes 1572872 | tf_op jit(solution)/shard_map/ppermute | solution.py:30
  32.5 118.8 %copy-start.14 = (bf16[2,128,1024]{2,1,0:T(8,128)(2,1)}, bf16[2,128,1024]{2,1,0:T(8,128)(2,1)S(1)}, u32[]{:S(2)}) copy-start(bf16[2,128,1024]{2,1,0:T(8,128)(2,1)S(1)} %collective-permute-done.4.rest_2_) | copy-start | bytes 1572868
  66.0 58.5 %collective-permute-start.6 = (bf16[2,128,1024]{2,1,0:T(8,128)(2,1)}, bf16[2,128,1024]{2,1,0:T(8,128)(2,1)}, u32[]{:S(2)}, u32[]{:S(2)}) collective-permute-start(bf16[2,128,1024]{2,1,0:T(8,128)(2,1)} %get-tuple-element.70), channel_id=1, source_target_pairs={{0,16},{4,20},{8,24},{12,28},{16,0},{20,4},{24,8},{28,12},{1,17},{... | collective-permute-start | bytes 1572872 | tf_op jit(solution)/shard_map/ppermute | solution.py:352
  113.2 79.4 %all-to-all-start.1 = ((bf16[4,2,128,1024]{3,2,1,0:T(8,128)(2,1)}), bf16[4,2,128,1024]{3,2,1,0:T(8,128)(2,1)S(1)}, u32[]{:S(2)}, u32[]{:S(2)}) async-start(bf16[4,2,128,1024]{3,2,1,0:T(8,128)(2,1)} %get-tuple-element.56), calls=%async_computation.1 | async-start | bytes 4194304 | tf_op jit(solution)/shard_map/all_to_all | solution.py:42
  120.9 30.3 %collective-permute-start.10 = (bf16[2,128,1024]{2,1,0:T(8,128)(2,1)}, bf16[2,128,1024]{2,1,0:T(8,128)(2,1)S(1)}, u32[]{:S(2)}, u32[]{:S(2)}) collective-permute-start(bf16[2,128,1024]{2,1,0:T(8,128)(2,1)} %get-tuple-element.80), channel_id=1, source_target_pairs={{0,20},{4,24},{8,28},{12,16},{20,0},{24,4},{28,8},{16,12},{1,21},{... | collective-permute-start | bytes 1572872 | tf_op jit(solution)/shard_map/ppermute | solution.py:352
  120.9 61.3 %collective-permute-start.11 = (bf16[2,128,1024]{2,1,0:T(8,128)(2,1)}, bf16[2,128,1024]{2,1,0:T(8,128)(2,1)S(1)}, u32[]{:S(2)}, u32[]{:S(2)}) collective-permute-start(bf16[2,128,1024]{2,1,0:T(8,128)(2,1)} %get-tuple-element.81), channel_id=1, source_target_pairs={{0,24},{4,28},{8,16},{12,20},{24,0},{28,4},{16,8},{20,12},{1,25},{... | collective-permute-start | bytes 1572872 | tf_op jit(solution)/shard_map/ppermute | solution.py:352
  122.1 69.6 %collective-permute-start.12 = (bf16[2,128,1024]{2,1,0:T(8,128)(2,1)S(1)}, bf16[2,128,1024]{2,1,0:T(8,128)(2,1)S(1)}, u32[]{:S(2)}, u32[]{:S(2)}) collective-permute-start(bf16[2,128,1024]{2,1,0:T(8,128)(2,1)S(1)} %copy-done.33), channel_id=1, source_target_pairs={{0,28},{4,16},{8,20},{12,24},{28,0},{16,4},{20,8},{24,12},{1,29},{... | collective-permute-start | bytes 1572872 | tf_op jit(solution)/shard_map/ppermute | solution.py:352
  124.5 1.0 copy-start.24
  125.5 1.0 copy-start.26
  126.5 1.0 copy-start.28
  127.6 1.0 copy-start.30
  192.5 31.6 %copy-start.11 = (bf16[2,128,1024]{2,1,0:T(8,128)(2,1)S(1)}, bf16[2,128,1024]{2,1,0:T(8,128)(2,1)}, u32[]{:S(2)}) copy-start(bf16[2,128,1024]{2,1,0:T(8,128)(2,1)} %get-tuple-element.66.rest_0_) | copy-start | bytes 1572868
  192.5 158.4 %all-to-all-start.2 = ((bf16[8,2,128,1024]{3,2,1,0:T(8,128)(2,1)}), bf16[8,2,128,1024]{3,2,1,0:T(8,128)(2,1)}, u32[]{:S(2)}, u32[]{:S(2)}) async-start(bf16[8,2,128,1024]{3,2,1,0:T(8,128)(2,1)} %get-tuple-element.104), calls=%async_computation.2 | async-start | bytes 8388608 | tf_op jit(solution)/shard_map/all_to_all | solution.py:62
  198.8 13.3 %collective-permute-start.7 = (bf16[2,128,1024]{2,1,0:T(8,128)(2,1)}, bf16[2,128,1024]{2,1,0:T(8,128)(2,1)S(1)}, u32[]{:S(2)}, u32[]{:S(2)}) collective-permute-start(bf16[2,128,1024]{2,1,0:T(8,128)(2,1)} %get-tuple-element.73), channel_id=1, source_target_pairs={{0,1},{1,0},{2,3},{3,2},{4,5},{5,4},{6,7},{7,6},{8,9},{9,8},{10,11... | collective-permute-start | bytes 1572872 | tf_op jit(solution)/shard_map/ppermute | solution.py:30
  199.1 13.8 %collective-permute-start.8 = (bf16[2,128,1024]{2,1,0:T(8,128)(2,1)}, bf16[2,128,1024]{2,1,0:T(8,128)(2,1)S(1)}, u32[]{:S(2)}, u32[]{:S(2)}) collective-permute-start(bf16[2,128,1024]{2,1,0:T(8,128)(2,1)} %get-tuple-element.74), channel_id=1, source_target_pairs={{0,2},{1,3},{2,0},{3,1},{4,6},{5,7},{6,4},{7,5},{8,10},{9,11},{10,... | collective-permute-start | bytes 1572872 | tf_op jit(solution)/shard_map/ppermute | solution.py:30
  199.3 23.9 %collective-permute-start.9 = (bf16[2,128,1024]{2,1,0:T(8,128)(2,1)}, bf16[2,128,1024]{2,1,0:T(8,128)(2,1)S(1)}, u32[]{:S(2)}, u32[]{:S(2)}) collective-permute-start(bf16[2,128,1024]{2,1,0:T(8,128)(2,1)} %get-tuple-element.75), channel_id=1, source_target_pairs={{0,3},{1,2},{2,1},{3,0},{4,7},{5,6},{6,5},{7,4},{8,11},{9,10},{10,... | collective-permute-start | bytes 1572872 | tf_op jit(solution)/shard_map/ppermute | solution.py:30
  224.2 1.0 copy-start.13
  225.2 1.0 copy-start.15
  226.3 1.0 copy-start.17
  227.3 1.0 copy-start.19
  228.3 1.0 copy-start.21
  230.4 117.3 %copy-start.3 = (bf16[2,128,1024]{2,1,0:T(8,128)(2,1)S(1)}, bf16[2,128,1024]{2,1,0:T(8,128)(2,1)}, u32[]{:S(2)}) copy-start(bf16[2,128,1024]{2,1,0:T(8,128)(2,1)} %get-tuple-element.72.refs_0_) | copy-start | bytes 1572868
  230.4 117.3 %copy-start.5 = (bf16[2,128,1024]{2,1,0:T(8,128)(2,1)S(1)}, bf16[2,128,1024]{2,1,0:T(8,128)(2,1)}, u32[]{:S(2)}) copy-start(bf16[2,128,1024]{2,1,0:T(8,128)(2,1)} %copy-done.4) | copy-start | bytes 1572868
  230.4 117.3 %copy-start.7 = (bf16[2,128,1024]{2,1,0:T(8,128)(2,1)S(1)}, bf16[2,128,1024]{2,1,0:T(8,128)(2,1)}, u32[]{:S(2)}) copy-start(bf16[2,128,1024]{2,1,0:T(8,128)(2,1)} %copy-done.6) | copy-start | bytes 1572868
  230.4 117.3 %copy-start.9 = (bf16[2,128,1024]{2,1,0:T(8,128)(2,1)S(1)}, bf16[2,128,1024]{2,1,0:T(8,128)(2,1)}, u32[]{:S(2)}) copy-start(bf16[2,128,1024]{2,1,0:T(8,128)(2,1)} %copy-done.8) | copy-start | bytes 1572868
  254.5 11.4 %collective-permute-start.13 = (bf16[2,128,1024]{2,1,0:T(8,128)(2,1)}, bf16[2,128,1024]{2,1,0:T(8,128)(2,1)S(1)}, u32[]{:S(2)}, u32[]{:S(2)}) collective-permute-start(bf16[2,128,1024]{2,1,0:T(8,128)(2,1)} %get-tuple-element.84), channel_id=1, source_target_pairs={{0,1},{1,0},{2,3},{3,2},{4,5},{5,4},{6,7},{7,6},{8,9},{9,8},{10,11... | collective-permute-start | bytes 1572872 | tf_op jit(solution)/shard_map/ppermute | solution.py:30
  254.8 11.1 %collective-permute-start.14 = (bf16[2,128,1024]{2,1,0:T(8,128)(2,1)}, bf16[2,128,1024]{2,1,0:T(8,128)(2,1)S(1)}, u32[]{:S(2)}, u32[]{:S(2)}) collective-permute-start(bf16[2,128,1024]{2,1,0:T(8,128)(2,1)} %get-tuple-element.85), channel_id=1, source_target_pairs={{0,2},{1,3},{2,0},{3,1},{4,6},{5,7},{6,4},{7,5},{8,10},{9,11},{10,... | collective-permute-start | bytes 1572872 | tf_op jit(solution)/shard_map/ppermute | solution.py:30
  256.0 22.9 %collective-permute-start.15 = (bf16[2,128,1024]{2,1,0:T(8,128)(2,1)}, bf16[2,128,1024]{2,1,0:T(8,128)(2,1)S(1)}, u32[]{:S(2)}, u32[]{:S(2)}) collective-permute-start(bf16[2,128,1024]{2,1,0:T(8,128)(2,1)} %get-tuple-element.86), channel_id=1, source_target_pairs={{0,3},{1,2},{2,1},{3,0},{4,7},{5,6},{6,5},{7,4},{8,11},{9,10},{10,... | collective-permute-start | bytes 1572872 | tf_op jit(solution)/shard_map/ppermute | solution.py:30
  257.2 66.0 %collective-permute-start.19 = (bf16[2,128,1024]{2,1,0:T(8,128)(2,1)}, bf16[2,128,1024]{2,1,0:T(8,128)(2,1)S(1)}, u32[]{:S(2)}, u32[]{:S(2)}) collective-permute-start(bf16[2,128,1024]{2,1,0:T(8,128)(2,1)} %get-tuple-element.97), channel_id=1, source_target_pairs={{0,16},{4,20},{8,24},{12,28},{16,0},{20,4},{24,8},{28,12},{1,17},{... | collective-permute-start | bytes 1572872 | tf_op jit(solution)/shard_map/ppermute | solution.py:352
  260.1 87.6 %collective-permute-start.20 = (bf16[2,128,1024]{2,1,0:T(8,128)(2,1)}, bf16[2,128,1024]{2,1,0:T(8,128)(2,1)S(1)}, u32[]{:S(2)}, u32[]{:S(2)}) collective-permute-start(bf16[2,128,1024]{2,1,0:T(8,128)(2,1)} %get-tuple-element.98), channel_id=1, source_target_pairs={{0,20},{4,24},{8,28},{12,16},{20,0},{24,4},{28,8},{16,12},{1,21},{... | collective-permute-start | bytes 1572872 | tf_op jit(solution)/shard_map/ppermute | solution.py:352
  278.9 76.8 %collective-permute-start.16 = (bf16[2,128,1024]{2,1,0:T(8,128)(2,1)}, bf16[2,128,1024]{2,1,0:T(8,128)(2,1)S(1)}, u32[]{:S(2)}, u32[]{:S(2)}) collective-permute-start(bf16[2,128,1024]{2,1,0:T(8,128)(2,1)} %get-tuple-element.94), channel_id=1, source_target_pairs={{0,4},{4,0},{8,12},{12,8},{16,20},{20,16},{24,28},{28,24},{1,5},{5... | collective-permute-start | bytes 1572872 | tf_op jit(solution)/shard_map/ppermute | solution.py:52
  281.2 74.5 %collective-permute-start.17 = (bf16[2,128,1024]{2,1,0:T(8,128)(2,1)}, bf16[2,128,1024]{2,1,0:T(8,128)(2,1)S(1)}, u32[]{:S(2)}, u32[]{:S(2)}) collective-permute-start(bf16[2,128,1024]{2,1,0:T(8,128)(2,1)} %get-tuple-element.95), channel_id=1, source_target_pairs={{0,8},{4,12},{8,0},{12,4},{16,24},{20,28},{24,16},{28,20},{1,9},{5... | collective-permute-start | bytes 1572872 | tf_op jit(solution)/shard_map/ppermute | solution.py:52
  284.5 74.9 %collective-permute-start.18 = (bf16[2,128,1024]{2,1,0:T(8,128)(2,1)}, bf16[2,128,1024]{2,1,0:T(8,128)(2,1)S(1)}, u32[]{:S(2)}, u32[]{:S(2)}) collective-permute-start(bf16[2,128,1024]{2,1,0:T(8,128)(2,1)} %get-tuple-element.96), channel_id=1, source_target_pairs={{0,12},{4,8},{8,4},{12,0},{16,28},{20,24},{24,20},{28,16},{1,13},{... | collective-permute-start | bytes 1572872 | tf_op jit(solution)/shard_map/ppermute | solution.py:52
  323.2 46.5 %collective-permute-start.21 = (bf16[2,128,1024]{2,1,0:T(8,128)(2,1)}, bf16[2,128,1024]{2,1,0:T(8,128)(2,1)}, u32[]{:S(2)}, u32[]{:S(2)}) collective-permute-start(bf16[2,128,1024]{2,1,0:T(8,128)(2,1)} %get-tuple-element.100), channel_id=1, source_target_pairs={{0,24},{4,28},{8,16},{12,20},{24,0},{28,4},{16,8},{20,12},{1,25},{... | collective-permute-start | bytes 1572872 | tf_op jit(solution)/shard_map/ppermute | solution.py:352
  347.7 31.6 %collective-permute-start.22 = (bf16[2,128,1024]{2,1,0:T(8,128)(2,1)}, bf16[2,128,1024]{2,1,0:T(8,128)(2,1)}, u32[]{:S(2)}, u32[]{:S(2)}) collective-permute-start(bf16[2,128,1024]{2,1,0:T(8,128)(2,1)} %get-tuple-element.102), channel_id=1, source_target_pairs={{0,28},{4,16},{8,20},{12,24},{28,0},{16,4},{20,8},{24,12},{1,29},{... | collective-permute-start | bytes 1572872 | tf_op jit(solution)/shard_map/ppermute | solution.py:352
  347.7 1.0 copy-start.10
  350.9 28.4 %copy-start.2 = (bf16[2,128,1024]{2,1,0:T(8,128)(2,1)S(1)}, bf16[2,128,1024]{2,1,0:T(8,128)(2,1)}, u32[]{:S(2)}) copy-start(bf16[2,128,1024]{2,1,0:T(8,128)(2,1)} %get-tuple-element.93.rest_0_) | copy-start | bytes 1572868
  (12 other events, 9.9 us)

commit v19 on v16

--- a/solution.py
+++ b/solution.py
@@ -165,7 +165,7 @@
     chunk = held.shape[-1]
     arriving, leaving = [], []
     for n, (seq, out) in enumerate(kv_views(outs, seqs, form)):
-        source = pool_ref.at[lists[0, seq, 0], :, :, first : first + chunk]
+        source = pool_ref.at[lists[0, seq], :, :, first : first + chunk]
         arriving.append(pltpu.make_async_copy(source, held.at[n], sems.at[0, n]))
         leaving.append(pltpu.make_async_copy(held.at[n], out, sems.at[1, n]))
         arriving[n].start()
@@ -312,7 +312,7 @@
     out_ref, acc = rest[-2], rest[-1]
     acc[...] = jnp.zeros_like(acc)
     for seq, piece in kv_views(rest[:pieces], seqs, form):
-        acc[lists[0, seq, 0]] += piece[...].astype(F32)
+        acc[lists[0, seq]] += piece[...].astype(F32)
     out_ref[...] = acc[...].astype(BF16)
 
 
@@ -353,6 +353,7 @@
 
 def local(seqs, parts, queries, kv_pool, send_lists, block_slots, grad_context):
     width = kv_pool.shape[-1]
+    send_lists = send_lists[:, :, 0]
     cut = (SHARE * width // DH // 16) * DH
     bounds = [(0, cut), (cut, width - cut)]
     firsts = [first for first, _ in bounds]
@@ -366,7 +367,8 @@
         swap_rows(pack(first, chunk, queries, grad_context, width, parts))
         for first, chunk in bounds
     ]
-    far = swap_far(after(far, rows), seqs)
+    far = after(far, rows)
+    far = swap_far(far[:2] + after(far[2:], early), seqs)
     near = swap_near(near, seqs)
 
     early = after(early, far[0])

time: 389 us -> 388 us (level)
  local copies, waits for them, and re-layouts: 15.9 us -> 21.7 us
  waiting for transfers between devices: 250 us -> 246 us
    all_to_all x2, waiting for transfers between devices: 73.9 us -> 54.7 us  [swap_pool(): return lax.all_to_all(array, 'enc', split_axis=0, concat_axis=0, tiled=True)]
    ppermute x8, waiting for transfers between devices: 100 us -> 112 us  [swap_far(): got.append(lax.ppermute(piece, 'enc', pairs))]
    unnamed x58 -> x73, local copies, waits for them, and re-layouts: 15.8 us -> 21.6 us
where the time goes in v19:
time: 388 us; the launch traced here: 383 us
  waiting for transfers between devices  246 us (63%)
  Pallas kernels  69.8 us (18%)
  starting transfers between devices  45.2 us (12%)
  local copies, waits for them, and re-layouts  21.7 us (6%)
    ppermute x8, waiting for transfers between devices, swap_far(): got.append(lax.ppermute(piece, 'enc', pairs))  112 us
    ppermute x12, waiting for transfers between devices, exchange(): return lax.ppermute(array, axis, pairs)  75.6 us
    all_to_all x2, waiting for transfers between devices, swap_pool(): return lax.all_to_all(array, 'enc', split_axis=0, concat_axis=0, tiled=True)  54.7 us
    pallas_call x2, Pallas kernels, attend(): pl.pallas_call(functools.partial(attend_kernel, seqs, parts, forms, piece...  46.7 us
    unnamed x73, local copies, waits for them, and re-layouts  21.6 us
    all_to_all x2, starting transfers between devices, swap_pool(): return lax.all_to_all(array, 'enc', split_axis=0, concat_axis=0, tiled=True)  11.9 us
    ppermute x8, starting transfers between devices, swap_far(): got.append(lax.ppermute(piece, 'enc', pairs))  11.2 us
    pallas_call x2, Pallas kernels, owner_sum(): pl.pallas_call(functools.partial(owner_kernel, seqs, form, len(back)), gr...  9.28 us
  transfers between devices with their start and end apart: 26, of which 17 were waited for; matrix products, arithmetic and copies ran while one was open for 0% of the time, Pallas kernels for 16%

profile of v19, /device:TPU:15, one launch (start us, length us, event | category | flops | bytes accessed | tf_op | source)
XLA Modules:
  0.0 383.4 jit_solution(16368021700306673911)
XLA Ops:
  1.3 4.1 %pick_entries.2 = bf16[8,2,128,1024]{3,2,1,0:T(8,128)(2,1)} custom-call(s32[1,8]{1,0:T(1,128)S(1)} %bitcast.1, bf16[4,2,128,2048]{3,2,1,0:T(8,128)(2,1)} %pool_ref.3), custom_call_target="tpu_custom_call" | custom-call | bytes 8388608 | tf_op jit(solution)/shard_map/pick_entries/pallas_call | solution.py:182
  5.4 5.6 %all-to-all-start = ((bf16[8,2,128,1024]{3,2,1,0:T(8,128)(2,1)}), bf16[8,2,128,1024]{3,2,1,0:T(8,128)(2,1)}, u32[]{:S(2)}, u32[]{:S(2)}) async-start(bf16[8,2,128,1024]{3,2,1,0:T(8,128)(2,1)} %pick_entries.2), calls=%async_computation | async-start | bytes 8388608 | tf_op jit(solution)/shard_map/all_to_all | solution.py:62
  11.1 4.4 %pick_entries.3 = (bf16[4,2,128,1024]{3,2,1,0:T(8,128)(2,1)}, bf16[2,128,1024]{2,1,0:T(8,128)(2,1)}, bf16[2,128,1024]{2,1,0:T(8,128)(2,1)}, bf16[2,128,1024]{2,1,0:T(8,128)(2,1)}, bf16[2,128,1024]{2,1,0:T(8,128)(2,1)}) custom-call(s32[1,8]{1,0:T(1,128)S(1)} %bitcast.2, bf16[4,2,128,2048]{3,2,1,0:T(8,128)(2,1)} %pool_ref.3), custom_call_target="tpu_custom_call" | custom-call | bytes 8388608 | tf_op jit(solution)/shard_map/pick_entries/pallas_call | solution.py:182
  16.1 1.6 pack_rows.3
  18.2 2.2 collective-permute-start.5
  20.4 1.6 pack_rows.2
  22.5 8.6 %collective-permute-done.3.rest_1_ = bf16[2,128,1024]{2,1,0:T(8,128)(2,1)S(1)} collective-permute-done((bf16[2,128,1024]{2,1,0:T(8,128)(2,1)}, bf16[2,128,1024]{2,1,0:T(8,128)(2,1)S(1)}, u32[]{:S(2)}, u32[]{:S(2)}) %collective-permute-start.3) | collective-permute-done | bytes 524320 | tf_op jit(solution)/shard_map/ppermute | solution.py:30
  32.9 9.4 %collective-permute-done.5.rest_3_ = bf16[2,128,1024]{2,1,0:T(8,128)(2,1)S(1)} collective-permute-done((bf16[2,128,1024]{2,1,0:T(8,128)(2,1)}, bf16[2,128,1024]{2,1,0:T(8,128)(2,1)S(1)}, u32[]{:S(2)}, u32[]{:S(2)}) %collective-permute-start.5) | collective-permute-done | bytes 524320 | tf_op jit(solution)/shard_map/ppermute | solution.py:30
  43.1 10.6 %collective-permute-done.rest_1_ = bf16[2,128,1024]{2,1,0:T(8,128)(2,1)S(1)} collective-permute-done((bf16[2,128,1024]{2,1,0:T(8,128)(2,1)}, bf16[2,128,1024]{2,1,0:T(8,128)(2,1)S(1)}, u32[]{:S(2)}, u32[]{:S(2)}) %collective-permute-start) | collective-permute-done | bytes 524320 | tf_op jit(solution)/shard_map/ppermute | solution.py:30
  55.3 9.5 %collective-permute-done.2.rest_3_ = bf16[2,128,1024]{2,1,0:T(8,128)(2,1)S(1)} collective-permute-done((bf16[2,128,1024]{2,1,0:T(8,128)(2,1)}, bf16[2,128,1024]{2,1,0:T(8,128)(2,1)S(1)}, u32[]{:S(2)}, u32[]{:S(2)}) %collective-permute-start.2) | collective-permute-done | bytes 524320 | tf_op jit(solution)/shard_map/ppermute | solution.py:30
  65.6 2.1 collective-permute-start.6
  67.8 1.5 collective-permute-start.10
  69.3 54.7 %all-to-all-done.rest_4_ = bf16[8,2,128,1024]{3,2,1,0:T(8,128)(2,1)} async-done(((bf16[8,2,128,1024]{3,2,1,0:T(8,128)(2,1)}), bf16[8,2,128,1024]{3,2,1,0:T(8,128)(2,1)}, u32[]{:S(2)}, u32[]{:S(2)}) %all-to-all-start) | async-done | bytes 4194336 | tf_op jit(solution)/shard_map/all_to_all | solution.py:62
  124.0 7.7 %all-to-all-start.1 = ((bf16[4,2,128,1024]{3,2,1,0:T(8,128)(2,1)}), bf16[4,2,128,1024]{3,2,1,0:T(8,128)(2,1)S(1)}, u32[]{:S(2)}, u32[]{:S(2)}) async-start(bf16[4,2,128,1024]{3,2,1,0:T(8,128)(2,1)} %get-tuple-element.55), calls=%async_computation.1 | async-start | bytes 4194304 | tf_op jit(solution)/shard_map/all_to_all | solution.py:42
  131.7 2.4 collective-permute-start.12
  134.2 1.1 collective-permute-done.6.rest_5_
  135.3 1.0 copy-done.26
  136.3 1.0 copy-done.28
  137.4 1.0 copy-done.30
  139.5 22.7 %attend_blocks.2 = (bf16[2,128,1024]{2,1,0:T(8,128)(2,1)}, bf16[2,128,1024]{2,1,0:T(8,128)(2,1)}, bf16[2,128,1024]{2,1,0:T(8,128)(2,1)}, bf16[2,128,1024]{2,1,0:T(8,128)(2,1)}, bf16[8,2,128,1024]{3,2,1,0:T(8,128)(2,1)}) custom-call(s32[1,8,2]{2,1,0:T(8,128)S(1)} %copy.9.uses, bf16[2,128,1024]{2,1,0:T(8,128)(2,1)S(1)} %copy-done.26, ...), custom_call_target="tpu_custom_call" | custom-call | flops 38654705664 | bytes 12582912 | tf_op jit(solution)/shard_map/attend_blocks/pallas_call | solution.py:290
  162.2 19.6 %collective-permute-done.11.rest_7_ = bf16[2,128,1024]{2,1,0:T(8,128)(2,1)S(1)} collective-permute-done((bf16[2,128,1024]{2,1,0:T(8,128)(2,1)}, bf16[2,128,1024]{2,1,0:T(8,128)(2,1)S(1)}, u32[]{:S(2)}, u32[]{:S(2)}) %collective-permute-start.11) | collective-permute-done | bytes 524320 | tf_op jit(solution)/shard_map/ppermute | solution.py:350
  182.6 8.7 %collective-permute-done.12.rest_8_ = bf16[2,128,1024]{2,1,0:T(8,128)(2,1)S(1)} collective-permute-done((bf16[2,128,1024]{2,1,0:T(8,128)(2,1)S(1)}, bf16[2,128,1024]{2,1,0:T(8,128)(2,1)S(1)}, u32[]{:S(2)}, u32[]{:S(2)}) %collective-permute-start.12) | collective-permute-done | bytes 524320 | tf_op jit(solution)/shard_map/ppermute | solution.py:350
  192.1 6.3 %all-to-all-start.2 = ((bf16[8,2,128,1024]{3,2,1,0:T(8,128)(2,1)}), bf16[8,2,128,1024]{3,2,1,0:T(8,128)(2,1)}, u32[]{:S(2)}, u32[]{:S(2)}) async-start(bf16[8,2,128,1024]{3,2,1,0:T(8,128)(2,1)} %get-tuple-element.102), calls=%async_computation.2 | async-start | bytes 8388608 | tf_op jit(solution)/shard_map/all_to_all | solution.py:62
  198.9 2.2 collective-permute-start.9
  201.1 10.6 %collective-permute-done.7.refs_1_ = bf16[2,128,1024]{2,1,0:T(8,128)(2,1)S(1)} collective-permute-done((bf16[2,128,1024]{2,1,0:T(8,128)(2,1)}, bf16[2,128,1024]{2,1,0:T(8,128)(2,1)S(1)}, u32[]{:S(2)}, u32[]{:S(2)}) %collective-permute-start.7) | collective-permute-done | bytes 524320 | tf_op jit(solution)/shard_map/ppermute | solution.py:30
  213.3 9.5 %collective-permute-done.9.refs_3_ = bf16[2,128,1024]{2,1,0:T(8,128)(2,1)S(1)} collective-permute-done((bf16[2,128,1024]{2,1,0:T(8,128)(2,1)S(1)}, bf16[2,128,1024]{2,1,0:T(8,128)(2,1)S(1)}, u32[]{:S(2)}, u32[]{:S(2)}) %collective-permute-start.9) | collective-permute-done | bytes 524320 | tf_op jit(solution)/shard_map/ppermute | solution.py:30
  223.7 1.0 copy-done.15
  224.8 1.0 copy-done.17
  225.8 1.0 copy-done.19
  227.9 1.0 copy-done.23
  229.0 1.0 copy-done.25
  230.0 24.0 %attend_blocks.3 = (bf16[2,128,1024]{2,1,0:T(8,128)(2,1)}, bf16[2,128,1024]{2,1,0:T(8,128)(2,1)}, bf16[2,128,1024]{2,1,0:T(8,128)(2,1)}, bf16[2,128,1024]{2,1,0:...) custom-call(s32[1,8,2]{2,1,0:T(8,128)S(1)} %copy.10.uses, ...), custom_call_target="tpu_custom_call" | custom-call | flops 38654705664 | bytes 12582912 | tf_op jit(solution)/shard_map/attend_blocks/pallas_call | solution.py:290
  254.4 1.2 collective-permute-start.14
  255.6 1.2 collective-permute-start.15
  256.8 2.9 collective-permute-start.19
  259.7 1.4 collective-permute-start.20
  261.1 4.3 %collective-permute-done.13.refs_5_ = bf16[2,128,1024]{2,1,0:T(8,128)(2,1)S(1)} collective-permute-done((bf16[2,128,1024]{2,1,0:T(8,128)(2,1)}, bf16[2,128,1024]{2,1,0:T(8,128)(2,1)S(1)}, u32[]{:S(2)}, u32[]{:S(2)}) %collective-permute-start.13) | collective-permute-done | bytes 524320 | tf_op jit(solution)/shard_map/ppermute | solution.py:30
  265.4 13.1 %collective-permute-done.15.refs_7_ = bf16[2,128,1024]{2,1,0:T(8,128)(2,1)S(1)} collective-permute-done((bf16[2,128,1024]{2,1,0:T(8,128)(2,1)}, bf16[2,128,1024]{2,1,0:T(8,128)(2,1)S(1)}, u32[]{:S(2)}, u32[]{:S(2)}) %collective-permute-start.15) | collective-permute-done | bytes 524320 | tf_op jit(solution)/shard_map/ppermute | solution.py:30
  278.5 2.3 collective-permute-start.16
  280.8 3.3 collective-permute-start.17
  284.1 38.7 %collective-permute-done.19.rest_4_ = bf16[2,128,1024]{2,1,0:T(8,128)(2,1)S(1)} collective-permute-done((bf16[2,128,1024]{2,1,0:T(8,128)(2,1)}, bf16[2,128,1024]{2,1,0:T(8,128)(2,1)S(1)}, u32[]{:S(2)}, u32[]{:S(2)}) %collective-permute-start.19) | collective-permute-done | bytes 524320 | tf_op jit(solution)/shard_map/ppermute | solution.py:350
  323.5 23.8 %collective-permute-done.20.rest_5_ = bf16[2,128,1024]{2,1,0:T(8,128)(2,1)S(1)} collective-permute-done((bf16[2,128,1024]{2,1,0:T(8,128)(2,1)}, bf16[2,128,1024]{2,1,0:T(8,128)(2,1)S(1)}, u32[]{:S(2)}, u32[]{:S(2)}) %collective-permute-start.20) | collective-permute-done | bytes 524320 | tf_op jit(solution)/shard_map/ppermute | solution.py:350
  348.4 2.1 unpack_rows.1
  350.5 4.8 %owner_sum.2.rest_8_ = bf16[4,2,128,2048]{3,2,1,0:T(8,128)(2,1)} custom-call(s32[1,8]{1,0:T(1,128)S(1)} %bitcast.3, bf16[8,2,128,1024]{3,2,1,0:T(8,128)(2,1)} %all-to-all-done.2.rest_0_), custom_call_target="tpu_custom_call" | custom-call | flops 2097152 | bytes 6291456 | tf_op jit(solution)/shard_map/owner_sum/pallas_call | solution.py:326
  355.4 3.6 collective-permute-done.18.rest_3_
  359.0 10.2 %collective-permute-done.21.rest_6_ = bf16[2,128,1024]{2,1,0:T(8,128)(2,1)} collective-permute-done((bf16[2,128,1024]{2,1,0:T(8,128)(2,1)}, bf16[2,128,1024]{2,1,0:T(8,128)(2,1)}, u32[]{:S(2)}, u32[]{:S(2)}) %collective-permute-start.21) | collective-permute-done | bytes 524320 | tf_op jit(solution)/shard_map/ppermute | solution.py:350
  369.2 9.7 %collective-permute-done.22.rest_7_ = bf16[2,128,1024]{2,1,0:T(8,128)(2,1)} collective-permute-done((bf16[2,128,1024]{2,1,0:T(8,128)(2,1)}, bf16[2,128,1024]{2,1,0:T(8,128)(2,1)}, u32[]{:S(2)}, u32[]{:S(2)}) %collective-permute-start.22) | collective-permute-done | bytes 524320 | tf_op jit(solution)/shard_map/ppermute | solution.py:350
  378.9 4.5 %owner_sum.3 = bf16[4,2,128,2048]{3,2,1,0:T(8,128)(2,1)} custom-call(s32[1,8]{1,0:T(1,128)S(1)} %bitcast.4, bf16[2,128,1024]{2,1,0:T(8,128)(2,1)S(1)} %copy-done.2, bf16[2,128,1024]{2,1,0:T(8,128)(2,1)S(1)} %collective-permute-done.16.rest_1_, bf16[2,128,1024]{2,1,0:T(8,128)(2,1)S(1)} %collective-permute-done.17.rest_2_, ...), custom_call_target="tpu_custom_call", output_to_operand_aliasing={{}: (9, {})} | custom-call | flops 2097152 | bytes 6291456 | tf_op jit(solution)/shard_map/owner_sum/pallas_call | solution.py:326
  (87 shorter events, 16.3 us)
Async XLA Ops:
  5.4 5.7 %copy-start.12 = (s32[1,8,1]{1,2,0:T(1,128)S(1)}, s32[1,8,1]{1,2,0:T(1,128)}, u32[]{:S(2)}) copy-start(s32[1,8,1]{1,2,0:T(1,128)} %param.7) | copy-start | bytes 100
  5.4 118.6 %all-to-all-start = ((bf16[8,2,128,1024]{3,2,1,0:T(8,128)(2,1)}), bf16[8,2,128,1024]{3,2,1,0:T(8,128)(2,1)}, u32[]{:S(2)}, u32[]{:S(2)}) async-start(bf16[8,2,128,1024]{3,2,1,0:T(8,128)(2,1)} %pick_entries.2), calls=%async_computation | async-start | bytes 8388608 | tf_op jit(solution)/shard_map/all_to_all | solution.py:62
  11.1 4.4 %copy-start = (bf16[1,128,8192]{2,1,0:T(8,128)(2,1)S(1)}, bf16[1,128,8192]{2,1,0:T(8,128)(2,1)}, u32[]{:S(2)}) copy-start(bf16[1,128,8192]{2,1,0:T(8,128)(2,1)} %q_ref.1) | copy-start | bytes 6291460
  11.1 5.0 %copy-start.1 = (bf16[1,128,8192]{2,1,0:T(8,128)(2,1)S(1)}, bf16[1,128,8192]{2,1,0:T(8,128)(2,1)}, u32[]{:S(2)}) copy-start(bf16[1,128,8192]{2,1,0:T(8,128)(2,1)} %g_ref.3) | copy-start | bytes 6291460
  16.1 51.6 %copy-start.33 = (s32[1,8,2]{1,2,0:T(2,128)S(1)}, s32[1,8,2]{1,2,0:T(2,128)}, u32[]{:S(2)}) copy-start(s32[1,8,2]{1,2,0:T(2,128)} %param.8) | copy-start | bytes 196
  17.6 13.4 %collective-permute-start.3 = (bf16[2,128,1024]{2,1,0:T(8,128)(2,1)}, bf16[2,128,1024]{2,1,0:T(8,128)(2,1)S(1)}, u32[]{:S(2)}, u32[]{:S(2)}) collective-permute-start(bf16[2,128,1024]{2,1,0:T(8,128)(2,1)} %get-tuple-element.66), channel_id=1, source_target_pairs={{0,1},{1,0},{2,3},{3,2},{4,5},{5,4},{6,7},{7,6},{8,9},{9,8},{10,11... | collective-permute-start | bytes 1572872 | tf_op jit(solution)/shard_map/ppermute | solution.py:30
  18.0 14.1 %collective-permute-start.4 = (bf16[2,128,1024]{2,1,0:T(8,128)(2,1)}, bf16[2,128,1024]{2,1,0:T(8,128)(2,1)S(1)}, u32[]{:S(2)}, u32[]{:S(2)}) collective-permute-start(bf16[2,128,1024]{2,1,0:T(8,128)(2,1)} %get-tuple-element.67), channel_id=1, source_target_pairs={{0,2},{1,3},{2,0},{3,1},{4,6},{5,7},{6,4},{7,5},{8,10},{9,11},{10,... | collective-permute-start | bytes 1572872 | tf_op jit(solution)/shard_map/ppermute | solution.py:30
  18.2 113.5 %copy-start.34 = (bf16[2,128,1024]{2,1,0:T(8,128)(2,1)S(1)}, bf16[2,128,1024]{2,1,0:T(8,128)(2,1)}, u32[]{:S(2)}) copy-start(bf16[2,128,1024]{2,1,0:T(8,128)(2,1)} %get-tuple-element.80) | copy-start | bytes 1572868
  18.2 24.1 %collective-permute-start.5 = (bf16[2,128,1024]{2,1,0:T(8,128)(2,1)}, bf16[2,128,1024]{2,1,0:T(8,128)(2,1)S(1)}, u32[]{:S(2)}, u32[]{:S(2)}) collective-permute-start(bf16[2,128,1024]{2,1,0:T(8,128)(2,1)} %get-tuple-element.68), channel_id=1, source_target_pairs={{0,3},{1,2},{2,1},{3,0},{4,7},{5,6},{6,5},{7,4},{8,11},{9,10},{10,... | collective-permute-start | bytes 1572872 | tf_op jit(solution)/shard_map/ppermute | solution.py:30
  21.9 31.8 %collective-permute-start = (bf16[2,128,1024]{2,1,0:T(8,128)(2,1)}, bf16[2,128,1024]{2,1,0:T(8,128)(2,1)S(1)}, u32[]{:S(2)}, u32[]{:S(2)}) collective-permute-start(bf16[2,128,1024]{2,1,0:T(8,128)(2,1)} %get-tuple-element.58), channel_id=1, source_target_pairs={{0,1},{1,0},{2,3},{3,2},{4,5},{5,4},{6,7},{7,6},{8,9},{9,8},{10,11... | collective-permute-start | bytes 1572872 | tf_op jit(solution)/shard_map/ppermute | solution.py:30
  22.2 32.3 %collective-permute-start.1 = (bf16[2,128,1024]{2,1,0:T(8,128)(2,1)}, bf16[2,128,1024]{2,1,0:T(8,128)(2,1)S(1)}, u32[]{:S(2)}, u32[]{:S(2)}) collective-permute-start(bf16[2,128,1024]{2,1,0:T(8,128)(2,1)} %get-tuple-element.59), channel_id=1, source_target_pairs={{0,2},{1,3},{2,0},{3,1},{4,6},{5,7},{6,4},{7,5},{8,10},{9,11},{10,... | collective-permute-start | bytes 1572872 | tf_op jit(solution)/shard_map/ppermute | solution.py:30
  31.9 32.9 %collective-permute-start.2 = (bf16[2,128,1024]{2,1,0:T(8,128)(2,1)}, bf16[2,128,1024]{2,1,0:T(8,128)(2,1)S(1)}, u32[]{:S(2)}, u32[]{:S(2)}) collective-permute-start(bf16[2,128,1024]{2,1,0:T(8,128)(2,1)} %get-tuple-element.60), channel_id=1, source_target_pairs={{0,3},{1,2},{2,1},{3,0},{4,7},{5,6},{6,5},{7,4},{8,11},{9,10},{10,... | collective-permute-start | bytes 1572872 | tf_op jit(solution)/shard_map/ppermute | solution.py:30
  65.6 69.7 %collective-permute-start.6 = (bf16[2,128,1024]{2,1,0:T(8,128)(2,1)}, bf16[2,128,1024]{2,1,0:T(8,128)(2,1)S(1)}, u32[]{:S(2)}, u32[]{:S(2)}) collective-permute-start(bf16[2,128,1024]{2,1,0:T(8,128)(2,1)} %get-tuple-element.69), channel_id=1, source_target_pairs={{0,16},{4,20},{8,24},{12,28},{16,0},{20,4},{24,8},{28,12},{1,17},{... | collective-permute-start | bytes 1572872 | tf_op jit(solution)/shard_map/ppermute | solution.py:350
  67.8 94.4 %collective-permute-start.10 = (bf16[2,128,1024]{2,1,0:T(8,128)(2,1)}, bf16[2,128,1024]{2,1,0:T(8,128)(2,1)}, u32[]{:S(2)}, u32[]{:S(2)}) collective-permute-start(bf16[2,128,1024]{2,1,0:T(8,128)(2,1)} %get-tuple-element.76), channel_id=1, source_target_pairs={{0,20},{4,24},{8,28},{12,16},{20,0},{24,4},{28,8},{16,12},{1,21},{... | collective-permute-start | bytes 1572872 | tf_op jit(solution)/shard_map/ppermute | solution.py:350
  124.0 68.1 %all-to-all-start.1 = ((bf16[4,2,128,1024]{3,2,1,0:T(8,128)(2,1)}), bf16[4,2,128,1024]{3,2,1,0:T(8,128)(2,1)S(1)}, u32[]{:S(2)}, u32[]{:S(2)}) async-start(bf16[4,2,128,1024]{3,2,1,0:T(8,128)(2,1)} %get-tuple-element.55), calls=%async_computation.1 | async-start | bytes 4194304 | tf_op jit(solution)/shard_map/all_to_all | solution.py:42
  131.7 50.1 %collective-permute-start.11 = (bf16[2,128,1024]{2,1,0:T(8,128)(2,1)}, bf16[2,128,1024]{2,1,0:T(8,128)(2,1)S(1)}, u32[]{:S(2)}, u32[]{:S(2)}) collective-permute-start(bf16[2,128,1024]{2,1,0:T(8,128)(2,1)} %get-tuple-element.79), channel_id=1, source_target_pairs={{0,24},{4,28},{8,16},{12,20},{24,0},{28,4},{16,8},{20,12},{1,25},{... | collective-permute-start | bytes 1572872 | tf_op jit(solution)/shard_map/ppermute | solution.py:350
  131.7 59.6 %collective-permute-start.12 = (bf16[2,128,1024]{2,1,0:T(8,128)(2,1)S(1)}, bf16[2,128,1024]{2,1,0:T(8,128)(2,1)S(1)}, u32[]{:S(2)}, u32[]{:S(2)}) collective-permute-start(bf16[2,128,1024]{2,1,0:T(8,128)(2,1)S(1)} %copy-done.34), channel_id=1, source_target_pairs={{0,28},{4,16},{8,20},{12,24},{28,0},{16,4},{20,8},{24,12},{1,29},{... | collective-permute-start | bytes 1572872 | tf_op jit(solution)/shard_map/ppermute | solution.py:350
  136.3 1.0 copy-start.28
  137.4 1.0 copy-start.30
  138.4 1.0 copy-start.32
  139.4 22.7 %copy-start.20 = (bf16[2,128,1024]{2,1,0:T(8,128)(2,1)}, bf16[2,128,1024]{2,1,0:T(8,128)(2,1)S(1)}, u32[]{:S(2)}) copy-start(bf16[2,128,1024]{2,1,0:T(8,128)(2,1)S(1)} %collective-permute-done.6.rest_5_) | copy-start | bytes 1572868
  192.1 6.8 %copy-start.35 = (bf16[2,128,1024]{2,1,0:T(8,128)(2,1)S(1)}, bf16[2,128,1024]{2,1,0:T(8,128)(2,1)}, u32[]{:S(2)}) copy-start(bf16[2,128,1024]{2,1,0:T(8,128)(2,1)} %get-tuple-element.74) | copy-start | bytes 1572868
  192.1 31.6 %copy-start.13 = (bf16[2,128,1024]{2,1,0:T(8,128)(2,1)S(1)}, bf16[2,128,1024]{2,1,0:T(8,128)(2,1)}, u32[]{:S(2)}) copy-start(bf16[2,128,1024]{2,1,0:T(8,128)(2,1)} %get-tuple-element.65.rest_0_) | copy-start | bytes 1572868
  192.1 158.4 %all-to-all-start.2 = ((bf16[8,2,128,1024]{3,2,1,0:T(8,128)(2,1)}), bf16[8,2,128,1024]{3,2,1,0:T(8,128)(2,1)}, u32[]{:S(2)}, u32[]{:S(2)}) async-start(bf16[8,2,128,1024]{3,2,1,0:T(8,128)(2,1)} %get-tuple-element.102), calls=%async_computation.2 | async-start | bytes 8388608 | tf_op jit(solution)/shard_map/all_to_all | solution.py:62
  198.4 13.3 %collective-permute-start.7 = (bf16[2,128,1024]{2,1,0:T(8,128)(2,1)}, bf16[2,128,1024]{2,1,0:T(8,128)(2,1)S(1)}, u32[]{:S(2)}, u32[]{:S(2)}) collective-permute-start(bf16[2,128,1024]{2,1,0:T(8,128)(2,1)} %get-tuple-element.72), channel_id=1, source_target_pairs={{0,1},{1,0},{2,3},{3,2},{4,5},{5,4},{6,7},{7,6},{8,9},{9,8},{10,11... | collective-permute-start | bytes 1572872 | tf_op jit(solution)/shard_map/ppermute | solution.py:30
  198.7 13.8 %collective-permute-start.8 = (bf16[2,128,1024]{2,1,0:T(8,128)(2,1)}, bf16[2,128,1024]{2,1,0:T(8,128)(2,1)S(1)}, u32[]{:S(2)}, u32[]{:S(2)}) collective-permute-start(bf16[2,128,1024]{2,1,0:T(8,128)(2,1)} %get-tuple-element.73), channel_id=1, source_target_pairs={{0,2},{1,3},{2,0},{3,1},{4,6},{5,7},{6,4},{7,5},{8,10},{9,11},{10,... | collective-permute-start | bytes 1572872 | tf_op jit(solution)/shard_map/ppermute | solution.py:30
  198.9 23.9 %collective-permute-start.9 = (bf16[2,128,1024]{2,1,0:T(8,128)(2,1)S(1)}, bf16[2,128,1024]{2,1,0:T(8,128)(2,1)S(1)}, u32[]{:S(2)}, u32[]{:S(2)}) collective-permute-start(bf16[2,128,1024]{2,1,0:T(8,128)(2,1)S(1)} %copy-done.35), channel_id=1, source_target_pairs={{0,3},{1,2},{2,1},{3,0},{4,7},{5,6},{6,5},{7,4},{8,11},{9,10},{10,... | collective-permute-start | bytes 1572872 | tf_op jit(solution)/shard_map/ppermute | solution.py:30
  223.7 1.0 copy-start.15
  224.8 1.0 copy-start.17
  225.8 1.0 copy-start.19
  226.9 1.0 copy-start.21
  227.9 1.0 copy-start.23
  230.0 117.3 %copy-start.3 = (bf16[2,128,1024]{2,1,0:T(8,128)(2,1)S(1)}, bf16[2,128,1024]{2,1,0:T(8,128)(2,1)}, u32[]{:S(2)}) copy-start(bf16[2,128,1024]{2,1,0:T(8,128)(2,1)} %get-tuple-element.71.refs_0_) | copy-start | bytes 1572868
  230.0 117.3 %copy-start.5 = (bf16[2,128,1024]{2,1,0:T(8,128)(2,1)S(1)}, bf16[2,128,1024]{2,1,0:T(8,128)(2,1)}, u32[]{:S(2)}) copy-start(bf16[2,128,1024]{2,1,0:T(8,128)(2,1)} %copy-done.4) | copy-start | bytes 1572868
  230.0 117.3 %copy-start.7 = (bf16[2,128,1024]{2,1,0:T(8,128)(2,1)S(1)}, bf16[2,128,1024]{2,1,0:T(8,128)(2,1)}, u32[]{:S(2)}) copy-start(bf16[2,128,1024]{2,1,0:T(8,128)(2,1)} %copy-done.6) | copy-start | bytes 1572868
  230.0 117.3 %copy-start.9 = (bf16[2,128,1024]{2,1,0:T(8,128)(2,1)S(1)}, bf16[2,128,1024]{2,1,0:T(8,128)(2,1)}, u32[]{:S(2)}) copy-start(bf16[2,128,1024]{2,1,0:T(8,128)(2,1)} %copy-done.8) | copy-start | bytes 1572868
  254.1 11.4 %collective-permute-start.13 = (bf16[2,128,1024]{2,1,0:T(8,128)(2,1)}, bf16[2,128,1024]{2,1,0:T(8,128)(2,1)S(1)}, u32[]{:S(2)}, u32[]{:S(2)}) collective-permute-start(bf16[2,128,1024]{2,1,0:T(8,128)(2,1)} %get-tuple-element.82), channel_id=1, source_target_pairs={{0,1},{1,0},{2,3},{3,2},{4,5},{5,4},{6,7},{7,6},{8,9},{9,8},{10,11... | collective-permute-start | bytes 1572872 | tf_op jit(solution)/shard_map/ppermute | solution.py:30
  254.4 11.1 %collective-permute-start.14 = (bf16[2,128,1024]{2,1,0:T(8,128)(2,1)}, bf16[2,128,1024]{2,1,0:T(8,128)(2,1)S(1)}, u32[]{:S(2)}, u32[]{:S(2)}) collective-permute-start(bf16[2,128,1024]{2,1,0:T(8,128)(2,1)} %get-tuple-element.83), channel_id=1, source_target_pairs={{0,2},{1,3},{2,0},{3,1},{4,6},{5,7},{6,4},{7,5},{8,10},{9,11},{10,... | collective-permute-start | bytes 1572872 | tf_op jit(solution)/shard_map/ppermute | solution.py:30
  255.6 22.9 %collective-permute-start.15 = (bf16[2,128,1024]{2,1,0:T(8,128)(2,1)}, bf16[2,128,1024]{2,1,0:T(8,128)(2,1)S(1)}, u32[]{:S(2)}, u32[]{:S(2)}) collective-permute-start(bf16[2,128,1024]{2,1,0:T(8,128)(2,1)} %get-tuple-element.84), channel_id=1, source_target_pairs={{0,3},{1,2},{2,1},{3,0},{4,7},{5,6},{6,5},{7,4},{8,11},{9,10},{10,... | collective-permute-start | bytes 1572872 | tf_op jit(solution)/shard_map/ppermute | solution.py:30
  256.8 66.0 %collective-permute-start.19 = (bf16[2,128,1024]{2,1,0:T(8,128)(2,1)}, bf16[2,128,1024]{2,1,0:T(8,128)(2,1)S(1)}, u32[]{:S(2)}, u32[]{:S(2)}) collective-permute-start(bf16[2,128,1024]{2,1,0:T(8,128)(2,1)} %get-tuple-element.95), channel_id=1, source_target_pairs={{0,16},{4,20},{8,24},{12,28},{16,0},{20,4},{24,8},{28,12},{1,17},{... | collective-permute-start | bytes 1572872 | tf_op jit(solution)/shard_map/ppermute | solution.py:350
  259.7 87.6 %collective-permute-start.20 = (bf16[2,128,1024]{2,1,0:T(8,128)(2,1)}, bf16[2,128,1024]{2,1,0:T(8,128)(2,1)S(1)}, u32[]{:S(2)}, u32[]{:S(2)}) collective-permute-start(bf16[2,128,1024]{2,1,0:T(8,128)(2,1)} %get-tuple-element.96), channel_id=1, source_target_pairs={{0,20},{4,24},{8,28},{12,16},{20,0},{24,4},{28,8},{16,12},{1,21},{... | collective-permute-start | bytes 1572872 | tf_op jit(solution)/shard_map/ppermute | solution.py:350
  278.5 76.8 %collective-permute-start.16 = (bf16[2,128,1024]{2,1,0:T(8,128)(2,1)}, bf16[2,128,1024]{2,1,0:T(8,128)(2,1)S(1)}, u32[]{:S(2)}, u32[]{:S(2)}) collective-permute-start(bf16[2,128,1024]{2,1,0:T(8,128)(2,1)} %get-tuple-element.92), channel_id=1, source_target_pairs={{0,4},{4,0},{8,12},{12,8},{16,20},{20,16},{24,28},{28,24},{1,5},{5... | collective-permute-start | bytes 1572872 | tf_op jit(solution)/shard_map/ppermute | solution.py:52
  280.8 74.5 %collective-permute-start.17 = (bf16[2,128,1024]{2,1,0:T(8,128)(2,1)}, bf16[2,128,1024]{2,1,0:T(8,128)(2,1)S(1)}, u32[]{:S(2)}, u32[]{:S(2)}) collective-permute-start(bf16[2,128,1024]{2,1,0:T(8,128)(2,1)} %get-tuple-element.93), channel_id=1, source_target_pairs={{0,8},{4,12},{8,0},{12,4},{16,24},{20,28},{24,16},{28,20},{1,9},{5... | collective-permute-start | bytes 1572872 | tf_op jit(solution)/shard_map/ppermute | solution.py:52
  284.1 74.9 %collective-permute-start.18 = (bf16[2,128,1024]{2,1,0:T(8,128)(2,1)}, bf16[2,128,1024]{2,1,0:T(8,128)(2,1)S(1)}, u32[]{:S(2)}, u32[]{:S(2)}) collective-permute-start(bf16[2,128,1024]{2,1,0:T(8,128)(2,1)} %get-tuple-element.94), channel_id=1, source_target_pairs={{0,12},{4,8},{8,4},{12,0},{16,28},{20,24},{24,20},{28,16},{1,13},{... | collective-permute-start | bytes 1572872 | tf_op jit(solution)/shard_map/ppermute | solution.py:52
  322.8 46.5 %collective-permute-start.21 = (bf16[2,128,1024]{2,1,0:T(8,128)(2,1)}, bf16[2,128,1024]{2,1,0:T(8,128)(2,1)}, u32[]{:S(2)}, u32[]{:S(2)}) collective-permute-start(bf16[2,128,1024]{2,1,0:T(8,128)(2,1)} %get-tuple-element.98), channel_id=1, source_target_pairs={{0,24},{4,28},{8,16},{12,20},{24,0},{28,4},{16,8},{20,12},{1,25},{... | collective-permute-start | bytes 1572872 | tf_op jit(solution)/shard_map/ppermute | solution.py:350
  347.3 31.6 %collective-permute-start.22 = (bf16[2,128,1024]{2,1,0:T(8,128)(2,1)}, bf16[2,128,1024]{2,1,0:T(8,128)(2,1)}, u32[]{:S(2)}, u32[]{:S(2)}) collective-permute-start(bf16[2,128,1024]{2,1,0:T(8,128)(2,1)} %get-tuple-element.100), channel_id=1, source_target_pairs={{0,28},{4,16},{8,20},{12,24},{28,0},{16,4},{20,8},{24,12},{1,29},{... | collective-permute-start | bytes 1572872 | tf_op jit(solution)/shard_map/ppermute | solution.py:350
  347.3 1.0 copy-start.10
  350.5 28.4 %copy-start.2 = (bf16[2,128,1024]{2,1,0:T(8,128)(2,1)S(1)}, bf16[2,128,1024]{2,1,0:T(8,128)(2,1)}, u32[]{:S(2)}) copy-start(bf16[2,128,1024]{2,1,0:T(8,128)(2,1)} %get-tuple-element.91.rest_0_) | copy-start | bytes 1572868
  (14 other events, 11.6 us)

commit v20 on v19

--- a/solution.py
+++ b/solution.py
@@ -372,20 +372,22 @@
     near = swap_near(near, seqs)
 
     early = after(early, far[0])
-    rows_out, whole = attend(seqs, (0, 0), block_slots, rows[0], [early])
-    token_parts = [swap_rows(rows_out)]
-    returns = [[swap_pool(after(whole[0], far))]]
-    block_slots = after(block_slots, token_parts[0])
+    rows_out, (near_back, *far_back) = attend(seqs, (0, 1), block_slots, rows[0], [early])
+    far_back = swap_far([after(*pair) for pair in zip(far_back, far)], seqs)
+    early_rows = after(rows_out, far_back)
     rows_out, back = attend(seqs, (1, 2), block_slots, rows[1], [near, *far])
-    near, far = back[: seqs // 2], back[seqs // 2 :]
+    near, far = back[: seqs // 2], list(back[seqs // 2 :])
+    far[:2] = [after(*pair) for pair in zip(far[:2], far_back)]
     far = swap_far(far, 2)
-    token_parts.append(swap_rows(rows_out))
-    near = swap_half(after(near, token_parts[1]), seqs)
-    returns.append([*near, *far])
+    token_parts = [swap_rows(after(rows_out, far_back))]
+    near_back = swap_near(after(near_back, token_parts[0]), seqs)
+    near = swap_half(after(near, token_parts[0]), seqs)
+    token_parts.insert(0, swap_rows(after(early_rows, near)))
+    returns = [[near_back, *far_back], [*near, *far]]
 
     context, grad_queries = unpack(token_parts, firsts, width, queries.shape)
     pool_grads = None
-    for first, form, back in zip(firsts, (0, 2), returns):
+    for first, form, back in zip(firsts, (1, 2), returns):
         pool_grads = owner_sum(first, form, send_lists, back, kv_pool.shape, pool_grads)
     return (context, grad_queries, pool_grads)
 

time: 388 us -> 442 us (1.14)
  waiting for transfers between devices: 246 us -> 276 us
  local copies, waits for them, and re-layouts: 21.7 us -> 32.8 us
  starting transfers between devices: 45.2 us -> 55.8 us
    ppermute x3, waiting for transfers between devices: 3.64 us -> 57.6 us  [swap_half(): got.append(lax.ppermute(pieces[step], 'enc', pairs))]
    ppermute x8 -> x12, waiting for transfers between devices: 112 us -> 96.3 us  [swap_far(): got.append(lax.ppermute(piece, 'enc', pairs))]
    ppermute x8 -> x12, starting transfers between devices: 11.2 us -> 25.4 us  [swap_far(): got.append(lax.ppermute(piece, 'enc', pairs))]
    unnamed x73 -> x93, local copies, waits for them, and re-layouts: 21.6 us -> 32.8 us
    ppermute x12, waiting for transfers between devices: 75.6 us -> 67.3 us  [exchange(): return lax.ppermute(array, axis, pairs)]
    all_to_all x2 -> x1, starting transfers between devices: 11.9 us -> 5.65 us  [swap_pool(): return lax.all_to_all(array, 'enc', split_axis=0, concat_axis=0, tiled=True)]
    all_to_all x1 -> x2, starting transfers between devices: 7.72 us -> 13.5 us  [swap_near(): lax.all_to_all(array, 'enc', split_axis=0, concat_axis=0, axis_index_grou...]
    all_to_all x2 -> x1, waiting for transfers between devices: 54.7 us -> 54.7 us  [swap_pool(): return lax.all_to_all(array, 'enc', split_axis=0, concat_axis=0, tiled=True)]
  transfers between devices with their start and end apart: 26 -> 30, of which waited for: 17 -> 19; matrix products, arithmetic and copies ran while one was open for 0% -> 0% of each run, Pallas kernels for 16% -> 14%
where the time goes in v20:
time: 442 us; the launch traced here: 435 us
  waiting for transfers between devices  276 us (62%)
  Pallas kernels  69.4 us (16%)
  starting transfers between devices  55.8 us (13%)
  local copies, waits for them, and re-layouts  32.8 us (7%)
    ppermute x12, waiting for transfers between devices, swap_far(): got.append(lax.ppermute(piece, 'enc', pairs))  96.3 us
    ppermute x12, waiting for transfers between devices, exchange(): return lax.ppermute(array, axis, pairs)  67.3 us
    ppermute x3, waiting for transfers between devices, swap_half(): got.append(lax.ppermute(pieces[step], 'enc', pairs))  57.6 us
    all_to_all x1, waiting for transfers between devices, swap_pool(): return lax.all_to_all(array, 'enc', split_axis=0, concat_axis=0, tiled=True)  54.7 us
    pallas_call x2, Pallas kernels, attend(): pl.pallas_call(functools.partial(attend_kernel, seqs, parts, forms, piece...  46.5 us
    unnamed x93, local copies, waits for them, and re-layouts  32.8 us
    ppermute x12, starting transfers between devices, swap_far(): got.append(lax.ppermute(piece, 'enc', pairs))  25.4 us
    all_to_all x2, starting transfers between devices, swap_near(): lax.all_to_all(array, 'enc', split_axis=0, concat_axis=0, axis_index_grou...  13.5 us
  transfers between devices with their start and end apart: 30, of which 19 were waited for; matrix products, arithmetic and copies ran while one was open for 0% of the time, Pallas kernels for 14%

profile of v20, /device:TPU:15, one launch (start us, length us, event | category | flops | bytes accessed | tf_op | source)
XLA Modules:
  0.0 434.7 jit_solution(17420918818028715169)
XLA Ops:
  1.3 4.1 pick_entries.2
  5.4 5.6 %all-to-all-start = ((bf16[8,2,128,1024]{3,2,1,0:T(8,128)(2,1)}), bf16[8,2,128,1024]{3,2,1,0:T(8,128)(2,1)}, u32[]{:S(2)}, u32[]{:S(2)}) async-start(bf16[8,2,128,1024]{3,2,1,0:T(8,128)(2,1)} %pick_entries.2), calls=%async_computation | async-start | bytes 8388608 | tf_op jit(solution)/shard_map/all_to_all | solution.py:62
  11.1 4.4 %pick_entries.3 = (bf16[4,2,128,1024]{3,2,1,0:T(8,128)(2,1)}, bf16[2,128,1024]{2,1,0:T(8,128)(2,1)}, bf16[2,128,1024]{2,1,0:T(8,128)(2,1)}, bf16[2,128,1024]{2,1,0:T(8,128)(2,1)}, bf16[2,128,1024]{2,1,0:T(8,128)(2,1)}) custom-call(s32[1,8]{1,0:T(1,128)S(1)} %bitcast.2, bf16[4,2,128,2048]{3,2,1,0:T(8,128)(2,1)} %pool_ref.3), custom_call_target="tpu_custom_call" | custom-call | bytes 8388608 | tf_op jit(solution)/shard_map/pick_entries/pallas_call | solution.py:182
  16.1 1.6 pack_rows.3
  18.2 2.2 collective-permute-start.5
  20.4 1.6 pack_rows.2
  22.5 8.6 %collective-permute-done.3.rest_1_ = bf16[2,128,1024]{2,1,0:T(8,128)(2,1)S(1)} collective-permute-done((bf16[2,128,1024]{2,1,0:T(8,128)(2,1)}, bf16[2,128,1024]{2,1,0:T(8,128)(2,1)S(1)}, u32[]{:S(2)}, u32[]{:S(2)}) %collective-permute-start.3) | collective-permute-done | bytes 524320 | tf_op jit(solution)/shard_map/ppermute | solution.py:30
  32.9 9.4 %collective-permute-done.5.rest_3_ = bf16[2,128,1024]{2,1,0:T(8,128)(2,1)S(1)} collective-permute-done((bf16[2,128,1024]{2,1,0:T(8,128)(2,1)}, bf16[2,128,1024]{2,1,0:T(8,128)(2,1)S(1)}, u32[]{:S(2)}, u32[]{:S(2)}) %collective-permute-start.5) | collective-permute-done | bytes 524320 | tf_op jit(solution)/shard_map/ppermute | solution.py:30
  43.1 10.6 %collective-permute-done.rest_1_ = bf16[2,128,1024]{2,1,0:T(8,128)(2,1)S(1)} collective-permute-done((bf16[2,128,1024]{2,1,0:T(8,128)(2,1)}, bf16[2,128,1024]{2,1,0:T(8,128)(2,1)S(1)}, u32[]{:S(2)}, u32[]{:S(2)}) %collective-permute-start) | collective-permute-done | bytes 524320 | tf_op jit(solution)/shard_map/ppermute | solution.py:30
  55.3 9.5 %collective-permute-done.2.rest_3_ = bf16[2,128,1024]{2,1,0:T(8,128)(2,1)S(1)} collective-permute-done((bf16[2,128,1024]{2,1,0:T(8,128)(2,1)}, bf16[2,128,1024]{2,1,0:T(8,128)(2,1)S(1)}, u32[]{:S(2)}, u32[]{:S(2)}) %collective-permute-start.2) | collective-permute-done | bytes 524320 | tf_op jit(solution)/shard_map/ppermute | solution.py:30
  65.6 2.1 collective-permute-start.6
  67.8 1.6 collective-permute-start.8
  69.3 54.7 %all-to-all-done.rest_4_ = bf16[8,2,128,1024]{3,2,1,0:T(8,128)(2,1)} async-done(((bf16[8,2,128,1024]{3,2,1,0:T(8,128)(2,1)}), bf16[8,2,128,1024]{3,2,1,0:T(8,128)(2,1)}, u32[]{:S(2)}, u32[]{:S(2)}) %all-to-all-start) | async-done | bytes 4194336 | tf_op jit(solution)/shard_map/all_to_all | solution.py:62
  124.0 7.7 %all-to-all-start.1 = ((bf16[4,2,128,1024]{3,2,1,0:T(8,128)(2,1)}), bf16[4,2,128,1024]{3,2,1,0:T(8,128)(2,1)S(1)}, u32[]{:S(2)}, u32[]{:S(2)}) async-start(bf16[4,2,128,1024]{3,2,1,0:T(8,128)(2,1)} %get-tuple-element.76), calls=%async_computation.1 | async-start | bytes 4194304 | tf_op jit(solution)/shard_map/all_to_all | solution.py:42
  131.7 2.4 collective-permute-start.12
  134.2 1.1 collective-permute-done.6.rest_5_
  135.3 1.0 copy-done.34
  137.4 1.0 copy-done.40
  139.5 22.7 %attend_blocks.2 = (bf16[2,128,1024]{2,1,0:T(8,128)(2,1)}, bf16[2,128,1024]{2,1,0:T(8,128)(2,1)}, bf16[2,128,1024]{2,1,0:T(8,128)(2,1)}, bf16[2,128,1024]{2,1,0:...) custom-call(s32[1,8,2]{2,1,0:T(8,128)S(1)} %copy.9.uses, ...), custom_call_target="tpu_custom_call" | custom-call | flops 38654705664 | bytes 12582912 | tf_op jit(solution)/shard_map/attend_blocks/pallas_call | solution.py:290
  162.2 3.1 collective-permute-start.7
  166.0 2.5 collective-permute-start.9
  168.5 41.4 %collective-permute-done.10.rest_7_ = bf16[2,128,1024]{2,1,0:T(8,128)(2,1)S(1)} collective-permute-done((bf16[2,128,1024]{2,1,0:T(8,128)(2,1)}, bf16[2,128,1024]{2,1,0:T(8,128)(2,1)S(1)}, u32[]{:S(2)}, u32[]{:S(2)}) %collective-permute-start.10) | collective-permute-done | bytes 524320 | tf_op jit(solution)/shard_map/ppermute | solution.py:350
  210.7 8.8 %collective-permute-done.12.rest_8_ = bf16[2,128,1024]{2,1,0:T(8,128)(2,1)S(1)} collective-permute-done((bf16[2,128,1024]{2,1,0:T(8,128)(2,1)}, bf16[2,128,1024]{2,1,0:T(8,128)(2,1)S(1)}, u32[]{:S(2)}, u32[]{:S(2)}) %collective-permute-start.12) | collective-permute-done | bytes 524320 | tf_op jit(solution)/shard_map/ppermute | solution.py:350
  220.4 3.3 collective-permute-start.13
  223.7 1.0 copy-done.23
  232.0 23.8 %attend_blocks.3 = (bf16[2,128,1024]{2,1,0:T(8,128)(2,1)}, bf16[2,128,1024]{2,1,0:T(8,128)(2,1)}, bf16[2,128,1024]{2,1,0:T(8,128)(2,1)}, bf16[2,128,1024]{2,1,0:...) custom-call(s32[1,8,2]{2,1,0:T(8,128)S(1)} %copy.9.uses, ...), custom_call_target="tpu_custom_call" | custom-call | flops 38654705664 | bytes 12582912 | tf_op jit(solution)/shard_map/attend_blocks/pallas_call | solution.py:290
  255.8 5.7 %collective-permute-done.9.rest_2_ = bf16[2,128,1024]{2,1,0:T(8,128)(2,1)S(1)} collective-permute-done((bf16[2,128,1024]{2,1,0:T(8,128)(2,1)}, bf16[2,128,1024]{2,1,0:T(8,128)(2,1)S(1)}, u32[]{:S(2)}, u32[]{:S(2)}) %collective-permute-start.9) | collective-permute-done | bytes 524320 | tf_op jit(solution)/shard_map/ppermute | solution.py:350
  261.5 8.6 %collective-permute-done.13.rest_4_ = bf16[2,128,1024]{2,1,0:T(8,128)(2,1)} collective-permute-done((bf16[2,128,1024]{2,1,0:T(8,128)(2,1)}, bf16[2,128,1024]{2,1,0:T(8,128)(2,1)}, u32[]{:S(2)}, u32[]{:S(2)}) %collective-permute-start.13) | collective-permute-done | bytes 524320 | tf_op jit(solution)/shard_map/ppermute | solution.py:350
  270.1 12.9 %collective-permute-done.11.rest_3_ = bf16[2,128,1024]{2,1,0:T(8,128)(2,1)} collective-permute-done((bf16[2,128,1024]{2,1,0:T(8,128)(2,1)}, bf16[2,128,1024]{2,1,0:T(8,128)(2,1)}, u32[]{:S(2)}, u32[]{:S(2)}) %collective-permute-start.11) | collective-permute-done | bytes 524320 | tf_op jit(solution)/shard_map/ppermute | solution.py:350
  283.5 2.2 collective-permute-start.16
  285.7 10.1 %collective-permute-done.14.refs_5_ = bf16[2,128,1024]{2,1,0:T(8,128)(2,1)S(1)} collective-permute-done((bf16[2,128,1024]{2,1,0:T(8,128)(2,1)}, bf16[2,128,1024]{2,1,0:T(8,128)(2,1)S(1)}, u32[]{:S(2)}, u32[]{:S(2)}) %collective-permute-start.14) | collective-permute-done | bytes 524320 | tf_op jit(solution)/shard_map/ppermute | solution.py:30
  297.5 9.6 %collective-permute-done.16.refs_7_ = bf16[2,128,1024]{2,1,0:T(8,128)(2,1)S(1)} collective-permute-done((bf16[2,128,1024]{2,1,0:T(8,128)(2,1)}, bf16[2,128,1024]{2,1,0:T(8,128)(2,1)S(1)}, u32[]{:S(2)}, u32[]{:S(2)}) %collective-permute-start.16) | collective-permute-done | bytes 524320 | tf_op jit(solution)/shard_map/ppermute | solution.py:30
  307.8 5.8 %all-to-all-start.2 = ((bf16[4,2,128,1024]{3,2,1,0:T(8,128)(2,1)}), bf16[4,2,128,1024]{3,2,1,0:T(8,128)(2,1)S(1)}, u32[]{:S(2)}, u32[]{:S(2)}) async-start(bf16[4,2,128,1024]{3,2,1,0:T(8,128)(2,1)} %get-tuple-element.144), calls=%async_computation.2 | async-start | bytes 4194304 | tf_op jit(solution)/shard_map/all_to_all | solution.py:42
  314.4 1.7 collective-permute-start.19
  316.1 2.0 collective-permute-start.23
  318.9 45.3 %collective-permute-done.18.rest_2_ = bf16[2,128,1024]{2,1,0:T(8,128)(2,1)S(1)} collective-permute-done((bf16[2,128,1024]{2,1,0:T(8,128)(2,1)}, bf16[2,128,1024]{2,1,0:T(8,128)(2,1)S(1)}, u32[]{:S(2)}, u32[]{:S(2)}) %collective-permute-start.18) | collective-permute-done | bytes 524320 | tf_op jit(solution)/shard_map/ppermute | solution.py:52
  365.0 12.3 %collective-permute-done.19.rest_3_ = bf16[2,128,1024]{2,1,0:T(8,128)(2,1)S(1)} collective-permute-done((bf16[2,128,1024]{2,1,0:T(8,128)(2,1)}, bf16[2,128,1024]{2,1,0:T(8,128)(2,1)S(1)}, u32[]{:S(2)}, u32[]{:S(2)}) %collective-permute-start.19) | collective-permute-done | bytes 524320 | tf_op jit(solution)/shard_map/ppermute | solution.py:52
  378.1 1.2 collective-permute-start.20
  379.5 1.2 collective-permute-start.22
  381.6 5.2 %collective-permute-start.25 = (bf16[2,128,1024]{2,1,0:T(8,128)(2,1)}, bf16[2,128,1024]{2,1,0:T(8,128)(2,1)}, u32[]{:S(2)}, u32[]{:S(2)}) collective-permute-start(bf16[2,128,1024]{2,1,0:T(8,128)(2,1)} %get-tuple-element.140), channel_id=1, source_target_pairs={{0,24},{4,28},{8,16},{12,20},{24,0},{28,4},{16,8},{20,12},{1,25},{... | collective-permute-start | bytes 1572872 | tf_op jit(solution)/shard_map/ppermute | solution.py:350
  387.6 3.3 collective-permute-start.26
  391.5 8.9 %collective-permute-done.22.refs_3_ = bf16[2,128,1024]{2,1,0:T(8,128)(2,1)S(1)} collective-permute-done((bf16[2,128,1024]{2,1,0:T(8,128)(2,1)}, bf16[2,128,1024]{2,1,0:T(8,128)(2,1)S(1)}, u32[]{:S(2)}, u32[]{:S(2)}) %collective-permute-start.22) | collective-permute-done | bytes 524320 | tf_op jit(solution)/shard_map/ppermute | solution.py:30
  400.4 1.0 copy-done.13
  405.6 2.1 unpack_rows.1
  407.8 4.6 %owner_sum.2.rest_8_ = bf16[4,2,128,2048]{3,2,1,0:T(8,128)(2,1)} custom-call(s32[1,8]{1,0:T(1,128)S(1)} %bitcast.3, bf16[4,2,128,1024]{3,2,1,0:T(8,128)(2,1)S(1)} %all-to-all-done.2.rest_0_, bf16[2,128,1024]{2,1,0:T(8,128)(2,1)S(1)} %collective-permute-done.7.rest_1_, bf16[2,128,1024]{2,1,0:T(8,128)(2,1)S(1)} %collective-permute-done.9.rest_2_, ...), custom_call_target="tpu_custom_call" | custom-call | flops 2097152 | bytes 6291456 | tf_op jit(solution)/shard_map/owner_sum/pallas_call | solution.py:326
  412.4 7.5 %collective-permute-done.25.rest_6_ = bf16[2,128,1024]{2,1,0:T(8,128)(2,1)} collective-permute-done((bf16[2,128,1024]{2,1,0:T(8,128)(2,1)}, bf16[2,128,1024]{2,1,0:T(8,128)(2,1)}, u32[]{:S(2)}, u32[]{:S(2)}) %collective-permute-start.25) | collective-permute-done | bytes 524320 | tf_op jit(solution)/shard_map/ppermute | solution.py:350
  420.0 10.2 %collective-permute-done.26.rest_7_ = bf16[2,128,1024]{2,1,0:T(8,128)(2,1)} collective-permute-done((bf16[2,128,1024]{2,1,0:T(8,128)(2,1)}, bf16[2,128,1024]{2,1,0:T(8,128)(2,1)}, u32[]{:S(2)}, u32[]{:S(2)}) %collective-permute-start.26) | collective-permute-done | bytes 524320 | tf_op jit(solution)/shard_map/ppermute | solution.py:350
  430.2 4.5 %owner_sum.3 = bf16[4,2,128,2048]{3,2,1,0:T(8,128)(2,1)} custom-call(s32[1,8]{1,0:T(1,128)S(1)} %bitcast.4, bf16[2,128,1024]{2,1,0:T(8,128)(2,1)S(1)} %copy-done.2, bf16[2,128,1024]{2,1,0:T(8,128)(2,1)S(1)} %copy-done.4, bf16[2,128,1024]{2,1,0:T(8,128)(2,1)S(1)} %copy-done.6, bf16[2,128,1024]{2,1,0:T(8,128)(2,1)S(1)} %copy-done.8, ...), custom_call_target="tpu_custom_call", output_to_operand_aliasing={{}: (9, {})} | custom-call | flops 2097152 | bytes 6291456 | tf_op jit(solution)/shard_map/owner_sum/pallas_call | solution.py:326
  (114 shorter events, 32.1 us)
Async XLA Ops:
  5.4 5.7 %copy-start.22 = (s32[1,8,1]{1,2,0:T(1,128)S(1)}, s32[1,8,1]{1,2,0:T(1,128)}, u32[]{:S(2)}) copy-start(s32[1,8,1]{1,2,0:T(1,128)} %param.7) | copy-start | bytes 100
  5.4 118.6 %all-to-all-start = ((bf16[8,2,128,1024]{3,2,1,0:T(8,128)(2,1)}), bf16[8,2,128,1024]{3,2,1,0:T(8,128)(2,1)}, u32[]{:S(2)}, u32[]{:S(2)}) async-start(bf16[8,2,128,1024]{3,2,1,0:T(8,128)(2,1)} %pick_entries.2), calls=%async_computation | async-start | bytes 8388608 | tf_op jit(solution)/shard_map/all_to_all | solution.py:62
  11.1 4.5 %copy-start = (bf16[1,128,8192]{2,1,0:T(8,128)(2,1)S(1)}, bf16[1,128,8192]{2,1,0:T(8,128)(2,1)}, u32[]{:S(2)}) copy-start(bf16[1,128,8192]{2,1,0:T(8,128)(2,1)} %q_ref.1) | copy-start | bytes 6291460
  11.1 5.0 %copy-start.1 = (bf16[1,128,8192]{2,1,0:T(8,128)(2,1)S(1)}, bf16[1,128,8192]{2,1,0:T(8,128)(2,1)}, u32[]{:S(2)}) copy-start(bf16[1,128,8192]{2,1,0:T(8,128)(2,1)} %g_ref.3) | copy-start | bytes 6291460
  17.6 13.4 %collective-permute-start.3 = (bf16[2,128,1024]{2,1,0:T(8,128)(2,1)}, bf16[2,128,1024]{2,1,0:T(8,128)(2,1)S(1)}, u32[]{:S(2)}, u32[]{:S(2)}) collective-permute-start(bf16[2,128,1024]{2,1,0:T(8,128)(2,1)} %get-tuple-element.87), channel_id=1, source_target_pairs={{0,1},{1,0},{2,3},{3,2},{4,5},{5,4},{6,7},{7,6},{8,9},{9,8},{10,11... | collective-permute-start | bytes 1572872 | tf_op jit(solution)/shard_map/ppermute | solution.py:30
  18.0 14.1 %collective-permute-start.4 = (bf16[2,128,1024]{2,1,0:T(8,128)(2,1)}, bf16[2,128,1024]{2,1,0:T(8,128)(2,1)S(1)}, u32[]{:S(2)}, u32[]{:S(2)}) collective-permute-start(bf16[2,128,1024]{2,1,0:T(8,128)(2,1)} %get-tuple-element.88), channel_id=1, source_target_pairs={{0,2},{1,3},{2,0},{3,1},{4,6},{5,7},{6,4},{7,5},{8,10},{9,11},{10,... | collective-permute-start | bytes 1572872 | tf_op jit(solution)/shard_map/ppermute | solution.py:30
  18.2 49.5 %copy-start.45 = (s32[1,8,2]{1,2,0:T(2,128)S(1)}, s32[1,8,2]{1,2,0:T(2,128)}, u32[]{:S(2)}) copy-start(s32[1,8,2]{1,2,0:T(2,128)} %param.8) | copy-start | bytes 196
  18.2 24.1 %collective-permute-start.5 = (bf16[2,128,1024]{2,1,0:T(8,128)(2,1)}, bf16[2,128,1024]{2,1,0:T(8,128)(2,1)S(1)}, u32[]{:S(2)}, u32[]{:S(2)}) collective-permute-start(bf16[2,128,1024]{2,1,0:T(8,128)(2,1)} %get-tuple-element.89), channel_id=1, source_target_pairs={{0,3},{1,2},{2,1},{3,0},{4,7},{5,6},{6,5},{7,4},{8,11},{9,10},{10,... | collective-permute-start | bytes 1572872 | tf_op jit(solution)/shard_map/ppermute | solution.py:30
  21.9 31.8 %collective-permute-start = (bf16[2,128,1024]{2,1,0:T(8,128)(2,1)}, bf16[2,128,1024]{2,1,0:T(8,128)(2,1)S(1)}, u32[]{:S(2)}, u32[]{:S(2)}) collective-permute-start(bf16[2,128,1024]{2,1,0:T(8,128)(2,1)} %get-tuple-element.79), channel_id=1, source_target_pairs={{0,1},{1,0},{2,3},{3,2},{4,5},{5,4},{6,7},{7,6},{8,9},{9,8},{10,11... | collective-permute-start | bytes 1572872 | tf_op jit(solution)/shard_map/ppermute | solution.py:30
  22.2 32.3 %collective-permute-start.1 = (bf16[2,128,1024]{2,1,0:T(8,128)(2,1)}, bf16[2,128,1024]{2,1,0:T(8,128)(2,1)S(1)}, u32[]{:S(2)}, u32[]{:S(2)}) collective-permute-start(bf16[2,128,1024]{2,1,0:T(8,128)(2,1)} %get-tuple-element.80), channel_id=1, source_target_pairs={{0,2},{1,3},{2,0},{3,1},{4,6},{5,7},{6,4},{7,5},{8,10},{9,11},{10,... | collective-permute-start | bytes 1572872 | tf_op jit(solution)/shard_map/ppermute | solution.py:30
  31.9 32.9 %collective-permute-start.2 = (bf16[2,128,1024]{2,1,0:T(8,128)(2,1)}, bf16[2,128,1024]{2,1,0:T(8,128)(2,1)S(1)}, u32[]{:S(2)}, u32[]{:S(2)}) collective-permute-start(bf16[2,128,1024]{2,1,0:T(8,128)(2,1)} %get-tuple-element.81), channel_id=1, source_target_pairs={{0,3},{1,2},{2,1},{3,0},{4,7},{5,6},{6,5},{7,4},{8,11},{9,10},{10,... | collective-permute-start | bytes 1572872 | tf_op jit(solution)/shard_map/ppermute | solution.py:30
  65.6 69.7 %collective-permute-start.6 = (bf16[2,128,1024]{2,1,0:T(8,128)(2,1)}, bf16[2,128,1024]{2,1,0:T(8,128)(2,1)S(1)}, u32[]{:S(2)}, u32[]{:S(2)}) collective-permute-start(bf16[2,128,1024]{2,1,0:T(8,128)(2,1)} %get-tuple-element.90), channel_id=1, source_target_pairs={{0,16},{4,20},{8,24},{12,28},{16,0},{20,4},{24,8},{28,12},{1,17},{... | collective-permute-start | bytes 1572872 | tf_op jit(solution)/shard_map/ppermute | solution.py:350
  67.8 97.4 %collective-permute-start.8 = (bf16[2,128,1024]{2,1,0:T(8,128)(2,1)}, bf16[2,128,1024]{2,1,0:T(8,128)(2,1)S(1)}, u32[]{:S(2)}, u32[]{:S(2)}) collective-permute-start(bf16[2,128,1024]{2,1,0:T(8,128)(2,1)} %get-tuple-element.99), channel_id=1, source_target_pairs={{0,20},{4,24},{8,28},{12,16},{20,0},{24,4},{28,8},{16,12},{1,21},{... | collective-permute-start | bytes 1572872 | tf_op jit(solution)/shard_map/ppermute | solution.py:350
  124.0 99.7 %all-to-all-start.1 = ((bf16[4,2,128,1024]{3,2,1,0:T(8,128)(2,1)}), bf16[4,2,128,1024]{3,2,1,0:T(8,128)(2,1)S(1)}, u32[]{:S(2)}, u32[]{:S(2)}) async-start(bf16[4,2,128,1024]{3,2,1,0:T(8,128)(2,1)} %get-tuple-element.76), calls=%async_computation.1 | async-start | bytes 4194304 | tf_op jit(solution)/shard_map/all_to_all | solution.py:42
  131.7 78.2 %collective-permute-start.10 = (bf16[2,128,1024]{2,1,0:T(8,128)(2,1)}, bf16[2,128,1024]{2,1,0:T(8,128)(2,1)S(1)}, u32[]{:S(2)}, u32[]{:S(2)}) collective-permute-start(bf16[2,128,1024]{2,1,0:T(8,128)(2,1)} %get-tuple-element.104), channel_id=1, source_target_pairs={{0,24},{4,28},{8,16},{12,20},{24,0},{28,4},{16,8},{20,12},{1,25},{... | collective-permute-start | bytes 1572872 | tf_op jit(solution)/shard_map/ppermute | solution.py:350
  131.7 87.8 %collective-permute-start.12 = (bf16[2,128,1024]{2,1,0:T(8,128)(2,1)}, bf16[2,128,1024]{2,1,0:T(8,128)(2,1)S(1)}, u32[]{:S(2)}, u32[]{:S(2)}) collective-permute-start(bf16[2,128,1024]{2,1,0:T(8,128)(2,1)} %get-tuple-element.107), channel_id=1, source_target_pairs={{0,28},{4,16},{8,20},{12,24},{28,0},{16,4},{20,8},{24,12},{1,29},{... | collective-permute-start | bytes 1572872 | tf_op jit(solution)/shard_map/ppermute | solution.py:350
  135.3 1.0 copy-start.34
  136.3 1.0 copy-start.36
  137.4 1.0 copy-start.40
  138.4 1.0 copy-start.44
  139.4 22.7 %copy-start.30 = (bf16[2,128,1024]{2,1,0:T(8,128)(2,1)}, bf16[2,128,1024]{2,1,0:T(8,128)(2,1)S(1)}, u32[]{:S(2)}) copy-start(bf16[2,128,1024]{2,1,0:T(8,128)(2,1)S(1)} %collective-permute-done.6.rest_5_) | copy-start | bytes 1572868
  162.2 93.7 %collective-permute-start.7 = (bf16[2,128,1024]{2,1,0:T(8,128)(2,1)}, bf16[2,128,1024]{2,1,0:T(8,128)(2,1)S(1)}, u32[]{:S(2)}, u32[]{:S(2)}) collective-permute-start(bf16[2,128,1024]{2,1,0:T(8,128)(2,1)} %get-tuple-element.97), channel_id=1, source_target_pairs={{0,16},{4,20},{8,24},{12,28},{16,0},{20,4},{24,8},{28,12},{1,17},{... | collective-permute-start | bytes 1572872 | tf_op jit(solution)/shard_map/ppermute | solution.py:350
  166.0 95.5 %collective-permute-start.9 = (bf16[2,128,1024]{2,1,0:T(8,128)(2,1)}, bf16[2,128,1024]{2,1,0:T(8,128)(2,1)S(1)}, u32[]{:S(2)}, u32[]{:S(2)}) collective-permute-start(bf16[2,128,1024]{2,1,0:T(8,128)(2,1)} %get-tuple-element.100), channel_id=1, source_target_pairs={{0,20},{4,24},{8,28},{12,16},{20,0},{24,4},{28,8},{16,12},{1,21},{... | collective-permute-start | bytes 1572872 | tf_op jit(solution)/shard_map/ppermute | solution.py:350
  220.4 49.7 %collective-permute-start.13 = (bf16[2,128,1024]{2,1,0:T(8,128)(2,1)}, bf16[2,128,1024]{2,1,0:T(8,128)(2,1)}, u32[]{:S(2)}, u32[]{:S(2)}) collective-permute-start(bf16[2,128,1024]{2,1,0:T(8,128)(2,1)} %get-tuple-element.108), channel_id=1, source_target_pairs={{0,28},{4,16},{8,20},{12,24},{28,0},{16,4},{20,8},{24,12},{1,29},{... | collective-permute-start | bytes 1572872 | tf_op jit(solution)/shard_map/ppermute | solution.py:350
  223.6 59.4 %collective-permute-start.11 = (bf16[2,128,1024]{2,1,0:T(8,128)(2,1)}, bf16[2,128,1024]{2,1,0:T(8,128)(2,1)}, u32[]{:S(2)}, u32[]{:S(2)}) collective-permute-start(bf16[2,128,1024]{2,1,0:T(8,128)(2,1)} %get-tuple-element.105), channel_id=1, source_target_pairs={{0,24},{4,28},{8,16},{12,20},{24,0},{28,4},{16,8},{20,12},{1,25},{... | collective-permute-start | bytes 1572872 | tf_op jit(solution)/shard_map/ppermute | solution.py:350
  223.7 1.0 copy-start.23
  224.7 1.0 copy-start.25
  283.0 12.8 %collective-permute-start.14 = (bf16[2,128,1024]{2,1,0:T(8,128)(2,1)}, bf16[2,128,1024]{2,1,0:T(8,128)(2,1)S(1)}, u32[]{:S(2)}, u32[]{:S(2)}) collective-permute-start(bf16[2,128,1024]{2,1,0:T(8,128)(2,1)} %get-tuple-element.122), channel_id=1, source_target_pairs={{0,1},{1,0},{2,3},{3,2},{4,5},{5,4},{6,7},{7,6},{8,9},{9,8},{10,11... | collective-permute-start | bytes 1572872 | tf_op jit(solution)/shard_map/ppermute | solution.py:30
  283.3 13.3 %collective-permute-start.15 = (bf16[2,128,1024]{2,1,0:T(8,128)(2,1)}, bf16[2,128,1024]{2,1,0:T(8,128)(2,1)S(1)}, u32[]{:S(2)}, u32[]{:S(2)}) collective-permute-start(bf16[2,128,1024]{2,1,0:T(8,128)(2,1)} %get-tuple-element.123), channel_id=1, source_target_pairs={{0,2},{1,3},{2,0},{3,1},{4,6},{5,7},{6,4},{7,5},{8,10},{9,11},{10,... | collective-permute-start | bytes 1572872 | tf_op jit(solution)/shard_map/ppermute | solution.py:30
  283.5 23.5 %collective-permute-start.16 = (bf16[2,128,1024]{2,1,0:T(8,128)(2,1)}, bf16[2,128,1024]{2,1,0:T(8,128)(2,1)S(1)}, u32[]{:S(2)}, u32[]{:S(2)}) collective-permute-start(bf16[2,128,1024]{2,1,0:T(8,128)(2,1)} %get-tuple-element.124), channel_id=1, source_target_pairs={{0,3},{1,2},{2,1},{3,0},{4,7},{5,6},{6,5},{7,4},{8,11},{9,10},{10,... | collective-permute-start | bytes 1572872 | tf_op jit(solution)/shard_map/ppermute | solution.py:30
  307.8 99.9 %all-to-all-start.2 = ((bf16[4,2,128,1024]{3,2,1,0:T(8,128)(2,1)}), bf16[4,2,128,1024]{3,2,1,0:T(8,128)(2,1)S(1)}, u32[]{:S(2)}, u32[]{:S(2)}) async-start(bf16[4,2,128,1024]{3,2,1,0:T(8,128)(2,1)} %get-tuple-element.144), calls=%async_computation.2 | async-start | bytes 4194304 | tf_op jit(solution)/shard_map/all_to_all | solution.py:42
  313.7 4.4 %collective-permute-start.17 = (bf16[2,128,1024]{2,1,0:T(8,128)(2,1)}, bf16[2,128,1024]{2,1,0:T(8,128)(2,1)S(1)}, u32[]{:S(2)}, u32[]{:S(2)}) collective-permute-start(bf16[2,128,1024]{2,1,0:T(8,128)(2,1)} %get-tuple-element.126), channel_id=1, source_target_pairs={{0,4},{4,0},{8,12},{12,8},{16,20},{20,16},{24,28},{28,24},{1,5},{5... | collective-permute-start | bytes 1572872 | tf_op jit(solution)/shard_map/ppermute | solution.py:52
  314.4 49.8 %collective-permute-start.18 = (bf16[2,128,1024]{2,1,0:T(8,128)(2,1)}, bf16[2,128,1024]{2,1,0:T(8,128)(2,1)S(1)}, u32[]{:S(2)}, u32[]{:S(2)}) collective-permute-start(bf16[2,128,1024]{2,1,0:T(8,128)(2,1)} %get-tuple-element.127), channel_id=1, source_target_pairs={{0,8},{4,12},{8,0},{12,4},{16,24},{20,28},{24,16},{28,20},{1,9},{5... | collective-permute-start | bytes 1572872 | tf_op jit(solution)/shard_map/ppermute | solution.py:52
  314.4 62.9 %collective-permute-start.19 = (bf16[2,128,1024]{2,1,0:T(8,128)(2,1)}, bf16[2,128,1024]{2,1,0:T(8,128)(2,1)S(1)}, u32[]{:S(2)}, u32[]{:S(2)}) collective-permute-start(bf16[2,128,1024]{2,1,0:T(8,128)(2,1)} %get-tuple-element.128), channel_id=1, source_target_pairs={{0,12},{4,8},{8,4},{12,0},{16,28},{20,24},{24,20},{28,16},{1,13},{... | collective-permute-start | bytes 1572872 | tf_op jit(solution)/shard_map/ppermute | solution.py:52
  316.1 64.6 %collective-permute-start.23 = (bf16[2,128,1024]{2,1,0:T(8,128)(2,1)}, bf16[2,128,1024]{2,1,0:T(8,128)(2,1)S(1)}, u32[]{:S(2)}, u32[]{:S(2)}) collective-permute-start(bf16[2,128,1024]{2,1,0:T(8,128)(2,1)} %get-tuple-element.136), channel_id=1, source_target_pairs={{0,16},{4,20},{8,24},{12,28},{16,0},{20,4},{24,8},{28,12},{1,17},{... | collective-permute-start | bytes 1572872 | tf_op jit(solution)/shard_map/ppermute | solution.py:350
  318.1 68.7 %collective-permute-start.24 = (bf16[2,128,1024]{2,1,0:T(8,128)(2,1)}, bf16[2,128,1024]{2,1,0:T(8,128)(2,1)S(1)}, u32[]{:S(2)}, u32[]{:S(2)}) collective-permute-start(bf16[2,128,1024]{2,1,0:T(8,128)(2,1)} %get-tuple-element.138), channel_id=1, source_target_pairs={{0,20},{4,24},{8,28},{12,16},{20,0},{24,4},{28,8},{16,12},{1,21},{... | collective-permute-start | bytes 1572872 | tf_op jit(solution)/shard_map/ppermute | solution.py:350
  378.1 12.8 %collective-permute-start.20 = (bf16[2,128,1024]{2,1,0:T(8,128)(2,1)}, bf16[2,128,1024]{2,1,0:T(8,128)(2,1)S(1)}, u32[]{:S(2)}, u32[]{:S(2)}) collective-permute-start(bf16[2,128,1024]{2,1,0:T(8,128)(2,1)} %get-tuple-element.130), channel_id=1, source_target_pairs={{0,1},{1,0},{2,3},{3,2},{4,5},{5,4},{6,7},{7,6},{8,9},{9,8},{10,11... | collective-permute-start | bytes 1572872 | tf_op jit(solution)/shard_map/ppermute | solution.py:30
  379.3 12.2 %collective-permute-start.21 = (bf16[2,128,1024]{2,1,0:T(8,128)(2,1)}, bf16[2,128,1024]{2,1,0:T(8,128)(2,1)S(1)}, u32[]{:S(2)}, u32[]{:S(2)}) collective-permute-start(bf16[2,128,1024]{2,1,0:T(8,128)(2,1)} %get-tuple-element.131), channel_id=1, source_target_pairs={{0,2},{1,3},{2,0},{3,1},{4,6},{5,7},{6,4},{7,5},{8,10},{9,11},{10,... | collective-permute-start | bytes 1572872 | tf_op jit(solution)/shard_map/ppermute | solution.py:30
  379.5 20.9 %collective-permute-start.22 = (bf16[2,128,1024]{2,1,0:T(8,128)(2,1)}, bf16[2,128,1024]{2,1,0:T(8,128)(2,1)S(1)}, u32[]{:S(2)}, u32[]{:S(2)}) collective-permute-start(bf16[2,128,1024]{2,1,0:T(8,128)(2,1)} %get-tuple-element.132), channel_id=1, source_target_pairs={{0,3},{1,2},{2,1},{3,0},{4,7},{5,6},{6,5},{7,4},{8,11},{9,10},{10,... | collective-permute-start | bytes 1572872 | tf_op jit(solution)/shard_map/ppermute | solution.py:30
  381.6 38.4 %collective-permute-start.25 = (bf16[2,128,1024]{2,1,0:T(8,128)(2,1)}, bf16[2,128,1024]{2,1,0:T(8,128)(2,1)}, u32[]{:S(2)}, u32[]{:S(2)}) collective-permute-start(bf16[2,128,1024]{2,1,0:T(8,128)(2,1)} %get-tuple-element.140), channel_id=1, source_target_pairs={{0,24},{4,28},{8,16},{12,20},{24,0},{28,4},{16,8},{20,12},{1,25},{... | collective-permute-start | bytes 1572872 | tf_op jit(solution)/shard_map/ppermute | solution.py:350
  387.6 42.6 %collective-permute-start.26 = (bf16[2,128,1024]{2,1,0:T(8,128)(2,1)}, bf16[2,128,1024]{2,1,0:T(8,128)(2,1)}, u32[]{:S(2)}, u32[]{:S(2)}) collective-permute-start(bf16[2,128,1024]{2,1,0:T(8,128)(2,1)} %get-tuple-element.142), channel_id=1, source_target_pairs={{0,28},{4,16},{8,20},{12,24},{28,0},{16,4},{20,8},{24,12},{1,29},{... | collective-permute-start | bytes 1572872 | tf_op jit(solution)/shard_map/ppermute | solution.py:350
  400.4 1.0 copy-start.13
  407.8 22.4 %copy-start.2 = (bf16[2,128,1024]{2,1,0:T(8,128)(2,1)S(1)}, bf16[2,128,1024]{2,1,0:T(8,128)(2,1)}, u32[]{:S(2)}) copy-start(bf16[2,128,1024]{2,1,0:T(8,128)(2,1)} %get-tuple-element.125.rest_0_) | copy-start | bytes 1572868
  407.8 22.4 %copy-start.4 = (bf16[2,128,1024]{2,1,0:T(8,128)(2,1)S(1)}, bf16[2,128,1024]{2,1,0:T(8,128)(2,1)}, u32[]{:S(2)}) copy-start(bf16[2,128,1024]{2,1,0:T(8,128)(2,1)} %copy-done.3) | copy-start | bytes 1572868
  407.8 22.4 %copy-start.6 = (bf16[2,128,1024]{2,1,0:T(8,128)(2,1)S(1)}, bf16[2,128,1024]{2,1,0:T(8,128)(2,1)}, u32[]{:S(2)}) copy-start(bf16[2,128,1024]{2,1,0:T(8,128)(2,1)} %copy-done.5) | copy-start | bytes 1572868
  407.8 22.4 %copy-start.8 = (bf16[2,128,1024]{2,1,0:T(8,128)(2,1)S(1)}, bf16[2,128,1024]{2,1,0:T(8,128)(2,1)}, u32[]{:S(2)}) copy-start(bf16[2,128,1024]{2,1,0:T(8,128)(2,1)} %copy-done.7) | copy-start | bytes 1572868
  407.8 22.4 %copy-start.10 = (bf16[2,128,1024]{2,1,0:T(8,128)(2,1)S(1)}, bf16[2,128,1024]{2,1,0:T(8,128)(2,1)}, u32[]{:S(2)}) copy-start(bf16[2,128,1024]{2,1,0:T(8,128)(2,1)} %copy-done.9) | copy-start | bytes 1572868
  407.8 22.4 %copy-start.12 = (bf16[2,128,1024]{2,1,0:T(8,128)(2,1)S(1)}, bf16[2,128,1024]{2,1,0:T(8,128)(2,1)}, u32[]{:S(2)}) copy-start(bf16[2,128,1024]{2,1,0:T(8,128)(2,1)} %copy-done.11) | copy-start | bytes 1572868
  (28 other events, 24.9 us)

commit v21 on v19

--- a/solution.py
+++ b/solution.py
@@ -12,7 +12,7 @@
 BLOCK = 64
 NBLEN = 128
 ATTEND_WEIGHT = 24
-SHARE = 8
+SHARE = 10
 F32 = jnp.float32
 BF16 = jnp.bfloat16
 LOG2E = 1.4426950408889634

time: 388 us -> 388 us (level)
  waiting for transfers between devices: 246 us -> 254 us
  local copies, waits for them, and re-layouts: 21.7 us -> 16 us
    all_to_all x2, waiting for transfers between devices: 54.7 us -> 68.6 us  [swap_pool(): return lax.all_to_all(array, 'enc', split_axis=0, concat_axis=0, tiled=True)]
    ppermute x8, waiting for transfers between devices: 112 us -> 101 us  [swap_far(): got.append(lax.ppermute(piece, 'enc', pairs))]
    ppermute x12, waiting for transfers between devices: 75.6 us -> 83.6 us  [exchange(): return lax.ppermute(array, axis, pairs)]
    unnamed x73 -> x53, local copies, waits for them, and re-layouts: 21.6 us -> 15.9 us
  transfers between devices with their start and end apart: 26 -> 26, of which waited for: 17 -> 13; matrix products, arithmetic and copies ran while one was open for 0% -> 0% of each run, Pallas kernels for 16% -> 16%
where the time goes in v21:
time: 388 us; the launch traced here: 384 us
  waiting for transfers between devices  254 us (65%)
  Pallas kernels  70.1 us (18%)
  starting transfers between devices  43.2 us (11%)
  local copies, waits for them, and re-layouts  16 us (4%)
    ppermute x8, waiting for transfers between devices, swap_far(): got.append(lax.ppermute(piece, 'enc', pairs))  101 us
    ppermute x12, waiting for transfers between devices, exchange(): return lax.ppermute(array, axis, pairs)  83.6 us
    all_to_all x2, waiting for transfers between devices, swap_pool(): return lax.all_to_all(array, 'enc', split_axis=0, concat_axis=0, tiled=True)  68.6 us
    pallas_call x2, Pallas kernels, attend(): pl.pallas_call(functools.partial(attend_kernel, seqs, parts, forms, piece...  45.7 us
    unnamed x53, local copies, waits for them, and re-layouts  15.9 us
    all_to_all x2, starting transfers between devices, swap_pool(): return lax.all_to_all(array, 'enc', split_axis=0, concat_axis=0, tiled=True)  11.7 us
    pallas_call x2, Pallas kernels, owner_sum(): pl.pallas_call(functools.partial(owner_kernel, seqs, form, len(back)), gr...  10.2 us
    ppermute x8, starting transfers between devices, swap_far(): got.append(lax.ppermute(piece, 'enc', pairs))  10 us
  transfers between devices with their start and end apart: 26, of which 13 were waited for; matrix products, arithmetic and copies ran while one was open for 0% of the time, Pallas kernels for 16%

profile of v21, /device:TPU:15, one launch (start us, length us, event | category | flops | bytes accessed | tf_op | source)
XLA Modules:
  0.0 383.8 jit_solution(6431706817575606169)
XLA Ops:
  1.3 5.2 %pick_entries.2 = bf16[8,2,128,1280]{3,2,1,0:T(8,128)(2,1)} custom-call(s32[1,8]{1,0:T(1,128)S(1)} %bitcast.1, bf16[4,2,128,2048]{3,2,1,0:T(8,128)(2,1)} %pool_ref.3), custom_call_target="tpu_custom_call" | custom-call | bytes 10485760 | tf_op jit(solution)/shard_map/pick_entries/pallas_call | solution.py:182
  6.5 5.6 %all-to-all-start = ((bf16[8,2,128,1280]{3,2,1,0:T(8,128)(2,1)}), bf16[8,2,128,1280]{3,2,1,0:T(8,128)(2,1)}, u32[]{:S(2)}, u32[]{:S(2)}) async-start(bf16[8,2,128,1280]{3,2,1,0:T(8,128)(2,1)} %pick_entries.2), calls=%async_computation | async-start | bytes 10485760 | tf_op jit(solution)/shard_map/all_to_all | solution.py:62
  12.2 3.6 pick_entries.3
  16.3 1.5 pack_rows.3
  18.1 1.8 pack_rows.2
  19.9 1.3 collective-permute-start
  21.4 1.2 collective-permute-start.2
  22.9 5.7 %collective-permute-done.3.rest_1_ = bf16[2,128,768]{2,1,0:T(8,128)(2,1)S(1)} collective-permute-done((bf16[2,128,768]{2,1,0:T(8,128)(2,1)}, bf16[2,128,768]{2,1,0:T(8,128)(2,1)S(1)}, u32[]{:S(2)}, u32[]{:S(2)}) %collective-permute-start.3) | collective-permute-done | bytes 393248 | tf_op jit(solution)/shard_map/ppermute | solution.py:30
  29.5 38.3 %collective-permute-done.4.rest_2_ = bf16[2,128,768]{2,1,0:T(8,128)(2,1)S(1)} collective-permute-done((bf16[2,128,768]{2,1,0:T(8,128)(2,1)S(1)}, bf16[2,128,768]{2,1,0:T(8,128)(2,1)S(1)}, u32[]{:S(2)}, u32[]{:S(2)}) %collective-permute-start.4) | collective-permute-done | bytes 393248 | tf_op jit(solution)/shard_map/ppermute | solution.py:30
  69.3 0.8 copy-done.8
  70.1 2.1 collective-permute-start.6
  72.3 1.1 collective-permute-start.10
  73.3 68.6 %all-to-all-done.rest_4_ = bf16[8,2,128,1280]{3,2,1,0:T(8,128)(2,1)} async-done(((bf16[8,2,128,1280]{3,2,1,0:T(8,128)(2,1)}), bf16[8,2,128,1280]{3,2,1,0:T(8,128)(2,1)}, u32[]{:S(2)}, u32[]{:S(2)}) %all-to-all-start) | async-done | bytes 5242912 | tf_op jit(solution)/shard_map/all_to_all | solution.py:62
  141.9 7.7 %all-to-all-start.1 = ((bf16[4,2,128,768]{3,2,1,0:T(8,128)(2,1)}), bf16[4,2,128,768]{3,2,1,0:T(8,128)(2,1)S(1)}, u32[]{:S(2)}, u32[]{:S(2)}) async-start(bf16[4,2,128,768]{3,2,1,0:T(8,128)(2,1)} %get-tuple-element.55), calls=%async_computation.1 | async-start | bytes 3145728 | tf_op jit(solution)/shard_map/all_to_all | solution.py:42
  149.6 2.4 collective-permute-start.12
  152.1 1.1 copy-done.7
  153.1 1.1 copy-done.9
  154.2 27.7 %attend_blocks.2 = (bf16[2,128,1280]{2,1,0:T(8,128)(2,1)}, bf16[2,128,1280]{2,1,0:T(8,128)(2,1)}, bf16[2,128,1280]{2,1,0:T(8,128)(2,1)}, bf16[2,128,1280]{2,1,0:T(8,128)(2,1)}, bf16[8,2,128,1280]{3,2,1,0:T(8,128)(2,1)}) custom-call(s32[1,8,2]{2,1,0:T(8,128)S(1)} %copy.9.uses, bf16[2,128,1280]{2,1,0:T(8,128)(2,1)S(1)} %copy-done.7, ...), custom_call_target="tpu_custom_call" | custom-call | flops 48318382080 | bytes 15728640 | tf_op jit(solution)/shard_map/attend_blocks/pallas_call | solution.py:290
  182.0 3.7 collective-permute-done.11.rest_7_
  186.4 6.1 %collective-permute-done.12.rest_8_ = bf16[2,128,768]{2,1,0:T(8,128)(2,1)S(1)} collective-permute-done((bf16[2,128,768]{2,1,0:T(8,128)(2,1)}, bf16[2,128,768]{2,1,0:T(8,128)(2,1)S(1)}, u32[]{:S(2)}, u32[]{:S(2)}) %collective-permute-start.12) | collective-permute-done | bytes 393248 | tf_op jit(solution)/shard_map/ppermute | solution.py:350
  193.3 6.0 %all-to-all-start.2 = ((bf16[8,2,128,1280]{3,2,1,0:T(8,128)(2,1)}), bf16[8,2,128,1280]{3,2,1,0:T(8,128)(2,1)}, u32[]{:S(2)}, u32[]{:S(2)}) async-start(bf16[8,2,128,1280]{3,2,1,0:T(8,128)(2,1)} %get-tuple-element.102), calls=%async_computation.2 | async-start | bytes 10485760 | tf_op jit(solution)/shard_map/all_to_all | solution.py:62
  199.8 2.2 collective-permute-start.9
  202.0 13.4 %collective-permute-done.7.refs_1_ = bf16[2,128,1280]{2,1,0:T(8,128)(2,1)S(1)} collective-permute-done((bf16[2,128,1280]{2,1,0:T(8,128)(2,1)}, bf16[2,128,1280]{2,1,0:T(8,128)(2,1)S(1)}, u32[]{:S(2)}, u32[]{:S(2)}) %collective-permute-start.7) | collective-permute-done | bytes 655392 | tf_op jit(solution)/shard_map/ppermute | solution.py:30
  215.3 13.9 %collective-permute-done.9.refs_3_ = bf16[2,128,1280]{2,1,0:T(8,128)(2,1)S(1)} collective-permute-done((bf16[2,128,1280]{2,1,0:T(8,128)(2,1)}, bf16[2,128,1280]{2,1,0:T(8,128)(2,1)S(1)}, u32[]{:S(2)}, u32[]{:S(2)}) %collective-permute-start.9) | collective-permute-done | bytes 655392 | tf_op jit(solution)/shard_map/ppermute | solution.py:30
  229.4 1.0 copy-done.10
  230.4 1.0 copy-done.12
  231.4 1.0 copy-done.14
  232.3 1.0 copy-done.16
  233.3 1.0 copy-done.18
  234.3 1.0 copy-done.20
  235.3 1.0 copy-done.22
  236.3 17.9 %attend_blocks.3 = (bf16[2,128,768]{2,1,0:T(8,128)(2,1)}, bf16[2,128,768]{2,1,0:T(8,128)(2,1)}, bf16[2,128,768]{2,1,0:T(8,128)(2,1)}, bf16[2,128,768]{2,1,0:T(8,...) custom-call(s32[1,8,2]{2,1,0:T(8,128)S(1)} %copy.10.uses, ...), custom_call_target="tpu_custom_call" | custom-call | flops 28991029248 | bytes 9437184 | tf_op jit(solution)/shard_map/attend_blocks/pallas_call | solution.py:290
  254.6 1.2 collective-permute-start.14
  255.8 1.2 collective-permute-start.15
  257.0 2.5 collective-permute-start.19
  259.4 1.2 collective-permute-start.20
  260.6 2.9 collective-permute-done.13.refs_5_
  263.5 9.5 %collective-permute-done.15.refs_7_ = bf16[2,128,768]{2,1,0:T(8,128)(2,1)S(1)} collective-permute-done((bf16[2,128,768]{2,1,0:T(8,128)(2,1)}, bf16[2,128,768]{2,1,0:T(8,128)(2,1)S(1)}, u32[]{:S(2)}, u32[]{:S(2)}) %collective-permute-start.15) | collective-permute-done | bytes 393248 | tf_op jit(solution)/shard_map/ppermute | solution.py:30
  273.0 2.4 collective-permute-start.16
  275.4 2.6 collective-permute-start.17
  278.0 59.7 %collective-permute-done.19.rest_4_ = bf16[2,128,768]{2,1,0:T(8,128)(2,1)S(1)} collective-permute-done((bf16[2,128,768]{2,1,0:T(8,128)(2,1)}, bf16[2,128,768]{2,1,0:T(8,128)(2,1)S(1)}, u32[]{:S(2)}, u32[]{:S(2)}) %collective-permute-start.19) | collective-permute-done | bytes 393248 | tf_op jit(solution)/shard_map/ppermute | solution.py:350
  338.5 18.1 %collective-permute-done.20.rest_5_ = bf16[2,128,768]{2,1,0:T(8,128)(2,1)S(1)} collective-permute-done((bf16[2,128,768]{2,1,0:T(8,128)(2,1)}, bf16[2,128,768]{2,1,0:T(8,128)(2,1)S(1)}, u32[]{:S(2)}, u32[]{:S(2)}) %collective-permute-start.20) | collective-permute-done | bytes 393248 | tf_op jit(solution)/shard_map/ppermute | solution.py:350
  356.6 1.0 copy-done.4
  357.6 2.1 unpack_rows.1
  359.8 6.2 %owner_sum.2.rest_8_ = bf16[4,2,128,2048]{3,2,1,0:T(8,128)(2,1)} custom-call(s32[1,8]{1,0:T(1,128)S(1)} %bitcast.3, bf16[8,2,128,1280]{3,2,1,0:T(8,128)(2,1)} %all-to-all-done.2.rest_0_), custom_call_target="tpu_custom_call" | custom-call | flops 2621440 | bytes 7864320 | tf_op jit(solution)/shard_map/owner_sum/pallas_call | solution.py:326
  366.0 6.9 %collective-permute-done.21.rest_6_ = bf16[2,128,768]{2,1,0:T(8,128)(2,1)} collective-permute-done((bf16[2,128,768]{2,1,0:T(8,128)(2,1)}, bf16[2,128,768]{2,1,0:T(8,128)(2,1)}, u32[]{:S(2)}, u32[]{:S(2)}) %collective-permute-start.21) | collective-permute-done | bytes 393248 | tf_op jit(solution)/shard_map/ppermute | solution.py:350
  372.9 6.9 %collective-permute-done.22.rest_7_ = bf16[2,128,768]{2,1,0:T(8,128)(2,1)} collective-permute-done((bf16[2,128,768]{2,1,0:T(8,128)(2,1)}, bf16[2,128,768]{2,1,0:T(8,128)(2,1)}, u32[]{:S(2)}, u32[]{:S(2)}) %collective-permute-start.22) | collective-permute-done | bytes 393248 | tf_op jit(solution)/shard_map/ppermute | solution.py:350
  379.9 4.0 %owner_sum.3 = bf16[4,2,128,2048]{3,2,1,0:T(8,128)(2,1)} custom-call(s32[1,8]{1,0:T(1,128)S(1)} %bitcast.4, bf16[2,128,768]{2,1,0:T(8,128)(2,1)S(1)} %copy-done.3, bf16[2,128,768]{2,1,0:T(8,128)(2,1)S(1)} %collective-permute-done.16.rest_1_, bf16[2,128,768]{2,1,0:T(8,128)(2,1)} %collective-permute-done.17.rest_2_, ...), custom_call_target="tpu_custom_call", output_to_operand_aliasing={{}: (9, {})} | custom-call | flops 1572864 | bytes 4718592 | tf_op jit(solution)/shard_map/owner_sum/pallas_call | solution.py:326
  (67 shorter events, 7.7 us)
Async XLA Ops:
  6.5 5.7 %copy-start.6 = (s32[1,8,1]{1,2,0:T(1,128)S(1)}, s32[1,8,1]{1,2,0:T(1,128)}, u32[]{:S(2)}) copy-start(s32[1,8,1]{1,2,0:T(1,128)} %param.7) | copy-start | bytes 100
  6.5 135.4 %all-to-all-start = ((bf16[8,2,128,1280]{3,2,1,0:T(8,128)(2,1)}), bf16[8,2,128,1280]{3,2,1,0:T(8,128)(2,1)}, u32[]{:S(2)}, u32[]{:S(2)}) async-start(bf16[8,2,128,1280]{3,2,1,0:T(8,128)(2,1)} %pick_entries.2), calls=%async_computation | async-start | bytes 10485760 | tf_op jit(solution)/shard_map/all_to_all | solution.py:62
  12.2 3.6 copy-start
  12.2 4.1 %copy-start.1 = (bf16[1,128,8192]{2,1,0:T(8,128)(2,1)S(1)}, bf16[1,128,8192]{2,1,0:T(8,128)(2,1)}, u32[]{:S(2)}) copy-start(bf16[1,128,8192]{2,1,0:T(8,128)(2,1)} %g_ref.3) | copy-start | bytes 6291460
  16.3 55.9 %copy-start.23 = (s32[1,8,2]{1,2,0:T(2,128)S(1)}, s32[1,8,2]{1,2,0:T(2,128)}, u32[]{:S(2)}) copy-start(s32[1,8,2]{1,2,0:T(2,128)} %param.8) | copy-start | bytes 196
  17.8 4.9 %copy-start.25 = (bf16[2,128,768]{2,1,0:T(8,128)(2,1)S(1)}, bf16[2,128,768]{2,1,0:T(8,128)(2,1)}, u32[]{:S(2)}) copy-start(bf16[2,128,768]{2,1,0:T(8,128)(2,1)} %get-tuple-element.67) | copy-start | bytes 1179652
  17.8 11.5 %copy-start.24 = (bf16[2,128,768]{2,1,0:T(8,128)(2,1)S(1)}, bf16[2,128,768]{2,1,0:T(8,128)(2,1)}, u32[]{:S(2)}) copy-start(bf16[2,128,768]{2,1,0:T(8,128)(2,1)} %get-tuple-element.68) | copy-start | bytes 1179652
  17.8 10.7 %collective-permute-start.3 = (bf16[2,128,768]{2,1,0:T(8,128)(2,1)}, bf16[2,128,768]{2,1,0:T(8,128)(2,1)S(1)}, u32[]{:S(2)}, u32[]{:S(2)}) collective-permute-start(bf16[2,128,768]{2,1,0:T(8,128)(2,1)} %get-tuple-element.66), channel_id=1, source_target_pairs={{0,1},{1,0},{2,3},{3,2},{4,5},{5,4},{6,7},{7,6},{8,9},{9,8},{10,11... | collective-permute-start | bytes 1179656 | tf_op jit(solution)/shard_map/ppermute | solution.py:30
  19.9 49.3 %collective-permute-start = (bf16[2,128,1280]{2,1,0:T(8,128)(2,1)}, bf16[2,128,1280]{2,1,0:T(8,128)(2,1)S(1)}, u32[]{:S(2)}, u32[]{:S(2)}) collective-permute-start(bf16[2,128,1280]{2,1,0:T(8,128)(2,1)} %get-tuple-element.58), channel_id=1, source_target_pairs={{0,1},{1,0},{2,3},{3,2},{4,5},{5,4},{6,7},{7,6},{8,9},{9,8},{10,11... | collective-permute-start | bytes 1966088 | tf_op jit(solution)/shard_map/ppermute | solution.py:30
  21.2 48.1 %collective-permute-start.1 = (bf16[2,128,1280]{2,1,0:T(8,128)(2,1)}, bf16[2,128,1280]{2,1,0:T(8,128)(2,1)S(1)}, u32[]{:S(2)}, u32[]{:S(2)}) collective-permute-start(bf16[2,128,1280]{2,1,0:T(8,128)(2,1)} %get-tuple-element.59), channel_id=1, source_target_pairs={{0,2},{1,3},{2,0},{3,1},{4,6},{5,7},{6,4},{7,5},{8,10},{9,11},{10,... | collective-permute-start | bytes 1966088 | tf_op jit(solution)/shard_map/ppermute | solution.py:30
  21.4 47.9 %collective-permute-start.2 = (bf16[2,128,1280]{2,1,0:T(8,128)(2,1)}, bf16[2,128,1280]{2,1,0:T(8,128)(2,1)S(1)}, u32[]{:S(2)}, u32[]{:S(2)}) collective-permute-start(bf16[2,128,1280]{2,1,0:T(8,128)(2,1)} %get-tuple-element.60), channel_id=1, source_target_pairs={{0,3},{1,2},{2,1},{3,0},{4,7},{5,6},{6,5},{7,4},{8,11},{9,10},{10,... | collective-permute-start | bytes 1966088 | tf_op jit(solution)/shard_map/ppermute | solution.py:30
  22.6 45.1 %collective-permute-start.4 = (bf16[2,128,768]{2,1,0:T(8,128)(2,1)S(1)}, bf16[2,128,768]{2,1,0:T(8,128)(2,1)S(1)}, u32[]{:S(2)}, u32[]{:S(2)}) collective-permute-start(bf16[2,128,768]{2,1,0:T(8,128)(2,1)S(1)} %copy-done.25), channel_id=1, source_target_pairs={{0,2},{1,3},{2,0},{3,1},{4,6},{5,7},{6,4},{7,5},{8,10},{9,11},{10,... | collective-permute-start | bytes 1179656 | tf_op jit(solution)/shard_map/ppermute | solution.py:30
  28.5 0.8 copy-start.11
  29.3 39.2 %collective-permute-start.5 = (bf16[2,128,768]{2,1,0:T(8,128)(2,1)S(1)}, bf16[2,128,768]{2,1,0:T(8,128)(2,1)S(1)}, u32[]{:S(2)}, u32[]{:S(2)}) collective-permute-start(bf16[2,128,768]{2,1,0:T(8,128)(2,1)S(1)} %copy-done.24), channel_id=1, source_target_pairs={{0,3},{1,2},{2,1},{3,0},{4,7},{5,6},{6,5},{7,4},{8,11},{9,10},{10,... | collective-permute-start | bytes 1179656 | tf_op jit(solution)/shard_map/ppermute | solution.py:30
  68.5 0.8 copy-start.15
  69.3 0.8 copy-start.8
  70.1 81.9 %collective-permute-start.6 = (bf16[2,128,768]{2,1,0:T(8,128)(2,1)}, bf16[2,128,768]{2,1,0:T(8,128)(2,1)S(1)}, u32[]{:S(2)}, u32[]{:S(2)}) collective-permute-start(bf16[2,128,768]{2,1,0:T(8,128)(2,1)} %get-tuple-element.69), channel_id=1, source_target_pairs={{0,16},{4,20},{8,24},{12,28},{16,0},{20,4},{24,8},{28,12},{1,17},{... | collective-permute-start | bytes 1179656 | tf_op jit(solution)/shard_map/ppermute | solution.py:350
  72.3 109.7 %collective-permute-start.10 = (bf16[2,128,768]{2,1,0:T(8,128)(2,1)}, bf16[2,128,768]{2,1,0:T(8,128)(2,1)}, u32[]{:S(2)}, u32[]{:S(2)}) collective-permute-start(bf16[2,128,768]{2,1,0:T(8,128)(2,1)} %get-tuple-element.76), channel_id=1, source_target_pairs={{0,20},{4,24},{8,28},{12,16},{20,0},{24,4},{28,8},{16,12},{1,21},{... | collective-permute-start | bytes 1179656 | tf_op jit(solution)/shard_map/ppermute | solution.py:350
  141.9 51.4 %all-to-all-start.1 = ((bf16[4,2,128,768]{3,2,1,0:T(8,128)(2,1)}), bf16[4,2,128,768]{3,2,1,0:T(8,128)(2,1)S(1)}, u32[]{:S(2)}, u32[]{:S(2)}) async-start(bf16[4,2,128,768]{3,2,1,0:T(8,128)(2,1)} %get-tuple-element.55), calls=%async_computation.1 | async-start | bytes 3145728 | tf_op jit(solution)/shard_map/all_to_all | solution.py:42
  149.6 36.1 %collective-permute-start.11 = (bf16[2,128,768]{2,1,0:T(8,128)(2,1)}, bf16[2,128,768]{2,1,0:T(8,128)(2,1)S(1)}, u32[]{:S(2)}, u32[]{:S(2)}) collective-permute-start(bf16[2,128,768]{2,1,0:T(8,128)(2,1)} %get-tuple-element.79), channel_id=1, source_target_pairs={{0,24},{4,28},{8,16},{12,20},{24,0},{28,4},{16,8},{20,12},{1,25},{... | collective-permute-start | bytes 1179656 | tf_op jit(solution)/shard_map/ppermute | solution.py:350
  149.6 42.9 %collective-permute-start.12 = (bf16[2,128,768]{2,1,0:T(8,128)(2,1)}, bf16[2,128,768]{2,1,0:T(8,128)(2,1)S(1)}, u32[]{:S(2)}, u32[]{:S(2)}) collective-permute-start(bf16[2,128,768]{2,1,0:T(8,128)(2,1)} %get-tuple-element.80), channel_id=1, source_target_pairs={{0,28},{4,16},{8,20},{12,24},{28,0},{16,4},{20,8},{24,12},{1,29},{... | collective-permute-start | bytes 1179656 | tf_op jit(solution)/shard_map/ppermute | solution.py:350
  152.1 1.1 copy-start.7
  153.1 1.1 copy-start.9
  154.2 27.7 %copy-start.17 = (bf16[2,128,768]{2,1,0:T(8,128)(2,1)}, bf16[2,128,768]{2,1,0:T(8,128)(2,1)S(1)}, u32[]{:S(2)}) copy-start(bf16[2,128,768]{2,1,0:T(8,128)(2,1)S(1)} %collective-permute-done.6.rest_5_) | copy-start | bytes 1179652
  193.3 166.5 %all-to-all-start.2 = ((bf16[8,2,128,1280]{3,2,1,0:T(8,128)(2,1)}), bf16[8,2,128,1280]{3,2,1,0:T(8,128)(2,1)}, u32[]{:S(2)}, u32[]{:S(2)}) async-start(bf16[8,2,128,1280]{3,2,1,0:T(8,128)(2,1)} %get-tuple-element.102), calls=%async_computation.2 | async-start | bytes 10485760 | tf_op jit(solution)/shard_map/all_to_all | solution.py:62
  199.3 16.0 %collective-permute-start.7 = (bf16[2,128,1280]{2,1,0:T(8,128)(2,1)}, bf16[2,128,1280]{2,1,0:T(8,128)(2,1)S(1)}, u32[]{:S(2)}, u32[]{:S(2)}) collective-permute-start(bf16[2,128,1280]{2,1,0:T(8,128)(2,1)} %get-tuple-element.72), channel_id=1, source_target_pairs={{0,1},{1,0},{2,3},{3,2},{4,5},{5,4},{6,7},{7,6},{8,9},{9,8},{10,11... | collective-permute-start | bytes 1966088 | tf_op jit(solution)/shard_map/ppermute | solution.py:30
  199.6 15.8 %collective-permute-start.8 = (bf16[2,128,1280]{2,1,0:T(8,128)(2,1)}, bf16[2,128,1280]{2,1,0:T(8,128)(2,1)S(1)}, u32[]{:S(2)}, u32[]{:S(2)}) collective-permute-start(bf16[2,128,1280]{2,1,0:T(8,128)(2,1)} %get-tuple-element.73), channel_id=1, source_target_pairs={{0,2},{1,3},{2,0},{3,1},{4,6},{5,7},{6,4},{7,5},{8,10},{9,11},{10,... | collective-permute-start | bytes 1966088 | tf_op jit(solution)/shard_map/ppermute | solution.py:30
  199.8 29.5 %collective-permute-start.9 = (bf16[2,128,1280]{2,1,0:T(8,128)(2,1)}, bf16[2,128,1280]{2,1,0:T(8,128)(2,1)S(1)}, u32[]{:S(2)}, u32[]{:S(2)}) collective-permute-start(bf16[2,128,1280]{2,1,0:T(8,128)(2,1)} %get-tuple-element.74), channel_id=1, source_target_pairs={{0,3},{1,2},{2,1},{3,0},{4,7},{5,6},{6,5},{7,4},{8,11},{9,10},{10,... | collective-permute-start | bytes 1966088 | tf_op jit(solution)/shard_map/ppermute | solution.py:30
  229.4 1.0 copy-start.10
  230.4 1.0 copy-start.12
  231.3 1.0 copy-start.14
  232.3 1.0 copy-start.16
  233.3 1.0 copy-start.18
  234.3 1.0 copy-start.20
  235.3 1.0 copy-start.22
  236.3 120.3 %copy-start.2 = (bf16[2,128,1280]{2,1,0:T(8,128)(2,1)S(1)}, bf16[2,128,1280]{2,1,0:T(8,128)(2,1)}, u32[]{:S(2)}) copy-start(bf16[2,128,1280]{2,1,0:T(8,128)(2,1)} %get-tuple-element.71.refs_0_) | copy-start | bytes 1966084
  254.3 9.3 %collective-permute-start.13 = (bf16[2,128,768]{2,1,0:T(8,128)(2,1)}, bf16[2,128,768]{2,1,0:T(8,128)(2,1)S(1)}, u32[]{:S(2)}, u32[]{:S(2)}) collective-permute-start(bf16[2,128,768]{2,1,0:T(8,128)(2,1)} %get-tuple-element.82), channel_id=1, source_target_pairs={{0,1},{1,0},{2,3},{3,2},{4,5},{5,4},{6,7},{7,6},{8,9},{9,8},{10,11... | collective-permute-start | bytes 1179656 | tf_op jit(solution)/shard_map/ppermute | solution.py:30
  254.6 9.0 %collective-permute-start.14 = (bf16[2,128,768]{2,1,0:T(8,128)(2,1)}, bf16[2,128,768]{2,1,0:T(8,128)(2,1)S(1)}, u32[]{:S(2)}, u32[]{:S(2)}) collective-permute-start(bf16[2,128,768]{2,1,0:T(8,128)(2,1)} %get-tuple-element.83), channel_id=1, source_target_pairs={{0,2},{1,3},{2,0},{3,1},{4,6},{5,7},{6,4},{7,5},{8,10},{9,11},{10,... | collective-permute-start | bytes 1179656 | tf_op jit(solution)/shard_map/ppermute | solution.py:30
  255.8 17.2 %collective-permute-start.15 = (bf16[2,128,768]{2,1,0:T(8,128)(2,1)}, bf16[2,128,768]{2,1,0:T(8,128)(2,1)S(1)}, u32[]{:S(2)}, u32[]{:S(2)}) collective-permute-start(bf16[2,128,768]{2,1,0:T(8,128)(2,1)} %get-tuple-element.84), channel_id=1, source_target_pairs={{0,3},{1,2},{2,1},{3,0},{4,7},{5,6},{6,5},{7,4},{8,11},{9,10},{10,... | collective-permute-start | bytes 1179656 | tf_op jit(solution)/shard_map/ppermute | solution.py:30
  257.0 80.7 %collective-permute-start.19 = (bf16[2,128,768]{2,1,0:T(8,128)(2,1)}, bf16[2,128,768]{2,1,0:T(8,128)(2,1)S(1)}, u32[]{:S(2)}, u32[]{:S(2)}) collective-permute-start(bf16[2,128,768]{2,1,0:T(8,128)(2,1)} %get-tuple-element.95), channel_id=1, source_target_pairs={{0,16},{4,20},{8,24},{12,28},{16,0},{20,4},{24,8},{28,12},{1,17},{... | collective-permute-start | bytes 1179656 | tf_op jit(solution)/shard_map/ppermute | solution.py:350
  259.4 97.2 %collective-permute-start.20 = (bf16[2,128,768]{2,1,0:T(8,128)(2,1)}, bf16[2,128,768]{2,1,0:T(8,128)(2,1)S(1)}, u32[]{:S(2)}, u32[]{:S(2)}) collective-permute-start(bf16[2,128,768]{2,1,0:T(8,128)(2,1)} %get-tuple-element.96), channel_id=1, source_target_pairs={{0,20},{4,24},{8,28},{12,16},{20,0},{24,4},{28,8},{16,12},{1,21},{... | collective-permute-start | bytes 1179656 | tf_op jit(solution)/shard_map/ppermute | solution.py:350
  273.0 93.0 %collective-permute-start.16 = (bf16[2,128,768]{2,1,0:T(8,128)(2,1)}, bf16[2,128,768]{2,1,0:T(8,128)(2,1)S(1)}, u32[]{:S(2)}, u32[]{:S(2)}) collective-permute-start(bf16[2,128,768]{2,1,0:T(8,128)(2,1)} %get-tuple-element.92), channel_id=1, source_target_pairs={{0,4},{4,0},{8,12},{12,8},{16,20},{20,16},{24,28},{28,24},{1,5},{5... | collective-permute-start | bytes 1179656 | tf_op jit(solution)/shard_map/ppermute | solution.py:52
  275.4 90.6 %collective-permute-start.17 = (bf16[2,128,768]{2,1,0:T(8,128)(2,1)}, bf16[2,128,768]{2,1,0:T(8,128)(2,1)}, u32[]{:S(2)}, u32[]{:S(2)}) collective-permute-start(bf16[2,128,768]{2,1,0:T(8,128)(2,1)} %get-tuple-element.93), channel_id=1, source_target_pairs={{0,8},{4,12},{8,0},{12,4},{16,24},{20,28},{24,16},{28,20},{1,9},{5... | collective-permute-start | bytes 1179656 | tf_op jit(solution)/shard_map/ppermute | solution.py:52
  278.0 88.1 %collective-permute-start.18 = (bf16[2,128,768]{2,1,0:T(8,128)(2,1)}, bf16[2,128,768]{2,1,0:T(8,128)(2,1)}, u32[]{:S(2)}, u32[]{:S(2)}) collective-permute-start(bf16[2,128,768]{2,1,0:T(8,128)(2,1)} %get-tuple-element.94), channel_id=1, source_target_pairs={{0,12},{4,8},{8,4},{12,0},{16,28},{20,24},{24,20},{28,16},{1,13},{... | collective-permute-start | bytes 1179656 | tf_op jit(solution)/shard_map/ppermute | solution.py:52
  337.7 35.2 %collective-permute-start.21 = (bf16[2,128,768]{2,1,0:T(8,128)(2,1)}, bf16[2,128,768]{2,1,0:T(8,128)(2,1)}, u32[]{:S(2)}, u32[]{:S(2)}) collective-permute-start(bf16[2,128,768]{2,1,0:T(8,128)(2,1)} %get-tuple-element.98), channel_id=1, source_target_pairs={{0,24},{4,28},{8,16},{12,20},{24,0},{28,4},{16,8},{20,12},{1,25},{... | collective-permute-start | bytes 1179656 | tf_op jit(solution)/shard_map/ppermute | solution.py:350
  356.6 23.2 %collective-permute-start.22 = (bf16[2,128,768]{2,1,0:T(8,128)(2,1)}, bf16[2,128,768]{2,1,0:T(8,128)(2,1)}, u32[]{:S(2)}, u32[]{:S(2)}) collective-permute-start(bf16[2,128,768]{2,1,0:T(8,128)(2,1)} %get-tuple-element.100), channel_id=1, source_target_pairs={{0,28},{4,16},{8,20},{12,24},{28,0},{16,4},{20,8},{24,12},{1,29},{... | collective-permute-start | bytes 1179656 | tf_op jit(solution)/shard_map/ppermute | solution.py:350
  356.6 1.0 copy-start.4
  359.8 20.1 %copy-start.3 = (bf16[2,128,768]{2,1,0:T(8,128)(2,1)S(1)}, bf16[2,128,768]{2,1,0:T(8,128)(2,1)}, u32[]{:S(2)}) copy-start(bf16[2,128,768]{2,1,0:T(8,128)(2,1)} %get-tuple-element.91.rest_0_) | copy-start | bytes 1179652
  (4 other events, 2.9 us)
